TPU v7x, 32 devices: a whole 2x2x4 slice. The times are simulated.
32 devices in a mesh: row: 8 (over z, core), col: 4 (over y, x).
Axes of the slice: x: 2, y: 2, z: 4, core: 2. Of those that a mesh axis runs over, the one named last changes fastest.
Arguments:
- height: float32 [1024, 1024], P('row', 'col'), may hold values from 0.5 to 1.5
- noise: float32 [1024, 1024], P('row', 'col'), may hold values from -8 to 8
Outputs:
- solution_field: float32 [1024, 1024], P('row', 'col')
- residual: float32 [1024, 1024], P('row', 'col')
All inputs are finite; a program needn't handle non-finite values.
Results may differ from a plain program's by a relative error of at most 0.0003.
Values sent between devices are 32-bit elements; how exact they have to be, the bound alone decides.
No kernel may reach another device: no remote copies, remote signals or barrier semaphores. Data moves between devices by JAX's collectives and lax.ppermute only.
A program may use at most 64 MiB of HBM per device.

v0:
```python
import jax
import jax.numpy as jnp
from jax import lax
from jax.sharding import PartitionSpec as P

SUB = 128
OV = 8
ITERS = 2


damping = 2.0 ** (-28)
highest = lax.Precision.HIGHEST


def extended_2(block, sides, width):
    for axis, dim in sides:
        count = lax.axis_size(axis)
        forward = [(i, i + 1) for i in range(count - 1)]
        backward = [(target, source) for source, target in forward]
        low = lax.ppermute(
            lax.slice_in_dim(block, block.shape[dim] - width, None, axis=dim), axis, forward
        )
        high = lax.ppermute(lax.slice_in_dim(block, 0, width, axis=dim), axis, backward)
        block = jnp.concatenate([low, block, high], axis=dim)
    return block


def sine_basis(count):
    steps = jnp.arange(1, count + 1, dtype=jnp.float32)
    basis = jnp.sqrt(2.0 / (count + 1.0)) * jnp.sin(
        jnp.pi * steps[:, None] * steps[None, :] / (count + 1.0)
    )
    eig = 2.0 - 2.0 * jnp.cos(jnp.pi * steps / (count + 1.0))
    return (basis, eig)


def eigen_solve(blocks, means, basis, eig):
    spectral = jnp.einsum("ba,nbc,cd->nad", basis, blocks, basis, precision=highest)
    spectral = spectral / (damping + means[:, None, None] * (eig[:, None] + eig[None, :]) ** 2)
    return jnp.einsum("ab,nbc,dc->nad", basis, spectral, basis, precision=highest)


def coarse_solve(sums):
    basis_r, eig_r = sine_basis(sums.shape[0])
    basis_c, eig_c = sine_basis(sums.shape[1])
    spectral = jnp.dot(jnp.dot(basis_r.T, sums, precision=highest), basis_c, precision=highest)
    scale = (eig_r[:, None] + eig_c[None, :]) / (SUB * SUB)
    spectral = spectral / (SUB * SUB * (damping + scale * scale))
    return jnp.dot(jnp.dot(basis_r, spectral, precision=highest), basis_c.T, precision=highest)


def inner_lap(padded):
    beside = padded[2:, 1:-1] + padded[:-2, 1:-1] + padded[1:-1, 2:] + padded[1:-1, :-2]
    return 4.0 * padded[1:-1, 1:-1] - beside


def global_total(value):
    return lax.psum(value, ("row", "col"))


def body(height, noise):
    rows_t, cols_t = noise.shape
    block_r = rows_t // SUB
    block_c = cols_t // SUB
    count_r = lax.axis_size("row")
    count_c = lax.axis_size("col")
    ext = SUB + 2 * OV
    basis, eig = sine_basis(ext)
    mobility = height * height * height
    mob_depth = 1
    mobility_deep = extended_2(mobility, (("row", 0), ("col", 1)), mob_depth)
    means = (
        mobility.reshape(block_r, SUB, block_c, SUB).mean(axis=(1, 3)).reshape(block_r * block_c)
    )

    def margin_of(resid):
        return extended_2(resid, (("row", 0), ("col", 1)), OV)

    solution_field = jnp.zeros_like(noise)
    residual = noise
    residual_wide = margin_of(noise)
    direction = noise
    norm_old = jnp.float32(1.0)
    for step in range(ITERS):
        wide = margin_of(residual) if step > 0 else residual_wide
        pieces = []
        first = 0
        for second in range(block_c):
            pieces.append(wide[first * SUB : first * SUB + ext, second * SUB : second * SUB + ext])
        blocks = jnp.stack(pieces)
        solved = eigen_solve(blocks, means, basis, eig)
        contribution = jnp.sum(blocks * solved)
        extended = jnp.zeros((rows_t + 2 * OV, cols_t + 2 * OV), jnp.float32)
        first = 0
        for second in range(block_c):
            extended = extended.at[
                first * SUB : first * SUB + ext, second * SUB : second * SUB + ext
            ].add(solved[first * block_c + second])
        empty = jnp.zeros((rows_t, cols_t), jnp.float32)
        vertical = empty.at[:OV].set(extended[:OV, OV:-OV]).at[-OV:].set(extended[-OV:, OV:-OV])
        sideways = (
            empty.at[:, :OV].set(extended[OV:-OV, :OV]).at[:, -OV:].set(extended[OV:-OV, -OV:])
        )
        diagonal = empty.at[:OV, :OV].set(extended[:OV, :OV]).at[:OV, -OV:].set(extended[:OV, -OV:])
        diagonal = (
            diagonal.at[-OV:, :OV].set(extended[-OV:, :OV]).at[-OV:, -OV:].set(extended[-OV:, -OV:])
        )
        stacked = jnp.stack([vertical, sideways, diagonal])
        arrived = extended_2(stacked, (("row", 1), ("col", 2)), OV)
        result = extended[OV:-OV, OV:-OV]
        result = result.at[:OV].add(arrived[0, :OV, OV:-OV]).at[-OV:].add(arrived[0, -OV:, OV:-OV])
        result = (
            result.at[:, :OV].add(arrived[1, OV:-OV, :OV]).at[:, -OV:].add(arrived[1, OV:-OV, -OV:])
        )
        result = (
            result.at[:OV, :OV].add(arrived[2, :OV, :OV]).at[:OV, -OV:].add(arrived[2, :OV, -OV:])
        )
        result = (
            result.at[-OV:, :OV]
            .add(arrived[2, -OV:, :OV])
            .at[-OV:, -OV:]
            .add(arrived[2, -OV:, -OV:])
        )
        sums = residual.reshape(block_r, SUB, block_c, SUB).sum(axis=(1, 3))
        precondition_row_at = lax.axis_index("row") * block_r
        precondition_col_at = lax.axis_index("col") * block_c
        placed = lax.dynamic_update_slice(
            jnp.zeros((count_r * block_r, count_c * block_c), jnp.float32),
            sums,
            (precondition_row_at, precondition_col_at),
        )
        whole, local_norm = lax.psum((placed, contribution), ("row", "col"))
        precondition_coarse = coarse_solve(whole)
        own = lax.dynamic_slice(
            precondition_coarse, (precondition_row_at, precondition_col_at), (block_r, block_c)
        )
        precond = result + jnp.broadcast_to(
            own[:, None, :, None], (block_r, SUB, block_c, SUB)
        ).reshape(rows_t, cols_t)
        norm_now = local_norm + jnp.sum(whole * precondition_coarse)
        precond, norm_now = (precond, norm_now)
        if step == 0:
            direction = precond
        else:
            direction = precond + norm_now / norm_old * direction
        apply_wide = extended_2(direction, (("row", 0), ("col", 1)), 2)
        weighted = mobility_deep * inner_lap(apply_wide)
        image = damping * direction + inner_lap(weighted)
        alpha = norm_now / global_total(jnp.sum(direction * image))
        solution_field = solution_field + alpha * direction
        residual = residual - alpha * image
        norm_old = norm_now
    return (solution_field, residual)


def solution(mesh):
    in_specs = (P("row", "col"), P("row", "col"))
    out_specs = (P("row", "col"), P("row", "col"))
    return jax.shard_map(body, mesh=mesh, in_specs=in_specs, out_specs=out_specs, check_vma=False)
```

profile of v0, /device:TPU:0, one launch (start us, length us, event | category | flops | bytes accessed | tf_op | source)
XLA Modules:
  0.0 331.1 jit_solution(8698158320426594796)
XLA Ops:
  1.3 2.3 collective-permute-start
  3.7 1.3 collective-permute-start.1
  6.0 1.4 collective-permute-start.9
  7.4 5.9 %collective-permute-start.8 = (f32[1,256]{1,0:T(1,128)S(1)}, f32[1,256]{1,0:T(1,128)S(1)}, u32[]{:S(2)}, u32[]{:S(2)}) collective-permute-start(f32[1,256]{1,0:T(1,128)S(1)} %get-tuple-element.482), channel_id=1, source_target_pairs={{0,4},{4,8},{8,12},{12,16},{16,20},{20,24},{24,28},{1,5},{5,9},{9,... | collective-permute-start | bytes 3080 | tf_op jit(solution)/shard_map/ppermute | solution.py:20
  15.8 3.4 %collective-permute-start.2 = (f32[144,8]{1,0:T(8,128)S(1)}, f32[144,8]{1,0:T(8,128)S(1)}, u32[]{:S(2)}, u32[]{:S(2)}) collective-permute-start(f32[144,8]{1,0:T(8,128)S(1)} %get-tuple-element.470), channel_id=1, source_target_pairs={{0,1},{1,2},{2,3},{4,5},{5,6},{6,7},{8,9},{9,10},{10,11},{12,13},{... | collective-permute-start | bytes 13832 | tf_op jit(solution)/shard_map/ppermute | solution.py:20
  19.2 1.3 collective-permute-start.3
  20.8 42.3 %psum.43 = f32[8,8]{1,0:T(8,128)S(1)} all-reduce(f32[8,8]{1,0:T(8,128)S(1)} %dynamic_update_slice.6), channel_id=1, replica_groups=mesh['row'=8,'col'=4] {'row','col'}, use_global_device_ids=true, to_apply=%region_6.0 | all-reduce | flops 64 | bytes 512 | tf_op jit(solution)/shard_map/psum | solution.py:132
  68.5 1.6 multiply_reduce_fusion.1
  71.8 2.0 slice_bitcast_fusion.24
  73.7 1.8 scatter.61
  78.4 1.3 collective-permute-start.5
  79.9 3.4 %collective-permute-done.5 = f32[3,8,256]{2,1,0:T(8,128)S(1)} collective-permute-done((f32[3,8,256]{2,1,0:T(8,128)S(1)}, f32[3,8,256]{2,1,0:T(8,128)S(1)}, u32[]{:S(2)}, u32[]{:S(2)}) %collective-permute-start.5) | collective-permute-done | bytes 24608 | tf_op jit(solution)/shard_map/ppermute | solution.py:23
  83.4 4.2 %collective-permute-start.6 = (f32[3,144,8]{2,1,0:T(8,128)S(1)}, f32[3,144,8]{2,1,0:T(8,128)S(1)}, u32[]{:S(2)}, u32[]{:S(2)}) collective-permute-start(f32[3,144,8]{2,1,0:T(8,128)S(1)} %get-tuple-element.451), channel_id=1, source_target_pairs={{0,1},{1,2},{2,3},{4,5},{5,6},{6,7},{8,9},{9,10},{10,11},{12,13},{... | collective-permute-start | bytes 41480 | tf_op jit(solution)/shard_map/ppermute | solution.py:20
  87.6 1.3 collective-permute-start.7
  89.0 2.8 collective-permute-done.6
  93.1 5.3 %collective-permute-done.7 = f32[3,144,8]{2,1,0:T(8,128)S(1)} collective-permute-done((f32[3,144,8]{2,1,0:T(8,128)S(1)}, f32[3,144,8]{2,1,0:T(8,128)S(1)}, u32[]{:S(2)}, u32[]{:S(2)}) %collective-permute-start.7) | collective-permute-done | bytes 13856 | tf_op jit(solution)/shard_map/ppermute | solution.py:23
  99.7 2.0 add_select_fusion.3
  101.6 1.8 scatter-add.79
  104.5 1.3 collective-permute-start.13
  105.8 4.0 %collective-permute-start.12 = (f32[2,256]{1,0:T(2,128)S(1)}, f32[2,256]{1,0:T(2,128)S(1)}, u32[]{:S(2)}, u32[]{:S(2)}) collective-permute-start(f32[2,256]{1,0:T(2,128)S(1)} %get-tuple-element.486), channel_id=1, source_target_pairs={{0,4},{4,8},{8,12},{12,16},{16,20},{20,24},{24,28},{1,5},{5,9},{9,... | collective-permute-start | bytes 6152 | tf_op jit(solution)/shard_map/ppermute | solution.py:20
  110.7 3.4 %collective-permute-start.14 = (f32[132,2]{1,0:T(8,128)S(1)}, f32[132,2]{1,0:T(8,128)S(1)}, u32[]{:S(2)}, u32[]{:S(2)}) collective-permute-start(f32[132,2]{1,0:T(8,128)S(1)} %get-tuple-element.477), channel_id=1, source_target_pairs={{0,1},{1,2},{2,3},{4,5},{5,6},{6,7},{8,9},{9,10},{10,11},{12,13},{... | collective-permute-start | bytes 3176 | tf_op jit(solution)/shard_map/ppermute | solution.py:20
  114.1 1.3 collective-permute-start.15
  116.8 5.2 %collective-permute-start.10 = (f32[130,1]{1,0:T(8,128)S(1)}, f32[130,1]{1,0:T(8,128)S(1)}, u32[]{:S(2)}, u32[]{:S(2)}) collective-permute-start(f32[130,1]{1,0:T(8,128)S(1)} %get-tuple-element.474), channel_id=1, source_target_pairs={{0,1},{1,2},{2,3},{4,5},{5,6},{6,7},{8,9},{9,10},{10,11},{12,13},{... | collective-permute-start | bytes 1568 | tf_op jit(solution)/shard_map/ppermute | solution.py:20
  122.3 1.6 collective-permute-done.10
  125.2 45.8 %all-reduce.9 = (f32[]{:T(128)}, f32[]{:T(128)}) all-reduce(f32[]{:T(128)} %get-tuple-element.494, f32[]{:T(128)} %get-tuple-element.444), channel_id=1, replica_groups=mesh['row'=8,'col'=4] {'row','col'}, use_global_device_ids=true, to_apply=%region_3.0 | all-reduce | flops 2 | bytes 16 | tf_op jit(solution)/shard_map/psum | solution.py:132
  172.9 1.3 collective-permute-start.17
  174.2 3.0 collective-permute-start.16
  178.1 4.2 %collective-permute-start.18 = (f32[144,8]{1,0:T(8,128)S(1)}, f32[144,8]{1,0:T(8,128)S(1)}, u32[]{:S(2)}, u32[]{:S(2)}) collective-permute-start(f32[144,8]{1,0:T(8,128)S(1)} %get-tuple-element.464), channel_id=1, source_target_pairs={{0,1},{1,2},{2,3},{4,5},{5,6},{6,7},{8,9},{9,10},{10,11},{12,13},{... | collective-permute-start | bytes 13832 | tf_op jit(solution)/shard_map/ppermute | solution.py:20
  182.3 1.3 collective-permute-start.19
  184.9 4.1 %collective-permute-done.19 = f32[144,8]{1,0:T(8,128)S(1)} collective-permute-done((f32[144,8]{1,0:T(8,128)S(1)}, f32[144,8]{1,0:T(8,128)S(1)}, u32[]{:S(2)}, u32[]{:S(2)}) %collective-permute-start.19) | collective-permute-done | bytes 4640 | tf_op jit(solution)/shard_map/ppermute | solution.py:23
  192.7 1.6 multiply_reduce_fusion
  195.7 2.0 slice_bitcast_fusion.18
  197.9 1.8 scatter.75
  201.3 1.7 collective-permute-start.20
  203.0 1.3 collective-permute-start.21
  204.3 43.6 %all-reduce.8 = (f32[]{:T(128)}, f32[8,8]{1,0:T(8,128)S(1)}) all-reduce(f32[]{:T(128)} %get-tuple-element.498, f32[8,8]{1,0:T(8,128)S(1)} %dynamic_update_slice.7), channel_id=1, replica_groups=mesh['row'=8,'col'=4] {'row','col'}, use_global_device_ids=true, to_apply=%region_14.0 | all-reduce | flops 65 | bytes 520 | tf_op jit(solution)/shard_map/psum | solution.py:132
  251.4 4.2 %collective-permute-start.22 = (f32[3,144,8]{2,1,0:T(8,128)S(1)}, f32[3,144,8]{2,1,0:T(8,128)S(1)}, u32[]{:S(2)}, u32[]{:S(2)}) collective-permute-start(f32[3,144,8]{2,1,0:T(8,128)S(1)} %get-tuple-element.449), channel_id=1, source_target_pairs={{0,1},{1,2},{2,3},{4,5},{5,6},{6,7},{8,9},{9,10},{10,11},{12,13},{... | collective-permute-start | bytes 41480 | tf_op jit(solution)/shard_map/ppermute | solution.py:20
  255.6 1.3 collective-permute-start.23
  256.9 3.2 collective-permute-done.22
  261.4 5.4 %collective-permute-done.23 = f32[3,144,8]{2,1,0:T(8,128)S(1)} collective-permute-done((f32[3,144,8]{2,1,0:T(8,128)S(1)}, f32[3,144,8]{2,1,0:T(8,128)S(1)}, u32[]{:S(2)}, u32[]{:S(2)}) %collective-permute-start.23) | collective-permute-done | bytes 13856 | tf_op jit(solution)/shard_map/ppermute | solution.py:23
  268.0 2.0 add_select_fusion.2
  270.0 1.8 scatter-add.95
  272.8 1.3 collective-permute-start.25
  274.1 3.0 collective-permute-start.24
  278.1 3.0 collective-permute-start.26
  281.1 1.3 collective-permute-start.27
  283.0 4.3 %collective-permute-done.27 = f32[132,2]{1,0:T(8,128)S(1)} collective-permute-done((f32[132,2]{1,0:T(8,128)S(1)}, f32[132,2]{1,0:T(8,128)S(1)}, u32[]{:S(2)}, u32[]{:S(2)}) %collective-permute-start.27) | collective-permute-done | bytes 1088 | tf_op jit(solution)/shard_map/ppermute | solution.py:23
  288.6 40.4 %psum.47 = f32[]{:T(128)} all-reduce(f32[]{:T(128)} %get-tuple-element.438), channel_id=1, replica_groups=mesh['row'=8,'col'=4] {'row','col'}, use_global_device_ids=true, to_apply=%region_20.0 | all-reduce | flops 1 | bytes 8 | tf_op jit(solution)/shard_map/psum | solution.py:58
  (153 shorter events, 40.9 us)
Async XLA Ops:
  1.3 14.3 %collective-permute-start = (f32[8,256]{1,0:T(8,128)S(1)}, f32[8,256]{1,0:T(8,128)S(1)}, u32[]{:S(2)}, u32[]{:S(2)}) collective-permute-start(f32[8,256]{1,0:T(8,128)S(1)} %get-tuple-element.491), channel_id=1, source_target_pairs={{0,4},{4,8},{8,12},{12,16},{16,20},{20,24},{24,28},{1,5},{5,9},{9,... | collective-permute-start | bytes 24584 | tf_op jit(solution)/shard_map/ppermute | solution.py:20
  3.7 12.0 %collective-permute-start.1 = (f32[8,256]{1,0:T(8,128)S(1)}, f32[8,256]{1,0:T(8,128)S(1)}, u32[]{:S(2)}, u32[]{:S(2)}) collective-permute-start(f32[8,256]{1,0:T(8,128)S(1)} %get-tuple-element.490), channel_id=1, source_target_pairs={{4,0},{8,4},{12,8},{16,12},{20,16},{24,20},{28,24},{5,1},{9,5},{13... | collective-permute-start | bytes 24584 | tf_op jit(solution)/shard_map/ppermute | solution.py:23
  5.9 9.7 %copy-start = (f32[128,256]{1,0:T(8,128)S(1)}, f32[128,256]{1,0:T(8,128)}, u32[]{:S(2)}) copy-start(f32[128,256]{1,0:T(8,128)} %param.75) | copy-start | bytes 393220
  6.0 103.8 %collective-permute-start.9 = (f32[1,256]{1,0:T(1,128)S(1)}, f32[1,256]{1,0:T(1,128)S(1)}, u32[]{:S(2)}, u32[]{:S(2)}) collective-permute-start(f32[1,256]{1,0:T(1,128)S(1)} %get-tuple-element.483), channel_id=1, source_target_pairs={{4,0},{8,4},{12,8},{16,12},{20,16},{24,20},{28,24},{5,1},{9,5},{13... | collective-permute-start | bytes 3080 | tf_op jit(solution)/shard_map/ppermute | solution.py:23
  7.4 102.4 %collective-permute-start.8 = (f32[1,256]{1,0:T(1,128)S(1)}, f32[1,256]{1,0:T(1,128)S(1)}, u32[]{:S(2)}, u32[]{:S(2)}) collective-permute-start(f32[1,256]{1,0:T(1,128)S(1)} %get-tuple-element.482), channel_id=1, source_target_pairs={{0,4},{4,8},{8,12},{12,16},{16,20},{20,24},{24,28},{1,5},{5,9},{9,... | collective-permute-start | bytes 3080 | tf_op jit(solution)/shard_map/ppermute | solution.py:20
  13.6 0.7 copy-start.1
  15.8 49.1 %collective-permute-start.2 = (f32[144,8]{1,0:T(8,128)S(1)}, f32[144,8]{1,0:T(8,128)S(1)}, u32[]{:S(2)}, u32[]{:S(2)}) collective-permute-start(f32[144,8]{1,0:T(8,128)S(1)} %get-tuple-element.470), channel_id=1, source_target_pairs={{0,1},{1,2},{2,3},{4,5},{5,6},{6,7},{8,9},{9,10},{10,11},{12,13},{... | collective-permute-start | bytes 13832 | tf_op jit(solution)/shard_map/ppermute | solution.py:20
  19.2 45.7 %collective-permute-start.3 = (f32[144,8]{1,0:T(8,128)S(1)}, f32[144,8]{1,0:T(8,128)S(1)}, u32[]{:S(2)}, u32[]{:S(2)}) collective-permute-start(f32[144,8]{1,0:T(8,128)S(1)} %get-tuple-element.471), channel_id=1, source_target_pairs={{1,0},{2,1},{3,2},{5,4},{6,5},{7,6},{9,8},{10,9},{11,10},{13,12},{... | collective-permute-start | bytes 13832 | tf_op jit(solution)/shard_map/ppermute | solution.py:23
  77.1 2.8 collective-permute-start.4
  78.4 4.9 %collective-permute-start.5 = (f32[3,8,256]{2,1,0:T(8,128)S(1)}, f32[3,8,256]{2,1,0:T(8,128)S(1)}, u32[]{:S(2)}, u32[]{:S(2)}) collective-permute-start(f32[3,8,256]{2,1,0:T(8,128)S(1)} %get-tuple-element.454), channel_id=1, source_target_pairs={{4,0},{8,4},{12,8},{16,12},{20,16},{24,20},{28,24},{5,1},{9,5},{13... | collective-permute-start | bytes 73736 | tf_op jit(solution)/shard_map/ppermute | solution.py:23
  83.4 8.3 %collective-permute-start.6 = (f32[3,144,8]{2,1,0:T(8,128)S(1)}, f32[3,144,8]{2,1,0:T(8,128)S(1)}, u32[]{:S(2)}, u32[]{:S(2)}) collective-permute-start(f32[3,144,8]{2,1,0:T(8,128)S(1)} %get-tuple-element.451), channel_id=1, source_target_pairs={{0,1},{1,2},{2,3},{4,5},{5,6},{6,7},{8,9},{9,10},{10,11},{12,13},{... | collective-permute-start | bytes 41480 | tf_op jit(solution)/shard_map/ppermute | solution.py:20
  87.6 10.8 %collective-permute-start.7 = (f32[3,144,8]{2,1,0:T(8,128)S(1)}, f32[3,144,8]{2,1,0:T(8,128)S(1)}, u32[]{:S(2)}, u32[]{:S(2)}) collective-permute-start(f32[3,144,8]{2,1,0:T(8,128)S(1)} %get-tuple-element.450), channel_id=1, source_target_pairs={{1,0},{2,1},{3,2},{5,4},{6,5},{7,6},{9,8},{10,9},{11,10},{13,12},{... | collective-permute-start | bytes 41480 | tf_op jit(solution)/shard_map/ppermute | solution.py:23
  104.5 5.4 %collective-permute-start.13 = (f32[2,256]{1,0:T(2,128)S(1)}, f32[2,256]{1,0:T(2,128)S(1)}, u32[]{:S(2)}, u32[]{:S(2)}) collective-permute-start(f32[2,256]{1,0:T(2,128)S(1)} %get-tuple-element.487), channel_id=1, source_target_pairs={{4,0},{8,4},{12,8},{16,12},{20,16},{24,20},{28,24},{5,1},{9,5},{13... | collective-permute-start | bytes 6152 | tf_op jit(solution)/shard_map/ppermute | solution.py:23
  105.8 4.8 %collective-permute-start.12 = (f32[2,256]{1,0:T(2,128)S(1)}, f32[2,256]{1,0:T(2,128)S(1)}, u32[]{:S(2)}, u32[]{:S(2)}) collective-permute-start(f32[2,256]{1,0:T(2,128)S(1)} %get-tuple-element.486), channel_id=1, source_target_pairs={{0,4},{4,8},{8,12},{12,16},{16,20},{20,24},{24,28},{1,5},{5,9},{9,... | collective-permute-start | bytes 6152 | tf_op jit(solution)/shard_map/ppermute | solution.py:20
  110.7 11.3 %collective-permute-start.14 = (f32[132,2]{1,0:T(8,128)S(1)}, f32[132,2]{1,0:T(8,128)S(1)}, u32[]{:S(2)}, u32[]{:S(2)}) collective-permute-start(f32[132,2]{1,0:T(8,128)S(1)} %get-tuple-element.477), channel_id=1, source_target_pairs={{0,1},{1,2},{2,3},{4,5},{5,6},{6,7},{8,9},{9,10},{10,11},{12,13},{... | collective-permute-start | bytes 3176 | tf_op jit(solution)/shard_map/ppermute | solution.py:20
  114.1 7.9 %collective-permute-start.15 = (f32[132,2]{1,0:T(8,128)S(1)}, f32[132,2]{1,0:T(8,128)S(1)}, u32[]{:S(2)}, u32[]{:S(2)}) collective-permute-start(f32[132,2]{1,0:T(8,128)S(1)} %get-tuple-element.476), channel_id=1, source_target_pairs={{1,0},{2,1},{3,2},{5,4},{6,5},{7,6},{9,8},{10,9},{11,10},{13,12},{... | collective-permute-start | bytes 3176 | tf_op jit(solution)/shard_map/ppermute | solution.py:23
  115.5 6.8 %collective-permute-start.11 = (f32[130,1]{1,0:T(8,128)S(1)}, f32[130,1]{1,0:T(8,128)S(1)}, u32[]{:S(2)}, u32[]{:S(2)}) collective-permute-start(f32[130,1]{1,0:T(8,128)S(1)} %get-tuple-element.475), channel_id=1, source_target_pairs={{1,0},{2,1},{3,2},{5,4},{6,5},{7,6},{9,8},{10,9},{11,10},{13,12},{... | collective-permute-start | bytes 1568 | tf_op jit(solution)/shard_map/ppermute | solution.py:23
  116.8 7.1 %collective-permute-start.10 = (f32[130,1]{1,0:T(8,128)S(1)}, f32[130,1]{1,0:T(8,128)S(1)}, u32[]{:S(2)}, u32[]{:S(2)}) collective-permute-start(f32[130,1]{1,0:T(8,128)S(1)} %get-tuple-element.474), channel_id=1, source_target_pairs={{0,1},{1,2},{2,3},{4,5},{5,6},{6,7},{8,9},{9,10},{10,11},{12,13},{... | collective-permute-start | bytes 1568 | tf_op jit(solution)/shard_map/ppermute | solution.py:20
  172.9 4.3 %collective-permute-start.17 = (f32[8,256]{1,0:T(8,128)S(1)}, f32[8,256]{1,0:T(8,128)S(1)}, u32[]{:S(2)}, u32[]{:S(2)}) collective-permute-start(f32[8,256]{1,0:T(8,128)S(1)} %get-tuple-element.481), channel_id=1, source_target_pairs={{4,0},{8,4},{12,8},{16,12},{20,16},{24,20},{28,24},{5,1},{9,5},{13... | collective-permute-start | bytes 24584 | tf_op jit(solution)/shard_map/ppermute | solution.py:23
  174.2 3.8 %collective-permute-start.16 = (f32[8,256]{1,0:T(8,128)S(1)}, f32[8,256]{1,0:T(8,128)S(1)}, u32[]{:S(2)}, u32[]{:S(2)}) collective-permute-start(f32[8,256]{1,0:T(8,128)S(1)} %get-tuple-element.480), channel_id=1, source_target_pairs={{0,4},{4,8},{8,12},{12,16},{16,20},{20,24},{24,28},{1,5},{5,9},{9,... | collective-permute-start | bytes 24584 | tf_op jit(solution)/shard_map/ppermute | solution.py:20
  178.1 6.8 %collective-permute-start.18 = (f32[144,8]{1,0:T(8,128)S(1)}, f32[144,8]{1,0:T(8,128)S(1)}, u32[]{:S(2)}, u32[]{:S(2)}) collective-permute-start(f32[144,8]{1,0:T(8,128)S(1)} %get-tuple-element.464), channel_id=1, source_target_pairs={{0,1},{1,2},{2,3},{4,5},{5,6},{6,7},{8,9},{9,10},{10,11},{12,13},{... | collective-permute-start | bytes 13832 | tf_op jit(solution)/shard_map/ppermute | solution.py:20
  182.3 6.7 %collective-permute-start.19 = (f32[144,8]{1,0:T(8,128)S(1)}, f32[144,8]{1,0:T(8,128)S(1)}, u32[]{:S(2)}, u32[]{:S(2)}) collective-permute-start(f32[144,8]{1,0:T(8,128)S(1)} %get-tuple-element.465), channel_id=1, source_target_pairs={{1,0},{2,1},{3,2},{5,4},{6,5},{7,6},{9,8},{10,9},{11,10},{13,12},{... | collective-permute-start | bytes 13832 | tf_op jit(solution)/shard_map/ppermute | solution.py:23
  201.3 49.9 %collective-permute-start.20 = (f32[3,8,256]{2,1,0:T(8,128)S(1)}, f32[3,8,256]{2,1,0:T(8,128)S(1)}, u32[]{:S(2)}, u32[]{:S(2)}) collective-permute-start(f32[3,8,256]{2,1,0:T(8,128)S(1)} %get-tuple-element.453), channel_id=1, source_target_pairs={{0,4},{4,8},{8,12},{12,16},{16,20},{20,24},{24,28},{1,5},{5,9},{9,... | collective-permute-start | bytes 73736 | tf_op jit(solution)/shard_map/ppermute | solution.py:20
  203.0 48.2 %collective-permute-start.21 = (f32[3,8,256]{2,1,0:T(8,128)S(1)}, f32[3,8,256]{2,1,0:T(8,128)S(1)}, u32[]{:S(2)}, u32[]{:S(2)}) collective-permute-start(f32[3,8,256]{2,1,0:T(8,128)S(1)} %get-tuple-element.452), channel_id=1, source_target_pairs={{4,0},{8,4},{12,8},{16,12},{20,16},{24,20},{28,24},{5,1},{9,5},{13... | collective-permute-start | bytes 73736 | tf_op jit(solution)/shard_map/ppermute | solution.py:23
  251.4 8.8 %collective-permute-start.22 = (f32[3,144,8]{2,1,0:T(8,128)S(1)}, f32[3,144,8]{2,1,0:T(8,128)S(1)}, u32[]{:S(2)}, u32[]{:S(2)}) collective-permute-start(f32[3,144,8]{2,1,0:T(8,128)S(1)} %get-tuple-element.449), channel_id=1, source_target_pairs={{0,1},{1,2},{2,3},{4,5},{5,6},{6,7},{8,9},{9,10},{10,11},{12,13},{... | collective-permute-start | bytes 41480 | tf_op jit(solution)/shard_map/ppermute | solution.py:20
  255.6 11.2 %collective-permute-start.23 = (f32[3,144,8]{2,1,0:T(8,128)S(1)}, f32[3,144,8]{2,1,0:T(8,128)S(1)}, u32[]{:S(2)}, u32[]{:S(2)}) collective-permute-start(f32[3,144,8]{2,1,0:T(8,128)S(1)} %get-tuple-element.448), channel_id=1, source_target_pairs={{1,0},{2,1},{3,2},{5,4},{6,5},{7,6},{9,8},{10,9},{11,10},{13,12},{... | collective-permute-start | bytes 41480 | tf_op jit(solution)/shard_map/ppermute | solution.py:23
  272.8 4.3 %collective-permute-start.25 = (f32[2,256]{1,0:T(2,128)S(1)}, f32[2,256]{1,0:T(2,128)S(1)}, u32[]{:S(2)}, u32[]{:S(2)}) collective-permute-start(f32[2,256]{1,0:T(2,128)S(1)} %get-tuple-element.479), channel_id=1, source_target_pairs={{4,0},{8,4},{12,8},{16,12},{20,16},{24,20},{28,24},{5,1},{9,5},{13... | collective-permute-start | bytes 6152 | tf_op jit(solution)/shard_map/ppermute | solution.py:23
  274.1 3.8 %collective-permute-start.24 = (f32[2,256]{1,0:T(2,128)S(1)}, f32[2,256]{1,0:T(2,128)S(1)}, u32[]{:S(2)}, u32[]{:S(2)}) collective-permute-start(f32[2,256]{1,0:T(2,128)S(1)} %get-tuple-element.478), channel_id=1, source_target_pairs={{0,4},{4,8},{8,12},{12,16},{16,20},{20,24},{24,28},{1,5},{5,9},{9,... | collective-permute-start | bytes 6152 | tf_op jit(solution)/shard_map/ppermute | solution.py:20
  278.1 4.9 %collective-permute-start.26 = (f32[132,2]{1,0:T(8,128)S(1)}, f32[132,2]{1,0:T(8,128)S(1)}, u32[]{:S(2)}, u32[]{:S(2)}) collective-permute-start(f32[132,2]{1,0:T(8,128)S(1)} %get-tuple-element.473), channel_id=1, source_target_pairs={{0,1},{1,2},{2,3},{4,5},{5,6},{6,7},{8,9},{9,10},{10,11},{12,13},{... | collective-permute-start | bytes 3176 | tf_op jit(solution)/shard_map/ppermute | solution.py:20
  281.1 6.2 %collective-permute-start.27 = (f32[132,2]{1,0:T(8,128)S(1)}, f32[132,2]{1,0:T(8,128)S(1)}, u32[]{:S(2)}, u32[]{:S(2)}) collective-permute-start(f32[132,2]{1,0:T(8,128)S(1)} %get-tuple-element.472), channel_id=1, source_target_pairs={{1,0},{2,1},{3,2},{5,4},{6,5},{7,6},{9,8},{10,9},{11,10},{13,12},{... | collective-permute-start | bytes 3176 | tf_op jit(solution)/shard_map/ppermute | solution.py:23
where the time goes:
time: 333 us; the launch traced here: 331 us
  blocking collectives  172 us (52%)
  starting transfers between devices  67 us (20%)
  waiting for transfers between devices  34.2 us (10%)
  other arithmetic  19.8 us (6%)
  local copies, waits for them, and re-layouts  19.2 us (6%)
  matrix products  13.4 us (4%)
  between operations  5.41 us (2%)
    psum x3, blocking collectives, body(): whole, local_norm = lax.psum((placed, contribution), ('row', 'col'))  132 us
    ppermute x14, starting transfers between devices, extended_2(): lax.ppermute(lax.slice_in_dim(block, block.shape[dim] - width, None, axis...  48.8 us
    psum x1, blocking collectives, global_total(): return lax.psum(value, ('row', 'col'))  40.4 us
    ppermute x14, waiting for transfers between devices, extended_2(): lax.ppermute(lax.slice_in_dim(block, 0, width, axis=dim), axis, backward)  22.6 us
    ppermute x14, starting transfers between devices, extended_2(): lax.ppermute(lax.slice_in_dim(block, 0, width, axis=dim), axis, backward)  18.2 us
    ppermute x14, waiting for transfers between devices, extended_2(): lax.ppermute(lax.slice_in_dim(block, block.shape[dim] - width, None, axis...  11.5 us
    another operation x11, other arithmetic  9.15 us
  transfers between devices with their start and end apart: 28, of which 14 were waited for; matrix products, arithmetic and copies ran while one was open for 9% of the time, Pallas kernels for 0%

commit v1 on v0

v1 whole, which is shorter than its diff:
```python
import functools

import jax
import jax.numpy as jnp
import numpy as np
from jax import lax
from jax.experimental import pallas as pl
from jax.experimental.pallas import tpu as pltpu
from jax.sharding import PartitionSpec as P

SUB = 128
OV = 8
EXT = SUB + 2 * OV
DAMP = 2.0**-28
SHRINK = 2.0**-20

TR, TC = 128, 256
FR, FC = 160, 384
SPEC = 192

highest = lax.Precision.HIGHEST


def sine(count):
    k = np.arange(1, count + 1, dtype=np.float64)
    basis = np.sqrt(2.0 / (count + 1.0)) * np.sin(np.pi * k[:, None] * k[None, :] / (count + 1.0))
    return basis, 2.0 - 2.0 * np.cos(np.pi * k / (count + 1.0))


def block_constants():
    basis, eig = sine(EXT)
    rows = np.zeros((FR, EXT))
    cols = np.zeros((FC, 2 * SPEC))
    for at in range(EXT):
        rows[(at - OV) % FR] = basis[at]
        for b in range(2):
            cols[(b * SUB + at - OV) % FC, b * SPEC : b * SPEC + EXT] = basis[at]
    scale = np.ones((EXT, 2 * SPEC))
    for b in range(2):
        scale[:, b * SPEC : b * SPEC + EXT] = (eig[:, None] + eig[None, :]) ** 2
    f32 = lambda x: np.ascontiguousarray(x, dtype=np.float32)
    return f32(rows), f32(rows.T), f32(cols), f32(cols.T), f32(scale)


def coarse_inverse(nr, nc, width):
    br, er = sine(nr)
    bc, ec = sine(nc)
    both = np.kron(br, bc)
    scale = (er[:, None] + ec[None, :]) / (SUB * SUB)
    values = (SUB * SUB * (DAMP + scale * scale)).reshape(-1)
    whole = np.zeros((width, width), np.float32)
    whole[: nr * nc, : nr * nc] = (both / values) @ both.T
    return whole


def dot(a, b):
    return lax.dot_general(
        a, b, (((1,), (0,)), ((), ())), precision=highest, preferred_element_type=jnp.float32
    )


def lap(x):
    rows, lanes = x.shape
    beside = pltpu.roll(x, 1, 0) + pltpu.roll(x, rows - 1, 0)
    beside = beside + (pltpu.roll(x, 1, 1) + pltpu.roll(x, lanes - 1, 1))
    return 4.0 * x - beside


def lanes_of(shape):
    return lax.broadcasted_iota(jnp.int32, shape, 1)


def rows_of(shape):
    return lax.broadcasted_iota(jnp.int32, shape, 0)


def total(x):
    return jnp.sum(jnp.sum(x, axis=0, keepdims=True), axis=1, keepdims=True)


def place():
    return lax.axis_index("row"), lax.axis_index("col")


def is_even(index):
    return lax.rem(index, 2) == 0


def grid_mask(shape, counts):
    i, j = place()
    rr, ll = rows_of(shape), lanes_of(shape)
    below = jnp.where(i < counts[0] - 1, 144, 128)
    above = jnp.where(i > 0, 144, 160)
    right = jnp.where(j < counts[1] - 1, 320, 256)
    left = jnp.where(j > 0, 320, 384)
    return ((rr < below) | (rr >= above)) & ((ll < right) | (ll >= left))


def table_at(values, counts):
    i, j = place()
    first = i * (2 * counts[1]) + 2 * j
    flat = rows_of((8, 128)) * 128 + lanes_of((8, 128))
    return jnp.where(flat == first, values[0], 0.0) + jnp.where(flat == first + 1, values[1], 0.0)


def as_row(table, width):
    return jnp.concatenate([table[k : k + 1] for k in range(width // 128)], axis=1)


def coarse_values(c_row, inverse):
    return dot(jnp.broadcast_to(c_row, (8, c_row.shape[1])), inverse)[:1]


def spread(g_row, counts):
    i, j = place()
    nr, nc = counts[0], 2 * counts[1]
    shape = (16, g_row.shape[1])
    which = rows_of(shape)
    r = i - 1 + which // 4
    c = 2 * j - 1 + which % 4
    inside = (r >= 0) & (r < nr) & (c >= 0) & (c < nc) & (which < 12)
    picked = jnp.where(inside & (lanes_of(shape) == r * nc + c), g_row, 0.0)
    picked = jnp.sum(picked, axis=1, keepdims=True)
    lane = lanes_of((1, 128))
    bands = []
    for d in range(3):
        left, first, second, right = (picked[4 * d + k : 4 * d + k + 1] for k in range(4))
        bands.append(
            jnp.concatenate(
                [
                    jnp.broadcast_to(first, (1, 128)),
                    jnp.broadcast_to(second, (1, 128)),
                    jnp.where(lane < 64, right, left),
                ],
                axis=1,
            )
        )
    return jnp.concatenate(
        [
            jnp.broadcast_to(bands[1], (128, FC)),
            jnp.broadcast_to(bands[2], (16, FC)),
            jnp.broadcast_to(bands[0], (16, FC)),
        ],
        axis=0,
    )


def local_solve(w, means, rows, rows_t, cols, cols_t, scale):
    lane = lanes_of((1, 2 * SPEC))
    mean = jnp.where(lane < SPEC, means[0], means[1])
    t = dot(dot(rows_t, w), cols)
    t = t / (DAMP + mean * scale)
    return dot(rows, dot(t, cols_t))


def core_sums(x):
    return [total(x[:, :128]), total(x[:, 128:256])]


def pack_columns(y):
    lane = lanes_of((FR, 128))
    packed = jnp.where(
        lane < 16,
        y[:, :128],
        jnp.where(lane >= 112, y[:, 128:256], pltpu.roll(y[:, 256:], 64, 1)),
    )
    turned = packed.T
    to_left = jnp.concatenate([turned[56:64], turned[:16]], axis=0)
    to_right = jnp.concatenate([turned[112:], turned[64:72]], axis=0)
    return to_left, to_right


def add_columns(y, from_left, from_right):
    turned = jnp.concatenate(
        [
            from_right[8:24],
            jnp.zeros((40, FR), jnp.float32),
            from_right[:8],
            from_left[16:24],
            jnp.zeros((40, FR), jnp.float32),
            from_left[:16],
        ],
        axis=0,
    )
    back = turned.T
    lane = lanes_of((FR, 128))
    rolled = pltpu.roll(back, 64, 1)
    first = y[:, :128] + jnp.where(lane < 8, rolled, 0.0)
    second = y[:, 128:256] + jnp.where(lane >= 120, rolled, 0.0)
    third = y[:, 256:] + jnp.where((lane < 16) | (lane >= 112), back, 0.0)
    return jnp.concatenate([first, second, third], axis=1)


def pack_rows(y):
    return jnp.concatenate([y[152:160], y[:16]], axis=0), y[112:136]


def add_rows(y, from_above, from_below):
    return jnp.concatenate(
        [
            y[:8] + from_above[16:24],
            y[8:120],
            y[120:144] + from_below,
            y[144:] + from_above[:16],
        ],
        axis=0,
    )


def begin_kernel(counts, r_ref, h_ref, a_ref, b_ref):
    j = lax.axis_index("col")
    even = is_even(j)
    r, h = r_ref[...], h_ref[...]
    lane = lanes_of((128, 128))
    packed = jnp.where(
        lane < 16,
        r[:, :128],
        jnp.where(
            lane < 64,
            pltpu.roll(h[:, :128], 16, 1),
            jnp.where(lane < 112, pltpu.roll(h[:, 128:], 112, 1), r[:, 128:]),
        ),
    )
    turned = packed.T
    left, right = turned[:32], turned[96:]
    table = table_at(core_sums(r), counts)
    a_ref[:32] = jnp.where(even, right, left)
    a_ref[32:] = table
    b_ref[:32] = jnp.where(even, left, right)
    b_ref[32:] = table


def widen_kernel(counts, r_ref, h_ref, ga_ref, gb_ref, tb_ref, r3_ref, h3_ref, a_ref, b_ref):
    i, j = place()
    even = is_even(j)
    ga, gb = ga_ref[:32], gb_ref[:32]
    from_right = jnp.where(even, ga, gb)
    from_left = jnp.where(even, gb, ga)
    turned = jnp.concatenate([from_right, jnp.zeros((64, 128), jnp.float32), from_left], axis=0)
    back = turned.T
    lane = lanes_of((128, 128))
    edge = (lane < 16) | (lane >= 112)
    r3 = jnp.where(edge, back, 0.0)
    h3 = jnp.where(
        lane < 16, pltpu.roll(back, 112, 1), jnp.where(lane >= 112, pltpu.roll(back, 16, 1), 0.0)
    )
    r3_ref[...] = r3
    h3_ref[...] = h3
    table = tb_ref[32:] + gb_ref[32:]
    r, h = r_ref[...], h_ref[...]
    even = is_even(i)
    top = [jnp.concatenate([r[:8], r3[:8]], axis=1), jnp.concatenate([h[:16], h3[:16]], axis=1)]
    low = [
        jnp.concatenate([r[120:], r3[120:]], axis=1),
        jnp.concatenate([h[112:], h3[112:]], axis=1),
    ]
    wide = jnp.concatenate([table, jnp.zeros((8, FC - 128), jnp.float32)], axis=1)
    a_ref[:8] = jnp.where(even, low[0], top[0])
    a_ref[8:24] = jnp.where(even, low[1], top[1])
    a_ref[24:] = wide
    b_ref[:8] = jnp.where(even, top[0], low[0])
    b_ref[8:24] = jnp.where(even, top[1], low[1])
    b_ref[24:] = wide


def first_kernel(
    counts,
    r_ref,
    h_ref,
    r3_ref,
    h3_ref,
    ga_ref,
    gb_ref,
    rows_ref,
    rows_t_ref,
    cols_ref,
    cols_t_ref,
    scale_ref,
    y_ref,
    m_ref,
    a_ref,
    b_ref,
):
    i, j = place()
    even = is_even(i)
    ga, gb = ga_ref[:24], gb_ref[:24]
    below = jnp.where(even, ga, gb)
    above = jnp.where(even, gb, ga)
    r = jnp.concatenate([r_ref[...], r3_ref[...]], axis=1)
    h = jnp.concatenate([h_ref[...], h3_ref[...]], axis=1)
    wide = jnp.concatenate([r, below[:8], jnp.zeros((16, FC), jnp.float32), above[:8]], axis=0)
    tall = jnp.concatenate([h, below[8:], above[8:]], axis=0)
    mobility = tall * tall * tall
    m_ref[...] = mobility
    means = [x / (SUB * SUB) for x in core_sums(mobility[:128])]
    y = local_solve(
        wide,
        means,
        rows_ref[...],
        rows_t_ref[...],
        cols_ref[...],
        cols_t_ref[...],
        scale_ref[...],
    )
    y_ref[...] = y
    to_left, to_right = pack_columns(y)
    even = is_even(j)
    a_ref[...] = jnp.where(even, to_right, to_left)
    b_ref[...] = jnp.where(even, to_left, to_right)


def columns_kernel(with_table, *refs):
    if with_table:
        y_ref, ga_ref, gb_ref, t_ref, gt_ref, out_ref, a_ref, b_ref, t_out = refs
    else:
        y_ref, ga_ref, gb_ref, out_ref, a_ref, b_ref = refs
    i, j = place()
    even = is_even(j)
    ga, gb = ga_ref[...], gb_ref[...]
    y = add_columns(y_ref[...], jnp.where(even, gb, ga), jnp.where(even, ga, gb))
    out_ref[...] = y
    to_above, to_below = pack_rows(y)
    even = is_even(i)
    a_ref[:24] = jnp.where(even, to_below, to_above)
    b_ref[...] = jnp.where(even, to_above, to_below)
    if with_table:
        inner = (lax.rem(j, 4) == 1) | (lax.rem(j, 4) == 2)
        table = jnp.where(inner, t_ref[...], gt_ref[...])
        t_out[...] = table
        a_ref[24:] = jnp.concatenate([table, jnp.zeros((8, FC - 128), jnp.float32)], axis=1)


def second_kernel(
    counts,
    width,
    y_ref,
    m_ref,
    ga_ref,
    gb_ref,
    t_ref,
    r_ref,
    inverse_ref,
    rows_ref,
    rows_t_ref,
    cols_ref,
    cols_t_ref,
    scale_ref,
    z_ref,
    w_ref,
    y2_ref,
    stats_ref,
    t_out,
    a_ref,
    b_ref,
):
    i, j = place()
    even = is_even(i)
    ga, gb = ga_ref[:24], gb_ref[...]
    s = add_rows(y_ref[...], jnp.where(even, gb, ga), jnp.where(even, ga, gb))
    mask = grid_mask((FR, FC), counts)
    s = jnp.where(mask, s, 0.0)
    inner = (lax.rem(i, 4) == 1) | (lax.rem(i, 4) == 2)
    table = jnp.where(inner, t_ref[...], ga_ref[24:, :128])
    t_out[...] = table
    coarse = spread(coarse_values(as_row(table, width), inverse_ref[...]), counts)
    mobility = m_ref[...]
    flow = mobility * (lap(s) + lap(coarse))
    z = s + coarse
    w = jnp.where(mask, DAMP * z + lap(flow), 0.0) * SHRINK
    zt, wt, rt, mt = z[:128, :256], w[:128, :256], r_ref[...], mobility[:128, :256]
    z_ref[...] = zt
    w_ref[...] = wt
    means = [x / (SUB * SUB) for x in core_sums(mt)]
    y = local_solve(
        w,
        means,
        rows_ref[...],
        rows_t_ref[...],
        cols_ref[...],
        cols_t_ref[...],
        scale_ref[...],
    )
    y2_ref[...] = y
    to_left, to_right = pack_columns(y)
    even = is_even(j)
    a_ref[...] = jnp.where(even, to_right, to_left)
    b_ref[...] = jnp.where(even, to_left, to_right)
    rz, zw = total(rt * zt), total(zt * wt)
    c1 = core_sums(wt)
    lane, row = lanes_of((1, 256)), rows_of((128, 1))
    along = (lane % 128 != 0) & (lane % 128 != 127)
    top, low = mt[:1], mt[127:]
    side = jnp.sum(jnp.where((row > 0) & (row < 127), mt, 0.0), axis=0, keepdims=True)

    def halves(x):
        return [
            jnp.sum(x[:, :128], axis=1, keepdims=True),
            jnp.sum(x[:, 128:], axis=1, keepdims=True),
        ]

    first, last = lane % 128 == 0, lane % 128 == 127
    zero = jnp.zeros((1, 1), jnp.float32)
    values = [
        [rz, zero],
        [zw, zero],
        c1,
        halves(jnp.where(along, top, 0.0)),
        halves(jnp.where(along, low, 0.0)),
        halves(jnp.where(first, side, 0.0)),
        halves(jnp.where(last, side, 0.0)),
        halves(jnp.where(first, top, 0.0)),
        halves(jnp.where(last, top, 0.0)),
        halves(jnp.where(first, low, 0.0)),
        halves(jnp.where(last, low, 0.0)),
    ]
    for k, pair in enumerate(values):
        stats_ref[k] = table_at(pair, counts)


def dots_kernel(
    counts, y_ref, m_ref, ga_ref, gb_ref, r_ref, w_ref, stats_ref, q_ref, v_ref, stats_out
):
    i, j = place()
    even = is_even(i)
    ga, gb = ga_ref[...], gb_ref[...]
    q = add_rows(y_ref[...], jnp.where(even, gb, ga), jnp.where(even, ga, gb))
    q = jnp.where(grid_mask((FR, FC), counts), q, 0.0)
    v = DAMP * q + lap(m_ref[...] * lap(q))
    qt, vt = q[:128, :256], v[:128, :256]
    q_ref[...] = qt
    v_ref[...] = vt
    zero = jnp.zeros((1, 1), jnp.float32)
    stats_out[:11] = stats_ref[:11]
    values = [
        core_sums(vt),
        [total(r_ref[...] * qt), zero],
        [total(w_ref[...] * qt), zero],
        [total(vt * qt), zero],
    ]
    for k, pair in enumerate(values):
        stats_out[11 + k] = table_at(pair, counts)
    stats_out[15] = jnp.zeros((8, 128), jnp.float32)


def end_kernel(
    counts,
    width,
    stats_ref,
    t_ref,
    inverse_ref,
    m_ref,
    r_ref,
    z_ref,
    w_ref,
    q_ref,
    v_ref,
    solution_ref,
    residual_ref,
):
    nc = 2 * counts[1]
    st = [as_row(stats_ref[k], width) for k in range(15)]

    def whole(x):
        return jnp.sum(x, axis=1, keepdims=True)

    rz, zw, rq, wq, qv = (whole(st[k]) for k in (0, 1, 12, 13, 14))
    c0, c1, sums_v = as_row(t_ref[...], width), st[2], st[11]
    g = coarse_values(c1, inverse_ref[...])
    lane = lanes_of((1, width))
    cell = lane < counts[0] * nc
    column = lane % nc
    up = jnp.where(lane >= nc, pltpu.roll(g, nc, 1), 0.0)
    down = jnp.where(lane < (counts[0] - 1) * nc, pltpu.roll(g, width - nc, 1), 0.0)
    left = jnp.where(column > 0, pltpu.roll(g, 1, 1), 0.0)
    right = jnp.where(column < nc - 1, pltpu.roll(g, width - 1, 1), 0.0)
    du, dd, dl, dr = g - up, g - down, g - left, g - right
    energy = DAMP * SUB * SUB * g * g
    energy = energy + st[3] * du * du + st[4] * dd * dd + st[5] * dl * dl + st[6] * dr * dr
    for weight, p, q in ((st[7], du, dl), (st[8], du, dr), (st[9], dd, dl), (st[10], dd, dr)):
        both = p + q
        energy = energy + weight * both * both
    ry = rq + whole(g * c0)
    yw = wq + whole(g * c1)
    yv = qv + whole(jnp.where(cell, 2.0 * g * sums_v + energy, 0.0))
    a = rz / zw
    rz1 = rz - a * ry - a * zw + a * a * yw
    beta1 = 1.0 + rz1 / rz
    dad = (beta1 * beta1 * zw - 2.0 * a * beta1 * yw) * (1.0 / SHRINK) + a * a * yv
    a1 = rz1 / dad
    coarse = spread(g, counts)
    y = q_ref[...] + coarse[:128, :256]
    image = DAMP * coarse + lap(m_ref[...] * lap(coarse))
    v = v_ref[...] + image[:128, :256]
    z, w = z_ref[...], w_ref[...]
    solution_ref[...] = (a * SHRINK) * z + a1 * (beta1 * z - a * y)
    residual_ref[...] = r_ref[...] - a * w - a1 * ((beta1 * (1.0 / SHRINK)) * w - a * v)


def call(kernel, outs, *args):
    shapes = [jax.ShapeDtypeStruct(s, jnp.float32) for s in outs]
    return pl.pallas_call(
        kernel,
        out_shape=shapes,
        compiler_params=pltpu.CompilerParams(vmem_limit_bytes=48 * 1024 * 1024),
    )(*args)


def swaps(count, offset):
    pairs = []
    for k in range(offset, count - 1, 2):
        pairs += [(k, k + 1), (k + 1, k)]
    return pairs


def across(count, bit):
    return [(k, k ^ bit) for k in range(count)]


def body(counts, height, noise):
    nr, nc = counts
    width = max(128, nr * nc * 2)
    rows, rows_t, cols, cols_t, scale = (jnp.asarray(x) for x in block_constants())
    inverse = jnp.asarray(coarse_inverse(nr, 2 * nc, width))
    basis = (rows, rows_t, cols, cols_t, scale)

    def swap_a(x, axis, count):
        return lax.ppermute(x, axis, swaps(count, 0))

    def swap_b(x, axis, count):
        return lax.ppermute(x, axis, swaps(count, 1))

    a, b = call(functools.partial(begin_kernel, counts), [(40, 128)] * 2, noise, height)
    ga = swap_a(a, "col", nc)
    b = b.at[32:].add(ga[32:])
    gb = swap_b(b, "col", nc)
    r3, h3, a, b = call(
        functools.partial(widen_kernel, counts),
        [(128, 128)] * 2 + [(32, FC)] * 2,
        noise,
        height,
        ga,
        gb,
        b,
    )
    ga = swap_a(a, "row", nr)
    b = b.at[24:].add(ga[24:])
    gb = swap_b(b, "row", nr)
    table = b[24:, :128] + gb[24:, :128]
    y, m, a, b = call(
        functools.partial(first_kernel, counts),
        [(FR, FC)] * 2 + [(24, FR)] * 2,
        noise,
        height,
        r3,
        h3,
        ga,
        gb,
        *basis,
    )
    for axis, count in (("row", nr), ("col", nc)):
        bit = 4
        while bit < count:
            table = table + lax.ppermute(table, axis, across(count, bit))
            bit *= 2
    whole_a = jnp.concatenate([a, jnp.pad(table, ((0, 0), (0, FR - 128)))], axis=0)
    ga = swap_a(whole_a, "col", nc)
    gb = swap_b(b, "col", nc)
    y, a, b, table = call(
        functools.partial(columns_kernel, True),
        [(FR, FC), (32, FC), (24, FC), (8, 128)],
        y,
        ga[:24],
        gb,
        table,
        ga[24:, :128],
    )
    ga = swap_a(a, "row", nr)
    gb = swap_b(b, "row", nr)
    z, w, y, stats, table, a, b = call(
        functools.partial(second_kernel, counts, width),
        [(TR, TC)] * 2 + [(FR, FC), (11, 8, 128), (8, 128)] + [(24, FR)] * 2,
        y,
        m,
        ga,
        gb,
        table,
        noise,
        inverse,
        *basis,
    )
    ga = swap_a(a, "col", nc)
    gb = swap_b(b, "col", nc)
    y, a, b = call(
        functools.partial(columns_kernel, False), [(FR, FC), (24, FC), (24, FC)], y, ga, gb
    )
    ga = swap_a(a, "row", nr)
    gb = swap_b(b, "row", nr)
    q, v, stats = call(
        functools.partial(dots_kernel, counts),
        [(TR, TC)] * 2 + [(16, 8, 128)],
        y,
        m,
        ga,
        gb,
        noise,
        w,
        stats,
    )
    used = width // 128
    stats = stats[:, :used]
    for axis, count in (("row", nr), ("col", nc)):
        bit = 1
        while bit < count:
            stats = stats + lax.ppermute(stats, axis, across(count, bit))
            bit *= 2
    return tuple(
        call(
            functools.partial(end_kernel, counts, width),
            [(TR, TC)] * 2,
            stats,
            table,
            inverse,
            m,
            noise,
            z,
            w,
            q,
            v,
        )
    )


def solution(mesh):
    counts = (mesh.shape["row"], mesh.shape["col"])
    spec = P("row", "col")
    return jax.shard_map(
        functools.partial(body, counts),
        mesh=mesh,
        in_specs=(spec, spec),
        out_specs=(spec, spec),
        check_vma=False,
    )
```

time: 333 us -> 75.6 us (0.23)
  blocking collectives: 172 us -> 0 us
  starting transfers between devices: 67 us -> 46.7 us
  other arithmetic: 19.8 us -> 0.07 us
  waiting for transfers between devices: 34.2 us -> 14.6 us
  local copies, waits for them, and re-layouts: 19.2 us -> 5.66 us
  matrix products: 13.4 us -> 0 us
  Pallas kernels: 0 us -> 7.27 us
  between operations: 5.41 us -> 0.88 us
    psum x4 -> x0, blocking collectives: 172 us -> none  [the longest x3 132 us: body(): whole, local_norm = lax.psum((placed, contribution), ('row', 'col'))]
    ppermute x28 -> x18, starting transfers between devices: 67 us -> 46.7 us  [the longest x6 19.1 us: swap_a(): return lax.ppermute(x, axis, swaps(count, 0))]
    ppermute x28 -> x18, waiting for transfers between devices: 34.2 us -> 14.6 us  [the longest x5 8.49 us: body(): stats = stats + lax.ppermute(stats, axis, across(count, bit))]
    dot_general x16 -> x0, matrix products: 13.4 us -> none  [the longest x4 5.08 us: eigen_solve(): jnp.einsum('ba,nbc,cd->nad', basis, blocks, basis, precision=highest)]
    another operation x17 -> x0, other arithmetic: 13.4 us -> none
    scatter-add x14 -> x0, local copies, waits for them, and re-layouts: 9.03 us -> none  [the longest x4 4.69 us: body(): result.at[:OV, :OV].add(arrived[2, :OV, :OV]).at[:OV, -OV:]]
    pallas_call x0 -> x8, Pallas kernels: none -> 7.27 us  [call(): pl.pallas_call(kernel, out_shape=shapes, compiler_params=pltpu.CompilerPa...]
    scatter x10 -> x0, local copies, waits for them, and re-layouts: 6.89 us -> none  [the longest x2 3.65 us: body(): empty.at[:OV, :OV].set(extended[:OV, :OV]).at[:OV, -OV:]]
  transfers between devices with their start and end apart: 28 -> 18, of which waited for: 14 -> 11; matrix products, arithmetic and copies ran while one was open for 9% -> 0% of each run, Pallas kernels for 0% -> 3%
where the time goes in v1:
time: 75.6 us; the launch traced here: 75.2 us
  starting transfers between devices  46.7 us (62%)
  waiting for transfers between devices  14.6 us (19%)
  Pallas kernels  7.27 us (10%)
  local copies, waits for them, and re-layouts  5.66 us (7%)
  between operations  0.88 us (1%)
    ppermute x6, starting transfers between devices, swap_a(): return lax.ppermute(x, axis, swaps(count, 0))  19.1 us
    ppermute x5, starting transfers between devices, body(): stats = stats + lax.ppermute(stats, axis, across(count, bit))  15.8 us
    ppermute x5, waiting for transfers between devices, body(): stats = stats + lax.ppermute(stats, axis, across(count, bit))  8.49 us
    ppermute x1, starting transfers between devices, body(): table = table + lax.ppermute(table, axis, across(count, bit))  7.84 us
    pallas_call x8, Pallas kernels, call(): pl.pallas_call(kernel, out_shape=shapes, compiler_params=pltpu.CompilerPa...  7.27 us
    ppermute x6, waiting for transfers between devices, swap_a(): return lax.ppermute(x, axis, swaps(count, 0))  6.1 us
    unnamed x22, local copies, waits for them, and re-layouts  5.65 us
    ppermute x6, starting transfers between devices, swap_b(): return lax.ppermute(x, axis, swaps(count, 1))  3.92 us
  transfers between devices with their start and end apart: 18, of which 11 were waited for; matrix products, arithmetic and copies ran while one was open for 0% of the time, Pallas kernels for 3%

profile of v1, /device:TPU:0, one launch (start us, length us, event | category | flops | bytes accessed | tf_op | source)
XLA Modules:
  0.0 75.2 jit_solution(2505437829509276026)
XLA Ops:
  0.6 0.0 copy-start
  0.6 0.9 %copy-done = f32[128,256]{1,0:T(8,128)S(1)} copy-done((f32[128,256]{1,0:T(8,128)S(1)}, f32[128,256]{1,0:T(8,128)}, u32[]{:S(2)}) %copy-start) | copy-done | bytes 131096
  1.5 0.9 %copy-done.4 = f32[128,256]{1,0:T(8,128)S(1)} copy-done((f32[128,256]{1,0:T(8,128)S(1)}, f32[128,256]{1,0:T(8,128)}, u32[]{:S(2)}) %copy-start.4) | copy-done | bytes 131096
  2.4 0.2 shard_map.95
  2.6 3.0 %collective-permute-start = (f32[40,128]{1,0:T(8,128)S(1)}, f32[40,128]{1,0:T(8,128)S(1)}, u32[]{:S(2)}, u32[]{:S(2)}) collective-permute-start(f32[40,128]{1,0:T(8,128)S(1)} %get-tuple-element.53), channel_id=1, source_target_pairs={{0,1},{1,0},{2,3},{3,2},{4,5},{5,4},{6,7},{7,6},{8,9},{9,8},{10,11... | collective-permute-start | bytes 61448 | tf_op jit(solution)/shard_map/ppermute | solution.py:527
  5.6 1.8 %collective-permute-done.ga_ref = f32[40,128]{1,0:T(8,128)S(1)} collective-permute-done((f32[40,128]{1,0:T(8,128)S(1)}, f32[40,128]{1,0:T(8,128)S(1)}, u32[]{:S(2)}, u32[]{:S(2)}) %collective-permute-start) | collective-permute-done | bytes 20512 | tf_op jit(solution)/shard_map/ppermute | solution.py:527
  7.4 0.7 collective-permute-start.1
  8.0 0.2 shard_map.96
  8.3 0.1 collective-permute-start.2
  8.3 1.2 %collective-permute-done.2.ga_ref = f32[32,384]{1,0:T(8,128)S(1)} collective-permute-done((f32[32,384]{1,0:T(8,128)S(1)}, f32[32,384]{1,0:T(8,128)S(1)}, u32[]{:S(2)}, u32[]{:S(2)}) %collective-permute-start.2) | collective-permute-done | bytes 49184 | tf_op jit(solution)/shard_map/ppermute | solution.py:527
  9.6 0.7 collective-permute-start.3
  10.2 0.0 collective-permute-done.3.gb_ref
  10.2 7.8 %collective-permute-start.4 = (f32[8,128]{1,0:T(8,128)S(1)}, f32[8,128]{1,0:T(8,128)S(1)}, u32[]{:S(2)}, u32[]{:S(2)}) collective-permute-start(f32[8,128]{1,0:T(8,128)S(1)} %slice_add_fusion.1), channel_id=1, source_target_pairs={{0,16},{4,20},{8,24},{12,28},{16,0},{20,4},{24,8},{28,12},{1,17},{... | collective-permute-start | bytes 12296 | tf_op jit(solution)/shard_map/ppermute | solution.py:563
  18.1 1.1 %copy-done.3 = f32[384,384]{1,0:T(8,128)S(1)} copy-done((f32[384,384]{1,0:T(8,128)S(1)}, f32[384,384]{1,0:T(8,128)}, u32[]{:S(2)}) %copy-start.3) | copy-done | bytes 589848
  19.1 0.9 %copy-done.5 = f32[144,384]{1,0:T(8,128)S(1)} copy-done((f32[144,384]{1,0:T(8,128)S(1)}, f32[144,384]{1,0:T(8,128)}, u32[]{:S(2)}) %copy-start.5) | copy-done | bytes 221208
  20.1 0.9 %copy-done.7 = f32[160,144]{1,0:T(8,128)S(1)} copy-done((f32[160,144]{1,0:T(8,128)S(1)}, f32[160,144]{1,0:T(8,128)}, u32[]{:S(2)}) %copy-start.7) | copy-done | bytes 92184
  21.0 0.9 %copy-done.9 = f32[144,160]{1,0:T(8,128)S(1)} copy-done((f32[144,160]{1,0:T(8,128)S(1)}, f32[144,160]{1,0:T(8,128)}, u32[]{:S(2)}) %copy-start.9) | copy-done | bytes 92184
  21.9 2.1 %shard_map.97 = (f32[160,384]{1,0:T(8,128)S(1)}, f32[160,384]{1,0:T(8,128)S(1)}, f32[24,160]{1,0:T(8,128)S(1)}, f32[24,160]{1,0:T(8,128)S(1)}) custom-call(f32[128,256]{1,0:T(8,128)S(1)} %copy-done, f32[128,256]{1,0:T(8,128)S(1)} %copy-done.4, f32[128,128]{1,0:T(8,128)S(1)} %get-tuple-element.55.r3_ref, f32[128,128]{1,0:T(8,128)S(1)} %get-tuple-element.56.h3_ref, ...), custom_call_target="tpu_custom_call" | custom-call | tf_op jit(solution)/shard_map/pallas_call | solution.py:501
  24.0 0.0 copy-start.6
  24.0 7.4 %collective-permute-start.5 = (f32[32,160]{1,0:T(8,128)S(1)}, f32[32,160]{1,0:T(8,128)S(1)}, u32[]{:S(2)}, u32[]{:S(2)}) collective-permute-start(f32[32,160]{1,0:T(8,128)S(1)} %select_maximum_fusion), channel_id=1, source_target_pairs={{0,1},{1,0},{2,3},{3,2},{4,5},{5,4},{6,7},{7,6},{8,9},{9,8},{10,11... | collective-permute-start | bytes 61448 | tf_op jit(solution)/shard_map/ppermute | solution.py:527
  31.5 0.7 collective-permute-start.6
  32.1 1.2 %collective-permute-done.5 = f32[32,160]{1,0:T(8,128)S(1)} collective-permute-done((f32[32,160]{1,0:T(8,128)S(1)}, f32[32,160]{1,0:T(8,128)S(1)}, u32[]{:S(2)}, u32[]{:S(2)}) %collective-permute-start.5) | collective-permute-done | bytes 20512 | tf_op jit(solution)/shard_map/ppermute | solution.py:527
  33.4 0.0 copy-start.1
  33.4 0.0 copy-start.10
  33.4 0.2 shard_map.98
  33.6 0.1 collective-permute-start.7
  33.7 0.7 collective-permute-start.8
  34.4 0.5 collective-permute-done.7.ga_ref
  34.9 2.8 %shard_map.99 = (f32[128,256]{1,0:T(8,128)S(1)}, f32[128,256]{1,0:T(8,128)S(1)}, f32[160,384]{1,0:T(8,128)S(1)}, f32[11,8,128]{2,1,0:T(8,128)S(1)}, f32[8,128]{1...) custom-call(f32[160,384]{1,0:T(8,128)S(1)} %get-tuple-element.62.y_ref, ...), custom_call_target="tpu_custom_call" | custom-call | tf_op jit(solution)/shard_map/pallas_call | solution.py:501
  37.7 4.7 %collective-permute-start.9 = (f32[24,160]{1,0:T(8,128)S(1)}, f32[24,160]{1,0:T(8,128)S(1)}, u32[]{:S(2)}, u32[]{:S(2)}) collective-permute-start(f32[24,160]{1,0:T(8,128)S(1)} %get-tuple-element.68), channel_id=1, source_target_pairs={{0,1},{1,0},{2,3},{3,2},{4,5},{5,4},{6,7},{7,6},{8,9},{9,8},{10,11... | collective-permute-start | bytes 46088 | tf_op jit(solution)/shard_map/ppermute | solution.py:527
  42.4 0.7 collective-permute-start.10
  43.1 1.1 %collective-permute-done.9.refs_1_ = f32[24,160]{1,0:T(8,128)S(1)} collective-permute-done((f32[24,160]{1,0:T(8,128)S(1)}, f32[24,160]{1,0:T(8,128)S(1)}, u32[]{:S(2)}, u32[]{:S(2)}) %collective-permute-start.9) | collective-permute-done | bytes 15392 | tf_op jit(solution)/shard_map/ppermute | solution.py:527
  44.3 0.2 shard_map.100
  44.4 3.7 %collective-permute-start.11 = (f32[24,384]{1,0:T(8,128)S(1)}, f32[24,384]{1,0:T(8,128)S(1)}, u32[]{:S(2)}, u32[]{:S(2)}) collective-permute-start(f32[24,384]{1,0:T(8,128)S(1)} %get-tuple-element.71), channel_id=1, source_target_pairs={{0,4},{4,0},{8,12},{12,8},{16,20},{20,16},{24,28},{28,24},{1,5},{5... | collective-permute-start | bytes 110600 | tf_op jit(solution)/shard_map/ppermute | solution.py:527
  48.2 0.7 collective-permute-start.12
  48.8 0.2 collective-permute-done.11.ga_ref
  49.0 0.4 shard_map.101
  49.5 4.9 %collective-permute-start.13 = (f32[16,1,128]{2,1,0:T(1,128)S(1)}, f32[16,1,128]{2,1,0:T(1,128)S(1)}, u32[]{:S(2)}, u32[]{:S(2)}) collective-permute-start(f32[16,1,128]{2,1,0:T(1,128)S(1)} %slice.68), channel_id=1, source_target_pairs={{0,4},{4,0},{8,12},{12,8},{16,20},{20,16},{24,28},{28,24},{1,5},{5... | collective-permute-start | bytes 24584 | tf_op jit(solution)/shard_map/ppermute | solution.py:614
  54.4 0.8 %collective-permute-done.13 = f32[16,1,128]{2,1,0:T(1,128)S(1)} collective-permute-done((f32[16,1,128]{2,1,0:T(1,128)S(1)}, f32[16,1,128]{2,1,0:T(1,128)S(1)}, u32[]{:S(2)}, u32[]{:S(2)}) %collective-permute-start.13) | collective-permute-done | bytes 8224 | tf_op jit(solution)/shard_map/ppermute | solution.py:614
  55.3 2.2 %collective-permute-start.14 = (f32[16,1,128]{2,1,0:T(1,128)S(1)}, f32[16,1,128]{2,1,0:T(1,128)S(1)}, u32[]{:S(2)}, u32[]{:S(2)}) collective-permute-start(f32[16,1,128]{2,1,0:T(1,128)S(1)} %slice_add_fusion.3), channel_id=1, source_target_pairs={{0,8},{4,12},{8,0},{12,4},{16,24},{20,28},{24,16},{28,20},{1,9},{5... | collective-permute-start | bytes 24584 | tf_op jit(solution)/shard_map/ppermute | solution.py:614
  57.4 1.6 %collective-permute-done.14 = f32[16,1,128]{2,1,0:T(1,128)S(1)} collective-permute-done((f32[16,1,128]{2,1,0:T(1,128)S(1)}, f32[16,1,128]{2,1,0:T(1,128)S(1)}, u32[]{:S(2)}, u32[]{:S(2)}) %collective-permute-start.14) | collective-permute-done | bytes 8224 | tf_op jit(solution)/shard_map/ppermute | solution.py:614
  59.1 1.8 %collective-permute-start.15 = (f32[16,1,128]{2,1,0:T(1,128)S(1)}, f32[16,1,128]{2,1,0:T(1,128)S(1)}, u32[]{:S(2)}, u32[]{:S(2)}) collective-permute-start(f32[16,1,128]{2,1,0:T(1,128)S(1)} %add.42), channel_id=1, source_target_pairs={{0,16},{4,20},{8,24},{12,28},{16,0},{20,4},{24,8},{28,12},{1,17},{... | collective-permute-start | bytes 24584 | tf_op jit(solution)/shard_map/ppermute | solution.py:614
  60.9 2.8 %collective-permute-done.15 = f32[16,1,128]{2,1,0:T(1,128)S(1)} collective-permute-done((f32[16,1,128]{2,1,0:T(1,128)S(1)}, f32[16,1,128]{2,1,0:T(1,128)S(1)}, u32[]{:S(2)}, u32[]{:S(2)}) %collective-permute-start.15) | collective-permute-done | bytes 8224 | tf_op jit(solution)/shard_map/ppermute | solution.py:614
  63.7 4.8 %collective-permute-start.16 = (f32[16,1,128]{2,1,0:T(1,128)S(1)}, f32[16,1,128]{2,1,0:T(1,128)S(1)}, u32[]{:S(2)}, u32[]{:S(2)}) collective-permute-start(f32[16,1,128]{2,1,0:T(1,128)S(1)} %add.43), channel_id=1, source_target_pairs={{0,1},{1,0},{2,3},{3,2},{4,5},{5,4},{6,7},{7,6},{8,9},{9,8},{10,11... | collective-permute-start | bytes 24584 | tf_op jit(solution)/shard_map/ppermute | solution.py:614
  68.5 1.6 %collective-permute-done.16 = f32[16,1,128]{2,1,0:T(1,128)S(1)} collective-permute-done((f32[16,1,128]{2,1,0:T(1,128)S(1)}, f32[16,1,128]{2,1,0:T(1,128)S(1)}, u32[]{:S(2)}, u32[]{:S(2)}) %collective-permute-start.16) | collective-permute-done | bytes 8224 | tf_op jit(solution)/shard_map/ppermute | solution.py:614
  70.2 2.1 %collective-permute-start.17 = (f32[16,1,128]{2,1,0:T(1,128)S(1)}, f32[16,1,128]{2,1,0:T(1,128)S(1)}, u32[]{:S(2)}, u32[]{:S(2)}) collective-permute-start(f32[16,1,128]{2,1,0:T(1,128)S(1)} %add.44), channel_id=1, source_target_pairs={{0,2},{1,3},{2,0},{3,1},{4,6},{5,7},{6,4},{7,5},{8,10},{9,11},{10,... | collective-permute-start | bytes 24584 | tf_op jit(solution)/shard_map/ppermute | solution.py:614
  72.3 1.6 %collective-permute-done.17 = f32[16,1,128]{2,1,0:T(1,128)S(1)} collective-permute-done((f32[16,1,128]{2,1,0:T(1,128)S(1)}, f32[16,1,128]{2,1,0:T(1,128)S(1)}, u32[]{:S(2)}, u32[]{:S(2)}) %collective-permute-start.17) | collective-permute-done | bytes 8224 | tf_op jit(solution)/shard_map/ppermute | solution.py:614
  73.9 1.3 %shard_map.102 = (f32[128,256]{1,0:T(8,128)}, f32[128,256]{1,0:T(8,128)}) custom-call(f32[16,1,128]{2,1,0:T(1,128)S(1)} %add.45.stats_ref, f32[8,128]{1,0:T(8,128)S(1)} %get-tuple-element.76.t_ref, f32[128,128]{1,0:T(8,128)S(1)} %copy-done.10, f32[160,384]{1,0:T(8,128)S(1)} %get-tuple-element.63.m_ref, f32[128,256]{1,0:T(8,128)S(1)} %copy-done.1, ...), custom_call_target="tpu_custom_call" | custom-call | tf_op jit(solution)/shard_map/pallas_call | solution.py:501
  (31 shorter events, 0.1 us)
Async XLA Ops:
  0.6 0.9 %copy-start = (f32[128,256]{1,0:T(8,128)S(1)}, f32[128,256]{1,0:T(8,128)}, u32[]{:S(2)}) copy-start(f32[128,256]{1,0:T(8,128)} %r_ref.11) | copy-start | bytes 393220
  1.5 0.9 %copy-start.4 = (f32[128,256]{1,0:T(8,128)S(1)}, f32[128,256]{1,0:T(8,128)}, u32[]{:S(2)}) copy-start(f32[128,256]{1,0:T(8,128)} %h_ref.5) | copy-start | bytes 393220
  2.4 15.6 %copy-start.2 = (f32[384,384]{1,0:T(8,128)S(1)}, f32[384,384]{1,0:T(8,128)}, u32[]{:S(2)}) copy-start(f32[384,384]{1,0:T(8,128)} %constant.75.clone.cols_t_ref) | copy-start | bytes 1769476
  2.6 4.8 %collective-permute-start = (f32[40,128]{1,0:T(8,128)S(1)}, f32[40,128]{1,0:T(8,128)S(1)}, u32[]{:S(2)}, u32[]{:S(2)}) collective-permute-start(f32[40,128]{1,0:T(8,128)S(1)} %get-tuple-element.53), channel_id=1, source_target_pairs={{0,1},{1,0},{2,3},{3,2},{4,5},{5,4},{6,7},{7,6},{8,9},{9,8},{10,11... | collective-permute-start | bytes 61448 | tf_op jit(solution)/shard_map/ppermute | solution.py:527
  7.4 0.7 collective-permute-start.1
  8.3 1.3 %collective-permute-start.2 = (f32[32,384]{1,0:T(8,128)S(1)}, f32[32,384]{1,0:T(8,128)S(1)}, u32[]{:S(2)}, u32[]{:S(2)}) collective-permute-start(f32[32,384]{1,0:T(8,128)S(1)} %get-tuple-element.57), channel_id=1, source_target_pairs={{0,4},{4,0},{8,12},{12,8},{16,20},{20,16},{24,28},{28,24},{1,5},{5... | collective-permute-start | bytes 147464 | tf_op jit(solution)/shard_map/ppermute | solution.py:527
  9.6 0.7 collective-permute-start.3
  10.2 13.7 %collective-permute-start.4 = (f32[8,128]{1,0:T(8,128)S(1)}, f32[8,128]{1,0:T(8,128)S(1)}, u32[]{:S(2)}, u32[]{:S(2)}) collective-permute-start(f32[8,128]{1,0:T(8,128)S(1)} %slice_add_fusion.1), channel_id=1, source_target_pairs={{0,16},{4,20},{8,24},{12,28},{16,0},{20,4},{24,8},{28,12},{1,17},{... | collective-permute-start | bytes 12296 | tf_op jit(solution)/shard_map/ppermute | solution.py:563
  18.1 1.1 %copy-start.3 = (f32[384,384]{1,0:T(8,128)S(1)}, f32[384,384]{1,0:T(8,128)}, u32[]{:S(2)}) copy-start(f32[384,384]{1,0:T(8,128)} %constant.74.clone.cols_ref) | copy-start | bytes 1769476
  19.1 0.9 %copy-start.5 = (f32[144,384]{1,0:T(8,128)S(1)}, f32[144,384]{1,0:T(8,128)}, u32[]{:S(2)}) copy-start(f32[144,384]{1,0:T(8,128)} %constant.76.clone.scale_ref) | copy-start | bytes 663556
  20.1 0.9 %copy-start.7 = (f32[160,144]{1,0:T(8,128)S(1)}, f32[160,144]{1,0:T(8,128)}, u32[]{:S(2)}) copy-start(f32[160,144]{1,0:T(8,128)} %constant.72.clone.rows_ref) | copy-start | bytes 276484
  21.0 0.9 %copy-start.9 = (f32[144,160]{1,0:T(8,128)S(1)}, f32[144,160]{1,0:T(8,128)}, u32[]{:S(2)}) copy-start(f32[144,160]{1,0:T(8,128)} %constant.73.clone.rows_t_ref) | copy-start | bytes 276484
  21.9 13.0 %copy-start.8 = (f32[160,144]{1,0:T(8,128)S(1)}, f32[160,144]{1,0:T(8,128)}, u32[]{:S(2)}) copy-start(f32[160,144]{1,0:T(8,128)} %constant.72.clone.rows_ref) | copy-start | bytes 276484
  24.0 10.9 %copy-start.6 = (f32[144,384]{1,0:T(8,128)S(1)}, f32[144,384]{1,0:T(8,128)}, u32[]{:S(2)}) copy-start(f32[144,384]{1,0:T(8,128)} %constant.76.clone.scale_ref) | copy-start | bytes 663556
  24.0 9.3 %collective-permute-start.5 = (f32[32,160]{1,0:T(8,128)S(1)}, f32[32,160]{1,0:T(8,128)S(1)}, u32[]{:S(2)}, u32[]{:S(2)}) collective-permute-start(f32[32,160]{1,0:T(8,128)S(1)} %select_maximum_fusion), channel_id=1, source_target_pairs={{0,1},{1,0},{2,3},{3,2},{4,5},{5,4},{6,7},{7,6},{8,9},{9,8},{10,11... | collective-permute-start | bytes 61448 | tf_op jit(solution)/shard_map/ppermute | solution.py:527
  31.5 1.9 %collective-permute-start.6 = (f32[24,160]{1,0:T(8,128)S(1)}, f32[24,160]{1,0:T(8,128)S(1)}, u32[]{:S(2)}, u32[]{:S(2)}) collective-permute-start(f32[24,160]{1,0:T(8,128)S(1)} %get-tuple-element.61), channel_id=1, source_target_pairs={{1,2},{2,1},{5,6},{6,5},{9,10},{10,9},{13,14},{14,13},{17,18},{18,... | collective-permute-start | bytes 46088 | tf_op jit(solution)/shard_map/ppermute | solution.py:530
  33.4 1.5 %copy-start.1 = (f32[128,256]{1,0:T(8,128)S(1)}, f32[128,256]{1,0:T(8,128)}, u32[]{:S(2)}) copy-start(f32[128,256]{1,0:T(8,128)} %r_ref.11) | copy-start | bytes 393220
  33.4 1.5 %copy-start.10 = (f32[128,128]{1,0:T(8,128)S(1)}, f32[128,128]{1,0:T(8,128)}, u32[]{:S(2)}) copy-start(f32[128,128]{1,0:T(8,128)} %constant.77.clone.inverse_ref) | copy-start | bytes 196612
  33.6 1.3 %collective-permute-start.7 = (f32[32,384]{1,0:T(8,128)S(1)}, f32[32,384]{1,0:T(8,128)S(1)}, u32[]{:S(2)}, u32[]{:S(2)}) collective-permute-start(f32[32,384]{1,0:T(8,128)S(1)} %get-tuple-element.64), channel_id=1, source_target_pairs={{0,4},{4,0},{8,12},{12,8},{16,20},{20,16},{24,28},{28,24},{1,5},{5... | collective-permute-start | bytes 147464 | tf_op jit(solution)/shard_map/ppermute | solution.py:527
  33.7 0.7 collective-permute-start.8
  37.7 6.5 %collective-permute-start.9 = (f32[24,160]{1,0:T(8,128)S(1)}, f32[24,160]{1,0:T(8,128)S(1)}, u32[]{:S(2)}, u32[]{:S(2)}) collective-permute-start(f32[24,160]{1,0:T(8,128)S(1)} %get-tuple-element.68), channel_id=1, source_target_pairs={{0,1},{1,0},{2,3},{3,2},{4,5},{5,4},{6,7},{7,6},{8,9},{9,8},{10,11... | collective-permute-start | bytes 46088 | tf_op jit(solution)/shard_map/ppermute | solution.py:527
  42.4 1.8 %collective-permute-start.10 = (f32[24,160]{1,0:T(8,128)S(1)}, f32[24,160]{1,0:T(8,128)S(1)}, u32[]{:S(2)}, u32[]{:S(2)}) collective-permute-start(f32[24,160]{1,0:T(8,128)S(1)} %get-tuple-element.69), channel_id=1, source_target_pairs={{1,2},{2,1},{5,6},{6,5},{9,10},{10,9},{13,14},{14,13},{17,18},{18,... | collective-permute-start | bytes 46088 | tf_op jit(solution)/shard_map/ppermute | solution.py:530
  44.4 4.6 %collective-permute-start.11 = (f32[24,384]{1,0:T(8,128)S(1)}, f32[24,384]{1,0:T(8,128)S(1)}, u32[]{:S(2)}, u32[]{:S(2)}) collective-permute-start(f32[24,384]{1,0:T(8,128)S(1)} %get-tuple-element.71), channel_id=1, source_target_pairs={{0,4},{4,0},{8,12},{12,8},{16,20},{20,16},{24,28},{28,24},{1,5},{5... | collective-permute-start | bytes 110600 | tf_op jit(solution)/shard_map/ppermute | solution.py:527
  48.2 0.9 %collective-permute-start.12 = (f32[24,384]{1,0:T(8,128)S(1)}, f32[24,384]{1,0:T(8,128)S(1)}, u32[]{:S(2)}, u32[]{:S(2)}) collective-permute-start(f32[24,384]{1,0:T(8,128)S(1)} %get-tuple-element.72), channel_id=1, source_target_pairs={{4,8},{8,4},{12,16},{16,12},{20,24},{24,20},{5,9},{9,5},{13,17},{1... | collective-permute-start | bytes 110600 | tf_op jit(solution)/shard_map/ppermute | solution.py:530
  49.5 5.7 %collective-permute-start.13 = (f32[16,1,128]{2,1,0:T(1,128)S(1)}, f32[16,1,128]{2,1,0:T(1,128)S(1)}, u32[]{:S(2)}, u32[]{:S(2)}) collective-permute-start(f32[16,1,128]{2,1,0:T(1,128)S(1)} %slice.68), channel_id=1, source_target_pairs={{0,4},{4,0},{8,12},{12,8},{16,20},{20,16},{24,28},{28,24},{1,5},{5... | collective-permute-start | bytes 24584 | tf_op jit(solution)/shard_map/ppermute | solution.py:614
  55.3 3.8 %collective-permute-start.14 = (f32[16,1,128]{2,1,0:T(1,128)S(1)}, f32[16,1,128]{2,1,0:T(1,128)S(1)}, u32[]{:S(2)}, u32[]{:S(2)}) collective-permute-start(f32[16,1,128]{2,1,0:T(1,128)S(1)} %slice_add_fusion.3), channel_id=1, source_target_pairs={{0,8},{4,12},{8,0},{12,4},{16,24},{20,28},{24,16},{28,20},{1,9},{5... | collective-permute-start | bytes 24584 | tf_op jit(solution)/shard_map/ppermute | solution.py:614
  59.1 4.6 %collective-permute-start.15 = (f32[16,1,128]{2,1,0:T(1,128)S(1)}, f32[16,1,128]{2,1,0:T(1,128)S(1)}, u32[]{:S(2)}, u32[]{:S(2)}) collective-permute-start(f32[16,1,128]{2,1,0:T(1,128)S(1)} %add.42), channel_id=1, source_target_pairs={{0,16},{4,20},{8,24},{12,28},{16,0},{20,4},{24,8},{28,12},{1,17},{... | collective-permute-start | bytes 24584 | tf_op jit(solution)/shard_map/ppermute | solution.py:614
  63.7 6.5 %collective-permute-start.16 = (f32[16,1,128]{2,1,0:T(1,128)S(1)}, f32[16,1,128]{2,1,0:T(1,128)S(1)}, u32[]{:S(2)}, u32[]{:S(2)}) collective-permute-start(f32[16,1,128]{2,1,0:T(1,128)S(1)} %add.43), channel_id=1, source_target_pairs={{0,1},{1,0},{2,3},{3,2},{4,5},{5,4},{6,7},{7,6},{8,9},{9,8},{10,11... | collective-permute-start | bytes 24584 | tf_op jit(solution)/shard_map/ppermute | solution.py:614
  70.2 3.7 %collective-permute-start.17 = (f32[16,1,128]{2,1,0:T(1,128)S(1)}, f32[16,1,128]{2,1,0:T(1,128)S(1)}, u32[]{:S(2)}, u32[]{:S(2)}) collective-permute-start(f32[16,1,128]{2,1,0:T(1,128)S(1)} %add.44), channel_id=1, source_target_pairs={{0,2},{1,3},{2,0},{3,1},{4,6},{5,7},{6,4},{7,5},{8,10},{9,11},{10,... | collective-permute-start | bytes 24584 | tf_op jit(solution)/shard_map/ppermute | solution.py:614

commit v2 on v1

v2 whole, which is shorter than its diff:
```python
import functools

import jax
import jax.numpy as jnp
import numpy as np
from jax import lax
from jax.experimental import pallas as pl
from jax.experimental.pallas import tpu as pltpu
from jax.sharding import PartitionSpec as P

SUB = 128
OV = 8
EXT = SUB + 2 * OV
DAMP = 2.0**-28
SHRINK = 2.0**-20

TR, TC = 128, 256
FR, FC = 160, 384
SPEC = 192

highest = lax.Precision.HIGHEST


def sine(count):
    k = np.arange(1, count + 1, dtype=np.float64)
    basis = np.sqrt(2.0 / (count + 1.0)) * np.sin(np.pi * k[:, None] * k[None, :] / (count + 1.0))
    return basis, 2.0 - 2.0 * np.cos(np.pi * k / (count + 1.0))


def block_constants():
    basis, eig = sine(EXT)
    rows = np.zeros((FR, EXT))
    cols = np.zeros((FC, 2 * SPEC))
    for at in range(EXT):
        rows[(at - OV) % FR] = basis[at]
        for b in range(2):
            cols[(b * SUB + at - OV) % FC, b * SPEC : b * SPEC + EXT] = basis[at]
    scale = np.ones((EXT, 2 * SPEC))
    for b in range(2):
        scale[:, b * SPEC : b * SPEC + EXT] = (eig[:, None] + eig[None, :]) ** 2
    wide = lambda x: np.pad(x, ((0, 0), (0, FC - x.shape[1])))
    return np.concatenate([cols, cols.T, scale, wide(rows), wide(rows.T)]).astype(np.float32)


def block_parts(ref):
    cols, cols_t, scale = ref[:FC], ref[FC : 2 * FC], ref[2 * FC : 2 * FC + EXT]
    at = 2 * FC + EXT
    return ref[at : at + FR, :EXT], ref[at + FR : at + FR + EXT, :FR], cols, cols_t, scale


def coarse_inverse(nr, nc, width):
    br, er = sine(nr)
    bc, ec = sine(nc)
    both = np.kron(br, bc).reshape(nr, nc // 2, 2, nr * nc).transpose(2, 0, 1, 3)
    both = both.reshape(nr * nc, nr * nc)
    scale = (er[:, None] + ec[None, :]) / (SUB * SUB)
    values = (SUB * SUB * (DAMP + scale * scale)).reshape(-1)
    whole = np.zeros((width, width), np.float32)
    whole[: nr * nc, : nr * nc] = (both / values) @ both.T
    return whole


def dot(a, b):
    return lax.dot_general(
        a, b, (((1,), (0,)), ((), ())), precision=highest, preferred_element_type=jnp.float32
    )


def lap(x):
    rows, lanes = x.shape
    beside = pltpu.roll(x, 1, 0) + pltpu.roll(x, rows - 1, 0)
    beside = beside + (pltpu.roll(x, 1, 1) + pltpu.roll(x, lanes - 1, 1))
    return 4.0 * x - beside


def lanes_of(shape):
    return lax.broadcasted_iota(jnp.int32, shape, 1)


def rows_of(shape):
    return lax.broadcasted_iota(jnp.int32, shape, 0)


def total(x):
    return jnp.sum(jnp.sum(x, axis=0, keepdims=True), axis=1, keepdims=True)


def place():
    return lax.axis_index("row"), lax.axis_index("col")


def is_even(index):
    return lax.rem(index, 2) == 0


def grid_mask(shape, counts):
    i, j = place()
    rr, ll = rows_of(shape), lanes_of(shape)
    below = jnp.where(i < counts[0] - 1, 144, 128)
    above = jnp.where(i > 0, 144, 160)
    right = jnp.where(j < counts[1] - 1, 320, 256)
    left = jnp.where(j > 0, 320, 384)
    return ((rr < below) | (rr >= above)) & ((ll < right) | (ll >= left))


def row_of(pairs):
    lane = lanes_of((1, 128))
    row = jnp.zeros((1, 128), jnp.float32)
    for k, (left, right) in enumerate(pairs):
        row = jnp.where(lane == k, left, jnp.where(lane == 64 + k, right, row))
    return row


def gathered(rows, width):
    devices = rows.shape[0]
    turned = rows.T
    parts = [turned[:16], turned[64:80]]
    if width > 2 * devices:
        parts.append(jnp.zeros((16, width - 2 * devices), jnp.float32))
    return jnp.concatenate(parts, axis=1)


def coarse_values(c_row, inverse):
    return dot(jnp.broadcast_to(c_row, (8, c_row.shape[1])), inverse)[:1]


def spread(g_row, counts):
    i, j = place()
    nr, nc = counts[0], 2 * counts[1]
    shape = (16, g_row.shape[1])
    which = rows_of(shape)
    r = i - 1 + which // 4
    c = 2 * j - 1 + which % 4
    inside = (r >= 0) & (r < nr) & (c >= 0) & (c < nc) & (which < 12)
    at = lax.rem(c + 2, 2) * (nr * counts[1]) + r * counts[1] + (c + 2) // 2 - 1
    picked = jnp.where(inside & (lanes_of(shape) == at), g_row, 0.0)
    picked = jnp.sum(picked, axis=1, keepdims=True)
    lane = lanes_of((1, 128))
    bands = []
    for d in range(3):
        left, first, second, right = (picked[4 * d + k : 4 * d + k + 1] for k in range(4))
        bands.append(
            jnp.concatenate(
                [
                    jnp.broadcast_to(first, (1, 128)),
                    jnp.broadcast_to(second, (1, 128)),
                    jnp.where(lane < 64, right, left),
                ],
                axis=1,
            )
        )
    return jnp.concatenate(
        [
            jnp.broadcast_to(bands[1], (128, FC)),
            jnp.broadcast_to(bands[2], (16, FC)),
            jnp.broadcast_to(bands[0], (16, FC)),
        ],
        axis=0,
    )


def local_solve(w, means, basis_ref):
    rows, rows_t, cols, cols_t, scale = block_parts(basis_ref)
    lane = lanes_of((1, 2 * SPEC))
    mean = jnp.where(lane < SPEC, means[0], means[1])
    t = dot(dot(rows_t, w), cols)
    t = t / (DAMP + mean * scale)
    return dot(rows, dot(t, cols_t))


def core_sums(x):
    return [total(x[:, :128]), total(x[:, 128:256])]


def pack_columns(y):
    lane = lanes_of((FR, 128))
    packed = jnp.where(
        lane < 16,
        y[:, :128],
        jnp.where(lane >= 112, y[:, 128:256], pltpu.roll(y[:, 256:], 64, 1)),
    )
    turned = packed.T
    to_left = jnp.concatenate([turned[56:64], turned[:16]], axis=0)
    to_right = jnp.concatenate([turned[112:], turned[64:72]], axis=0)
    return to_left, to_right


def add_columns(y, from_left, from_right):
    turned = jnp.concatenate(
        [
            from_right[8:24],
            jnp.zeros((40, FR), jnp.float32),
            from_right[:8],
            from_left[16:24],
            jnp.zeros((40, FR), jnp.float32),
            from_left[:16],
        ],
        axis=0,
    )
    back = turned.T
    lane = lanes_of((FR, 128))
    rolled = pltpu.roll(back, 64, 1)
    first = y[:, :128] + jnp.where(lane < 8, rolled, 0.0)
    second = y[:, 128:256] + jnp.where(lane >= 120, rolled, 0.0)
    third = y[:, 256:] + jnp.where((lane < 16) | (lane >= 112), back, 0.0)
    return jnp.concatenate([first, second, third], axis=1)


def pack_rows(y):
    return jnp.concatenate([y[152:160], y[:16]], axis=0), y[112:136]


def add_rows(y, from_above, from_below):
    return jnp.concatenate(
        [
            y[:8] + from_above[16:24],
            y[8:120],
            y[120:144] + from_below,
            y[144:] + from_above[:16],
        ],
        axis=0,
    )


def sides(index, count, a, b):
    even = is_even(index)
    before = jnp.where(index > 0, jnp.where(even, b, a), 0.0)
    after = jnp.where(index < count - 1, jnp.where(even, a, b), 0.0)
    return before, after


def send(index, a_ref, b_ref, before, after):
    even = is_even(index)
    a_ref[...] = jnp.where(even, after, before)
    b_ref[...] = jnp.where(even, before, after)


def begin_kernel(counts, r_hbm, h_hbm, r_ref, h_ref, a_ref, b_ref, sums_ref, sems):
    copies = [
        pltpu.make_async_copy(r_hbm, r_ref, sems.at[0]),
        pltpu.make_async_copy(h_hbm, h_ref, sems.at[1]),
    ]
    for copy in copies:
        copy.start()
    for copy in copies:
        copy.wait()
    r, h = r_ref[...], h_ref[...]
    lane = lanes_of((128, 128))
    packed = jnp.where(
        lane < 16,
        r[:, :128],
        jnp.where(
            lane < 64,
            pltpu.roll(h[:, :128], 16, 1),
            jnp.where(lane < 112, pltpu.roll(h[:, 128:], 112, 1), r[:, 128:]),
        ),
    )
    turned = packed.T
    send(lax.axis_index("col"), a_ref, b_ref, turned[:32], turned[96:])
    sums_ref[...] = row_of([core_sums(r)])


def widen_kernel(counts, r_ref, h_ref, ga_ref, gb_ref, r3_ref, h3_ref, a_ref, b_ref):
    i, j = place()
    from_left, from_right = sides(j, counts[1], ga_ref[...], gb_ref[...])
    turned = jnp.concatenate([from_right, jnp.zeros((64, 128), jnp.float32), from_left], axis=0)
    back = turned.T
    lane = lanes_of((128, 128))
    edge = (lane < 16) | (lane >= 112)
    r3 = jnp.where(edge, back, 0.0)
    h3 = jnp.where(
        lane < 16, pltpu.roll(back, 112, 1), jnp.where(lane >= 112, pltpu.roll(back, 16, 1), 0.0)
    )
    r3_ref[...] = r3
    h3_ref[...] = h3
    r, h = r_ref[...], h_ref[...]

    def strip(r_rows, h_rows):
        return jnp.concatenate(
            [
                jnp.concatenate([r[r_rows], r3[r_rows]], axis=1),
                jnp.concatenate([h[h_rows], h3[h_rows]], axis=1),
            ],
            axis=0,
        )

    send(i, a_ref, b_ref, strip(slice(0, 8), slice(0, 16)), strip(slice(120, 128), slice(112, 128)))


def first_kernel(
    counts, r_ref, h_ref, r3_ref, h3_ref, ga_ref, gb_ref, basis_ref, y_ref, m_ref, a_ref, b_ref
):
    i, j = place()
    above, below = sides(i, counts[0], ga_ref[...], gb_ref[...])
    r = jnp.concatenate([r_ref[...], r3_ref[...]], axis=1)
    h = jnp.concatenate([h_ref[...], h3_ref[...]], axis=1)
    wide = jnp.concatenate([r, below[:8], jnp.zeros((16, FC), jnp.float32), above[:8]], axis=0)
    tall = jnp.concatenate([h, below[8:], above[8:]], axis=0)
    mobility = tall * tall * tall
    m_ref[...] = mobility
    means = [x / (SUB * SUB) for x in core_sums(mobility[:128])]
    y = local_solve(wide, means, basis_ref)
    y_ref[...] = y
    send(j, a_ref, b_ref, *pack_columns(y))


def columns_kernel(counts, y_ref, ga_ref, gb_ref, out_ref, a_ref, b_ref):
    i, j = place()
    y = add_columns(y_ref[...], *sides(j, counts[1], ga_ref[...], gb_ref[...]))
    out_ref[...] = y
    send(i, a_ref, b_ref, *pack_rows(y))


def second_kernel(
    counts,
    width,
    y_ref,
    m_ref,
    ga_ref,
    gb_ref,
    sums_ref,
    r_ref,
    inverse_ref,
    basis_ref,
    z_ref,
    w_ref,
    y2_ref,
    stats_ref,
    a_ref,
    b_ref,
):
    i, j = place()
    s = add_rows(y_ref[...], *sides(i, counts[0], ga_ref[...], gb_ref[...]))
    mask = grid_mask((FR, FC), counts)
    s = jnp.where(mask, s, 0.0)
    c0 = gathered(sums_ref[...], width)[:1]
    coarse = spread(coarse_values(c0, inverse_ref[...]), counts)
    mobility = m_ref[...]
    flow = mobility * (lap(s) + lap(coarse))
    z = s + coarse
    w = jnp.where(mask, DAMP * z + lap(flow), 0.0) * SHRINK
    zt, wt, rt, mt = z[:128, :256], w[:128, :256], r_ref[...], mobility[:128, :256]
    z_ref[...] = zt
    w_ref[...] = wt
    means = [x / (SUB * SUB) for x in core_sums(mt)]
    y = local_solve(w, means, basis_ref)
    y2_ref[...] = y
    send(j, a_ref, b_ref, *pack_columns(y))
    lane, row = lanes_of((1, 256)), rows_of((128, 1))
    along = (lane % 128 != 0) & (lane % 128 != 127)
    top, low = mt[:1], mt[127:]
    side = jnp.sum(jnp.where((row > 0) & (row < 127), mt, 0.0), axis=0, keepdims=True)

    def halves(x):
        return [
            jnp.sum(x[:, :128], axis=1, keepdims=True),
            jnp.sum(x[:, 128:], axis=1, keepdims=True),
        ]

    first, last = lane % 128 == 0, lane % 128 == 127
    stats_ref[...] = row_of(
        [
            core_sums(rt * zt),
            core_sums(zt * wt),
            core_sums(wt),
            halves(jnp.where(along, top, 0.0)),
            halves(jnp.where(along, low, 0.0)),
            halves(jnp.where(first, side, 0.0)),
            halves(jnp.where(last, side, 0.0)),
            halves(jnp.where(first, top, 0.0)),
            halves(jnp.where(last, top, 0.0)),
            halves(jnp.where(first, low, 0.0)),
            halves(jnp.where(last, low, 0.0)),
        ]
    )


def dots_kernel(
    counts, y_ref, m_ref, ga_ref, gb_ref, r_ref, w_ref, stats_ref, q_ref, v_ref, stats_out
):
    i, j = place()
    q = add_rows(y_ref[...], *sides(i, counts[0], ga_ref[...], gb_ref[...]))
    q = jnp.where(grid_mask((FR, FC), counts), q, 0.0)
    v = DAMP * q + lap(m_ref[...] * lap(q))
    qt, vt = q[:128, :256], v[:128, :256]
    q_ref[...] = qt
    v_ref[...] = vt
    rest = [
        core_sums(vt),
        core_sums(r_ref[...] * qt),
        core_sums(w_ref[...] * qt),
        core_sums(vt * qt),
    ]
    zero = jnp.zeros((1, 1), jnp.float32)
    row = stats_ref[...] + row_of([[zero, zero]] * 11 + rest)
    stats_out[...] = jnp.broadcast_to(row, stats_out.shape)


def end_kernel(
    counts,
    width,
    stats_ref,
    sums_ref,
    inverse_ref,
    m_ref,
    r_ref,
    z_ref,
    w_ref,
    q_ref,
    v_ref,
    solution_ref,
    residual_ref,
):
    tiles_c = counts[1]
    devices = counts[0] * tiles_c
    table = gathered(stats_ref[...], width)
    st = [table[k : k + 1] for k in range(15)]

    def whole(x):
        return jnp.sum(x, axis=1, keepdims=True)

    rz, zw, rq, wq, qv = (whole(st[k]) for k in (0, 1, 12, 13, 14))
    c0, c1, sums_v = gathered(sums_ref[...], width)[:1], st[2], st[11]
    g = coarse_values(c1, inverse_ref[...])
    lane = lanes_of((1, width))
    cell = lane < 2 * devices
    on_left = lane < devices
    device = lane % devices
    column = device % tiles_c

    def from_lane(distance):
        return pltpu.roll(g, distance % width, 1)

    up = jnp.where(device >= tiles_c, from_lane(tiles_c), 0.0)
    down = jnp.where(device < devices - tiles_c, from_lane(-tiles_c), 0.0)
    left = jnp.where(
        on_left, jnp.where(column > 0, from_lane(1 - devices), 0.0), from_lane(devices)
    )
    right = jnp.where(
        on_left,
        from_lane(-devices),
        jnp.where(column < tiles_c - 1, from_lane(devices - 1), 0.0),
    )
    du, dd, dl, dr = g - up, g - down, g - left, g - right
    energy = DAMP * SUB * SUB * g * g
    energy = energy + st[3] * du * du + st[4] * dd * dd + st[5] * dl * dl + st[6] * dr * dr
    for weight, p, q in ((st[7], du, dl), (st[8], du, dr), (st[9], dd, dl), (st[10], dd, dr)):
        both = p + q
        energy = energy + weight * both * both
    ry = rq + whole(g * c0)
    yw = wq + whole(g * c1)
    yv = qv + whole(jnp.where(cell, 2.0 * g * sums_v + energy, 0.0))
    a = rz / zw
    rz1 = rz - a * ry - a * zw + a * a * yw
    beta1 = 1.0 + rz1 / rz
    dad = (beta1 * beta1 * zw - 2.0 * a * beta1 * yw) * (1.0 / SHRINK) + a * a * yv
    a1 = rz1 / dad
    coarse = spread(g, counts)
    y = q_ref[...] + coarse[:128, :256]
    image = DAMP * coarse + lap(m_ref[...] * lap(coarse))
    v = v_ref[...] + image[:128, :256]
    z, w = z_ref[...], w_ref[...]
    solution_ref[...] = (a * SHRINK) * z + a1 * (beta1 * z - a * y)
    residual_ref[...] = r_ref[...] - a * w - a1 * ((beta1 * (1.0 / SHRINK)) * w - a * v)


def call(kernel, outs, *args, **options):
    shapes = [jax.ShapeDtypeStruct(s, jnp.float32) for s in outs]
    return pl.pallas_call(
        kernel,
        out_shape=shapes,
        compiler_params=pltpu.CompilerParams(vmem_limit_bytes=48 * 1024 * 1024),
        **options,
    )(*args)


def pairs_from(count, offset):
    found = []
    for k in range(offset, count, 2):
        found += [(k, (k + 1) % count), ((k + 1) % count, k)]
    return found


def body(counts, height, noise):
    nr, nc = counts
    devices = nr * nc
    width = max(128, devices * 2)
    basis = jnp.asarray(block_constants())
    inverse = jnp.asarray(coarse_inverse(nr, 2 * nc, width))
    both = ("row", "col")

    def swap(a, b, axis):
        count = lax.axis_size(axis)
        return (
            lax.ppermute(a, axis, pairs_from(count, 0)),
            lax.ppermute(b, axis, pairs_from(count, 1)),
        )

    r, h, a, b, sums = call(
        functools.partial(begin_kernel, counts),
        [(TR, TC)] * 2 + [(32, 128)] * 2 + [(1, 128)],
        noise,
        height,
        in_specs=[pl.BlockSpec(memory_space=pltpu.HBM)] * 2,
        scratch_shapes=[pltpu.SemaphoreType.DMA((2,))],
    )
    sums = lax.all_gather(sums, both, axis=0, tiled=True)
    ga, gb = swap(a, b, "col")
    r3, h3, a, b = call(
        functools.partial(widen_kernel, counts),
        [(128, 128)] * 2 + [(24, FC)] * 2,
        r,
        h,
        ga,
        gb,
    )
    ga, gb = swap(a, b, "row")
    y, m, a, b = call(
        functools.partial(first_kernel, counts),
        [(FR, FC)] * 2 + [(24, FR)] * 2,
        r,
        h,
        r3,
        h3,
        ga,
        gb,
        basis,
    )
    ga, gb = swap(a, b, "col")
    y, a, b = call(
        functools.partial(columns_kernel, counts), [(FR, FC)] + [(24, FC)] * 2, y, ga, gb
    )
    ga, gb = swap(a, b, "row")
    z, w, y, stats, a, b = call(
        functools.partial(second_kernel, counts, width),
        [(TR, TC)] * 2 + [(FR, FC), (1, 128)] + [(24, FR)] * 2,
        y,
        m,
        ga,
        gb,
        sums,
        r,
        inverse,
        basis,
    )
    ga, gb = swap(a, b, "col")
    y, a, b = call(
        functools.partial(columns_kernel, counts), [(FR, FC)] + [(24, FC)] * 2, y, ga, gb
    )
    ga, gb = swap(a, b, "row")
    q, v, stats = call(
        functools.partial(dots_kernel, counts),
        [(TR, TC)] * 2 + [(devices, 128)],
        y,
        m,
        ga,
        gb,
        r,
        w,
        stats,
    )
    stats = lax.all_to_all(stats, both, 0, 0, tiled=True)
    return tuple(
        call(
            functools.partial(end_kernel, counts, width),
            [(TR, TC)] * 2,
            stats,
            sums,
            inverse,
            m,
            r,
            z,
            w,
            q,
            v,
        )
    )


def solution(mesh):
    counts = (mesh.shape["row"], mesh.shape["col"])
    spec = P("row", "col")
    return jax.shard_map(
        functools.partial(body, counts),
        mesh=mesh,
        in_specs=(spec, spec),
        out_specs=(spec, spec),
        check_vma=False,
    )
```

time: 75.6 us -> 119 us (1.57)
  blocking collectives: 0 us -> 75.5 us
  starting transfers between devices: 46.7 us -> 13.9 us
  local copies, waits for them, and re-layouts: 5.66 us -> 3.35 us
  waiting for transfers between devices: 14.6 us -> 16.9 us
    all_gather x0 -> x1, blocking collectives: none -> 66.2 us  [body(): sums = lax.all_gather(sums, both, axis=0, tiled=True)]
    ppermute x18 -> x12, starting transfers between devices: 46.7 us -> 13.9 us  [the longest x6 10 us: swap(): lax.ppermute(b, axis, pairs_from(count, 1))]
    all_to_all x0 -> x1, blocking collectives: none -> 9.29 us  [body(): stats = lax.all_to_all(stats, both, 0, 0, tiled=True)]
    ppermute x18 -> x12, waiting for transfers between devices: 14.6 us -> 16.9 us  [the longest x6 11.1 us: swap(): lax.ppermute(b, axis, pairs_from(count, 1))]
    unnamed x22 -> x10, local copies, waits for them, and re-layouts: 5.65 us -> 3.35 us
  transfers between devices with their start and end apart: 18 -> 12, of which waited for: 11 -> 9; matrix products, arithmetic and copies ran while one was open for 0% -> 0% of each run, Pallas kernels for 3% -> 0%
where the time goes in v2:
time: 119 us; the launch traced here: 118 us
  blocking collectives  75.5 us (63%)
  waiting for transfers between devices  16.9 us (14%)
  starting transfers between devices  13.9 us (12%)
  Pallas kernels  7.87 us (7%)
  local copies, waits for them, and re-layouts  3.35 us (3%)
    all_gather x1, blocking collectives, body(): sums = lax.all_gather(sums, both, axis=0, tiled=True)  66.2 us
    ppermute x6, waiting for transfers between devices, swap(): lax.ppermute(b, axis, pairs_from(count, 1))  11.1 us
    ppermute x6, starting transfers between devices, swap(): lax.ppermute(b, axis, pairs_from(count, 1))  10 us
    all_to_all x1, blocking collectives, body(): stats = lax.all_to_all(stats, both, 0, 0, tiled=True)  9.29 us
    pallas_call x8, Pallas kernels, call(): pl.pallas_call(kernel, out_shape=shapes, compiler_params=pltpu.CompilerPa...  7.87 us
    ppermute x6, waiting for transfers between devices, swap(): lax.ppermute(a, axis, pairs_from(count, 0))  5.82 us
    ppermute x6, starting transfers between devices, swap(): lax.ppermute(a, axis, pairs_from(count, 0))  3.87 us
    unnamed x10, local copies, waits for them, and re-layouts  3.35 us
  transfers between devices with their start and end apart: 12, of which 9 were waited for; matrix products, arithmetic and copies ran while one was open for 0% of the time, Pallas kernels for 0%

profile of v2, /device:TPU:0, one launch (start us, length us, event | category | flops | bytes accessed | tf_op | source)
XLA Modules:
  0.0 118.4 jit_solution(7942043122263079702)
XLA Ops:
  0.6 0.0 copy-start.2
  0.6 0.0 copy-start.3
  0.7 0.9 copy-done.3
  1.6 0.0 copy-start.4
  1.6 0.9 copy-done.4
  2.5 0.5 shard_map.59
  3.0 3.0 %collective-permute-start = (f32[32,128]{1,0:T(8,128)S(1)}, f32[32,128]{1,0:T(8,128)S(1)}, u32[]{:S(2)}, u32[]{:S(2)}) collective-permute-start(f32[32,128]{1,0:T(8,128)S(1)} %get-tuple-element.32), channel_id=1, source_target_pairs={{0,1},{1,0},{2,3},{3,2},{4,5},{5,4},{6,7},{7,6},{8,9},{9,8},{10,11... | collective-permute-start | bytes 49160 | tf_op jit(solution)/shard_map/ppermute | solution.py:495
  6.0 1.5 %collective-permute-start.1 = (f32[32,128]{1,0:T(8,128)S(1)}, f32[32,128]{1,0:T(8,128)S(1)}, u32[]{:S(2)}, u32[]{:S(2)}) collective-permute-start(f32[32,128]{1,0:T(8,128)S(1)} %get-tuple-element.33), channel_id=1, source_target_pairs={{1,2},{2,1},{3,0},{0,3},{5,6},{6,5},{7,4},{4,7},{9,10},{10,9},{11,... | collective-permute-start | bytes 49160 | tf_op jit(solution)/shard_map/ppermute | solution.py:496
  7.5 0.2 collective-permute-done.ga_ref
  7.7 2.9 %collective-permute-done.1.gb_ref = f32[32,128]{1,0:T(8,128)S(1)} collective-permute-done((f32[32,128]{1,0:T(8,128)S(1)}, f32[32,128]{1,0:T(8,128)S(1)}, u32[]{:S(2)}, u32[]{:S(2)}) %collective-permute-start.1) | collective-permute-done | bytes 16416 | tf_op jit(solution)/shard_map/ppermute | solution.py:496
  10.6 0.2 shard_map.60
  10.8 0.1 collective-permute-start.2
  10.9 3.7 %collective-permute-start.3 = (f32[24,384]{1,0:T(8,128)S(1)}, f32[24,384]{1,0:T(8,128)S(1)}, u32[]{:S(2)}, u32[]{:S(2)}) collective-permute-start(f32[24,384]{1,0:T(8,128)S(1)} %get-tuple-element.37), channel_id=1, source_target_pairs={{4,8},{8,4},{12,16},{16,12},{20,24},{24,20},{28,0},{0,28},{5,9},{9... | collective-permute-start | bytes 110600 | tf_op jit(solution)/shard_map/ppermute | solution.py:496
  14.6 0.0 collective-permute-done.2.ga_ref
  14.6 1.7 %collective-permute-done.3.gb_ref = f32[24,384]{1,0:T(8,128)S(1)} collective-permute-done((f32[24,384]{1,0:T(8,128)S(1)}, f32[24,384]{1,0:T(8,128)S(1)}, u32[]{:S(2)}, u32[]{:S(2)}) %collective-permute-start.3) | collective-permute-done | bytes 36896 | tf_op jit(solution)/shard_map/ppermute | solution.py:496
  16.4 0.0 copy-start
  16.4 1.5 %copy-done = f32[1216,384]{1,0:T(8,128)S(1)} copy-done((f32[1216,384]{1,0:T(8,128)S(1)}, f32[1216,384]{1,0:T(8,128)}, u32[]{:S(2)}) %copy-start) | copy-done | bytes 1867800
  17.9 0.0 copy-start.1
  17.9 2.1 %shard_map.61 = (f32[160,384]{1,0:T(8,128)S(1)}, f32[160,384]{1,0:T(8,128)S(1)}, f32[24,160]{1,0:T(8,128)S(1)}, f32[24,160]{1,0:T(8,128)S(1)}) custom-call(f32[128,256]{1,0:T(8,128)S(1)} %get-tuple-element.30.r_ref, f32[128,256]{1,0:T(8,128)S(1)} %get-tuple-element.31.h_ref, f32[128,128]{1,0:T(8,128)S(1)} %get-tuple-element.34.r3_ref, ...), custom_call_target="tpu_custom_call" | custom-call | tf_op jit(solution)/shard_map/pallas_call | solution.py:469
  20.0 0.6 collective-permute-start.4
  20.6 2.4 %collective-permute-start.5 = (f32[24,160]{1,0:T(8,128)S(1)}, f32[24,160]{1,0:T(8,128)S(1)}, u32[]{:S(2)}, u32[]{:S(2)}) collective-permute-start(f32[24,160]{1,0:T(8,128)S(1)} %get-tuple-element.40), channel_id=1, source_target_pairs={{1,2},{2,1},{3,0},{0,3},{5,6},{6,5},{7,4},{4,7},{9,10},{10,9},{11,... | collective-permute-start | bytes 46088 | tf_op jit(solution)/shard_map/ppermute | solution.py:496
  23.0 0.9 collective-permute-done.4.ga_ref
  23.9 1.4 %collective-permute-done.5.gb_ref = f32[24,160]{1,0:T(8,128)S(1)} collective-permute-done((f32[24,160]{1,0:T(8,128)S(1)}, f32[24,160]{1,0:T(8,128)S(1)}, u32[]{:S(2)}, u32[]{:S(2)}) %collective-permute-start.5) | collective-permute-done | bytes 15392 | tf_op jit(solution)/shard_map/ppermute | solution.py:496
  25.3 0.2 shard_map.62
  25.5 0.1 collective-permute-start.6
  25.6 2.1 %collective-permute-start.7 = (f32[24,384]{1,0:T(8,128)S(1)}, f32[24,384]{1,0:T(8,128)S(1)}, u32[]{:S(2)}, u32[]{:S(2)}) collective-permute-start(f32[24,384]{1,0:T(8,128)S(1)} %get-tuple-element.44), channel_id=1, source_target_pairs={{4,8},{8,4},{12,16},{16,12},{20,24},{24,20},{28,0},{0,28},{5,9},{9... | collective-permute-start | bytes 110600 | tf_op jit(solution)/shard_map/ppermute | solution.py:496
  27.7 66.2 %all-gather = f32[32,1,128]{2,1,0:T(1,128)S(1)} all-gather(f32[1,1,128]{2,1,0:T(1,128)S(1)} %bitcast.10), channel_id=1, replica_groups=mesh['row'=8,'col'=4] {'row','col'}, dimensions={0}, use_global_device_ids=true | all-gather | bytes 16896 | tf_op jit(solution)/shard_map/all_gather | solution.py:507
  93.9 0.0 collective-permute-done.6.ga_ref
  93.9 0.0 collective-permute-done.7.gb_ref
  94.0 0.0 copy-done.2
  94.0 0.0 copy-done.1
  94.0 2.9 %shard_map.63 = (f32[128,256]{1,0:T(8,128)S(1)}, f32[128,256]{1,0:T(8,128)S(1)}, f32[160,384]{1,0:T(8,128)S(1)}, f32[1,128]{1,0:T(1,128)S(1)}, f32[24,160]{1,0:T(8,128)S(1)}, /*index=5*/f32[24,160]{1,0:T(8,128)S(1)}) custom-call(f32[160,384]{1,0:T(8,128)S(1)} %get-tuple-element.41.y_ref, f32[160,384]{1,0:T(8,128)S(1)} %get-tuple-element.42.m_ref, ...), custom_call_target="tpu_custom_call" | custom-call | tf_op jit(solution)/shard_map/pallas_call | solution.py:469
  96.9 0.1 collective-permute-start.8
  96.9 0.2 collective-permute-start.9
  97.1 3.6 %collective-permute-done.8.ga_ref = f32[24,160]{1,0:T(8,128)S(1)} collective-permute-done((f32[24,160]{1,0:T(8,128)S(1)}, f32[24,160]{1,0:T(8,128)S(1)}, u32[]{:S(2)}, u32[]{:S(2)}) %collective-permute-start.8) | collective-permute-done | bytes 15392 | tf_op jit(solution)/shard_map/ppermute | solution.py:495
  100.8 1.0 collective-permute-done.9.gb_ref
  101.7 0.2 shard_map.64
  101.9 0.1 collective-permute-start.10
  102.0 0.1 collective-permute-start.11
  102.1 1.1 collective-permute-done.10.ga_ref
  103.2 4.0 %collective-permute-done.11.gb_ref = f32[24,384]{1,0:T(8,128)S(1)} collective-permute-done((f32[24,384]{1,0:T(8,128)S(1)}, f32[24,384]{1,0:T(8,128)S(1)}, u32[]{:S(2)}, u32[]{:S(2)}) %collective-permute-start.11) | collective-permute-done | bytes 36896 | tf_op jit(solution)/shard_map/ppermute | solution.py:496
  107.2 0.4 shard_map.65
  107.7 9.3 %all_to_all.11 = f32[32,1,128]{2,1,0:T(1,128)S(1)} all-to-all(f32[32,1,128]{2,1,0:T(1,128)S(1)} %bitcast.9), channel_id=1, replica_groups=mesh['row'=8,'col'=4] {'row','col'}, dimensions={0} | all-to-all | bytes 32768 | tf_op jit(solution)/shard_map/all_to_all | solution.py:562
  117.0 1.4 %shard_map.66 = (f32[128,256]{1,0:T(8,128)}, f32[128,256]{1,0:T(8,128)}) custom-call(f32[32,128]{1,0:T(8,128)S(1)} %bitcast.8, f32[32,128]{1,0:T(8,128)S(1)} %bitcast.7, f32[128,128]{1,0:T(8,128)S(1)} %copy-done.2, f32[160,384]{1,0:T(8,128)S(1)} %get-tuple-element.42.m_ref, f32[128,256]{1,0:T(8,128)S(1)} %get-tuple-element.30.r_ref, ...), custom_call_target="tpu_custom_call" | custom-call | tf_op jit(solution)/shard_map/pallas_call | solution.py:469
Async XLA Ops:
  0.6 93.3 %copy-start.2 = (f32[128,128]{1,0:T(8,128)S(1)}, f32[128,128]{1,0:T(8,128)}, u32[]{:S(2)}) copy-start(f32[128,128]{1,0:T(8,128)} %constant.5.clone.inverse_ref) | copy-start | bytes 196612
  0.6 0.9 copy-start.3
  1.6 0.9 copy-start.4
  3.0 4.7 %collective-permute-start = (f32[32,128]{1,0:T(8,128)S(1)}, f32[32,128]{1,0:T(8,128)S(1)}, u32[]{:S(2)}, u32[]{:S(2)}) collective-permute-start(f32[32,128]{1,0:T(8,128)S(1)} %get-tuple-element.32), channel_id=1, source_target_pairs={{0,1},{1,0},{2,3},{3,2},{4,5},{5,4},{6,7},{7,6},{8,9},{9,8},{10,11... | collective-permute-start | bytes 49160 | tf_op jit(solution)/shard_map/ppermute | solution.py:495
  6.0 4.6 %collective-permute-start.1 = (f32[32,128]{1,0:T(8,128)S(1)}, f32[32,128]{1,0:T(8,128)S(1)}, u32[]{:S(2)}, u32[]{:S(2)}) collective-permute-start(f32[32,128]{1,0:T(8,128)S(1)} %get-tuple-element.33), channel_id=1, source_target_pairs={{1,2},{2,1},{3,0},{0,3},{5,6},{6,5},{7,4},{4,7},{9,10},{10,9},{11,... | collective-permute-start | bytes 49160 | tf_op jit(solution)/shard_map/ppermute | solution.py:496
  10.8 3.8 %collective-permute-start.2 = (f32[24,384]{1,0:T(8,128)S(1)}, f32[24,384]{1,0:T(8,128)S(1)}, u32[]{:S(2)}, u32[]{:S(2)}) collective-permute-start(f32[24,384]{1,0:T(8,128)S(1)} %get-tuple-element.36), channel_id=1, source_target_pairs={{0,4},{4,0},{8,12},{12,8},{16,20},{20,16},{24,28},{28,24},{1,5},{5... | collective-permute-start | bytes 110600 | tf_op jit(solution)/shard_map/ppermute | solution.py:495
  10.9 5.5 %collective-permute-start.3 = (f32[24,384]{1,0:T(8,128)S(1)}, f32[24,384]{1,0:T(8,128)S(1)}, u32[]{:S(2)}, u32[]{:S(2)}) collective-permute-start(f32[24,384]{1,0:T(8,128)S(1)} %get-tuple-element.37), channel_id=1, source_target_pairs={{4,8},{8,4},{12,16},{16,12},{20,24},{24,20},{28,0},{0,28},{5,9},{9... | collective-permute-start | bytes 110600 | tf_op jit(solution)/shard_map/ppermute | solution.py:496
  16.4 1.5 %copy-start = (f32[1216,384]{1,0:T(8,128)S(1)}, f32[1216,384]{1,0:T(8,128)}, u32[]{:S(2)}) copy-start(f32[1216,384]{1,0:T(8,128)} %constant.4.clone.basis_ref) | copy-start | bytes 5603332
  17.9 76.1 %copy-start.1 = (f32[1216,384]{1,0:T(8,128)S(1)}, f32[1216,384]{1,0:T(8,128)}, u32[]{:S(2)}) copy-start(f32[1216,384]{1,0:T(8,128)} %constant.4.clone.basis_ref) | copy-start | bytes 5603332
  20.0 3.9 %collective-permute-start.4 = (f32[24,160]{1,0:T(8,128)S(1)}, f32[24,160]{1,0:T(8,128)S(1)}, u32[]{:S(2)}, u32[]{:S(2)}) collective-permute-start(f32[24,160]{1,0:T(8,128)S(1)} %get-tuple-element.39), channel_id=1, source_target_pairs={{0,1},{1,0},{2,3},{3,2},{4,5},{5,4},{6,7},{7,6},{8,9},{9,8},{10,11... | collective-permute-start | bytes 46088 | tf_op jit(solution)/shard_map/ppermute | solution.py:495
  20.6 4.7 %collective-permute-start.5 = (f32[24,160]{1,0:T(8,128)S(1)}, f32[24,160]{1,0:T(8,128)S(1)}, u32[]{:S(2)}, u32[]{:S(2)}) collective-permute-start(f32[24,160]{1,0:T(8,128)S(1)} %get-tuple-element.40), channel_id=1, source_target_pairs={{1,2},{2,1},{3,0},{0,3},{5,6},{6,5},{7,4},{4,7},{9,10},{10,9},{11,... | collective-permute-start | bytes 46088 | tf_op jit(solution)/shard_map/ppermute | solution.py:496
  25.5 68.5 %collective-permute-start.6 = (f32[24,384]{1,0:T(8,128)S(1)}, f32[24,384]{1,0:T(8,128)S(1)}, u32[]{:S(2)}, u32[]{:S(2)}) collective-permute-start(f32[24,384]{1,0:T(8,128)S(1)} %get-tuple-element.43), channel_id=1, source_target_pairs={{0,4},{4,0},{8,12},{12,8},{16,20},{20,16},{24,28},{28,24},{1,5},{5... | collective-permute-start | bytes 110600 | tf_op jit(solution)/shard_map/ppermute | solution.py:495
  25.6 68.4 %collective-permute-start.7 = (f32[24,384]{1,0:T(8,128)S(1)}, f32[24,384]{1,0:T(8,128)S(1)}, u32[]{:S(2)}, u32[]{:S(2)}) collective-permute-start(f32[24,384]{1,0:T(8,128)S(1)} %get-tuple-element.44), channel_id=1, source_target_pairs={{4,8},{8,4},{12,16},{16,12},{20,24},{24,20},{28,0},{0,28},{5,9},{9... | collective-permute-start | bytes 110600 | tf_op jit(solution)/shard_map/ppermute | solution.py:496
  96.9 3.9 %collective-permute-start.8 = (f32[24,160]{1,0:T(8,128)S(1)}, f32[24,160]{1,0:T(8,128)S(1)}, u32[]{:S(2)}, u32[]{:S(2)}) collective-permute-start(f32[24,160]{1,0:T(8,128)S(1)} %get-tuple-element.47), channel_id=1, source_target_pairs={{0,1},{1,0},{2,3},{3,2},{4,5},{5,4},{6,7},{7,6},{8,9},{9,8},{10,11... | collective-permute-start | bytes 46088 | tf_op jit(solution)/shard_map/ppermute | solution.py:495
  96.9 4.8 %collective-permute-start.9 = (f32[24,160]{1,0:T(8,128)S(1)}, f32[24,160]{1,0:T(8,128)S(1)}, u32[]{:S(2)}, u32[]{:S(2)}) collective-permute-start(f32[24,160]{1,0:T(8,128)S(1)} %get-tuple-element.48), channel_id=1, source_target_pairs={{1,2},{2,1},{3,0},{0,3},{5,6},{6,5},{7,4},{4,7},{9,10},{10,9},{11,... | collective-permute-start | bytes 46088 | tf_op jit(solution)/shard_map/ppermute | solution.py:496
  101.9 1.3 %collective-permute-start.10 = (f32[24,384]{1,0:T(8,128)S(1)}, f32[24,384]{1,0:T(8,128)S(1)}, u32[]{:S(2)}, u32[]{:S(2)}) collective-permute-start(f32[24,384]{1,0:T(8,128)S(1)} %get-tuple-element.50), channel_id=1, source_target_pairs={{0,4},{4,0},{8,12},{12,8},{16,20},{20,16},{24,28},{28,24},{1,5},{5... | collective-permute-start | bytes 110600 | tf_op jit(solution)/shard_map/ppermute | solution.py:495
  102.0 5.2 %collective-permute-start.11 = (f32[24,384]{1,0:T(8,128)S(1)}, f32[24,384]{1,0:T(8,128)S(1)}, u32[]{:S(2)}, u32[]{:S(2)}) collective-permute-start(f32[24,384]{1,0:T(8,128)S(1)} %get-tuple-element.51), channel_id=1, source_target_pairs={{4,8},{8,4},{12,16},{16,12},{20,24},{24,20},{28,0},{0,28},{5,9},{9... | collective-permute-start | bytes 110600 | tf_op jit(solution)/shard_map/ppermute | solution.py:496

commit v3 on v2

--- a/solution.py
+++ b/solution.py
@@ -39,13 +39,24 @@
     for b in range(2):
         scale[:, b * SPEC : b * SPEC + EXT] = (eig[:, None] + eig[None, :]) ** 2
     wide = lambda x: np.pad(x, ((0, 0), (0, FC - x.shape[1])))
-    return np.concatenate([cols, cols.T, scale, wide(rows), wide(rows.T)]).astype(np.float32)
+    return [cols, cols.T, scale, wide(rows), wide(rows.T)]
 
 
 def block_parts(ref):
     cols, cols_t, scale = ref[:FC], ref[FC : 2 * FC], ref[2 * FC : 2 * FC + EXT]
     at = 2 * FC + EXT
     return ref[at : at + FR, :EXT], ref[at + FR : at + FR + EXT, :FR], cols, cols_t, scale
+
+
+def coarse_part(ref, width):
+    at = 2 * FC + 2 * EXT + FR
+    parts = [ref[at + k * width : at + (k + 1) * width] for k in range(-(-width // FC))]
+    return (parts[0] if len(parts) == 1 else jnp.concatenate(parts, axis=1))[:, :width]
+
+
+def constants(nr, nc, width):
+    inverse = coarse_inverse(nr, nc, -(-width // FC) * FC)[:width]
+    return np.concatenate([*block_constants(), *np.split(inverse, inverse.shape[1] // FC, 1)], dtype=np.float32)
 
 
 def coarse_inverse(nr, nc, width):
@@ -101,6 +112,30 @@
     right = jnp.where(j < counts[1] - 1, 320, 256)
     left = jnp.where(j > 0, 320, 384)
     return ((rr < below) | (rr >= above)) & ((ll < right) | (ll >= left))
+
+
+def flat_place(counts):
+    i, j = place()
+    nr, nc = counts
+    shape = table_shape(counts)
+    flat = rows_of(shape) * 128 + lanes_of(shape)
+    device = flat % (nr * nc)
+    return flat, (device // nc + nr - i) % nr, (device % nc + nc - j) % nc
+
+
+def table_shape(counts):
+    return (-(-2 * counts[0] * counts[1] // 1024) * 8, 128)
+
+
+def table_of(values, counts):
+    flat, rows, cols = flat_place(counts)
+    devices = counts[0] * counts[1]
+    own = jnp.where(flat < devices, values[0], jnp.where(flat < 2 * devices, values[1], 0.0))
+    return jnp.where((rows == 0) & (cols == 0), own, 0.0)
+
+
+def as_row(table, width):
+    return jnp.concatenate([table[k : k + 1] for k in range(width // 128)], axis=1)
 
 
 def row_of(pairs):
@@ -229,22 +264,18 @@
     return before, after
 
 
+def next_table(index, a, b):
+    return jnp.where(is_even(index), a, b)[24:, :128]
+
+
 def send(index, a_ref, b_ref, before, after):
     even = is_even(index)
     a_ref[...] = jnp.where(even, after, before)
     b_ref[...] = jnp.where(even, before, after)
 
 
-def begin_kernel(counts, r_hbm, h_hbm, r_ref, h_ref, a_ref, b_ref, sums_ref, sems):
-    copies = [
-        pltpu.make_async_copy(r_hbm, r_ref, sems.at[0]),
-        pltpu.make_async_copy(h_hbm, h_ref, sems.at[1]),
-    ]
-    for copy in copies:
-        copy.start()
-    for copy in copies:
-        copy.wait()
-    r, h = r_ref[...], h_ref[...]
+def begin_kernel(counts, both_ref, a_ref, b_ref):
+    r, h = both_ref[:TR], both_ref[TR:]
     lane = lanes_of((128, 128))
     packed = jnp.where(
         lane < 16,
@@ -256,13 +287,19 @@
         ),
     )
     turned = packed.T
-    send(lax.axis_index("col"), a_ref, b_ref, turned[:32], turned[96:])
-    sums_ref[...] = row_of([core_sums(r)])
-
-
-def widen_kernel(counts, r_ref, h_ref, ga_ref, gb_ref, r3_ref, h3_ref, a_ref, b_ref):
-    i, j = place()
-    from_left, from_right = sides(j, counts[1], ga_ref[...], gb_ref[...])
+    table = table_of(core_sums(r), counts)
+    send(
+        lax.axis_index("col"),
+        a_ref,
+        b_ref,
+        jnp.concatenate([turned[:32], table], axis=0),
+        jnp.concatenate([turned[96:], table], axis=0),
+    )
+
+
+def widen_kernel(counts, both_ref, ga_ref, gb_ref, r3_ref, h3_ref, table_ref, a_ref, b_ref):
+    i, j = place()
+    from_left, from_right = sides(j, counts[1], ga_ref[:32], gb_ref[:32])
     turned = jnp.concatenate([from_right, jnp.zeros((64, 128), jnp.float32), from_left], axis=0)
     back = turned.T
     lane = lanes_of((128, 128))
@@ -273,13 +310,17 @@
     )
     r3_ref[...] = r3
     h3_ref[...] = h3
-    r, h = r_ref[...], h_ref[...]
+    r, h = both_ref[:TR], both_ref[TR:]
+    table = table_of(core_sums(r), counts) + ga_ref[32:] + gb_ref[32:]
+    table_ref[...] = table
+    wide = jnp.concatenate([table, jnp.zeros((table.shape[0], FC - 128), jnp.float32)], axis=1)
 
     def strip(r_rows, h_rows):
         return jnp.concatenate(
             [
                 jnp.concatenate([r[r_rows], r3[r_rows]], axis=1),
                 jnp.concatenate([h[h_rows], h3[h_rows]], axis=1),
+                wide,
             ],
             axis=0,
         )
@@ -288,12 +329,12 @@
 
 
 def first_kernel(
-    counts, r_ref, h_ref, r3_ref, h3_ref, ga_ref, gb_ref, basis_ref, y_ref, m_ref, a_ref, b_ref
+    counts, both_ref, r3_ref, h3_ref, ga_ref, gb_ref, basis_ref, y_ref, m_ref, a_ref, b_ref
 ):
     i, j = place()
-    above, below = sides(i, counts[0], ga_ref[...], gb_ref[...])
-    r = jnp.concatenate([r_ref[...], r3_ref[...]], axis=1)
-    h = jnp.concatenate([h_ref[...], h3_ref[...]], axis=1)
+    above, below = sides(i, counts[0], ga_ref[:24], gb_ref[:24])
+    r = jnp.concatenate([both_ref[:TR], r3_ref[...]], axis=1)
+    h = jnp.concatenate([both_ref[TR:], h3_ref[...]], axis=1)
     wide = jnp.concatenate([r, below[:8], jnp.zeros((16, FC), jnp.float32), above[:8]], axis=0)
     tall = jnp.concatenate([h, below[8:], above[8:]], axis=0)
     mobility = tall * tall * tall
@@ -304,11 +345,23 @@
     send(j, a_ref, b_ref, *pack_columns(y))
 
 
-def columns_kernel(counts, y_ref, ga_ref, gb_ref, out_ref, a_ref, b_ref):
-    i, j = place()
-    y = add_columns(y_ref[...], *sides(j, counts[1], ga_ref[...], gb_ref[...]))
+def columns_kernel(counts, y_ref, ga_ref, gb_ref, *refs):
+    i, j = place()
+    y = add_columns(y_ref[...], *sides(j, counts[1], ga_ref[:24], gb_ref[:24]))
+    strips = pack_rows(y)
+    if len(refs) == 5:
+        table_ref, out_ref, table_out, a_ref, b_ref = refs
+        cols = flat_place(counts)[2]
+        table = table_ref[...] + jnp.where(
+            cols % 4 == 2, next_table(j, ga_ref[...], gb_ref[...]), 0.0
+        )
+        table_out[...] = table
+        wide = jnp.concatenate([table, jnp.zeros((table.shape[0], FC - 128), jnp.float32)], axis=1)
+        strips = [jnp.concatenate([x, wide], axis=0) for x in strips]
+    else:
+        out_ref, a_ref, b_ref = refs
     out_ref[...] = y
-    send(i, a_ref, b_ref, *pack_rows(y))
+    send(i, a_ref, b_ref, *strips)
 
 
 def second_kernel(
@@ -318,28 +371,31 @@
     m_ref,
     ga_ref,
     gb_ref,
-    sums_ref,
-    r_ref,
-    inverse_ref,
+    table_ref,
+    both_ref,
     basis_ref,
     z_ref,
     w_ref,
     y2_ref,
+    table_out,
     stats_ref,
     a_ref,
     b_ref,
 ):
     i, j = place()
-    s = add_rows(y_ref[...], *sides(i, counts[0], ga_ref[...], gb_ref[...]))
+    s = add_rows(y_ref[...], *sides(i, counts[0], ga_ref[:24], gb_ref[:24]))
     mask = grid_mask((FR, FC), counts)
     s = jnp.where(mask, s, 0.0)
-    c0 = gathered(sums_ref[...], width)[:1]
-    coarse = spread(coarse_values(c0, inverse_ref[...]), counts)
+    rows = flat_place(counts)[1]
+    table = table_ref[...] + jnp.where(rows % 4 == 2, next_table(i, ga_ref[...], gb_ref[...]), 0.0)
+    table_out[...] = table
+    c0 = as_row(table, width)
+    coarse = spread(coarse_values(c0, coarse_part(basis_ref, width)), counts)
     mobility = m_ref[...]
     flow = mobility * (lap(s) + lap(coarse))
     z = s + coarse
     w = jnp.where(mask, DAMP * z + lap(flow), 0.0) * SHRINK
-    zt, wt, rt, mt = z[:128, :256], w[:128, :256], r_ref[...], mobility[:128, :256]
+    zt, wt, rt, mt = z[:128, :256], w[:128, :256], both_ref[:TR], mobility[:128, :256]
     z_ref[...] = zt
     w_ref[...] = wt
     means = [x / (SUB * SUB) for x in core_sums(mt)]
@@ -376,7 +432,7 @@
 
 
 def dots_kernel(
-    counts, y_ref, m_ref, ga_ref, gb_ref, r_ref, w_ref, stats_ref, q_ref, v_ref, stats_out
+    counts, y_ref, m_ref, ga_ref, gb_ref, both_ref, w_ref, stats_ref, q_ref, v_ref, stats_out
 ):
     i, j = place()
     q = add_rows(y_ref[...], *sides(i, counts[0], ga_ref[...], gb_ref[...]))
@@ -387,7 +443,7 @@
     v_ref[...] = vt
     rest = [
         core_sums(vt),
-        core_sums(r_ref[...] * qt),
+        core_sums(both_ref[:TR] * qt),
         core_sums(w_ref[...] * qt),
         core_sums(vt * qt),
     ]
@@ -400,10 +456,10 @@
     counts,
     width,
     stats_ref,
-    sums_ref,
-    inverse_ref,
+    table_ref,
+    basis_ref,
     m_ref,
-    r_ref,
+    both_ref,
     z_ref,
     w_ref,
     q_ref,
@@ -420,8 +476,8 @@
         return jnp.sum(x, axis=1, keepdims=True)
 
     rz, zw, rq, wq, qv = (whole(st[k]) for k in (0, 1, 12, 13, 14))
-    c0, c1, sums_v = gathered(sums_ref[...], width)[:1], st[2], st[11]
-    g = coarse_values(c1, inverse_ref[...])
+    c0, c1, sums_v = as_row(table_ref[...], width), st[2], st[11]
+    g = coarse_values(c1, coarse_part(basis_ref, width))
     lane = lanes_of((1, width))
     cell = lane < 2 * devices
     on_left = lane < devices
@@ -461,16 +517,16 @@
     v = v_ref[...] + image[:128, :256]
     z, w = z_ref[...], w_ref[...]
     solution_ref[...] = (a * SHRINK) * z + a1 * (beta1 * z - a * y)
-    residual_ref[...] = r_ref[...] - a * w - a1 * ((beta1 * (1.0 / SHRINK)) * w - a * v)
-
-
-def call(kernel, outs, *args, **options):
+    residual_ref[...] = both_ref[:TR] - a * w - a1 * ((beta1 * (1.0 / SHRINK)) * w - a * v)
+
+
+def call(kernel, outs, *args, flops=10**9):
     shapes = [jax.ShapeDtypeStruct(s, jnp.float32) for s in outs]
     return pl.pallas_call(
         kernel,
         out_shape=shapes,
         compiler_params=pltpu.CompilerParams(vmem_limit_bytes=48 * 1024 * 1024),
-        **options,
+        cost_estimate=pl.CostEstimate(flops=flops, bytes_accessed=10**6, transcendentals=0),
     )(*args)
 
 
@@ -485,9 +541,9 @@
     nr, nc = counts
     devices = nr * nc
     width = max(128, devices * 2)
-    basis = jnp.asarray(block_constants())
-    inverse = jnp.asarray(coarse_inverse(nr, 2 * nc, width))
-    both = ("row", "col")
+    basis = jnp.asarray(constants(nr, 2 * nc, width))
+    both_axes = ("row", "col")
+    depth = table_shape(counts)[0]
 
     def swap(a, b, axis):
         count = lax.axis_size(axis)
@@ -496,51 +552,55 @@
             lax.ppermute(b, axis, pairs_from(count, 1)),
         )
 
-    r, h, a, b, sums = call(
-        functools.partial(begin_kernel, counts),
-        [(TR, TC)] * 2 + [(32, 128)] * 2 + [(1, 128)],
-        noise,
-        height,
-        in_specs=[pl.BlockSpec(memory_space=pltpu.HBM)] * 2,
-        scratch_shapes=[pltpu.SemaphoreType.DMA((2,))],
-    )
-    sums = lax.all_gather(sums, both, axis=0, tiled=True)
+    first = lax.broadcasted_iota(jnp.int32, (2, TR, TC), 0) == 0
+    both = jnp.where(first, noise[None], height[None]).reshape(2 * TR, TC)
+    a, b = call(functools.partial(begin_kernel, counts), [(32 + depth, 128)] * 2, both)
     ga, gb = swap(a, b, "col")
-    r3, h3, a, b = call(
+    r3, h3, table, a, b = call(
         functools.partial(widen_kernel, counts),
-        [(128, 128)] * 2 + [(24, FC)] * 2,
-        r,
-        h,
+        [(128, 128)] * 2 + [(depth, 128)] + [(24 + depth, FC)] * 2,
+        both,
         ga,
         gb,
     )
     ga, gb = swap(a, b, "row")
+    table = table + ga[24:, :128] + gb[24:, :128]
     y, m, a, b = call(
         functools.partial(first_kernel, counts),
         [(FR, FC)] * 2 + [(24, FR)] * 2,
-        r,
-        h,
+        both,
         r3,
         h3,
         ga,
         gb,
         basis,
     )
-    ga, gb = swap(a, b, "col")
-    y, a, b = call(
-        functools.partial(columns_kernel, counts), [(FR, FC)] + [(24, FC)] * 2, y, ga, gb
+    for axis, count in (("row", nr), ("col", nc)):
+        step = count // 2
+        while step >= 4:
+            shift = [(k, (k + step) % count) for k in range(count)]
+            table = table + lax.ppermute(table, axis, shift)
+            step //= 2
+    wide = jnp.pad(table, ((0, 0), (0, FR - 128)))
+    ga, gb = swap(*(jnp.concatenate([x, wide], axis=0) for x in (a, b)), "col")
+    y, table, a, b = call(
+        functools.partial(columns_kernel, counts),
+        [(FR, FC), (depth, 128)] + [(24 + depth, FC)] * 2,
+        y,
+        ga,
+        gb,
+        table,
     )
     ga, gb = swap(a, b, "row")
-    z, w, y, stats, a, b = call(
+    z, w, y, table, stats, a, b = call(
         functools.partial(second_kernel, counts, width),
-        [(TR, TC)] * 2 + [(FR, FC), (1, 128)] + [(24, FR)] * 2,
+        [(TR, TC)] * 2 + [(FR, FC), (depth, 128), (1, 128)] + [(24, FR)] * 2,
         y,
         m,
         ga,
         gb,
-        sums,
-        r,
-        inverse,
+        table,
+        both,
         basis,
     )
     ga, gb = swap(a, b, "col")
@@ -555,20 +615,20 @@
         m,
         ga,
         gb,
-        r,
+        both,
         w,
         stats,
     )
-    stats = lax.all_to_all(stats, both, 0, 0, tiled=True)
+    stats = lax.all_to_all(stats, both_axes, 0, 0, tiled=True)
     return tuple(
         call(
             functools.partial(end_kernel, counts, width),
             [(TR, TC)] * 2,
             stats,
-            sums,
-            inverse,
+            table,
+            basis,
             m,
-            r,
+            both,
             z,
             w,
             q,

time: 119 us -> 56.6 us (0.48)
  blocking collectives: 75.5 us -> 8.86 us
  waiting for transfers between devices: 16.9 us -> 21.2 us
  local copies, waits for them, and re-layouts: 3.35 us -> 0.08 us
  starting transfers between devices: 13.9 us -> 17.1 us
    all_gather x1 -> x0, blocking collectives: 66.2 us -> none  [body(): sums = lax.all_gather(sums, both, axis=0, tiled=True)]
    ppermute x6, waiting for transfers between devices: 11.1 us -> 16.3 us  [swap(): lax.ppermute(b, axis, pairs_from(count, 1))]
    unnamed x10 -> x2, local copies, waits for them, and re-layouts: 3.35 us -> 0.01 us
    ppermute x6, waiting for transfers between devices: 5.82 us -> 3.03 us  [swap(): lax.ppermute(a, axis, pairs_from(count, 0))]
    ppermute x6, starting transfers between devices: 3.87 us -> 6.25 us  [swap(): lax.ppermute(a, axis, pairs_from(count, 0))]
    ppermute x0 -> x1, waiting for transfers between devices: none -> 1.8 us  [body(): table = table + lax.ppermute(table, axis, shift)]
  transfers between devices with their start and end apart: 12 -> 13, of which waited for: 9 -> 11; matrix products, arithmetic and copies ran while one was open for 0% -> 0% of each run, Pallas kernels for 0% -> 4%
where the time goes in v3:
time: 56.6 us; the launch traced here: 56.4 us
  waiting for transfers between devices  21.2 us (37%)
  starting transfers between devices  17.1 us (30%)
  blocking collectives  8.86 us (16%)
  Pallas kernels  7.47 us (13%)
  other arithmetic  1.09 us (2%)
  between operations  0.73 us (1%)
    ppermute x6, waiting for transfers between devices, swap(): lax.ppermute(b, axis, pairs_from(count, 1))  16.3 us
    ppermute x6, starting transfers between devices, swap(): lax.ppermute(b, axis, pairs_from(count, 1))  10.2 us
    all_to_all x1, blocking collectives, body(): stats = lax.all_to_all(stats, both_axes, 0, 0, tiled=True)  8.86 us
    pallas_call x8, Pallas kernels, call(): pl.pallas_call(kernel, out_shape=shapes, compiler_params=pltpu.CompilerPa...  7.47 us
    ppermute x6, starting transfers between devices, swap(): lax.ppermute(a, axis, pairs_from(count, 0))  6.25 us
    ppermute x6, waiting for transfers between devices, swap(): lax.ppermute(a, axis, pairs_from(count, 0))  3.03 us
    ppermute x1, waiting for transfers between devices, body(): table = table + lax.ppermute(table, axis, shift)  1.8 us
  transfers between devices with their start and end apart: 13, of which 11 were waited for; matrix products, arithmetic and copies ran while one was open for 0% of the time, Pallas kernels for 4%

profile of v3, /device:TPU:0, one launch (start us, length us, event | category | flops | bytes accessed | tf_op | source)
XLA Modules:
  0.0 56.4 jit_solution(1156546504394022438)
XLA Ops:
  0.6 0.1 broadcast_bitcast_fusion
  0.7 1.1 %bitcast_select_fusion.both_ref = f32[256,256]{1,0:T(8,128)S(1)} fusion(f32[128,256]{1,0:T(8,128)} %param.3, f32[128,256]{1,0:T(8,128)} %param.4, pred[256]{0:T(512)(128)(4,1)S(1)} %broadcast_bitcast_fusion), kind=kLoop, calls=%fused_computation | loop fusion | flops 65536 | bytes 524544 | tf_op jit(solution)/shard_map/jit(_where)/select_n | solution.py:556
  1.8 0.2 shard_map.50
  2.0 0.0 copy-start
  2.0 3.0 %collective-permute-start = (f32[40,128]{1,0:T(8,128)S(1)}, f32[40,128]{1,0:T(8,128)S(1)}, u32[]{:S(2)}, u32[]{:S(2)}) collective-permute-start(f32[40,128]{1,0:T(8,128)S(1)} %get-tuple-element.30), channel_id=1, source_target_pairs={{0,1},{1,0},{2,3},{3,2},{4,5},{5,4},{6,7},{7,6},{8,9},{9,8},{10,11... | collective-permute-start | bytes 61448 | tf_op jit(solution)/shard_map/ppermute | solution.py:551
  5.0 1.5 %collective-permute-start.1 = (f32[40,128]{1,0:T(8,128)S(1)}, f32[40,128]{1,0:T(8,128)S(1)}, u32[]{:S(2)}, u32[]{:S(2)}) collective-permute-start(f32[40,128]{1,0:T(8,128)S(1)} %get-tuple-element.31), channel_id=1, source_target_pairs={{1,2},{2,1},{3,0},{0,3},{5,6},{6,5},{7,4},{4,7},{9,10},{10,9},{11,... | collective-permute-start | bytes 61448 | tf_op jit(solution)/shard_map/ppermute | solution.py:552
  6.5 0.3 collective-permute-done.ga_ref
  6.7 2.9 %collective-permute-done.1.gb_ref = f32[40,128]{1,0:T(8,128)S(1)} collective-permute-done((f32[40,128]{1,0:T(8,128)S(1)}, f32[40,128]{1,0:T(8,128)S(1)}, u32[]{:S(2)}, u32[]{:S(2)}) %collective-permute-start.1) | collective-permute-done | bytes 20512 | tf_op jit(solution)/shard_map/ppermute | solution.py:552
  9.7 0.2 shard_map.51
  9.8 0.1 collective-permute-start.2
  9.9 3.7 %collective-permute-start.3 = (f32[32,384]{1,0:T(8,128)S(1)}, f32[32,384]{1,0:T(8,128)S(1)}, u32[]{:S(2)}, u32[]{:S(2)}) collective-permute-start(f32[32,384]{1,0:T(8,128)S(1)} %get-tuple-element.35), channel_id=1, source_target_pairs={{4,8},{8,4},{12,16},{16,12},{20,24},{24,20},{28,0},{0,28},{5,9},{9... | collective-permute-start | bytes 147464 | tf_op jit(solution)/shard_map/ppermute | solution.py:552
  13.6 0.0 collective-permute-done.2.ga_ref
  13.6 1.9 %collective-permute-done.3.gb_ref = f32[32,384]{1,0:T(8,128)S(1)} collective-permute-done((f32[32,384]{1,0:T(8,128)S(1)}, f32[32,384]{1,0:T(8,128)S(1)}, u32[]{:S(2)}, u32[]{:S(2)}) %collective-permute-start.3) | collective-permute-done | bytes 49184 | tf_op jit(solution)/shard_map/ppermute | solution.py:552
  15.5 0.6 %collective-permute-start.4 = (f32[8,128]{1,0:T(8,128)S(1)}, f32[8,128]{1,0:T(8,128)S(1)}, u32[]{:S(2)}, u32[]{:S(2)}) collective-permute-start(f32[8,128]{1,0:T(8,128)S(1)} %slice_add_fusion), channel_id=1, source_target_pairs={{0,16},{4,20},{8,24},{12,28},{16,0},{20,4},{24,8},{28,12},{1,17},{... | collective-permute-start | bytes 12296 | tf_op jit(solution)/shard_map/ppermute | solution.py:582
  16.1 0.0 copy-done
  16.1 2.1 %shard_map.52 = (f32[160,384]{1,0:T(8,128)S(1)}, f32[160,384]{1,0:T(8,128)S(1)}, f32[24,160]{1,0:T(8,128)S(1)}, f32[24,160]{1,0:T(8,128)S(1)}) custom-call(f32[256,256]{1,0:T(8,128)S(1)} %bitcast_select_fusion.both_ref, f32[128,128]{1,0:T(8,128)S(1)} %get-tuple-element.32.r3_ref, f32[128,128]{1,0:T(8,128)S(1)} %get-tuple-element.33.h3_ref, ...), custom_call_target="tpu_custom_call" | custom-call | flops 1000000000 | bytes 1000000 | tf_op jit(solution)/shard_map/pallas_call | solution.py:525
  18.2 1.8 %collective-permute-done.4 = f32[8,128]{1,0:T(8,128)S(1)} collective-permute-done((f32[8,128]{1,0:T(8,128)S(1)}, f32[8,128]{1,0:T(8,128)S(1)}, u32[]{:S(2)}, u32[]{:S(2)}) %collective-permute-start.4) | collective-permute-done | bytes 4128 | tf_op jit(solution)/shard_map/ppermute | solution.py:582
  20.0 1.6 %collective-permute-start.6 = (f32[32,160]{1,0:T(8,128)S(1)}, f32[32,160]{1,0:T(8,128)S(1)}, u32[]{:S(2)}, u32[]{:S(2)}) collective-permute-start(f32[32,160]{1,0:T(8,128)S(1)} %get-tuple-element.58), channel_id=1, source_target_pairs={{1,2},{2,1},{3,0},{0,3},{5,6},{6,5},{7,4},{4,7},{9,10},{10,9},{11,... | collective-permute-start | bytes 61448 | tf_op jit(solution)/shard_map/ppermute | solution.py:552
  21.6 1.5 %collective-permute-start.5 = (f32[32,160]{1,0:T(8,128)S(1)}, f32[32,160]{1,0:T(8,128)S(1)}, u32[]{:S(2)}, u32[]{:S(2)}) collective-permute-start(f32[32,160]{1,0:T(8,128)S(1)} %get-tuple-element.59), channel_id=1, source_target_pairs={{0,1},{1,0},{2,3},{3,2},{4,5},{5,4},{6,7},{7,6},{8,9},{9,8},{10,11... | collective-permute-start | bytes 61448 | tf_op jit(solution)/shard_map/ppermute | solution.py:551
  23.1 1.8 %collective-permute-done.6.gb_ref = f32[32,160]{1,0:T(8,128)S(1)} collective-permute-done((f32[32,160]{1,0:T(8,128)S(1)}, f32[32,160]{1,0:T(8,128)S(1)}, u32[]{:S(2)}, u32[]{:S(2)}) %collective-permute-start.6) | collective-permute-done | bytes 20512 | tf_op jit(solution)/shard_map/ppermute | solution.py:552
  24.9 0.6 %collective-permute-done.5.ga_ref = f32[32,160]{1,0:T(8,128)S(1)} collective-permute-done((f32[32,160]{1,0:T(8,128)S(1)}, f32[32,160]{1,0:T(8,128)S(1)}, u32[]{:S(2)}, u32[]{:S(2)}) %collective-permute-start.5) | collective-permute-done | bytes 20512 | tf_op jit(solution)/shard_map/ppermute | solution.py:551
  25.5 0.2 shard_map.53
  25.7 0.1 collective-permute-start.7
  25.8 2.1 %collective-permute-start.8 = (f32[32,384]{1,0:T(8,128)S(1)}, f32[32,384]{1,0:T(8,128)S(1)}, u32[]{:S(2)}, u32[]{:S(2)}) collective-permute-start(f32[32,384]{1,0:T(8,128)S(1)} %get-tuple-element.43), channel_id=1, source_target_pairs={{4,8},{8,4},{12,16},{16,12},{20,24},{24,20},{28,0},{0,28},{5,9},{9... | collective-permute-start | bytes 147464 | tf_op jit(solution)/shard_map/ppermute | solution.py:552
  27.9 0.0 collective-permute-done.7.ga_ref
  27.9 3.3 %collective-permute-done.8.gb_ref = f32[32,384]{1,0:T(8,128)S(1)} collective-permute-done((f32[32,384]{1,0:T(8,128)S(1)}, f32[32,384]{1,0:T(8,128)S(1)}, u32[]{:S(2)}, u32[]{:S(2)}) %collective-permute-start.8) | collective-permute-done | bytes 49184 | tf_op jit(solution)/shard_map/ppermute | solution.py:552
  31.2 2.8 %shard_map.54 = (f32[128,256]{1,0:T(8,128)S(1)}, f32[128,256]{1,0:T(8,128)S(1)}, f32[160,384]{1,0:T(8,128)S(1)}, f32[8,128]{1,0:T(8,128)S(1)}, f32[1,128]{1,0:T(...) custom-call(f32[160,384]{1,0:T(8,128)S(1)} %get-tuple-element.40.y_ref, ...), custom_call_target="tpu_custom_call" | custom-call | flops 1000000000 | bytes 1000000 | tf_op jit(solution)/shard_map/pallas_call | solution.py:525
  34.0 1.5 %collective-permute-start.9 = (f32[24,160]{1,0:T(8,128)S(1)}, f32[24,160]{1,0:T(8,128)S(1)}, u32[]{:S(2)}, u32[]{:S(2)}) collective-permute-start(f32[24,160]{1,0:T(8,128)S(1)} %get-tuple-element.46), channel_id=1, source_target_pairs={{0,1},{1,0},{2,3},{3,2},{4,5},{5,4},{6,7},{7,6},{8,9},{9,8},{10,11... | collective-permute-start | bytes 46088 | tf_op jit(solution)/shard_map/ppermute | solution.py:551
  35.5 0.9 %collective-permute-start.10 = (f32[24,160]{1,0:T(8,128)S(1)}, f32[24,160]{1,0:T(8,128)S(1)}, u32[]{:S(2)}, u32[]{:S(2)}) collective-permute-start(f32[24,160]{1,0:T(8,128)S(1)} %get-tuple-element.47), channel_id=1, source_target_pairs={{1,2},{2,1},{3,0},{0,3},{5,6},{6,5},{7,4},{4,7},{9,10},{10,9},{11,... | collective-permute-start | bytes 46088 | tf_op jit(solution)/shard_map/ppermute | solution.py:552
  36.4 1.4 %collective-permute-done.9.ga_ref = f32[24,160]{1,0:T(8,128)S(1)} collective-permute-done((f32[24,160]{1,0:T(8,128)S(1)}, f32[24,160]{1,0:T(8,128)S(1)}, u32[]{:S(2)}, u32[]{:S(2)}) %collective-permute-start.9) | collective-permute-done | bytes 15392 | tf_op jit(solution)/shard_map/ppermute | solution.py:551
  37.9 2.4 %collective-permute-done.10.gb_ref = f32[24,160]{1,0:T(8,128)S(1)} collective-permute-done((f32[24,160]{1,0:T(8,128)S(1)}, f32[24,160]{1,0:T(8,128)S(1)}, u32[]{:S(2)}, u32[]{:S(2)}) %collective-permute-start.10) | collective-permute-done | bytes 15392 | tf_op jit(solution)/shard_map/ppermute | solution.py:552
  40.3 0.2 shard_map.55
  40.4 0.1 collective-permute-start.11
  40.5 0.5 collective-permute-start.12
  41.0 0.7 %collective-permute-done.11.ga_ref = f32[24,384]{1,0:T(8,128)S(1)} collective-permute-done((f32[24,384]{1,0:T(8,128)S(1)}, f32[24,384]{1,0:T(8,128)S(1)}, u32[]{:S(2)}, u32[]{:S(2)}) %collective-permute-start.11) | collective-permute-done | bytes 36896 | tf_op jit(solution)/shard_map/ppermute | solution.py:551
  41.7 4.0 %collective-permute-done.12.gb_ref = f32[24,384]{1,0:T(8,128)S(1)} collective-permute-done((f32[24,384]{1,0:T(8,128)S(1)}, f32[24,384]{1,0:T(8,128)S(1)}, u32[]{:S(2)}, u32[]{:S(2)}) %collective-permute-start.12) | collective-permute-done | bytes 36896 | tf_op jit(solution)/shard_map/ppermute | solution.py:552
  45.8 0.4 shard_map.56
  46.2 8.9 %all_to_all.11 = f32[32,1,128]{2,1,0:T(1,128)S(1)} all-to-all(f32[32,1,128]{2,1,0:T(1,128)S(1)} %bitcast.11), channel_id=1, replica_groups=mesh['row'=8,'col'=4] {'row','col'}, dimensions={0} | all-to-all | bytes 32768 | tf_op jit(solution)/shard_map/all_to_all | solution.py:622
  55.1 1.4 %shard_map.57 = (f32[128,256]{1,0:T(8,128)}, f32[128,256]{1,0:T(8,128)}) custom-call(f32[32,128]{1,0:T(8,128)S(1)} %bitcast.10, f32[8,128]{1,0:T(8,128)S(1)} %get-tuple-element.54.table_ref, f32[1344,384]{1,0:T(8,128)S(1)} %copy-done, f32[160,384]{1,0:T(8,128)S(1)} %get-tuple-element.41.m_ref, f32[256,256]{1,0:T(8,128)S(1)} %bitcast_select_fusion.both_ref, ...), custom_call_target="tpu_custom_call" | custom-call | flops 1000000000 | bytes 1000000 | tf_op jit(solution)/shard_map/pallas_call | solution.py:525
  (4 shorter events, 0.0 us)
Async XLA Ops:
  2.0 14.2 %copy-start = (f32[1344,384]{1,0:T(8,128)S(1)}, f32[1344,384]{1,0:T(8,128)}, u32[]{:S(2)}) copy-start(f32[1344,384]{1,0:T(8,128)} %constant.7.clone.basis_ref) | copy-start | bytes 6193156
  2.0 4.8 %collective-permute-start = (f32[40,128]{1,0:T(8,128)S(1)}, f32[40,128]{1,0:T(8,128)S(1)}, u32[]{:S(2)}, u32[]{:S(2)}) collective-permute-start(f32[40,128]{1,0:T(8,128)S(1)} %get-tuple-element.30), channel_id=1, source_target_pairs={{0,1},{1,0},{2,3},{3,2},{4,5},{5,4},{6,7},{7,6},{8,9},{9,8},{10,11... | collective-permute-start | bytes 61448 | tf_op jit(solution)/shard_map/ppermute | solution.py:551
  5.0 4.7 %collective-permute-start.1 = (f32[40,128]{1,0:T(8,128)S(1)}, f32[40,128]{1,0:T(8,128)S(1)}, u32[]{:S(2)}, u32[]{:S(2)}) collective-permute-start(f32[40,128]{1,0:T(8,128)S(1)} %get-tuple-element.31), channel_id=1, source_target_pairs={{1,2},{2,1},{3,0},{0,3},{5,6},{6,5},{7,4},{4,7},{9,10},{10,9},{11,... | collective-permute-start | bytes 61448 | tf_op jit(solution)/shard_map/ppermute | solution.py:552
  9.8 3.8 %collective-permute-start.2 = (f32[32,384]{1,0:T(8,128)S(1)}, f32[32,384]{1,0:T(8,128)S(1)}, u32[]{:S(2)}, u32[]{:S(2)}) collective-permute-start(f32[32,384]{1,0:T(8,128)S(1)} %get-tuple-element.34), channel_id=1, source_target_pairs={{0,4},{4,0},{8,12},{12,8},{16,20},{20,16},{24,28},{28,24},{1,5},{5... | collective-permute-start | bytes 147464 | tf_op jit(solution)/shard_map/ppermute | solution.py:551
  9.9 5.6 %collective-permute-start.3 = (f32[32,384]{1,0:T(8,128)S(1)}, f32[32,384]{1,0:T(8,128)S(1)}, u32[]{:S(2)}, u32[]{:S(2)}) collective-permute-start(f32[32,384]{1,0:T(8,128)S(1)} %get-tuple-element.35), channel_id=1, source_target_pairs={{4,8},{8,4},{12,16},{16,12},{20,24},{24,20},{28,0},{0,28},{5,9},{9... | collective-permute-start | bytes 147464 | tf_op jit(solution)/shard_map/ppermute | solution.py:552
  15.5 4.5 %collective-permute-start.4 = (f32[8,128]{1,0:T(8,128)S(1)}, f32[8,128]{1,0:T(8,128)S(1)}, u32[]{:S(2)}, u32[]{:S(2)}) collective-permute-start(f32[8,128]{1,0:T(8,128)S(1)} %slice_add_fusion), channel_id=1, source_target_pairs={{0,16},{4,20},{8,24},{12,28},{16,0},{20,4},{24,8},{28,12},{1,17},{... | collective-permute-start | bytes 12296 | tf_op jit(solution)/shard_map/ppermute | solution.py:582
  20.0 4.9 %collective-permute-start.6 = (f32[32,160]{1,0:T(8,128)S(1)}, f32[32,160]{1,0:T(8,128)S(1)}, u32[]{:S(2)}, u32[]{:S(2)}) collective-permute-start(f32[32,160]{1,0:T(8,128)S(1)} %get-tuple-element.58), channel_id=1, source_target_pairs={{1,2},{2,1},{3,0},{0,3},{5,6},{6,5},{7,4},{4,7},{9,10},{10,9},{11,... | collective-permute-start | bytes 61448 | tf_op jit(solution)/shard_map/ppermute | solution.py:552
  21.6 3.9 %collective-permute-start.5 = (f32[32,160]{1,0:T(8,128)S(1)}, f32[32,160]{1,0:T(8,128)S(1)}, u32[]{:S(2)}, u32[]{:S(2)}) collective-permute-start(f32[32,160]{1,0:T(8,128)S(1)} %get-tuple-element.59), channel_id=1, source_target_pairs={{0,1},{1,0},{2,3},{3,2},{4,5},{5,4},{6,7},{7,6},{8,9},{9,8},{10,11... | collective-permute-start | bytes 61448 | tf_op jit(solution)/shard_map/ppermute | solution.py:551
  25.7 2.2 %collective-permute-start.7 = (f32[32,384]{1,0:T(8,128)S(1)}, f32[32,384]{1,0:T(8,128)S(1)}, u32[]{:S(2)}, u32[]{:S(2)}) collective-permute-start(f32[32,384]{1,0:T(8,128)S(1)} %get-tuple-element.42), channel_id=1, source_target_pairs={{0,4},{4,0},{8,12},{12,8},{16,20},{20,16},{24,28},{28,24},{1,5},{5... | collective-permute-start | bytes 147464 | tf_op jit(solution)/shard_map/ppermute | solution.py:551
  25.8 5.4 %collective-permute-start.8 = (f32[32,384]{1,0:T(8,128)S(1)}, f32[32,384]{1,0:T(8,128)S(1)}, u32[]{:S(2)}, u32[]{:S(2)}) collective-permute-start(f32[32,384]{1,0:T(8,128)S(1)} %get-tuple-element.43), channel_id=1, source_target_pairs={{4,8},{8,4},{12,16},{16,12},{20,24},{24,20},{28,0},{0,28},{5,9},{9... | collective-permute-start | bytes 147464 | tf_op jit(solution)/shard_map/ppermute | solution.py:552
  34.0 3.9 %collective-permute-start.9 = (f32[24,160]{1,0:T(8,128)S(1)}, f32[24,160]{1,0:T(8,128)S(1)}, u32[]{:S(2)}, u32[]{:S(2)}) collective-permute-start(f32[24,160]{1,0:T(8,128)S(1)} %get-tuple-element.46), channel_id=1, source_target_pairs={{0,1},{1,0},{2,3},{3,2},{4,5},{5,4},{6,7},{7,6},{8,9},{9,8},{10,11... | collective-permute-start | bytes 46088 | tf_op jit(solution)/shard_map/ppermute | solution.py:551
  35.5 4.7 %collective-permute-start.10 = (f32[24,160]{1,0:T(8,128)S(1)}, f32[24,160]{1,0:T(8,128)S(1)}, u32[]{:S(2)}, u32[]{:S(2)}) collective-permute-start(f32[24,160]{1,0:T(8,128)S(1)} %get-tuple-element.47), channel_id=1, source_target_pairs={{1,2},{2,1},{3,0},{0,3},{5,6},{6,5},{7,4},{4,7},{9,10},{10,9},{11,... | collective-permute-start | bytes 46088 | tf_op jit(solution)/shard_map/ppermute | solution.py:552
  40.4 1.3 %collective-permute-start.11 = (f32[24,384]{1,0:T(8,128)S(1)}, f32[24,384]{1,0:T(8,128)S(1)}, u32[]{:S(2)}, u32[]{:S(2)}) collective-permute-start(f32[24,384]{1,0:T(8,128)S(1)} %get-tuple-element.49), channel_id=1, source_target_pairs={{0,4},{4,0},{8,12},{12,8},{16,20},{20,16},{24,28},{28,24},{1,5},{5... | collective-permute-start | bytes 110600 | tf_op jit(solution)/shard_map/ppermute | solution.py:551
  40.5 5.2 %collective-permute-start.12 = (f32[24,384]{1,0:T(8,128)S(1)}, f32[24,384]{1,0:T(8,128)S(1)}, u32[]{:S(2)}, u32[]{:S(2)}) collective-permute-start(f32[24,384]{1,0:T(8,128)S(1)} %get-tuple-element.50), channel_id=1, source_target_pairs={{4,8},{8,4},{12,16},{16,12},{20,24},{24,20},{28,0},{0,28},{5,9},{9... | collective-permute-start | bytes 110600 | tf_op jit(solution)/shard_map/ppermute | solution.py:552

commit v4 on v3

--- a/solution.py
+++ b/solution.py
@@ -264,8 +264,29 @@
     return before, after
 
 
-def next_table(index, a, b):
-    return jnp.where(is_even(index), a, b)[24:, :128]
+def side_columns(ref, count, depth):
+    j = lax.axis_index("col")
+    left = ref[jnp.maximum(j - 1, 0), :depth]
+    right = ref[jnp.minimum(j + 1, count - 1), :depth]
+    return jnp.where(j > 0, left, 0.0), jnp.where(j < count - 1, right, 0.0)
+
+
+def send_columns(ref, to_left, to_right):
+    j = lax.axis_index("col")
+    for k in range(ref.shape[0]):
+        ref[k] = jnp.where(k > j, to_right, to_left)
+
+
+def row_tables(index, nr, rows, a, b):
+    even = is_even(index)
+    after = jnp.where(even, a, b)[24:, :128]
+    before = jnp.where(even, b, a)[24:, :128]
+    if nr == 4:
+        return jnp.where(rows == 2, after, 0.0)
+    far = rows % 8
+    return jnp.where(
+        (far == 2) | (far == 5), after, jnp.where((far == 3) | (far == 6), before, 0.0)
+    )
 
 
 def send(index, a_ref, b_ref, before, after):
@@ -274,7 +295,7 @@
     b_ref[...] = jnp.where(even, before, after)
 
 
-def begin_kernel(counts, both_ref, a_ref, b_ref):
+def begin_kernel(counts, both_ref, out_ref):
     r, h = both_ref[:TR], both_ref[TR:]
     lane = lanes_of((128, 128))
     packed = jnp.where(
@@ -288,18 +309,16 @@
     )
     turned = packed.T
     table = table_of(core_sums(r), counts)
-    send(
-        lax.axis_index("col"),
-        a_ref,
-        b_ref,
+    send_columns(
+        out_ref,
         jnp.concatenate([turned[:32], table], axis=0),
         jnp.concatenate([turned[96:], table], axis=0),
     )
 
 
-def widen_kernel(counts, both_ref, ga_ref, gb_ref, r3_ref, h3_ref, table_ref, a_ref, b_ref):
+def widen_kernel(counts, both_ref, got_ref, r3_ref, h3_ref, table_ref, a_ref, b_ref):
     i, j = place()
-    from_left, from_right = sides(j, counts[1], ga_ref[:32], gb_ref[:32])
+    from_left, from_right = side_columns(got_ref, counts[1], 32)
     turned = jnp.concatenate([from_right, jnp.zeros((64, 128), jnp.float32), from_left], axis=0)
     back = turned.T
     lane = lanes_of((128, 128))
@@ -311,7 +330,7 @@
     r3_ref[...] = r3
     h3_ref[...] = h3
     r, h = both_ref[:TR], both_ref[TR:]
-    table = table_of(core_sums(r), counts) + ga_ref[32:] + gb_ref[32:]
+    table = sum(got_ref[k, 32:] for k in range(counts[1]))
     table_ref[...] = table
     wide = jnp.concatenate([table, jnp.zeros((table.shape[0], FC - 128), jnp.float32)], axis=1)
 
@@ -329,7 +348,7 @@
 
 
 def first_kernel(
-    counts, both_ref, r3_ref, h3_ref, ga_ref, gb_ref, basis_ref, y_ref, m_ref, a_ref, b_ref
+    counts, both_ref, r3_ref, h3_ref, ga_ref, gb_ref, basis_ref, y_ref, m_ref, out_ref
 ):
     i, j = place()
     above, below = sides(i, counts[0], ga_ref[:24], gb_ref[:24])
@@ -342,26 +361,19 @@
     means = [x / (SUB * SUB) for x in core_sums(mobility[:128])]
     y = local_solve(wide, means, basis_ref)
     y_ref[...] = y
-    send(j, a_ref, b_ref, *pack_columns(y))
-
-
-def columns_kernel(counts, y_ref, ga_ref, gb_ref, *refs):
-    i, j = place()
-    y = add_columns(y_ref[...], *sides(j, counts[1], ga_ref[:24], gb_ref[:24]))
+    send_columns(out_ref, *pack_columns(y))
+
+
+def columns_kernel(counts, y_ref, got_ref, *refs):
+    y = add_columns(y_ref[...], *side_columns(got_ref, counts[1], 24))
     strips = pack_rows(y)
-    if len(refs) == 5:
-        table_ref, out_ref, table_out, a_ref, b_ref = refs
-        cols = flat_place(counts)[2]
-        table = table_ref[...] + jnp.where(
-            cols % 4 == 2, next_table(j, ga_ref[...], gb_ref[...]), 0.0
-        )
-        table_out[...] = table
+    if len(refs) == 4:
+        table = refs[0][...]
         wide = jnp.concatenate([table, jnp.zeros((table.shape[0], FC - 128), jnp.float32)], axis=1)
         strips = [jnp.concatenate([x, wide], axis=0) for x in strips]
-    else:
-        out_ref, a_ref, b_ref = refs
+    out_ref, a_ref, b_ref = refs[-3:]
     out_ref[...] = y
-    send(i, a_ref, b_ref, *strips)
+    send(lax.axis_index("row"), a_ref, b_ref, *strips)
 
 
 def second_kernel(
@@ -379,15 +391,14 @@
     y2_ref,
     table_out,
     stats_ref,
-    a_ref,
-    b_ref,
+    out_ref,
 ):
     i, j = place()
     s = add_rows(y_ref[...], *sides(i, counts[0], ga_ref[:24], gb_ref[:24]))
     mask = grid_mask((FR, FC), counts)
     s = jnp.where(mask, s, 0.0)
     rows = flat_place(counts)[1]
-    table = table_ref[...] + jnp.where(rows % 4 == 2, next_table(i, ga_ref[...], gb_ref[...]), 0.0)
+    table = table_ref[...] + row_tables(i, counts[0], rows, ga_ref[...], gb_ref[...])
     table_out[...] = table
     c0 = as_row(table, width)
     coarse = spread(coarse_values(c0, coarse_part(basis_ref, width)), counts)
@@ -401,7 +412,7 @@
     means = [x / (SUB * SUB) for x in core_sums(mt)]
     y = local_solve(w, means, basis_ref)
     y2_ref[...] = y
-    send(j, a_ref, b_ref, *pack_columns(y))
+    send_columns(out_ref, *pack_columns(y))
     lane, row = lanes_of((1, 256)), rows_of((128, 1))
     along = (lane % 128 != 0) & (lane % 128 != 127)
     top, low = mt[:1], mt[127:]
@@ -545,29 +556,34 @@
     both_axes = ("row", "col")
     depth = table_shape(counts)[0]
 
-    def swap(a, b, axis):
-        count = lax.axis_size(axis)
-        return (
-            lax.ppermute(a, axis, pairs_from(count, 0)),
-            lax.ppermute(b, axis, pairs_from(count, 1)),
-        )
-
-    first = lax.broadcasted_iota(jnp.int32, (2, TR, TC), 0) == 0
-    both = jnp.where(first, noise[None], height[None]).reshape(2 * TR, TC)
-    a, b = call(functools.partial(begin_kernel, counts), [(32 + depth, 128)] * 2, both)
-    ga, gb = swap(a, b, "col")
+    def columns(x):
+        return lax.all_to_all(x, "col", 0, 0, tiled=True)
+
+    def rows(a, b):
+        return lax.ppermute(a, "row", pairs_from(nr, 0)), lax.ppermute(b, "row", pairs_from(nr, 1))
+
+    def row_shift(x, step):
+        return lax.ppermute(x, "row", [(k, (k + step) % nr) for k in range(nr)])
+
+    both = jnp.pad(noise, ((0, TR), (0, 0))) + jnp.pad(height, ((TR, 0), (0, 0)))
+    out = call(functools.partial(begin_kernel, counts), [(nc, 32 + depth, 128)], both)[0]
     r3, h3, table, a, b = call(
         functools.partial(widen_kernel, counts),
         [(128, 128)] * 2 + [(depth, 128)] + [(24 + depth, FC)] * 2,
         both,
-        ga,
-        gb,
-    )
-    ga, gb = swap(a, b, "row")
-    table = table + ga[24:, :128] + gb[24:, :128]
-    y, m, a, b = call(
+        columns(out),
+    )
+    step = nr // 2
+    while step >= 8:
+        table = table + row_shift(table, step)
+        step //= 2
+    if nr > 8:
+        a, b = (x.at[24:, :128].set(table) for x in (a, b))
+    ga, gb = rows(a, b)
+    far = row_shift(table, 4) if nr >= 8 else 0.0
+    y, m, out = call(
         functools.partial(first_kernel, counts),
-        [(FR, FC)] * 2 + [(24, FR)] * 2,
+        [(FR, FC)] * 2 + [(nc, 24, FR)],
         both,
         r3,
         h3,
@@ -575,26 +591,18 @@
         gb,
         basis,
     )
-    for axis, count in (("row", nr), ("col", nc)):
-        step = count // 2
-        while step >= 4:
-            shift = [(k, (k + step) % count) for k in range(count)]
-            table = table + lax.ppermute(table, axis, shift)
-            step //= 2
-    wide = jnp.pad(table, ((0, 0), (0, FR - 128)))
-    ga, gb = swap(*(jnp.concatenate([x, wide], axis=0) for x in (a, b)), "col")
-    y, table, a, b = call(
+    table = table + ga[24:, :128] + gb[24:, :128] + far
+    y, a, b = call(
         functools.partial(columns_kernel, counts),
-        [(FR, FC), (depth, 128)] + [(24 + depth, FC)] * 2,
+        [(FR, FC)] + [(24 + depth, FC)] * 2,
         y,
-        ga,
-        gb,
+        columns(out),
         table,
     )
-    ga, gb = swap(a, b, "row")
-    z, w, y, table, stats, a, b = call(
+    ga, gb = rows(a, b)
+    z, w, y, table, stats, out = call(
         functools.partial(second_kernel, counts, width),
-        [(TR, TC)] * 2 + [(FR, FC), (depth, 128), (1, 128)] + [(24, FR)] * 2,
+        [(TR, TC)] * 2 + [(FR, FC), (depth, 128), (1, 128), (nc, 24, FR)],
         y,
         m,
         ga,
@@ -603,11 +611,13 @@
         both,
         basis,
     )
-    ga, gb = swap(a, b, "col")
     y, a, b = call(
-        functools.partial(columns_kernel, counts), [(FR, FC)] + [(24, FC)] * 2, y, ga, gb
-    )
-    ga, gb = swap(a, b, "row")
+        functools.partial(columns_kernel, counts),
+        [(FR, FC)] + [(24, FC)] * 2,
+        y,
+        columns(out),
+    )
+    ga, gb = rows(a, b)
     q, v, stats = call(
         functools.partial(dots_kernel, counts),
         [(TR, TC)] * 2 + [(devices, 128)],

time: 56.6 us -> 60.8 us (1.074)
  blocking collectives: 8.86 us -> 26.2 us
  waiting for transfers between devices: 21.2 us -> 13.8 us
  starting transfers between devices: 17.1 us -> 10.8 us
    all_to_all x0 -> x2, blocking collectives: none -> 17.3 us  [columns(): return lax.all_to_all(x, 'col', 0, 0, tiled=True)]
    ppermute x13 -> x7, waiting for transfers between devices: 21.2 us -> 8.93 us  [the longest x3 8.92 us: rows(): lax.ppermute(b, 'row', pairs_from(nr, 1))]
    ppermute x13 -> x7, starting transfers between devices: 17.1 us -> 7.48 us  [the longest x3 7.26 us: rows(): lax.ppermute(b, 'row', pairs_from(nr, 1))]
    all_to_all x0 -> x1, waiting for transfers between devices: none -> 4.88 us  [columns(): return lax.all_to_all(x, 'col', 0, 0, tiled=True)]
    all_to_all x0 -> x1, starting transfers between devices: none -> 3.3 us  [columns(): return lax.all_to_all(x, 'col', 0, 0, tiled=True)]
    select_n x1 -> x0, other arithmetic: 1.07 us -> none  [body(): both = jnp.where(first, noise[None], height[None]).reshape(2 * TR, TC)]
    add x2, other arithmetic: 0.01 us -> 0.99 us  [the longest x1 0.99 us: body(): jnp.pad(noise, ((0, TR), (0, 0))) + jnp.pad(height, ((TR, 0), (0, 0)))]
  transfers between devices with their start and end apart: 13 -> 8, of which waited for: 11 -> 4; matrix products, arithmetic and copies ran while one was open for 0% -> 0% of each run, Pallas kernels for 4% -> 5%
where the time goes in v4:
time: 60.8 us; the launch traced here: 60.5 us
  blocking collectives  26.2 us (43%)
  waiting for transfers between devices  13.8 us (23%)
  starting transfers between devices  10.8 us (18%)
  Pallas kernels  8.04 us (13%)
  other arithmetic  0.99 us (2%)
  between operations  0.73 us (1%)
    all_to_all x2, blocking collectives, columns(): return lax.all_to_all(x, 'col', 0, 0, tiled=True)  17.3 us
    ppermute x3, waiting for transfers between devices, rows(): lax.ppermute(b, 'row', pairs_from(nr, 1))  8.92 us
    all_to_all x1, blocking collectives, body(): stats = lax.all_to_all(stats, both_axes, 0, 0, tiled=True)  8.86 us
    pallas_call x8, Pallas kernels, call(): pl.pallas_call(kernel, out_shape=shapes, compiler_params=pltpu.CompilerPa...  8.04 us
    ppermute x3, starting transfers between devices, rows(): lax.ppermute(b, 'row', pairs_from(nr, 1))  7.26 us
    all_to_all x1, waiting for transfers between devices, columns(): return lax.all_to_all(x, 'col', 0, 0, tiled=True)  4.88 us
    all_to_all x1, starting transfers between devices, columns(): return lax.all_to_all(x, 'col', 0, 0, tiled=True)  3.3 us
  transfers between devices with their start and end apart: 8, of which 4 were waited for; matrix products, arithmetic and copies ran while one was open for 0% of the time, Pallas kernels for 5%

profile of v4, /device:TPU:0, one launch (start us, length us, event | category | flops | bytes accessed | tf_op | source)
XLA Modules:
  0.0 60.5 jit_solution(1329496075942304260)
XLA Ops:
  0.6 1.0 %pad_add_fusion.both_ref = f32[256,256]{1,0:T(8,128)S(1)} fusion(f32[128,256]{1,0:T(8,128)} %param.3, f32[128,256]{1,0:T(8,128)} %param.4), kind=kLoop, calls=%fused_computation | loop fusion | flops 65536 | bytes 524288 | tf_op jit(solution)/shard_map/add | solution.py:568
  1.6 0.2 shard_map.50
  1.8 0.0 copy-start
  1.8 10.0 %all_to_all.26.got_ref = f32[4,40,128]{2,1,0:T(8,128)S(1)} all-to-all(f32[4,40,128]{2,1,0:T(8,128)S(1)} %shard_map.50), channel_id=1, replica_groups=mesh['row'=8,'col'=4] {'col'}, dimensions={0} | all-to-all | bytes 163840 | tf_op jit(solution)/shard_map/all_to_all | solution.py:560
  11.8 0.2 shard_map.51
  12.0 0.1 collective-permute-start
  12.1 3.7 %collective-permute-start.1 = (f32[32,384]{1,0:T(8,128)S(1)}, f32[32,384]{1,0:T(8,128)S(1)}, u32[]{:S(2)}, u32[]{:S(2)}) collective-permute-start(f32[32,384]{1,0:T(8,128)S(1)} %get-tuple-element.28), channel_id=1, source_target_pairs={{4,8},{8,4},{12,16},{16,12},{20,24},{24,20},{28,0},{0,28},{5,9},{9... | collective-permute-start | bytes 147464 | tf_op jit(solution)/shard_map/ppermute | solution.py:563
  15.8 0.0 collective-permute-start.2
  15.8 0.0 collective-permute-done.ga_ref
  15.8 1.9 %collective-permute-done.1.gb_ref = f32[32,384]{1,0:T(8,128)S(1)} collective-permute-done((f32[32,384]{1,0:T(8,128)S(1)}, f32[32,384]{1,0:T(8,128)S(1)}, u32[]{:S(2)}, u32[]{:S(2)}) %collective-permute-start.1) | collective-permute-done | bytes 49184 | tf_op jit(solution)/shard_map/ppermute | solution.py:563
  17.6 0.0 copy-done
  17.7 2.7 %shard_map.52 = (f32[160,384]{1,0:T(8,128)S(1)}, f32[160,384]{1,0:T(8,128)S(1)}, f32[4,24,160]{2,1,0:T(8,128)}) custom-call(f32[256,256]{1,0:T(8,128)S(1)} %pad_add_fusion.both_ref, f32[128,128]{1,0:T(8,128)S(1)} %get-tuple-element.25.r3_ref, f32[128,128]{1,0:T(8,128)S(1)} %get-tuple-element.26.h3_ref, f32[32,384]{1,0:T(8,128)S(1)} %collective-permute-done.ga_ref, ...), custom_call_target="tpu_custom_call" | custom-call | flops 1000000000 | bytes 1000000 | tf_op jit(solution)/shard_map/pallas_call | solution.py:536
  20.4 3.3 %all-to-all-start.1 = ((f32[4,24,160]{2,1,0:T(8,128)}), f32[4,24,160]{2,1,0:T(8,128)S(1)}, u32[]{:S(2)}, u32[]{:S(2)}) async-start(f32[4,24,160]{2,1,0:T(8,128)} %get-tuple-element.30), calls=%async_computation.1 | async-start | bytes 196608 | tf_op jit(solution)/shard_map/all_to_all | solution.py:560
  23.7 0.0 collective-permute-done.2
  23.7 4.9 %all-to-all-done.1.got_ref = f32[4,24,160]{2,1,0:T(8,128)S(1)} async-done(((f32[4,24,160]{2,1,0:T(8,128)}), f32[4,24,160]{2,1,0:T(8,128)S(1)}, u32[]{:S(2)}, u32[]{:S(2)}) %all-to-all-start.1) | async-done | bytes 61472 | tf_op jit(solution)/shard_map/all_to_all | solution.py:560
  28.6 0.2 shard_map.53
  28.8 0.1 collective-permute-start.3
  28.8 2.4 %collective-permute-start.4 = (f32[32,384]{1,0:T(8,128)S(1)}, f32[32,384]{1,0:T(8,128)S(1)}, u32[]{:S(2)}, u32[]{:S(2)}) collective-permute-start(f32[32,384]{1,0:T(8,128)S(1)} %get-tuple-element.35), channel_id=1, source_target_pairs={{4,8},{8,4},{12,16},{16,12},{20,24},{24,20},{28,0},{0,28},{5,9},{9... | collective-permute-start | bytes 147464 | tf_op jit(solution)/shard_map/ppermute | solution.py:563
  31.2 0.0 collective-permute-done.3.ga_ref
  31.2 3.0 %collective-permute-done.4.gb_ref = f32[32,384]{1,0:T(8,128)S(1)} collective-permute-done((f32[32,384]{1,0:T(8,128)S(1)}, f32[32,384]{1,0:T(8,128)S(1)}, u32[]{:S(2)}, u32[]{:S(2)}) %collective-permute-start.4) | collective-permute-done | bytes 49184 | tf_op jit(solution)/shard_map/ppermute | solution.py:563
  34.2 2.8 %shard_map.54 = (f32[128,256]{1,0:T(8,128)S(1)}, f32[128,256]{1,0:T(8,128)S(1)}, f32[160,384]{1,0:T(8,128)S(1)}, f32[8,128]{1,0:T(8,128)S(1)}, f32[1,128]{1,0:T(1,128)S(1)}, /*index=5*/f32[4,24,160]{2,1,0:T(8,128)S(1)}) custom-call(f32[160,384]{1,0:T(8,128)S(1)} %get-tuple-element.32.y_ref, f32[160,384]{1,0:T(8,128)S(1)} %get-tuple-element.33.m_ref, ...), custom_call_target="tpu_custom_call" | custom-call | flops 1000000000 | bytes 1000000 | tf_op jit(solution)/shard_map/pallas_call | solution.py:536
  37.0 7.3 %all_to_all.27.got_ref = f32[4,24,160]{2,1,0:T(8,128)S(1)} all-to-all(f32[4,24,160]{2,1,0:T(8,128)S(1)} %get-tuple-element.37), channel_id=1, replica_groups=mesh['row'=8,'col'=4] {'col'}, dimensions={0} | all-to-all | bytes 122880 | tf_op jit(solution)/shard_map/all_to_all | solution.py:560
  44.3 0.2 shard_map.55
  44.5 0.1 collective-permute-start.5
  44.6 1.2 %collective-permute-start.6 = (f32[24,384]{1,0:T(8,128)S(1)}, f32[24,384]{1,0:T(8,128)S(1)}, u32[]{:S(2)}, u32[]{:S(2)}) collective-permute-start(f32[24,384]{1,0:T(8,128)S(1)} %get-tuple-element.40), channel_id=1, source_target_pairs={{4,8},{8,4},{12,16},{16,12},{20,24},{24,20},{28,0},{0,28},{5,9},{9... | collective-permute-start | bytes 110600 | tf_op jit(solution)/shard_map/ppermute | solution.py:563
  45.8 0.0 collective-permute-done.5.ga_ref
  45.8 4.0 %collective-permute-done.6.gb_ref = f32[24,384]{1,0:T(8,128)S(1)} collective-permute-done((f32[24,384]{1,0:T(8,128)S(1)}, f32[24,384]{1,0:T(8,128)S(1)}, u32[]{:S(2)}, u32[]{:S(2)}) %collective-permute-start.6) | collective-permute-done | bytes 36896 | tf_op jit(solution)/shard_map/ppermute | solution.py:563
  49.8 0.4 shard_map.56
  50.3 8.9 %all_to_all.28 = f32[32,1,128]{2,1,0:T(1,128)S(1)} all-to-all(f32[32,1,128]{2,1,0:T(1,128)S(1)} %bitcast.5), channel_id=1, replica_groups=mesh['row'=8,'col'=4] {'row','col'}, dimensions={0} | all-to-all | bytes 32768 | tf_op jit(solution)/shard_map/all_to_all | solution.py:632
  59.1 1.4 %shard_map.57 = (f32[128,256]{1,0:T(8,128)}, f32[128,256]{1,0:T(8,128)}) custom-call(f32[32,128]{1,0:T(8,128)S(1)} %bitcast.4, f32[8,128]{1,0:T(8,128)S(1)} %get-tuple-element.44.table_ref, f32[1344,384]{1,0:T(8,128)S(1)} %copy-done, f32[160,384]{1,0:T(8,128)S(1)} %get-tuple-element.33.m_ref, f32[256,256]{1,0:T(8,128)S(1)} %pad_add_fusion.both_ref, ...), custom_call_target="tpu_custom_call" | custom-call | flops 1000000000 | bytes 1000000 | tf_op jit(solution)/shard_map/pallas_call | solution.py:536
  (1 shorter events, 0.0 us)
Async XLA Ops:
  1.8 15.9 %copy-start = (f32[1344,384]{1,0:T(8,128)S(1)}, f32[1344,384]{1,0:T(8,128)}, u32[]{:S(2)}) copy-start(f32[1344,384]{1,0:T(8,128)} %constant.5.clone.basis_ref) | copy-start | bytes 6193156
  12.0 3.8 %collective-permute-start = (f32[32,384]{1,0:T(8,128)S(1)}, f32[32,384]{1,0:T(8,128)S(1)}, u32[]{:S(2)}, u32[]{:S(2)}) collective-permute-start(f32[32,384]{1,0:T(8,128)S(1)} %get-tuple-element.27), channel_id=1, source_target_pairs={{0,4},{4,0},{8,12},{12,8},{16,20},{20,16},{24,28},{28,24},{1,5},{5... | collective-permute-start | bytes 147464 | tf_op jit(solution)/shard_map/ppermute | solution.py:563
  12.1 5.6 %collective-permute-start.1 = (f32[32,384]{1,0:T(8,128)S(1)}, f32[32,384]{1,0:T(8,128)S(1)}, u32[]{:S(2)}, u32[]{:S(2)}) collective-permute-start(f32[32,384]{1,0:T(8,128)S(1)} %get-tuple-element.28), channel_id=1, source_target_pairs={{4,8},{8,4},{12,16},{16,12},{20,24},{24,20},{28,0},{0,28},{5,9},{9... | collective-permute-start | bytes 147464 | tf_op jit(solution)/shard_map/ppermute | solution.py:563
  15.8 7.9 %collective-permute-start.2 = (f32[8,128]{1,0:T(8,128)S(1)}, f32[8,128]{1,0:T(8,128)S(1)}, u32[]{:S(2)}, u32[]{:S(2)}) collective-permute-start(f32[8,128]{1,0:T(8,128)S(1)} %get-tuple-element.31), channel_id=1, source_target_pairs={{0,16},{4,20},{8,24},{12,28},{16,0},{20,4},{24,8},{28,12},{1,17},{... | collective-permute-start | bytes 12296 | tf_op jit(solution)/shard_map/ppermute | solution.py:566
  20.4 8.2 %all-to-all-start.1 = ((f32[4,24,160]{2,1,0:T(8,128)}), f32[4,24,160]{2,1,0:T(8,128)S(1)}, u32[]{:S(2)}, u32[]{:S(2)}) async-start(f32[4,24,160]{2,1,0:T(8,128)} %get-tuple-element.30), calls=%async_computation.1 | async-start | bytes 196608 | tf_op jit(solution)/shard_map/all_to_all | solution.py:560
  28.8 2.4 %collective-permute-start.3 = (f32[32,384]{1,0:T(8,128)S(1)}, f32[32,384]{1,0:T(8,128)S(1)}, u32[]{:S(2)}, u32[]{:S(2)}) collective-permute-start(f32[32,384]{1,0:T(8,128)S(1)} %get-tuple-element.34), channel_id=1, source_target_pairs={{0,4},{4,0},{8,12},{12,8},{16,20},{20,16},{24,28},{28,24},{1,5},{5... | collective-permute-start | bytes 147464 | tf_op jit(solution)/shard_map/ppermute | solution.py:563
  28.8 5.4 %collective-permute-start.4 = (f32[32,384]{1,0:T(8,128)S(1)}, f32[32,384]{1,0:T(8,128)S(1)}, u32[]{:S(2)}, u32[]{:S(2)}) collective-permute-start(f32[32,384]{1,0:T(8,128)S(1)} %get-tuple-element.35), channel_id=1, source_target_pairs={{4,8},{8,4},{12,16},{16,12},{20,24},{24,20},{28,0},{0,28},{5,9},{9... | collective-permute-start | bytes 147464 | tf_op jit(solution)/shard_map/ppermute | solution.py:563
  44.5 1.3 %collective-permute-start.5 = (f32[24,384]{1,0:T(8,128)S(1)}, f32[24,384]{1,0:T(8,128)S(1)}, u32[]{:S(2)}, u32[]{:S(2)}) collective-permute-start(f32[24,384]{1,0:T(8,128)S(1)} %get-tuple-element.39), channel_id=1, source_target_pairs={{0,4},{4,0},{8,12},{12,8},{16,20},{20,16},{24,28},{28,24},{1,5},{5... | collective-permute-start | bytes 110600 | tf_op jit(solution)/shard_map/ppermute | solution.py:563
  44.6 5.2 %collective-permute-start.6 = (f32[24,384]{1,0:T(8,128)S(1)}, f32[24,384]{1,0:T(8,128)S(1)}, u32[]{:S(2)}, u32[]{:S(2)}) collective-permute-start(f32[24,384]{1,0:T(8,128)S(1)} %get-tuple-element.40), channel_id=1, source_target_pairs={{4,8},{8,4},{12,16},{16,12},{20,24},{24,20},{28,0},{0,28},{5,9},{9... | collective-permute-start | bytes 110600 | tf_op jit(solution)/shard_map/ppermute | solution.py:563

commit v5 on v3

--- a/solution.py
+++ b/solution.py
@@ -16,7 +16,7 @@
 
 TR, TC = 128, 256
 FR, FC = 160, 384
-SPEC = 192
+SPEC = 256
 
 highest = lax.Precision.HIGHEST
 
@@ -29,34 +29,36 @@
 
 def block_constants():
     basis, eig = sine(EXT)
-    rows = np.zeros((FR, EXT))
-    cols = np.zeros((FC, 2 * SPEC))
-    for at in range(EXT):
-        rows[(at - OV) % FR] = basis[at]
-        for b in range(2):
-            cols[(b * SUB + at - OV) % FC, b * SPEC : b * SPEC + EXT] = basis[at]
-    scale = np.ones((EXT, 2 * SPEC))
-    for b in range(2):
-        scale[:, b * SPEC : b * SPEC + EXT] = (eig[:, None] + eig[None, :]) ** 2
-    wide = lambda x: np.pad(x, ((0, 0), (0, FC - x.shape[1])))
-    return [cols, cols.T, scale, wide(rows), wide(rows.T)]
-
-
-def block_parts(ref):
-    cols, cols_t, scale = ref[:FC], ref[FC : 2 * FC], ref[2 * FC : 2 * FC + EXT]
-    at = 2 * FC + EXT
-    return ref[at : at + FR, :EXT], ref[at + FR : at + FR + EXT, :FR], cols, cols_t, scale
+    rows = np.roll(basis, -OV, 0)
+    cols = np.pad(basis, ((0, SPEC - EXT), (0, SPEC - EXT)))
+    scale = np.pad((eig[:, None] + eig[None, :]) ** 2, ((0, 0), (0, SPEC - EXT)))
+    wide = lambda x: np.pad(x, ((0, 0), (0, 2 * SPEC - x.shape[1])))
+    return [np.tile(scale, (1, 2)), wide(rows), wide(rows.T), wide(cols)]
+
+
+def rows_part(ref):
+    return ref[EXT : 2 * EXT, :EXT]
+
+
+def rows_t_part(ref):
+    return ref[2 * EXT : 3 * EXT, :EXT]
+
+
+def cols_part(ref):
+    return ref[3 * EXT : 3 * EXT + SPEC, :SPEC]
 
 
 def coarse_part(ref, width):
-    at = 2 * FC + 2 * EXT + FR
-    parts = [ref[at + k * width : at + (k + 1) * width] for k in range(-(-width // FC))]
+    at, lanes = 3 * EXT + SPEC, 2 * SPEC
+    parts = [ref[at + k * width : at + (k + 1) * width] for k in range(-(-width // lanes))]
     return (parts[0] if len(parts) == 1 else jnp.concatenate(parts, axis=1))[:, :width]
 
 
 def constants(nr, nc, width):
-    inverse = coarse_inverse(nr, nc, -(-width // FC) * FC)[:width]
-    return np.concatenate([*block_constants(), *np.split(inverse, inverse.shape[1] // FC, 1)], dtype=np.float32)
+    lanes = 2 * SPEC
+    inverse = coarse_inverse(nr, nc, -(-width // lanes) * lanes)[:width]
+    parts = [*block_constants(), *np.split(inverse, inverse.shape[1] // lanes, 1)]
+    return np.concatenate(parts).astype(np.float32)
 
 
 def coarse_inverse(nr, nc, width):
@@ -71,9 +73,9 @@
     return whole
 
 
-def dot(a, b):
+def dot(a, b, side=0):
     return lax.dot_general(
-        a, b, (((1,), (0,)), ((), ())), precision=highest, preferred_element_type=jnp.float32
+        a, b, (((1,), (side,)), ((), ())), precision=highest, preferred_element_type=jnp.float32
     )
 
 
@@ -194,46 +196,54 @@
     )
 
 
-def local_solve(w, means, basis_ref):
-    rows, rows_t, cols, cols_t, scale = block_parts(basis_ref)
+def column_transform(w, basis_ref):
+    w = pltpu.roll(w, OV, 1)
+    cols = cols_part(basis_ref)
+    return jnp.concatenate([dot(w[:, :256], cols), dot(w[:, 128:], cols)], axis=1)
+
+
+def weights(means, basis_ref):
     lane = lanes_of((1, 2 * SPEC))
     mean = jnp.where(lane < SPEC, means[0], means[1])
-    t = dot(dot(rows_t, w), cols)
-    t = t / (DAMP + mean * scale)
-    return dot(rows, dot(t, cols_t))
+    return 1.0 / (DAMP + mean * basis_ref[:EXT])
+
+
+def strips_of(t, basis_ref):
+    cols = cols_part(basis_ref)
+    left = dot(cols[:24], t[:, :SPEC], 1)
+    right = dot(cols[EXT - 24 : EXT], t[:, SPEC:], 1)
+    both = dot(jnp.concatenate([left, right], axis=0), rows_t_part(basis_ref))
+    return both[:24], both[24:]
+
+
+def solution_of(t, basis_ref):
+    v = dot(rows_part(basis_ref), t)
+    cols = cols_part(basis_ref)
+    first, second = dot(v[:, :SPEC], cols), dot(v[:, SPEC:], cols)
+    y = jnp.concatenate(
+        [first[:, :128], first[:, 128:] + second[:, :128], second[:, 128:]], axis=1
+    )
+    return pltpu.roll(y, FC - OV, 1)
 
 
 def core_sums(x):
     return [total(x[:, :128]), total(x[:, 128:256])]
-
-
-def pack_columns(y):
-    lane = lanes_of((FR, 128))
-    packed = jnp.where(
-        lane < 16,
-        y[:, :128],
-        jnp.where(lane >= 112, y[:, 128:256], pltpu.roll(y[:, 256:], 64, 1)),
-    )
-    turned = packed.T
-    to_left = jnp.concatenate([turned[56:64], turned[:16]], axis=0)
-    to_right = jnp.concatenate([turned[112:], turned[64:72]], axis=0)
-    return to_left, to_right
 
 
 def add_columns(y, from_left, from_right):
     turned = jnp.concatenate(
         [
             from_right[8:24],
-            jnp.zeros((40, FR), jnp.float32),
+            jnp.zeros((40, EXT), jnp.float32),
             from_right[:8],
             from_left[16:24],
-            jnp.zeros((40, FR), jnp.float32),
+            jnp.zeros((40, EXT), jnp.float32),
             from_left[:16],
         ],
         axis=0,
     )
     back = turned.T
-    lane = lanes_of((FR, 128))
+    lane = lanes_of((EXT, 128))
     rolled = pltpu.roll(back, 64, 1)
     first = y[:, :128] + jnp.where(lane < 8, rolled, 0.0)
     second = y[:, 128:256] + jnp.where(lane >= 120, rolled, 0.0)
@@ -242,16 +252,18 @@
 
 
 def pack_rows(y):
-    return jnp.concatenate([y[152:160], y[:16]], axis=0), y[112:136]
+    return jnp.concatenate([y[136:], y[:16]], axis=0), y[112:136]
 
 
 def add_rows(y, from_above, from_below):
     return jnp.concatenate(
         [
-            y[:8] + from_above[16:24],
+            y[:8] + from_above[16:],
             y[8:120],
-            y[120:144] + from_below,
-            y[144:] + from_above[:16],
+            y[120:136] + from_below[:16],
+            from_below[16:],
+            from_above[:8],
+            y[136:] + from_above[8:16],
         ],
         axis=0,
     )
@@ -266,6 +278,18 @@
 
 def next_table(index, a, b):
     return jnp.where(is_even(index), a, b)[24:, :128]
+
+
+def row_tables(index, nr, rows, a, b):
+    even = is_even(index)
+    after = jnp.where(even, a, b)[24:, :128]
+    before = jnp.where(even, b, a)[24:, :128]
+    if nr == 4:
+        return jnp.where(rows == 2, after, 0.0)
+    far = rows % 8
+    return jnp.where(
+        (far == 2) | (far == 5), after, jnp.where((far == 3) | (far == 6), before, 0.0)
+    )
 
 
 def send(index, a_ref, b_ref, before, after):
@@ -328,21 +352,29 @@
     send(i, a_ref, b_ref, strip(slice(0, 8), slice(0, 16)), strip(slice(120, 128), slice(112, 128)))
 
 
-def first_kernel(
-    counts, both_ref, r3_ref, h3_ref, ga_ref, gb_ref, basis_ref, y_ref, m_ref, a_ref, b_ref
-):
+def forward_kernel(both_ref, r3_ref, basis_ref, u_ref, weights_ref):
+    r, h = both_ref[:TR], both_ref[TR:]
+    u_ref[...] = column_transform(jnp.concatenate([r, r3_ref[...]], axis=1), basis_ref)
+    means = [x / (SUB * SUB) for x in core_sums(h * h * h)]
+    weights_ref[...] = weights(means, basis_ref)
+
+
+def first_kernel(counts, ga_ref, gb_ref, u_ref, weights_ref, basis_ref, t_ref, a_ref, b_ref):
     i, j = place()
-    above, below = sides(i, counts[0], ga_ref[:24], gb_ref[:24])
-    r = jnp.concatenate([both_ref[:TR], r3_ref[...]], axis=1)
+    above, below = sides(i, counts[0], ga_ref[:8], gb_ref[:8])
+    halo = column_transform(jnp.concatenate([below, above], axis=0), basis_ref)
+    u = jnp.concatenate([u_ref[...], halo], axis=0)
+    t = dot(rows_t_part(basis_ref), u) * weights_ref[...]
+    t_ref[...] = t
+    send(j, a_ref, b_ref, *strips_of(t, basis_ref))
+
+
+def inverse_kernel(counts, t_ref, basis_ref, both_ref, h3_ref, ga_ref, gb_ref, y_ref, m_ref):
+    y_ref[...] = solution_of(t_ref[...], basis_ref)
+    above, below = sides(lax.axis_index("row"), counts[0], ga_ref[8:24], gb_ref[8:24])
     h = jnp.concatenate([both_ref[TR:], h3_ref[...]], axis=1)
-    wide = jnp.concatenate([r, below[:8], jnp.zeros((16, FC), jnp.float32), above[:8]], axis=0)
-    tall = jnp.concatenate([h, below[8:], above[8:]], axis=0)
-    mobility = tall * tall * tall
-    m_ref[...] = mobility
-    means = [x / (SUB * SUB) for x in core_sums(mobility[:128])]
-    y = local_solve(wide, means, basis_ref)
-    y_ref[...] = y
-    send(j, a_ref, b_ref, *pack_columns(y))
+    tall = jnp.concatenate([h, below, above], axis=0)
+    m_ref[...] = tall * tall * tall
 
 
 def columns_kernel(counts, y_ref, ga_ref, gb_ref, *refs):
@@ -372,13 +404,12 @@
     ga_ref,
     gb_ref,
     table_ref,
-    both_ref,
+    weights_ref,
     basis_ref,
     z_ref,
     w_ref,
-    y2_ref,
+    t_ref,
     table_out,
-    stats_ref,
     a_ref,
     b_ref,
 ):
@@ -387,7 +418,7 @@
     mask = grid_mask((FR, FC), counts)
     s = jnp.where(mask, s, 0.0)
     rows = flat_place(counts)[1]
-    table = table_ref[...] + jnp.where(rows % 4 == 2, next_table(i, ga_ref[...], gb_ref[...]), 0.0)
+    table = table_ref[...] + row_tables(i, counts[0], rows, ga_ref[...], gb_ref[...])
     table_out[...] = table
     c0 = as_row(table, width)
     coarse = spread(coarse_values(c0, coarse_part(basis_ref, width)), counts)
@@ -395,13 +426,17 @@
     flow = mobility * (lap(s) + lap(coarse))
     z = s + coarse
     w = jnp.where(mask, DAMP * z + lap(flow), 0.0) * SHRINK
-    zt, wt, rt, mt = z[:128, :256], w[:128, :256], both_ref[:TR], mobility[:128, :256]
-    z_ref[...] = zt
-    w_ref[...] = wt
-    means = [x / (SUB * SUB) for x in core_sums(mt)]
-    y = local_solve(w, means, basis_ref)
-    y2_ref[...] = y
-    send(j, a_ref, b_ref, *pack_columns(y))
+    z_ref[...] = z[:128, :256]
+    w_ref[...] = w[:128, :256]
+    u = column_transform(jnp.concatenate([w[:136], w[152:]], axis=0), basis_ref)
+    t = dot(rows_t_part(basis_ref), u) * weights_ref[...]
+    t_ref[...] = t
+    send(j, a_ref, b_ref, *strips_of(t, basis_ref))
+
+
+def inverse_stats_kernel(t_ref, basis_ref, both_ref, m_ref, z_ref, w_ref, y_ref, stats_ref):
+    y_ref[...] = solution_of(t_ref[...], basis_ref)
+    rt, mt, zt, wt = both_ref[:TR], m_ref[:TR, :TC], z_ref[...], w_ref[...]
     lane, row = lanes_of((1, 256)), rows_of((128, 1))
     along = (lane % 128 != 0) & (lane % 128 != 127)
     top, low = mt[:1], mt[127:]
@@ -547,13 +582,13 @@
 
     def swap(a, b, axis):
         count = lax.axis_size(axis)
-        return (
-            lax.ppermute(a, axis, pairs_from(count, 0)),
-            lax.ppermute(b, axis, pairs_from(count, 1)),
-        )
-
-    first = lax.broadcasted_iota(jnp.int32, (2, TR, TC), 0) == 0
-    both = jnp.where(first, noise[None], height[None]).reshape(2 * TR, TC)
+        gb = lax.ppermute(b, axis, pairs_from(count, 1))
+        return lax.ppermute(a, axis, pairs_from(count, 0)), gb
+
+    def row_shift(x, step):
+        return lax.ppermute(x, "row", [(k, (k + step) % nr) for k in range(nr)])
+
+    both = jnp.pad(noise, ((0, TR), (0, 0))) + jnp.pad(height, ((TR, 0), (0, 0)))
     a, b = call(functools.partial(begin_kernel, counts), [(32 + depth, 128)] * 2, both)
     ga, gb = swap(a, b, "col")
     r3, h3, table, a, b = call(
@@ -563,49 +598,65 @@
         ga,
         gb,
     )
+    step = nr // 2
+    while step >= 8:
+        table = table + row_shift(table, step)
+        step //= 2
+    if nr > 8:
+        a, b = (x.at[24:, :128].set(table) for x in (a, b))
     ga, gb = swap(a, b, "row")
-    table = table + ga[24:, :128] + gb[24:, :128]
-    y, m, a, b = call(
+    far = row_shift(table, 4) if nr >= 8 else 0.0
+    u, weight = call(forward_kernel, [(TR, 2 * SPEC), (EXT, 2 * SPEC)], both, r3, basis)
+    t, a, b = call(
         functools.partial(first_kernel, counts),
-        [(FR, FC)] * 2 + [(24, FR)] * 2,
+        [(EXT, 2 * SPEC)] + [(24, EXT)] * 2,
+        ga,
+        gb,
+        u,
+        weight,
+        basis,
+    )
+    table = table + ga[24:, :128] + gb[24:, :128] + far
+    step = nc // 2
+    while step >= 4:
+        table = table + lax.ppermute(table, "col", [(k, (k + step) % nc) for k in range(nc)])
+        step //= 2
+    wide = jnp.pad(table, ((0, 0), (0, EXT - 128)))
+    y, m = call(
+        functools.partial(inverse_kernel, counts),
+        [(EXT, FC), (FR, FC)],
+        t,
+        basis,
         both,
-        r3,
         h3,
         ga,
         gb,
-        basis,
-    )
-    for axis, count in (("row", nr), ("col", nc)):
-        step = count // 2
-        while step >= 4:
-            shift = [(k, (k + step) % count) for k in range(count)]
-            table = table + lax.ppermute(table, axis, shift)
-            step //= 2
-    wide = jnp.pad(table, ((0, 0), (0, FR - 128)))
+    )
     ga, gb = swap(*(jnp.concatenate([x, wide], axis=0) for x in (a, b)), "col")
     y, table, a, b = call(
         functools.partial(columns_kernel, counts),
-        [(FR, FC), (depth, 128)] + [(24 + depth, FC)] * 2,
+        [(EXT, FC), (depth, 128)] + [(24 + depth, FC)] * 2,
         y,
         ga,
         gb,
         table,
     )
     ga, gb = swap(a, b, "row")
-    z, w, y, table, stats, a, b = call(
+    z, w, t, table, a, b = call(
         functools.partial(second_kernel, counts, width),
-        [(TR, TC)] * 2 + [(FR, FC), (depth, 128), (1, 128)] + [(24, FR)] * 2,
+        [(TR, TC)] * 2 + [(EXT, 2 * SPEC), (depth, 128)] + [(24, EXT)] * 2,
         y,
         m,
         ga,
         gb,
         table,
-        both,
+        weight,
         basis,
     )
     ga, gb = swap(a, b, "col")
+    y, stats = call(inverse_stats_kernel, [(EXT, FC), (1, 128)], t, basis, both, m, z, w)
     y, a, b = call(
-        functools.partial(columns_kernel, counts), [(FR, FC)] + [(24, FC)] * 2, y, ga, gb
+        functools.partial(columns_kernel, counts), [(EXT, FC)] + [(24, FC)] * 2, y, ga, gb
     )
     ga, gb = swap(a, b, "row")
     q, v, stats = call(

time: 56.6 us -> 54.8 us (0.968)
  starting transfers between devices: 17.1 us -> 14.8 us
    ppermute x13, starting transfers between devices: 17.1 us -> 14.8 us  [the longest x6 6.2 us: swap(): return (lax.ppermute(a, axis, pairs_from(count, 0)), gb)]
    select_n x1 -> x0, other arithmetic: 1.07 us -> none  [body(): both = jnp.where(first, noise[None], height[None]).reshape(2 * TR, TC)]
    add x2, other arithmetic: 0.01 us -> 0.99 us  [the longest x1 0.99 us: body(): jnp.pad(noise, ((0, TR), (0, 0))) + jnp.pad(height, ((TR, 0), (0, 0)))]
    pallas_call x8 -> x11, Pallas kernels: 7.47 us -> 7.84 us  [call(): pl.pallas_call(kernel, out_shape=shapes, compiler_params=pltpu.CompilerPa...]
where the time goes in v5:
time: 54.8 us; the launch traced here: 54.6 us
  waiting for transfers between devices  21.4 us (39%)
  starting transfers between devices  14.8 us (27%)
  blocking collectives  8.86 us (16%)
  Pallas kernels  7.84 us (14%)
  other arithmetic  1 us (2%)
  between operations  0.74 us (1%)
    ppermute x6, waiting for transfers between devices, swap(): gb = lax.ppermute(b, axis, pairs_from(count, 1))  18 us
    all_to_all x1, blocking collectives, body(): stats = lax.all_to_all(stats, both_axes, 0, 0, tiled=True)  8.86 us
    pallas_call x11, Pallas kernels, call(): pl.pallas_call(kernel, out_shape=shapes, compiler_params=pltpu.CompilerPa...  7.84 us
    ppermute x6, starting transfers between devices, swap(): return (lax.ppermute(a, axis, pairs_from(count, 0)), gb)  6.2 us
    ppermute x6, starting transfers between devices, swap(): gb = lax.ppermute(b, axis, pairs_from(count, 1))  5.97 us
    ppermute x6, waiting for transfers between devices, swap(): return (lax.ppermute(a, axis, pairs_from(count, 0)), gb)  3.31 us
    ppermute x1, starting transfers between devices, row_shift(): return lax.ppermute(x, 'row', [(k, (k + step) % nr) for k in range(nr)])  2.65 us
  transfers between devices with their start and end apart: 13, of which 11 were waited for; matrix products, arithmetic and copies ran while one was open for 0% of the time, Pallas kernels for 4%

profile of v5, /device:TPU:0, one launch (start us, length us, event | category | flops | bytes accessed | tf_op | source)
XLA Modules:
  0.0 54.6 jit_solution(2329130446062374808)
XLA Ops:
  0.6 1.0 %pad_add_fusion.both_ref = f32[256,256]{1,0:T(8,128)S(1)} fusion(f32[128,256]{1,0:T(8,128)} %param.3, f32[128,256]{1,0:T(8,128)} %param.4), kind=kLoop, calls=%fused_computation | loop fusion | flops 65536 | bytes 524288 | tf_op jit(solution)/shard_map/add | solution.py:591
  1.6 0.2 shard_map.50
  1.8 3.0 %collective-permute-start = (f32[40,128]{1,0:T(8,128)S(1)}, f32[40,128]{1,0:T(8,128)S(1)}, u32[]{:S(2)}, u32[]{:S(2)}) collective-permute-start(f32[40,128]{1,0:T(8,128)S(1)} %get-tuple-element.34), channel_id=1, source_target_pairs={{0,1},{1,0},{2,3},{3,2},{4,5},{5,4},{6,7},{7,6},{8,9},{9,8},{10,11... | collective-permute-start | bytes 61448 | tf_op jit(solution)/shard_map/ppermute | solution.py:586
  4.8 0.0 copy-start
  4.8 1.5 %collective-permute-start.1 = (f32[40,128]{1,0:T(8,128)S(1)}, f32[40,128]{1,0:T(8,128)S(1)}, u32[]{:S(2)}, u32[]{:S(2)}) collective-permute-start(f32[40,128]{1,0:T(8,128)S(1)} %get-tuple-element.35), channel_id=1, source_target_pairs={{1,2},{2,1},{3,0},{0,3},{5,6},{6,5},{7,4},{4,7},{9,10},{10,9},{11,... | collective-permute-start | bytes 61448 | tf_op jit(solution)/shard_map/ppermute | solution.py:585
  6.3 0.3 collective-permute-done.ga_ref
  6.6 2.9 %collective-permute-done.1.gb_ref = f32[40,128]{1,0:T(8,128)S(1)} collective-permute-done((f32[40,128]{1,0:T(8,128)S(1)}, f32[40,128]{1,0:T(8,128)S(1)}, u32[]{:S(2)}, u32[]{:S(2)}) %collective-permute-start.1) | collective-permute-done | bytes 20512 | tf_op jit(solution)/shard_map/ppermute | solution.py:585
  9.5 0.2 shard_map.51
  9.7 2.7 %collective-permute-start.4 = (f32[8,128]{1,0:T(8,128)S(1)}, f32[8,128]{1,0:T(8,128)S(1)}, u32[]{:S(2)}, u32[]{:S(2)}) collective-permute-start(f32[8,128]{1,0:T(8,128)S(1)} %get-tuple-element.45), channel_id=1, source_target_pairs={{0,16},{4,20},{8,24},{12,28},{16,0},{20,4},{24,8},{28,12},{1,17},{... | collective-permute-start | bytes 12296 | tf_op jit(solution)/shard_map/ppermute | solution.py:589
  12.3 0.0 collective-permute-start.2
  12.3 1.5 %collective-permute-start.3 = (f32[32,384]{1,0:T(8,128)S(1)}, f32[32,384]{1,0:T(8,128)S(1)}, u32[]{:S(2)}, u32[]{:S(2)}) collective-permute-start(f32[32,384]{1,0:T(8,128)S(1)} %get-tuple-element.37), channel_id=1, source_target_pairs={{4,8},{8,4},{12,16},{16,12},{20,24},{24,20},{28,0},{0,28},{5,9},{9... | collective-permute-start | bytes 147464 | tf_op jit(solution)/shard_map/ppermute | solution.py:585
  13.8 0.0 copy-done
  13.8 0.4 shard_map.52
  14.2 0.0 collective-permute-done.4
  14.2 0.0 collective-permute-done.2.ga_ref
  14.2 3.5 %collective-permute-done.3.gb_ref = f32[32,384]{1,0:T(8,128)S(1)} collective-permute-done((f32[32,384]{1,0:T(8,128)S(1)}, f32[32,384]{1,0:T(8,128)S(1)}, u32[]{:S(2)}, u32[]{:S(2)}) %collective-permute-start.3) | collective-permute-done | bytes 49184 | tf_op jit(solution)/shard_map/ppermute | solution.py:585
  17.8 1.3 %shard_map.53 = (f32[144,512]{1,0:T(8,128)S(1)}, f32[24,144]{1,0:T(8,128)S(1)}, f32[24,144]{1,0:T(8,128)S(1)}) custom-call(f32[32,384]{1,0:T(8,128)S(1)} %collective-permute-done.2.ga_ref, f32[32,384]{1,0:T(8,128)S(1)} %collective-permute-done.3.gb_ref, f32[128,512]{1,0:T(8,128)S(1)} %get-tuple-element.39.u_ref, ...), custom_call_target="tpu_custom_call" | custom-call | flops 1000000000 | bytes 1000000 | tf_op jit(solution)/shard_map/pallas_call | solution.py:560
  19.1 1.6 %collective-permute-start.6 = (f32[32,144]{1,0:T(8,128)S(1)}, f32[32,144]{1,0:T(8,128)S(1)}, u32[]{:S(2)}, u32[]{:S(2)}) collective-permute-start(f32[32,144]{1,0:T(8,128)S(1)} %get-tuple-element.66), channel_id=1, source_target_pairs={{1,2},{2,1},{3,0},{0,3},{5,6},{6,5},{7,4},{4,7},{9,10},{10,9},{11,... | collective-permute-start | bytes 55304 | tf_op jit(solution)/shard_map/ppermute | solution.py:585
  20.7 1.5 %collective-permute-start.5 = (f32[32,144]{1,0:T(8,128)S(1)}, f32[32,144]{1,0:T(8,128)S(1)}, u32[]{:S(2)}, u32[]{:S(2)}) collective-permute-start(f32[32,144]{1,0:T(8,128)S(1)} %get-tuple-element.67), channel_id=1, source_target_pairs={{0,1},{1,0},{2,3},{3,2},{4,5},{5,4},{6,7},{7,6},{8,9},{9,8},{10,11... | collective-permute-start | bytes 55304 | tf_op jit(solution)/shard_map/ppermute | solution.py:586
  22.1 0.8 %shard_map.54 = (f32[144,384]{1,0:T(8,128)S(1)}, f32[160,384]{1,0:T(8,128)S(1)}) custom-call(f32[144,512]{1,0:T(8,128)S(1)} %get-tuple-element.41.t_ref, f32[816,512]{1,0:T(8,128)S(1)} %copy-done, f32[256,256]{1,0:T(8,128)S(1)} %pad_add_fusion.both_ref, f32[128,128]{1,0:T(8,128)S(1)} %get-tuple-element.42.h3_ref, ...), custom_call_target="tpu_custom_call" | custom-call | flops 1000000000 | bytes 1000000 | tf_op jit(solution)/shard_map/pallas_call | solution.py:560
  23.0 1.0 %collective-permute-done.6.gb_ref = f32[32,144]{1,0:T(8,128)S(1)} collective-permute-done((f32[32,144]{1,0:T(8,128)S(1)}, f32[32,144]{1,0:T(8,128)S(1)}, u32[]{:S(2)}, u32[]{:S(2)}) %collective-permute-start.6) | collective-permute-done | bytes 18464 | tf_op jit(solution)/shard_map/ppermute | solution.py:585
  24.0 0.6 %collective-permute-done.5.ga_ref = f32[32,144]{1,0:T(8,128)S(1)} collective-permute-done((f32[32,144]{1,0:T(8,128)S(1)}, f32[32,144]{1,0:T(8,128)S(1)}, u32[]{:S(2)}, u32[]{:S(2)}) %collective-permute-start.5) | collective-permute-done | bytes 18464 | tf_op jit(solution)/shard_map/ppermute | solution.py:586
  24.6 0.2 shard_map.55
  24.8 0.1 collective-permute-start.7
  24.8 0.5 collective-permute-start.8
  25.3 0.7 %collective-permute-done.7.ga_ref = f32[32,384]{1,0:T(8,128)S(1)} collective-permute-done((f32[32,384]{1,0:T(8,128)S(1)}, f32[32,384]{1,0:T(8,128)S(1)}, u32[]{:S(2)}, u32[]{:S(2)}) %collective-permute-start.7) | collective-permute-done | bytes 49184 | tf_op jit(solution)/shard_map/ppermute | solution.py:586
  26.1 4.2 %collective-permute-done.8.gb_ref = f32[32,384]{1,0:T(8,128)S(1)} collective-permute-done((f32[32,384]{1,0:T(8,128)S(1)}, f32[32,384]{1,0:T(8,128)S(1)}, u32[]{:S(2)}, u32[]{:S(2)}) %collective-permute-start.8) | collective-permute-done | bytes 49184 | tf_op jit(solution)/shard_map/ppermute | solution.py:585
  30.2 1.9 %shard_map.56 = (f32[128,256]{1,0:T(8,128)S(1)}, f32[128,256]{1,0:T(8,128)S(1)}, f32[144,512]{1,0:T(8,128)S(1)}, f32[8,128]{1,0:T(8,128)S(1)}, f32[24,144]{1,0:T(8,128)S(1)}, /*index=5*/f32[24,144]{1,0:T(8,128)S(1)}) custom-call(f32[144,384]{1,0:T(8,128)S(1)} %get-tuple-element.47.y_ref, f32[160,384]{1,0:T(8,128)S(1)} %get-tuple-element.48.m_ref, ...), custom_call_target="tpu_custom_call" | custom-call | flops 1000000000 | bytes 1000000 | tf_op jit(solution)/shard_map/pallas_call | solution.py:560
  32.2 1.6 %collective-permute-start.9 = (f32[24,144]{1,0:T(8,128)S(1)}, f32[24,144]{1,0:T(8,128)S(1)}, u32[]{:S(2)}, u32[]{:S(2)}) collective-permute-start(f32[24,144]{1,0:T(8,128)S(1)} %get-tuple-element.56), channel_id=1, source_target_pairs={{0,1},{1,0},{2,3},{3,2},{4,5},{5,4},{6,7},{7,6},{8,9},{9,8},{10,11... | collective-permute-start | bytes 41480 | tf_op jit(solution)/shard_map/ppermute | solution.py:586
  33.7 0.9 %collective-permute-start.10 = (f32[24,144]{1,0:T(8,128)S(1)}, f32[24,144]{1,0:T(8,128)S(1)}, u32[]{:S(2)}, u32[]{:S(2)}) collective-permute-start(f32[24,144]{1,0:T(8,128)S(1)} %get-tuple-element.57), channel_id=1, source_target_pairs={{1,2},{2,1},{3,0},{0,3},{5,6},{6,5},{7,4},{4,7},{9,10},{10,9},{11,... | collective-permute-start | bytes 41480 | tf_op jit(solution)/shard_map/ppermute | solution.py:585
  34.6 0.8 %shard_map.57 = (f32[144,384]{1,0:T(8,128)S(1)}, f32[1,128]{1,0:T(1,128)S(1)}) custom-call(f32[144,512]{1,0:T(8,128)S(1)} %get-tuple-element.52.t_ref, f32[816,512]{1,0:T(8,128)S(1)} %copy-done, f32[256,256]{1,0:T(8,128)S(1)} %pad_add_fusion.both_ref, f32[160,384]{1,0:T(8,128)S(1)} %get-tuple-element.48.m_ref, f32[128,256]{1,0:T(8,128)S(1)} %get-tuple-element.53.z_ref, ...), custom_call_target="tpu_custom_call" | custom-call | flops 1000000000 | bytes 1000000 | tf_op jit(solution)/shard_map/pallas_call | solution.py:560
  35.5 0.6 %collective-permute-done.9.ga_ref = f32[24,144]{1,0:T(8,128)S(1)} collective-permute-done((f32[24,144]{1,0:T(8,128)S(1)}, f32[24,144]{1,0:T(8,128)S(1)}, u32[]{:S(2)}, u32[]{:S(2)}) %collective-permute-start.9) | collective-permute-done | bytes 13856 | tf_op jit(solution)/shard_map/ppermute | solution.py:586
  36.1 2.4 %collective-permute-done.10.gb_ref = f32[24,144]{1,0:T(8,128)S(1)} collective-permute-done((f32[24,144]{1,0:T(8,128)S(1)}, f32[24,144]{1,0:T(8,128)S(1)}, u32[]{:S(2)}, u32[]{:S(2)}) %collective-permute-start.10) | collective-permute-done | bytes 13856 | tf_op jit(solution)/shard_map/ppermute | solution.py:585
  38.5 0.2 shard_map.58
  38.6 0.1 collective-permute-start.11
  38.7 0.1 collective-permute-start.12
  38.8 1.1 %collective-permute-done.11.ga_ref = f32[24,384]{1,0:T(8,128)S(1)} collective-permute-done((f32[24,384]{1,0:T(8,128)S(1)}, f32[24,384]{1,0:T(8,128)S(1)}, u32[]{:S(2)}, u32[]{:S(2)}) %collective-permute-start.11) | collective-permute-done | bytes 36896 | tf_op jit(solution)/shard_map/ppermute | solution.py:586
  39.9 4.0 %collective-permute-done.12.gb_ref = f32[24,384]{1,0:T(8,128)S(1)} collective-permute-done((f32[24,384]{1,0:T(8,128)S(1)}, f32[24,384]{1,0:T(8,128)S(1)}, u32[]{:S(2)}, u32[]{:S(2)}) %collective-permute-start.12) | collective-permute-done | bytes 36896 | tf_op jit(solution)/shard_map/ppermute | solution.py:585
  44.0 0.4 shard_map.59
  44.4 8.9 %all_to_all.11 = f32[32,1,128]{2,1,0:T(1,128)S(1)} all-to-all(f32[32,1,128]{2,1,0:T(1,128)S(1)} %bitcast.5), channel_id=1, replica_groups=mesh['row'=8,'col'=4] {'row','col'}, dimensions={0} | all-to-all | bytes 32768 | tf_op jit(solution)/shard_map/all_to_all | solution.py:673
  53.3 1.4 %shard_map.60 = (f32[128,256]{1,0:T(8,128)}, f32[128,256]{1,0:T(8,128)}) custom-call(f32[32,128]{1,0:T(8,128)S(1)} %bitcast.4, f32[8,128]{1,0:T(8,128)S(1)} %get-tuple-element.63.table_ref, f32[816,512]{1,0:T(8,128)S(1)} %copy-done, f32[160,384]{1,0:T(8,128)S(1)} %get-tuple-element.48.m_ref, f32[256,256]{1,0:T(8,128)S(1)} %pad_add_fusion.both_ref, ...), custom_call_target="tpu_custom_call" | custom-call | flops 1000000000 | bytes 1000000 | tf_op jit(solution)/shard_map/pallas_call | solution.py:560
  (2 shorter events, 0.0 us)
Async XLA Ops:
  1.8 4.8 %collective-permute-start = (f32[40,128]{1,0:T(8,128)S(1)}, f32[40,128]{1,0:T(8,128)S(1)}, u32[]{:S(2)}, u32[]{:S(2)}) collective-permute-start(f32[40,128]{1,0:T(8,128)S(1)} %get-tuple-element.34), channel_id=1, source_target_pairs={{0,1},{1,0},{2,3},{3,2},{4,5},{5,4},{6,7},{7,6},{8,9},{9,8},{10,11... | collective-permute-start | bytes 61448 | tf_op jit(solution)/shard_map/ppermute | solution.py:586
  4.8 9.0 %copy-start = (f32[816,512]{1,0:T(8,128)S(1)}, f32[816,512]{1,0:T(8,128)}, u32[]{:S(2)}) copy-start(f32[816,512]{1,0:T(8,128)} %constant.5.clone.basis_ref) | copy-start | bytes 5013508
  4.8 4.7 %collective-permute-start.1 = (f32[40,128]{1,0:T(8,128)S(1)}, f32[40,128]{1,0:T(8,128)S(1)}, u32[]{:S(2)}, u32[]{:S(2)}) collective-permute-start(f32[40,128]{1,0:T(8,128)S(1)} %get-tuple-element.35), channel_id=1, source_target_pairs={{1,2},{2,1},{3,0},{0,3},{5,6},{6,5},{7,4},{4,7},{9,10},{10,9},{11,... | collective-permute-start | bytes 61448 | tf_op jit(solution)/shard_map/ppermute | solution.py:585
  9.7 4.6 %collective-permute-start.4 = (f32[8,128]{1,0:T(8,128)S(1)}, f32[8,128]{1,0:T(8,128)S(1)}, u32[]{:S(2)}, u32[]{:S(2)}) collective-permute-start(f32[8,128]{1,0:T(8,128)S(1)} %get-tuple-element.45), channel_id=1, source_target_pairs={{0,16},{4,20},{8,24},{12,28},{16,0},{20,4},{24,8},{28,12},{1,17},{... | collective-permute-start | bytes 12296 | tf_op jit(solution)/shard_map/ppermute | solution.py:589
  12.3 1.9 %collective-permute-start.2 = (f32[32,384]{1,0:T(8,128)S(1)}, f32[32,384]{1,0:T(8,128)S(1)}, u32[]{:S(2)}, u32[]{:S(2)}) collective-permute-start(f32[32,384]{1,0:T(8,128)S(1)} %get-tuple-element.36), channel_id=1, source_target_pairs={{0,4},{4,0},{8,12},{12,8},{16,20},{20,16},{24,28},{28,24},{1,5},{5... | collective-permute-start | bytes 147464 | tf_op jit(solution)/shard_map/ppermute | solution.py:586
  12.3 5.4 %collective-permute-start.3 = (f32[32,384]{1,0:T(8,128)S(1)}, f32[32,384]{1,0:T(8,128)S(1)}, u32[]{:S(2)}, u32[]{:S(2)}) collective-permute-start(f32[32,384]{1,0:T(8,128)S(1)} %get-tuple-element.37), channel_id=1, source_target_pairs={{4,8},{8,4},{12,16},{16,12},{20,24},{24,20},{28,0},{0,28},{5,9},{9... | collective-permute-start | bytes 147464 | tf_op jit(solution)/shard_map/ppermute | solution.py:585
  19.1 4.9 %collective-permute-start.6 = (f32[32,144]{1,0:T(8,128)S(1)}, f32[32,144]{1,0:T(8,128)S(1)}, u32[]{:S(2)}, u32[]{:S(2)}) collective-permute-start(f32[32,144]{1,0:T(8,128)S(1)} %get-tuple-element.66), channel_id=1, source_target_pairs={{1,2},{2,1},{3,0},{0,3},{5,6},{6,5},{7,4},{4,7},{9,10},{10,9},{11,... | collective-permute-start | bytes 55304 | tf_op jit(solution)/shard_map/ppermute | solution.py:585
  20.7 3.9 %collective-permute-start.5 = (f32[32,144]{1,0:T(8,128)S(1)}, f32[32,144]{1,0:T(8,128)S(1)}, u32[]{:S(2)}, u32[]{:S(2)}) collective-permute-start(f32[32,144]{1,0:T(8,128)S(1)} %get-tuple-element.67), channel_id=1, source_target_pairs={{0,1},{1,0},{2,3},{3,2},{4,5},{5,4},{6,7},{7,6},{8,9},{9,8},{10,11... | collective-permute-start | bytes 55304 | tf_op jit(solution)/shard_map/ppermute | solution.py:586
  24.8 1.3 %collective-permute-start.7 = (f32[32,384]{1,0:T(8,128)S(1)}, f32[32,384]{1,0:T(8,128)S(1)}, u32[]{:S(2)}, u32[]{:S(2)}) collective-permute-start(f32[32,384]{1,0:T(8,128)S(1)} %get-tuple-element.49), channel_id=1, source_target_pairs={{0,4},{4,0},{8,12},{12,8},{16,20},{20,16},{24,28},{28,24},{1,5},{5... | collective-permute-start | bytes 147464 | tf_op jit(solution)/shard_map/ppermute | solution.py:586
  24.8 5.4 %collective-permute-start.8 = (f32[32,384]{1,0:T(8,128)S(1)}, f32[32,384]{1,0:T(8,128)S(1)}, u32[]{:S(2)}, u32[]{:S(2)}) collective-permute-start(f32[32,384]{1,0:T(8,128)S(1)} %get-tuple-element.50), channel_id=1, source_target_pairs={{4,8},{8,4},{12,16},{16,12},{20,24},{24,20},{28,0},{0,28},{5,9},{9... | collective-permute-start | bytes 147464 | tf_op jit(solution)/shard_map/ppermute | solution.py:585
  32.2 3.9 %collective-permute-start.9 = (f32[24,144]{1,0:T(8,128)S(1)}, f32[24,144]{1,0:T(8,128)S(1)}, u32[]{:S(2)}, u32[]{:S(2)}) collective-permute-start(f32[24,144]{1,0:T(8,128)S(1)} %get-tuple-element.56), channel_id=1, source_target_pairs={{0,1},{1,0},{2,3},{3,2},{4,5},{5,4},{6,7},{7,6},{8,9},{9,8},{10,11... | collective-permute-start | bytes 41480 | tf_op jit(solution)/shard_map/ppermute | solution.py:586
  33.7 4.7 %collective-permute-start.10 = (f32[24,144]{1,0:T(8,128)S(1)}, f32[24,144]{1,0:T(8,128)S(1)}, u32[]{:S(2)}, u32[]{:S(2)}) collective-permute-start(f32[24,144]{1,0:T(8,128)S(1)} %get-tuple-element.57), channel_id=1, source_target_pairs={{1,2},{2,1},{3,0},{0,3},{5,6},{6,5},{7,4},{4,7},{9,10},{10,9},{11,... | collective-permute-start | bytes 41480 | tf_op jit(solution)/shard_map/ppermute | solution.py:585
  38.6 1.3 %collective-permute-start.11 = (f32[24,384]{1,0:T(8,128)S(1)}, f32[24,384]{1,0:T(8,128)S(1)}, u32[]{:S(2)}, u32[]{:S(2)}) collective-permute-start(f32[24,384]{1,0:T(8,128)S(1)} %get-tuple-element.59), channel_id=1, source_target_pairs={{0,4},{4,0},{8,12},{12,8},{16,20},{20,16},{24,28},{28,24},{1,5},{5... | collective-permute-start | bytes 110600 | tf_op jit(solution)/shard_map/ppermute | solution.py:586
  38.7 5.2 %collective-permute-start.12 = (f32[24,384]{1,0:T(8,128)S(1)}, f32[24,384]{1,0:T(8,128)S(1)}, u32[]{:S(2)}, u32[]{:S(2)}) collective-permute-start(f32[24,384]{1,0:T(8,128)S(1)} %get-tuple-element.60), channel_id=1, source_target_pairs={{4,8},{8,4},{12,16},{16,12},{20,24},{24,20},{28,0},{0,28},{5,9},{9... | collective-permute-start | bytes 110600 | tf_op jit(solution)/shard_map/ppermute | solution.py:585

commit v6 on v5

--- a/solution.py
+++ b/solution.py
@@ -2,6 +2,7 @@
 
 import jax
 import jax.numpy as jnp
+import ml_dtypes
 import numpy as np
 from jax import lax
 from jax.experimental import pallas as pl
@@ -33,7 +34,12 @@
     cols = np.pad(basis, ((0, SPEC - EXT), (0, SPEC - EXT)))
     scale = np.pad((eig[:, None] + eig[None, :]) ** 2, ((0, 0), (0, SPEC - EXT)))
     wide = lambda x: np.pad(x, ((0, 0), (0, 2 * SPEC - x.shape[1])))
-    return [np.tile(scale, (1, 2)), wide(rows), wide(rows.T), wide(cols)]
+    high = rows.T.astype(ml_dtypes.bfloat16).astype(np.float64)
+    low = (rows.T - high).astype(ml_dtypes.bfloat16).astype(np.float64)
+    tile = np.concatenate([x[:, :SUB] for x in (high, high, low)], 1)
+    halo = np.concatenate([x[:, SUB:] for x in (high, high, low)], 1)
+    whole = np.concatenate([high, high, low], 1)
+    return [np.tile(scale, (1, 2)), *(wide(x) for x in (rows, rows.T, cols, whole, np.hstack([tile, halo])))]
 
 
 def rows_part(ref):
@@ -48,8 +54,23 @@
     return ref[3 * EXT : 3 * EXT + SPEC, :SPEC]
 
 
+def whole_rows(ref):
+    at = 3 * EXT + SPEC
+    return ref[at : at + EXT, : 3 * EXT]
+
+
+def tile_rows(ref):
+    at = 4 * EXT + SPEC
+    return ref[at : at + EXT, : 3 * SUB]
+
+
+def halo_rows(ref):
+    at = 4 * EXT + SPEC
+    return ref[at : at + EXT, 3 * SUB : 3 * EXT]
+
+
 def coarse_part(ref, width):
-    at, lanes = 3 * EXT + SPEC, 2 * SPEC
+    at, lanes = 5 * EXT + SPEC, 2 * SPEC
     parts = [ref[at + k * width : at + (k + 1) * width] for k in range(-(-width // lanes))]
     return (parts[0] if len(parts) == 1 else jnp.concatenate(parts, axis=1))[:, :width]
 
@@ -196,10 +217,31 @@
     )
 
 
+def halves_of(x):
+    high = x.astype(jnp.bfloat16)
+    return high, (x - high.astype(jnp.float32)).astype(jnp.bfloat16)
+
+
+def product(a, b):
+    return lax.dot_general(a, b, (((1,), (0,)), ((), ())), preferred_element_type=jnp.float32)
+
+
 def column_transform(w, basis_ref):
-    w = pltpu.roll(w, OV, 1)
-    cols = cols_part(basis_ref)
-    return jnp.concatenate([dot(w[:, :256], cols), dot(w[:, 128:], cols)], axis=1)
+    high, low = halves_of(pltpu.roll(w, OV, 1))
+    cols, rest = halves_of(cols_part(basis_ref))
+    cols = jnp.concatenate([cols, rest, cols], axis=0)
+
+    def block(at):
+        part = slice(at, at + SPEC)
+        return product(jnp.concatenate([high[:, part], high[:, part], low[:, part]], axis=1), cols)
+
+    return jnp.concatenate([block(0), block(128)], axis=1)
+
+
+def row_transform(u, basis_ref, part):
+    high, low = halves_of(u)
+    rows = part(basis_ref).astype(jnp.bfloat16)
+    return product(rows, jnp.concatenate([high, low, high], axis=0))
 
 
 def weights(means, basis_ref):
@@ -208,12 +250,12 @@
     return 1.0 / (DAMP + mean * basis_ref[:EXT])
 
 
-def strips_of(t, basis_ref):
+def strips_of(t, basis_ref, deep):
     cols = cols_part(basis_ref)
-    left = dot(cols[:24], t[:, :SPEC], 1)
-    right = dot(cols[EXT - 24 : EXT], t[:, SPEC:], 1)
+    left = dot(cols[:deep], t[:, :SPEC], 1)
+    right = dot(cols[EXT - deep : EXT], t[:, SPEC:], 1)
     both = dot(jnp.concatenate([left, right], axis=0), rows_t_part(basis_ref))
-    return both[:24], both[24:]
+    return both[:deep], both[deep:]
 
 
 def solution_of(t, basis_ref):
@@ -231,16 +273,10 @@
 
 
 def add_columns(y, from_left, from_right):
+    far = from_left.shape[0] - OV
+    gap = jnp.zeros((56 - far, EXT), jnp.float32)
     turned = jnp.concatenate(
-        [
-            from_right[8:24],
-            jnp.zeros((40, EXT), jnp.float32),
-            from_right[:8],
-            from_left[16:24],
-            jnp.zeros((40, EXT), jnp.float32),
-            from_left[:16],
-        ],
-        axis=0,
+        [from_right[8:], gap, from_right[:8], from_left[far:], gap, from_left[:far]], axis=0
     )
     back = turned.T
     lane = lanes_of((EXT, 128))
@@ -251,19 +287,21 @@
     return jnp.concatenate([first, second, third], axis=1)
 
 
-def pack_rows(y):
-    return jnp.concatenate([y[136:], y[:16]], axis=0), y[112:136]
+def pack_rows(y, deep):
+    return jnp.concatenate([y[136:], y[: deep - 8]], axis=0), y[136 - deep : 136]
 
 
 def add_rows(y, from_above, from_below):
+    far = from_above.shape[0] - OV
+    none = jnp.zeros((8, FC), jnp.float32)
     return jnp.concatenate(
         [
-            y[:8] + from_above[16:],
+            y[:8] + from_above[far:],
             y[8:120],
             y[120:136] + from_below[:16],
-            from_below[16:],
-            from_above[:8],
-            y[136:] + from_above[8:16],
+            from_below[16:] if far == 16 else none,
+            from_above[:8] if far == 16 else none,
+            y[136:] + from_above[far - 8 : far],
         ],
         axis=0,
     )
@@ -298,7 +336,7 @@
     b_ref[...] = jnp.where(even, before, after)
 
 
-def begin_kernel(counts, both_ref, a_ref, b_ref):
+def begin_kernel(counts, both_ref, b_ref, a_ref):
     r, h = both_ref[:TR], both_ref[TR:]
     lane = lanes_of((128, 128))
     packed = jnp.where(
@@ -321,7 +359,7 @@
     )
 
 
-def widen_kernel(counts, both_ref, ga_ref, gb_ref, r3_ref, h3_ref, table_ref, a_ref, b_ref):
+def widen_kernel(counts, both_ref, gb_ref, ga_ref, r3_ref, h3_ref, table_ref, b_ref, a_ref):
     i, j = place()
     from_left, from_right = sides(j, counts[1], ga_ref[:32], gb_ref[:32])
     turned = jnp.concatenate([from_right, jnp.zeros((64, 128), jnp.float32), from_left], axis=0)
@@ -352,24 +390,38 @@
     send(i, a_ref, b_ref, strip(slice(0, 8), slice(0, 16)), strip(slice(120, 128), slice(112, 128)))
 
 
-def forward_kernel(both_ref, r3_ref, basis_ref, u_ref, weights_ref):
+def forward_kernel(both_ref, r3_ref, basis_ref, table_ref, t_ref, weights_ref, table_out):
     r, h = both_ref[:TR], both_ref[TR:]
-    u_ref[...] = column_transform(jnp.concatenate([r, r3_ref[...]], axis=1), basis_ref)
+    u = column_transform(jnp.concatenate([r, r3_ref[...]], axis=1), basis_ref)
+    t_ref[...] = row_transform(u, basis_ref, tile_rows)
     means = [x / (SUB * SUB) for x in core_sums(h * h * h)]
     weights_ref[...] = weights(means, basis_ref)
-
-
-def first_kernel(counts, ga_ref, gb_ref, u_ref, weights_ref, basis_ref, t_ref, a_ref, b_ref):
+    table_out[...] = table_ref[...]
+
+
+def first_kernel(
+    counts,
+    gb_ref,
+    ga_ref,
+    tile_ref,
+    weights_ref,
+    basis_ref,
+    table_ref,
+    t_ref,
+    table_out,
+    b_ref,
+    a_ref,
+):
     i, j = place()
     above, below = sides(i, counts[0], ga_ref[:8], gb_ref[:8])
-    halo = column_transform(jnp.concatenate([below, above], axis=0), basis_ref)
-    u = jnp.concatenate([u_ref[...], halo], axis=0)
-    t = dot(rows_t_part(basis_ref), u) * weights_ref[...]
+    u = column_transform(jnp.concatenate([below, above], axis=0), basis_ref)
+    t = (tile_ref[...] + row_transform(u, basis_ref, halo_rows)) * weights_ref[...]
     t_ref[...] = t
-    send(j, a_ref, b_ref, *strips_of(t, basis_ref))
-
-
-def inverse_kernel(counts, t_ref, basis_ref, both_ref, h3_ref, ga_ref, gb_ref, y_ref, m_ref):
+    send(j, a_ref, b_ref, *strips_of(t, basis_ref, 24))
+    table_out[...] = table_ref[...] + ga_ref[24:, :128] + gb_ref[24:, :128]
+
+
+def inverse_kernel(counts, t_ref, basis_ref, both_ref, h3_ref, gb_ref, ga_ref, y_ref, m_ref):
     y_ref[...] = solution_of(t_ref[...], basis_ref)
     above, below = sides(lax.axis_index("row"), counts[0], ga_ref[8:24], gb_ref[8:24])
     h = jnp.concatenate([both_ref[TR:], h3_ref[...]], axis=1)
@@ -377,12 +429,14 @@
     m_ref[...] = tall * tall * tall
 
 
-def columns_kernel(counts, y_ref, ga_ref, gb_ref, *refs):
+def columns_kernel(counts, y_ref, *refs):
     i, j = place()
-    y = add_columns(y_ref[...], *sides(j, counts[1], ga_ref[:24], gb_ref[:24]))
-    strips = pack_rows(y)
+    (ga_ref, gb_ref), refs = (refs[:2] if len(refs) == 7 else refs[1::-1]), refs[2:]
+    deep = 24 if len(refs) == 5 else 16
+    y = add_columns(y_ref[...], *sides(j, counts[1], ga_ref[:deep], gb_ref[:deep]))
+    strips = pack_rows(y, deep)
     if len(refs) == 5:
-        table_ref, out_ref, table_out, a_ref, b_ref = refs
+        table_ref, out_ref, table_out, b_ref, a_ref = refs
         cols = flat_place(counts)[2]
         table = table_ref[...] + jnp.where(
             cols % 4 == 2, next_table(j, ga_ref[...], gb_ref[...]), 0.0
@@ -391,7 +445,7 @@
         wide = jnp.concatenate([table, jnp.zeros((table.shape[0], FC - 128), jnp.float32)], axis=1)
         strips = [jnp.concatenate([x, wide], axis=0) for x in strips]
     else:
-        out_ref, a_ref, b_ref = refs
+        out_ref, b_ref, a_ref = refs
     out_ref[...] = y
     send(i, a_ref, b_ref, *strips)
 
@@ -401,8 +455,8 @@
     width,
     y_ref,
     m_ref,
+    gb_ref,
     ga_ref,
-    gb_ref,
     table_ref,
     weights_ref,
     basis_ref,
@@ -410,8 +464,8 @@
     w_ref,
     t_ref,
     table_out,
+    b_ref,
     a_ref,
-    b_ref,
 ):
     i, j = place()
     s = add_rows(y_ref[...], *sides(i, counts[0], ga_ref[:24], gb_ref[:24]))
@@ -429,9 +483,9 @@
     z_ref[...] = z[:128, :256]
     w_ref[...] = w[:128, :256]
     u = column_transform(jnp.concatenate([w[:136], w[152:]], axis=0), basis_ref)
-    t = dot(rows_t_part(basis_ref), u) * weights_ref[...]
+    t = row_transform(u, basis_ref, whole_rows) * weights_ref[...]
     t_ref[...] = t
-    send(j, a_ref, b_ref, *strips_of(t, basis_ref))
+    send(j, a_ref, b_ref, *strips_of(t, basis_ref, 16))
 
 
 def inverse_stats_kernel(t_ref, basis_ref, both_ref, m_ref, z_ref, w_ref, y_ref, stats_ref):
@@ -467,7 +521,7 @@
 
 
 def dots_kernel(
-    counts, y_ref, m_ref, ga_ref, gb_ref, both_ref, w_ref, stats_ref, q_ref, v_ref, stats_out
+    counts, y_ref, m_ref, gb_ref, ga_ref, both_ref, w_ref, stats_ref, q_ref, v_ref, stats_out
 ):
     i, j = place()
     q = add_rows(y_ref[...], *sides(i, counts[0], ga_ref[...], gb_ref[...]))
@@ -589,14 +643,14 @@
         return lax.ppermute(x, "row", [(k, (k + step) % nr) for k in range(nr)])
 
     both = jnp.pad(noise, ((0, TR), (0, 0))) + jnp.pad(height, ((TR, 0), (0, 0)))
-    a, b = call(functools.partial(begin_kernel, counts), [(32 + depth, 128)] * 2, both)
+    b, a = call(functools.partial(begin_kernel, counts), [(32 + depth, 128)] * 2, both)
     ga, gb = swap(a, b, "col")
-    r3, h3, table, a, b = call(
+    r3, h3, table, b, a = call(
         functools.partial(widen_kernel, counts),
         [(128, 128)] * 2 + [(depth, 128)] + [(24 + depth, FC)] * 2,
         both,
+        gb,
         ga,
-        gb,
     )
     step = nr // 2
     while step >= 8:
@@ -605,18 +659,21 @@
     if nr > 8:
         a, b = (x.at[24:, :128].set(table) for x in (a, b))
     ga, gb = swap(a, b, "row")
+    t, weight, table = call(
+        forward_kernel, [(EXT, 2 * SPEC)] * 2 + [(depth, 128)], both, r3, basis, table
+    )
     far = row_shift(table, 4) if nr >= 8 else 0.0
-    u, weight = call(forward_kernel, [(TR, 2 * SPEC), (EXT, 2 * SPEC)], both, r3, basis)
-    t, a, b = call(
+    t, table, b, a = call(
         functools.partial(first_kernel, counts),
-        [(EXT, 2 * SPEC)] + [(24, EXT)] * 2,
+        [(EXT, 2 * SPEC), (depth, 128)] + [(24, EXT)] * 2,
+        gb,
         ga,
-        gb,
-        u,
+        t,
         weight,
         basis,
-    )
-    table = table + ga[24:, :128] + gb[24:, :128] + far
+        table,
+    )
+    table = table + far
     step = nc // 2
     while step >= 4:
         table = table + lax.ppermute(table, "col", [(k, (k + step) % nc) for k in range(nc)])
@@ -629,11 +686,11 @@
         basis,
         both,
         h3,
+        gb,
         ga,
-        gb,
     )
     ga, gb = swap(*(jnp.concatenate([x, wide], axis=0) for x in (a, b)), "col")
-    y, table, a, b = call(
+    y, table, b, a = call(
         functools.partial(columns_kernel, counts),
         [(EXT, FC), (depth, 128)] + [(24 + depth, FC)] * 2,
         y,
@@ -642,21 +699,21 @@
         table,
     )
     ga, gb = swap(a, b, "row")
-    z, w, t, table, a, b = call(
+    z, w, t, table, b, a = call(
         functools.partial(second_kernel, counts, width),
-        [(TR, TC)] * 2 + [(EXT, 2 * SPEC), (depth, 128)] + [(24, EXT)] * 2,
+        [(TR, TC)] * 2 + [(EXT, 2 * SPEC), (depth, 128)] + [(16, EXT)] * 2,
         y,
         m,
+        gb,
         ga,
-        gb,
         table,
         weight,
         basis,
     )
     ga, gb = swap(a, b, "col")
     y, stats = call(inverse_stats_kernel, [(EXT, FC), (1, 128)], t, basis, both, m, z, w)
-    y, a, b = call(
-        functools.partial(columns_kernel, counts), [(EXT, FC)] + [(24, FC)] * 2, y, ga, gb
+    y, b, a = call(
+        functools.partial(columns_kernel, counts), [(EXT, FC)] + [(16, FC)] * 2, y, gb, ga
     )
     ga, gb = swap(a, b, "row")
     q, v, stats = call(
@@ -664,8 +721,8 @@
         [(TR, TC)] * 2 + [(devices, 128)],
         y,
         m,
+        gb,
         ga,
-        gb,
         both,
         w,
         stats,

time: 54.8 us -> 50.9 us (0.929)
  waiting for transfers between devices: 21.4 us -> 17.9 us
    ppermute x6, waiting for transfers between devices: 18 us -> 14.3 us  [swap(): gb = lax.ppermute(b, axis, pairs_from(count, 1))]
    ppermute x6, starting transfers between devices: 5.97 us -> 9.12 us  [swap(): gb = lax.ppermute(b, axis, pairs_from(count, 1))]
    ppermute x6, starting transfers between devices: 6.2 us -> 3.32 us  [swap(): return (lax.ppermute(a, axis, pairs_from(count, 0)), gb)]
  transfers between devices with their start and end apart: 13 -> 13, of which waited for: 11 -> 9; matrix products, arithmetic and copies ran while one was open for 0% -> 0% of each run, Pallas kernels for 4% -> 6%
where the time goes in v6:
time: 50.9 us; the launch traced here: 50.8 us
  waiting for transfers between devices  17.9 us (35%)
  starting transfers between devices  14.9 us (29%)
  blocking collectives  8.86 us (17%)
  Pallas kernels  7.42 us (15%)
  other arithmetic  1 us (2%)
  between operations  0.73 us (1%)
    ppermute x6, waiting for transfers between devices, swap(): gb = lax.ppermute(b, axis, pairs_from(count, 1))  14.3 us
    ppermute x6, starting transfers between devices, swap(): gb = lax.ppermute(b, axis, pairs_from(count, 1))  9.12 us
    all_to_all x1, blocking collectives, body(): stats = lax.all_to_all(stats, both_axes, 0, 0, tiled=True)  8.86 us
    pallas_call x11, Pallas kernels, call(): pl.pallas_call(kernel, out_shape=shapes, compiler_params=pltpu.CompilerPa...  7.42 us
    ppermute x6, starting transfers between devices, swap(): return (lax.ppermute(a, axis, pairs_from(count, 0)), gb)  3.32 us
    ppermute x6, waiting for transfers between devices, swap(): return (lax.ppermute(a, axis, pairs_from(count, 0)), gb)  3.15 us
    ppermute x1, starting transfers between devices, row_shift(): return lax.ppermute(x, 'row', [(k, (k + step) % nr) for k in range(nr)])  2.43 us
  transfers between devices with their start and end apart: 13, of which 9 were waited for; matrix products, arithmetic and copies ran while one was open for 0% of the time, Pallas kernels for 6%

profile of v6, /device:TPU:0, one launch (start us, length us, event | category | flops | bytes accessed | tf_op | source)
XLA Modules:
  0.0 50.8 jit_solution(5829739889772451279)
XLA Ops:
  0.6 1.0 %pad_add_fusion.both_ref = f32[256,256]{1,0:T(8,128)S(1)} fusion(f32[128,256]{1,0:T(8,128)} %param.3, f32[128,256]{1,0:T(8,128)} %param.4), kind=kLoop, calls=%fused_computation | loop fusion | flops 65536 | bytes 524288 | tf_op jit(solution)/shard_map/add | solution.py:645
  1.6 0.2 shard_map.50
  1.8 0.0 copy-start
  1.8 4.0 %collective-permute-start = (f32[40,128]{1,0:T(8,128)S(1)}, f32[40,128]{1,0:T(8,128)S(1)}, u32[]{:S(2)}, u32[]{:S(2)}) collective-permute-start(f32[40,128]{1,0:T(8,128)S(1)} %get-tuple-element.36), channel_id=1, source_target_pairs={{1,2},{2,1},{3,0},{0,3},{5,6},{6,5},{7,4},{4,7},{9,10},{10,9},{11,... | collective-permute-start | bytes 61448 | tf_op jit(solution)/shard_map/ppermute | solution.py:639
  5.8 0.5 %collective-permute-start.1 = (f32[40,128]{1,0:T(8,128)S(1)}, f32[40,128]{1,0:T(8,128)S(1)}, u32[]{:S(2)}, u32[]{:S(2)}) collective-permute-start(f32[40,128]{1,0:T(8,128)S(1)} %get-tuple-element.37), channel_id=1, source_target_pairs={{0,1},{1,0},{2,3},{3,2},{4,5},{5,4},{6,7},{7,6},{8,9},{9,8},{10,11... | collective-permute-start | bytes 61448 | tf_op jit(solution)/shard_map/ppermute | solution.py:640
  6.3 1.2 %collective-permute-done.gb_ref = f32[40,128]{1,0:T(8,128)S(1)} collective-permute-done((f32[40,128]{1,0:T(8,128)S(1)}, f32[40,128]{1,0:T(8,128)S(1)}, u32[]{:S(2)}, u32[]{:S(2)}) %collective-permute-start) | collective-permute-done | bytes 20512 | tf_op jit(solution)/shard_map/ppermute | solution.py:639
  7.5 2.0 %collective-permute-done.1.ga_ref = f32[40,128]{1,0:T(8,128)S(1)} collective-permute-done((f32[40,128]{1,0:T(8,128)S(1)}, f32[40,128]{1,0:T(8,128)S(1)}, u32[]{:S(2)}, u32[]{:S(2)}) %collective-permute-start.1) | collective-permute-done | bytes 20512 | tf_op jit(solution)/shard_map/ppermute | solution.py:640
  9.5 0.2 shard_map.51
  9.7 2.0 %collective-permute-start.2 = (f32[32,384]{1,0:T(8,128)S(1)}, f32[32,384]{1,0:T(8,128)S(1)}, u32[]{:S(2)}, u32[]{:S(2)}) collective-permute-start(f32[32,384]{1,0:T(8,128)S(1)} %get-tuple-element.38), channel_id=1, source_target_pairs={{4,8},{8,4},{12,16},{16,12},{20,24},{24,20},{28,0},{0,28},{5,9},{9... | collective-permute-start | bytes 147464 | tf_op jit(solution)/shard_map/ppermute | solution.py:639
  11.7 0.0 collective-permute-start.3
  11.7 0.0 copy-done
  11.7 0.6 %shard_map.52 = (f32[144,512]{1,0:T(8,128)S(1)}, f32[144,512]{1,0:T(8,128)S(1)}, f32[8,128]{1,0:T(8,128)S(1)}) custom-call(f32[256,256]{1,0:T(8,128)S(1)} %pad_add_fusion.both_ref, f32[128,128]{1,0:T(8,128)S(1)} %get-tuple-element.40.r3_ref, f32[1104,512]{1,0:T(8,128)S(1)} %copy-done, f32[8,128]{1,0:T(8,128)S(1)} %get-tuple-element.41.table_ref), custom_call_target="tpu_custom_call" | custom-call | flops 1000000000 | bytes 1000000 | tf_op jit(solution)/shard_map/pallas_call | solution.py:614
  12.3 2.4 %collective-permute-start.4 = (f32[8,128]{1,0:T(8,128)S(1)}, f32[8,128]{1,0:T(8,128)S(1)}, u32[]{:S(2)}, u32[]{:S(2)}) collective-permute-start(f32[8,128]{1,0:T(8,128)S(1)} %get-tuple-element.44.table_ref), channel_id=1, source_target_pairs={{0,16},{4,20},{8,24},{12,28},{16,0},{20,4},{24,8},{28,12},{1,17},{... | collective-permute-start | bytes 12296 | tf_op jit(solution)/shard_map/ppermute | solution.py:643
  14.7 0.6 %collective-permute-done.2.gb_ref = f32[32,384]{1,0:T(8,128)S(1)} collective-permute-done((f32[32,384]{1,0:T(8,128)S(1)}, f32[32,384]{1,0:T(8,128)S(1)}, u32[]{:S(2)}, u32[]{:S(2)}) %collective-permute-start.2) | collective-permute-done | bytes 49184 | tf_op jit(solution)/shard_map/ppermute | solution.py:639
  15.4 0.0 collective-permute-done.3.ga_ref
  15.4 1.0 %shard_map.53 = (f32[144,512]{1,0:T(8,128)S(1)}, f32[8,128]{1,0:T(8,128)S(1)}, f32[24,144]{1,0:T(8,128)S(1)}, f32[24,144]{1,0:T(8,128)S(1)}) custom-call(f32[32,384]{1,0:T(8,128)S(1)} %collective-permute-done.2.gb_ref, f32[32,384]{1,0:T(8,128)S(1)} %collective-permute-done.3.ga_ref, f32[144,512]{1,0:T(8,128)S(1)} %get-tuple-element.42.tile_ref, ...), custom_call_target="tpu_custom_call" | custom-call | flops 1000000000 | bytes 1000000 | tf_op jit(solution)/shard_map/pallas_call | solution.py:614
  16.4 0.5 collective-permute-done.4
  16.9 0.9 %collective-permute-start.6 = (f32[32,144]{1,0:T(8,128)S(1)}, f32[32,144]{1,0:T(8,128)S(1)}, u32[]{:S(2)}, u32[]{:S(2)}) collective-permute-start(f32[32,144]{1,0:T(8,128)S(1)} %get-tuple-element.70), channel_id=1, source_target_pairs={{1,2},{2,1},{3,0},{0,3},{5,6},{6,5},{7,4},{4,7},{9,10},{10,9},{11,... | collective-permute-start | bytes 55304 | tf_op jit(solution)/shard_map/ppermute | solution.py:639
  17.8 1.0 %collective-permute-start.5 = (f32[32,144]{1,0:T(8,128)S(1)}, f32[32,144]{1,0:T(8,128)S(1)}, u32[]{:S(2)}, u32[]{:S(2)}) collective-permute-start(f32[32,144]{1,0:T(8,128)S(1)} %get-tuple-element.71), channel_id=1, source_target_pairs={{0,1},{1,0},{2,3},{3,2},{4,5},{5,4},{6,7},{7,6},{8,9},{9,8},{10,11... | collective-permute-start | bytes 55304 | tf_op jit(solution)/shard_map/ppermute | solution.py:640
  18.8 0.8 %shard_map.54 = (f32[144,384]{1,0:T(8,128)S(1)}, f32[160,384]{1,0:T(8,128)S(1)}) custom-call(f32[144,512]{1,0:T(8,128)S(1)} %get-tuple-element.45.t_ref, f32[1104,512]{1,0:T(8,128)S(1)} %copy-done, f32[256,256]{1,0:T(8,128)S(1)} %pad_add_fusion.both_ref, f32[128,128]{1,0:T(8,128)S(1)} %get-tuple-element.46.h3_ref, ...), custom_call_target="tpu_custom_call" | custom-call | flops 1000000000 | bytes 1000000 | tf_op jit(solution)/shard_map/pallas_call | solution.py:614
  19.6 2.2 %collective-permute-done.6.refs_1_ = f32[32,144]{1,0:T(8,128)S(1)} collective-permute-done((f32[32,144]{1,0:T(8,128)S(1)}, f32[32,144]{1,0:T(8,128)S(1)}, u32[]{:S(2)}, u32[]{:S(2)}) %collective-permute-start.6) | collective-permute-done | bytes 18464 | tf_op jit(solution)/shard_map/ppermute | solution.py:639
  21.8 0.0 collective-permute-done.5.refs_0_
  21.8 0.2 shard_map.55
  21.9 0.1 collective-permute-start.7
  22.1 1.4 %collective-permute-start.8 = (f32[32,384]{1,0:T(8,128)S(1)}, f32[32,384]{1,0:T(8,128)S(1)}, u32[]{:S(2)}, u32[]{:S(2)}) collective-permute-start(f32[32,384]{1,0:T(8,128)S(1)} %get-tuple-element.54), channel_id=1, source_target_pairs={{0,4},{4,0},{8,12},{12,8},{16,20},{20,16},{24,28},{28,24},{1,5},{5... | collective-permute-start | bytes 147464 | tf_op jit(solution)/shard_map/ppermute | solution.py:640
  23.5 3.8 %collective-permute-done.7.gb_ref = f32[32,384]{1,0:T(8,128)S(1)} collective-permute-done((f32[32,384]{1,0:T(8,128)S(1)}, f32[32,384]{1,0:T(8,128)S(1)}, u32[]{:S(2)}, u32[]{:S(2)}) %collective-permute-start.7) | collective-permute-done | bytes 49184 | tf_op jit(solution)/shard_map/ppermute | solution.py:639
  27.3 0.0 collective-permute-done.8.ga_ref
  27.3 1.7 %shard_map.56 = (f32[128,256]{1,0:T(8,128)S(1)}, f32[128,256]{1,0:T(8,128)S(1)}, f32[144,512]{1,0:T(8,128)S(1)}, f32[8,128]{1,0:T(8,128)S(1)}, f32[16,144]{1,0:T(8,128)S(1)}, /*index=5*/f32[16,144]{1,0:T(8,128)S(1)}) custom-call(f32[144,384]{1,0:T(8,128)S(1)} %get-tuple-element.51.y_ref, f32[160,384]{1,0:T(8,128)S(1)} %get-tuple-element.52.m_ref, ...), custom_call_target="tpu_custom_call" | custom-call | flops 1000000000 | bytes 1000000 | tf_op jit(solution)/shard_map/pallas_call | solution.py:614
  29.0 2.0 %collective-permute-start.9 = (f32[16,144]{1,0:T(8,128)S(1)}, f32[16,144]{1,0:T(8,128)S(1)}, u32[]{:S(2)}, u32[]{:S(2)}) collective-permute-start(f32[16,144]{1,0:T(8,128)S(1)} %get-tuple-element.60), channel_id=1, source_target_pairs={{1,2},{2,1},{3,0},{0,3},{5,6},{6,5},{7,4},{4,7},{9,10},{10,9},{11,... | collective-permute-start | bytes 27656 | tf_op jit(solution)/shard_map/ppermute | solution.py:639
  31.1 0.4 collective-permute-start.10
  31.4 0.8 %shard_map.57 = (f32[144,384]{1,0:T(8,128)S(1)}, f32[1,128]{1,0:T(1,128)S(1)}) custom-call(f32[144,512]{1,0:T(8,128)S(1)} %get-tuple-element.56.t_ref, f32[1104,512]{1,0:T(8,128)S(1)} %copy-done, f32[256,256]{1,0:T(8,128)S(1)} %pad_add_fusion.both_ref, f32[160,384]{1,0:T(8,128)S(1)} %get-tuple-element.52.m_ref, f32[128,256]{1,0:T(8,128)S(1)} %get-tuple-element.57.z_ref, ...), custom_call_target="tpu_custom_call" | custom-call | flops 1000000000 | bytes 1000000 | tf_op jit(solution)/shard_map/pallas_call | solution.py:614
  32.2 1.4 %collective-permute-done.9.refs_0_ = f32[16,144]{1,0:T(8,128)S(1)} collective-permute-done((f32[16,144]{1,0:T(8,128)S(1)}, f32[16,144]{1,0:T(8,128)S(1)}, u32[]{:S(2)}, u32[]{:S(2)}) %collective-permute-start.9) | collective-permute-done | bytes 9248 | tf_op jit(solution)/shard_map/ppermute | solution.py:639
  33.7 1.1 %collective-permute-done.10.refs_1_ = f32[16,144]{1,0:T(8,128)S(1)} collective-permute-done((f32[16,144]{1,0:T(8,128)S(1)}, f32[16,144]{1,0:T(8,128)S(1)}, u32[]{:S(2)}, u32[]{:S(2)}) %collective-permute-start.10) | collective-permute-done | bytes 9248 | tf_op jit(solution)/shard_map/ppermute | solution.py:640
  34.8 0.2 shard_map.58
  35.0 0.1 collective-permute-start.11
  35.1 0.1 collective-permute-start.12
  35.1 5.0 %collective-permute-done.11.gb_ref = f32[16,384]{1,0:T(8,128)S(1)} collective-permute-done((f32[16,384]{1,0:T(8,128)S(1)}, f32[16,384]{1,0:T(8,128)S(1)}, u32[]{:S(2)}, u32[]{:S(2)}) %collective-permute-start.11) | collective-permute-done | bytes 24608 | tf_op jit(solution)/shard_map/ppermute | solution.py:639
  40.1 0.0 collective-permute-done.12.ga_ref
  40.1 0.4 shard_map.59
  40.5 8.9 %all_to_all.11 = f32[32,1,128]{2,1,0:T(1,128)S(1)} all-to-all(f32[32,1,128]{2,1,0:T(1,128)S(1)} %bitcast.5), channel_id=1, replica_groups=mesh['row'=8,'col'=4] {'row','col'}, dimensions={0} | all-to-all | bytes 32768 | tf_op jit(solution)/shard_map/all_to_all | solution.py:730
  49.4 1.4 %shard_map.60 = (f32[128,256]{1,0:T(8,128)}, f32[128,256]{1,0:T(8,128)}) custom-call(f32[32,128]{1,0:T(8,128)S(1)} %bitcast.4, f32[8,128]{1,0:T(8,128)S(1)} %get-tuple-element.67.table_ref, f32[1104,512]{1,0:T(8,128)S(1)} %copy-done, f32[160,384]{1,0:T(8,128)S(1)} %get-tuple-element.52.m_ref, f32[256,256]{1,0:T(8,128)S(1)} %pad_add_fusion.both_ref, ...), custom_call_target="tpu_custom_call" | custom-call | flops 1000000000 | bytes 1000000 | tf_op jit(solution)/shard_map/pallas_call | solution.py:614
  (2 shorter events, 0.0 us)
Async XLA Ops:
  1.8 9.9 %copy-start = (f32[1104,512]{1,0:T(8,128)S(1)}, f32[1104,512]{1,0:T(8,128)}, u32[]{:S(2)}) copy-start(f32[1104,512]{1,0:T(8,128)} %constant.5.clone.basis_ref) | copy-start | bytes 6782980
  1.8 5.7 %collective-permute-start = (f32[40,128]{1,0:T(8,128)S(1)}, f32[40,128]{1,0:T(8,128)S(1)}, u32[]{:S(2)}, u32[]{:S(2)}) collective-permute-start(f32[40,128]{1,0:T(8,128)S(1)} %get-tuple-element.36), channel_id=1, source_target_pairs={{1,2},{2,1},{3,0},{0,3},{5,6},{6,5},{7,4},{4,7},{9,10},{10,9},{11,... | collective-permute-start | bytes 61448 | tf_op jit(solution)/shard_map/ppermute | solution.py:639
  5.8 3.8 %collective-permute-start.1 = (f32[40,128]{1,0:T(8,128)S(1)}, f32[40,128]{1,0:T(8,128)S(1)}, u32[]{:S(2)}, u32[]{:S(2)}) collective-permute-start(f32[40,128]{1,0:T(8,128)S(1)} %get-tuple-element.37), channel_id=1, source_target_pairs={{0,1},{1,0},{2,3},{3,2},{4,5},{5,4},{6,7},{7,6},{8,9},{9,8},{10,11... | collective-permute-start | bytes 61448 | tf_op jit(solution)/shard_map/ppermute | solution.py:640
  9.7 5.6 %collective-permute-start.2 = (f32[32,384]{1,0:T(8,128)S(1)}, f32[32,384]{1,0:T(8,128)S(1)}, u32[]{:S(2)}, u32[]{:S(2)}) collective-permute-start(f32[32,384]{1,0:T(8,128)S(1)} %get-tuple-element.38), channel_id=1, source_target_pairs={{4,8},{8,4},{12,16},{16,12},{20,24},{24,20},{28,0},{0,28},{5,9},{9... | collective-permute-start | bytes 147464 | tf_op jit(solution)/shard_map/ppermute | solution.py:639
  11.7 3.7 %collective-permute-start.3 = (f32[32,384]{1,0:T(8,128)S(1)}, f32[32,384]{1,0:T(8,128)S(1)}, u32[]{:S(2)}, u32[]{:S(2)}) collective-permute-start(f32[32,384]{1,0:T(8,128)S(1)} %get-tuple-element.39), channel_id=1, source_target_pairs={{0,4},{4,0},{8,12},{12,8},{16,20},{20,16},{24,28},{28,24},{1,5},{5... | collective-permute-start | bytes 147464 | tf_op jit(solution)/shard_map/ppermute | solution.py:640
  12.3 4.6 %collective-permute-start.4 = (f32[8,128]{1,0:T(8,128)S(1)}, f32[8,128]{1,0:T(8,128)S(1)}, u32[]{:S(2)}, u32[]{:S(2)}) collective-permute-start(f32[8,128]{1,0:T(8,128)S(1)} %get-tuple-element.44.table_ref), channel_id=1, source_target_pairs={{0,16},{4,20},{8,24},{12,28},{16,0},{20,4},{24,8},{28,12},{1,17},{... | collective-permute-start | bytes 12296 | tf_op jit(solution)/shard_map/ppermute | solution.py:643
  16.9 4.9 %collective-permute-start.6 = (f32[32,144]{1,0:T(8,128)S(1)}, f32[32,144]{1,0:T(8,128)S(1)}, u32[]{:S(2)}, u32[]{:S(2)}) collective-permute-start(f32[32,144]{1,0:T(8,128)S(1)} %get-tuple-element.70), channel_id=1, source_target_pairs={{1,2},{2,1},{3,0},{0,3},{5,6},{6,5},{7,4},{4,7},{9,10},{10,9},{11,... | collective-permute-start | bytes 55304 | tf_op jit(solution)/shard_map/ppermute | solution.py:639
  17.8 3.9 %collective-permute-start.5 = (f32[32,144]{1,0:T(8,128)S(1)}, f32[32,144]{1,0:T(8,128)S(1)}, u32[]{:S(2)}, u32[]{:S(2)}) collective-permute-start(f32[32,144]{1,0:T(8,128)S(1)} %get-tuple-element.71), channel_id=1, source_target_pairs={{0,1},{1,0},{2,3},{3,2},{4,5},{5,4},{6,7},{7,6},{8,9},{9,8},{10,11... | collective-permute-start | bytes 55304 | tf_op jit(solution)/shard_map/ppermute | solution.py:640
  21.9 5.4 %collective-permute-start.7 = (f32[32,384]{1,0:T(8,128)S(1)}, f32[32,384]{1,0:T(8,128)S(1)}, u32[]{:S(2)}, u32[]{:S(2)}) collective-permute-start(f32[32,384]{1,0:T(8,128)S(1)} %get-tuple-element.53), channel_id=1, source_target_pairs={{4,8},{8,4},{12,16},{16,12},{20,24},{24,20},{28,0},{0,28},{5,9},{9... | collective-permute-start | bytes 147464 | tf_op jit(solution)/shard_map/ppermute | solution.py:639
  22.1 5.3 %collective-permute-start.8 = (f32[32,384]{1,0:T(8,128)S(1)}, f32[32,384]{1,0:T(8,128)S(1)}, u32[]{:S(2)}, u32[]{:S(2)}) collective-permute-start(f32[32,384]{1,0:T(8,128)S(1)} %get-tuple-element.54), channel_id=1, source_target_pairs={{0,4},{4,0},{8,12},{12,8},{16,20},{20,16},{24,28},{28,24},{1,5},{5... | collective-permute-start | bytes 147464 | tf_op jit(solution)/shard_map/ppermute | solution.py:640
  29.0 4.7 %collective-permute-start.9 = (f32[16,144]{1,0:T(8,128)S(1)}, f32[16,144]{1,0:T(8,128)S(1)}, u32[]{:S(2)}, u32[]{:S(2)}) collective-permute-start(f32[16,144]{1,0:T(8,128)S(1)} %get-tuple-element.60), channel_id=1, source_target_pairs={{1,2},{2,1},{3,0},{0,3},{5,6},{6,5},{7,4},{4,7},{9,10},{10,9},{11,... | collective-permute-start | bytes 27656 | tf_op jit(solution)/shard_map/ppermute | solution.py:639
  31.1 3.7 %collective-permute-start.10 = (f32[16,144]{1,0:T(8,128)S(1)}, f32[16,144]{1,0:T(8,128)S(1)}, u32[]{:S(2)}, u32[]{:S(2)}) collective-permute-start(f32[16,144]{1,0:T(8,128)S(1)} %get-tuple-element.61), channel_id=1, source_target_pairs={{0,1},{1,0},{2,3},{3,2},{4,5},{5,4},{6,7},{7,6},{8,9},{9,8},{10,11... | collective-permute-start | bytes 27656 | tf_op jit(solution)/shard_map/ppermute | solution.py:640
  35.0 5.1 %collective-permute-start.11 = (f32[16,384]{1,0:T(8,128)S(1)}, f32[16,384]{1,0:T(8,128)S(1)}, u32[]{:S(2)}, u32[]{:S(2)}) collective-permute-start(f32[16,384]{1,0:T(8,128)S(1)} %get-tuple-element.63), channel_id=1, source_target_pairs={{4,8},{8,4},{12,16},{16,12},{20,24},{24,20},{28,0},{0,28},{5,9},{9... | collective-permute-start | bytes 73736 | tf_op jit(solution)/shard_map/ppermute | solution.py:639
  35.1 5.0 %collective-permute-start.12 = (f32[16,384]{1,0:T(8,128)S(1)}, f32[16,384]{1,0:T(8,128)S(1)}, u32[]{:S(2)}, u32[]{:S(2)}) collective-permute-start(f32[16,384]{1,0:T(8,128)S(1)} %get-tuple-element.64), channel_id=1, source_target_pairs={{0,4},{4,0},{8,12},{12,8},{16,20},{20,16},{24,28},{28,24},{1,5},{5... | collective-permute-start | bytes 73736 | tf_op jit(solution)/shard_map/ppermute | solution.py:640

commit v7 on v6

--- a/solution.py
+++ b/solution.py
@@ -359,7 +359,7 @@
     )
 
 
-def widen_kernel(counts, both_ref, gb_ref, ga_ref, r3_ref, h3_ref, table_ref, b_ref, a_ref):
+def widen_kernel(counts, both_ref, gb_ref, ga_ref, r3_ref, h3_ref, b_ref, a_ref, table_ref):
     i, j = place()
     from_left, from_right = sides(j, counts[1], ga_ref[:32], gb_ref[:32])
     turned = jnp.concatenate([from_right, jnp.zeros((64, 128), jnp.float32), from_left], axis=0)
@@ -390,13 +390,17 @@
     send(i, a_ref, b_ref, strip(slice(0, 8), slice(0, 16)), strip(slice(120, 128), slice(112, 128)))
 
 
-def forward_kernel(both_ref, r3_ref, basis_ref, table_ref, t_ref, weights_ref, table_out):
-    r, h = both_ref[:TR], both_ref[TR:]
-    u = column_transform(jnp.concatenate([r, r3_ref[...]], axis=1), basis_ref)
-    t_ref[...] = row_transform(u, basis_ref, tile_rows)
+def weights_kernel(both_ref, table_ref, basis_ref, weights_ref, table_out):
+    h = both_ref[TR:]
     means = [x / (SUB * SUB) for x in core_sums(h * h * h)]
     weights_ref[...] = weights(means, basis_ref)
     table_out[...] = table_ref[...]
+
+
+def forward_kernel(both_ref, r3_ref, basis_ref, t_ref):
+    r = both_ref[:TR]
+    u = column_transform(jnp.concatenate([r, r3_ref[...]], axis=1), basis_ref)
+    t_ref[...] = row_transform(u, basis_ref, tile_rows)
 
 
 def first_kernel(
@@ -619,10 +623,11 @@
     )(*args)
 
 
-def pairs_from(count, offset):
+def pairs_from(count, offset, wrap=True):
     found = []
     for k in range(offset, count, 2):
-        found += [(k, (k + 1) % count), ((k + 1) % count, k)]
+        other = (k + 1) % count
+        found += [(k, other), (other, k)] if wrap or other > k else [(k, k), (other, other)]
     return found
 
 
@@ -634,9 +639,9 @@
     both_axes = ("row", "col")
     depth = table_shape(counts)[0]
 
-    def swap(a, b, axis):
+    def swap(a, b, axis, wrap=True):
         count = lax.axis_size(axis)
-        gb = lax.ppermute(b, axis, pairs_from(count, 1))
+        gb = lax.ppermute(b, axis, pairs_from(count, 1, wrap))
         return lax.ppermute(a, axis, pairs_from(count, 0)), gb
 
     def row_shift(x, step):
@@ -645,9 +650,9 @@
     both = jnp.pad(noise, ((0, TR), (0, 0))) + jnp.pad(height, ((TR, 0), (0, 0)))
     b, a = call(functools.partial(begin_kernel, counts), [(32 + depth, 128)] * 2, both)
     ga, gb = swap(a, b, "col")
-    r3, h3, table, b, a = call(
+    r3, h3, b, a, table = call(
         functools.partial(widen_kernel, counts),
-        [(128, 128)] * 2 + [(depth, 128)] + [(24 + depth, FC)] * 2,
+        [(128, 128)] * 2 + [(24 + depth, FC)] * 2 + [(depth, 128)],
         both,
         gb,
         ga,
@@ -659,10 +664,9 @@
     if nr > 8:
         a, b = (x.at[24:, :128].set(table) for x in (a, b))
     ga, gb = swap(a, b, "row")
-    t, weight, table = call(
-        forward_kernel, [(EXT, 2 * SPEC)] * 2 + [(depth, 128)], both, r3, basis, table
-    )
+    weight, table = call(weights_kernel, [(EXT, 2 * SPEC), (depth, 128)], both, table, basis)
     far = row_shift(table, 4) if nr >= 8 else 0.0
+    t = call(forward_kernel, [(EXT, 2 * SPEC)], both, r3, basis)[0]
     t, table, b, a = call(
         functools.partial(first_kernel, counts),
         [(EXT, 2 * SPEC), (depth, 128)] + [(24, EXT)] * 2,
@@ -710,12 +714,12 @@
         weight,
         basis,
     )
-    ga, gb = swap(a, b, "col")
+    ga, gb = swap(a, b, "col", False)
     y, stats = call(inverse_stats_kernel, [(EXT, FC), (1, 128)], t, basis, both, m, z, w)
     y, b, a = call(
         functools.partial(columns_kernel, counts), [(EXT, FC)] + [(16, FC)] * 2, y, gb, ga
     )
-    ga, gb = swap(a, b, "row")
+    ga, gb = swap(a, b, "row", False)
     q, v, stats = call(
         functools.partial(dots_kernel, counts),
         [(TR, TC)] * 2 + [(devices, 128)],

time: 50.9 us -> 51.7 us (1.016)
  waiting for transfers between devices: 17.9 us -> 11.5 us
  starting transfers between devices: 14.9 us -> 18.6 us
  blocking collectives: 8.86 us -> 12.1 us
    ppermute x6, waiting for transfers between devices: 14.3 us -> 7.65 us  [swap(): gb = lax.ppermute(b, axis, pairs_from(count, 1, wrap))]
    ppermute x6, starting transfers between devices: 3.32 us -> 7.47 us  [swap(): return (lax.ppermute(a, axis, pairs_from(count, 0)), gb)]
    all_to_all x1, blocking collectives: 8.86 us -> 12.1 us  [body(): stats = lax.all_to_all(stats, both_axes, 0, 0, tiled=True)]
    ppermute x6, waiting for transfers between devices: 3.15 us -> 3.84 us  [swap(): return (lax.ppermute(a, axis, pairs_from(count, 0)), gb)]
    pallas_call x11 -> x12, Pallas kernels: 7.42 us -> 7.55 us  [call(): pl.pallas_call(kernel, out_shape=shapes, compiler_params=pltpu.CompilerPa...]
  transfers between devices with their start and end apart: 13 -> 13, of which waited for: 9 -> 8; matrix products, arithmetic and copies ran while one was open for 0% -> 0% of each run, Pallas kernels for 6% -> 6%
where the time goes in v7:
time: 51.7 us; the launch traced here: 51.5 us
  starting transfers between devices  18.6 us (36%)
  blocking collectives  12.1 us (23%)
  waiting for transfers between devices  11.5 us (22%)
  Pallas kernels  7.55 us (15%)
  other arithmetic  1 us (2%)
  between operations  0.74 us (1%)
    all_to_all x1, blocking collectives, body(): stats = lax.all_to_all(stats, both_axes, 0, 0, tiled=True)  12.1 us
    ppermute x6, starting transfers between devices, swap(): gb = lax.ppermute(b, axis, pairs_from(count, 1, wrap))  8.75 us
    ppermute x6, waiting for transfers between devices, swap(): gb = lax.ppermute(b, axis, pairs_from(count, 1, wrap))  7.65 us
    pallas_call x12, Pallas kernels, call(): pl.pallas_call(kernel, out_shape=shapes, compiler_params=pltpu.CompilerPa...  7.55 us
    ppermute x6, starting transfers between devices, swap(): return (lax.ppermute(a, axis, pairs_from(count, 0)), gb)  7.47 us
    ppermute x6, waiting for transfers between devices, swap(): return (lax.ppermute(a, axis, pairs_from(count, 0)), gb)  3.84 us
    ppermute x1, starting transfers between devices, row_shift(): return lax.ppermute(x, 'row', [(k, (k + step) % nr) for k in range(nr)])  2.43 us
  transfers between devices with their start and end apart: 13, of which 8 were waited for; matrix products, arithmetic and copies ran while one was open for 0% of the time, Pallas kernels for 6%

profile of v7, /device:TPU:0, one launch (start us, length us, event | category | flops | bytes accessed | tf_op | source)
XLA Modules:
  0.0 51.5 jit_solution(6593617169979286192)
XLA Ops:
  0.6 1.0 %pad_add_fusion.both_ref = f32[256,256]{1,0:T(8,128)S(1)} fusion(f32[128,256]{1,0:T(8,128)} %param.3, f32[128,256]{1,0:T(8,128)} %param.4), kind=kLoop, calls=%fused_computation | loop fusion | flops 65536 | bytes 524288 | tf_op jit(solution)/shard_map/add | solution.py:650
  1.6 0.2 shard_map.50
  1.8 0.0 copy-start
  1.8 4.0 %collective-permute-start = (f32[40,128]{1,0:T(8,128)S(1)}, f32[40,128]{1,0:T(8,128)S(1)}, u32[]{:S(2)}, u32[]{:S(2)}) collective-permute-start(f32[40,128]{1,0:T(8,128)S(1)} %get-tuple-element.35), channel_id=1, source_target_pairs={{1,2},{2,1},{3,0},{0,3},{5,6},{6,5},{7,4},{4,7},{9,10},{10,9},{11,... | collective-permute-start | bytes 61448 | tf_op jit(solution)/shard_map/ppermute | solution.py:644
  5.8 0.5 %collective-permute-start.1 = (f32[40,128]{1,0:T(8,128)S(1)}, f32[40,128]{1,0:T(8,128)S(1)}, u32[]{:S(2)}, u32[]{:S(2)}) collective-permute-start(f32[40,128]{1,0:T(8,128)S(1)} %get-tuple-element.36), channel_id=1, source_target_pairs={{0,1},{1,0},{2,3},{3,2},{4,5},{5,4},{6,7},{7,6},{8,9},{9,8},{10,11... | collective-permute-start | bytes 61448 | tf_op jit(solution)/shard_map/ppermute | solution.py:645
  6.3 1.2 %collective-permute-done.gb_ref = f32[40,128]{1,0:T(8,128)S(1)} collective-permute-done((f32[40,128]{1,0:T(8,128)S(1)}, f32[40,128]{1,0:T(8,128)S(1)}, u32[]{:S(2)}, u32[]{:S(2)}) %collective-permute-start) | collective-permute-done | bytes 20512 | tf_op jit(solution)/shard_map/ppermute | solution.py:644
  7.5 2.0 %collective-permute-done.1.ga_ref = f32[40,128]{1,0:T(8,128)S(1)} collective-permute-done((f32[40,128]{1,0:T(8,128)S(1)}, f32[40,128]{1,0:T(8,128)S(1)}, u32[]{:S(2)}, u32[]{:S(2)}) %collective-permute-start.1) | collective-permute-done | bytes 20512 | tf_op jit(solution)/shard_map/ppermute | solution.py:645
  9.5 0.2 shard_map.51
  9.7 2.0 %collective-permute-start.2 = (f32[32,384]{1,0:T(8,128)S(1)}, f32[32,384]{1,0:T(8,128)S(1)}, u32[]{:S(2)}, u32[]{:S(2)}) collective-permute-start(f32[32,384]{1,0:T(8,128)S(1)} %get-tuple-element.37), channel_id=1, source_target_pairs={{4,8},{8,4},{12,16},{16,12},{20,24},{24,20},{28,0},{0,28},{5,9},{9... | collective-permute-start | bytes 147464 | tf_op jit(solution)/shard_map/ppermute | solution.py:644
  11.7 0.0 collective-permute-start.3
  11.7 0.0 copy-done
  11.7 0.1 shard_map.53
  11.9 2.4 %collective-permute-start.4 = (f32[8,128]{1,0:T(8,128)S(1)}, f32[8,128]{1,0:T(8,128)S(1)}, u32[]{:S(2)}, u32[]{:S(2)}) collective-permute-start(f32[8,128]{1,0:T(8,128)S(1)} %get-tuple-element.42.table_ref), channel_id=1, source_target_pairs={{0,16},{4,20},{8,24},{12,28},{16,0},{20,4},{24,8},{28,12},{1,17},{... | collective-permute-start | bytes 12296 | tf_op jit(solution)/shard_map/ppermute | solution.py:648
  14.3 0.6 %shard_map.52.tile_ref = f32[144,512]{1,0:T(8,128)S(1)} custom-call(f32[256,256]{1,0:T(8,128)S(1)} %pad_add_fusion.both_ref, f32[128,128]{1,0:T(8,128)S(1)} %get-tuple-element.39.r3_ref, f32[1104,512]{1,0:T(8,128)S(1)} %copy-done), custom_call_target="tpu_custom_call" | custom-call | flops 1000000000 | bytes 1000000 | tf_op jit(solution)/shard_map/pallas_call | solution.py:618
  14.9 0.5 collective-permute-done.2.gb_ref
  15.4 0.0 collective-permute-done.3.ga_ref
  15.4 1.0 %shard_map.54 = (f32[144,512]{1,0:T(8,128)S(1)}, f32[8,128]{1,0:T(8,128)S(1)}, f32[24,144]{1,0:T(8,128)S(1)}, f32[24,144]{1,0:T(8,128)S(1)}) custom-call(f32[32,384]{1,0:T(8,128)S(1)} %collective-permute-done.2.gb_ref, f32[32,384]{1,0:T(8,128)S(1)} %collective-permute-done.3.ga_ref, f32[144,512]{1,0:T(8,128)S(1)} %shard_map.52.tile_ref, ...), custom_call_target="tpu_custom_call" | custom-call | flops 1000000000 | bytes 1000000 | tf_op jit(solution)/shard_map/pallas_call | solution.py:618
  16.4 0.1 collective-permute-done.4
  16.5 0.9 %collective-permute-start.6 = (f32[32,144]{1,0:T(8,128)S(1)}, f32[32,144]{1,0:T(8,128)S(1)}, u32[]{:S(2)}, u32[]{:S(2)}) collective-permute-start(f32[32,144]{1,0:T(8,128)S(1)} %get-tuple-element.68), channel_id=1, source_target_pairs={{1,2},{2,1},{3,0},{0,3},{5,6},{6,5},{7,4},{4,7},{9,10},{10,9},{11,... | collective-permute-start | bytes 55304 | tf_op jit(solution)/shard_map/ppermute | solution.py:644
  17.4 1.0 %collective-permute-start.5 = (f32[32,144]{1,0:T(8,128)S(1)}, f32[32,144]{1,0:T(8,128)S(1)}, u32[]{:S(2)}, u32[]{:S(2)}) collective-permute-start(f32[32,144]{1,0:T(8,128)S(1)} %get-tuple-element.69), channel_id=1, source_target_pairs={{0,1},{1,0},{2,3},{3,2},{4,5},{5,4},{6,7},{7,6},{8,9},{9,8},{10,11... | collective-permute-start | bytes 55304 | tf_op jit(solution)/shard_map/ppermute | solution.py:645
  18.5 0.8 %shard_map.55 = (f32[144,384]{1,0:T(8,128)S(1)}, f32[160,384]{1,0:T(8,128)S(1)}) custom-call(f32[144,512]{1,0:T(8,128)S(1)} %get-tuple-element.43.t_ref, f32[1104,512]{1,0:T(8,128)S(1)} %copy-done, f32[256,256]{1,0:T(8,128)S(1)} %pad_add_fusion.both_ref, f32[128,128]{1,0:T(8,128)S(1)} %get-tuple-element.44.h3_ref, ...), custom_call_target="tpu_custom_call" | custom-call | flops 1000000000 | bytes 1000000 | tf_op jit(solution)/shard_map/pallas_call | solution.py:618
  19.3 2.1 %collective-permute-done.6.refs_1_ = f32[32,144]{1,0:T(8,128)S(1)} collective-permute-done((f32[32,144]{1,0:T(8,128)S(1)}, f32[32,144]{1,0:T(8,128)S(1)}, u32[]{:S(2)}, u32[]{:S(2)}) %collective-permute-start.6) | collective-permute-done | bytes 18464 | tf_op jit(solution)/shard_map/ppermute | solution.py:644
  21.3 0.0 collective-permute-done.5.refs_0_
  21.3 0.2 shard_map.56
  21.5 0.5 %collective-permute-start.7 = (f32[32,384]{1,0:T(8,128)S(1)}, f32[32,384]{1,0:T(8,128)S(1)}, u32[]{:S(2)}, u32[]{:S(2)}) collective-permute-start(f32[32,384]{1,0:T(8,128)S(1)} %get-tuple-element.51), channel_id=1, source_target_pairs={{4,8},{8,4},{12,16},{16,12},{20,24},{24,20},{28,0},{0,28},{5,9},{9... | collective-permute-start | bytes 147464 | tf_op jit(solution)/shard_map/ppermute | solution.py:644
  22.1 1.0 %collective-permute-start.8 = (f32[32,384]{1,0:T(8,128)S(1)}, f32[32,384]{1,0:T(8,128)S(1)}, u32[]{:S(2)}, u32[]{:S(2)}) collective-permute-start(f32[32,384]{1,0:T(8,128)S(1)} %get-tuple-element.52), channel_id=1, source_target_pairs={{0,4},{4,0},{8,12},{12,8},{16,20},{20,16},{24,28},{28,24},{1,5},{5... | collective-permute-start | bytes 147464 | tf_op jit(solution)/shard_map/ppermute | solution.py:645
  23.1 3.8 %collective-permute-done.7.gb_ref = f32[32,384]{1,0:T(8,128)S(1)} collective-permute-done((f32[32,384]{1,0:T(8,128)S(1)}, f32[32,384]{1,0:T(8,128)S(1)}, u32[]{:S(2)}, u32[]{:S(2)}) %collective-permute-start.7) | collective-permute-done | bytes 49184 | tf_op jit(solution)/shard_map/ppermute | solution.py:644
  26.9 0.0 collective-permute-done.8.ga_ref
  26.9 1.7 %shard_map.57 = (f32[128,256]{1,0:T(8,128)S(1)}, f32[128,256]{1,0:T(8,128)S(1)}, f32[144,512]{1,0:T(8,128)S(1)}, f32[8,128]{1,0:T(8,128)S(1)}, f32[16,144]{1,0:T(8,128)S(1)}, /*index=5*/f32[16,144]{1,0:T(8,128)S(1)}) custom-call(f32[144,384]{1,0:T(8,128)S(1)} %get-tuple-element.49.y_ref, f32[160,384]{1,0:T(8,128)S(1)} %get-tuple-element.50.m_ref, ...), custom_call_target="tpu_custom_call" | custom-call | flops 1000000000 | bytes 1000000 | tf_op jit(solution)/shard_map/pallas_call | solution.py:618
  28.6 0.7 %collective-permute-start.9 = (f32[16,144]{1,0:T(8,128)S(1)}, f32[16,144]{1,0:T(8,128)S(1)}, u32[]{:S(2)}, u32[]{:S(2)}) collective-permute-start(f32[16,144]{1,0:T(8,128)S(1)} %get-tuple-element.58), channel_id=1, source_target_pairs={{1,2},{2,1},{3,3},{0,0},{5,6},{6,5},{7,7},{4,4},{9,10},{10,9},{11,... | collective-permute-start | bytes 27656 | tf_op jit(solution)/shard_map/ppermute | solution.py:644
  29.3 3.8 %collective-permute-start.10 = (f32[16,144]{1,0:T(8,128)S(1)}, f32[16,144]{1,0:T(8,128)S(1)}, u32[]{:S(2)}, u32[]{:S(2)}) collective-permute-start(f32[16,144]{1,0:T(8,128)S(1)} %get-tuple-element.59), channel_id=1, source_target_pairs={{0,1},{1,0},{2,3},{3,2},{4,5},{5,4},{6,7},{7,6},{8,9},{9,8},{10,11... | collective-permute-start | bytes 27656 | tf_op jit(solution)/shard_map/ppermute | solution.py:645
  33.1 0.8 %shard_map.58 = (f32[144,384]{1,0:T(8,128)S(1)}, f32[1,128]{1,0:T(1,128)S(1)}) custom-call(f32[144,512]{1,0:T(8,128)S(1)} %get-tuple-element.54.t_ref, f32[1104,512]{1,0:T(8,128)S(1)} %copy-done, f32[256,256]{1,0:T(8,128)S(1)} %pad_add_fusion.both_ref, f32[160,384]{1,0:T(8,128)S(1)} %get-tuple-element.50.m_ref, f32[128,256]{1,0:T(8,128)S(1)} %get-tuple-element.55.z_ref, ...), custom_call_target="tpu_custom_call" | custom-call | flops 1000000000 | bytes 1000000 | tf_op jit(solution)/shard_map/pallas_call | solution.py:618
  33.9 0.0 collective-permute-done.9.refs_0_
  34.0 1.0 %collective-permute-done.10.refs_1_ = f32[16,144]{1,0:T(8,128)S(1)} collective-permute-done((f32[16,144]{1,0:T(8,128)S(1)}, f32[16,144]{1,0:T(8,128)S(1)}, u32[]{:S(2)}, u32[]{:S(2)}) %collective-permute-start.10) | collective-permute-done | bytes 9248 | tf_op jit(solution)/shard_map/ppermute | solution.py:645
  34.9 0.2 shard_map.59
  35.1 0.7 %collective-permute-start.11 = (f32[16,384]{1,0:T(8,128)S(1)}, f32[16,384]{1,0:T(8,128)S(1)}, u32[]{:S(2)}, u32[]{:S(2)}) collective-permute-start(f32[16,384]{1,0:T(8,128)S(1)} %get-tuple-element.61), channel_id=1, source_target_pairs={{4,8},{8,4},{12,16},{16,12},{20,24},{24,20},{28,28},{0,0},{5,9},{9... | collective-permute-start | bytes 73736 | tf_op jit(solution)/shard_map/ppermute | solution.py:644
  35.8 1.1 %collective-permute-start.12 = (f32[16,384]{1,0:T(8,128)S(1)}, f32[16,384]{1,0:T(8,128)S(1)}, u32[]{:S(2)}, u32[]{:S(2)}) collective-permute-start(f32[16,384]{1,0:T(8,128)S(1)} %get-tuple-element.62), channel_id=1, source_target_pairs={{0,4},{4,0},{8,12},{12,8},{16,20},{20,16},{24,28},{28,24},{1,5},{5... | collective-permute-start | bytes 73736 | tf_op jit(solution)/shard_map/ppermute | solution.py:645
  36.8 0.0 collective-permute-done.11.gb_ref
  36.8 0.8 %collective-permute-done.12.ga_ref = f32[16,384]{1,0:T(8,128)S(1)} collective-permute-done((f32[16,384]{1,0:T(8,128)S(1)}, f32[16,384]{1,0:T(8,128)S(1)}, u32[]{:S(2)}, u32[]{:S(2)}) %collective-permute-start.12) | collective-permute-done | bytes 24608 | tf_op jit(solution)/shard_map/ppermute | solution.py:645
  37.7 0.4 shard_map.60
  38.1 12.1 %all_to_all.11 = f32[32,1,128]{2,1,0:T(1,128)S(1)} all-to-all(f32[32,1,128]{2,1,0:T(1,128)S(1)} %bitcast.5), channel_id=1, replica_groups=mesh['row'=8,'col'=4] {'row','col'}, dimensions={0} | all-to-all | bytes 32768 | tf_op jit(solution)/shard_map/all_to_all | solution.py:734
  50.2 1.4 %shard_map.61 = (f32[128,256]{1,0:T(8,128)}, f32[128,256]{1,0:T(8,128)}) custom-call(f32[32,128]{1,0:T(8,128)S(1)} %bitcast.4, f32[8,128]{1,0:T(8,128)S(1)} %get-tuple-element.65.table_ref, f32[1104,512]{1,0:T(8,128)S(1)} %copy-done, f32[160,384]{1,0:T(8,128)S(1)} %get-tuple-element.50.m_ref, f32[256,256]{1,0:T(8,128)S(1)} %pad_add_fusion.both_ref, ...), custom_call_target="tpu_custom_call" | custom-call | flops 1000000000 | bytes 1000000 | tf_op jit(solution)/shard_map/pallas_call | solution.py:618
  (2 shorter events, 0.0 us)
Async XLA Ops:
  1.8 9.9 %copy-start = (f32[1104,512]{1,0:T(8,128)S(1)}, f32[1104,512]{1,0:T(8,128)}, u32[]{:S(2)}) copy-start(f32[1104,512]{1,0:T(8,128)} %constant.5.clone.basis_ref) | copy-start | bytes 6782980
  1.8 5.7 %collective-permute-start = (f32[40,128]{1,0:T(8,128)S(1)}, f32[40,128]{1,0:T(8,128)S(1)}, u32[]{:S(2)}, u32[]{:S(2)}) collective-permute-start(f32[40,128]{1,0:T(8,128)S(1)} %get-tuple-element.35), channel_id=1, source_target_pairs={{1,2},{2,1},{3,0},{0,3},{5,6},{6,5},{7,4},{4,7},{9,10},{10,9},{11,... | collective-permute-start | bytes 61448 | tf_op jit(solution)/shard_map/ppermute | solution.py:644
  5.8 3.8 %collective-permute-start.1 = (f32[40,128]{1,0:T(8,128)S(1)}, f32[40,128]{1,0:T(8,128)S(1)}, u32[]{:S(2)}, u32[]{:S(2)}) collective-permute-start(f32[40,128]{1,0:T(8,128)S(1)} %get-tuple-element.36), channel_id=1, source_target_pairs={{0,1},{1,0},{2,3},{3,2},{4,5},{5,4},{6,7},{7,6},{8,9},{9,8},{10,11... | collective-permute-start | bytes 61448 | tf_op jit(solution)/shard_map/ppermute | solution.py:645
  9.7 5.6 %collective-permute-start.2 = (f32[32,384]{1,0:T(8,128)S(1)}, f32[32,384]{1,0:T(8,128)S(1)}, u32[]{:S(2)}, u32[]{:S(2)}) collective-permute-start(f32[32,384]{1,0:T(8,128)S(1)} %get-tuple-element.37), channel_id=1, source_target_pairs={{4,8},{8,4},{12,16},{16,12},{20,24},{24,20},{28,0},{0,28},{5,9},{9... | collective-permute-start | bytes 147464 | tf_op jit(solution)/shard_map/ppermute | solution.py:644
  11.7 3.7 %collective-permute-start.3 = (f32[32,384]{1,0:T(8,128)S(1)}, f32[32,384]{1,0:T(8,128)S(1)}, u32[]{:S(2)}, u32[]{:S(2)}) collective-permute-start(f32[32,384]{1,0:T(8,128)S(1)} %get-tuple-element.38), channel_id=1, source_target_pairs={{0,4},{4,0},{8,12},{12,8},{16,20},{20,16},{24,28},{28,24},{1,5},{5... | collective-permute-start | bytes 147464 | tf_op jit(solution)/shard_map/ppermute | solution.py:645
  11.9 4.6 %collective-permute-start.4 = (f32[8,128]{1,0:T(8,128)S(1)}, f32[8,128]{1,0:T(8,128)S(1)}, u32[]{:S(2)}, u32[]{:S(2)}) collective-permute-start(f32[8,128]{1,0:T(8,128)S(1)} %get-tuple-element.42.table_ref), channel_id=1, source_target_pairs={{0,16},{4,20},{8,24},{12,28},{16,0},{20,4},{24,8},{28,12},{1,17},{... | collective-permute-start | bytes 12296 | tf_op jit(solution)/shard_map/ppermute | solution.py:648
  16.5 4.9 %collective-permute-start.6 = (f32[32,144]{1,0:T(8,128)S(1)}, f32[32,144]{1,0:T(8,128)S(1)}, u32[]{:S(2)}, u32[]{:S(2)}) collective-permute-start(f32[32,144]{1,0:T(8,128)S(1)} %get-tuple-element.68), channel_id=1, source_target_pairs={{1,2},{2,1},{3,0},{0,3},{5,6},{6,5},{7,4},{4,7},{9,10},{10,9},{11,... | collective-permute-start | bytes 55304 | tf_op jit(solution)/shard_map/ppermute | solution.py:644
  17.4 3.9 %collective-permute-start.5 = (f32[32,144]{1,0:T(8,128)S(1)}, f32[32,144]{1,0:T(8,128)S(1)}, u32[]{:S(2)}, u32[]{:S(2)}) collective-permute-start(f32[32,144]{1,0:T(8,128)S(1)} %get-tuple-element.69), channel_id=1, source_target_pairs={{0,1},{1,0},{2,3},{3,2},{4,5},{5,4},{6,7},{7,6},{8,9},{9,8},{10,11... | collective-permute-start | bytes 55304 | tf_op jit(solution)/shard_map/ppermute | solution.py:645
  21.5 5.4 %collective-permute-start.7 = (f32[32,384]{1,0:T(8,128)S(1)}, f32[32,384]{1,0:T(8,128)S(1)}, u32[]{:S(2)}, u32[]{:S(2)}) collective-permute-start(f32[32,384]{1,0:T(8,128)S(1)} %get-tuple-element.51), channel_id=1, source_target_pairs={{4,8},{8,4},{12,16},{16,12},{20,24},{24,20},{28,0},{0,28},{5,9},{9... | collective-permute-start | bytes 147464 | tf_op jit(solution)/shard_map/ppermute | solution.py:644
  22.1 4.8 %collective-permute-start.8 = (f32[32,384]{1,0:T(8,128)S(1)}, f32[32,384]{1,0:T(8,128)S(1)}, u32[]{:S(2)}, u32[]{:S(2)}) collective-permute-start(f32[32,384]{1,0:T(8,128)S(1)} %get-tuple-element.52), channel_id=1, source_target_pairs={{0,4},{4,0},{8,12},{12,8},{16,20},{20,16},{24,28},{28,24},{1,5},{5... | collective-permute-start | bytes 147464 | tf_op jit(solution)/shard_map/ppermute | solution.py:645
  28.6 5.3 %collective-permute-start.9 = (f32[16,144]{1,0:T(8,128)S(1)}, f32[16,144]{1,0:T(8,128)S(1)}, u32[]{:S(2)}, u32[]{:S(2)}) collective-permute-start(f32[16,144]{1,0:T(8,128)S(1)} %get-tuple-element.58), channel_id=1, source_target_pairs={{1,2},{2,1},{3,3},{0,0},{5,6},{6,5},{7,7},{4,4},{9,10},{10,9},{11,... | collective-permute-start | bytes 27656 | tf_op jit(solution)/shard_map/ppermute | solution.py:644
  29.3 5.6 %collective-permute-start.10 = (f32[16,144]{1,0:T(8,128)S(1)}, f32[16,144]{1,0:T(8,128)S(1)}, u32[]{:S(2)}, u32[]{:S(2)}) collective-permute-start(f32[16,144]{1,0:T(8,128)S(1)} %get-tuple-element.59), channel_id=1, source_target_pairs={{0,1},{1,0},{2,3},{3,2},{4,5},{5,4},{6,7},{7,6},{8,9},{9,8},{10,11... | collective-permute-start | bytes 27656 | tf_op jit(solution)/shard_map/ppermute | solution.py:645
  35.1 1.7 %collective-permute-start.11 = (f32[16,384]{1,0:T(8,128)S(1)}, f32[16,384]{1,0:T(8,128)S(1)}, u32[]{:S(2)}, u32[]{:S(2)}) collective-permute-start(f32[16,384]{1,0:T(8,128)S(1)} %get-tuple-element.61), channel_id=1, source_target_pairs={{4,8},{8,4},{12,16},{16,12},{20,24},{24,20},{28,28},{0,0},{5,9},{9... | collective-permute-start | bytes 73736 | tf_op jit(solution)/shard_map/ppermute | solution.py:644
  35.8 1.9 %collective-permute-start.12 = (f32[16,384]{1,0:T(8,128)S(1)}, f32[16,384]{1,0:T(8,128)S(1)}, u32[]{:S(2)}, u32[]{:S(2)}) collective-permute-start(f32[16,384]{1,0:T(8,128)S(1)} %get-tuple-element.62), channel_id=1, source_target_pairs={{0,4},{4,0},{8,12},{12,8},{16,20},{20,16},{24,28},{28,24},{1,5},{5... | collective-permute-start | bytes 73736 | tf_op jit(solution)/shard_map/ppermute | solution.py:645

commit v8 on v7

--- a/solution.py
+++ b/solution.py
@@ -623,11 +623,23 @@
     )(*args)
 
 
-def pairs_from(count, offset, wrap=True):
+def pairs_from(count, offset):
     found = []
     for k in range(offset, count, 2):
-        other = (k + 1) % count
-        found += [(k, other), (other, k)] if wrap or other > k else [(k, k), (other, other)]
+        found += [(k, (k + 1) % count), ((k + 1) % count, k)]
+    return found
+
+
+def near_pairs(counts, axis):
+    found = []
+    for i in range(counts[0]):
+        for j in range(counts[1]):
+            at = [i, j]
+            if 0 < at[axis] < counts[axis] - 1:
+                at[axis] += 1 if at[axis] % 2 else -1
+            else:
+                at[1 - axis] ^= 1
+            found.append((i * counts[1] + j, at[0] * counts[1] + at[1]))
     return found
 
 
@@ -641,7 +653,10 @@
 
     def swap(a, b, axis, wrap=True):
         count = lax.axis_size(axis)
-        gb = lax.ppermute(b, axis, pairs_from(count, 1, wrap))
+        if wrap:
+            gb = lax.ppermute(b, axis, pairs_from(count, 1))
+        else:
+            gb = lax.ppermute(b, both_axes, near_pairs(counts, both_axes.index(axis)))
         return lax.ppermute(a, axis, pairs_from(count, 0)), gb
 
     def row_shift(x, step):

time: 51.7 us -> 48.3 us (0.934)
  blocking collectives: 12.1 us -> 9.19 us
  starting transfers between devices: 18.6 us -> 16.9 us
  waiting for transfers between devices: 11.5 us -> 12.8 us
    all_to_all x1, blocking collectives: 12.1 us -> 9.19 us  [body(): stats = lax.all_to_all(stats, both_axes, 0, 0, tiled=True)]
    ppermute x6, starting transfers between devices: 7.47 us -> 5.1 us  [swap(): return (lax.ppermute(a, axis, pairs_from(count, 0)), gb)]
    ppermute x6, waiting for transfers between devices: 7.65 us -> 9.62 us  [the longest x4 7.65 us: swap(): gb = lax.ppermute(b, axis, pairs_from(count, 1))]
    ppermute x6, waiting for transfers between devices: 3.84 us -> 3.08 us  [swap(): return (lax.ppermute(a, axis, pairs_from(count, 0)), gb)]
    ppermute x6, starting transfers between devices: 8.75 us -> 9.34 us  [the longest x4 7.42 us: swap(): gb = lax.ppermute(b, axis, pairs_from(count, 1))]
  transfers between devices with their start and end apart: 13 -> 13, of which waited for: 8 -> 8; matrix products, arithmetic and copies ran while one was open for 0% -> 0% of each run, Pallas kernels for 6% -> 7%
where the time goes in v8:
time: 48.3 us; the launch traced here: 48.1 us
  starting transfers between devices  16.9 us (35%)
  waiting for transfers between devices  12.8 us (27%)
  blocking collectives  9.19 us (19%)
  Pallas kernels  7.56 us (16%)
  other arithmetic  1 us (2%)
  between operations  0.73 us (2%)
    all_to_all x1, blocking collectives, body(): stats = lax.all_to_all(stats, both_axes, 0, 0, tiled=True)  9.19 us
    ppermute x4, waiting for transfers between devices, swap(): gb = lax.ppermute(b, axis, pairs_from(count, 1))  7.65 us
    pallas_call x12, Pallas kernels, call(): pl.pallas_call(kernel, out_shape=shapes, compiler_params=pltpu.CompilerPa...  7.56 us
    ppermute x4, starting transfers between devices, swap(): gb = lax.ppermute(b, axis, pairs_from(count, 1))  7.42 us
    ppermute x6, starting transfers between devices, swap(): return (lax.ppermute(a, axis, pairs_from(count, 0)), gb)  5.1 us
    ppermute x6, waiting for transfers between devices, swap(): return (lax.ppermute(a, axis, pairs_from(count, 0)), gb)  3.08 us
    ppermute x1, starting transfers between devices, row_shift(): return lax.ppermute(x, 'row', [(k, (k + step) % nr) for k in range(nr)])  2.43 us
    ppermute x2, waiting for transfers between devices, swap(): gb = lax.ppermute(b, both_axes, near_pairs(counts, both_axes.index(axis)))  1.98 us
  transfers between devices with their start and end apart: 13, of which 8 were waited for; matrix products, arithmetic and copies ran while one was open for 0% of the time, Pallas kernels for 7%

profile of v8, /device:TPU:0, one launch (start us, length us, event | category | flops | bytes accessed | tf_op | source)
XLA Modules:
  0.0 48.1 jit_solution(6544913226231468475)
XLA Ops:
  0.6 1.0 %pad_add_fusion.both_ref = f32[256,256]{1,0:T(8,128)S(1)} fusion(f32[128,256]{1,0:T(8,128)} %param.3, f32[128,256]{1,0:T(8,128)} %param.4), kind=kLoop, calls=%fused_computation | loop fusion | flops 65536 | bytes 524288 | tf_op jit(solution)/shard_map/add | solution.py:665
  1.6 0.2 shard_map.50
  1.8 0.0 copy-start
  1.8 4.0 %collective-permute-start = (f32[40,128]{1,0:T(8,128)S(1)}, f32[40,128]{1,0:T(8,128)S(1)}, u32[]{:S(2)}, u32[]{:S(2)}) collective-permute-start(f32[40,128]{1,0:T(8,128)S(1)} %get-tuple-element.35), channel_id=1, source_target_pairs={{1,2},{2,1},{3,0},{0,3},{5,6},{6,5},{7,4},{4,7},{9,10},{10,9},{11,... | collective-permute-start | bytes 61448 | tf_op jit(solution)/shard_map/ppermute | solution.py:657
  5.8 0.5 %collective-permute-start.1 = (f32[40,128]{1,0:T(8,128)S(1)}, f32[40,128]{1,0:T(8,128)S(1)}, u32[]{:S(2)}, u32[]{:S(2)}) collective-permute-start(f32[40,128]{1,0:T(8,128)S(1)} %get-tuple-element.36), channel_id=1, source_target_pairs={{0,1},{1,0},{2,3},{3,2},{4,5},{5,4},{6,7},{7,6},{8,9},{9,8},{10,11... | collective-permute-start | bytes 61448 | tf_op jit(solution)/shard_map/ppermute | solution.py:660
  6.3 1.2 %collective-permute-done.gb_ref = f32[40,128]{1,0:T(8,128)S(1)} collective-permute-done((f32[40,128]{1,0:T(8,128)S(1)}, f32[40,128]{1,0:T(8,128)S(1)}, u32[]{:S(2)}, u32[]{:S(2)}) %collective-permute-start) | collective-permute-done | bytes 20512 | tf_op jit(solution)/shard_map/ppermute | solution.py:657
  7.5 2.0 %collective-permute-done.1.ga_ref = f32[40,128]{1,0:T(8,128)S(1)} collective-permute-done((f32[40,128]{1,0:T(8,128)S(1)}, f32[40,128]{1,0:T(8,128)S(1)}, u32[]{:S(2)}, u32[]{:S(2)}) %collective-permute-start.1) | collective-permute-done | bytes 20512 | tf_op jit(solution)/shard_map/ppermute | solution.py:660
  9.5 0.2 shard_map.51
  9.7 2.0 %collective-permute-start.2 = (f32[32,384]{1,0:T(8,128)S(1)}, f32[32,384]{1,0:T(8,128)S(1)}, u32[]{:S(2)}, u32[]{:S(2)}) collective-permute-start(f32[32,384]{1,0:T(8,128)S(1)} %get-tuple-element.37), channel_id=1, source_target_pairs={{4,8},{8,4},{12,16},{16,12},{20,24},{24,20},{28,0},{0,28},{5,9},{9... | collective-permute-start | bytes 147464 | tf_op jit(solution)/shard_map/ppermute | solution.py:657
  11.7 0.0 collective-permute-start.3
  11.7 0.0 copy-done
  11.7 0.1 shard_map.53
  11.9 2.4 %collective-permute-start.4 = (f32[8,128]{1,0:T(8,128)S(1)}, f32[8,128]{1,0:T(8,128)S(1)}, u32[]{:S(2)}, u32[]{:S(2)}) collective-permute-start(f32[8,128]{1,0:T(8,128)S(1)} %get-tuple-element.42.table_ref), channel_id=1, source_target_pairs={{0,16},{4,20},{8,24},{12,28},{16,0},{20,4},{24,8},{28,12},{1,17},{... | collective-permute-start | bytes 12296 | tf_op jit(solution)/shard_map/ppermute | solution.py:663
  14.3 0.6 %shard_map.52.tile_ref = f32[144,512]{1,0:T(8,128)S(1)} custom-call(f32[256,256]{1,0:T(8,128)S(1)} %pad_add_fusion.both_ref, f32[128,128]{1,0:T(8,128)S(1)} %get-tuple-element.39.r3_ref, f32[1104,512]{1,0:T(8,128)S(1)} %copy-done), custom_call_target="tpu_custom_call" | custom-call | flops 1000000000 | bytes 1000000 | tf_op jit(solution)/shard_map/pallas_call | solution.py:618
  14.9 0.5 %collective-permute-done.2.gb_ref = f32[32,384]{1,0:T(8,128)S(1)} collective-permute-done((f32[32,384]{1,0:T(8,128)S(1)}, f32[32,384]{1,0:T(8,128)S(1)}, u32[]{:S(2)}, u32[]{:S(2)}) %collective-permute-start.2) | collective-permute-done | bytes 49184 | tf_op jit(solution)/shard_map/ppermute | solution.py:657
  15.4 0.0 collective-permute-done.3.ga_ref
  15.4 1.0 %shard_map.54 = (f32[144,512]{1,0:T(8,128)S(1)}, f32[8,128]{1,0:T(8,128)S(1)}, f32[24,144]{1,0:T(8,128)S(1)}, f32[24,144]{1,0:T(8,128)S(1)}) custom-call(f32[32,384]{1,0:T(8,128)S(1)} %collective-permute-done.2.gb_ref, f32[32,384]{1,0:T(8,128)S(1)} %collective-permute-done.3.ga_ref, f32[144,512]{1,0:T(8,128)S(1)} %shard_map.52.tile_ref, ...), custom_call_target="tpu_custom_call" | custom-call | flops 1000000000 | bytes 1000000 | tf_op jit(solution)/shard_map/pallas_call | solution.py:618
  16.4 0.1 collective-permute-done.4
  16.5 0.9 %collective-permute-start.6 = (f32[32,144]{1,0:T(8,128)S(1)}, f32[32,144]{1,0:T(8,128)S(1)}, u32[]{:S(2)}, u32[]{:S(2)}) collective-permute-start(f32[32,144]{1,0:T(8,128)S(1)} %get-tuple-element.68), channel_id=1, source_target_pairs={{1,2},{2,1},{3,0},{0,3},{5,6},{6,5},{7,4},{4,7},{9,10},{10,9},{11,... | collective-permute-start | bytes 55304 | tf_op jit(solution)/shard_map/ppermute | solution.py:657
  17.4 1.0 %collective-permute-start.5 = (f32[32,144]{1,0:T(8,128)S(1)}, f32[32,144]{1,0:T(8,128)S(1)}, u32[]{:S(2)}, u32[]{:S(2)}) collective-permute-start(f32[32,144]{1,0:T(8,128)S(1)} %get-tuple-element.69), channel_id=1, source_target_pairs={{0,1},{1,0},{2,3},{3,2},{4,5},{5,4},{6,7},{7,6},{8,9},{9,8},{10,11... | collective-permute-start | bytes 55304 | tf_op jit(solution)/shard_map/ppermute | solution.py:660
  18.5 0.8 %shard_map.55 = (f32[144,384]{1,0:T(8,128)S(1)}, f32[160,384]{1,0:T(8,128)S(1)}) custom-call(f32[144,512]{1,0:T(8,128)S(1)} %get-tuple-element.43.t_ref, f32[1104,512]{1,0:T(8,128)S(1)} %copy-done, f32[256,256]{1,0:T(8,128)S(1)} %pad_add_fusion.both_ref, f32[128,128]{1,0:T(8,128)S(1)} %get-tuple-element.44.h3_ref, ...), custom_call_target="tpu_custom_call" | custom-call | flops 1000000000 | bytes 1000000 | tf_op jit(solution)/shard_map/pallas_call | solution.py:618
  19.3 2.1 %collective-permute-done.6.refs_1_ = f32[32,144]{1,0:T(8,128)S(1)} collective-permute-done((f32[32,144]{1,0:T(8,128)S(1)}, f32[32,144]{1,0:T(8,128)S(1)}, u32[]{:S(2)}, u32[]{:S(2)}) %collective-permute-start.6) | collective-permute-done | bytes 18464 | tf_op jit(solution)/shard_map/ppermute | solution.py:657
  21.3 0.0 collective-permute-done.5.refs_0_
  21.3 0.2 shard_map.56
  21.5 0.5 %collective-permute-start.7 = (f32[32,384]{1,0:T(8,128)S(1)}, f32[32,384]{1,0:T(8,128)S(1)}, u32[]{:S(2)}, u32[]{:S(2)}) collective-permute-start(f32[32,384]{1,0:T(8,128)S(1)} %get-tuple-element.51), channel_id=1, source_target_pairs={{4,8},{8,4},{12,16},{16,12},{20,24},{24,20},{28,0},{0,28},{5,9},{9... | collective-permute-start | bytes 147464 | tf_op jit(solution)/shard_map/ppermute | solution.py:657
  22.1 1.0 %collective-permute-start.8 = (f32[32,384]{1,0:T(8,128)S(1)}, f32[32,384]{1,0:T(8,128)S(1)}, u32[]{:S(2)}, u32[]{:S(2)}) collective-permute-start(f32[32,384]{1,0:T(8,128)S(1)} %get-tuple-element.52), channel_id=1, source_target_pairs={{0,4},{4,0},{8,12},{12,8},{16,20},{20,16},{24,28},{28,24},{1,5},{5... | collective-permute-start | bytes 147464 | tf_op jit(solution)/shard_map/ppermute | solution.py:660
  23.1 3.8 %collective-permute-done.7.gb_ref = f32[32,384]{1,0:T(8,128)S(1)} collective-permute-done((f32[32,384]{1,0:T(8,128)S(1)}, f32[32,384]{1,0:T(8,128)S(1)}, u32[]{:S(2)}, u32[]{:S(2)}) %collective-permute-start.7) | collective-permute-done | bytes 49184 | tf_op jit(solution)/shard_map/ppermute | solution.py:657
  26.9 0.0 collective-permute-done.8.ga_ref
  26.9 1.7 %shard_map.57 = (f32[128,256]{1,0:T(8,128)S(1)}, f32[128,256]{1,0:T(8,128)S(1)}, f32[144,512]{1,0:T(8,128)S(1)}, f32[8,128]{1,0:T(8,128)S(1)}, f32[16,144]{1,0:T(8,128)S(1)}, /*index=5*/f32[16,144]{1,0:T(8,128)S(1)}) custom-call(f32[144,384]{1,0:T(8,128)S(1)} %get-tuple-element.49.y_ref, f32[160,384]{1,0:T(8,128)S(1)} %get-tuple-element.50.m_ref, ...), custom_call_target="tpu_custom_call" | custom-call | flops 1000000000 | bytes 1000000 | tf_op jit(solution)/shard_map/pallas_call | solution.py:618
  28.6 0.0 collective-permute-start.9
  28.6 2.5 %collective-permute-start.10 = (f32[16,144]{1,0:T(8,128)S(1)}, f32[16,144]{1,0:T(8,128)S(1)}, u32[]{:S(2)}, u32[]{:S(2)}) collective-permute-start(f32[16,144]{1,0:T(8,128)S(1)} %get-tuple-element.59), channel_id=1, source_target_pairs={{0,1},{1,0},{2,3},{3,2},{4,5},{5,4},{6,7},{7,6},{8,9},{9,8},{10,11... | collective-permute-start | bytes 27656 | tf_op jit(solution)/shard_map/ppermute | solution.py:660
  31.1 0.8 %shard_map.58 = (f32[144,384]{1,0:T(8,128)S(1)}, f32[1,128]{1,0:T(1,128)S(1)}) custom-call(f32[144,512]{1,0:T(8,128)S(1)} %get-tuple-element.54.t_ref, f32[1104,512]{1,0:T(8,128)S(1)} %copy-done, f32[256,256]{1,0:T(8,128)S(1)} %pad_add_fusion.both_ref, f32[160,384]{1,0:T(8,128)S(1)} %get-tuple-element.50.m_ref, f32[128,256]{1,0:T(8,128)S(1)} %get-tuple-element.55.z_ref, ...), custom_call_target="tpu_custom_call" | custom-call | flops 1000000000 | bytes 1000000 | tf_op jit(solution)/shard_map/pallas_call | solution.py:618
  32.0 0.0 collective-permute-done.9.refs_0_
  32.0 1.0 %collective-permute-done.10.refs_1_ = f32[16,144]{1,0:T(8,128)S(1)} collective-permute-done((f32[16,144]{1,0:T(8,128)S(1)}, f32[16,144]{1,0:T(8,128)S(1)}, u32[]{:S(2)}, u32[]{:S(2)}) %collective-permute-start.10) | collective-permute-done | bytes 9248 | tf_op jit(solution)/shard_map/ppermute | solution.py:660
  33.0 0.2 shard_map.59
  33.2 1.9 %collective-permute-start.11 = (f32[16,384]{1,0:T(8,128)S(1)}, f32[16,384]{1,0:T(8,128)S(1)}, u32[]{:S(2)}, u32[]{:S(2)}) collective-permute-start(f32[16,384]{1,0:T(8,128)S(1)} %get-tuple-element.61), channel_id=1, source_target_pairs={{0,1},{1,0},{2,3},{3,2},{4,8},{5,9},{6,10},{7,11},{8,4},{9,5},{10,... | collective-permute-start | bytes 73736 | tf_op jit(solution)/shard_map/ppermute | solution.py:659
  35.1 0.0 collective-permute-start.12
  35.1 2.0 %collective-permute-done.11.gb_ref = f32[16,384]{1,0:T(8,128)S(1)} collective-permute-done((f32[16,384]{1,0:T(8,128)S(1)}, f32[16,384]{1,0:T(8,128)S(1)}, u32[]{:S(2)}, u32[]{:S(2)}) %collective-permute-start.11) | collective-permute-done | bytes 24608 | tf_op jit(solution)/shard_map/ppermute | solution.py:659
  37.1 0.0 collective-permute-done.12.ga_ref
  37.1 0.4 shard_map.60
  37.6 9.2 %all_to_all.11 = f32[32,1,128]{2,1,0:T(1,128)S(1)} all-to-all(f32[32,1,128]{2,1,0:T(1,128)S(1)} %bitcast.5), channel_id=1, replica_groups=mesh['row'=8,'col'=4] {'row','col'}, dimensions={0} | all-to-all | bytes 32768 | tf_op jit(solution)/shard_map/all_to_all | solution.py:749
  46.7 1.4 %shard_map.61 = (f32[128,256]{1,0:T(8,128)}, f32[128,256]{1,0:T(8,128)}) custom-call(f32[32,128]{1,0:T(8,128)S(1)} %bitcast.4, f32[8,128]{1,0:T(8,128)S(1)} %get-tuple-element.65.table_ref, f32[1104,512]{1,0:T(8,128)S(1)} %copy-done, f32[160,384]{1,0:T(8,128)S(1)} %get-tuple-element.50.m_ref, f32[256,256]{1,0:T(8,128)S(1)} %pad_add_fusion.both_ref, ...), custom_call_target="tpu_custom_call" | custom-call | flops 1000000000 | bytes 1000000 | tf_op jit(solution)/shard_map/pallas_call | solution.py:618
  (2 shorter events, 0.0 us)
Async XLA Ops:
  1.8 9.9 %copy-start = (f32[1104,512]{1,0:T(8,128)S(1)}, f32[1104,512]{1,0:T(8,128)}, u32[]{:S(2)}) copy-start(f32[1104,512]{1,0:T(8,128)} %constant.5.clone.basis_ref) | copy-start | bytes 6782980
  1.8 5.7 %collective-permute-start = (f32[40,128]{1,0:T(8,128)S(1)}, f32[40,128]{1,0:T(8,128)S(1)}, u32[]{:S(2)}, u32[]{:S(2)}) collective-permute-start(f32[40,128]{1,0:T(8,128)S(1)} %get-tuple-element.35), channel_id=1, source_target_pairs={{1,2},{2,1},{3,0},{0,3},{5,6},{6,5},{7,4},{4,7},{9,10},{10,9},{11,... | collective-permute-start | bytes 61448 | tf_op jit(solution)/shard_map/ppermute | solution.py:657
  5.8 3.8 %collective-permute-start.1 = (f32[40,128]{1,0:T(8,128)S(1)}, f32[40,128]{1,0:T(8,128)S(1)}, u32[]{:S(2)}, u32[]{:S(2)}) collective-permute-start(f32[40,128]{1,0:T(8,128)S(1)} %get-tuple-element.36), channel_id=1, source_target_pairs={{0,1},{1,0},{2,3},{3,2},{4,5},{5,4},{6,7},{7,6},{8,9},{9,8},{10,11... | collective-permute-start | bytes 61448 | tf_op jit(solution)/shard_map/ppermute | solution.py:660
  9.7 5.6 %collective-permute-start.2 = (f32[32,384]{1,0:T(8,128)S(1)}, f32[32,384]{1,0:T(8,128)S(1)}, u32[]{:S(2)}, u32[]{:S(2)}) collective-permute-start(f32[32,384]{1,0:T(8,128)S(1)} %get-tuple-element.37), channel_id=1, source_target_pairs={{4,8},{8,4},{12,16},{16,12},{20,24},{24,20},{28,0},{0,28},{5,9},{9... | collective-permute-start | bytes 147464 | tf_op jit(solution)/shard_map/ppermute | solution.py:657
  11.7 3.7 %collective-permute-start.3 = (f32[32,384]{1,0:T(8,128)S(1)}, f32[32,384]{1,0:T(8,128)S(1)}, u32[]{:S(2)}, u32[]{:S(2)}) collective-permute-start(f32[32,384]{1,0:T(8,128)S(1)} %get-tuple-element.38), channel_id=1, source_target_pairs={{0,4},{4,0},{8,12},{12,8},{16,20},{20,16},{24,28},{28,24},{1,5},{5... | collective-permute-start | bytes 147464 | tf_op jit(solution)/shard_map/ppermute | solution.py:660
  11.9 4.6 %collective-permute-start.4 = (f32[8,128]{1,0:T(8,128)S(1)}, f32[8,128]{1,0:T(8,128)S(1)}, u32[]{:S(2)}, u32[]{:S(2)}) collective-permute-start(f32[8,128]{1,0:T(8,128)S(1)} %get-tuple-element.42.table_ref), channel_id=1, source_target_pairs={{0,16},{4,20},{8,24},{12,28},{16,0},{20,4},{24,8},{28,12},{1,17},{... | collective-permute-start | bytes 12296 | tf_op jit(solution)/shard_map/ppermute | solution.py:663
  16.5 4.9 %collective-permute-start.6 = (f32[32,144]{1,0:T(8,128)S(1)}, f32[32,144]{1,0:T(8,128)S(1)}, u32[]{:S(2)}, u32[]{:S(2)}) collective-permute-start(f32[32,144]{1,0:T(8,128)S(1)} %get-tuple-element.68), channel_id=1, source_target_pairs={{1,2},{2,1},{3,0},{0,3},{5,6},{6,5},{7,4},{4,7},{9,10},{10,9},{11,... | collective-permute-start | bytes 55304 | tf_op jit(solution)/shard_map/ppermute | solution.py:657
  17.4 3.9 %collective-permute-start.5 = (f32[32,144]{1,0:T(8,128)S(1)}, f32[32,144]{1,0:T(8,128)S(1)}, u32[]{:S(2)}, u32[]{:S(2)}) collective-permute-start(f32[32,144]{1,0:T(8,128)S(1)} %get-tuple-element.69), channel_id=1, source_target_pairs={{0,1},{1,0},{2,3},{3,2},{4,5},{5,4},{6,7},{7,6},{8,9},{9,8},{10,11... | collective-permute-start | bytes 55304 | tf_op jit(solution)/shard_map/ppermute | solution.py:660
  21.5 5.4 %collective-permute-start.7 = (f32[32,384]{1,0:T(8,128)S(1)}, f32[32,384]{1,0:T(8,128)S(1)}, u32[]{:S(2)}, u32[]{:S(2)}) collective-permute-start(f32[32,384]{1,0:T(8,128)S(1)} %get-tuple-element.51), channel_id=1, source_target_pairs={{4,8},{8,4},{12,16},{16,12},{20,24},{24,20},{28,0},{0,28},{5,9},{9... | collective-permute-start | bytes 147464 | tf_op jit(solution)/shard_map/ppermute | solution.py:657
  22.1 4.8 %collective-permute-start.8 = (f32[32,384]{1,0:T(8,128)S(1)}, f32[32,384]{1,0:T(8,128)S(1)}, u32[]{:S(2)}, u32[]{:S(2)}) collective-permute-start(f32[32,384]{1,0:T(8,128)S(1)} %get-tuple-element.52), channel_id=1, source_target_pairs={{0,4},{4,0},{8,12},{12,8},{16,20},{20,16},{24,28},{28,24},{1,5},{5... | collective-permute-start | bytes 147464 | tf_op jit(solution)/shard_map/ppermute | solution.py:660
  28.6 3.4 %collective-permute-start.9 = (f32[16,144]{1,0:T(8,128)S(1)}, f32[16,144]{1,0:T(8,128)S(1)}, u32[]{:S(2)}, u32[]{:S(2)}) collective-permute-start(f32[16,144]{1,0:T(8,128)S(1)} %get-tuple-element.58), channel_id=1, source_target_pairs={{0,4},{1,2},{2,1},{3,7},{4,0},{5,6},{6,5},{7,3},{8,12},{9,10},{10,... | collective-permute-start | bytes 27656 | tf_op jit(solution)/shard_map/ppermute | solution.py:659
  28.6 4.4 %collective-permute-start.10 = (f32[16,144]{1,0:T(8,128)S(1)}, f32[16,144]{1,0:T(8,128)S(1)}, u32[]{:S(2)}, u32[]{:S(2)}) collective-permute-start(f32[16,144]{1,0:T(8,128)S(1)} %get-tuple-element.59), channel_id=1, source_target_pairs={{0,1},{1,0},{2,3},{3,2},{4,5},{5,4},{6,7},{7,6},{8,9},{9,8},{10,11... | collective-permute-start | bytes 27656 | tf_op jit(solution)/shard_map/ppermute | solution.py:660
  33.2 3.9 %collective-permute-start.11 = (f32[16,384]{1,0:T(8,128)S(1)}, f32[16,384]{1,0:T(8,128)S(1)}, u32[]{:S(2)}, u32[]{:S(2)}) collective-permute-start(f32[16,384]{1,0:T(8,128)S(1)} %get-tuple-element.61), channel_id=1, source_target_pairs={{0,1},{1,0},{2,3},{3,2},{4,8},{5,9},{6,10},{7,11},{8,4},{9,5},{10,... | collective-permute-start | bytes 73736 | tf_op jit(solution)/shard_map/ppermute | solution.py:659
  35.1 2.0 %collective-permute-start.12 = (f32[16,384]{1,0:T(8,128)S(1)}, f32[16,384]{1,0:T(8,128)S(1)}, u32[]{:S(2)}, u32[]{:S(2)}) collective-permute-start(f32[16,384]{1,0:T(8,128)S(1)} %get-tuple-element.62), channel_id=1, source_target_pairs={{0,4},{4,0},{8,12},{12,8},{16,20},{20,16},{24,28},{28,24},{1,5},{5... | collective-permute-start | bytes 73736 | tf_op jit(solution)/shard_map/ppermute | solution.py:660

commit v9 on v8

--- a/solution.py
+++ b/solution.py
@@ -47,7 +47,7 @@
 
 
 def rows_t_part(ref):
-    return ref[2 * EXT : 3 * EXT, :EXT]
+    return ref[2 * EXT : 3 * EXT, :256]
 
 
 def cols_part(ref):
@@ -250,12 +250,55 @@
     return 1.0 / (DAMP + mean * basis_ref[:EXT])
 
 
+def packed(parts, width):
+    lane = lanes_of((8, 128))
+    out = parts[0]
+    for k, part in enumerate(parts[1:], 1):
+        out = jnp.where(lane >= k * width, pltpu.roll(part, k * width, 1), out)
+    return jnp.where(lane < len(parts) * width, out, 0.0)
+
+
+def unpacked(block, k, width):
+    return pltpu.roll(block, (128 - k * width) % 128, 1)
+
+
+def pack_strip(strip):
+    parts = [strip[at : at + 8, 128:] for at in range(0, strip.shape[0], 8)]
+    return jnp.concatenate([strip[:, :128], packed(parts, EXT - SUB)], axis=0)
+
+
+def unpack_strip(message):
+    deep = message.shape[0] - 8
+    parts = [unpacked(message[deep:], k, EXT - SUB) for k in range(deep // 8)]
+    return message[:deep], jnp.concatenate(parts, axis=0)
+
+
+def around(tile):
+    return pltpu.roll(tile, 16, 1)
+
+
+def pack_rows_message(rows, table):
+    parts = [around(rows[at : at + 8, 256:]) for at in range(0, rows.shape[0], 8)]
+    last = jnp.concatenate([packed(parts, 32), table], axis=1)
+    return jnp.concatenate([rows[:, :256], last], axis=0)
+
+
+def unpack_rows(message, start, stop):
+    block = message[message.shape[0] - 8 :, :128]
+    lane = lanes_of((8, 128))
+    thirds = []
+    for k in range(start // 8, stop // 8):
+        part = pltpu.roll(unpacked(block, k, 32), 112, 1)
+        thirds.append(jnp.where((lane < 16) | (lane >= 112), part, 0.0))
+    return jnp.concatenate([message[start:stop], jnp.concatenate(thirds, axis=0)], axis=1)
+
+
 def strips_of(t, basis_ref, deep):
     cols = cols_part(basis_ref)
     left = dot(cols[:deep], t[:, :SPEC], 1)
     right = dot(cols[EXT - deep : EXT], t[:, SPEC:], 1)
     both = dot(jnp.concatenate([left, right], axis=0), rows_t_part(basis_ref))
-    return both[:deep], both[deep:]
+    return pack_strip(both[:deep]), pack_strip(both[deep:])
 
 
 def solution_of(t, basis_ref):
@@ -273,12 +316,16 @@
 
 
 def add_columns(y, from_left, from_right):
-    far = from_left.shape[0] - OV
-    gap = jnp.zeros((56 - far, EXT), jnp.float32)
-    turned = jnp.concatenate(
-        [from_right[8:], gap, from_right[:8], from_left[far:], gap, from_left[:far]], axis=0
-    )
-    back = turned.T
+    left, right = unpack_strip(from_left), unpack_strip(from_right)
+    far = left[0].shape[0] - OV
+    gap = jnp.zeros((56 - far, 128), jnp.float32)
+
+    def turn(k):
+        return jnp.concatenate(
+            [right[k][8:], gap, right[k][:8], left[k][far:], gap, left[k][:far]], axis=0
+        ).T
+
+    back = jnp.concatenate([turn(0), turn(1)[: EXT - SUB]], axis=0)
     lane = lanes_of((EXT, 128))
     rolled = pltpu.roll(back, 64, 1)
     first = y[:, :128] + jnp.where(lane < 8, rolled, 0.0)
@@ -315,13 +362,13 @@
 
 
 def next_table(index, a, b):
-    return jnp.where(is_even(index), a, b)[24:, :128]
+    return jnp.where(is_even(index), a, b)[32:]
 
 
 def row_tables(index, nr, rows, a, b):
     even = is_even(index)
-    after = jnp.where(even, a, b)[24:, :128]
-    before = jnp.where(even, b, a)[24:, :128]
+    after = jnp.where(even, a, b)[24:, 128:]
+    before = jnp.where(even, b, a)[24:, 128:]
     if nr == 4:
         return jnp.where(rows == 2, after, 0.0)
     far = rows % 8
@@ -340,12 +387,12 @@
     r, h = both_ref[:TR], both_ref[TR:]
     lane = lanes_of((128, 128))
     packed = jnp.where(
-        lane < 16,
+        lane < 8,
         r[:, :128],
         jnp.where(
             lane < 64,
-            pltpu.roll(h[:, :128], 16, 1),
-            jnp.where(lane < 112, pltpu.roll(h[:, 128:], 112, 1), r[:, 128:]),
+            pltpu.roll(h[:, :128], 8, 1),
+            jnp.where(lane < 120, pltpu.roll(h[:, 128:], 120, 1), r[:, 128:]),
         ),
     )
     turned = packed.T
@@ -354,38 +401,36 @@
         lax.axis_index("col"),
         a_ref,
         b_ref,
-        jnp.concatenate([turned[:32], table], axis=0),
-        jnp.concatenate([turned[96:], table], axis=0),
+        jnp.concatenate([turned[:24], table], axis=0),
+        jnp.concatenate([turned[104:], table], axis=0),
     )
 
 
 def widen_kernel(counts, both_ref, gb_ref, ga_ref, r3_ref, h3_ref, b_ref, a_ref, table_ref):
     i, j = place()
-    from_left, from_right = sides(j, counts[1], ga_ref[:32], gb_ref[:32])
-    turned = jnp.concatenate([from_right, jnp.zeros((64, 128), jnp.float32), from_left], axis=0)
+    from_left, from_right = sides(j, counts[1], ga_ref[:24], gb_ref[:24])
+    turned = jnp.concatenate([from_right, jnp.zeros((80, 128), jnp.float32), from_left], axis=0)
     back = turned.T
     lane = lanes_of((128, 128))
-    edge = (lane < 16) | (lane >= 112)
-    r3 = jnp.where(edge, back, 0.0)
+    r3 = jnp.where((lane < 8) | (lane >= 120), back, 0.0)
     h3 = jnp.where(
-        lane < 16, pltpu.roll(back, 112, 1), jnp.where(lane >= 112, pltpu.roll(back, 16, 1), 0.0)
+        lane < 16, pltpu.roll(back, 120, 1), jnp.where(lane >= 112, pltpu.roll(back, 8, 1), 0.0)
     )
     r3_ref[...] = r3
     h3_ref[...] = h3
     r, h = both_ref[:TR], both_ref[TR:]
-    table = table_of(core_sums(r), counts) + ga_ref[32:] + gb_ref[32:]
+    table = table_of(core_sums(r), counts) + ga_ref[24:] + gb_ref[24:]
     table_ref[...] = table
-    wide = jnp.concatenate([table, jnp.zeros((table.shape[0], FC - 128), jnp.float32)], axis=1)
 
     def strip(r_rows, h_rows):
-        return jnp.concatenate(
+        rows = jnp.concatenate(
             [
                 jnp.concatenate([r[r_rows], r3[r_rows]], axis=1),
                 jnp.concatenate([h[h_rows], h3[h_rows]], axis=1),
-                wide,
             ],
             axis=0,
         )
+        return pack_rows_message(rows, table)
 
     send(i, a_ref, b_ref, strip(slice(0, 8), slice(0, 16)), strip(slice(120, 128), slice(112, 128)))
 
@@ -417,19 +462,20 @@
     a_ref,
 ):
     i, j = place()
-    above, below = sides(i, counts[0], ga_ref[:8], gb_ref[:8])
-    u = column_transform(jnp.concatenate([below, above], axis=0), basis_ref)
+    above, below = sides(i, counts[0], ga_ref[...], gb_ref[...])
+    halo = jnp.concatenate([unpack_rows(below, 0, 8), unpack_rows(above, 0, 8)], axis=0)
+    u = column_transform(halo, basis_ref)
     t = (tile_ref[...] + row_transform(u, basis_ref, halo_rows)) * weights_ref[...]
     t_ref[...] = t
     send(j, a_ref, b_ref, *strips_of(t, basis_ref, 24))
-    table_out[...] = table_ref[...] + ga_ref[24:, :128] + gb_ref[24:, :128]
+    table_out[...] = table_ref[...] + ga_ref[24:, 128:] + gb_ref[24:, 128:]
 
 
 def inverse_kernel(counts, t_ref, basis_ref, both_ref, h3_ref, gb_ref, ga_ref, y_ref, m_ref):
     y_ref[...] = solution_of(t_ref[...], basis_ref)
-    above, below = sides(lax.axis_index("row"), counts[0], ga_ref[8:24], gb_ref[8:24])
+    above, below = sides(lax.axis_index("row"), counts[0], ga_ref[...], gb_ref[...])
     h = jnp.concatenate([both_ref[TR:], h3_ref[...]], axis=1)
-    tall = jnp.concatenate([h, below, above], axis=0)
+    tall = jnp.concatenate([h, unpack_rows(below, 8, 24), unpack_rows(above, 8, 24)], axis=0)
     m_ref[...] = tall * tall * tall
 
 
@@ -437,7 +483,7 @@
     i, j = place()
     (ga_ref, gb_ref), refs = (refs[:2] if len(refs) == 7 else refs[1::-1]), refs[2:]
     deep = 24 if len(refs) == 5 else 16
-    y = add_columns(y_ref[...], *sides(j, counts[1], ga_ref[:deep], gb_ref[:deep]))
+    y = add_columns(y_ref[...], *sides(j, counts[1], ga_ref[: deep + 8], gb_ref[: deep + 8]))
     strips = pack_rows(y, deep)
     if len(refs) == 5:
         table_ref, out_ref, table_out, b_ref, a_ref = refs
@@ -446,12 +492,11 @@
             cols % 4 == 2, next_table(j, ga_ref[...], gb_ref[...]), 0.0
         )
         table_out[...] = table
-        wide = jnp.concatenate([table, jnp.zeros((table.shape[0], FC - 128), jnp.float32)], axis=1)
-        strips = [jnp.concatenate([x, wide], axis=0) for x in strips]
     else:
         out_ref, b_ref, a_ref = refs
+        table = jnp.zeros((8, 128), jnp.float32)
     out_ref[...] = y
-    send(i, a_ref, b_ref, *strips)
+    send(i, a_ref, b_ref, *(pack_rows_message(x, table) for x in strips))
 
 
 def second_kernel(
@@ -472,7 +517,8 @@
     a_ref,
 ):
     i, j = place()
-    s = add_rows(y_ref[...], *sides(i, counts[0], ga_ref[:24], gb_ref[:24]))
+    above, below = sides(i, counts[0], ga_ref[...], gb_ref[...])
+    s = add_rows(y_ref[...], unpack_rows(above, 0, 24), unpack_rows(below, 0, 24))
     mask = grid_mask((FR, FC), counts)
     s = jnp.where(mask, s, 0.0)
     rows = flat_place(counts)[1]
@@ -528,7 +574,8 @@
     counts, y_ref, m_ref, gb_ref, ga_ref, both_ref, w_ref, stats_ref, q_ref, v_ref, stats_out
 ):
     i, j = place()
-    q = add_rows(y_ref[...], *sides(i, counts[0], ga_ref[...], gb_ref[...]))
+    above, below = sides(i, counts[0], ga_ref[...], gb_ref[...])
+    q = add_rows(y_ref[...], unpack_rows(above, 0, 16), unpack_rows(below, 0, 16))
     q = jnp.where(grid_mask((FR, FC), counts), q, 0.0)
     v = DAMP * q + lap(m_ref[...] * lap(q))
     qt, vt = q[:128, :256], v[:128, :256]
@@ -663,11 +710,11 @@
         return lax.ppermute(x, "row", [(k, (k + step) % nr) for k in range(nr)])
 
     both = jnp.pad(noise, ((0, TR), (0, 0))) + jnp.pad(height, ((TR, 0), (0, 0)))
-    b, a = call(functools.partial(begin_kernel, counts), [(32 + depth, 128)] * 2, both)
+    b, a = call(functools.partial(begin_kernel, counts), [(24 + depth, 128)] * 2, both)
     ga, gb = swap(a, b, "col")
     r3, h3, b, a, table = call(
         functools.partial(widen_kernel, counts),
-        [(128, 128)] * 2 + [(24 + depth, FC)] * 2 + [(depth, 128)],
+        [(128, 128)] * 2 + [(24 + depth, 256)] * 2 + [(depth, 128)],
         both,
         gb,
         ga,
@@ -677,14 +724,14 @@
         table = table + row_shift(table, step)
         step //= 2
     if nr > 8:
-        a, b = (x.at[24:, :128].set(table) for x in (a, b))
+        a, b = (x.at[24:, 128:].set(table) for x in (a, b))
     ga, gb = swap(a, b, "row")
     weight, table = call(weights_kernel, [(EXT, 2 * SPEC), (depth, 128)], both, table, basis)
     far = row_shift(table, 4) if nr >= 8 else 0.0
     t = call(forward_kernel, [(EXT, 2 * SPEC)], both, r3, basis)[0]
     t, table, b, a = call(
         functools.partial(first_kernel, counts),
-        [(EXT, 2 * SPEC), (depth, 128)] + [(24, EXT)] * 2,
+        [(EXT, 2 * SPEC), (depth, 128)] + [(32, 128)] * 2,
         gb,
         ga,
         t,
@@ -697,7 +744,6 @@
     while step >= 4:
         table = table + lax.ppermute(table, "col", [(k, (k + step) % nc) for k in range(nc)])
         step //= 2
-    wide = jnp.pad(table, ((0, 0), (0, EXT - 128)))
     y, m = call(
         functools.partial(inverse_kernel, counts),
         [(EXT, FC), (FR, FC)],
@@ -708,10 +754,10 @@
         gb,
         ga,
     )
-    ga, gb = swap(*(jnp.concatenate([x, wide], axis=0) for x in (a, b)), "col")
+    ga, gb = swap(*(jnp.concatenate([x, table], axis=0) for x in (a, b)), "col")
     y, table, b, a = call(
         functools.partial(columns_kernel, counts),
-        [(EXT, FC), (depth, 128)] + [(24 + depth, FC)] * 2,
+        [(EXT, FC), (depth, 128)] + [(24 + depth, 256)] * 2,
         y,
         ga,
         gb,
@@ -720,7 +766,7 @@
     ga, gb = swap(a, b, "row")
     z, w, t, table, b, a = call(
         functools.partial(second_kernel, counts, width),
-        [(TR, TC)] * 2 + [(EXT, 2 * SPEC), (depth, 128)] + [(16, EXT)] * 2,
+        [(TR, TC)] * 2 + [(EXT, 2 * SPEC), (depth, 128)] + [(24, 128)] * 2,
         y,
         m,
         gb,
@@ -732,7 +778,7 @@
     ga, gb = swap(a, b, "col", False)
     y, stats = call(inverse_stats_kernel, [(EXT, FC), (1, 128)], t, basis, both, m, z, w)
     y, b, a = call(
-        functools.partial(columns_kernel, counts), [(EXT, FC)] + [(16, FC)] * 2, y, gb, ga
+        functools.partial(columns_kernel, counts), [(EXT, FC)] + [(24, 256)] * 2, y, gb, ga
     )
     ga, gb = swap(a, b, "row", False)
     q, v, stats = call(

time: 48.3 us -> 48.6 us (level)
  Pallas kernels: 7.56 us -> 8.11 us
    ppermute x1, waiting for transfers between devices: 0.06 us -> 0.89 us  [row_shift(): return lax.ppermute(x, 'row', [(k, (k + step) % nr) for k in range(nr)])]
    ppermute x4, waiting for transfers between devices: 7.65 us -> 6.92 us  [swap(): gb = lax.ppermute(b, axis, pairs_from(count, 1))]
    pallas_call x12, Pallas kernels: 7.56 us -> 8.11 us  [call(): pl.pallas_call(kernel, out_shape=shapes, compiler_params=pltpu.CompilerPa...]
    ppermute x4, starting transfers between devices: 7.42 us -> 6.91 us  [swap(): gb = lax.ppermute(b, axis, pairs_from(count, 1))]
where the time goes in v9:
time: 48.6 us; the launch traced here: 48.4 us
  starting transfers between devices  16.6 us (34%)
  waiting for transfers between devices  12.8 us (26%)
  blocking collectives  9.26 us (19%)
  Pallas kernels  8.11 us (17%)
  other arithmetic  1 us (2%)
  between operations  0.72 us (1%)
    all_to_all x1, blocking collectives, body(): stats = lax.all_to_all(stats, both_axes, 0, 0, tiled=True)  9.26 us
    pallas_call x12, Pallas kernels, call(): pl.pallas_call(kernel, out_shape=shapes, compiler_params=pltpu.CompilerPa...  8.11 us
    ppermute x4, waiting for transfers between devices, swap(): gb = lax.ppermute(b, axis, pairs_from(count, 1))  6.92 us
    ppermute x4, starting transfers between devices, swap(): gb = lax.ppermute(b, axis, pairs_from(count, 1))  6.91 us
    ppermute x6, starting transfers between devices, swap(): return (lax.ppermute(a, axis, pairs_from(count, 0)), gb)  5.26 us
    ppermute x6, waiting for transfers between devices, swap(): return (lax.ppermute(a, axis, pairs_from(count, 0)), gb)  3.01 us
    ppermute x1, starting transfers between devices, row_shift(): return lax.ppermute(x, 'row', [(k, (k + step) % nr) for k in range(nr)])  2.47 us
    ppermute x2, starting transfers between devices, swap(): gb = lax.ppermute(b, both_axes, near_pairs(counts, both_axes.index(axis)))  1.96 us
  transfers between devices with their start and end apart: 13, of which 8 were waited for; matrix products, arithmetic and copies ran while one was open for 0% of the time, Pallas kernels for 7%

profile of v9, /device:TPU:0, one launch (start us, length us, event | category | flops | bytes accessed | tf_op | source)
XLA Modules:
  0.0 48.4 jit_solution(18445367764994598462)
XLA Ops:
  0.6 1.0 %pad_add_fusion.both_ref = f32[256,256]{1,0:T(8,128)S(1)} fusion(f32[128,256]{1,0:T(8,128)} %param.3, f32[128,256]{1,0:T(8,128)} %param.4), kind=kLoop, calls=%fused_computation | loop fusion | flops 65536 | bytes 524288 | tf_op jit(solution)/shard_map/add | solution.py:712
  1.6 0.2 shard_map.50
  1.8 0.0 copy-start
  1.8 4.0 %collective-permute-start = (f32[32,128]{1,0:T(8,128)S(1)}, f32[32,128]{1,0:T(8,128)S(1)}, u32[]{:S(2)}, u32[]{:S(2)}) collective-permute-start(f32[32,128]{1,0:T(8,128)S(1)} %get-tuple-element.35), channel_id=1, source_target_pairs={{1,2},{2,1},{3,0},{0,3},{5,6},{6,5},{7,4},{4,7},{9,10},{10,9},{11,... | collective-permute-start | bytes 49160 | tf_op jit(solution)/shard_map/ppermute | solution.py:704
  5.8 0.5 %collective-permute-start.1 = (f32[32,128]{1,0:T(8,128)S(1)}, f32[32,128]{1,0:T(8,128)S(1)}, u32[]{:S(2)}, u32[]{:S(2)}) collective-permute-start(f32[32,128]{1,0:T(8,128)S(1)} %get-tuple-element.36), channel_id=1, source_target_pairs={{0,1},{1,0},{2,3},{3,2},{4,5},{5,4},{6,7},{7,6},{8,9},{9,8},{10,11... | collective-permute-start | bytes 49160 | tf_op jit(solution)/shard_map/ppermute | solution.py:707
  6.3 1.2 %collective-permute-done.gb_ref = f32[32,128]{1,0:T(8,128)S(1)} collective-permute-done((f32[32,128]{1,0:T(8,128)S(1)}, f32[32,128]{1,0:T(8,128)S(1)}, u32[]{:S(2)}, u32[]{:S(2)}) %collective-permute-start) | collective-permute-done | bytes 16416 | tf_op jit(solution)/shard_map/ppermute | solution.py:704
  7.5 2.0 %collective-permute-done.1.ga_ref = f32[32,128]{1,0:T(8,128)S(1)} collective-permute-done((f32[32,128]{1,0:T(8,128)S(1)}, f32[32,128]{1,0:T(8,128)S(1)}, u32[]{:S(2)}, u32[]{:S(2)}) %collective-permute-start.1) | collective-permute-done | bytes 16416 | tf_op jit(solution)/shard_map/ppermute | solution.py:707
  9.5 0.3 shard_map.51
  9.8 1.9 %collective-permute-start.2 = (f32[32,256]{1,0:T(8,128)S(1)}, f32[32,256]{1,0:T(8,128)S(1)}, u32[]{:S(2)}, u32[]{:S(2)}) collective-permute-start(f32[32,256]{1,0:T(8,128)S(1)} %get-tuple-element.37), channel_id=1, source_target_pairs={{4,8},{8,4},{12,16},{16,12},{20,24},{24,20},{28,0},{0,28},{5,9},{9... | collective-permute-start | bytes 98312 | tf_op jit(solution)/shard_map/ppermute | solution.py:704
  11.7 0.0 collective-permute-start.3
  11.7 0.0 copy-done
  11.7 0.6 %shard_map.52.tile_ref = f32[144,512]{1,0:T(8,128)S(1)} custom-call(f32[256,256]{1,0:T(8,128)S(1)} %pad_add_fusion.both_ref, f32[128,128]{1,0:T(8,128)S(1)} %get-tuple-element.39.r3_ref, f32[1104,512]{1,0:T(8,128)S(1)} %copy-done), custom_call_target="tpu_custom_call" | custom-call | flops 1000000000 | bytes 1000000 | tf_op jit(solution)/shard_map/pallas_call | solution.py:665
  12.3 0.2 shard_map.53
  12.5 2.5 %collective-permute-start.4 = (f32[8,128]{1,0:T(8,128)S(1)}, f32[8,128]{1,0:T(8,128)S(1)}, u32[]{:S(2)}, u32[]{:S(2)}) collective-permute-start(f32[8,128]{1,0:T(8,128)S(1)} %get-tuple-element.42.table_ref), channel_id=1, source_target_pairs={{0,16},{4,20},{8,24},{12,28},{16,0},{20,4},{24,8},{28,12},{1,17},{... | collective-permute-start | bytes 12296 | tf_op jit(solution)/shard_map/ppermute | solution.py:710
  14.9 0.1 collective-permute-done.2.gb_ref
  15.0 0.0 collective-permute-done.3.ga_ref
  15.0 1.1 %shard_map.54 = (f32[144,512]{1,0:T(8,128)S(1)}, f32[8,128]{1,0:T(8,128)S(1)}, f32[32,128]{1,0:T(8,128)S(1)}, f32[32,128]{1,0:T(8,128)S(1)}) custom-call(f32[32,256]{1,0:T(8,128)S(1)} %collective-permute-done.2.gb_ref, f32[32,256]{1,0:T(8,128)S(1)} %collective-permute-done.3.ga_ref, f32[144,512]{1,0:T(8,128)S(1)} %shard_map.52.tile_ref, ...), custom_call_target="tpu_custom_call" | custom-call | flops 1000000000 | bytes 1000000 | tf_op jit(solution)/shard_map/pallas_call | solution.py:665
  16.1 0.9 %collective-permute-done.4 = f32[8,128]{1,0:T(8,128)S(1)} collective-permute-done((f32[8,128]{1,0:T(8,128)S(1)}, f32[8,128]{1,0:T(8,128)S(1)}, u32[]{:S(2)}, u32[]{:S(2)}) %collective-permute-start.4) | collective-permute-done | bytes 4128 | tf_op jit(solution)/shard_map/ppermute | solution.py:710
  17.0 1.0 %collective-permute-start.6 = (f32[40,128]{1,0:T(8,128)S(1)}, f32[40,128]{1,0:T(8,128)S(1)}, u32[]{:S(2)}, u32[]{:S(2)}) collective-permute-start(f32[40,128]{1,0:T(8,128)S(1)} %get-tuple-element.68), channel_id=1, source_target_pairs={{1,2},{2,1},{3,0},{0,3},{5,6},{6,5},{7,4},{4,7},{9,10},{10,9},{11,... | collective-permute-start | bytes 61448 | tf_op jit(solution)/shard_map/ppermute | solution.py:704
  18.0 0.9 %collective-permute-start.5 = (f32[40,128]{1,0:T(8,128)S(1)}, f32[40,128]{1,0:T(8,128)S(1)}, u32[]{:S(2)}, u32[]{:S(2)}) collective-permute-start(f32[40,128]{1,0:T(8,128)S(1)} %get-tuple-element.69), channel_id=1, source_target_pairs={{0,1},{1,0},{2,3},{3,2},{4,5},{5,4},{6,7},{7,6},{8,9},{9,8},{10,11... | collective-permute-start | bytes 61448 | tf_op jit(solution)/shard_map/ppermute | solution.py:707
  18.9 0.8 %shard_map.55 = (f32[144,384]{1,0:T(8,128)S(1)}, f32[160,384]{1,0:T(8,128)S(1)}) custom-call(f32[144,512]{1,0:T(8,128)S(1)} %get-tuple-element.43.t_ref, f32[1104,512]{1,0:T(8,128)S(1)} %copy-done, f32[256,256]{1,0:T(8,128)S(1)} %pad_add_fusion.both_ref, f32[128,128]{1,0:T(8,128)S(1)} %get-tuple-element.44.h3_ref, ...), custom_call_target="tpu_custom_call" | custom-call | flops 1000000000 | bytes 1000000 | tf_op jit(solution)/shard_map/pallas_call | solution.py:665
  19.8 2.0 %collective-permute-done.6.refs_1_ = f32[40,128]{1,0:T(8,128)S(1)} collective-permute-done((f32[40,128]{1,0:T(8,128)S(1)}, f32[40,128]{1,0:T(8,128)S(1)}, u32[]{:S(2)}, u32[]{:S(2)}) %collective-permute-start.6) | collective-permute-done | bytes 20512 | tf_op jit(solution)/shard_map/ppermute | solution.py:704
  21.8 0.0 collective-permute-done.5.refs_0_
  21.8 0.3 shard_map.56
  22.1 0.0 collective-permute-start.7
  22.1 1.5 %collective-permute-start.8 = (f32[32,256]{1,0:T(8,128)S(1)}, f32[32,256]{1,0:T(8,128)S(1)}, u32[]{:S(2)}, u32[]{:S(2)}) collective-permute-start(f32[32,256]{1,0:T(8,128)S(1)} %get-tuple-element.52), channel_id=1, source_target_pairs={{0,4},{4,0},{8,12},{12,8},{16,20},{20,16},{24,28},{28,24},{1,5},{5... | collective-permute-start | bytes 98312 | tf_op jit(solution)/shard_map/ppermute | solution.py:707
  23.6 3.6 %collective-permute-done.7.gb_ref = f32[32,256]{1,0:T(8,128)S(1)} collective-permute-done((f32[32,256]{1,0:T(8,128)S(1)}, f32[32,256]{1,0:T(8,128)S(1)}, u32[]{:S(2)}, u32[]{:S(2)}) %collective-permute-start.7) | collective-permute-done | bytes 32800 | tf_op jit(solution)/shard_map/ppermute | solution.py:704
  27.3 0.0 collective-permute-done.8.ga_ref
  27.3 1.8 %shard_map.57 = (f32[128,256]{1,0:T(8,128)S(1)}, f32[128,256]{1,0:T(8,128)S(1)}, f32[144,512]{1,0:T(8,128)S(1)}, f32[8,128]{1,0:T(8,128)S(1)}, f32[24,128]{1,0:T(8,128)S(1)}, /*index=5*/f32[24,128]{1,0:T(8,128)S(1)}) custom-call(f32[144,384]{1,0:T(8,128)S(1)} %get-tuple-element.49.y_ref, f32[160,384]{1,0:T(8,128)S(1)} %get-tuple-element.50.m_ref, ...), custom_call_target="tpu_custom_call" | custom-call | flops 1000000000 | bytes 1000000 | tf_op jit(solution)/shard_map/pallas_call | solution.py:665
  29.0 0.0 collective-permute-start.9
  29.1 2.3 %collective-permute-start.10 = (f32[24,128]{1,0:T(8,128)S(1)}, f32[24,128]{1,0:T(8,128)S(1)}, u32[]{:S(2)}, u32[]{:S(2)}) collective-permute-start(f32[24,128]{1,0:T(8,128)S(1)} %get-tuple-element.59), channel_id=1, source_target_pairs={{0,1},{1,0},{2,3},{3,2},{4,5},{5,4},{6,7},{7,6},{8,9},{9,8},{10,11... | collective-permute-start | bytes 36872 | tf_op jit(solution)/shard_map/ppermute | solution.py:707
  31.4 0.8 %shard_map.58 = (f32[144,384]{1,0:T(8,128)S(1)}, f32[1,128]{1,0:T(1,128)S(1)}) custom-call(f32[144,512]{1,0:T(8,128)S(1)} %get-tuple-element.54.t_ref, f32[1104,512]{1,0:T(8,128)S(1)} %copy-done, f32[256,256]{1,0:T(8,128)S(1)} %pad_add_fusion.both_ref, f32[160,384]{1,0:T(8,128)S(1)} %get-tuple-element.50.m_ref, f32[128,256]{1,0:T(8,128)S(1)} %get-tuple-element.55.z_ref, ...), custom_call_target="tpu_custom_call" | custom-call | flops 1000000000 | bytes 1000000 | tf_op jit(solution)/shard_map/pallas_call | solution.py:665
  32.2 0.0 collective-permute-done.9.refs_0_
  32.2 1.0 %collective-permute-done.10.refs_1_ = f32[24,128]{1,0:T(8,128)S(1)} collective-permute-done((f32[24,128]{1,0:T(8,128)S(1)}, f32[24,128]{1,0:T(8,128)S(1)}, u32[]{:S(2)}, u32[]{:S(2)}) %collective-permute-start.10) | collective-permute-done | bytes 12320 | tf_op jit(solution)/shard_map/ppermute | solution.py:707
  33.2 0.3 shard_map.59
  33.5 1.9 %collective-permute-start.11 = (f32[24,256]{1,0:T(8,128)S(1)}, f32[24,256]{1,0:T(8,128)S(1)}, u32[]{:S(2)}, u32[]{:S(2)}) collective-permute-start(f32[24,256]{1,0:T(8,128)S(1)} %get-tuple-element.61), channel_id=1, source_target_pairs={{0,1},{1,0},{2,3},{3,2},{4,8},{5,9},{6,10},{7,11},{8,4},{9,5},{10,... | collective-permute-start | bytes 73736 | tf_op jit(solution)/shard_map/ppermute | solution.py:706
  35.4 0.0 collective-permute-start.12
  35.4 1.9 %collective-permute-done.11.gb_ref = f32[24,256]{1,0:T(8,128)S(1)} collective-permute-done((f32[24,256]{1,0:T(8,128)S(1)}, f32[24,256]{1,0:T(8,128)S(1)}, u32[]{:S(2)}, u32[]{:S(2)}) %collective-permute-start.11) | collective-permute-done | bytes 24608 | tf_op jit(solution)/shard_map/ppermute | solution.py:706
  37.4 0.0 collective-permute-done.12.ga_ref
  37.4 0.5 shard_map.60
  37.8 9.3 %all_to_all.11 = f32[32,1,128]{2,1,0:T(1,128)S(1)} all-to-all(f32[32,1,128]{2,1,0:T(1,128)S(1)} %bitcast.5), channel_id=1, replica_groups=mesh['row'=8,'col'=4] {'row','col'}, dimensions={0} | all-to-all | bytes 32768 | tf_op jit(solution)/shard_map/all_to_all | solution.py:795
  47.1 1.4 %shard_map.61 = (f32[128,256]{1,0:T(8,128)}, f32[128,256]{1,0:T(8,128)}) custom-call(f32[32,128]{1,0:T(8,128)S(1)} %bitcast.4, f32[8,128]{1,0:T(8,128)S(1)} %get-tuple-element.65.table_ref, f32[1104,512]{1,0:T(8,128)S(1)} %copy-done, f32[160,384]{1,0:T(8,128)S(1)} %get-tuple-element.50.m_ref, f32[256,256]{1,0:T(8,128)S(1)} %pad_add_fusion.both_ref, ...), custom_call_target="tpu_custom_call" | custom-call | flops 1000000000 | bytes 1000000 | tf_op jit(solution)/shard_map/pallas_call | solution.py:665
  (2 shorter events, 0.0 us)
Async XLA Ops:
  1.8 10.0 %copy-start = (f32[1104,512]{1,0:T(8,128)S(1)}, f32[1104,512]{1,0:T(8,128)}, u32[]{:S(2)}) copy-start(f32[1104,512]{1,0:T(8,128)} %constant.5.clone.basis_ref) | copy-start | bytes 6782980
  1.8 5.7 %collective-permute-start = (f32[32,128]{1,0:T(8,128)S(1)}, f32[32,128]{1,0:T(8,128)S(1)}, u32[]{:S(2)}, u32[]{:S(2)}) collective-permute-start(f32[32,128]{1,0:T(8,128)S(1)} %get-tuple-element.35), channel_id=1, source_target_pairs={{1,2},{2,1},{3,0},{0,3},{5,6},{6,5},{7,4},{4,7},{9,10},{10,9},{11,... | collective-permute-start | bytes 49160 | tf_op jit(solution)/shard_map/ppermute | solution.py:704
  5.8 3.7 %collective-permute-start.1 = (f32[32,128]{1,0:T(8,128)S(1)}, f32[32,128]{1,0:T(8,128)S(1)}, u32[]{:S(2)}, u32[]{:S(2)}) collective-permute-start(f32[32,128]{1,0:T(8,128)S(1)} %get-tuple-element.36), channel_id=1, source_target_pairs={{0,1},{1,0},{2,3},{3,2},{4,5},{5,4},{6,7},{7,6},{8,9},{9,8},{10,11... | collective-permute-start | bytes 49160 | tf_op jit(solution)/shard_map/ppermute | solution.py:707
  9.8 5.2 %collective-permute-start.2 = (f32[32,256]{1,0:T(8,128)S(1)}, f32[32,256]{1,0:T(8,128)S(1)}, u32[]{:S(2)}, u32[]{:S(2)}) collective-permute-start(f32[32,256]{1,0:T(8,128)S(1)} %get-tuple-element.37), channel_id=1, source_target_pairs={{4,8},{8,4},{12,16},{16,12},{20,24},{24,20},{28,0},{0,28},{5,9},{9... | collective-permute-start | bytes 98312 | tf_op jit(solution)/shard_map/ppermute | solution.py:704
  11.7 3.3 %collective-permute-start.3 = (f32[32,256]{1,0:T(8,128)S(1)}, f32[32,256]{1,0:T(8,128)S(1)}, u32[]{:S(2)}, u32[]{:S(2)}) collective-permute-start(f32[32,256]{1,0:T(8,128)S(1)} %get-tuple-element.38), channel_id=1, source_target_pairs={{0,4},{4,0},{8,12},{12,8},{16,20},{20,16},{24,28},{28,24},{1,5},{5... | collective-permute-start | bytes 98312 | tf_op jit(solution)/shard_map/ppermute | solution.py:707
  12.5 4.6 %collective-permute-start.4 = (f32[8,128]{1,0:T(8,128)S(1)}, f32[8,128]{1,0:T(8,128)S(1)}, u32[]{:S(2)}, u32[]{:S(2)}) collective-permute-start(f32[8,128]{1,0:T(8,128)S(1)} %get-tuple-element.42.table_ref), channel_id=1, source_target_pairs={{0,16},{4,20},{8,24},{12,28},{16,0},{20,4},{24,8},{28,12},{1,17},{... | collective-permute-start | bytes 12296 | tf_op jit(solution)/shard_map/ppermute | solution.py:710
  17.0 4.7 %collective-permute-start.6 = (f32[40,128]{1,0:T(8,128)S(1)}, f32[40,128]{1,0:T(8,128)S(1)}, u32[]{:S(2)}, u32[]{:S(2)}) collective-permute-start(f32[40,128]{1,0:T(8,128)S(1)} %get-tuple-element.68), channel_id=1, source_target_pairs={{1,2},{2,1},{3,0},{0,3},{5,6},{6,5},{7,4},{4,7},{9,10},{10,9},{11,... | collective-permute-start | bytes 61448 | tf_op jit(solution)/shard_map/ppermute | solution.py:704
  18.0 3.8 %collective-permute-start.5 = (f32[40,128]{1,0:T(8,128)S(1)}, f32[40,128]{1,0:T(8,128)S(1)}, u32[]{:S(2)}, u32[]{:S(2)}) collective-permute-start(f32[40,128]{1,0:T(8,128)S(1)} %get-tuple-element.69), channel_id=1, source_target_pairs={{0,1},{1,0},{2,3},{3,2},{4,5},{5,4},{6,7},{7,6},{8,9},{9,8},{10,11... | collective-permute-start | bytes 61448 | tf_op jit(solution)/shard_map/ppermute | solution.py:707
  22.1 5.2 %collective-permute-start.7 = (f32[32,256]{1,0:T(8,128)S(1)}, f32[32,256]{1,0:T(8,128)S(1)}, u32[]{:S(2)}, u32[]{:S(2)}) collective-permute-start(f32[32,256]{1,0:T(8,128)S(1)} %get-tuple-element.51), channel_id=1, source_target_pairs={{4,8},{8,4},{12,16},{16,12},{20,24},{24,20},{28,0},{0,28},{5,9},{9... | collective-permute-start | bytes 98312 | tf_op jit(solution)/shard_map/ppermute | solution.py:704
  22.1 5.1 %collective-permute-start.8 = (f32[32,256]{1,0:T(8,128)S(1)}, f32[32,256]{1,0:T(8,128)S(1)}, u32[]{:S(2)}, u32[]{:S(2)}) collective-permute-start(f32[32,256]{1,0:T(8,128)S(1)} %get-tuple-element.52), channel_id=1, source_target_pairs={{0,4},{4,0},{8,12},{12,8},{16,20},{20,16},{24,28},{28,24},{1,5},{5... | collective-permute-start | bytes 98312 | tf_op jit(solution)/shard_map/ppermute | solution.py:707
  29.0 3.2 %collective-permute-start.9 = (f32[24,128]{1,0:T(8,128)S(1)}, f32[24,128]{1,0:T(8,128)S(1)}, u32[]{:S(2)}, u32[]{:S(2)}) collective-permute-start(f32[24,128]{1,0:T(8,128)S(1)} %get-tuple-element.58), channel_id=1, source_target_pairs={{0,4},{1,2},{2,1},{3,7},{4,0},{5,6},{6,5},{7,3},{8,12},{9,10},{10,... | collective-permute-start | bytes 36872 | tf_op jit(solution)/shard_map/ppermute | solution.py:706
  29.1 4.1 %collective-permute-start.10 = (f32[24,128]{1,0:T(8,128)S(1)}, f32[24,128]{1,0:T(8,128)S(1)}, u32[]{:S(2)}, u32[]{:S(2)}) collective-permute-start(f32[24,128]{1,0:T(8,128)S(1)} %get-tuple-element.59), channel_id=1, source_target_pairs={{0,1},{1,0},{2,3},{3,2},{4,5},{5,4},{6,7},{7,6},{8,9},{9,8},{10,11... | collective-permute-start | bytes 36872 | tf_op jit(solution)/shard_map/ppermute | solution.py:707
  33.5 3.9 %collective-permute-start.11 = (f32[24,256]{1,0:T(8,128)S(1)}, f32[24,256]{1,0:T(8,128)S(1)}, u32[]{:S(2)}, u32[]{:S(2)}) collective-permute-start(f32[24,256]{1,0:T(8,128)S(1)} %get-tuple-element.61), channel_id=1, source_target_pairs={{0,1},{1,0},{2,3},{3,2},{4,8},{5,9},{6,10},{7,11},{8,4},{9,5},{10,... | collective-permute-start | bytes 73736 | tf_op jit(solution)/shard_map/ppermute | solution.py:706
  35.4 1.9 %collective-permute-start.12 = (f32[24,256]{1,0:T(8,128)S(1)}, f32[24,256]{1,0:T(8,128)S(1)}, u32[]{:S(2)}, u32[]{:S(2)}) collective-permute-start(f32[24,256]{1,0:T(8,128)S(1)} %get-tuple-element.62), channel_id=1, source_target_pairs={{0,4},{4,0},{8,12},{12,8},{16,20},{20,16},{24,28},{28,24},{1,5},{5... | collective-permute-start | bytes 73736 | tf_op jit(solution)/shard_map/ppermute | solution.py:707

commit v10 on v8

--- a/solution.py
+++ b/solution.py
@@ -137,24 +137,22 @@
     return ((rr < below) | (rr >= above)) & ((ll < right) | (ll >= left))
 
 
-def flat_place(counts):
-    i, j = place()
-    nr, nc = counts
-    shape = table_shape(counts)
-    flat = rows_of(shape) * 128 + lanes_of(shape)
-    device = flat % (nr * nc)
-    return flat, (device // nc + nr - i) % nr, (device % nc + nc - j) % nc
-
-
 def table_shape(counts):
     return (-(-2 * counts[0] * counts[1] // 1024) * 8, 128)
 
 
 def table_of(values, counts):
-    flat, rows, cols = flat_place(counts)
+    i, j = place()
     devices = counts[0] * counts[1]
-    own = jnp.where(flat < devices, values[0], jnp.where(flat < 2 * devices, values[1], 0.0))
-    return jnp.where((rows == 0) & (cols == 0), own, 0.0)
+    shape = table_shape(counts)
+    at = rows_of(shape) * 128 + lanes_of(shape) - (i * counts[1] + j)
+    return jnp.where(at == 0, values[0], jnp.where(at == devices, values[1], 0.0))
+
+
+def merged(table, *others):
+    for other in others:
+        table = jnp.where(table != 0.0, table, other)
+    return table
 
 
 def as_row(table, width):
@@ -314,29 +312,13 @@
     return before, after
 
 
-def next_table(index, a, b):
-    return jnp.where(is_even(index), a, b)[24:, :128]
-
-
-def row_tables(index, nr, rows, a, b):
-    even = is_even(index)
-    after = jnp.where(even, a, b)[24:, :128]
-    before = jnp.where(even, b, a)[24:, :128]
-    if nr == 4:
-        return jnp.where(rows == 2, after, 0.0)
-    far = rows % 8
-    return jnp.where(
-        (far == 2) | (far == 5), after, jnp.where((far == 3) | (far == 6), before, 0.0)
-    )
-
-
 def send(index, a_ref, b_ref, before, after):
     even = is_even(index)
     a_ref[...] = jnp.where(even, after, before)
     b_ref[...] = jnp.where(even, before, after)
 
 
-def begin_kernel(counts, both_ref, b_ref, a_ref):
+def begin_kernel(counts, both_ref, b_ref, a_ref, table_ref):
     r, h = both_ref[:TR], both_ref[TR:]
     lane = lanes_of((128, 128))
     packed = jnp.where(
@@ -350,6 +332,7 @@
     )
     turned = packed.T
     table = table_of(core_sums(r), counts)
+    table_ref[...] = table
     send(
         lax.axis_index("col"),
         a_ref,
@@ -359,7 +342,7 @@
     )
 
 
-def widen_kernel(counts, both_ref, gb_ref, ga_ref, r3_ref, h3_ref, b_ref, a_ref, table_ref):
+def widen_kernel(counts, both_ref, own_ref, gb_ref, ga_ref, r3_ref, h3_ref, b_ref, a_ref, table_ref):
     i, j = place()
     from_left, from_right = sides(j, counts[1], ga_ref[:32], gb_ref[:32])
     turned = jnp.concatenate([from_right, jnp.zeros((64, 128), jnp.float32), from_left], axis=0)
@@ -373,7 +356,7 @@
     r3_ref[...] = r3
     h3_ref[...] = h3
     r, h = both_ref[:TR], both_ref[TR:]
-    table = table_of(core_sums(r), counts) + ga_ref[32:] + gb_ref[32:]
+    table = merged(own_ref[...], ga_ref[32:], gb_ref[32:])
     table_ref[...] = table
     wide = jnp.concatenate([table, jnp.zeros((table.shape[0], FC - 128), jnp.float32)], axis=1)
 
@@ -422,29 +405,30 @@
     t = (tile_ref[...] + row_transform(u, basis_ref, halo_rows)) * weights_ref[...]
     t_ref[...] = t
     send(j, a_ref, b_ref, *strips_of(t, basis_ref, 24))
-    table_out[...] = table_ref[...] + ga_ref[24:, :128] + gb_ref[24:, :128]
-
-
-def inverse_kernel(counts, t_ref, basis_ref, both_ref, h3_ref, gb_ref, ga_ref, y_ref, m_ref):
-    y_ref[...] = solution_of(t_ref[...], basis_ref)
+    table_out[...] = merged(table_ref[...], ga_ref[24:, :128], gb_ref[24:, :128])
+
+
+def mobility_kernel(counts, both_ref, h3_ref, gb_ref, ga_ref, table_ref, m_ref, table_out):
     above, below = sides(lax.axis_index("row"), counts[0], ga_ref[8:24], gb_ref[8:24])
     h = jnp.concatenate([both_ref[TR:], h3_ref[...]], axis=1)
     tall = jnp.concatenate([h, below, above], axis=0)
     m_ref[...] = tall * tall * tall
+    table_out[...] = table_ref[...]
+
+
+def inverse_kernel(t_ref, basis_ref, y_ref):
+    y_ref[...] = solution_of(t_ref[...], basis_ref)
 
 
 def columns_kernel(counts, y_ref, *refs):
     i, j = place()
-    (ga_ref, gb_ref), refs = (refs[:2] if len(refs) == 7 else refs[1::-1]), refs[2:]
-    deep = 24 if len(refs) == 5 else 16
+    (ga_ref, gb_ref), refs = (refs[:2] if len(refs) == 8 else refs[1::-1]), refs[2:]
+    deep = 24 if len(refs) == 6 else 16
     y = add_columns(y_ref[...], *sides(j, counts[1], ga_ref[:deep], gb_ref[:deep]))
     strips = pack_rows(y, deep)
-    if len(refs) == 5:
-        table_ref, out_ref, table_out, b_ref, a_ref = refs
-        cols = flat_place(counts)[2]
-        table = table_ref[...] + jnp.where(
-            cols % 4 == 2, next_table(j, ga_ref[...], gb_ref[...]), 0.0
-        )
+    if len(refs) == 6:
+        table_ref, far_ref, out_ref, table_out, b_ref, a_ref = refs
+        table = merged(table_ref[...], far_ref[...], ga_ref[24:, :128], gb_ref[24:, :128])
         table_out[...] = table
         wide = jnp.concatenate([table, jnp.zeros((table.shape[0], FC - 128), jnp.float32)], axis=1)
         strips = [jnp.concatenate([x, wide], axis=0) for x in strips]
@@ -475,8 +459,7 @@
     s = add_rows(y_ref[...], *sides(i, counts[0], ga_ref[:24], gb_ref[:24]))
     mask = grid_mask((FR, FC), counts)
     s = jnp.where(mask, s, 0.0)
-    rows = flat_place(counts)[1]
-    table = table_ref[...] + row_tables(i, counts[0], rows, ga_ref[...], gb_ref[...])
+    table = merged(table_ref[...], ga_ref[24:, :128], gb_ref[24:, :128])
     table_out[...] = table
     c0 = as_row(table, width)
     coarse = spread(coarse_values(c0, coarse_part(basis_ref, width)), counts)
@@ -630,7 +613,7 @@
     return found
 
 
-def near_pairs(counts, axis):
+def near_pairs(counts, axis, bit):
     found = []
     for i in range(counts[0]):
         for j in range(counts[1]):
@@ -638,9 +621,27 @@
             if 0 < at[axis] < counts[axis] - 1:
                 at[axis] += 1 if at[axis] % 2 else -1
             else:
-                at[1 - axis] ^= 1
+                at[1 - axis] ^= bit
             found.append((i * counts[1] + j, at[0] * counts[1] + at[1]))
     return found
+
+
+def xor_pairs(counts, rows, cols):
+    flat = [(i, j) for i in range(counts[0]) for j in range(counts[1])]
+    return [(i * counts[1] + j, (i ^ rows) * counts[1] + (j ^ cols)) for i, j in flat]
+
+
+def spreads(counts):
+    known = np.eye(counts[0] * counts[1], dtype=bool)
+
+    def meet(*swaps):
+        return np.logical_or.reduce([known, *(known[[b for _, b in pairs]] for pairs in swaps)])
+
+    even = [xor_pairs(counts, 0, 1), xor_pairs(counts, 1, 0)]
+    known = meet(even[0], near_pairs(counts, 1, 1))
+    known = meet(even[1], near_pairs(counts, 0, 1), xor_pairs(counts, 4, 0))
+    known = meet(even[0], near_pairs(counts, 1, 2), xor_pairs(counts, 2, 3))
+    return meet(even[1], near_pairs(counts, 0, 1)).all()
 
 
 def body(counts, height, noise):
@@ -651,36 +652,35 @@
     both_axes = ("row", "col")
     depth = table_shape(counts)[0]
 
-    def swap(a, b, axis, wrap=True):
-        count = lax.axis_size(axis)
-        if wrap:
-            gb = lax.ppermute(b, axis, pairs_from(count, 1))
-        else:
-            gb = lax.ppermute(b, both_axes, near_pairs(counts, both_axes.index(axis)))
-        return lax.ppermute(a, axis, pairs_from(count, 0)), gb
-
-    def row_shift(x, step):
-        return lax.ppermute(x, "row", [(k, (k + step) % nr) for k in range(nr)])
+    def swap(a, b, axis, bit=1):
+        gb = lax.ppermute(b, both_axes, near_pairs(counts, both_axes.index(axis), bit))
+        return lax.ppermute(a, axis, pairs_from(lax.axis_size(axis), 0)), gb
+
+    def small_swap(x, rows, cols):
+        return lax.ppermute(x, both_axes, xor_pairs(counts, rows, cols))
 
     both = jnp.pad(noise, ((0, TR), (0, 0))) + jnp.pad(height, ((TR, 0), (0, 0)))
-    b, a = call(functools.partial(begin_kernel, counts), [(32 + depth, 128)] * 2, both)
+    b, a, table = call(
+        functools.partial(begin_kernel, counts), [(32 + depth, 128)] * 2 + [(depth, 128)], both
+    )
+    if not spreads(counts):
+        for axis, count in enumerate(counts):
+            bit = 1
+            while bit < count:
+                table = table + small_swap(table, *((0, bit) if axis else (bit, 0)))
+                bit *= 2
     ga, gb = swap(a, b, "col")
     r3, h3, b, a, table = call(
         functools.partial(widen_kernel, counts),
         [(128, 128)] * 2 + [(24 + depth, FC)] * 2 + [(depth, 128)],
         both,
+        table,
         gb,
         ga,
     )
-    step = nr // 2
-    while step >= 8:
-        table = table + row_shift(table, step)
-        step //= 2
-    if nr > 8:
-        a, b = (x.at[24:, :128].set(table) for x in (a, b))
     ga, gb = swap(a, b, "row")
     weight, table = call(weights_kernel, [(EXT, 2 * SPEC), (depth, 128)], both, table, basis)
-    far = row_shift(table, 4) if nr >= 8 else 0.0
+    far = small_swap(table, 4, 0)
     t = call(forward_kernel, [(EXT, 2 * SPEC)], both, r3, basis)[0]
     t, table, b, a = call(
         functools.partial(first_kernel, counts),
@@ -692,23 +692,20 @@
         basis,
         table,
     )
-    table = table + far
-    step = nc // 2
-    while step >= 4:
-        table = table + lax.ppermute(table, "col", [(k, (k + step) % nc) for k in range(nc)])
-        step //= 2
+    table = merged(table, far)
     wide = jnp.pad(table, ((0, 0), (0, EXT - 128)))
-    y, m = call(
-        functools.partial(inverse_kernel, counts),
-        [(EXT, FC), (FR, FC)],
-        t,
-        basis,
+    m, table_too = call(
+        functools.partial(mobility_kernel, counts),
+        [(FR, FC), (depth, 128)],
         both,
         h3,
         gb,
         ga,
-    )
-    ga, gb = swap(*(jnp.concatenate([x, wide], axis=0) for x in (a, b)), "col")
+        table,
+    )
+    y = call(inverse_kernel, [(EXT, FC)], t, basis)[0]
+    ga, gb = swap(*(jnp.concatenate([x, wide], axis=0) for x in (a, b)), "col", 2)
+    far = small_swap(table_too, 2, 3)
     y, table, b, a = call(
         functools.partial(columns_kernel, counts),
         [(EXT, FC), (depth, 128)] + [(24 + depth, FC)] * 2,
@@ -716,6 +713,7 @@
         ga,
         gb,
         table,
+        far,
     )
     ga, gb = swap(a, b, "row")
     z, w, t, table, b, a = call(
@@ -729,12 +727,12 @@
         weight,
         basis,
     )
-    ga, gb = swap(a, b, "col", False)
+    ga, gb = swap(a, b, "col")
     y, stats = call(inverse_stats_kernel, [(EXT, FC), (1, 128)], t, basis, both, m, z, w)
     y, b, a = call(
         functools.partial(columns_kernel, counts), [(EXT, FC)] + [(16, FC)] * 2, y, gb, ga
     )
-    ga, gb = swap(a, b, "row", False)
+    ga, gb = swap(a, b, "row")
     q, v, stats = call(
         functools.partial(dots_kernel, counts),
         [(TR, TC)] * 2 + [(devices, 128)],

time: 48.3 us -> 49.5 us (1.025)
  starting transfers between devices: 16.9 us -> 20 us
  waiting for transfers between devices: 12.8 us -> 10.2 us
  blocking collectives: 9.19 us -> 9.87 us
    ppermute x13 -> x14, starting transfers between devices: 16.9 us -> 20 us  [the longest x6 8.78 us: swap(): return (lax.ppermute(a, axis, pairs_from(lax.axis_size(axis), 0)), gb)]
    ppermute x13 -> x14, waiting for transfers between devices: 12.8 us -> 10.2 us  [the longest x6 4.5 us: swap(): lax.ppermute(b, both_axes, near_pairs(counts, both_axes.index(axis), bit))]
    all_to_all x1, blocking collectives: 9.19 us -> 9.87 us  [body(): stats = lax.all_to_all(stats, both_axes, 0, 0, tiled=True)]
    pallas_call x12 -> x13, Pallas kernels: 7.56 us -> 7.56 us  [call(): pl.pallas_call(kernel, out_shape=shapes, compiler_params=pltpu.CompilerPa...]
  transfers between devices with their start and end apart: 13 -> 14, of which waited for: 8 -> 6; matrix products, arithmetic and copies ran while one was open for 0% -> 0% of each run, Pallas kernels for 7% -> 7%
where the time goes in v10:
time: 49.5 us; the launch traced here: 49.4 us
  starting transfers between devices  20 us (40%)
  waiting for transfers between devices  10.2 us (21%)
  blocking collectives  9.87 us (20%)
  Pallas kernels  7.56 us (15%)
  other arithmetic  1 us (2%)
  between operations  0.75 us (2%)
    all_to_all x1, blocking collectives, body(): stats = lax.all_to_all(stats, both_axes, 0, 0, tiled=True)  9.87 us
    ppermute x6, starting transfers between devices, swap(): return (lax.ppermute(a, axis, pairs_from(lax.axis_size(axis), 0)), gb)  8.78 us
    pallas_call x13, Pallas kernels, call(): pl.pallas_call(kernel, out_shape=shapes, compiler_params=pltpu.CompilerPa...  7.56 us
    ppermute x6, starting transfers between devices, swap(): lax.ppermute(b, both_axes, near_pairs(counts, both_axes.index(axis), bit))  6.14 us
    ppermute x2, starting transfers between devices, small_swap(): return lax.ppermute(x, both_axes, xor_pairs(counts, rows, cols))  5.1 us
    ppermute x6, waiting for transfers between devices, swap(): lax.ppermute(b, both_axes, near_pairs(counts, both_axes.index(axis), bit))  4.5 us
    ppermute x6, waiting for transfers between devices, swap(): return (lax.ppermute(a, axis, pairs_from(lax.axis_size(axis), 0)), gb)  3.15 us
    ppermute x2, waiting for transfers between devices, small_swap(): return lax.ppermute(x, both_axes, xor_pairs(counts, rows, cols))  2.52 us
  transfers between devices with their start and end apart: 14, of which 6 were waited for; matrix products, arithmetic and copies ran while one was open for 0% of the time, Pallas kernels for 7%

profile of v10, /device:TPU:0, one launch (start us, length us, event | category | flops | bytes accessed | tf_op | source)
XLA Modules:
  0.0 49.4 jit_solution(1996490587232968635)
XLA Ops:
  0.6 1.0 %pad_add_fusion.both_ref = f32[256,256]{1,0:T(8,128)S(1)} fusion(f32[128,256]{1,0:T(8,128)} %param.3, f32[128,256]{1,0:T(8,128)} %param.4), kind=kLoop, calls=%fused_computation | loop fusion | flops 65536 | bytes 524288 | tf_op jit(solution)/shard_map/add | solution.py:662
  1.6 0.2 shard_map.50
  1.8 0.0 copy-start
  1.8 0.5 %collective-permute-start = (f32[40,128]{1,0:T(8,128)S(1)}, f32[40,128]{1,0:T(8,128)S(1)}, u32[]{:S(2)}, u32[]{:S(2)}) collective-permute-start(f32[40,128]{1,0:T(8,128)S(1)} %get-tuple-element.37), channel_id=1, source_target_pairs={{0,4},{1,2},{2,1},{3,7},{4,0},{5,6},{6,5},{7,3},{8,12},{9,10},{10,... | collective-permute-start | bytes 61448 | tf_op jit(solution)/shard_map/ppermute | solution.py:656
  2.3 4.0 %collective-permute-start.1 = (f32[40,128]{1,0:T(8,128)S(1)}, f32[40,128]{1,0:T(8,128)S(1)}, u32[]{:S(2)}, u32[]{:S(2)}) collective-permute-start(f32[40,128]{1,0:T(8,128)S(1)} %get-tuple-element.38), channel_id=1, source_target_pairs={{0,1},{1,0},{2,3},{3,2},{4,5},{5,4},{6,7},{7,6},{8,9},{9,8},{10,11... | collective-permute-start | bytes 61448 | tf_op jit(solution)/shard_map/ppermute | solution.py:657
  6.3 0.0 collective-permute-done.gb_ref
  6.3 2.0 %collective-permute-done.1.ga_ref = f32[40,128]{1,0:T(8,128)S(1)} collective-permute-done((f32[40,128]{1,0:T(8,128)S(1)}, f32[40,128]{1,0:T(8,128)S(1)}, u32[]{:S(2)}, u32[]{:S(2)}) %collective-permute-start.1) | collective-permute-done | bytes 20512 | tf_op jit(solution)/shard_map/ppermute | solution.py:657
  8.3 0.2 shard_map.51
  8.5 1.9 %collective-permute-start.2 = (f32[32,384]{1,0:T(8,128)S(1)}, f32[32,384]{1,0:T(8,128)S(1)}, u32[]{:S(2)}, u32[]{:S(2)}) collective-permute-start(f32[32,384]{1,0:T(8,128)S(1)} %get-tuple-element.39), channel_id=1, source_target_pairs={{0,1},{1,0},{2,3},{3,2},{4,8},{5,9},{6,10},{7,11},{8,4},{9,5},{10,... | collective-permute-start | bytes 147464 | tf_op jit(solution)/shard_map/ppermute | solution.py:656
  10.3 0.0 collective-permute-start.3
  10.3 0.0 copy-done
  10.4 0.1 shard_map.53
  10.5 2.5 %collective-permute-start.4 = (f32[8,128]{1,0:T(8,128)S(1)}, f32[8,128]{1,0:T(8,128)S(1)}, u32[]{:S(2)}, u32[]{:S(2)}) collective-permute-start(f32[8,128]{1,0:T(8,128)S(1)} %get-tuple-element.44.table_ref), channel_id=1, source_target_pairs={{0,16},{1,17},{2,18},{3,19},{4,20},{5,21},{6,22},{7,23},{8,24},{9,... | collective-permute-start | bytes 12296 | tf_op jit(solution)/shard_map/ppermute | solution.py:660
  13.0 0.6 %shard_map.52.tile_ref = f32[144,512]{1,0:T(8,128)S(1)} custom-call(f32[256,256]{1,0:T(8,128)S(1)} %pad_add_fusion.both_ref, f32[128,128]{1,0:T(8,128)S(1)} %get-tuple-element.41.r3_ref, f32[1104,512]{1,0:T(8,128)S(1)} %copy-done), custom_call_target="tpu_custom_call" | custom-call | flops 1000000000 | bytes 1000000 | tf_op jit(solution)/shard_map/pallas_call | solution.py:601
  13.6 0.0 collective-permute-done.2.gb_ref
  13.6 0.0 collective-permute-done.3.ga_ref
  13.6 1.0 %shard_map.54 = (f32[144,512]{1,0:T(8,128)S(1)}, f32[8,128]{1,0:T(8,128)S(1)}, f32[24,144]{1,0:T(8,128)S(1)}, f32[24,144]{1,0:T(8,128)S(1)}) custom-call(f32[32,384]{1,0:T(8,128)S(1)} %collective-permute-done.2.gb_ref, f32[32,384]{1,0:T(8,128)S(1)} %collective-permute-done.3.ga_ref, f32[144,512]{1,0:T(8,128)S(1)} %shard_map.52.tile_ref, ...), custom_call_target="tpu_custom_call" | custom-call | flops 1000000000 | bytes 1000000 | tf_op jit(solution)/shard_map/pallas_call | solution.py:601
  14.6 0.4 collective-permute-done.4
  15.1 1.5 %collective-permute-start.6 = (f32[32,144]{1,0:T(8,128)S(1)}, f32[32,144]{1,0:T(8,128)S(1)}, u32[]{:S(2)}, u32[]{:S(2)}) collective-permute-start(f32[32,144]{1,0:T(8,128)S(1)} %get-tuple-element.70), channel_id=1, source_target_pairs={{0,8},{1,2},{2,1},{3,11},{4,12},{5,6},{6,5},{7,15},{8,0},{9,10},{1... | collective-permute-start | bytes 55304 | tf_op jit(solution)/shard_map/ppermute | solution.py:656
  16.6 1.7 %collective-permute-start.5 = (f32[32,144]{1,0:T(8,128)S(1)}, f32[32,144]{1,0:T(8,128)S(1)}, u32[]{:S(2)}, u32[]{:S(2)}) collective-permute-start(f32[32,144]{1,0:T(8,128)S(1)} %get-tuple-element.71), channel_id=1, source_target_pairs={{0,1},{1,0},{2,3},{3,2},{4,5},{5,4},{6,7},{7,6},{8,9},{9,8},{10,11... | collective-permute-start | bytes 55304 | tf_op jit(solution)/shard_map/ppermute | solution.py:657
  18.3 2.6 %collective-permute-start.7 = (f32[8,128]{1,0:T(8,128)S(1)}, f32[8,128]{1,0:T(8,128)S(1)}, u32[]{:S(2)}, u32[]{:S(2)}) collective-permute-start(f32[8,128]{1,0:T(8,128)S(1)} %get-tuple-element.50), channel_id=1, source_target_pairs={{0,11},{1,10},{2,9},{3,8},{4,15},{5,14},{6,13},{7,12},{8,3},{9,2},... | collective-permute-start | bytes 12296 | tf_op jit(solution)/shard_map/ppermute | solution.py:660
  20.9 0.8 %shard_map.55.y_ref = f32[144,384]{1,0:T(8,128)S(1)} custom-call(f32[144,512]{1,0:T(8,128)S(1)} %get-tuple-element.45.t_ref, f32[1104,512]{1,0:T(8,128)S(1)} %copy-done), custom_call_target="tpu_custom_call" | custom-call | flops 1000000000 | bytes 1000000 | tf_op jit(solution)/shard_map/pallas_call | solution.py:601
  21.7 2.1 %collective-permute-done.7.refs_3_ = f32[8,128]{1,0:T(8,128)S(1)} collective-permute-done((f32[8,128]{1,0:T(8,128)S(1)}, f32[8,128]{1,0:T(8,128)S(1)}, u32[]{:S(2)}, u32[]{:S(2)}) %collective-permute-start.7) | collective-permute-done | bytes 4128 | tf_op jit(solution)/shard_map/ppermute | solution.py:660
  23.8 0.0 collective-permute-done.6.refs_1_
  23.8 0.0 collective-permute-done.5.refs_0_
  23.8 0.2 shard_map.57
  24.0 0.4 collective-permute-start.8
  24.4 1.3 %collective-permute-start.9 = (f32[32,384]{1,0:T(8,128)S(1)}, f32[32,384]{1,0:T(8,128)S(1)}, u32[]{:S(2)}, u32[]{:S(2)}) collective-permute-start(f32[32,384]{1,0:T(8,128)S(1)} %get-tuple-element.54), channel_id=1, source_target_pairs={{0,4},{4,0},{8,12},{12,8},{16,20},{20,16},{24,28},{28,24},{1,5},{5... | collective-permute-start | bytes 147464 | tf_op jit(solution)/shard_map/ppermute | solution.py:657
  25.7 2.4 %collective-permute-done.8.gb_ref = f32[32,384]{1,0:T(8,128)S(1)} collective-permute-done((f32[32,384]{1,0:T(8,128)S(1)}, f32[32,384]{1,0:T(8,128)S(1)}, u32[]{:S(2)}, u32[]{:S(2)}) %collective-permute-start.8) | collective-permute-done | bytes 49184 | tf_op jit(solution)/shard_map/ppermute | solution.py:656
  28.1 0.0 collective-permute-done.9.ga_ref
  28.1 1.7 %shard_map.58 = (f32[128,256]{1,0:T(8,128)S(1)}, f32[128,256]{1,0:T(8,128)S(1)}, f32[144,512]{1,0:T(8,128)S(1)}, f32[8,128]{1,0:T(8,128)S(1)}, f32[16,144]{1,0:T(8,128)S(1)}, /*index=5*/f32[16,144]{1,0:T(8,128)S(1)}) custom-call(f32[144,384]{1,0:T(8,128)S(1)} %get-tuple-element.51.y_ref, f32[160,384]{1,0:T(8,128)S(1)} %get-tuple-element.52.m_ref, ...), custom_call_target="tpu_custom_call" | custom-call | flops 1000000000 | bytes 1000000 | tf_op jit(solution)/shard_map/pallas_call | solution.py:601
  29.8 0.0 collective-permute-start.10
  29.8 1.8 %collective-permute-start.11 = (f32[16,144]{1,0:T(8,128)S(1)}, f32[16,144]{1,0:T(8,128)S(1)}, u32[]{:S(2)}, u32[]{:S(2)}) collective-permute-start(f32[16,144]{1,0:T(8,128)S(1)} %get-tuple-element.61), channel_id=1, source_target_pairs={{0,1},{1,0},{2,3},{3,2},{4,5},{5,4},{6,7},{7,6},{8,9},{9,8},{10,11... | collective-permute-start | bytes 27656 | tf_op jit(solution)/shard_map/ppermute | solution.py:657
  31.6 0.8 %shard_map.59 = (f32[144,384]{1,0:T(8,128)S(1)}, f32[1,128]{1,0:T(1,128)S(1)}) custom-call(f32[144,512]{1,0:T(8,128)S(1)} %get-tuple-element.56.t_ref, f32[1104,512]{1,0:T(8,128)S(1)} %copy-done, f32[256,256]{1,0:T(8,128)S(1)} %pad_add_fusion.both_ref, f32[160,384]{1,0:T(8,128)S(1)} %get-tuple-element.52.m_ref, f32[128,256]{1,0:T(8,128)S(1)} %get-tuple-element.57.z_ref, ...), custom_call_target="tpu_custom_call" | custom-call | flops 1000000000 | bytes 1000000 | tf_op jit(solution)/shard_map/pallas_call | solution.py:601
  32.4 0.0 collective-permute-done.10.refs_0_
  32.4 1.2 %collective-permute-done.11.refs_1_ = f32[16,144]{1,0:T(8,128)S(1)} collective-permute-done((f32[16,144]{1,0:T(8,128)S(1)}, f32[16,144]{1,0:T(8,128)S(1)}, u32[]{:S(2)}, u32[]{:S(2)}) %collective-permute-start.11) | collective-permute-done | bytes 9248 | tf_op jit(solution)/shard_map/ppermute | solution.py:657
  33.6 0.2 shard_map.60
  33.8 1.8 %collective-permute-start.12 = (f32[16,384]{1,0:T(8,128)S(1)}, f32[16,384]{1,0:T(8,128)S(1)}, u32[]{:S(2)}, u32[]{:S(2)}) collective-permute-start(f32[16,384]{1,0:T(8,128)S(1)} %get-tuple-element.63), channel_id=1, source_target_pairs={{0,1},{1,0},{2,3},{3,2},{4,8},{5,9},{6,10},{7,11},{8,4},{9,5},{10,... | collective-permute-start | bytes 73736 | tf_op jit(solution)/shard_map/ppermute | solution.py:656
  35.6 0.0 collective-permute-start.13
  35.6 2.1 %collective-permute-done.12.gb_ref = f32[16,384]{1,0:T(8,128)S(1)} collective-permute-done((f32[16,384]{1,0:T(8,128)S(1)}, f32[16,384]{1,0:T(8,128)S(1)}, u32[]{:S(2)}, u32[]{:S(2)}) %collective-permute-start.12) | collective-permute-done | bytes 24608 | tf_op jit(solution)/shard_map/ppermute | solution.py:656
  37.7 0.0 collective-permute-done.13.ga_ref
  37.7 0.4 shard_map.61
  38.1 9.9 %all_to_all.11 = f32[32,1,128]{2,1,0:T(1,128)S(1)} all-to-all(f32[32,1,128]{2,1,0:T(1,128)S(1)} %bitcast.5), channel_id=1, replica_groups=mesh['row'=8,'col'=4] {'row','col'}, dimensions={0} | all-to-all | bytes 32768 | tf_op jit(solution)/shard_map/all_to_all | solution.py:747
  48.0 1.4 %shard_map.62 = (f32[128,256]{1,0:T(8,128)}, f32[128,256]{1,0:T(8,128)}) custom-call(f32[32,128]{1,0:T(8,128)S(1)} %bitcast.4, f32[8,128]{1,0:T(8,128)S(1)} %get-tuple-element.67.table_ref, f32[1104,512]{1,0:T(8,128)S(1)} %copy-done, f32[160,384]{1,0:T(8,128)S(1)} %get-tuple-element.52.m_ref, f32[256,256]{1,0:T(8,128)S(1)} %pad_add_fusion.both_ref, ...), custom_call_target="tpu_custom_call" | custom-call | flops 1000000000 | bytes 1000000 | tf_op jit(solution)/shard_map/pallas_call | solution.py:601
  (3 shorter events, 0.0 us)
Async XLA Ops:
  1.8 8.6 %copy-start = (f32[1104,512]{1,0:T(8,128)S(1)}, f32[1104,512]{1,0:T(8,128)}, u32[]{:S(2)}) copy-start(f32[1104,512]{1,0:T(8,128)} %constant.6.clone.basis_ref) | copy-start | bytes 6782980
  1.8 4.5 %collective-permute-start = (f32[40,128]{1,0:T(8,128)S(1)}, f32[40,128]{1,0:T(8,128)S(1)}, u32[]{:S(2)}, u32[]{:S(2)}) collective-permute-start(f32[40,128]{1,0:T(8,128)S(1)} %get-tuple-element.37), channel_id=1, source_target_pairs={{0,4},{1,2},{2,1},{3,7},{4,0},{5,6},{6,5},{7,3},{8,12},{9,10},{10,... | collective-permute-start | bytes 61448 | tf_op jit(solution)/shard_map/ppermute | solution.py:656
  2.3 6.0 %collective-permute-start.1 = (f32[40,128]{1,0:T(8,128)S(1)}, f32[40,128]{1,0:T(8,128)S(1)}, u32[]{:S(2)}, u32[]{:S(2)}) collective-permute-start(f32[40,128]{1,0:T(8,128)S(1)} %get-tuple-element.38), channel_id=1, source_target_pairs={{0,1},{1,0},{2,3},{3,2},{4,5},{5,4},{6,7},{7,6},{8,9},{9,8},{10,11... | collective-permute-start | bytes 61448 | tf_op jit(solution)/shard_map/ppermute | solution.py:657
  8.5 5.1 %collective-permute-start.2 = (f32[32,384]{1,0:T(8,128)S(1)}, f32[32,384]{1,0:T(8,128)S(1)}, u32[]{:S(2)}, u32[]{:S(2)}) collective-permute-start(f32[32,384]{1,0:T(8,128)S(1)} %get-tuple-element.39), channel_id=1, source_target_pairs={{0,1},{1,0},{2,3},{3,2},{4,8},{5,9},{6,10},{7,11},{8,4},{9,5},{10,... | collective-permute-start | bytes 147464 | tf_op jit(solution)/shard_map/ppermute | solution.py:656
  10.3 3.3 %collective-permute-start.3 = (f32[32,384]{1,0:T(8,128)S(1)}, f32[32,384]{1,0:T(8,128)S(1)}, u32[]{:S(2)}, u32[]{:S(2)}) collective-permute-start(f32[32,384]{1,0:T(8,128)S(1)} %get-tuple-element.40), channel_id=1, source_target_pairs={{0,4},{4,0},{8,12},{12,8},{16,20},{20,16},{24,28},{28,24},{1,5},{5... | collective-permute-start | bytes 147464 | tf_op jit(solution)/shard_map/ppermute | solution.py:657
  10.5 4.6 %collective-permute-start.4 = (f32[8,128]{1,0:T(8,128)S(1)}, f32[8,128]{1,0:T(8,128)S(1)}, u32[]{:S(2)}, u32[]{:S(2)}) collective-permute-start(f32[8,128]{1,0:T(8,128)S(1)} %get-tuple-element.44.table_ref), channel_id=1, source_target_pairs={{0,16},{1,17},{2,18},{3,19},{4,20},{5,21},{6,22},{7,23},{8,24},{9,... | collective-permute-start | bytes 12296 | tf_op jit(solution)/shard_map/ppermute | solution.py:660
  15.1 8.7 %collective-permute-start.6 = (f32[32,144]{1,0:T(8,128)S(1)}, f32[32,144]{1,0:T(8,128)S(1)}, u32[]{:S(2)}, u32[]{:S(2)}) collective-permute-start(f32[32,144]{1,0:T(8,128)S(1)} %get-tuple-element.70), channel_id=1, source_target_pairs={{0,8},{1,2},{2,1},{3,11},{4,12},{5,6},{6,5},{7,15},{8,0},{9,10},{1... | collective-permute-start | bytes 55304 | tf_op jit(solution)/shard_map/ppermute | solution.py:656
  16.6 7.2 %collective-permute-start.5 = (f32[32,144]{1,0:T(8,128)S(1)}, f32[32,144]{1,0:T(8,128)S(1)}, u32[]{:S(2)}, u32[]{:S(2)}) collective-permute-start(f32[32,144]{1,0:T(8,128)S(1)} %get-tuple-element.71), channel_id=1, source_target_pairs={{0,1},{1,0},{2,3},{3,2},{4,5},{5,4},{6,7},{7,6},{8,9},{9,8},{10,11... | collective-permute-start | bytes 55304 | tf_op jit(solution)/shard_map/ppermute | solution.py:657
  18.3 5.5 %collective-permute-start.7 = (f32[8,128]{1,0:T(8,128)S(1)}, f32[8,128]{1,0:T(8,128)S(1)}, u32[]{:S(2)}, u32[]{:S(2)}) collective-permute-start(f32[8,128]{1,0:T(8,128)S(1)} %get-tuple-element.50), channel_id=1, source_target_pairs={{0,11},{1,10},{2,9},{3,8},{4,15},{5,14},{6,13},{7,12},{8,3},{9,2},... | collective-permute-start | bytes 12296 | tf_op jit(solution)/shard_map/ppermute | solution.py:660
  24.0 4.2 %collective-permute-start.8 = (f32[32,384]{1,0:T(8,128)S(1)}, f32[32,384]{1,0:T(8,128)S(1)}, u32[]{:S(2)}, u32[]{:S(2)}) collective-permute-start(f32[32,384]{1,0:T(8,128)S(1)} %get-tuple-element.53), channel_id=1, source_target_pairs={{0,1},{1,0},{2,3},{3,2},{4,8},{5,9},{6,10},{7,11},{8,4},{9,5},{10,... | collective-permute-start | bytes 147464 | tf_op jit(solution)/shard_map/ppermute | solution.py:656
  24.4 3.7 %collective-permute-start.9 = (f32[32,384]{1,0:T(8,128)S(1)}, f32[32,384]{1,0:T(8,128)S(1)}, u32[]{:S(2)}, u32[]{:S(2)}) collective-permute-start(f32[32,384]{1,0:T(8,128)S(1)} %get-tuple-element.54), channel_id=1, source_target_pairs={{0,4},{4,0},{8,12},{12,8},{16,20},{20,16},{24,28},{28,24},{1,5},{5... | collective-permute-start | bytes 147464 | tf_op jit(solution)/shard_map/ppermute | solution.py:657
  29.8 2.6 %collective-permute-start.10 = (f32[16,144]{1,0:T(8,128)S(1)}, f32[16,144]{1,0:T(8,128)S(1)}, u32[]{:S(2)}, u32[]{:S(2)}) collective-permute-start(f32[16,144]{1,0:T(8,128)S(1)} %get-tuple-element.60), channel_id=1, source_target_pairs={{0,4},{1,2},{2,1},{3,7},{4,0},{5,6},{6,5},{7,3},{8,12},{9,10},{10,... | collective-permute-start | bytes 27656 | tf_op jit(solution)/shard_map/ppermute | solution.py:656
  29.8 3.8 %collective-permute-start.11 = (f32[16,144]{1,0:T(8,128)S(1)}, f32[16,144]{1,0:T(8,128)S(1)}, u32[]{:S(2)}, u32[]{:S(2)}) collective-permute-start(f32[16,144]{1,0:T(8,128)S(1)} %get-tuple-element.61), channel_id=1, source_target_pairs={{0,1},{1,0},{2,3},{3,2},{4,5},{5,4},{6,7},{7,6},{8,9},{9,8},{10,11... | collective-permute-start | bytes 27656 | tf_op jit(solution)/shard_map/ppermute | solution.py:657
  33.8 3.9 %collective-permute-start.12 = (f32[16,384]{1,0:T(8,128)S(1)}, f32[16,384]{1,0:T(8,128)S(1)}, u32[]{:S(2)}, u32[]{:S(2)}) collective-permute-start(f32[16,384]{1,0:T(8,128)S(1)} %get-tuple-element.63), channel_id=1, source_target_pairs={{0,1},{1,0},{2,3},{3,2},{4,8},{5,9},{6,10},{7,11},{8,4},{9,5},{10,... | collective-permute-start | bytes 73736 | tf_op jit(solution)/shard_map/ppermute | solution.py:656
  35.6 2.1 %collective-permute-start.13 = (f32[16,384]{1,0:T(8,128)S(1)}, f32[16,384]{1,0:T(8,128)S(1)}, u32[]{:S(2)}, u32[]{:S(2)}) collective-permute-start(f32[16,384]{1,0:T(8,128)S(1)} %get-tuple-element.64), channel_id=1, source_target_pairs={{0,4},{4,0},{8,12},{12,8},{16,20},{20,16},{24,28},{28,24},{1,5},{5... | collective-permute-start | bytes 73736 | tf_op jit(solution)/shard_map/ppermute | solution.py:657

commit v11 on v10

--- a/solution.py
+++ b/solution.py
@@ -38,8 +38,11 @@
     low = (rows.T - high).astype(ml_dtypes.bfloat16).astype(np.float64)
     tile = np.concatenate([x[:, :SUB] for x in (high, high, low)], 1)
     halo = np.concatenate([x[:, SUB:] for x in (high, high, low)], 1)
-    whole = np.concatenate([high, high, low], 1)
-    return [np.tile(scale, (1, 2)), *(wide(x) for x in (rows, rows.T, cols, whole, np.hstack([tile, halo])))]
+    inner = np.concatenate([x[:, 16:112] for x in (high, high, low)], 1)
+    at = [*range(136, 144), *range(16), *range(112, 136)]
+    edge = np.concatenate([x[:, at] for x in (high, high, low)], 1)
+    turned = np.hstack([rows.T, np.zeros((EXT, 256 - EXT)), edge])
+    return [np.tile(scale, (1, 2)), *(wide(x) for x in (rows, turned, cols, inner, np.hstack([tile, halo])))]
 
 
 def rows_part(ref):
@@ -47,16 +50,20 @@
 
 
 def rows_t_part(ref):
-    return ref[2 * EXT : 3 * EXT, :EXT]
+    return ref[2 * EXT : 3 * EXT, :256]
 
 
 def cols_part(ref):
     return ref[3 * EXT : 3 * EXT + SPEC, :SPEC]
 
 
-def whole_rows(ref):
+def inner_rows(ref):
     at = 3 * EXT + SPEC
-    return ref[at : at + EXT, : 3 * EXT]
+    return ref[at : at + EXT, : 3 * 96]
+
+
+def edge_rows(ref):
+    return ref[2 * EXT : 3 * EXT, 256 : 256 + 3 * 48]
 
 
 def tile_rows(ref):
@@ -127,14 +134,20 @@
     return lax.rem(index, 2) == 0
 
 
-def grid_mask(shape, counts):
-    i, j = place()
-    rr, ll = rows_of(shape), lanes_of(shape)
-    below = jnp.where(i < counts[0] - 1, 144, 128)
-    above = jnp.where(i > 0, 144, 160)
+def column_mask(counts):
+    j = lax.axis_index("col")
+    lane = lanes_of((1, FC))
     right = jnp.where(j < counts[1] - 1, 320, 256)
     left = jnp.where(j > 0, 320, 384)
-    return ((rr < below) | (rr >= above)) & ((ll < right) | (ll >= left))
+    return (lane < right) | (lane >= left)
+
+
+def edge_mask(counts):
+    i = lax.axis_index("row")
+    row = rows_of((80, 1))
+    first = jnp.where(i > 0, 0, 16)
+    last = jnp.where(i < counts[0] - 1, 80, 64)
+    return (row >= first) & (row < last) & column_mask(counts)
 
 
 def table_shape(counts):
@@ -180,7 +193,7 @@
     return dot(jnp.broadcast_to(c_row, (8, c_row.shape[1])), inverse)[:1]
 
 
-def spread(g_row, counts):
+def band_rows(g_row, counts):
     i, j = place()
     nr, nc = counts[0], 2 * counts[1]
     shape = (16, g_row.shape[1])
@@ -191,28 +204,46 @@
     at = lax.rem(c + 2, 2) * (nr * counts[1]) + r * counts[1] + (c + 2) // 2 - 1
     picked = jnp.where(inside & (lanes_of(shape) == at), g_row, 0.0)
     picked = jnp.sum(picked, axis=1, keepdims=True)
-    lane = lanes_of((1, 128))
+    lane = lanes_of((1, FC))
     bands = []
     for d in range(3):
         left, first, second, right = (picked[4 * d + k : 4 * d + k + 1] for k in range(4))
         bands.append(
-            jnp.concatenate(
-                [
-                    jnp.broadcast_to(first, (1, 128)),
-                    jnp.broadcast_to(second, (1, 128)),
-                    jnp.where(lane < 64, right, left),
-                ],
-                axis=1,
+            jnp.where(
+                lane < 128,
+                first,
+                jnp.where(lane < 256, second, jnp.where(lane < 320, right, left)),
             )
         )
+    return bands
+
+
+def edge_bands(bands):
+    above, on, below = bands
     return jnp.concatenate(
         [
-            jnp.broadcast_to(bands[1], (128, FC)),
-            jnp.broadcast_to(bands[2], (16, FC)),
-            jnp.broadcast_to(bands[0], (16, FC)),
+            jnp.broadcast_to(above, (16, FC)),
+            jnp.broadcast_to(on, (48, FC)),
+            jnp.broadcast_to(below, (16, FC)),
         ],
         axis=0,
     )
+
+
+def jumps(row):
+    step = row - pltpu.roll(row, 1, 1)
+    lane = lanes_of((1, FC))
+    at = [jnp.sum(jnp.where(lane == k, step, 0.0), axis=1, keepdims=True) for k in (0, 128, 256)]
+    return jnp.where(
+        (lane < 64) | (lane >= 320), at[0], jnp.where(lane < 192, at[1], at[2])
+    )
+
+
+def edge_steps():
+    lane = lanes_of((1, FC))
+    up = (lane == 0) | (lane == 128) | (lane == 256)
+    down = (lane == FC - 1) | (lane == 127) | (lane == 255)
+    return jnp.where(up, 1.0, jnp.where(down, -1.0, 0.0))
 
 
 def halves_of(x):
@@ -252,7 +283,7 @@
     cols = cols_part(basis_ref)
     left = dot(cols[:deep], t[:, :SPEC], 1)
     right = dot(cols[EXT - deep : EXT], t[:, SPEC:], 1)
-    both = dot(jnp.concatenate([left, right], axis=0), rows_t_part(basis_ref))
+    both = dot(jnp.concatenate([left, right], axis=0), rows_t_part(basis_ref)[:, :EXT])
     return both[:deep], both[deep:]
 
 
@@ -289,20 +320,29 @@
     return jnp.concatenate([y[136:], y[: deep - 8]], axis=0), y[136 - deep : 136]
 
 
-def add_rows(y, from_above, from_below):
+def edges(y, from_above, from_below):
     far = from_above.shape[0] - OV
     none = jnp.zeros((8, FC), jnp.float32)
     return jnp.concatenate(
         [
+            from_above[:8] if far == 16 else none,
+            y[136:] + from_above[far - 8 : far],
             y[:8] + from_above[far:],
-            y[8:120],
+            y[8:24],
+            y[104:120],
             y[120:136] + from_below[:16],
             from_below[16:] if far == 16 else none,
-            from_above[:8] if far == 16 else none,
-            y[136:] + from_above[far - 8 : far],
         ],
         axis=0,
     )
+
+
+def edge_part(frame):
+    return jnp.concatenate([frame[144:], frame[:24], frame[104:144]], axis=0)
+
+
+def with_edges(edge, inner):
+    return jnp.concatenate([edge[16:32, :TC], inner, edge[48:64, :TC]], axis=0)
 
 
 def sides(index, count, a, b):
@@ -408,27 +448,26 @@
     table_out[...] = merged(table_ref[...], ga_ref[24:, :128], gb_ref[24:, :128])
 
 
-def mobility_kernel(counts, both_ref, h3_ref, gb_ref, ga_ref, table_ref, m_ref, table_out):
+def mobility_kernel(counts, both_ref, h3_ref, gb_ref, ga_ref, m_ref):
     above, below = sides(lax.axis_index("row"), counts[0], ga_ref[8:24], gb_ref[8:24])
     h = jnp.concatenate([both_ref[TR:], h3_ref[...]], axis=1)
     tall = jnp.concatenate([h, below, above], axis=0)
     m_ref[...] = tall * tall * tall
-    table_out[...] = table_ref[...]
-
-
-def inverse_kernel(t_ref, basis_ref, y_ref):
+
+
+def inverse_kernel(t_ref, basis_ref, table_ref, y_ref):
     y_ref[...] = solution_of(t_ref[...], basis_ref)
 
 
 def columns_kernel(counts, y_ref, *refs):
     i, j = place()
-    (ga_ref, gb_ref), refs = (refs[:2] if len(refs) == 8 else refs[1::-1]), refs[2:]
-    deep = 24 if len(refs) == 6 else 16
+    (ga_ref, gb_ref), refs = (refs[:2] if len(refs) == 7 else refs[1::-1]), refs[2:]
+    deep = 24 if len(refs) == 5 else 16
     y = add_columns(y_ref[...], *sides(j, counts[1], ga_ref[:deep], gb_ref[:deep]))
     strips = pack_rows(y, deep)
-    if len(refs) == 6:
-        table_ref, far_ref, out_ref, table_out, b_ref, a_ref = refs
-        table = merged(table_ref[...], far_ref[...], ga_ref[24:, :128], gb_ref[24:, :128])
+    if len(refs) == 5:
+        table_ref, out_ref, table_out, b_ref, a_ref = refs
+        table = merged(table_ref[...], ga_ref[24:, :128], gb_ref[24:, :128])
         table_out[...] = table
         wide = jnp.concatenate([table, jnp.zeros((table.shape[0], FC - 128), jnp.float32)], axis=1)
         strips = [jnp.concatenate([x, wide], axis=0) for x in strips]
@@ -436,6 +475,23 @@
         out_ref, b_ref, a_ref = refs
     out_ref[...] = y
     send(i, a_ref, b_ref, *strips)
+
+
+def inner_kernel(
+    counts, y_ref, m_ref, basis_ref, table_ref, w_ref, f_ref, gw_ref, gf_ref, table_out
+):
+    mask = column_mask(counts)
+    s = jnp.where(mask, y_ref[8:120], 0.0)
+    m = m_ref[8:120]
+    w = DAMP * s + lap(m * lap(s))
+    w = jnp.where(mask, w[8:104], 0.0) * SHRINK
+    f = lap(m * edge_steps())
+    f = jnp.where(mask, f[8:104], 0.0) * SHRINK
+    w_ref[...] = w[:, :TC]
+    f_ref[...] = f[:, :TC]
+    gw_ref[...] = row_transform(w, basis_ref, inner_rows)
+    gf_ref[...] = row_transform(f, basis_ref, inner_rows)
+    table_out[...] = table_ref[...]
 
 
 def second_kernel(
@@ -446,6 +502,11 @@
     gb_ref,
     ga_ref,
     table_ref,
+    far_ref,
+    inner_w_ref,
+    f_ref,
+    gw_ref,
+    gf_ref,
     weights_ref,
     basis_ref,
     z_ref,
@@ -456,21 +517,29 @@
     a_ref,
 ):
     i, j = place()
-    s = add_rows(y_ref[...], *sides(i, counts[0], ga_ref[:24], gb_ref[:24]))
-    mask = grid_mask((FR, FC), counts)
+    y = y_ref[...]
+    mask = edge_mask(counts)
+    s = edges(y, *sides(i, counts[0], ga_ref[:24], gb_ref[:24]))
     s = jnp.where(mask, s, 0.0)
-    table = merged(table_ref[...], ga_ref[24:, :128], gb_ref[24:, :128])
+    table = merged(table_ref[...], far_ref[...], ga_ref[24:, :128], gb_ref[24:, :128])
     table_out[...] = table
-    c0 = as_row(table, width)
-    coarse = spread(coarse_values(c0, coarse_part(basis_ref, width)), counts)
-    mobility = m_ref[...]
-    flow = mobility * (lap(s) + lap(coarse))
+    g = coarse_values(as_row(table, width), coarse_part(basis_ref, width))
+    bands = band_rows(g, counts)
+    coarse = edge_bands(bands)
+    m = edge_part(m_ref)
+    flow = m * (lap(s) + lap(coarse))
     z = s + coarse
     w = jnp.where(mask, DAMP * z + lap(flow), 0.0) * SHRINK
-    z_ref[...] = z[:128, :256]
-    w_ref[...] = w[:128, :256]
-    u = column_transform(jnp.concatenate([w[:136], w[152:]], axis=0), basis_ref)
-    t = row_transform(u, basis_ref, whole_rows) * weights_ref[...]
+    step = jumps(bands[1])
+    damped = (DAMP * SHRINK) * bands[1]
+    z_ref[...] = with_edges(z, y[16:112, :TC] + bands[1][:, :TC])
+    w_ref[...] = with_edges(w, inner_w_ref[...] + step[:, :TC] * f_ref[...] + damped[:, :TC])
+    lane = lanes_of((EXT, 256))
+    ones = jnp.where((lane >= 16) & (lane < 112), rows_t_part(basis_ref), 0.0)
+    ones = jnp.sum(ones, axis=1, keepdims=True)
+    u = gw_ref[...] + step * gf_ref[...] + ones * damped
+    u = u + row_transform(jnp.concatenate([w[8:32], w[48:72]], axis=0), basis_ref, edge_rows)
+    t = column_transform(u, basis_ref) * weights_ref[...]
     t_ref[...] = t
     send(j, a_ref, b_ref, *strips_of(t, basis_ref, 16))
 
@@ -507,22 +576,35 @@
     )
 
 
+def inner_dots_kernel(counts, y_ref, m_ref, both_ref, w_ref, stats_ref, v_ref, stats_out):
+    q = jnp.where(column_mask(counts), y_ref[8:120], 0.0)
+    v = (DAMP * q + lap(m_ref[8:120] * lap(q)))[8:104, :TC]
+    q = q[8:104, :TC]
+    v_ref[...] = v
+    rest = [
+        core_sums(v),
+        core_sums(both_ref[16:112] * q),
+        core_sums(w_ref[16:112] * q),
+        core_sums(v * q),
+    ]
+    zero = jnp.zeros((1, 1), jnp.float32)
+    stats_out[...] = stats_ref[...] + row_of([[zero, zero]] * 11 + rest)
+
+
 def dots_kernel(
-    counts, y_ref, m_ref, gb_ref, ga_ref, both_ref, w_ref, stats_ref, q_ref, v_ref, stats_out
+    counts, y_ref, m_ref, gb_ref, ga_ref, both_ref, w_ref, stats_ref, inner_v_ref, q_ref, v_ref, stats_out
 ):
     i, j = place()
-    q = add_rows(y_ref[...], *sides(i, counts[0], ga_ref[...], gb_ref[...]))
-    q = jnp.where(grid_mask((FR, FC), counts), q, 0.0)
-    v = DAMP * q + lap(m_ref[...] * lap(q))
-    qt, vt = q[:128, :256], v[:128, :256]
-    q_ref[...] = qt
-    v_ref[...] = vt
-    rest = [
-        core_sums(vt),
-        core_sums(both_ref[:TR] * qt),
-        core_sums(w_ref[...] * qt),
-        core_sums(vt * qt),
-    ]
+    y = y_ref[...]
+    q = edges(y, *sides(i, counts[0], ga_ref[...], gb_ref[...]))
+    q = jnp.where(edge_mask(counts), q, 0.0)
+    v = DAMP * q + lap(edge_part(m_ref) * lap(q))
+    q_ref[...] = with_edges(q, y[16:112, :TC])
+    v_ref[...] = with_edges(v, inner_v_ref[...])
+    qe, ve = (jnp.concatenate([x[16:32, :TC], x[48:64, :TC]], axis=0) for x in (q, v))
+    re = jnp.concatenate([both_ref[:16], both_ref[112:128]], axis=0)
+    we = jnp.concatenate([w_ref[:16], w_ref[112:]], axis=0)
+    rest = [core_sums(ve), core_sums(re * qe), core_sums(we * qe), core_sums(ve * qe)]
     zero = jnp.zeros((1, 1), jnp.float32)
     row = stats_ref[...] + row_of([[zero, zero]] * 11 + rest)
     stats_out[...] = jnp.broadcast_to(row, stats_out.shape)
@@ -587,7 +669,15 @@
     beta1 = 1.0 + rz1 / rz
     dad = (beta1 * beta1 * zw - 2.0 * a * beta1 * yw) * (1.0 / SHRINK) + a * a * yv
     a1 = rz1 / dad
-    coarse = spread(g, counts)
+    above, on, below = band_rows(g, counts)
+    coarse = jnp.concatenate(
+        [
+            jnp.broadcast_to(on, (128, FC)),
+            jnp.broadcast_to(below, (16, FC)),
+            jnp.broadcast_to(above, (16, FC)),
+        ],
+        axis=0,
+    )
     y = q_ref[...] + coarse[:128, :256]
     image = DAMP * coarse + lap(m_ref[...] * lap(coarse))
     v = v_ref[...] + image[:128, :256]
@@ -638,10 +728,10 @@
         return np.logical_or.reduce([known, *(known[[b for _, b in pairs]] for pairs in swaps)])
 
     even = [xor_pairs(counts, 0, 1), xor_pairs(counts, 1, 0)]
-    known = meet(even[0], near_pairs(counts, 1, 1))
-    known = meet(even[1], near_pairs(counts, 0, 1), xor_pairs(counts, 4, 0))
-    known = meet(even[0], near_pairs(counts, 1, 2), xor_pairs(counts, 2, 3))
-    return meet(even[1], near_pairs(counts, 0, 1)).all()
+    known = meet(even[0], near_pairs(counts, 1, 4))
+    known = meet(even[1], near_pairs(counts, 0, 1), xor_pairs(counts, 4, 2))
+    known = meet(even[0], near_pairs(counts, 1, 3))
+    return meet(even[1], near_pairs(counts, 0, 1), xor_pairs(counts, 2, 2)).all()
 
 
 def body(counts, height, noise):
@@ -669,7 +759,7 @@
             while bit < count:
                 table = table + small_swap(table, *((0, bit) if axis else (bit, 0)))
                 bit *= 2
-    ga, gb = swap(a, b, "col")
+    ga, gb = swap(a, b, "col", 4)
     r3, h3, b, a, table = call(
         functools.partial(widen_kernel, counts),
         [(128, 128)] * 2 + [(24 + depth, FC)] * 2 + [(depth, 128)],
@@ -680,7 +770,7 @@
     )
     ga, gb = swap(a, b, "row")
     weight, table = call(weights_kernel, [(EXT, 2 * SPEC), (depth, 128)], both, table, basis)
-    far = small_swap(table, 4, 0)
+    far = small_swap(table, 4, 2)
     t = call(forward_kernel, [(EXT, 2 * SPEC)], both, r3, basis)[0]
     t, table, b, a = call(
         functools.partial(first_kernel, counts),
@@ -694,18 +784,9 @@
     )
     table = merged(table, far)
     wide = jnp.pad(table, ((0, 0), (0, EXT - 128)))
-    m, table_too = call(
-        functools.partial(mobility_kernel, counts),
-        [(FR, FC), (depth, 128)],
-        both,
-        h3,
-        gb,
-        ga,
-        table,
-    )
-    y = call(inverse_kernel, [(EXT, FC)], t, basis)[0]
-    ga, gb = swap(*(jnp.concatenate([x, wide], axis=0) for x in (a, b)), "col", 2)
-    far = small_swap(table_too, 2, 3)
+    m = call(functools.partial(mobility_kernel, counts), [(FR, FC)], both, h3, gb, ga)[0]
+    y = call(inverse_kernel, [(EXT, FC)], t, basis, table)[0]
+    ga, gb = swap(*(jnp.concatenate([x, wide], axis=0) for x in (a, b)), "col", 3)
     y, table, b, a = call(
         functools.partial(columns_kernel, counts),
         [(EXT, FC), (depth, 128)] + [(24 + depth, FC)] * 2,
@@ -713,9 +794,17 @@
         ga,
         gb,
         table,
-        far,
     )
     ga, gb = swap(a, b, "row")
+    inner_w, f, gw, gf, table_too = call(
+        functools.partial(inner_kernel, counts),
+        [(96, TC)] * 2 + [(EXT, FC)] * 2 + [(depth, 128)],
+        y,
+        m,
+        basis,
+        table,
+    )
+    far = small_swap(table_too, 2, 2)
     z, w, t, table, b, a = call(
         functools.partial(second_kernel, counts, width),
         [(TR, TC)] * 2 + [(EXT, 2 * SPEC), (depth, 128)] + [(16, EXT)] * 2,
@@ -724,6 +813,11 @@
         gb,
         ga,
         table,
+        far,
+        inner_w,
+        f,
+        gw,
+        gf,
         weight,
         basis,
     )
@@ -733,6 +827,15 @@
         functools.partial(columns_kernel, counts), [(EXT, FC)] + [(16, FC)] * 2, y, gb, ga
     )
     ga, gb = swap(a, b, "row")
+    inner_v, stats = call(
+        functools.partial(inner_dots_kernel, counts),
+        [(96, TC), (1, 128)],
+        y,
+        m,
+        both,
+        w,
+        stats,
+    )
     q, v, stats = call(
         functools.partial(dots_kernel, counts),
         [(TR, TC)] * 2 + [(devices, 128)],
@@ -743,6 +846,7 @@
         both,
         w,
         stats,
+        inner_v,
     )
     stats = lax.all_to_all(stats, both_axes, 0, 0, tiled=True)
     return tuple(

time: 49.5 us -> 51.5 us (1.040)
  waiting for transfers between devices: 10.2 us -> 12.4 us
  starting transfers between devices: 20 us -> 19.3 us
  Pallas kernels: 7.56 us -> 8.18 us
    ppermute x6, starting transfers between devices: 6.14 us -> 8.29 us  [swap(): lax.ppermute(b, both_axes, near_pairs(counts, both_axes.index(axis), bit))]
    ppermute x6, starting transfers between devices: 8.78 us -> 6.71 us  [swap(): return (lax.ppermute(a, axis, pairs_from(lax.axis_size(axis), 0)), gb)]
    ppermute x2, waiting for transfers between devices: 2.52 us -> 4.16 us  [small_swap(): return lax.ppermute(x, both_axes, xor_pairs(counts, rows, cols))]
    ppermute x6, waiting for transfers between devices: 3.15 us -> 4.75 us  [swap(): return (lax.ppermute(a, axis, pairs_from(lax.axis_size(axis), 0)), gb)]
    ppermute x6, waiting for transfers between devices: 4.5 us -> 3.52 us  [swap(): lax.ppermute(b, both_axes, near_pairs(counts, both_axes.index(axis), bit))]
    ppermute x2, starting transfers between devices: 5.1 us -> 4.28 us  [small_swap(): return lax.ppermute(x, both_axes, xor_pairs(counts, rows, cols))]
    pallas_call x13 -> x15, Pallas kernels: 7.56 us -> 8.18 us  [call(): pl.pallas_call(kernel, out_shape=shapes, compiler_params=pltpu.CompilerPa...]
  transfers between devices with their start and end apart: 14 -> 14, of which waited for: 6 -> 8; matrix products, arithmetic and copies ran while one was open for 0% -> 0% of each run, Pallas kernels for 7% -> 7%
where the time goes in v11:
time: 51.5 us; the launch traced here: 51.3 us
  starting transfers between devices  19.3 us (37%)
  waiting for transfers between devices  12.4 us (24%)
  blocking collectives  9.64 us (19%)
  Pallas kernels  8.18 us (16%)
  other arithmetic  1 us (2%)
  between operations  0.78 us (2%)
    all_to_all x1, blocking collectives, body(): stats = lax.all_to_all(stats, both_axes, 0, 0, tiled=True)  9.64 us
    ppermute x6, starting transfers between devices, swap(): lax.ppermute(b, both_axes, near_pairs(counts, both_axes.index(axis), bit))  8.29 us
    pallas_call x15, Pallas kernels, call(): pl.pallas_call(kernel, out_shape=shapes, compiler_params=pltpu.CompilerPa...  8.18 us
    ppermute x6, starting transfers between devices, swap(): return (lax.ppermute(a, axis, pairs_from(lax.axis_size(axis), 0)), gb)  6.71 us
    ppermute x6, waiting for transfers between devices, swap(): return (lax.ppermute(a, axis, pairs_from(lax.axis_size(axis), 0)), gb)  4.75 us
    ppermute x2, starting transfers between devices, small_swap(): return lax.ppermute(x, both_axes, xor_pairs(counts, rows, cols))  4.28 us
    ppermute x2, waiting for transfers between devices, small_swap(): return lax.ppermute(x, both_axes, xor_pairs(counts, rows, cols))  4.16 us
    ppermute x6, waiting for transfers between devices, swap(): lax.ppermute(b, both_axes, near_pairs(counts, both_axes.index(axis), bit))  3.52 us
  transfers between devices with their start and end apart: 14, of which 8 were waited for; matrix products, arithmetic and copies ran while one was open for 0% of the time, Pallas kernels for 7%

profile of v11, /device:TPU:0, one launch (start us, length us, event | category | flops | bytes accessed | tf_op | source)
XLA Modules:
  0.0 51.3 jit_solution(8264116160027708732)
XLA Ops:
  0.6 1.0 %pad_add_fusion.both_ref = f32[256,256]{1,0:T(8,128)S(1)} fusion(f32[128,256]{1,0:T(8,128)} %param.3, f32[128,256]{1,0:T(8,128)} %param.4), kind=kLoop, calls=%fused_computation | loop fusion | flops 65536 | bytes 524288 | tf_op jit(solution)/shard_map/add | solution.py:752
  1.6 0.2 shard_map.50
  1.8 0.0 copy-start
  1.8 4.1 %collective-permute-start = (f32[40,128]{1,0:T(8,128)S(1)}, f32[40,128]{1,0:T(8,128)S(1)}, u32[]{:S(2)}, u32[]{:S(2)}) collective-permute-start(f32[40,128]{1,0:T(8,128)S(1)} %get-tuple-element.42), channel_id=1, source_target_pairs={{0,16},{1,2},{2,1},{3,19},{4,20},{5,6},{6,5},{7,23},{8,24},{9,10},... | collective-permute-start | bytes 61448 | tf_op jit(solution)/shard_map/ppermute | solution.py:746
  5.9 0.4 collective-permute-start.1
  6.3 1.4 %collective-permute-done.gb_ref = f32[40,128]{1,0:T(8,128)S(1)} collective-permute-done((f32[40,128]{1,0:T(8,128)S(1)}, f32[40,128]{1,0:T(8,128)S(1)}, u32[]{:S(2)}, u32[]{:S(2)}) %collective-permute-start) | collective-permute-done | bytes 20512 | tf_op jit(solution)/shard_map/ppermute | solution.py:746
  7.7 2.0 %collective-permute-done.1.ga_ref = f32[40,128]{1,0:T(8,128)S(1)} collective-permute-done((f32[40,128]{1,0:T(8,128)S(1)}, f32[40,128]{1,0:T(8,128)S(1)}, u32[]{:S(2)}, u32[]{:S(2)}) %collective-permute-start.1) | collective-permute-done | bytes 20512 | tf_op jit(solution)/shard_map/ppermute | solution.py:747
  9.7 0.2 shard_map.51
  9.9 0.5 collective-permute-start.2
  10.3 1.3 %collective-permute-start.3 = (f32[32,384]{1,0:T(8,128)S(1)}, f32[32,384]{1,0:T(8,128)S(1)}, u32[]{:S(2)}, u32[]{:S(2)}) collective-permute-start(f32[32,384]{1,0:T(8,128)S(1)} %get-tuple-element.45), channel_id=1, source_target_pairs={{0,4},{4,0},{8,12},{12,8},{16,20},{20,16},{24,28},{28,24},{1,5},{5... | collective-permute-start | bytes 147464 | tf_op jit(solution)/shard_map/ppermute | solution.py:747
  11.6 0.0 copy-done
  11.6 0.1 shard_map.53
  11.8 2.5 %collective-permute-start.4 = (f32[8,128]{1,0:T(8,128)S(1)}, f32[8,128]{1,0:T(8,128)S(1)}, u32[]{:S(2)}, u32[]{:S(2)}) collective-permute-start(f32[8,128]{1,0:T(8,128)S(1)} %get-tuple-element.49.table_ref), channel_id=1, source_target_pairs={{0,18},{1,19},{2,16},{3,17},{4,22},{5,23},{6,20},{7,21},{8,26},{9,... | collective-permute-start | bytes 12296 | tf_op jit(solution)/shard_map/ppermute | solution.py:750
  14.3 0.6 %shard_map.52.tile_ref = f32[144,512]{1,0:T(8,128)S(1)} custom-call(f32[256,256]{1,0:T(8,128)S(1)} %pad_add_fusion.both_ref, f32[128,128]{1,0:T(8,128)S(1)} %get-tuple-element.46.r3_ref, f32[1104,512]{1,0:T(8,128)S(1)} %copy-done), custom_call_target="tpu_custom_call" | custom-call | flops 1000000000 | bytes 1000000 | tf_op jit(solution)/shard_map/pallas_call | solution.py:691
  14.8 0.0 collective-permute-done.2.gb_ref
  14.8 0.0 collective-permute-done.3.ga_ref
  14.8 1.0 %shard_map.54 = (f32[144,512]{1,0:T(8,128)S(1)}, f32[8,128]{1,0:T(8,128)S(1)}, f32[24,144]{1,0:T(8,128)S(1)}, f32[24,144]{1,0:T(8,128)S(1)}) custom-call(f32[32,384]{1,0:T(8,128)S(1)} %collective-permute-done.2.gb_ref, f32[32,384]{1,0:T(8,128)S(1)} %collective-permute-done.3.ga_ref, f32[144,512]{1,0:T(8,128)S(1)} %shard_map.52.tile_ref, ...), custom_call_target="tpu_custom_call" | custom-call | flops 1000000000 | bytes 1000000 | tf_op jit(solution)/shard_map/pallas_call | solution.py:691
  15.9 1.4 %collective-permute-done.4 = f32[8,128]{1,0:T(8,128)S(1)} collective-permute-done((f32[8,128]{1,0:T(8,128)S(1)}, f32[8,128]{1,0:T(8,128)S(1)}, u32[]{:S(2)}, u32[]{:S(2)}) %collective-permute-start.4) | collective-permute-done | bytes 4128 | tf_op jit(solution)/shard_map/ppermute | solution.py:750
  17.3 0.8 %shard_map.55.y_ref = f32[144,384]{1,0:T(8,128)S(1)} custom-call(f32[144,512]{1,0:T(8,128)S(1)} %get-tuple-element.50.t_ref, f32[1104,512]{1,0:T(8,128)S(1)} %copy-done, f32[8,128]{1,0:T(8,128)S(1)} %compare_select_fusion.table_ref.refs_2_), custom_call_target="tpu_custom_call" | custom-call | flops 1000000000 | bytes 1000000 | tf_op jit(solution)/shard_map/pallas_call | solution.py:691
  18.1 0.1 collective-permute-start.6
  18.2 2.8 %collective-permute-start.5 = (f32[32,144]{1,0:T(8,128)S(1)}, f32[32,144]{1,0:T(8,128)S(1)}, u32[]{:S(2)}, u32[]{:S(2)}) collective-permute-start(f32[32,144]{1,0:T(8,128)S(1)} %get-tuple-element.81), channel_id=1, source_target_pairs={{0,1},{1,0},{2,3},{3,2},{4,5},{5,4},{6,7},{7,6},{8,9},{9,8},{10,11... | collective-permute-start | bytes 55304 | tf_op jit(solution)/shard_map/ppermute | solution.py:747
  21.0 0.5 %collective-permute-done.6.refs_1_ = f32[32,144]{1,0:T(8,128)S(1)} collective-permute-done((f32[32,144]{1,0:T(8,128)S(1)}, f32[32,144]{1,0:T(8,128)S(1)}, u32[]{:S(2)}, u32[]{:S(2)}) %collective-permute-start.6) | collective-permute-done | bytes 18464 | tf_op jit(solution)/shard_map/ppermute | solution.py:746
  21.5 1.7 %collective-permute-done.5.refs_0_ = f32[32,144]{1,0:T(8,128)S(1)} collective-permute-done((f32[32,144]{1,0:T(8,128)S(1)}, f32[32,144]{1,0:T(8,128)S(1)}, u32[]{:S(2)}, u32[]{:S(2)}) %collective-permute-start.5) | collective-permute-done | bytes 18464 | tf_op jit(solution)/shard_map/ppermute | solution.py:747
  23.2 0.2 shard_map.56
  23.4 1.7 %collective-permute-start.7 = (f32[32,384]{1,0:T(8,128)S(1)}, f32[32,384]{1,0:T(8,128)S(1)}, u32[]{:S(2)}, u32[]{:S(2)}) collective-permute-start(f32[32,384]{1,0:T(8,128)S(1)} %get-tuple-element.56), channel_id=1, source_target_pairs={{0,1},{1,0},{2,3},{3,2},{4,8},{5,9},{6,10},{7,11},{8,4},{9,5},{10,... | collective-permute-start | bytes 147464 | tf_op jit(solution)/shard_map/ppermute | solution.py:746
  25.1 0.0 collective-permute-start.8
  25.1 0.6 %shard_map.58 = (f32[96,256]{1,0:T(8,128)S(1)}, f32[96,256]{1,0:T(8,128)S(1)}, f32[144,384]{1,0:T(8,128)S(1)}, f32[144,384]{1,0:T(8,128)S(1)}, f32[8,128]{1,0:T(8,128)S(1)}) custom-call(f32[144,384]{1,0:T(8,128)S(1)} %get-tuple-element.54.y_ref, f32[160,384]{1,0:T(8,128)S(1)} %shard_map.57.m_ref, f32[1104,512]{1,0:T(8,128)S(1)} %copy-done, ...), custom_call_target="tpu_custom_call" | custom-call | flops 1000000000 | bytes 1000000 | tf_op jit(solution)/shard_map/pallas_call | solution.py:691
  25.7 1.8 %collective-permute-start.9 = (f32[8,128]{1,0:T(8,128)S(1)}, f32[8,128]{1,0:T(8,128)S(1)}, u32[]{:S(2)}, u32[]{:S(2)}) collective-permute-start(f32[8,128]{1,0:T(8,128)S(1)} %get-tuple-element.59), channel_id=1, source_target_pairs={{0,10},{1,11},{2,8},{3,9},{4,14},{5,15},{6,12},{7,13},{8,2},{9,3},... | collective-permute-start | bytes 12296 | tf_op jit(solution)/shard_map/ppermute | solution.py:750
  27.6 2.7 %collective-permute-done.9.far_ref = f32[8,128]{1,0:T(8,128)S(1)} collective-permute-done((f32[8,128]{1,0:T(8,128)S(1)}, f32[8,128]{1,0:T(8,128)S(1)}, u32[]{:S(2)}, u32[]{:S(2)}) %collective-permute-start.9) | collective-permute-done | bytes 4128 | tf_op jit(solution)/shard_map/ppermute | solution.py:750
  30.3 0.0 collective-permute-done.7.gb_ref
  30.3 0.0 collective-permute-done.8.ga_ref
  30.3 1.5 %shard_map.59 = (f32[128,256]{1,0:T(8,128)S(1)}, f32[128,256]{1,0:T(8,128)S(1)}, f32[144,512]{1,0:T(8,128)S(1)}, f32[8,128]{1,0:T(8,128)S(1)}, f32[16,144]{1,0:T(8,128)S(1)}, /*index=5*/f32[16,144]{1,0:T(8,128)S(1)}) custom-call(f32[144,384]{1,0:T(8,128)S(1)} %get-tuple-element.54.y_ref, f32[160,384]{1,0:T(8,128)S(1)} %shard_map.57.m_ref, ...), custom_call_target="tpu_custom_call" | custom-call | flops 1000000000 | bytes 1000000 | tf_op jit(solution)/shard_map/pallas_call | solution.py:691
  31.8 0.0 collective-permute-start.10
  31.8 2.2 %collective-permute-start.11 = (f32[16,144]{1,0:T(8,128)S(1)}, f32[16,144]{1,0:T(8,128)S(1)}, u32[]{:S(2)}, u32[]{:S(2)}) collective-permute-start(f32[16,144]{1,0:T(8,128)S(1)} %get-tuple-element.69), channel_id=1, source_target_pairs={{0,1},{1,0},{2,3},{3,2},{4,5},{5,4},{6,7},{7,6},{8,9},{9,8},{10,11... | collective-permute-start | bytes 27656 | tf_op jit(solution)/shard_map/ppermute | solution.py:747
  34.1 0.8 %shard_map.60 = (f32[144,384]{1,0:T(8,128)S(1)}, f32[1,128]{1,0:T(1,128)S(1)}) custom-call(f32[144,512]{1,0:T(8,128)S(1)} %get-tuple-element.64.t_ref, f32[1104,512]{1,0:T(8,128)S(1)} %copy-done, f32[256,256]{1,0:T(8,128)S(1)} %pad_add_fusion.both_ref, f32[160,384]{1,0:T(8,128)S(1)} %shard_map.57.m_ref, f32[128,256]{1,0:T(8,128)S(1)} %get-tuple-element.65.z_ref, ...), custom_call_target="tpu_custom_call" | custom-call | flops 1000000000 | bytes 1000000 | tf_op jit(solution)/shard_map/pallas_call | solution.py:691
  34.9 0.0 collective-permute-done.10.refs_0_
  34.9 1.0 %collective-permute-done.11.refs_1_ = f32[16,144]{1,0:T(8,128)S(1)} collective-permute-done((f32[16,144]{1,0:T(8,128)S(1)}, f32[16,144]{1,0:T(8,128)S(1)}, u32[]{:S(2)}, u32[]{:S(2)}) %collective-permute-start.11) | collective-permute-done | bytes 9248 | tf_op jit(solution)/shard_map/ppermute | solution.py:747
  36.0 0.2 shard_map.61
  36.1 1.9 %collective-permute-start.12 = (f32[16,384]{1,0:T(8,128)S(1)}, f32[16,384]{1,0:T(8,128)S(1)}, u32[]{:S(2)}, u32[]{:S(2)}) collective-permute-start(f32[16,384]{1,0:T(8,128)S(1)} %get-tuple-element.71), channel_id=1, source_target_pairs={{0,1},{1,0},{2,3},{3,2},{4,8},{5,9},{6,10},{7,11},{8,4},{9,5},{10,... | collective-permute-start | bytes 73736 | tf_op jit(solution)/shard_map/ppermute | solution.py:746
  38.1 0.0 collective-permute-start.13
  38.1 0.4 shard_map.62
  38.4 1.6 %collective-permute-done.12.gb_ref = f32[16,384]{1,0:T(8,128)S(1)} collective-permute-done((f32[16,384]{1,0:T(8,128)S(1)}, f32[16,384]{1,0:T(8,128)S(1)}, u32[]{:S(2)}, u32[]{:S(2)}) %collective-permute-start.12) | collective-permute-done | bytes 24608 | tf_op jit(solution)/shard_map/ppermute | solution.py:746
  40.0 0.0 collective-permute-done.13.ga_ref
  40.0 0.3 shard_map.63
  40.3 9.6 %all_to_all.11 = f32[32,1,128]{2,1,0:T(1,128)S(1)} all-to-all(f32[32,1,128]{2,1,0:T(1,128)S(1)} %bitcast.5), channel_id=1, replica_groups=mesh['row'=8,'col'=4] {'row','col'}, dimensions={0} | all-to-all | bytes 32768 | tf_op jit(solution)/shard_map/all_to_all | solution.py:851
  49.9 1.4 %shard_map.64 = (f32[128,256]{1,0:T(8,128)}, f32[128,256]{1,0:T(8,128)}) custom-call(f32[32,128]{1,0:T(8,128)S(1)} %bitcast.4, f32[8,128]{1,0:T(8,128)S(1)} %get-tuple-element.77.table_ref, f32[1104,512]{1,0:T(8,128)S(1)} %copy-done, f32[160,384]{1,0:T(8,128)S(1)} %shard_map.57.m_ref, f32[256,256]{1,0:T(8,128)S(1)} %pad_add_fusion.both_ref, ...), custom_call_target="tpu_custom_call" | custom-call | flops 1000000000 | bytes 1000000 | tf_op jit(solution)/shard_map/pallas_call | solution.py:691
  (3 shorter events, 0.0 us)
Async XLA Ops:
  1.8 9.9 %copy-start = (f32[1104,512]{1,0:T(8,128)S(1)}, f32[1104,512]{1,0:T(8,128)}, u32[]{:S(2)}) copy-start(f32[1104,512]{1,0:T(8,128)} %constant.6.clone.basis_ref) | copy-start | bytes 6782980
  1.8 5.9 %collective-permute-start = (f32[40,128]{1,0:T(8,128)S(1)}, f32[40,128]{1,0:T(8,128)S(1)}, u32[]{:S(2)}, u32[]{:S(2)}) collective-permute-start(f32[40,128]{1,0:T(8,128)S(1)} %get-tuple-element.42), channel_id=1, source_target_pairs={{0,16},{1,2},{2,1},{3,19},{4,20},{5,6},{6,5},{7,23},{8,24},{9,10},... | collective-permute-start | bytes 61448 | tf_op jit(solution)/shard_map/ppermute | solution.py:746
  5.9 3.8 %collective-permute-start.1 = (f32[40,128]{1,0:T(8,128)S(1)}, f32[40,128]{1,0:T(8,128)S(1)}, u32[]{:S(2)}, u32[]{:S(2)}) collective-permute-start(f32[40,128]{1,0:T(8,128)S(1)} %get-tuple-element.43), channel_id=1, source_target_pairs={{0,1},{1,0},{2,3},{3,2},{4,5},{5,4},{6,7},{7,6},{8,9},{9,8},{10,11... | collective-permute-start | bytes 61448 | tf_op jit(solution)/shard_map/ppermute | solution.py:747
  9.9 4.9 %collective-permute-start.2 = (f32[32,384]{1,0:T(8,128)S(1)}, f32[32,384]{1,0:T(8,128)S(1)}, u32[]{:S(2)}, u32[]{:S(2)}) collective-permute-start(f32[32,384]{1,0:T(8,128)S(1)} %get-tuple-element.44), channel_id=1, source_target_pairs={{0,1},{1,0},{2,3},{3,2},{4,8},{5,9},{6,10},{7,11},{8,4},{9,5},{10,... | collective-permute-start | bytes 147464 | tf_op jit(solution)/shard_map/ppermute | solution.py:746
  10.3 4.5 %collective-permute-start.3 = (f32[32,384]{1,0:T(8,128)S(1)}, f32[32,384]{1,0:T(8,128)S(1)}, u32[]{:S(2)}, u32[]{:S(2)}) collective-permute-start(f32[32,384]{1,0:T(8,128)S(1)} %get-tuple-element.45), channel_id=1, source_target_pairs={{0,4},{4,0},{8,12},{12,8},{16,20},{20,16},{24,28},{28,24},{1,5},{5... | collective-permute-start | bytes 147464 | tf_op jit(solution)/shard_map/ppermute | solution.py:747
  11.8 5.5 %collective-permute-start.4 = (f32[8,128]{1,0:T(8,128)S(1)}, f32[8,128]{1,0:T(8,128)S(1)}, u32[]{:S(2)}, u32[]{:S(2)}) collective-permute-start(f32[8,128]{1,0:T(8,128)S(1)} %get-tuple-element.49.table_ref), channel_id=1, source_target_pairs={{0,18},{1,19},{2,16},{3,17},{4,22},{5,23},{6,20},{7,21},{8,26},{9,... | collective-permute-start | bytes 12296 | tf_op jit(solution)/shard_map/ppermute | solution.py:750
  18.1 3.4 %collective-permute-start.6 = (f32[32,144]{1,0:T(8,128)S(1)}, f32[32,144]{1,0:T(8,128)S(1)}, u32[]{:S(2)}, u32[]{:S(2)}) collective-permute-start(f32[32,144]{1,0:T(8,128)S(1)} %get-tuple-element.80), channel_id=1, source_target_pairs={{0,12},{1,2},{2,1},{3,15},{4,8},{5,6},{6,5},{7,11},{8,4},{9,10},{1... | collective-permute-start | bytes 55304 | tf_op jit(solution)/shard_map/ppermute | solution.py:746
  18.2 5.0 %collective-permute-start.5 = (f32[32,144]{1,0:T(8,128)S(1)}, f32[32,144]{1,0:T(8,128)S(1)}, u32[]{:S(2)}, u32[]{:S(2)}) collective-permute-start(f32[32,144]{1,0:T(8,128)S(1)} %get-tuple-element.81), channel_id=1, source_target_pairs={{0,1},{1,0},{2,3},{3,2},{4,5},{5,4},{6,7},{7,6},{8,9},{9,8},{10,11... | collective-permute-start | bytes 55304 | tf_op jit(solution)/shard_map/ppermute | solution.py:747
  23.4 6.9 %collective-permute-start.7 = (f32[32,384]{1,0:T(8,128)S(1)}, f32[32,384]{1,0:T(8,128)S(1)}, u32[]{:S(2)}, u32[]{:S(2)}) collective-permute-start(f32[32,384]{1,0:T(8,128)S(1)} %get-tuple-element.56), channel_id=1, source_target_pairs={{0,1},{1,0},{2,3},{3,2},{4,8},{5,9},{6,10},{7,11},{8,4},{9,5},{10,... | collective-permute-start | bytes 147464 | tf_op jit(solution)/shard_map/ppermute | solution.py:746
  25.1 5.2 %collective-permute-start.8 = (f32[32,384]{1,0:T(8,128)S(1)}, f32[32,384]{1,0:T(8,128)S(1)}, u32[]{:S(2)}, u32[]{:S(2)}) collective-permute-start(f32[32,384]{1,0:T(8,128)S(1)} %get-tuple-element.57), channel_id=1, source_target_pairs={{0,4},{4,0},{8,12},{12,8},{16,20},{20,16},{24,28},{28,24},{1,5},{5... | collective-permute-start | bytes 147464 | tf_op jit(solution)/shard_map/ppermute | solution.py:747
  25.7 4.6 %collective-permute-start.9 = (f32[8,128]{1,0:T(8,128)S(1)}, f32[8,128]{1,0:T(8,128)S(1)}, u32[]{:S(2)}, u32[]{:S(2)}) collective-permute-start(f32[8,128]{1,0:T(8,128)S(1)} %get-tuple-element.59), channel_id=1, source_target_pairs={{0,10},{1,11},{2,8},{3,9},{4,14},{5,15},{6,12},{7,13},{8,2},{9,3},... | collective-permute-start | bytes 12296 | tf_op jit(solution)/shard_map/ppermute | solution.py:750
  31.8 3.1 %collective-permute-start.10 = (f32[16,144]{1,0:T(8,128)S(1)}, f32[16,144]{1,0:T(8,128)S(1)}, u32[]{:S(2)}, u32[]{:S(2)}) collective-permute-start(f32[16,144]{1,0:T(8,128)S(1)} %get-tuple-element.68), channel_id=1, source_target_pairs={{0,4},{1,2},{2,1},{3,7},{4,0},{5,6},{6,5},{7,3},{8,12},{9,10},{10,... | collective-permute-start | bytes 27656 | tf_op jit(solution)/shard_map/ppermute | solution.py:746
  31.8 4.1 %collective-permute-start.11 = (f32[16,144]{1,0:T(8,128)S(1)}, f32[16,144]{1,0:T(8,128)S(1)}, u32[]{:S(2)}, u32[]{:S(2)}) collective-permute-start(f32[16,144]{1,0:T(8,128)S(1)} %get-tuple-element.69), channel_id=1, source_target_pairs={{0,1},{1,0},{2,3},{3,2},{4,5},{5,4},{6,7},{7,6},{8,9},{9,8},{10,11... | collective-permute-start | bytes 27656 | tf_op jit(solution)/shard_map/ppermute | solution.py:747
  36.1 3.9 %collective-permute-start.12 = (f32[16,384]{1,0:T(8,128)S(1)}, f32[16,384]{1,0:T(8,128)S(1)}, u32[]{:S(2)}, u32[]{:S(2)}) collective-permute-start(f32[16,384]{1,0:T(8,128)S(1)} %get-tuple-element.71), channel_id=1, source_target_pairs={{0,1},{1,0},{2,3},{3,2},{4,8},{5,9},{6,10},{7,11},{8,4},{9,5},{10,... | collective-permute-start | bytes 73736 | tf_op jit(solution)/shard_map/ppermute | solution.py:746
  38.1 2.0 %collective-permute-start.13 = (f32[16,384]{1,0:T(8,128)S(1)}, f32[16,384]{1,0:T(8,128)S(1)}, u32[]{:S(2)}, u32[]{:S(2)}) collective-permute-start(f32[16,384]{1,0:T(8,128)S(1)} %get-tuple-element.72), channel_id=1, source_target_pairs={{0,4},{4,0},{8,12},{12,8},{16,20},{20,16},{24,28},{28,24},{1,5},{5... | collective-permute-start | bytes 73736 | tf_op jit(solution)/shard_map/ppermute | solution.py:747

commit v12 on v11

--- a/solution.py
+++ b/solution.py
@@ -180,15 +180,6 @@
     return row
 
 
-def gathered(rows, width):
-    devices = rows.shape[0]
-    turned = rows.T
-    parts = [turned[:16], turned[64:80]]
-    if width > 2 * devices:
-        parts.append(jnp.zeros((16, width - 2 * devices), jnp.float32))
-    return jnp.concatenate(parts, axis=1)
-
-
 def coarse_values(c_row, inverse):
     return dot(jnp.broadcast_to(c_row, (8, c_row.shape[1])), inverse)[:1]
 
@@ -204,10 +195,14 @@
     at = lax.rem(c + 2, 2) * (nr * counts[1]) + r * counts[1] + (c + 2) // 2 - 1
     picked = jnp.where(inside & (lanes_of(shape) == at), g_row, 0.0)
     picked = jnp.sum(picked, axis=1, keepdims=True)
+    return as_bands([picked[k : k + 1] for k in range(12)])
+
+
+def as_bands(values):
     lane = lanes_of((1, FC))
     bands = []
     for d in range(3):
-        left, first, second, right = (picked[4 * d + k : 4 * d + k + 1] for k in range(4))
+        left, first, second, right = values[4 * d : 4 * d + 4]
         bands.append(
             jnp.where(
                 lane < 128,
@@ -448,15 +443,12 @@
     table_out[...] = merged(table_ref[...], ga_ref[24:, :128], gb_ref[24:, :128])
 
 
-def mobility_kernel(counts, both_ref, h3_ref, gb_ref, ga_ref, m_ref):
+def inverse_kernel(counts, t_ref, basis_ref, both_ref, h3_ref, gb_ref, ga_ref, y_ref, m_ref):
+    y_ref[...] = solution_of(t_ref[...], basis_ref)
     above, below = sides(lax.axis_index("row"), counts[0], ga_ref[8:24], gb_ref[8:24])
     h = jnp.concatenate([both_ref[TR:], h3_ref[...]], axis=1)
     tall = jnp.concatenate([h, below, above], axis=0)
     m_ref[...] = tall * tall * tall
-
-
-def inverse_kernel(t_ref, basis_ref, table_ref, y_ref):
-    y_ref[...] = solution_of(t_ref[...], basis_ref)
 
 
 def columns_kernel(counts, y_ref, *refs):
@@ -477,9 +469,7 @@
     send(i, a_ref, b_ref, *strips)
 
 
-def inner_kernel(
-    counts, y_ref, m_ref, basis_ref, table_ref, w_ref, f_ref, gw_ref, gf_ref, table_out
-):
+def inner_kernel(counts, y_ref, m_ref, basis_ref, w_ref, f_ref, gw_ref, gf_ref):
     mask = column_mask(counts)
     s = jnp.where(mask, y_ref[8:120], 0.0)
     m = m_ref[8:120]
@@ -491,7 +481,6 @@
     f_ref[...] = f[:, :TC]
     gw_ref[...] = row_transform(w, basis_ref, inner_rows)
     gf_ref[...] = row_transform(f, basis_ref, inner_rows)
-    table_out[...] = table_ref[...]
 
 
 def second_kernel(
@@ -502,7 +491,6 @@
     gb_ref,
     ga_ref,
     table_ref,
-    far_ref,
     inner_w_ref,
     f_ref,
     gw_ref,
@@ -512,7 +500,6 @@
     z_ref,
     w_ref,
     t_ref,
-    table_out,
     b_ref,
     a_ref,
 ):
@@ -521,8 +508,7 @@
     mask = edge_mask(counts)
     s = edges(y, *sides(i, counts[0], ga_ref[:24], gb_ref[:24]))
     s = jnp.where(mask, s, 0.0)
-    table = merged(table_ref[...], far_ref[...], ga_ref[24:, :128], gb_ref[24:, :128])
-    table_out[...] = table
+    table = merged(table_ref[...], ga_ref[24:, :128], gb_ref[24:, :128])
     g = coarse_values(as_row(table, width), coarse_part(basis_ref, width))
     bands = band_rows(g, counts)
     coarse = edge_bands(bands)
@@ -559,6 +545,7 @@
         ]
 
     first, last = lane % 128 == 0, lane % 128 == 127
+    zero = jnp.zeros((1, 1), jnp.float32)
     stats_ref[...] = row_of(
         [
             core_sums(rt * zt),
@@ -572,6 +559,8 @@
             halves(jnp.where(last, top, 0.0)),
             halves(jnp.where(first, low, 0.0)),
             halves(jnp.where(last, low, 0.0)),
+            *[[zero, zero]] * 4,
+            core_sums(rt),
         ]
     )
 
@@ -614,9 +603,9 @@
     counts,
     width,
     stats_ref,
-    table_ref,
     basis_ref,
     m_ref,
+    f_ref,
     both_ref,
     z_ref,
     w_ref,
@@ -625,62 +614,69 @@
     solution_ref,
     residual_ref,
 ):
+    i, j = place()
     tiles_c = counts[1]
     devices = counts[0] * tiles_c
-    table = gathered(stats_ref[...], width)
-    st = [table[k : k + 1] for k in range(15)]
-
-    def whole(x):
-        return jnp.sum(x, axis=1, keepdims=True)
-
-    rz, zw, rq, wq, qv = (whole(st[k]) for k in (0, 1, 12, 13, 14))
-    c0, c1, sums_v = as_row(table_ref[...], width), st[2], st[11]
-    g = coarse_values(c1, coarse_part(basis_ref, width))
-    lane = lanes_of((1, width))
-    cell = lane < 2 * devices
-    on_left = lane < devices
-    device = lane % devices
+    rows = stats_ref[...]
+    st = jnp.concatenate([rows, pltpu.roll(rows, 64, 1)], axis=0)
+    inverse = coarse_part(basis_ref, width)[: 2 * devices, : 2 * devices]
+    g = jnp.broadcast_to(dot(inverse, st)[:, 2:3], st.shape)
+    lane, row = lanes_of(st.shape), rows_of(st.shape)
+    device = row % devices
     column = device % tiles_c
-
-    def from_lane(distance):
-        return pltpu.roll(g, distance % width, 1)
-
-    up = jnp.where(device >= tiles_c, from_lane(tiles_c), 0.0)
-    down = jnp.where(device < devices - tiles_c, from_lane(-tiles_c), 0.0)
-    left = jnp.where(
-        on_left, jnp.where(column > 0, from_lane(1 - devices), 0.0), from_lane(devices)
-    )
+    on_left = row < devices
+
+    def from_row(distance):
+        return pltpu.roll(g, distance % (2 * devices), 0)
+
+    up = jnp.where(device >= tiles_c, from_row(tiles_c), 0.0)
+    down = jnp.where(device < devices - tiles_c, from_row(-tiles_c), 0.0)
+    left = jnp.where(on_left, jnp.where(column > 0, from_row(1 - devices), 0.0), from_row(devices))
     right = jnp.where(
-        on_left,
-        from_lane(-devices),
-        jnp.where(column < tiles_c - 1, from_lane(devices - 1), 0.0),
+        on_left, from_row(-devices), jnp.where(column < tiles_c - 1, from_row(devices - 1), 0.0)
     )
     du, dd, dl, dr = g - up, g - down, g - left, g - right
-    energy = DAMP * SUB * SUB * g * g
-    energy = energy + st[3] * du * du + st[4] * dd * dd + st[5] * dl * dl + st[6] * dr * dr
-    for weight, p, q in ((st[7], du, dl), (st[8], du, dr), (st[9], dd, dl), (st[10], dd, dr)):
-        both = p + q
-        energy = energy + weight * both * both
-    ry = rq + whole(g * c0)
-    yw = wq + whole(g * c1)
-    yv = qv + whole(jnp.where(cell, 2.0 * g * sums_v + energy, 0.0))
+    across = jnp.where(
+        (lane == 3) | (lane == 7) | (lane == 8),
+        du,
+        jnp.where((lane == 4) | (lane == 9) | (lane == 10), dd, 0.0),
+    )
+    across = across + jnp.where(
+        (lane == 5) | (lane == 7) | (lane == 9),
+        dl,
+        jnp.where((lane == 6) | (lane == 8) | (lane == 10), dr, 0.0),
+    )
+    factor = jnp.where((lane == 2) | (lane == 15), g, across * across)
+    factor = jnp.where(lane == 11, 2.0 * g, factor)
+    factor = jnp.where((lane < 2) | ((lane >= 12) & (lane < 15)), 1.0, factor)
+    terms = jnp.where(lane == 16, (DAMP * SUB * SUB) * g * g, st * factor)
+    sums = jnp.sum(terms, axis=0, keepdims=True)
+
+    def whole(wanted):
+        return jnp.sum(jnp.where(wanted, sums, 0.0), axis=1, keepdims=True)
+
+    at = lanes_of((1, 128))
+    rz, zw = whole(at == 0), whole(at == 1)
+    ry = whole((at == 12) | (at == 15))
+    yw = whole((at == 13) | (at == 2))
+    yv = whole(((at >= 3) & (at < 12)) | (at == 14) | (at == 16))
     a = rz / zw
     rz1 = rz - a * ry - a * zw + a * a * yw
     beta1 = 1.0 + rz1 / rz
     dad = (beta1 * beta1 * zw - 2.0 * a * beta1 * yw) * (1.0 / SHRINK) + a * a * yv
     a1 = rz1 / dad
-    above, on, below = band_rows(g, counts)
-    coarse = jnp.concatenate(
-        [
-            jnp.broadcast_to(on, (128, FC)),
-            jnp.broadcast_to(below, (16, FC)),
-            jnp.broadcast_to(above, (16, FC)),
-        ],
-        axis=0,
-    )
-    y = q_ref[...] + coarse[:128, :256]
-    image = DAMP * coarse + lap(m_ref[...] * lap(coarse))
-    v = v_ref[...] + image[:128, :256]
+    r = i - 1 + lane // 4
+    c = 2 * j - 1 + lane % 4
+    inside = (r >= 0) & (r < counts[0]) & (c >= 0) & (c < 2 * tiles_c) & (lane < 12)
+    where = lax.rem(c + 2, 2) * devices + r * tiles_c + (c + 2) // 2 - 1
+    picked = jnp.sum(jnp.where(inside & (row == where), g, 0.0), axis=0, keepdims=True)
+    bands = as_bands([picked[:, k : k + 1] for k in range(12)])
+    on = bands[1][:, :TC]
+    coarse = edge_bands(bands)
+    image = DAMP * coarse + lap(edge_part(m_ref) * lap(coarse))
+    image = with_edges(image, (jumps(bands[1]) * (1.0 / SHRINK))[:, :TC] * f_ref[...] + DAMP * on)
+    y = q_ref[...] + on
+    v = v_ref[...] + image
     z, w = z_ref[...], w_ref[...]
     solution_ref[...] = (a * SHRINK) * z + a1 * (beta1 * z - a * y)
     residual_ref[...] = both_ref[:TR] - a * w - a1 * ((beta1 * (1.0 / SHRINK)) * w - a * v)
@@ -703,15 +699,15 @@
     return found
 
 
-def near_pairs(counts, axis, bit):
+def odd_pairs(counts, axis, bit):
     found = []
     for i in range(counts[0]):
         for j in range(counts[1]):
             at = [i, j]
-            if 0 < at[axis] < counts[axis] - 1:
-                at[axis] += 1 if at[axis] % 2 else -1
+            if bit and at[axis] in (0, counts[axis] - 1):
+                at[1 - axis] ^= bit
             else:
-                at[1 - axis] ^= bit
+                at[axis] = (at[axis] + (1 if at[axis] % 2 else -1)) % counts[axis]
             found.append((i * counts[1] + j, at[0] * counts[1] + at[1]))
     return found
 
@@ -728,10 +724,10 @@
         return np.logical_or.reduce([known, *(known[[b for _, b in pairs]] for pairs in swaps)])
 
     even = [xor_pairs(counts, 0, 1), xor_pairs(counts, 1, 0)]
-    known = meet(even[0], near_pairs(counts, 1, 4))
-    known = meet(even[1], near_pairs(counts, 0, 1), xor_pairs(counts, 4, 2))
-    known = meet(even[0], near_pairs(counts, 1, 3))
-    return meet(even[1], near_pairs(counts, 0, 1), xor_pairs(counts, 2, 2)).all()
+    known = meet(even[0], odd_pairs(counts, 1, 0))
+    known = meet(even[1], odd_pairs(counts, 0, 0), xor_pairs(counts, 4, 0))
+    known = meet(even[0], odd_pairs(counts, 1, 1))
+    return meet(even[1], odd_pairs(counts, 0, 0)).all()
 
 
 def body(counts, height, noise):
@@ -742,8 +738,8 @@
     both_axes = ("row", "col")
     depth = table_shape(counts)[0]
 
-    def swap(a, b, axis, bit=1):
-        gb = lax.ppermute(b, both_axes, near_pairs(counts, both_axes.index(axis), bit))
+    def swap(a, b, axis, bit=0):
+        gb = lax.ppermute(b, both_axes, odd_pairs(counts, both_axes.index(axis), bit))
         return lax.ppermute(a, axis, pairs_from(lax.axis_size(axis), 0)), gb
 
     def small_swap(x, rows, cols):
@@ -759,7 +755,7 @@
             while bit < count:
                 table = table + small_swap(table, *((0, bit) if axis else (bit, 0)))
                 bit *= 2
-    ga, gb = swap(a, b, "col", 4)
+    ga, gb = swap(a, b, "col")
     r3, h3, b, a, table = call(
         functools.partial(widen_kernel, counts),
         [(128, 128)] * 2 + [(24 + depth, FC)] * 2 + [(depth, 128)],
@@ -770,7 +766,7 @@
     )
     ga, gb = swap(a, b, "row")
     weight, table = call(weights_kernel, [(EXT, 2 * SPEC), (depth, 128)], both, table, basis)
-    far = small_swap(table, 4, 2)
+    far = small_swap(table, 4, 0)
     t = call(forward_kernel, [(EXT, 2 * SPEC)], both, r3, basis)[0]
     t, table, b, a = call(
         functools.partial(first_kernel, counts),
@@ -784,9 +780,17 @@
     )
     table = merged(table, far)
     wide = jnp.pad(table, ((0, 0), (0, EXT - 128)))
-    m = call(functools.partial(mobility_kernel, counts), [(FR, FC)], both, h3, gb, ga)[0]
-    y = call(inverse_kernel, [(EXT, FC)], t, basis, table)[0]
-    ga, gb = swap(*(jnp.concatenate([x, wide], axis=0) for x in (a, b)), "col", 3)
+    y, m = call(
+        functools.partial(inverse_kernel, counts),
+        [(EXT, FC), (FR, FC)],
+        t,
+        basis,
+        both,
+        h3,
+        gb,
+        ga,
+    )
+    ga, gb = swap(*(jnp.concatenate([x, wide], axis=0) for x in (a, b)), "col", 1)
     y, table, b, a = call(
         functools.partial(columns_kernel, counts),
         [(EXT, FC), (depth, 128)] + [(24 + depth, FC)] * 2,
@@ -796,24 +800,21 @@
         table,
     )
     ga, gb = swap(a, b, "row")
-    inner_w, f, gw, gf, table_too = call(
+    inner_w, f, gw, gf = call(
         functools.partial(inner_kernel, counts),
-        [(96, TC)] * 2 + [(EXT, FC)] * 2 + [(depth, 128)],
+        [(96, TC)] * 2 + [(EXT, FC)] * 2,
         y,
         m,
         basis,
-        table,
-    )
-    far = small_swap(table_too, 2, 2)
-    z, w, t, table, b, a = call(
+    )
+    z, w, t, b, a = call(
         functools.partial(second_kernel, counts, width),
-        [(TR, TC)] * 2 + [(EXT, 2 * SPEC), (depth, 128)] + [(16, EXT)] * 2,
+        [(TR, TC)] * 2 + [(EXT, 2 * SPEC)] + [(16, EXT)] * 2,
         y,
         m,
         gb,
         ga,
         table,
-        far,
         inner_w,
         f,
         gw,
@@ -821,12 +822,12 @@
         weight,
         basis,
     )
-    ga, gb = swap(a, b, "col")
+    ga, gb = swap(a, b, "col", 1)
     y, stats = call(inverse_stats_kernel, [(EXT, FC), (1, 128)], t, basis, both, m, z, w)
     y, b, a = call(
         functools.partial(columns_kernel, counts), [(EXT, FC)] + [(16, FC)] * 2, y, gb, ga
     )
-    ga, gb = swap(a, b, "row")
+    ga, gb = swap(a, b, "row", 1)
     inner_v, stats = call(
         functools.partial(inner_dots_kernel, counts),
         [(96, TC), (1, 128)],
@@ -854,9 +855,9 @@
             functools.partial(end_kernel, counts, width),
             [(TR, TC)] * 2,
             stats,
-            table,
             basis,
             m,
+            f,
             both,
             z,
             w,

time: 51.5 us -> 47.8 us (0.928)
  starting transfers between devices: 19.3 us -> 17.5 us
  waiting for transfers between devices: 12.4 us -> 11.1 us
    ppermute x2 -> x1, waiting for transfers between devices: 4.16 us -> 0.07 us  [small_swap(): return lax.ppermute(x, both_axes, xor_pairs(counts, rows, cols))]
    ppermute x6, waiting for transfers between devices: 3.52 us -> 6.57 us  [swap(): lax.ppermute(b, both_axes, odd_pairs(counts, both_axes.index(axis), bit))]
    ppermute x2 -> x1, starting transfers between devices: 4.28 us -> 2.43 us  [small_swap(): return lax.ppermute(x, both_axes, xor_pairs(counts, rows, cols))]
    pallas_call x15 -> x14, Pallas kernels: 8.18 us -> 8.05 us  [call(): pl.pallas_call(kernel, out_shape=shapes, compiler_params=pltpu.CompilerPa...]
  transfers between devices with their start and end apart: 14 -> 13, of which waited for: 8 -> 8; matrix products, arithmetic and copies ran while one was open for 0% -> 0% of each run, Pallas kernels for 7% -> 9%
where the time goes in v12:
time: 47.8 us; the launch traced here: 47.7 us
  starting transfers between devices  17.5 us (37%)
  waiting for transfers between devices  11.1 us (23%)
  blocking collectives  9.2 us (19%)
  Pallas kernels  8.05 us (17%)
  other arithmetic  1 us (2%)
  between operations  0.76 us (2%)
    all_to_all x1, blocking collectives, body(): stats = lax.all_to_all(stats, both_axes, 0, 0, tiled=True)  9.2 us
    ppermute x6, starting transfers between devices, swap(): lax.ppermute(b, both_axes, odd_pairs(counts, both_axes.index(axis), bit))  8.74 us
    pallas_call x14, Pallas kernels, call(): pl.pallas_call(kernel, out_shape=shapes, compiler_params=pltpu.CompilerPa...  8.05 us
    ppermute x6, waiting for transfers between devices, swap(): lax.ppermute(b, both_axes, odd_pairs(counts, both_axes.index(axis), bit))  6.57 us
    ppermute x6, starting transfers between devices, swap(): return (lax.ppermute(a, axis, pairs_from(lax.axis_size(axis), 0)), gb)  6.38 us
    ppermute x6, waiting for transfers between devices, swap(): return (lax.ppermute(a, axis, pairs_from(lax.axis_size(axis), 0)), gb)  4.48 us
    ppermute x1, starting transfers between devices, small_swap(): return lax.ppermute(x, both_axes, xor_pairs(counts, rows, cols))  2.43 us
    add x1, other arithmetic, body(): jnp.pad(noise, ((0, TR), (0, 0))) + jnp.pad(height, ((TR, 0), (0, 0)))  0.99 us
  transfers between devices with their start and end apart: 13, of which 8 were waited for; matrix products, arithmetic and copies ran while one was open for 0% of the time, Pallas kernels for 9%

profile of v12, /device:TPU:0, one launch (start us, length us, event | category | flops | bytes accessed | tf_op | source)
XLA Modules:
  0.0 47.7 jit_solution(3406512167511158)
XLA Ops:
  0.6 1.0 %pad_add_fusion.both_ref = f32[256,256]{1,0:T(8,128)S(1)} fusion(f32[128,256]{1,0:T(8,128)} %param.3, f32[128,256]{1,0:T(8,128)} %param.4), kind=kLoop, calls=%fused_computation | loop fusion | flops 65536 | bytes 524288 | tf_op jit(solution)/shard_map/add | solution.py:748
  1.6 0.2 shard_map.50
  1.8 0.0 copy-start
  1.8 4.0 %collective-permute-start = (f32[40,128]{1,0:T(8,128)S(1)}, f32[40,128]{1,0:T(8,128)S(1)}, u32[]{:S(2)}, u32[]{:S(2)}) collective-permute-start(f32[40,128]{1,0:T(8,128)S(1)} %get-tuple-element.42), channel_id=1, source_target_pairs={{0,3},{1,2},{2,1},{3,0},{4,7},{5,6},{6,5},{7,4},{8,11},{9,10},{10,... | collective-permute-start | bytes 61448 | tf_op jit(solution)/shard_map/ppermute | solution.py:742
  5.8 0.5 %collective-permute-start.1 = (f32[40,128]{1,0:T(8,128)S(1)}, f32[40,128]{1,0:T(8,128)S(1)}, u32[]{:S(2)}, u32[]{:S(2)}) collective-permute-start(f32[40,128]{1,0:T(8,128)S(1)} %get-tuple-element.43), channel_id=1, source_target_pairs={{0,1},{1,0},{2,3},{3,2},{4,5},{5,4},{6,7},{7,6},{8,9},{9,8},{10,11... | collective-permute-start | bytes 61448 | tf_op jit(solution)/shard_map/ppermute | solution.py:743
  6.3 1.2 %collective-permute-done.gb_ref = f32[40,128]{1,0:T(8,128)S(1)} collective-permute-done((f32[40,128]{1,0:T(8,128)S(1)}, f32[40,128]{1,0:T(8,128)S(1)}, u32[]{:S(2)}, u32[]{:S(2)}) %collective-permute-start) | collective-permute-done | bytes 20512 | tf_op jit(solution)/shard_map/ppermute | solution.py:742
  7.5 2.0 %collective-permute-done.1.ga_ref = f32[40,128]{1,0:T(8,128)S(1)} collective-permute-done((f32[40,128]{1,0:T(8,128)S(1)}, f32[40,128]{1,0:T(8,128)S(1)}, u32[]{:S(2)}, u32[]{:S(2)}) %collective-permute-start.1) | collective-permute-done | bytes 20512 | tf_op jit(solution)/shard_map/ppermute | solution.py:743
  9.5 0.2 shard_map.51
  9.7 2.0 %collective-permute-start.2 = (f32[32,384]{1,0:T(8,128)S(1)}, f32[32,384]{1,0:T(8,128)S(1)}, u32[]{:S(2)}, u32[]{:S(2)}) collective-permute-start(f32[32,384]{1,0:T(8,128)S(1)} %get-tuple-element.44), channel_id=1, source_target_pairs={{0,28},{1,29},{2,30},{3,31},{4,8},{5,9},{6,10},{7,11},{8,4},{9,5},... | collective-permute-start | bytes 147464 | tf_op jit(solution)/shard_map/ppermute | solution.py:742
  11.7 0.0 collective-permute-start.3
  11.7 0.0 copy-done
  11.7 0.1 shard_map.53
  11.9 2.4 %collective-permute-start.4 = (f32[8,128]{1,0:T(8,128)S(1)}, f32[8,128]{1,0:T(8,128)S(1)}, u32[]{:S(2)}, u32[]{:S(2)}) collective-permute-start(f32[8,128]{1,0:T(8,128)S(1)} %get-tuple-element.49.table_ref), channel_id=1, source_target_pairs={{0,16},{1,17},{2,18},{3,19},{4,20},{5,21},{6,22},{7,23},{8,24},{9,... | collective-permute-start | bytes 12296 | tf_op jit(solution)/shard_map/ppermute | solution.py:746
  14.3 0.6 %shard_map.52.tile_ref = f32[144,512]{1,0:T(8,128)S(1)} custom-call(f32[256,256]{1,0:T(8,128)S(1)} %pad_add_fusion.both_ref, f32[128,128]{1,0:T(8,128)S(1)} %get-tuple-element.46.r3_ref, f32[1104,512]{1,0:T(8,128)S(1)} %copy-done), custom_call_target="tpu_custom_call" | custom-call | flops 1000000000 | bytes 1000000 | tf_op jit(solution)/shard_map/pallas_call | solution.py:687
  14.9 0.5 %collective-permute-done.2.gb_ref = f32[32,384]{1,0:T(8,128)S(1)} collective-permute-done((f32[32,384]{1,0:T(8,128)S(1)}, f32[32,384]{1,0:T(8,128)S(1)}, u32[]{:S(2)}, u32[]{:S(2)}) %collective-permute-start.2) | collective-permute-done | bytes 49184 | tf_op jit(solution)/shard_map/ppermute | solution.py:742
  15.4 0.0 collective-permute-done.3.ga_ref
  15.4 1.0 %shard_map.54 = (f32[144,512]{1,0:T(8,128)S(1)}, f32[8,128]{1,0:T(8,128)S(1)}, f32[24,144]{1,0:T(8,128)S(1)}, f32[24,144]{1,0:T(8,128)S(1)}) custom-call(f32[32,384]{1,0:T(8,128)S(1)} %collective-permute-done.2.gb_ref, f32[32,384]{1,0:T(8,128)S(1)} %collective-permute-done.3.ga_ref, f32[144,512]{1,0:T(8,128)S(1)} %shard_map.52.tile_ref, ...), custom_call_target="tpu_custom_call" | custom-call | flops 1000000000 | bytes 1000000 | tf_op jit(solution)/shard_map/pallas_call | solution.py:687
  16.4 0.1 collective-permute-done.4
  16.5 0.1 collective-permute-start.6
  16.6 1.9 %collective-permute-start.5 = (f32[32,144]{1,0:T(8,128)S(1)}, f32[32,144]{1,0:T(8,128)S(1)}, u32[]{:S(2)}, u32[]{:S(2)}) collective-permute-start(f32[32,144]{1,0:T(8,128)S(1)} %get-tuple-element.81), channel_id=1, source_target_pairs={{0,1},{1,0},{2,3},{3,2},{4,5},{5,4},{6,7},{7,6},{8,9},{9,8},{10,11... | collective-permute-start | bytes 55304 | tf_op jit(solution)/shard_map/ppermute | solution.py:743
  18.5 0.8 %shard_map.55 = (f32[144,384]{1,0:T(8,128)S(1)}, f32[160,384]{1,0:T(8,128)S(1)}) custom-call(f32[144,512]{1,0:T(8,128)S(1)} %get-tuple-element.50.t_ref, f32[1104,512]{1,0:T(8,128)S(1)} %copy-done, f32[256,256]{1,0:T(8,128)S(1)} %pad_add_fusion.both_ref, f32[128,128]{1,0:T(8,128)S(1)} %get-tuple-element.51.h3_ref, ...), custom_call_target="tpu_custom_call" | custom-call | flops 1000000000 | bytes 1000000 | tf_op jit(solution)/shard_map/pallas_call | solution.py:687
  19.3 0.0 collective-permute-done.6.refs_1_
  19.3 1.4 %collective-permute-done.5.refs_0_ = f32[32,144]{1,0:T(8,128)S(1)} collective-permute-done((f32[32,144]{1,0:T(8,128)S(1)}, f32[32,144]{1,0:T(8,128)S(1)}, u32[]{:S(2)}, u32[]{:S(2)}) %collective-permute-start.5) | collective-permute-done | bytes 18464 | tf_op jit(solution)/shard_map/ppermute | solution.py:743
  20.7 0.2 shard_map.56
  20.9 0.8 %collective-permute-start.7 = (f32[32,384]{1,0:T(8,128)S(1)}, f32[32,384]{1,0:T(8,128)S(1)}, u32[]{:S(2)}, u32[]{:S(2)}) collective-permute-start(f32[32,384]{1,0:T(8,128)S(1)} %get-tuple-element.58), channel_id=1, source_target_pairs={{0,28},{1,29},{2,30},{3,31},{4,8},{5,9},{6,10},{7,11},{8,4},{9,5},... | collective-permute-start | bytes 147464 | tf_op jit(solution)/shard_map/ppermute | solution.py:742
  21.7 0.8 %collective-permute-start.8 = (f32[32,384]{1,0:T(8,128)S(1)}, f32[32,384]{1,0:T(8,128)S(1)}, u32[]{:S(2)}, u32[]{:S(2)}) collective-permute-start(f32[32,384]{1,0:T(8,128)S(1)} %get-tuple-element.59), channel_id=1, source_target_pairs={{0,4},{4,0},{8,12},{12,8},{16,20},{20,16},{24,28},{28,24},{1,5},{5... | collective-permute-start | bytes 147464 | tf_op jit(solution)/shard_map/ppermute | solution.py:743
  22.5 0.6 %shard_map.57 = (f32[96,256]{1,0:T(8,128)S(1)}, f32[96,256]{1,0:T(8,128)S(1)}, f32[144,384]{1,0:T(8,128)S(1)}, f32[144,384]{1,0:T(8,128)S(1)}) custom-call(f32[144,384]{1,0:T(8,128)S(1)} %get-tuple-element.56.y_ref, f32[160,384]{1,0:T(8,128)S(1)} %get-tuple-element.57.m_ref, f32[1104,512]{1,0:T(8,128)S(1)} %copy-done), custom_call_target="tpu_custom_call" | custom-call | flops 1000000000 | bytes 1000000 | tf_op jit(solution)/shard_map/pallas_call | solution.py:687
  23.0 3.2 %collective-permute-done.7.gb_ref = f32[32,384]{1,0:T(8,128)S(1)} collective-permute-done((f32[32,384]{1,0:T(8,128)S(1)}, f32[32,384]{1,0:T(8,128)S(1)}, u32[]{:S(2)}, u32[]{:S(2)}) %collective-permute-start.7) | collective-permute-done | bytes 49184 | tf_op jit(solution)/shard_map/ppermute | solution.py:742
  26.3 0.0 collective-permute-done.8.ga_ref
  26.3 1.5 %shard_map.58 = (f32[128,256]{1,0:T(8,128)S(1)}, f32[128,256]{1,0:T(8,128)S(1)}, f32[144,512]{1,0:T(8,128)S(1)}, f32[16,144]{1,0:T(8,128)S(1)}, f32[16,144]{1,0:T(8,128)S(1)}) custom-call(f32[144,384]{1,0:T(8,128)S(1)} %get-tuple-element.56.y_ref, f32[160,384]{1,0:T(8,128)S(1)} %get-tuple-element.57.m_ref, f32[32,384]{1,0:T(8,128)S(1)} %collective-permute-done.7.gb_ref, ...), custom_call_target="tpu_custom_call" | custom-call | flops 1000000000 | bytes 1000000 | tf_op jit(solution)/shard_map/pallas_call | solution.py:687
  27.8 0.0 collective-permute-start.9
  27.8 3.2 %collective-permute-start.10 = (f32[16,144]{1,0:T(8,128)S(1)}, f32[16,144]{1,0:T(8,128)S(1)}, u32[]{:S(2)}, u32[]{:S(2)}) collective-permute-start(f32[16,144]{1,0:T(8,128)S(1)} %get-tuple-element.70), channel_id=1, source_target_pairs={{0,1},{1,0},{2,3},{3,2},{4,5},{5,4},{6,7},{7,6},{8,9},{9,8},{10,11... | collective-permute-start | bytes 27656 | tf_op jit(solution)/shard_map/ppermute | solution.py:743
  31.0 0.8 %shard_map.59 = (f32[144,384]{1,0:T(8,128)S(1)}, f32[1,128]{1,0:T(1,128)S(1)}) custom-call(f32[144,512]{1,0:T(8,128)S(1)} %get-tuple-element.65.t_ref, f32[1104,512]{1,0:T(8,128)S(1)} %copy-done, f32[256,256]{1,0:T(8,128)S(1)} %pad_add_fusion.both_ref, f32[160,384]{1,0:T(8,128)S(1)} %get-tuple-element.57.m_ref, f32[128,256]{1,0:T(8,128)S(1)} %get-tuple-element.66.z_ref, ...), custom_call_target="tpu_custom_call" | custom-call | flops 1000000000 | bytes 1000000 | tf_op jit(solution)/shard_map/pallas_call | solution.py:687
  31.8 0.0 collective-permute-done.9.refs_0_
  31.8 1.0 %collective-permute-done.10.refs_1_ = f32[16,144]{1,0:T(8,128)S(1)} collective-permute-done((f32[16,144]{1,0:T(8,128)S(1)}, f32[16,144]{1,0:T(8,128)S(1)}, u32[]{:S(2)}, u32[]{:S(2)}) %collective-permute-start.10) | collective-permute-done | bytes 9248 | tf_op jit(solution)/shard_map/ppermute | solution.py:743
  32.9 0.2 shard_map.60
  33.0 1.9 %collective-permute-start.11 = (f32[16,384]{1,0:T(8,128)S(1)}, f32[16,384]{1,0:T(8,128)S(1)}, u32[]{:S(2)}, u32[]{:S(2)}) collective-permute-start(f32[16,384]{1,0:T(8,128)S(1)} %get-tuple-element.72), channel_id=1, source_target_pairs={{0,1},{1,0},{2,3},{3,2},{4,8},{5,9},{6,10},{7,11},{8,4},{9,5},{10,... | collective-permute-start | bytes 73736 | tf_op jit(solution)/shard_map/ppermute | solution.py:742
  35.0 0.0 collective-permute-start.12
  35.0 0.4 shard_map.61
  35.3 1.6 %collective-permute-done.11.gb_ref = f32[16,384]{1,0:T(8,128)S(1)} collective-permute-done((f32[16,384]{1,0:T(8,128)S(1)}, f32[16,384]{1,0:T(8,128)S(1)}, u32[]{:S(2)}, u32[]{:S(2)}) %collective-permute-start.11) | collective-permute-done | bytes 24608 | tf_op jit(solution)/shard_map/ppermute | solution.py:742
  36.9 0.0 collective-permute-done.12.ga_ref
  36.9 0.3 shard_map.62
  37.2 9.2 %all_to_all.11 = f32[32,1,128]{2,1,0:T(1,128)S(1)} all-to-all(f32[32,1,128]{2,1,0:T(1,128)S(1)} %bitcast.5), channel_id=1, replica_groups=mesh['row'=8,'col'=4] {'row','col'}, dimensions={0} | all-to-all | bytes 32768 | tf_op jit(solution)/shard_map/all_to_all | solution.py:852
  46.4 1.3 %shard_map.63 = (f32[128,256]{1,0:T(8,128)}, f32[128,256]{1,0:T(8,128)}) custom-call(f32[32,128]{1,0:T(8,128)S(1)} %bitcast.4, f32[1104,512]{1,0:T(8,128)S(1)} %copy-done, f32[160,384]{1,0:T(8,128)S(1)} %get-tuple-element.57.m_ref, f32[96,256]{1,0:T(8,128)S(1)} %get-tuple-element.62.f_ref, f32[256,256]{1,0:T(8,128)S(1)} %pad_add_fusion.both_ref, ...), custom_call_target="tpu_custom_call" | custom-call | flops 1000000000 | bytes 1000000 | tf_op jit(solution)/shard_map/pallas_call | solution.py:687
  (2 shorter events, 0.0 us)
Async XLA Ops:
  1.8 9.9 %copy-start = (f32[1104,512]{1,0:T(8,128)S(1)}, f32[1104,512]{1,0:T(8,128)}, u32[]{:S(2)}) copy-start(f32[1104,512]{1,0:T(8,128)} %constant.6.clone.basis_ref) | copy-start | bytes 6782980
  1.8 5.7 %collective-permute-start = (f32[40,128]{1,0:T(8,128)S(1)}, f32[40,128]{1,0:T(8,128)S(1)}, u32[]{:S(2)}, u32[]{:S(2)}) collective-permute-start(f32[40,128]{1,0:T(8,128)S(1)} %get-tuple-element.42), channel_id=1, source_target_pairs={{0,3},{1,2},{2,1},{3,0},{4,7},{5,6},{6,5},{7,4},{8,11},{9,10},{10,... | collective-permute-start | bytes 61448 | tf_op jit(solution)/shard_map/ppermute | solution.py:742
  5.8 3.8 %collective-permute-start.1 = (f32[40,128]{1,0:T(8,128)S(1)}, f32[40,128]{1,0:T(8,128)S(1)}, u32[]{:S(2)}, u32[]{:S(2)}) collective-permute-start(f32[40,128]{1,0:T(8,128)S(1)} %get-tuple-element.43), channel_id=1, source_target_pairs={{0,1},{1,0},{2,3},{3,2},{4,5},{5,4},{6,7},{7,6},{8,9},{9,8},{10,11... | collective-permute-start | bytes 61448 | tf_op jit(solution)/shard_map/ppermute | solution.py:743
  9.7 5.6 %collective-permute-start.2 = (f32[32,384]{1,0:T(8,128)S(1)}, f32[32,384]{1,0:T(8,128)S(1)}, u32[]{:S(2)}, u32[]{:S(2)}) collective-permute-start(f32[32,384]{1,0:T(8,128)S(1)} %get-tuple-element.44), channel_id=1, source_target_pairs={{0,28},{1,29},{2,30},{3,31},{4,8},{5,9},{6,10},{7,11},{8,4},{9,5},... | collective-permute-start | bytes 147464 | tf_op jit(solution)/shard_map/ppermute | solution.py:742
  11.7 3.7 %collective-permute-start.3 = (f32[32,384]{1,0:T(8,128)S(1)}, f32[32,384]{1,0:T(8,128)S(1)}, u32[]{:S(2)}, u32[]{:S(2)}) collective-permute-start(f32[32,384]{1,0:T(8,128)S(1)} %get-tuple-element.45), channel_id=1, source_target_pairs={{0,4},{4,0},{8,12},{12,8},{16,20},{20,16},{24,28},{28,24},{1,5},{5... | collective-permute-start | bytes 147464 | tf_op jit(solution)/shard_map/ppermute | solution.py:743
  11.9 4.6 %collective-permute-start.4 = (f32[8,128]{1,0:T(8,128)S(1)}, f32[8,128]{1,0:T(8,128)S(1)}, u32[]{:S(2)}, u32[]{:S(2)}) collective-permute-start(f32[8,128]{1,0:T(8,128)S(1)} %get-tuple-element.49.table_ref), channel_id=1, source_target_pairs={{0,16},{1,17},{2,18},{3,19},{4,20},{5,21},{6,22},{7,23},{8,24},{9,... | collective-permute-start | bytes 12296 | tf_op jit(solution)/shard_map/ppermute | solution.py:746
  16.5 2.8 %collective-permute-start.6 = (f32[32,144]{1,0:T(8,128)S(1)}, f32[32,144]{1,0:T(8,128)S(1)}, u32[]{:S(2)}, u32[]{:S(2)}) collective-permute-start(f32[32,144]{1,0:T(8,128)S(1)} %get-tuple-element.80), channel_id=1, source_target_pairs={{0,4},{1,2},{2,1},{3,7},{4,0},{5,6},{6,5},{7,3},{8,12},{9,10},{10,... | collective-permute-start | bytes 55304 | tf_op jit(solution)/shard_map/ppermute | solution.py:742
  16.6 4.2 %collective-permute-start.5 = (f32[32,144]{1,0:T(8,128)S(1)}, f32[32,144]{1,0:T(8,128)S(1)}, u32[]{:S(2)}, u32[]{:S(2)}) collective-permute-start(f32[32,144]{1,0:T(8,128)S(1)} %get-tuple-element.81), channel_id=1, source_target_pairs={{0,1},{1,0},{2,3},{3,2},{4,5},{5,4},{6,7},{7,6},{8,9},{9,8},{10,11... | collective-permute-start | bytes 55304 | tf_op jit(solution)/shard_map/ppermute | solution.py:743
  20.9 5.4 %collective-permute-start.7 = (f32[32,384]{1,0:T(8,128)S(1)}, f32[32,384]{1,0:T(8,128)S(1)}, u32[]{:S(2)}, u32[]{:S(2)}) collective-permute-start(f32[32,384]{1,0:T(8,128)S(1)} %get-tuple-element.58), channel_id=1, source_target_pairs={{0,28},{1,29},{2,30},{3,31},{4,8},{5,9},{6,10},{7,11},{8,4},{9,5},... | collective-permute-start | bytes 147464 | tf_op jit(solution)/shard_map/ppermute | solution.py:742
  21.7 4.6 %collective-permute-start.8 = (f32[32,384]{1,0:T(8,128)S(1)}, f32[32,384]{1,0:T(8,128)S(1)}, u32[]{:S(2)}, u32[]{:S(2)}) collective-permute-start(f32[32,384]{1,0:T(8,128)S(1)} %get-tuple-element.59), channel_id=1, source_target_pairs={{0,4},{4,0},{8,12},{12,8},{16,20},{20,16},{24,28},{28,24},{1,5},{5... | collective-permute-start | bytes 147464 | tf_op jit(solution)/shard_map/ppermute | solution.py:743
  27.8 4.0 %collective-permute-start.9 = (f32[16,144]{1,0:T(8,128)S(1)}, f32[16,144]{1,0:T(8,128)S(1)}, u32[]{:S(2)}, u32[]{:S(2)}) collective-permute-start(f32[16,144]{1,0:T(8,128)S(1)} %get-tuple-element.69), channel_id=1, source_target_pairs={{0,4},{1,2},{2,1},{3,7},{4,0},{5,6},{6,5},{7,3},{8,12},{9,10},{10,... | collective-permute-start | bytes 27656 | tf_op jit(solution)/shard_map/ppermute | solution.py:742
  27.8 5.1 %collective-permute-start.10 = (f32[16,144]{1,0:T(8,128)S(1)}, f32[16,144]{1,0:T(8,128)S(1)}, u32[]{:S(2)}, u32[]{:S(2)}) collective-permute-start(f32[16,144]{1,0:T(8,128)S(1)} %get-tuple-element.70), channel_id=1, source_target_pairs={{0,1},{1,0},{2,3},{3,2},{4,5},{5,4},{6,7},{7,6},{8,9},{9,8},{10,11... | collective-permute-start | bytes 27656 | tf_op jit(solution)/shard_map/ppermute | solution.py:743
  33.0 3.9 %collective-permute-start.11 = (f32[16,384]{1,0:T(8,128)S(1)}, f32[16,384]{1,0:T(8,128)S(1)}, u32[]{:S(2)}, u32[]{:S(2)}) collective-permute-start(f32[16,384]{1,0:T(8,128)S(1)} %get-tuple-element.72), channel_id=1, source_target_pairs={{0,1},{1,0},{2,3},{3,2},{4,8},{5,9},{6,10},{7,11},{8,4},{9,5},{10,... | collective-permute-start | bytes 73736 | tf_op jit(solution)/shard_map/ppermute | solution.py:742
  35.0 2.0 %collective-permute-start.12 = (f32[16,384]{1,0:T(8,128)S(1)}, f32[16,384]{1,0:T(8,128)S(1)}, u32[]{:S(2)}, u32[]{:S(2)}) collective-permute-start(f32[16,384]{1,0:T(8,128)S(1)} %get-tuple-element.73), channel_id=1, source_target_pairs={{0,4},{4,0},{8,12},{12,8},{16,20},{20,16},{24,28},{28,24},{1,5},{5... | collective-permute-start | bytes 73736 | tf_op jit(solution)/shard_map/ppermute | solution.py:743

commit v13 on v12

--- a/solution.py
+++ b/solution.py
@@ -180,22 +180,16 @@
     return row
 
 
-def coarse_values(c_row, inverse):
-    return dot(jnp.broadcast_to(c_row, (8, c_row.shape[1])), inverse)[:1]
-
-
-def band_rows(g_row, counts):
+def near_inverse(counts, inverse):
     i, j = place()
     nr, nc = counts[0], 2 * counts[1]
-    shape = (16, g_row.shape[1])
+    shape = (16, inverse.shape[0])
     which = rows_of(shape)
     r = i - 1 + which // 4
     c = 2 * j - 1 + which % 4
     inside = (r >= 0) & (r < nr) & (c >= 0) & (c < nc) & (which < 12)
     at = lax.rem(c + 2, 2) * (nr * counts[1]) + r * counts[1] + (c + 2) // 2 - 1
-    picked = jnp.where(inside & (lanes_of(shape) == at), g_row, 0.0)
-    picked = jnp.sum(picked, axis=1, keepdims=True)
-    return as_bands([picked[k : k + 1] for k in range(12)])
+    return dot(jnp.where(inside & (lanes_of(shape) == at), 1.0, 0.0), inverse)
 
 
 def as_bands(values):
@@ -266,12 +260,6 @@
     high, low = halves_of(u)
     rows = part(basis_ref).astype(jnp.bfloat16)
     return product(rows, jnp.concatenate([high, low, high], axis=0))
-
-
-def weights(means, basis_ref):
-    lane = lanes_of((1, 2 * SPEC))
-    mean = jnp.where(lane < SPEC, means[0], means[1])
-    return 1.0 / (DAMP + mean * basis_ref[:EXT])
 
 
 def strips_of(t, basis_ref, deep):
@@ -408,17 +396,19 @@
     send(i, a_ref, b_ref, strip(slice(0, 8), slice(0, 16)), strip(slice(120, 128), slice(112, 128)))
 
 
-def weights_kernel(both_ref, table_ref, basis_ref, weights_ref, table_out):
+def means_kernel(both_ref, table_ref, basis_ref, means_ref, table_out):
     h = both_ref[TR:]
-    means = [x / (SUB * SUB) for x in core_sums(h * h * h)]
-    weights_ref[...] = weights(means, basis_ref)
+    lane = lanes_of((1, 2 * SPEC))
+    left, right = (x / (SUB * SUB) for x in core_sums(h * h * h))
+    means_ref[...] = jnp.where(lane < SPEC, left, right)
     table_out[...] = table_ref[...]
 
 
-def forward_kernel(both_ref, r3_ref, basis_ref, t_ref):
+def forward_kernel(both_ref, r3_ref, means_ref, basis_ref, t_ref, weights_ref):
     r = both_ref[:TR]
     u = column_transform(jnp.concatenate([r, r3_ref[...]], axis=1), basis_ref)
     t_ref[...] = row_transform(u, basis_ref, tile_rows)
+    weights_ref[...] = 1.0 / (DAMP + means_ref[...] * basis_ref[:EXT])
 
 
 def first_kernel(
@@ -469,7 +459,7 @@
     send(i, a_ref, b_ref, *strips)
 
 
-def inner_kernel(counts, y_ref, m_ref, basis_ref, w_ref, f_ref, gw_ref, gf_ref):
+def inner_kernel(counts, width, y_ref, m_ref, basis_ref, w_ref, f_ref, gw_ref, gf_ref, near_ref):
     mask = column_mask(counts)
     s = jnp.where(mask, y_ref[8:120], 0.0)
     m = m_ref[8:120]
@@ -481,6 +471,7 @@
     f_ref[...] = f[:, :TC]
     gw_ref[...] = row_transform(w, basis_ref, inner_rows)
     gf_ref[...] = row_transform(f, basis_ref, inner_rows)
+    near_ref[...] = near_inverse(counts, coarse_part(basis_ref, width))
 
 
 def second_kernel(
@@ -495,6 +486,7 @@
     f_ref,
     gw_ref,
     gf_ref,
+    near_ref,
     weights_ref,
     basis_ref,
     z_ref,
@@ -509,8 +501,8 @@
     s = edges(y, *sides(i, counts[0], ga_ref[:24], gb_ref[:24]))
     s = jnp.where(mask, s, 0.0)
     table = merged(table_ref[...], ga_ref[24:, :128], gb_ref[24:, :128])
-    g = coarse_values(as_row(table, width), coarse_part(basis_ref, width))
-    bands = band_rows(g, counts)
+    picked = jnp.sum(near_ref[...] * as_row(table, width), axis=1, keepdims=True)
+    bands = as_bands([picked[k : k + 1] for k in range(12)])
     coarse = edge_bands(bands)
     m = edge_part(m_ref)
     flow = m * (lap(s) + lap(coarse))
@@ -613,6 +605,9 @@
     v_ref,
     solution_ref,
     residual_ref,
+    solution_vmem,
+    residual_vmem,
+    sems,
 ):
     i, j = place()
     tiles_c = counts[1]
@@ -678,17 +673,24 @@
     y = q_ref[...] + on
     v = v_ref[...] + image
     z, w = z_ref[...], w_ref[...]
-    solution_ref[...] = (a * SHRINK) * z + a1 * (beta1 * z - a * y)
-    residual_ref[...] = both_ref[:TR] - a * w - a1 * ((beta1 * (1.0 / SHRINK)) * w - a * v)
-
-
-def call(kernel, outs, *args, flops=10**9):
+    first = pltpu.make_async_copy(solution_vmem, solution_ref, sems.at[0])
+    second = pltpu.make_async_copy(residual_vmem, residual_ref, sems.at[1])
+    solution_vmem[...] = (a * SHRINK) * z + a1 * (beta1 * z - a * y)
+    first.start()
+    residual_vmem[...] = both_ref[:TR] - a * w - a1 * ((beta1 * (1.0 / SHRINK)) * w - a * v)
+    second.start()
+    first.wait()
+    second.wait()
+
+
+def call(kernel, outs, *args, flops=10**9, **options):
     shapes = [jax.ShapeDtypeStruct(s, jnp.float32) for s in outs]
     return pl.pallas_call(
         kernel,
         out_shape=shapes,
         compiler_params=pltpu.CompilerParams(vmem_limit_bytes=48 * 1024 * 1024),
         cost_estimate=pl.CostEstimate(flops=flops, bytes_accessed=10**6, transcendentals=0),
+        **options,
     )(*args)
 
 
@@ -724,9 +726,9 @@
         return np.logical_or.reduce([known, *(known[[b for _, b in pairs]] for pairs in swaps)])
 
     even = [xor_pairs(counts, 0, 1), xor_pairs(counts, 1, 0)]
+    known = meet(even[0], odd_pairs(counts, 1, 1))
+    known = meet(even[1], odd_pairs(counts, 0, 0), xor_pairs(counts, 4, 0))
     known = meet(even[0], odd_pairs(counts, 1, 0))
-    known = meet(even[1], odd_pairs(counts, 0, 0), xor_pairs(counts, 4, 0))
-    known = meet(even[0], odd_pairs(counts, 1, 1))
     return meet(even[1], odd_pairs(counts, 0, 0)).all()
 
 
@@ -755,7 +757,7 @@
             while bit < count:
                 table = table + small_swap(table, *((0, bit) if axis else (bit, 0)))
                 bit *= 2
-    ga, gb = swap(a, b, "col")
+    ga, gb = swap(a, b, "col", 1)
     r3, h3, b, a, table = call(
         functools.partial(widen_kernel, counts),
         [(128, 128)] * 2 + [(24 + depth, FC)] * 2 + [(depth, 128)],
@@ -765,9 +767,9 @@
         ga,
     )
     ga, gb = swap(a, b, "row")
-    weight, table = call(weights_kernel, [(EXT, 2 * SPEC), (depth, 128)], both, table, basis)
+    means, table = call(means_kernel, [(1, 2 * SPEC), (depth, 128)], both, table, basis)
     far = small_swap(table, 4, 0)
-    t = call(forward_kernel, [(EXT, 2 * SPEC)], both, r3, basis)[0]
+    t, weight = call(forward_kernel, [(EXT, 2 * SPEC)] * 2, both, r3, means, basis)
     t, table, b, a = call(
         functools.partial(first_kernel, counts),
         [(EXT, 2 * SPEC), (depth, 128)] + [(24, EXT)] * 2,
@@ -790,7 +792,7 @@
         gb,
         ga,
     )
-    ga, gb = swap(*(jnp.concatenate([x, wide], axis=0) for x in (a, b)), "col", 1)
+    ga, gb = swap(*(jnp.concatenate([x, wide], axis=0) for x in (a, b)), "col")
     y, table, b, a = call(
         functools.partial(columns_kernel, counts),
         [(EXT, FC), (depth, 128)] + [(24 + depth, FC)] * 2,
@@ -800,9 +802,9 @@
         table,
     )
     ga, gb = swap(a, b, "row")
-    inner_w, f, gw, gf = call(
-        functools.partial(inner_kernel, counts),
-        [(96, TC)] * 2 + [(EXT, FC)] * 2,
+    inner_w, f, gw, gf, near = call(
+        functools.partial(inner_kernel, counts, width),
+        [(96, TC)] * 2 + [(EXT, FC)] * 2 + [(16, width)],
         y,
         m,
         basis,
@@ -819,6 +821,7 @@
         f,
         gw,
         gf,
+        near,
         weight,
         basis,
     )
@@ -863,6 +866,8 @@
             w,
             q,
             v,
+            out_specs=[pl.BlockSpec(memory_space=pl.ANY)] * 2,
+            scratch_shapes=[pltpu.VMEM((TR, TC), jnp.float32)] * 2 + [pltpu.SemaphoreType.DMA((2,))],
         )
     )
 

time: 47.8 us -> 50.1 us (1.048)
  waiting for transfers between devices: 11.1 us -> 13.7 us
    ppermute x6, starting transfers between devices: 8.74 us -> 4.1 us  [swap(): lax.ppermute(b, both_axes, odd_pairs(counts, both_axes.index(axis), bit))]
    ppermute x6, starting transfers between devices: 6.38 us -> 10.7 us  [swap(): return (lax.ppermute(a, axis, pairs_from(lax.axis_size(axis), 0)), gb)]
    ppermute x6, waiting for transfers between devices: 6.57 us -> 9.97 us  [swap(): lax.ppermute(b, both_axes, odd_pairs(counts, both_axes.index(axis), bit))]
    ppermute x6, waiting for transfers between devices: 4.48 us -> 3.7 us  [swap(): return (lax.ppermute(a, axis, pairs_from(lax.axis_size(axis), 0)), gb)]
  transfers between devices with their start and end apart: 13 -> 13, of which waited for: 8 -> 7; matrix products, arithmetic and copies ran while one was open for 0% -> 0% of each run, Pallas kernels for 9% -> 8%
where the time goes in v13:
time: 50.1 us; the launch traced here: 49.9 us
  starting transfers between devices  17.4 us (35%)
  waiting for transfers between devices  13.7 us (27%)
  blocking collectives  9.2 us (18%)
  Pallas kernels  7.85 us (16%)
  other arithmetic  1 us (2%)
  between operations  0.77 us (2%)
    ppermute x6, starting transfers between devices, swap(): return (lax.ppermute(a, axis, pairs_from(lax.axis_size(axis), 0)), gb)  10.7 us
    ppermute x6, waiting for transfers between devices, swap(): lax.ppermute(b, both_axes, odd_pairs(counts, both_axes.index(axis), bit))  9.97 us
    all_to_all x1, blocking collectives, body(): stats = lax.all_to_all(stats, both_axes, 0, 0, tiled=True)  9.2 us
    pallas_call x14, Pallas kernels, call(): pl.pallas_call(kernel, out_shape=shapes, compiler_params=pltpu.CompilerPa...  7.85 us
    ppermute x6, starting transfers between devices, swap(): lax.ppermute(b, both_axes, odd_pairs(counts, both_axes.index(axis), bit))  4.1 us
    ppermute x6, waiting for transfers between devices, swap(): return (lax.ppermute(a, axis, pairs_from(lax.axis_size(axis), 0)), gb)  3.7 us
    ppermute x1, starting transfers between devices, small_swap(): return lax.ppermute(x, both_axes, xor_pairs(counts, rows, cols))  2.59 us
  transfers between devices with their start and end apart: 13, of which 7 were waited for; matrix products, arithmetic and copies ran while one was open for 0% of the time, Pallas kernels for 8%

profile of v13, /device:TPU:0, one launch (start us, length us, event | category | flops | bytes accessed | tf_op | source)
XLA Modules:
  0.0 49.9 jit_solution(4780431111987208241)
XLA Ops:
  0.6 1.0 %pad_add_fusion.both_ref = f32[256,256]{1,0:T(8,128)S(1)} fusion(f32[128,256]{1,0:T(8,128)} %param.3, f32[128,256]{1,0:T(8,128)} %param.4), kind=kLoop, calls=%fused_computation | loop fusion | flops 65536 | bytes 524288 | tf_op jit(solution)/shard_map/add | solution.py:750
  1.6 0.2 shard_map.50
  1.8 0.0 copy-start
  1.8 0.5 %collective-permute-start = (f32[40,128]{1,0:T(8,128)S(1)}, f32[40,128]{1,0:T(8,128)S(1)}, u32[]{:S(2)}, u32[]{:S(2)}) collective-permute-start(f32[40,128]{1,0:T(8,128)S(1)} %get-tuple-element.45), channel_id=1, source_target_pairs={{0,4},{1,2},{2,1},{3,7},{4,0},{5,6},{6,5},{7,3},{8,12},{9,10},{10,... | collective-permute-start | bytes 61448 | tf_op jit(solution)/shard_map/ppermute | solution.py:744
  2.3 4.0 %collective-permute-start.1 = (f32[40,128]{1,0:T(8,128)S(1)}, f32[40,128]{1,0:T(8,128)S(1)}, u32[]{:S(2)}, u32[]{:S(2)}) collective-permute-start(f32[40,128]{1,0:T(8,128)S(1)} %get-tuple-element.46), channel_id=1, source_target_pairs={{0,1},{1,0},{2,3},{3,2},{4,5},{5,4},{6,7},{7,6},{8,9},{9,8},{10,11... | collective-permute-start | bytes 61448 | tf_op jit(solution)/shard_map/ppermute | solution.py:745
  6.3 0.0 collective-permute-done.gb_ref
  6.3 2.0 %collective-permute-done.1.ga_ref = f32[40,128]{1,0:T(8,128)S(1)} collective-permute-done((f32[40,128]{1,0:T(8,128)S(1)}, f32[40,128]{1,0:T(8,128)S(1)}, u32[]{:S(2)}, u32[]{:S(2)}) %collective-permute-start.1) | collective-permute-done | bytes 20512 | tf_op jit(solution)/shard_map/ppermute | solution.py:745
  8.3 0.2 shard_map.51
  8.5 0.0 copy-done
  8.5 0.1 shard_map.52
  8.6 2.6 %collective-permute-start.4 = (f32[8,128]{1,0:T(8,128)S(1)}, f32[8,128]{1,0:T(8,128)S(1)}, u32[]{:S(2)}, u32[]{:S(2)}) collective-permute-start(f32[8,128]{1,0:T(8,128)S(1)} %get-tuple-element.54.table_ref), channel_id=1, source_target_pairs={{0,16},{1,17},{2,18},{3,19},{4,20},{5,21},{6,22},{7,23},{8,24},{9,... | collective-permute-start | bytes 12296 | tf_op jit(solution)/shard_map/ppermute | solution.py:748
  11.2 0.0 collective-permute-start.2
  11.2 1.7 %collective-permute-start.3 = (f32[32,384]{1,0:T(8,128)S(1)}, f32[32,384]{1,0:T(8,128)S(1)}, u32[]{:S(2)}, u32[]{:S(2)}) collective-permute-start(f32[32,384]{1,0:T(8,128)S(1)} %get-tuple-element.48), channel_id=1, source_target_pairs={{0,4},{4,0},{8,12},{12,8},{16,20},{20,16},{24,28},{28,24},{1,5},{5... | collective-permute-start | bytes 147464 | tf_op jit(solution)/shard_map/ppermute | solution.py:745
  12.9 0.6 %shard_map.53 = (f32[144,512]{1,0:T(8,128)S(1)}, f32[144,512]{1,0:T(8,128)S(1)}) custom-call(f32[256,256]{1,0:T(8,128)S(1)} %pad_add_fusion.both_ref, f32[128,128]{1,0:T(8,128)S(1)} %get-tuple-element.49.r3_ref, f32[1,512]{1,0:T(1,128)S(1)} %get-tuple-element.51.means_ref, f32[1104,512]{1,0:T(8,128)S(1)} %copy-done), custom_call_target="tpu_custom_call" | custom-call | flops 1000000000 | bytes 1000000 | tf_op jit(solution)/shard_map/pallas_call | solution.py:688
  13.4 3.1 %collective-permute-done.2.gb_ref = f32[32,384]{1,0:T(8,128)S(1)} collective-permute-done((f32[32,384]{1,0:T(8,128)S(1)}, f32[32,384]{1,0:T(8,128)S(1)}, u32[]{:S(2)}, u32[]{:S(2)}) %collective-permute-start.2) | collective-permute-done | bytes 49184 | tf_op jit(solution)/shard_map/ppermute | solution.py:744
  16.5 0.0 collective-permute-done.3.ga_ref
  16.5 1.0 %shard_map.54 = (f32[144,512]{1,0:T(8,128)S(1)}, f32[8,128]{1,0:T(8,128)S(1)}, f32[24,144]{1,0:T(8,128)S(1)}, f32[24,144]{1,0:T(8,128)S(1)}) custom-call(f32[32,384]{1,0:T(8,128)S(1)} %collective-permute-done.2.gb_ref, f32[32,384]{1,0:T(8,128)S(1)} %collective-permute-done.3.ga_ref, f32[144,512]{1,0:T(8,128)S(1)} %get-tuple-element.52.tile_ref, ...), custom_call_target="tpu_custom_call" | custom-call | flops 1000000000 | bytes 1000000 | tf_op jit(solution)/shard_map/pallas_call | solution.py:688
  17.5 0.0 collective-permute-done.4
  17.5 1.5 %collective-permute-start.6 = (f32[32,144]{1,0:T(8,128)S(1)}, f32[32,144]{1,0:T(8,128)S(1)}, u32[]{:S(2)}, u32[]{:S(2)}) collective-permute-start(f32[32,144]{1,0:T(8,128)S(1)} %get-tuple-element.86), channel_id=1, source_target_pairs={{0,3},{1,2},{2,1},{3,0},{4,7},{5,6},{6,5},{7,4},{8,11},{9,10},{10,... | collective-permute-start | bytes 55304 | tf_op jit(solution)/shard_map/ppermute | solution.py:744
  19.0 1.8 %collective-permute-start.5 = (f32[32,144]{1,0:T(8,128)S(1)}, f32[32,144]{1,0:T(8,128)S(1)}, u32[]{:S(2)}, u32[]{:S(2)}) collective-permute-start(f32[32,144]{1,0:T(8,128)S(1)} %get-tuple-element.87), channel_id=1, source_target_pairs={{0,1},{1,0},{2,3},{3,2},{4,5},{5,4},{6,7},{7,6},{8,9},{9,8},{10,11... | collective-permute-start | bytes 55304 | tf_op jit(solution)/shard_map/ppermute | solution.py:745
  20.9 0.8 %shard_map.55 = (f32[144,384]{1,0:T(8,128)S(1)}, f32[160,384]{1,0:T(8,128)S(1)}) custom-call(f32[144,512]{1,0:T(8,128)S(1)} %get-tuple-element.55.t_ref, f32[1104,512]{1,0:T(8,128)S(1)} %copy-done, f32[256,256]{1,0:T(8,128)S(1)} %pad_add_fusion.both_ref, f32[128,128]{1,0:T(8,128)S(1)} %get-tuple-element.56.h3_ref, ...), custom_call_target="tpu_custom_call" | custom-call | flops 1000000000 | bytes 1000000 | tf_op jit(solution)/shard_map/pallas_call | solution.py:688
  21.7 0.7 %collective-permute-done.6.refs_1_ = f32[32,144]{1,0:T(8,128)S(1)} collective-permute-done((f32[32,144]{1,0:T(8,128)S(1)}, f32[32,144]{1,0:T(8,128)S(1)}, u32[]{:S(2)}, u32[]{:S(2)}) %collective-permute-start.6) | collective-permute-done | bytes 18464 | tf_op jit(solution)/shard_map/ppermute | solution.py:744
  22.4 0.7 %collective-permute-done.5.refs_0_ = f32[32,144]{1,0:T(8,128)S(1)} collective-permute-done((f32[32,144]{1,0:T(8,128)S(1)}, f32[32,144]{1,0:T(8,128)S(1)}, u32[]{:S(2)}, u32[]{:S(2)}) %collective-permute-start.5) | collective-permute-done | bytes 18464 | tf_op jit(solution)/shard_map/ppermute | solution.py:745
  23.1 0.2 shard_map.56
  23.3 0.1 collective-permute-start.7
  23.4 0.1 collective-permute-start.8
  23.4 0.7 %shard_map.57 = (f32[96,256]{1,0:T(8,128)S(1)}, f32[96,256]{1,0:T(8,128)S(1)}, f32[144,384]{1,0:T(8,128)S(1)}, f32[144,384]{1,0:T(8,128)S(1)}, f32[16,128]{1,0:T(8,128)S(1)}) custom-call(f32[144,384]{1,0:T(8,128)S(1)} %get-tuple-element.61.y_ref, f32[160,384]{1,0:T(8,128)S(1)} %get-tuple-element.62.m_ref, f32[1104,512]{1,0:T(8,128)S(1)} %copy-done), custom_call_target="tpu_custom_call" | custom-call | flops 1000000000 | bytes 1000000 | tf_op jit(solution)/shard_map/pallas_call | solution.py:688
  24.1 4.6 %collective-permute-done.7.gb_ref = f32[32,384]{1,0:T(8,128)S(1)} collective-permute-done((f32[32,384]{1,0:T(8,128)S(1)}, f32[32,384]{1,0:T(8,128)S(1)}, u32[]{:S(2)}, u32[]{:S(2)}) %collective-permute-start.7) | collective-permute-done | bytes 49184 | tf_op jit(solution)/shard_map/ppermute | solution.py:744
  28.7 0.0 collective-permute-done.8.ga_ref
  28.7 1.3 %shard_map.58 = (f32[128,256]{1,0:T(8,128)S(1)}, f32[128,256]{1,0:T(8,128)S(1)}, f32[144,512]{1,0:T(8,128)S(1)}, f32[16,144]{1,0:T(8,128)S(1)}, f32[16,144]{1,0:T(8,128)S(1)}) custom-call(f32[144,384]{1,0:T(8,128)S(1)} %get-tuple-element.61.y_ref, f32[160,384]{1,0:T(8,128)S(1)} %get-tuple-element.62.m_ref, f32[32,384]{1,0:T(8,128)S(1)} %collective-permute-done.7.gb_ref, ...), custom_call_target="tpu_custom_call" | custom-call | flops 1000000000 | bytes 1000000 | tf_op jit(solution)/shard_map/pallas_call | solution.py:688
  29.9 0.1 collective-permute-start.9
  30.0 3.2 %collective-permute-start.10 = (f32[16,144]{1,0:T(8,128)S(1)}, f32[16,144]{1,0:T(8,128)S(1)}, u32[]{:S(2)}, u32[]{:S(2)}) collective-permute-start(f32[16,144]{1,0:T(8,128)S(1)} %get-tuple-element.76), channel_id=1, source_target_pairs={{0,1},{1,0},{2,3},{3,2},{4,5},{5,4},{6,7},{7,6},{8,9},{9,8},{10,11... | collective-permute-start | bytes 27656 | tf_op jit(solution)/shard_map/ppermute | solution.py:745
  33.2 0.8 %shard_map.59 = (f32[144,384]{1,0:T(8,128)S(1)}, f32[1,128]{1,0:T(1,128)S(1)}) custom-call(f32[144,512]{1,0:T(8,128)S(1)} %get-tuple-element.71.t_ref, f32[1104,512]{1,0:T(8,128)S(1)} %copy-done, f32[256,256]{1,0:T(8,128)S(1)} %pad_add_fusion.both_ref, f32[160,384]{1,0:T(8,128)S(1)} %get-tuple-element.62.m_ref, f32[128,256]{1,0:T(8,128)S(1)} %get-tuple-element.72.z_ref, ...), custom_call_target="tpu_custom_call" | custom-call | flops 1000000000 | bytes 1000000 | tf_op jit(solution)/shard_map/pallas_call | solution.py:688
  34.0 0.0 collective-permute-done.9.refs_0_
  34.0 1.0 %collective-permute-done.10.refs_1_ = f32[16,144]{1,0:T(8,128)S(1)} collective-permute-done((f32[16,144]{1,0:T(8,128)S(1)}, f32[16,144]{1,0:T(8,128)S(1)}, u32[]{:S(2)}, u32[]{:S(2)}) %collective-permute-start.10) | collective-permute-done | bytes 9248 | tf_op jit(solution)/shard_map/ppermute | solution.py:745
  35.1 0.2 shard_map.60
  35.2 1.9 %collective-permute-start.11 = (f32[16,384]{1,0:T(8,128)S(1)}, f32[16,384]{1,0:T(8,128)S(1)}, u32[]{:S(2)}, u32[]{:S(2)}) collective-permute-start(f32[16,384]{1,0:T(8,128)S(1)} %get-tuple-element.78), channel_id=1, source_target_pairs={{0,1},{1,0},{2,3},{3,2},{4,8},{5,9},{6,10},{7,11},{8,4},{9,5},{10,... | collective-permute-start | bytes 73736 | tf_op jit(solution)/shard_map/ppermute | solution.py:744
  37.2 0.0 collective-permute-start.12
  37.2 0.4 shard_map.61
  37.5 1.6 %collective-permute-done.11.gb_ref = f32[16,384]{1,0:T(8,128)S(1)} collective-permute-done((f32[16,384]{1,0:T(8,128)S(1)}, f32[16,384]{1,0:T(8,128)S(1)}, u32[]{:S(2)}, u32[]{:S(2)}) %collective-permute-start.11) | collective-permute-done | bytes 24608 | tf_op jit(solution)/shard_map/ppermute | solution.py:744
  39.1 0.0 collective-permute-done.12.ga_ref
  39.1 0.3 shard_map.62
  39.4 9.2 %all_to_all.11 = f32[32,1,128]{2,1,0:T(1,128)S(1)} all-to-all(f32[32,1,128]{2,1,0:T(1,128)S(1)} %bitcast.5), channel_id=1, replica_groups=mesh['row'=8,'col'=4] {'row','col'}, dimensions={0} | all-to-all | bytes 32768 | tf_op jit(solution)/shard_map/all_to_all | solution.py:855
  48.6 1.3 %shard_map.63 = (f32[128,256]{1,0:T(8,128)}, f32[128,256]{1,0:T(8,128)}) custom-call(f32[32,128]{1,0:T(8,128)S(1)} %bitcast.4, f32[1104,512]{1,0:T(8,128)S(1)} %copy-done, f32[160,384]{1,0:T(8,128)S(1)} %get-tuple-element.62.m_ref, f32[96,256]{1,0:T(8,128)S(1)} %get-tuple-element.67.f_ref, f32[256,256]{1,0:T(8,128)S(1)} %pad_add_fusion.both_ref, ...), custom_call_target="tpu_custom_call" | custom-call | flops 1000000000 | bytes 1000000 | tf_op jit(solution)/shard_map/pallas_call | solution.py:688
  (2 shorter events, 0.0 us)
Async XLA Ops:
  1.8 6.7 %copy-start = (f32[1104,512]{1,0:T(8,128)S(1)}, f32[1104,512]{1,0:T(8,128)}, u32[]{:S(2)}) copy-start(f32[1104,512]{1,0:T(8,128)} %constant.6.clone.basis_ref) | copy-start | bytes 6782980
  1.8 4.5 %collective-permute-start = (f32[40,128]{1,0:T(8,128)S(1)}, f32[40,128]{1,0:T(8,128)S(1)}, u32[]{:S(2)}, u32[]{:S(2)}) collective-permute-start(f32[40,128]{1,0:T(8,128)S(1)} %get-tuple-element.45), channel_id=1, source_target_pairs={{0,4},{1,2},{2,1},{3,7},{4,0},{5,6},{6,5},{7,3},{8,12},{9,10},{10,... | collective-permute-start | bytes 61448 | tf_op jit(solution)/shard_map/ppermute | solution.py:744
  2.3 6.0 %collective-permute-start.1 = (f32[40,128]{1,0:T(8,128)S(1)}, f32[40,128]{1,0:T(8,128)S(1)}, u32[]{:S(2)}, u32[]{:S(2)}) collective-permute-start(f32[40,128]{1,0:T(8,128)S(1)} %get-tuple-element.46), channel_id=1, source_target_pairs={{0,1},{1,0},{2,3},{3,2},{4,5},{5,4},{6,7},{7,6},{8,9},{9,8},{10,11... | collective-permute-start | bytes 61448 | tf_op jit(solution)/shard_map/ppermute | solution.py:745
  8.6 8.9 %collective-permute-start.4 = (f32[8,128]{1,0:T(8,128)S(1)}, f32[8,128]{1,0:T(8,128)S(1)}, u32[]{:S(2)}, u32[]{:S(2)}) collective-permute-start(f32[8,128]{1,0:T(8,128)S(1)} %get-tuple-element.54.table_ref), channel_id=1, source_target_pairs={{0,16},{1,17},{2,18},{3,19},{4,20},{5,21},{6,22},{7,23},{8,24},{9,... | collective-permute-start | bytes 12296 | tf_op jit(solution)/shard_map/ppermute | solution.py:748
  11.2 5.3 %collective-permute-start.2 = (f32[32,384]{1,0:T(8,128)S(1)}, f32[32,384]{1,0:T(8,128)S(1)}, u32[]{:S(2)}, u32[]{:S(2)}) collective-permute-start(f32[32,384]{1,0:T(8,128)S(1)} %get-tuple-element.47), channel_id=1, source_target_pairs={{0,28},{1,29},{2,30},{3,31},{4,8},{5,9},{6,10},{7,11},{8,4},{9,5},... | collective-permute-start | bytes 147464 | tf_op jit(solution)/shard_map/ppermute | solution.py:744
  11.2 5.3 %collective-permute-start.3 = (f32[32,384]{1,0:T(8,128)S(1)}, f32[32,384]{1,0:T(8,128)S(1)}, u32[]{:S(2)}, u32[]{:S(2)}) collective-permute-start(f32[32,384]{1,0:T(8,128)S(1)} %get-tuple-element.48), channel_id=1, source_target_pairs={{0,4},{4,0},{8,12},{12,8},{16,20},{20,16},{24,28},{28,24},{1,5},{5... | collective-permute-start | bytes 147464 | tf_op jit(solution)/shard_map/ppermute | solution.py:745
  17.5 4.9 %collective-permute-start.6 = (f32[32,144]{1,0:T(8,128)S(1)}, f32[32,144]{1,0:T(8,128)S(1)}, u32[]{:S(2)}, u32[]{:S(2)}) collective-permute-start(f32[32,144]{1,0:T(8,128)S(1)} %get-tuple-element.86), channel_id=1, source_target_pairs={{0,3},{1,2},{2,1},{3,0},{4,7},{5,6},{6,5},{7,4},{8,11},{9,10},{10,... | collective-permute-start | bytes 55304 | tf_op jit(solution)/shard_map/ppermute | solution.py:744
  19.0 4.0 %collective-permute-start.5 = (f32[32,144]{1,0:T(8,128)S(1)}, f32[32,144]{1,0:T(8,128)S(1)}, u32[]{:S(2)}, u32[]{:S(2)}) collective-permute-start(f32[32,144]{1,0:T(8,128)S(1)} %get-tuple-element.87), channel_id=1, source_target_pairs={{0,1},{1,0},{2,3},{3,2},{4,5},{5,4},{6,7},{7,6},{8,9},{9,8},{10,11... | collective-permute-start | bytes 55304 | tf_op jit(solution)/shard_map/ppermute | solution.py:745
  23.3 5.4 %collective-permute-start.7 = (f32[32,384]{1,0:T(8,128)S(1)}, f32[32,384]{1,0:T(8,128)S(1)}, u32[]{:S(2)}, u32[]{:S(2)}) collective-permute-start(f32[32,384]{1,0:T(8,128)S(1)} %get-tuple-element.63), channel_id=1, source_target_pairs={{0,28},{1,29},{2,30},{3,31},{4,8},{5,9},{6,10},{7,11},{8,4},{9,5},... | collective-permute-start | bytes 147464 | tf_op jit(solution)/shard_map/ppermute | solution.py:744
  23.4 5.3 %collective-permute-start.8 = (f32[32,384]{1,0:T(8,128)S(1)}, f32[32,384]{1,0:T(8,128)S(1)}, u32[]{:S(2)}, u32[]{:S(2)}) collective-permute-start(f32[32,384]{1,0:T(8,128)S(1)} %get-tuple-element.64), channel_id=1, source_target_pairs={{0,4},{4,0},{8,12},{12,8},{16,20},{20,16},{24,28},{28,24},{1,5},{5... | collective-permute-start | bytes 147464 | tf_op jit(solution)/shard_map/ppermute | solution.py:745
  29.9 4.1 %collective-permute-start.9 = (f32[16,144]{1,0:T(8,128)S(1)}, f32[16,144]{1,0:T(8,128)S(1)}, u32[]{:S(2)}, u32[]{:S(2)}) collective-permute-start(f32[16,144]{1,0:T(8,128)S(1)} %get-tuple-element.75), channel_id=1, source_target_pairs={{0,4},{1,2},{2,1},{3,7},{4,0},{5,6},{6,5},{7,3},{8,12},{9,10},{10,... | collective-permute-start | bytes 27656 | tf_op jit(solution)/shard_map/ppermute | solution.py:744
  30.0 5.0 %collective-permute-start.10 = (f32[16,144]{1,0:T(8,128)S(1)}, f32[16,144]{1,0:T(8,128)S(1)}, u32[]{:S(2)}, u32[]{:S(2)}) collective-permute-start(f32[16,144]{1,0:T(8,128)S(1)} %get-tuple-element.76), channel_id=1, source_target_pairs={{0,1},{1,0},{2,3},{3,2},{4,5},{5,4},{6,7},{7,6},{8,9},{9,8},{10,11... | collective-permute-start | bytes 27656 | tf_op jit(solution)/shard_map/ppermute | solution.py:745
  35.2 3.9 %collective-permute-start.11 = (f32[16,384]{1,0:T(8,128)S(1)}, f32[16,384]{1,0:T(8,128)S(1)}, u32[]{:S(2)}, u32[]{:S(2)}) collective-permute-start(f32[16,384]{1,0:T(8,128)S(1)} %get-tuple-element.78), channel_id=1, source_target_pairs={{0,1},{1,0},{2,3},{3,2},{4,8},{5,9},{6,10},{7,11},{8,4},{9,5},{10,... | collective-permute-start | bytes 73736 | tf_op jit(solution)/shard_map/ppermute | solution.py:744
  37.2 2.0 %collective-permute-start.12 = (f32[16,384]{1,0:T(8,128)S(1)}, f32[16,384]{1,0:T(8,128)S(1)}, u32[]{:S(2)}, u32[]{:S(2)}) collective-permute-start(f32[16,384]{1,0:T(8,128)S(1)} %get-tuple-element.79), channel_id=1, source_target_pairs={{0,4},{4,0},{8,12},{12,8},{16,20},{20,16},{24,28},{28,24},{1,5},{5... | collective-permute-start | bytes 73736 | tf_op jit(solution)/shard_map/ppermute | solution.py:745

commit v14 on v12

--- a/solution.py
+++ b/solution.py
@@ -180,22 +180,16 @@
     return row
 
 
-def coarse_values(c_row, inverse):
-    return dot(jnp.broadcast_to(c_row, (8, c_row.shape[1])), inverse)[:1]
-
-
-def band_rows(g_row, counts):
+def near_inverse(counts, inverse):
     i, j = place()
     nr, nc = counts[0], 2 * counts[1]
-    shape = (16, g_row.shape[1])
+    shape = (16, inverse.shape[0])
     which = rows_of(shape)
     r = i - 1 + which // 4
     c = 2 * j - 1 + which % 4
     inside = (r >= 0) & (r < nr) & (c >= 0) & (c < nc) & (which < 12)
     at = lax.rem(c + 2, 2) * (nr * counts[1]) + r * counts[1] + (c + 2) // 2 - 1
-    picked = jnp.where(inside & (lanes_of(shape) == at), g_row, 0.0)
-    picked = jnp.sum(picked, axis=1, keepdims=True)
-    return as_bands([picked[k : k + 1] for k in range(12)])
+    return dot(jnp.where(inside & (lanes_of(shape) == at), 1.0, 0.0), inverse)
 
 
 def as_bands(values):
@@ -469,7 +463,7 @@
     send(i, a_ref, b_ref, *strips)
 
 
-def inner_kernel(counts, y_ref, m_ref, basis_ref, w_ref, f_ref, gw_ref, gf_ref):
+def inner_kernel(counts, width, y_ref, m_ref, basis_ref, w_ref, f_ref, gw_ref, gf_ref, near_ref):
     mask = column_mask(counts)
     s = jnp.where(mask, y_ref[8:120], 0.0)
     m = m_ref[8:120]
@@ -481,6 +475,7 @@
     f_ref[...] = f[:, :TC]
     gw_ref[...] = row_transform(w, basis_ref, inner_rows)
     gf_ref[...] = row_transform(f, basis_ref, inner_rows)
+    near_ref[...] = near_inverse(counts, coarse_part(basis_ref, width))
 
 
 def second_kernel(
@@ -495,6 +490,7 @@
     f_ref,
     gw_ref,
     gf_ref,
+    near_ref,
     weights_ref,
     basis_ref,
     z_ref,
@@ -509,8 +505,8 @@
     s = edges(y, *sides(i, counts[0], ga_ref[:24], gb_ref[:24]))
     s = jnp.where(mask, s, 0.0)
     table = merged(table_ref[...], ga_ref[24:, :128], gb_ref[24:, :128])
-    g = coarse_values(as_row(table, width), coarse_part(basis_ref, width))
-    bands = band_rows(g, counts)
+    picked = jnp.sum(near_ref[...] * as_row(table, width), axis=1, keepdims=True)
+    bands = as_bands([picked[k : k + 1] for k in range(12)])
     coarse = edge_bands(bands)
     m = edge_part(m_ref)
     flow = m * (lap(s) + lap(coarse))
@@ -800,9 +796,9 @@
         table,
     )
     ga, gb = swap(a, b, "row")
-    inner_w, f, gw, gf = call(
-        functools.partial(inner_kernel, counts),
-        [(96, TC)] * 2 + [(EXT, FC)] * 2,
+    inner_w, f, gw, gf, near = call(
+        functools.partial(inner_kernel, counts, width),
+        [(96, TC)] * 2 + [(EXT, FC)] * 2 + [(16, width)],
         y,
         m,
         basis,
@@ -819,6 +815,7 @@
         f,
         gw,
         gf,
+        near,
         weight,
         basis,
     )

time: 47.8 us -> 47.7 us (level)
  no operation moved by 1% of the time
where the time goes in v14:
time: 47.7 us; the launch traced here: 47.5 us
  starting transfers between devices  17.6 us (37%)
  waiting for transfers between devices  11.1 us (23%)
  blocking collectives  9.2 us (19%)
  Pallas kernels  7.86 us (16%)
  other arithmetic  1 us (2%)
  between operations  0.75 us (2%)
    all_to_all x1, blocking collectives, body(): stats = lax.all_to_all(stats, both_axes, 0, 0, tiled=True)  9.2 us
    ppermute x6, starting transfers between devices, swap(): lax.ppermute(b, both_axes, odd_pairs(counts, both_axes.index(axis), bit))  8.83 us
    pallas_call x14, Pallas kernels, call(): pl.pallas_call(kernel, out_shape=shapes, compiler_params=pltpu.CompilerPa...  7.86 us
    ppermute x6, waiting for transfers between devices, swap(): lax.ppermute(b, both_axes, odd_pairs(counts, both_axes.index(axis), bit))  6.5 us
    ppermute x6, starting transfers between devices, swap(): return (lax.ppermute(a, axis, pairs_from(lax.axis_size(axis), 0)), gb)  6.37 us
    ppermute x6, waiting for transfers between devices, swap(): return (lax.ppermute(a, axis, pairs_from(lax.axis_size(axis), 0)), gb)  4.48 us
    ppermute x1, starting transfers between devices, small_swap(): return lax.ppermute(x, both_axes, xor_pairs(counts, rows, cols))  2.43 us
    add x1, other arithmetic, body(): jnp.pad(noise, ((0, TR), (0, 0))) + jnp.pad(height, ((TR, 0), (0, 0)))  0.99 us
  transfers between devices with their start and end apart: 13, of which 8 were waited for; matrix products, arithmetic and copies ran while one was open for 0% of the time, Pallas kernels for 9%

profile of v14, /device:TPU:0, one launch (start us, length us, event | category | flops | bytes accessed | tf_op | source)
XLA Modules:
  0.0 47.5 jit_solution(3991134578797389355)
XLA Ops:
  0.6 1.0 %pad_add_fusion.both_ref = f32[256,256]{1,0:T(8,128)S(1)} fusion(f32[128,256]{1,0:T(8,128)} %param.3, f32[128,256]{1,0:T(8,128)} %param.4), kind=kLoop, calls=%fused_computation | loop fusion | flops 65536 | bytes 524288 | tf_op jit(solution)/shard_map/add | solution.py:744
  1.6 0.2 shard_map.50
  1.8 0.0 copy-start
  1.8 4.0 %collective-permute-start = (f32[40,128]{1,0:T(8,128)S(1)}, f32[40,128]{1,0:T(8,128)S(1)}, u32[]{:S(2)}, u32[]{:S(2)}) collective-permute-start(f32[40,128]{1,0:T(8,128)S(1)} %get-tuple-element.43), channel_id=1, source_target_pairs={{0,3},{1,2},{2,1},{3,0},{4,7},{5,6},{6,5},{7,4},{8,11},{9,10},{10,... | collective-permute-start | bytes 61448 | tf_op jit(solution)/shard_map/ppermute | solution.py:738
  5.8 0.5 %collective-permute-start.1 = (f32[40,128]{1,0:T(8,128)S(1)}, f32[40,128]{1,0:T(8,128)S(1)}, u32[]{:S(2)}, u32[]{:S(2)}) collective-permute-start(f32[40,128]{1,0:T(8,128)S(1)} %get-tuple-element.44), channel_id=1, source_target_pairs={{0,1},{1,0},{2,3},{3,2},{4,5},{5,4},{6,7},{7,6},{8,9},{9,8},{10,11... | collective-permute-start | bytes 61448 | tf_op jit(solution)/shard_map/ppermute | solution.py:739
  6.3 1.2 %collective-permute-done.gb_ref = f32[40,128]{1,0:T(8,128)S(1)} collective-permute-done((f32[40,128]{1,0:T(8,128)S(1)}, f32[40,128]{1,0:T(8,128)S(1)}, u32[]{:S(2)}, u32[]{:S(2)}) %collective-permute-start) | collective-permute-done | bytes 20512 | tf_op jit(solution)/shard_map/ppermute | solution.py:738
  7.5 2.0 %collective-permute-done.1.ga_ref = f32[40,128]{1,0:T(8,128)S(1)} collective-permute-done((f32[40,128]{1,0:T(8,128)S(1)}, f32[40,128]{1,0:T(8,128)S(1)}, u32[]{:S(2)}, u32[]{:S(2)}) %collective-permute-start.1) | collective-permute-done | bytes 20512 | tf_op jit(solution)/shard_map/ppermute | solution.py:739
  9.5 0.2 shard_map.51
  9.7 2.0 %collective-permute-start.2 = (f32[32,384]{1,0:T(8,128)S(1)}, f32[32,384]{1,0:T(8,128)S(1)}, u32[]{:S(2)}, u32[]{:S(2)}) collective-permute-start(f32[32,384]{1,0:T(8,128)S(1)} %get-tuple-element.45), channel_id=1, source_target_pairs={{0,28},{1,29},{2,30},{3,31},{4,8},{5,9},{6,10},{7,11},{8,4},{9,5},... | collective-permute-start | bytes 147464 | tf_op jit(solution)/shard_map/ppermute | solution.py:738
  11.7 0.0 collective-permute-start.3
  11.7 0.0 copy-done
  11.7 0.1 shard_map.53
  11.9 2.4 %collective-permute-start.4 = (f32[8,128]{1,0:T(8,128)S(1)}, f32[8,128]{1,0:T(8,128)S(1)}, u32[]{:S(2)}, u32[]{:S(2)}) collective-permute-start(f32[8,128]{1,0:T(8,128)S(1)} %get-tuple-element.50.table_ref), channel_id=1, source_target_pairs={{0,16},{1,17},{2,18},{3,19},{4,20},{5,21},{6,22},{7,23},{8,24},{9,... | collective-permute-start | bytes 12296 | tf_op jit(solution)/shard_map/ppermute | solution.py:742
  14.3 0.6 %shard_map.52.tile_ref = f32[144,512]{1,0:T(8,128)S(1)} custom-call(f32[256,256]{1,0:T(8,128)S(1)} %pad_add_fusion.both_ref, f32[128,128]{1,0:T(8,128)S(1)} %get-tuple-element.47.r3_ref, f32[1104,512]{1,0:T(8,128)S(1)} %copy-done), custom_call_target="tpu_custom_call" | custom-call | flops 1000000000 | bytes 1000000 | tf_op jit(solution)/shard_map/pallas_call | solution.py:683
  14.9 0.5 %collective-permute-done.2.gb_ref = f32[32,384]{1,0:T(8,128)S(1)} collective-permute-done((f32[32,384]{1,0:T(8,128)S(1)}, f32[32,384]{1,0:T(8,128)S(1)}, u32[]{:S(2)}, u32[]{:S(2)}) %collective-permute-start.2) | collective-permute-done | bytes 49184 | tf_op jit(solution)/shard_map/ppermute | solution.py:738
  15.4 0.0 collective-permute-done.3.ga_ref
  15.4 1.0 %shard_map.54 = (f32[144,512]{1,0:T(8,128)S(1)}, f32[8,128]{1,0:T(8,128)S(1)}, f32[24,144]{1,0:T(8,128)S(1)}, f32[24,144]{1,0:T(8,128)S(1)}) custom-call(f32[32,384]{1,0:T(8,128)S(1)} %collective-permute-done.2.gb_ref, f32[32,384]{1,0:T(8,128)S(1)} %collective-permute-done.3.ga_ref, f32[144,512]{1,0:T(8,128)S(1)} %shard_map.52.tile_ref, ...), custom_call_target="tpu_custom_call" | custom-call | flops 1000000000 | bytes 1000000 | tf_op jit(solution)/shard_map/pallas_call | solution.py:683
  16.4 0.1 collective-permute-done.4
  16.5 0.1 collective-permute-start.6
  16.6 1.9 %collective-permute-start.5 = (f32[32,144]{1,0:T(8,128)S(1)}, f32[32,144]{1,0:T(8,128)S(1)}, u32[]{:S(2)}, u32[]{:S(2)}) collective-permute-start(f32[32,144]{1,0:T(8,128)S(1)} %get-tuple-element.83), channel_id=1, source_target_pairs={{0,1},{1,0},{2,3},{3,2},{4,5},{5,4},{6,7},{7,6},{8,9},{9,8},{10,11... | collective-permute-start | bytes 55304 | tf_op jit(solution)/shard_map/ppermute | solution.py:739
  18.5 0.8 %shard_map.55 = (f32[144,384]{1,0:T(8,128)S(1)}, f32[160,384]{1,0:T(8,128)S(1)}) custom-call(f32[144,512]{1,0:T(8,128)S(1)} %get-tuple-element.51.t_ref, f32[1104,512]{1,0:T(8,128)S(1)} %copy-done, f32[256,256]{1,0:T(8,128)S(1)} %pad_add_fusion.both_ref, f32[128,128]{1,0:T(8,128)S(1)} %get-tuple-element.52.h3_ref, ...), custom_call_target="tpu_custom_call" | custom-call | flops 1000000000 | bytes 1000000 | tf_op jit(solution)/shard_map/pallas_call | solution.py:683
  19.3 0.0 collective-permute-done.6.refs_1_
  19.3 1.4 %collective-permute-done.5.refs_0_ = f32[32,144]{1,0:T(8,128)S(1)} collective-permute-done((f32[32,144]{1,0:T(8,128)S(1)}, f32[32,144]{1,0:T(8,128)S(1)}, u32[]{:S(2)}, u32[]{:S(2)}) %collective-permute-start.5) | collective-permute-done | bytes 18464 | tf_op jit(solution)/shard_map/ppermute | solution.py:739
  20.7 0.2 shard_map.56
  20.9 0.8 %collective-permute-start.7 = (f32[32,384]{1,0:T(8,128)S(1)}, f32[32,384]{1,0:T(8,128)S(1)}, u32[]{:S(2)}, u32[]{:S(2)}) collective-permute-start(f32[32,384]{1,0:T(8,128)S(1)} %get-tuple-element.59), channel_id=1, source_target_pairs={{0,28},{1,29},{2,30},{3,31},{4,8},{5,9},{6,10},{7,11},{8,4},{9,5},... | collective-permute-start | bytes 147464 | tf_op jit(solution)/shard_map/ppermute | solution.py:738
  21.7 0.8 %collective-permute-start.8 = (f32[32,384]{1,0:T(8,128)S(1)}, f32[32,384]{1,0:T(8,128)S(1)}, u32[]{:S(2)}, u32[]{:S(2)}) collective-permute-start(f32[32,384]{1,0:T(8,128)S(1)} %get-tuple-element.60), channel_id=1, source_target_pairs={{0,4},{4,0},{8,12},{12,8},{16,20},{20,16},{24,28},{28,24},{1,5},{5... | collective-permute-start | bytes 147464 | tf_op jit(solution)/shard_map/ppermute | solution.py:739
  22.5 0.7 %shard_map.57 = (f32[96,256]{1,0:T(8,128)S(1)}, f32[96,256]{1,0:T(8,128)S(1)}, f32[144,384]{1,0:T(8,128)S(1)}, f32[144,384]{1,0:T(8,128)S(1)}, f32[16,128]{1,0:T(8,128)S(1)}) custom-call(f32[144,384]{1,0:T(8,128)S(1)} %get-tuple-element.57.y_ref, f32[160,384]{1,0:T(8,128)S(1)} %get-tuple-element.58.m_ref, f32[1104,512]{1,0:T(8,128)S(1)} %copy-done), custom_call_target="tpu_custom_call" | custom-call | flops 1000000000 | bytes 1000000 | tf_op jit(solution)/shard_map/pallas_call | solution.py:683
  23.1 3.2 %collective-permute-done.7.gb_ref = f32[32,384]{1,0:T(8,128)S(1)} collective-permute-done((f32[32,384]{1,0:T(8,128)S(1)}, f32[32,384]{1,0:T(8,128)S(1)}, u32[]{:S(2)}, u32[]{:S(2)}) %collective-permute-start.7) | collective-permute-done | bytes 49184 | tf_op jit(solution)/shard_map/ppermute | solution.py:738
  26.3 0.0 collective-permute-done.8.ga_ref
  26.3 1.3 %shard_map.58 = (f32[128,256]{1,0:T(8,128)S(1)}, f32[128,256]{1,0:T(8,128)S(1)}, f32[144,512]{1,0:T(8,128)S(1)}, f32[16,144]{1,0:T(8,128)S(1)}, f32[16,144]{1,0:T(8,128)S(1)}) custom-call(f32[144,384]{1,0:T(8,128)S(1)} %get-tuple-element.57.y_ref, f32[160,384]{1,0:T(8,128)S(1)} %get-tuple-element.58.m_ref, f32[32,384]{1,0:T(8,128)S(1)} %collective-permute-done.7.gb_ref, ...), custom_call_target="tpu_custom_call" | custom-call | flops 1000000000 | bytes 1000000 | tf_op jit(solution)/shard_map/pallas_call | solution.py:683
  27.5 0.1 collective-permute-start.9
  27.6 3.2 %collective-permute-start.10 = (f32[16,144]{1,0:T(8,128)S(1)}, f32[16,144]{1,0:T(8,128)S(1)}, u32[]{:S(2)}, u32[]{:S(2)}) collective-permute-start(f32[16,144]{1,0:T(8,128)S(1)} %get-tuple-element.72), channel_id=1, source_target_pairs={{0,1},{1,0},{2,3},{3,2},{4,5},{5,4},{6,7},{7,6},{8,9},{9,8},{10,11... | collective-permute-start | bytes 27656 | tf_op jit(solution)/shard_map/ppermute | solution.py:739
  30.8 0.8 %shard_map.59 = (f32[144,384]{1,0:T(8,128)S(1)}, f32[1,128]{1,0:T(1,128)S(1)}) custom-call(f32[144,512]{1,0:T(8,128)S(1)} %get-tuple-element.67.t_ref, f32[1104,512]{1,0:T(8,128)S(1)} %copy-done, f32[256,256]{1,0:T(8,128)S(1)} %pad_add_fusion.both_ref, f32[160,384]{1,0:T(8,128)S(1)} %get-tuple-element.58.m_ref, f32[128,256]{1,0:T(8,128)S(1)} %get-tuple-element.68.z_ref, ...), custom_call_target="tpu_custom_call" | custom-call | flops 1000000000 | bytes 1000000 | tf_op jit(solution)/shard_map/pallas_call | solution.py:683
  31.6 0.0 collective-permute-done.9.refs_0_
  31.6 1.1 %collective-permute-done.10.refs_1_ = f32[16,144]{1,0:T(8,128)S(1)} collective-permute-done((f32[16,144]{1,0:T(8,128)S(1)}, f32[16,144]{1,0:T(8,128)S(1)}, u32[]{:S(2)}, u32[]{:S(2)}) %collective-permute-start.10) | collective-permute-done | bytes 9248 | tf_op jit(solution)/shard_map/ppermute | solution.py:739
  32.7 0.2 shard_map.60
  32.9 1.9 %collective-permute-start.11 = (f32[16,384]{1,0:T(8,128)S(1)}, f32[16,384]{1,0:T(8,128)S(1)}, u32[]{:S(2)}, u32[]{:S(2)}) collective-permute-start(f32[16,384]{1,0:T(8,128)S(1)} %get-tuple-element.74), channel_id=1, source_target_pairs={{0,1},{1,0},{2,3},{3,2},{4,8},{5,9},{6,10},{7,11},{8,4},{9,5},{10,... | collective-permute-start | bytes 73736 | tf_op jit(solution)/shard_map/ppermute | solution.py:738
  34.8 0.0 collective-permute-start.12
  34.8 0.4 shard_map.61
  35.1 1.6 %collective-permute-done.11.gb_ref = f32[16,384]{1,0:T(8,128)S(1)} collective-permute-done((f32[16,384]{1,0:T(8,128)S(1)}, f32[16,384]{1,0:T(8,128)S(1)}, u32[]{:S(2)}, u32[]{:S(2)}) %collective-permute-start.11) | collective-permute-done | bytes 24608 | tf_op jit(solution)/shard_map/ppermute | solution.py:738
  36.7 0.0 collective-permute-done.12.ga_ref
  36.7 0.3 shard_map.62
  37.0 9.2 %all_to_all.11 = f32[32,1,128]{2,1,0:T(1,128)S(1)} all-to-all(f32[32,1,128]{2,1,0:T(1,128)S(1)} %bitcast.5), channel_id=1, replica_groups=mesh['row'=8,'col'=4] {'row','col'}, dimensions={0} | all-to-all | bytes 32768 | tf_op jit(solution)/shard_map/all_to_all | solution.py:849
  46.2 1.3 %shard_map.63 = (f32[128,256]{1,0:T(8,128)}, f32[128,256]{1,0:T(8,128)}) custom-call(f32[32,128]{1,0:T(8,128)S(1)} %bitcast.4, f32[1104,512]{1,0:T(8,128)S(1)} %copy-done, f32[160,384]{1,0:T(8,128)S(1)} %get-tuple-element.58.m_ref, f32[96,256]{1,0:T(8,128)S(1)} %get-tuple-element.63.f_ref, f32[256,256]{1,0:T(8,128)S(1)} %pad_add_fusion.both_ref, ...), custom_call_target="tpu_custom_call" | custom-call | flops 1000000000 | bytes 1000000 | tf_op jit(solution)/shard_map/pallas_call | solution.py:683
  (2 shorter events, 0.0 us)
Async XLA Ops:
  1.8 9.9 %copy-start = (f32[1104,512]{1,0:T(8,128)S(1)}, f32[1104,512]{1,0:T(8,128)}, u32[]{:S(2)}) copy-start(f32[1104,512]{1,0:T(8,128)} %constant.6.clone.basis_ref) | copy-start | bytes 6782980
  1.8 5.7 %collective-permute-start = (f32[40,128]{1,0:T(8,128)S(1)}, f32[40,128]{1,0:T(8,128)S(1)}, u32[]{:S(2)}, u32[]{:S(2)}) collective-permute-start(f32[40,128]{1,0:T(8,128)S(1)} %get-tuple-element.43), channel_id=1, source_target_pairs={{0,3},{1,2},{2,1},{3,0},{4,7},{5,6},{6,5},{7,4},{8,11},{9,10},{10,... | collective-permute-start | bytes 61448 | tf_op jit(solution)/shard_map/ppermute | solution.py:738
  5.8 3.8 %collective-permute-start.1 = (f32[40,128]{1,0:T(8,128)S(1)}, f32[40,128]{1,0:T(8,128)S(1)}, u32[]{:S(2)}, u32[]{:S(2)}) collective-permute-start(f32[40,128]{1,0:T(8,128)S(1)} %get-tuple-element.44), channel_id=1, source_target_pairs={{0,1},{1,0},{2,3},{3,2},{4,5},{5,4},{6,7},{7,6},{8,9},{9,8},{10,11... | collective-permute-start | bytes 61448 | tf_op jit(solution)/shard_map/ppermute | solution.py:739
  9.7 5.6 %collective-permute-start.2 = (f32[32,384]{1,0:T(8,128)S(1)}, f32[32,384]{1,0:T(8,128)S(1)}, u32[]{:S(2)}, u32[]{:S(2)}) collective-permute-start(f32[32,384]{1,0:T(8,128)S(1)} %get-tuple-element.45), channel_id=1, source_target_pairs={{0,28},{1,29},{2,30},{3,31},{4,8},{5,9},{6,10},{7,11},{8,4},{9,5},... | collective-permute-start | bytes 147464 | tf_op jit(solution)/shard_map/ppermute | solution.py:738
  11.7 3.7 %collective-permute-start.3 = (f32[32,384]{1,0:T(8,128)S(1)}, f32[32,384]{1,0:T(8,128)S(1)}, u32[]{:S(2)}, u32[]{:S(2)}) collective-permute-start(f32[32,384]{1,0:T(8,128)S(1)} %get-tuple-element.46), channel_id=1, source_target_pairs={{0,4},{4,0},{8,12},{12,8},{16,20},{20,16},{24,28},{28,24},{1,5},{5... | collective-permute-start | bytes 147464 | tf_op jit(solution)/shard_map/ppermute | solution.py:739
  11.9 4.6 %collective-permute-start.4 = (f32[8,128]{1,0:T(8,128)S(1)}, f32[8,128]{1,0:T(8,128)S(1)}, u32[]{:S(2)}, u32[]{:S(2)}) collective-permute-start(f32[8,128]{1,0:T(8,128)S(1)} %get-tuple-element.50.table_ref), channel_id=1, source_target_pairs={{0,16},{1,17},{2,18},{3,19},{4,20},{5,21},{6,22},{7,23},{8,24},{9,... | collective-permute-start | bytes 12296 | tf_op jit(solution)/shard_map/ppermute | solution.py:742
  16.5 2.8 %collective-permute-start.6 = (f32[32,144]{1,0:T(8,128)S(1)}, f32[32,144]{1,0:T(8,128)S(1)}, u32[]{:S(2)}, u32[]{:S(2)}) collective-permute-start(f32[32,144]{1,0:T(8,128)S(1)} %get-tuple-element.82), channel_id=1, source_target_pairs={{0,4},{1,2},{2,1},{3,7},{4,0},{5,6},{6,5},{7,3},{8,12},{9,10},{10,... | collective-permute-start | bytes 55304 | tf_op jit(solution)/shard_map/ppermute | solution.py:738
  16.6 4.2 %collective-permute-start.5 = (f32[32,144]{1,0:T(8,128)S(1)}, f32[32,144]{1,0:T(8,128)S(1)}, u32[]{:S(2)}, u32[]{:S(2)}) collective-permute-start(f32[32,144]{1,0:T(8,128)S(1)} %get-tuple-element.83), channel_id=1, source_target_pairs={{0,1},{1,0},{2,3},{3,2},{4,5},{5,4},{6,7},{7,6},{8,9},{9,8},{10,11... | collective-permute-start | bytes 55304 | tf_op jit(solution)/shard_map/ppermute | solution.py:739
  20.9 5.4 %collective-permute-start.7 = (f32[32,384]{1,0:T(8,128)S(1)}, f32[32,384]{1,0:T(8,128)S(1)}, u32[]{:S(2)}, u32[]{:S(2)}) collective-permute-start(f32[32,384]{1,0:T(8,128)S(1)} %get-tuple-element.59), channel_id=1, source_target_pairs={{0,28},{1,29},{2,30},{3,31},{4,8},{5,9},{6,10},{7,11},{8,4},{9,5},... | collective-permute-start | bytes 147464 | tf_op jit(solution)/shard_map/ppermute | solution.py:738
  21.7 4.6 %collective-permute-start.8 = (f32[32,384]{1,0:T(8,128)S(1)}, f32[32,384]{1,0:T(8,128)S(1)}, u32[]{:S(2)}, u32[]{:S(2)}) collective-permute-start(f32[32,384]{1,0:T(8,128)S(1)} %get-tuple-element.60), channel_id=1, source_target_pairs={{0,4},{4,0},{8,12},{12,8},{16,20},{20,16},{24,28},{28,24},{1,5},{5... | collective-permute-start | bytes 147464 | tf_op jit(solution)/shard_map/ppermute | solution.py:739
  27.5 4.1 %collective-permute-start.9 = (f32[16,144]{1,0:T(8,128)S(1)}, f32[16,144]{1,0:T(8,128)S(1)}, u32[]{:S(2)}, u32[]{:S(2)}) collective-permute-start(f32[16,144]{1,0:T(8,128)S(1)} %get-tuple-element.71), channel_id=1, source_target_pairs={{0,4},{1,2},{2,1},{3,7},{4,0},{5,6},{6,5},{7,3},{8,12},{9,10},{10,... | collective-permute-start | bytes 27656 | tf_op jit(solution)/shard_map/ppermute | solution.py:738
  27.6 5.0 %collective-permute-start.10 = (f32[16,144]{1,0:T(8,128)S(1)}, f32[16,144]{1,0:T(8,128)S(1)}, u32[]{:S(2)}, u32[]{:S(2)}) collective-permute-start(f32[16,144]{1,0:T(8,128)S(1)} %get-tuple-element.72), channel_id=1, source_target_pairs={{0,1},{1,0},{2,3},{3,2},{4,5},{5,4},{6,7},{7,6},{8,9},{9,8},{10,11... | collective-permute-start | bytes 27656 | tf_op jit(solution)/shard_map/ppermute | solution.py:739
  32.9 3.9 %collective-permute-start.11 = (f32[16,384]{1,0:T(8,128)S(1)}, f32[16,384]{1,0:T(8,128)S(1)}, u32[]{:S(2)}, u32[]{:S(2)}) collective-permute-start(f32[16,384]{1,0:T(8,128)S(1)} %get-tuple-element.74), channel_id=1, source_target_pairs={{0,1},{1,0},{2,3},{3,2},{4,8},{5,9},{6,10},{7,11},{8,4},{9,5},{10,... | collective-permute-start | bytes 73736 | tf_op jit(solution)/shard_map/ppermute | solution.py:738
  34.8 2.0 %collective-permute-start.12 = (f32[16,384]{1,0:T(8,128)S(1)}, f32[16,384]{1,0:T(8,128)S(1)}, u32[]{:S(2)}, u32[]{:S(2)}) collective-permute-start(f32[16,384]{1,0:T(8,128)S(1)} %get-tuple-element.75), channel_id=1, source_target_pairs={{0,4},{4,0},{8,12},{12,8},{16,20},{20,16},{24,28},{28,24},{1,5},{5... | collective-permute-start | bytes 73736 | tf_op jit(solution)/shard_map/ppermute | solution.py:739

commit v15 on v14

--- a/solution.py
+++ b/solution.py
@@ -720,8 +720,9 @@
         return np.logical_or.reduce([known, *(known[[b for _, b in pairs]] for pairs in swaps)])
 
     even = [xor_pairs(counts, 0, 1), xor_pairs(counts, 1, 0)]
+    own = meet(xor_pairs(counts, 4, 0), xor_pairs(counts, 4, 2))
     known = meet(even[0], odd_pairs(counts, 1, 0))
-    known = meet(even[1], odd_pairs(counts, 0, 0), xor_pairs(counts, 4, 0))
+    known = meet(even[1], odd_pairs(counts, 0, 0)) | own
     known = meet(even[0], odd_pairs(counts, 1, 1))
     return meet(even[1], odd_pairs(counts, 0, 0)).all()
 
@@ -752,6 +753,8 @@
                 table = table + small_swap(table, *((0, bit) if axis else (bit, 0)))
                 bit *= 2
     ga, gb = swap(a, b, "col")
+    weight, own = call(weights_kernel, [(EXT, 2 * SPEC), (depth, 128)], both, table, basis)
+    far = [small_swap(own, 4, 0), small_swap(own, 4, 2)]
     r3, h3, b, a, table = call(
         functools.partial(widen_kernel, counts),
         [(128, 128)] * 2 + [(24 + depth, FC)] * 2 + [(depth, 128)],
@@ -761,8 +764,6 @@
         ga,
     )
     ga, gb = swap(a, b, "row")
-    weight, table = call(weights_kernel, [(EXT, 2 * SPEC), (depth, 128)], both, table, basis)
-    far = small_swap(table, 4, 0)
     t = call(forward_kernel, [(EXT, 2 * SPEC)], both, r3, basis)[0]
     t, table, b, a = call(
         functools.partial(first_kernel, counts),
@@ -774,7 +775,7 @@
         basis,
         table,
     )
-    table = merged(table, far)
+    table = merged(table, *far)
     wide = jnp.pad(table, ((0, 0), (0, EXT - 128)))
     y, m = call(
         functools.partial(inverse_kernel, counts),

time: 47.7 us -> 48.6 us (1.019)
  starting transfers between devices: 17.6 us -> 18.1 us
    ppermute x6, waiting for transfers between devices: 6.5 us -> 8.53 us  [swap(): lax.ppermute(b, both_axes, odd_pairs(counts, both_axes.index(axis), bit))]
    ppermute x6, waiting for transfers between devices: 4.48 us -> 2.82 us  [swap(): return (lax.ppermute(a, axis, pairs_from(lax.axis_size(axis), 0)), gb)]
    ppermute x1 -> x2, starting transfers between devices: 2.43 us -> 2.73 us  [small_swap(): return lax.ppermute(x, both_axes, xor_pairs(counts, rows, cols))]
  transfers between devices with their start and end apart: 13 -> 14, of which waited for: 8 -> 6; matrix products, arithmetic and copies ran while one was open for 0% -> 0% of each run, Pallas kernels for 9% -> 9%
where the time goes in v15:
time: 48.6 us; the launch traced here: 48.5 us
  starting transfers between devices  18.1 us (37%)
  waiting for transfers between devices  11.3 us (23%)
  blocking collectives  9.23 us (19%)
  Pallas kernels  7.86 us (16%)
  other arithmetic  1.15 us (2%)
  between operations  0.78 us (2%)
    all_to_all x1, blocking collectives, body(): stats = lax.all_to_all(stats, both_axes, 0, 0, tiled=True)  9.23 us
    ppermute x6, starting transfers between devices, swap(): lax.ppermute(b, both_axes, odd_pairs(counts, both_axes.index(axis), bit))  8.92 us
    ppermute x6, waiting for transfers between devices, swap(): lax.ppermute(b, both_axes, odd_pairs(counts, both_axes.index(axis), bit))  8.53 us
    pallas_call x14, Pallas kernels, call(): pl.pallas_call(kernel, out_shape=shapes, compiler_params=pltpu.CompilerPa...  7.86 us
    ppermute x6, starting transfers between devices, swap(): return (lax.ppermute(a, axis, pairs_from(lax.axis_size(axis), 0)), gb)  6.45 us
    ppermute x6, waiting for transfers between devices, swap(): return (lax.ppermute(a, axis, pairs_from(lax.axis_size(axis), 0)), gb)  2.82 us
    ppermute x2, starting transfers between devices, small_swap(): return lax.ppermute(x, both_axes, xor_pairs(counts, rows, cols))  2.73 us
    add x1, other arithmetic, body(): jnp.pad(noise, ((0, TR), (0, 0))) + jnp.pad(height, ((TR, 0), (0, 0)))  1.14 us
  transfers between devices with their start and end apart: 14, of which 6 were waited for; matrix products, arithmetic and copies ran while one was open for 0% of the time, Pallas kernels for 9%

profile of v15, /device:TPU:0, one launch (start us, length us, event | category | flops | bytes accessed | tf_op | source)
XLA Modules:
  0.0 48.5 jit_solution(7577895073350221377)
XLA Ops:
  0.6 0.0 copy-start
  0.6 1.1 %pad_add_fusion.both_ref = f32[256,256]{1,0:T(8,128)S(1)} fusion(f32[128,256]{1,0:T(8,128)} %param.3, f32[128,256]{1,0:T(8,128)} %param.4), kind=kLoop, calls=%fused_computation | loop fusion | flops 65536 | bytes 524288 | tf_op jit(solution)/shard_map/add | solution.py:745
  1.8 0.2 shard_map.50
  1.9 4.0 %collective-permute-start = (f32[40,128]{1,0:T(8,128)S(1)}, f32[40,128]{1,0:T(8,128)S(1)}, u32[]{:S(2)}, u32[]{:S(2)}) collective-permute-start(f32[40,128]{1,0:T(8,128)S(1)} %get-tuple-element.43), channel_id=1, source_target_pairs={{0,3},{1,2},{2,1},{3,0},{4,7},{5,6},{6,5},{7,4},{8,11},{9,10},{10,... | collective-permute-start | bytes 61448 | tf_op jit(solution)/shard_map/ppermute | solution.py:739
  5.9 0.5 %collective-permute-start.1 = (f32[40,128]{1,0:T(8,128)S(1)}, f32[40,128]{1,0:T(8,128)S(1)}, u32[]{:S(2)}, u32[]{:S(2)}) collective-permute-start(f32[40,128]{1,0:T(8,128)S(1)} %get-tuple-element.44), channel_id=1, source_target_pairs={{0,1},{1,0},{2,3},{3,2},{4,5},{5,4},{6,7},{7,6},{8,9},{9,8},{10,11... | collective-permute-start | bytes 61448 | tf_op jit(solution)/shard_map/ppermute | solution.py:740
  6.4 0.0 copy-done
  6.4 0.1 shard_map.53
  6.6 2.6 %collective-permute-start.5 = (f32[8,128]{1,0:T(8,128)S(1)}, f32[8,128]{1,0:T(8,128)S(1)}, u32[]{:S(2)}, u32[]{:S(2)}) collective-permute-start(f32[8,128]{1,0:T(8,128)S(1)} %get-tuple-element.55), channel_id=1, source_target_pairs={{0,18},{1,19},{2,16},{3,17},{4,22},{5,23},{6,20},{7,21},{8,26},{9,... | collective-permute-start | bytes 12296 | tf_op jit(solution)/shard_map/ppermute | solution.py:743
  9.2 0.1 collective-permute-start.4
  9.3 0.0 collective-permute-done.gb_ref
  9.3 0.4 collective-permute-done.1.ga_ref
  9.7 0.2 shard_map.51
  9.9 2.0 %collective-permute-start.2 = (f32[32,384]{1,0:T(8,128)S(1)}, f32[32,384]{1,0:T(8,128)S(1)}, u32[]{:S(2)}, u32[]{:S(2)}) collective-permute-start(f32[32,384]{1,0:T(8,128)S(1)} %get-tuple-element.45), channel_id=1, source_target_pairs={{0,28},{1,29},{2,30},{3,31},{4,8},{5,9},{6,10},{7,11},{8,4},{9,5},... | collective-permute-start | bytes 147464 | tf_op jit(solution)/shard_map/ppermute | solution.py:739
  11.9 0.0 collective-permute-start.3
  11.9 0.6 %shard_map.52.tile_ref = f32[144,512]{1,0:T(8,128)S(1)} custom-call(f32[256,256]{1,0:T(8,128)S(1)} %pad_add_fusion.both_ref, f32[128,128]{1,0:T(8,128)S(1)} %get-tuple-element.47.r3_ref, f32[1104,512]{1,0:T(8,128)S(1)} %copy-done), custom_call_target="tpu_custom_call" | custom-call | flops 1000000000 | bytes 1000000 | tf_op jit(solution)/shard_map/pallas_call | solution.py:683
  12.4 3.1 %collective-permute-done.2.gb_ref = f32[32,384]{1,0:T(8,128)S(1)} collective-permute-done((f32[32,384]{1,0:T(8,128)S(1)}, f32[32,384]{1,0:T(8,128)S(1)}, u32[]{:S(2)}, u32[]{:S(2)}) %collective-permute-start.2) | collective-permute-done | bytes 49184 | tf_op jit(solution)/shard_map/ppermute | solution.py:739
  15.5 0.0 collective-permute-done.3.ga_ref
  15.5 1.0 %shard_map.54 = (f32[144,512]{1,0:T(8,128)S(1)}, f32[8,128]{1,0:T(8,128)S(1)}, f32[24,144]{1,0:T(8,128)S(1)}, f32[24,144]{1,0:T(8,128)S(1)}) custom-call(f32[32,384]{1,0:T(8,128)S(1)} %collective-permute-done.2.gb_ref, f32[32,384]{1,0:T(8,128)S(1)} %collective-permute-done.3.ga_ref, f32[144,512]{1,0:T(8,128)S(1)} %shard_map.52.tile_ref, ...), custom_call_target="tpu_custom_call" | custom-call | flops 1000000000 | bytes 1000000 | tf_op jit(solution)/shard_map/pallas_call | solution.py:683
  16.5 0.0 collective-permute-done.5
  16.5 0.0 collective-permute-done.4
  16.6 0.1 collective-permute-start.7
  16.7 2.8 %collective-permute-start.6 = (f32[32,144]{1,0:T(8,128)S(1)}, f32[32,144]{1,0:T(8,128)S(1)}, u32[]{:S(2)}, u32[]{:S(2)}) collective-permute-start(f32[32,144]{1,0:T(8,128)S(1)} %get-tuple-element.83), channel_id=1, source_target_pairs={{0,1},{1,0},{2,3},{3,2},{4,5},{5,4},{6,7},{7,6},{8,9},{9,8},{10,11... | collective-permute-start | bytes 55304 | tf_op jit(solution)/shard_map/ppermute | solution.py:740
  19.5 0.8 %shard_map.55 = (f32[144,384]{1,0:T(8,128)S(1)}, f32[160,384]{1,0:T(8,128)S(1)}) custom-call(f32[144,512]{1,0:T(8,128)S(1)} %get-tuple-element.50.t_ref, f32[1104,512]{1,0:T(8,128)S(1)} %copy-done, f32[256,256]{1,0:T(8,128)S(1)} %pad_add_fusion.both_ref, f32[128,128]{1,0:T(8,128)S(1)} %get-tuple-element.51.h3_ref, ...), custom_call_target="tpu_custom_call" | custom-call | flops 1000000000 | bytes 1000000 | tf_op jit(solution)/shard_map/pallas_call | solution.py:683
  20.3 0.0 collective-permute-done.7.refs_1_
  20.3 1.4 %collective-permute-done.6.refs_0_ = f32[32,144]{1,0:T(8,128)S(1)} collective-permute-done((f32[32,144]{1,0:T(8,128)S(1)}, f32[32,144]{1,0:T(8,128)S(1)}, u32[]{:S(2)}, u32[]{:S(2)}) %collective-permute-start.6) | collective-permute-done | bytes 18464 | tf_op jit(solution)/shard_map/ppermute | solution.py:740
  21.7 0.2 shard_map.56
  21.9 0.9 %collective-permute-start.8 = (f32[32,384]{1,0:T(8,128)S(1)}, f32[32,384]{1,0:T(8,128)S(1)}, u32[]{:S(2)}, u32[]{:S(2)}) collective-permute-start(f32[32,384]{1,0:T(8,128)S(1)} %get-tuple-element.59), channel_id=1, source_target_pairs={{0,28},{1,29},{2,30},{3,31},{4,8},{5,9},{6,10},{7,11},{8,4},{9,5},... | collective-permute-start | bytes 147464 | tf_op jit(solution)/shard_map/ppermute | solution.py:739
  22.8 0.0 collective-permute-start.9
  22.8 0.7 %shard_map.57 = (f32[96,256]{1,0:T(8,128)S(1)}, f32[96,256]{1,0:T(8,128)S(1)}, f32[144,384]{1,0:T(8,128)S(1)}, f32[144,384]{1,0:T(8,128)S(1)}, f32[16,128]{1,0:T(8,128)S(1)}) custom-call(f32[144,384]{1,0:T(8,128)S(1)} %get-tuple-element.57.y_ref, f32[160,384]{1,0:T(8,128)S(1)} %get-tuple-element.58.m_ref, f32[1104,512]{1,0:T(8,128)S(1)} %copy-done), custom_call_target="tpu_custom_call" | custom-call | flops 1000000000 | bytes 1000000 | tf_op jit(solution)/shard_map/pallas_call | solution.py:683
  23.5 3.8 %collective-permute-done.8.gb_ref = f32[32,384]{1,0:T(8,128)S(1)} collective-permute-done((f32[32,384]{1,0:T(8,128)S(1)}, f32[32,384]{1,0:T(8,128)S(1)}, u32[]{:S(2)}, u32[]{:S(2)}) %collective-permute-start.8) | collective-permute-done | bytes 49184 | tf_op jit(solution)/shard_map/ppermute | solution.py:739
  27.3 0.0 collective-permute-done.9.ga_ref
  27.3 1.3 %shard_map.58 = (f32[128,256]{1,0:T(8,128)S(1)}, f32[128,256]{1,0:T(8,128)S(1)}, f32[144,512]{1,0:T(8,128)S(1)}, f32[16,144]{1,0:T(8,128)S(1)}, f32[16,144]{1,0:T(8,128)S(1)}) custom-call(f32[144,384]{1,0:T(8,128)S(1)} %get-tuple-element.57.y_ref, f32[160,384]{1,0:T(8,128)S(1)} %get-tuple-element.58.m_ref, f32[32,384]{1,0:T(8,128)S(1)} %collective-permute-done.8.gb_ref, ...), custom_call_target="tpu_custom_call" | custom-call | flops 1000000000 | bytes 1000000 | tf_op jit(solution)/shard_map/pallas_call | solution.py:683
  28.5 0.1 collective-permute-start.10
  28.7 3.1 %collective-permute-start.11 = (f32[16,144]{1,0:T(8,128)S(1)}, f32[16,144]{1,0:T(8,128)S(1)}, u32[]{:S(2)}, u32[]{:S(2)}) collective-permute-start(f32[16,144]{1,0:T(8,128)S(1)} %get-tuple-element.72), channel_id=1, source_target_pairs={{0,1},{1,0},{2,3},{3,2},{4,5},{5,4},{6,7},{7,6},{8,9},{9,8},{10,11... | collective-permute-start | bytes 27656 | tf_op jit(solution)/shard_map/ppermute | solution.py:740
  31.7 0.8 %shard_map.59 = (f32[144,384]{1,0:T(8,128)S(1)}, f32[1,128]{1,0:T(1,128)S(1)}) custom-call(f32[144,512]{1,0:T(8,128)S(1)} %get-tuple-element.67.t_ref, f32[1104,512]{1,0:T(8,128)S(1)} %copy-done, f32[256,256]{1,0:T(8,128)S(1)} %pad_add_fusion.both_ref, f32[160,384]{1,0:T(8,128)S(1)} %get-tuple-element.58.m_ref, f32[128,256]{1,0:T(8,128)S(1)} %get-tuple-element.68.z_ref, ...), custom_call_target="tpu_custom_call" | custom-call | flops 1000000000 | bytes 1000000 | tf_op jit(solution)/shard_map/pallas_call | solution.py:683
  32.6 0.0 collective-permute-done.10.refs_0_
  32.6 1.1 %collective-permute-done.11.refs_1_ = f32[16,144]{1,0:T(8,128)S(1)} collective-permute-done((f32[16,144]{1,0:T(8,128)S(1)}, f32[16,144]{1,0:T(8,128)S(1)}, u32[]{:S(2)}, u32[]{:S(2)}) %collective-permute-start.11) | collective-permute-done | bytes 9248 | tf_op jit(solution)/shard_map/ppermute | solution.py:740
  33.6 0.2 shard_map.60
  33.8 1.9 %collective-permute-start.12 = (f32[16,384]{1,0:T(8,128)S(1)}, f32[16,384]{1,0:T(8,128)S(1)}, u32[]{:S(2)}, u32[]{:S(2)}) collective-permute-start(f32[16,384]{1,0:T(8,128)S(1)} %get-tuple-element.74), channel_id=1, source_target_pairs={{0,1},{1,0},{2,3},{3,2},{4,8},{5,9},{6,10},{7,11},{8,4},{9,5},{10,... | collective-permute-start | bytes 73736 | tf_op jit(solution)/shard_map/ppermute | solution.py:739
  35.7 0.0 collective-permute-start.13
  35.7 0.4 shard_map.61
  36.1 1.6 %collective-permute-done.12.gb_ref = f32[16,384]{1,0:T(8,128)S(1)} collective-permute-done((f32[16,384]{1,0:T(8,128)S(1)}, f32[16,384]{1,0:T(8,128)S(1)}, u32[]{:S(2)}, u32[]{:S(2)}) %collective-permute-start.12) | collective-permute-done | bytes 24608 | tf_op jit(solution)/shard_map/ppermute | solution.py:739
  37.7 0.0 collective-permute-done.13.ga_ref
  37.7 0.3 shard_map.62
  38.0 9.2 %all_to_all.11 = f32[32,1,128]{2,1,0:T(1,128)S(1)} all-to-all(f32[32,1,128]{2,1,0:T(1,128)S(1)} %bitcast.5), channel_id=1, replica_groups=mesh['row'=8,'col'=4] {'row','col'}, dimensions={0} | all-to-all | bytes 32768 | tf_op jit(solution)/shard_map/all_to_all | solution.py:850
  47.2 1.3 %shard_map.63 = (f32[128,256]{1,0:T(8,128)}, f32[128,256]{1,0:T(8,128)}) custom-call(f32[32,128]{1,0:T(8,128)S(1)} %bitcast.4, f32[1104,512]{1,0:T(8,128)S(1)} %copy-done, f32[160,384]{1,0:T(8,128)S(1)} %get-tuple-element.58.m_ref, f32[96,256]{1,0:T(8,128)S(1)} %get-tuple-element.63.f_ref, f32[256,256]{1,0:T(8,128)S(1)} %pad_add_fusion.both_ref, ...), custom_call_target="tpu_custom_call" | custom-call | flops 1000000000 | bytes 1000000 | tf_op jit(solution)/shard_map/pallas_call | solution.py:683
  (2 shorter events, 0.0 us)
Async XLA Ops:
  0.6 5.8 %copy-start = (f32[1104,512]{1,0:T(8,128)S(1)}, f32[1104,512]{1,0:T(8,128)}, u32[]{:S(2)}) copy-start(f32[1104,512]{1,0:T(8,128)} %constant.6.clone.basis_ref) | copy-start | bytes 6782980
  1.9 7.4 %collective-permute-start = (f32[40,128]{1,0:T(8,128)S(1)}, f32[40,128]{1,0:T(8,128)S(1)}, u32[]{:S(2)}, u32[]{:S(2)}) collective-permute-start(f32[40,128]{1,0:T(8,128)S(1)} %get-tuple-element.43), channel_id=1, source_target_pairs={{0,3},{1,2},{2,1},{3,0},{4,7},{5,6},{6,5},{7,4},{8,11},{9,10},{10,... | collective-permute-start | bytes 61448 | tf_op jit(solution)/shard_map/ppermute | solution.py:739
  5.9 3.8 %collective-permute-start.1 = (f32[40,128]{1,0:T(8,128)S(1)}, f32[40,128]{1,0:T(8,128)S(1)}, u32[]{:S(2)}, u32[]{:S(2)}) collective-permute-start(f32[40,128]{1,0:T(8,128)S(1)} %get-tuple-element.44), channel_id=1, source_target_pairs={{0,1},{1,0},{2,3},{3,2},{4,5},{5,4},{6,7},{7,6},{8,9},{9,8},{10,11... | collective-permute-start | bytes 61448 | tf_op jit(solution)/shard_map/ppermute | solution.py:740
  6.6 9.9 %collective-permute-start.5 = (f32[8,128]{1,0:T(8,128)S(1)}, f32[8,128]{1,0:T(8,128)S(1)}, u32[]{:S(2)}, u32[]{:S(2)}) collective-permute-start(f32[8,128]{1,0:T(8,128)S(1)} %get-tuple-element.55), channel_id=1, source_target_pairs={{0,18},{1,19},{2,16},{3,17},{4,22},{5,23},{6,20},{7,21},{8,26},{9,... | collective-permute-start | bytes 12296 | tf_op jit(solution)/shard_map/ppermute | solution.py:743
  9.2 7.4 %collective-permute-start.4 = (f32[8,128]{1,0:T(8,128)S(1)}, f32[8,128]{1,0:T(8,128)S(1)}, u32[]{:S(2)}, u32[]{:S(2)}) collective-permute-start(f32[8,128]{1,0:T(8,128)S(1)} %get-tuple-element.55), channel_id=1, source_target_pairs={{0,16},{1,17},{2,18},{3,19},{4,20},{5,21},{6,22},{7,23},{8,24},{9,... | collective-permute-start | bytes 12296 | tf_op jit(solution)/shard_map/ppermute | solution.py:743
  9.9 5.6 %collective-permute-start.2 = (f32[32,384]{1,0:T(8,128)S(1)}, f32[32,384]{1,0:T(8,128)S(1)}, u32[]{:S(2)}, u32[]{:S(2)}) collective-permute-start(f32[32,384]{1,0:T(8,128)S(1)} %get-tuple-element.45), channel_id=1, source_target_pairs={{0,28},{1,29},{2,30},{3,31},{4,8},{5,9},{6,10},{7,11},{8,4},{9,5},... | collective-permute-start | bytes 147464 | tf_op jit(solution)/shard_map/ppermute | solution.py:739
  11.9 3.7 %collective-permute-start.3 = (f32[32,384]{1,0:T(8,128)S(1)}, f32[32,384]{1,0:T(8,128)S(1)}, u32[]{:S(2)}, u32[]{:S(2)}) collective-permute-start(f32[32,384]{1,0:T(8,128)S(1)} %get-tuple-element.46), channel_id=1, source_target_pairs={{0,4},{4,0},{8,12},{12,8},{16,20},{20,16},{24,28},{28,24},{1,5},{5... | collective-permute-start | bytes 147464 | tf_op jit(solution)/shard_map/ppermute | solution.py:740
  16.6 3.7 %collective-permute-start.7 = (f32[32,144]{1,0:T(8,128)S(1)}, f32[32,144]{1,0:T(8,128)S(1)}, u32[]{:S(2)}, u32[]{:S(2)}) collective-permute-start(f32[32,144]{1,0:T(8,128)S(1)} %get-tuple-element.82), channel_id=1, source_target_pairs={{0,4},{1,2},{2,1},{3,7},{4,0},{5,6},{6,5},{7,3},{8,12},{9,10},{10,... | collective-permute-start | bytes 55304 | tf_op jit(solution)/shard_map/ppermute | solution.py:739
  16.7 5.1 %collective-permute-start.6 = (f32[32,144]{1,0:T(8,128)S(1)}, f32[32,144]{1,0:T(8,128)S(1)}, u32[]{:S(2)}, u32[]{:S(2)}) collective-permute-start(f32[32,144]{1,0:T(8,128)S(1)} %get-tuple-element.83), channel_id=1, source_target_pairs={{0,1},{1,0},{2,3},{3,2},{4,5},{5,4},{6,7},{7,6},{8,9},{9,8},{10,11... | collective-permute-start | bytes 55304 | tf_op jit(solution)/shard_map/ppermute | solution.py:740
  21.9 5.4 %collective-permute-start.8 = (f32[32,384]{1,0:T(8,128)S(1)}, f32[32,384]{1,0:T(8,128)S(1)}, u32[]{:S(2)}, u32[]{:S(2)}) collective-permute-start(f32[32,384]{1,0:T(8,128)S(1)} %get-tuple-element.59), channel_id=1, source_target_pairs={{0,28},{1,29},{2,30},{3,31},{4,8},{5,9},{6,10},{7,11},{8,4},{9,5},... | collective-permute-start | bytes 147464 | tf_op jit(solution)/shard_map/ppermute | solution.py:739
  22.8 4.5 %collective-permute-start.9 = (f32[32,384]{1,0:T(8,128)S(1)}, f32[32,384]{1,0:T(8,128)S(1)}, u32[]{:S(2)}, u32[]{:S(2)}) collective-permute-start(f32[32,384]{1,0:T(8,128)S(1)} %get-tuple-element.60), channel_id=1, source_target_pairs={{0,4},{4,0},{8,12},{12,8},{16,20},{20,16},{24,28},{28,24},{1,5},{5... | collective-permute-start | bytes 147464 | tf_op jit(solution)/shard_map/ppermute | solution.py:740
  28.5 4.0 %collective-permute-start.10 = (f32[16,144]{1,0:T(8,128)S(1)}, f32[16,144]{1,0:T(8,128)S(1)}, u32[]{:S(2)}, u32[]{:S(2)}) collective-permute-start(f32[16,144]{1,0:T(8,128)S(1)} %get-tuple-element.71), channel_id=1, source_target_pairs={{0,4},{1,2},{2,1},{3,7},{4,0},{5,6},{6,5},{7,3},{8,12},{9,10},{10,... | collective-permute-start | bytes 27656 | tf_op jit(solution)/shard_map/ppermute | solution.py:739
  28.7 5.0 %collective-permute-start.11 = (f32[16,144]{1,0:T(8,128)S(1)}, f32[16,144]{1,0:T(8,128)S(1)}, u32[]{:S(2)}, u32[]{:S(2)}) collective-permute-start(f32[16,144]{1,0:T(8,128)S(1)} %get-tuple-element.72), channel_id=1, source_target_pairs={{0,1},{1,0},{2,3},{3,2},{4,5},{5,4},{6,7},{7,6},{8,9},{9,8},{10,11... | collective-permute-start | bytes 27656 | tf_op jit(solution)/shard_map/ppermute | solution.py:740
  33.8 3.9 %collective-permute-start.12 = (f32[16,384]{1,0:T(8,128)S(1)}, f32[16,384]{1,0:T(8,128)S(1)}, u32[]{:S(2)}, u32[]{:S(2)}) collective-permute-start(f32[16,384]{1,0:T(8,128)S(1)} %get-tuple-element.74), channel_id=1, source_target_pairs={{0,1},{1,0},{2,3},{3,2},{4,8},{5,9},{6,10},{7,11},{8,4},{9,5},{10,... | collective-permute-start | bytes 73736 | tf_op jit(solution)/shard_map/ppermute | solution.py:739
  35.7 2.0 %collective-permute-start.13 = (f32[16,384]{1,0:T(8,128)S(1)}, f32[16,384]{1,0:T(8,128)S(1)}, u32[]{:S(2)}, u32[]{:S(2)}) collective-permute-start(f32[16,384]{1,0:T(8,128)S(1)} %get-tuple-element.75), channel_id=1, source_target_pairs={{0,4},{4,0},{8,12},{12,8},{16,20},{20,16},{24,28},{28,24},{1,5},{5... | collective-permute-start | bytes 73736 | tf_op jit(solution)/shard_map/ppermute | solution.py:740

commit v16 on v14

--- a/solution.py
+++ b/solution.py
@@ -369,6 +369,38 @@
         jnp.concatenate([turned[:32], table], axis=0),
         jnp.concatenate([turned[96:], table], axis=0),
     )
+
+
+def statistics_kernel(both_ref, table_ref, stats_ref, table_out):
+    h = both_ref[TR:]
+    mt = h * h * h
+    lane, row = lanes_of((1, 256)), rows_of((128, 1))
+    along = (lane % 128 != 0) & (lane % 128 != 127)
+    top, low = mt[:1], mt[127:]
+    side = jnp.sum(jnp.where((row > 0) & (row < 127), mt, 0.0), axis=0, keepdims=True)
+
+    def halves(x):
+        return [
+            jnp.sum(x[:, :128], axis=1, keepdims=True),
+            jnp.sum(x[:, 128:], axis=1, keepdims=True),
+        ]
+
+    first, last = lane % 128 == 0, lane % 128 == 127
+    zero = jnp.zeros((1, 1), jnp.float32)
+    stats_ref[...] = row_of(
+        [
+            *[[zero, zero]] * 3,
+            halves(jnp.where(along, top, 0.0)),
+            halves(jnp.where(along, low, 0.0)),
+            halves(jnp.where(first, side, 0.0)),
+            halves(jnp.where(last, side, 0.0)),
+            halves(jnp.where(first, top, 0.0)),
+            halves(jnp.where(last, top, 0.0)),
+            halves(jnp.where(first, low, 0.0)),
+            halves(jnp.where(last, low, 0.0)),
+        ]
+    )
+    table_out[...] = table_ref[...]
 
 
 def widen_kernel(counts, both_ref, own_ref, gb_ref, ga_ref, r3_ref, h3_ref, b_ref, a_ref, table_ref):
@@ -526,39 +558,12 @@
     send(j, a_ref, b_ref, *strips_of(t, basis_ref, 16))
 
 
-def inverse_stats_kernel(t_ref, basis_ref, both_ref, m_ref, z_ref, w_ref, y_ref, stats_ref):
+def inverse_stats_kernel(t_ref, basis_ref, both_ref, z_ref, w_ref, edge_stats_ref, y_ref, stats_ref):
     y_ref[...] = solution_of(t_ref[...], basis_ref)
-    rt, mt, zt, wt = both_ref[:TR], m_ref[:TR, :TC], z_ref[...], w_ref[...]
-    lane, row = lanes_of((1, 256)), rows_of((128, 1))
-    along = (lane % 128 != 0) & (lane % 128 != 127)
-    top, low = mt[:1], mt[127:]
-    side = jnp.sum(jnp.where((row > 0) & (row < 127), mt, 0.0), axis=0, keepdims=True)
-
-    def halves(x):
-        return [
-            jnp.sum(x[:, :128], axis=1, keepdims=True),
-            jnp.sum(x[:, 128:], axis=1, keepdims=True),
-        ]
-
-    first, last = lane % 128 == 0, lane % 128 == 127
+    rt, zt, wt = both_ref[:TR], z_ref[...], w_ref[...]
     zero = jnp.zeros((1, 1), jnp.float32)
-    stats_ref[...] = row_of(
-        [
-            core_sums(rt * zt),
-            core_sums(zt * wt),
-            core_sums(wt),
-            halves(jnp.where(along, top, 0.0)),
-            halves(jnp.where(along, low, 0.0)),
-            halves(jnp.where(first, side, 0.0)),
-            halves(jnp.where(last, side, 0.0)),
-            halves(jnp.where(first, top, 0.0)),
-            halves(jnp.where(last, top, 0.0)),
-            halves(jnp.where(first, low, 0.0)),
-            halves(jnp.where(last, low, 0.0)),
-            *[[zero, zero]] * 4,
-            core_sums(rt),
-        ]
-    )
+    sums = [core_sums(rt * zt), core_sums(zt * wt), core_sums(wt), *[[zero, zero]] * 12, core_sums(rt)]
+    stats_ref[...] = edge_stats_ref[...] + row_of(sums)
 
 
 def inner_dots_kernel(counts, y_ref, m_ref, both_ref, w_ref, stats_ref, v_ref, stats_out):
@@ -700,10 +705,10 @@
     for i in range(counts[0]):
         for j in range(counts[1]):
             at = [i, j]
-            if bit and at[axis] in (0, counts[axis] - 1):
+            if at[axis] in (0, counts[axis] - 1):
                 at[1 - axis] ^= bit
             else:
-                at[axis] = (at[axis] + (1 if at[axis] % 2 else -1)) % counts[axis]
+                at[axis] += 1 if at[axis] % 2 else -1
             found.append((i * counts[1] + j, at[0] * counts[1] + at[1]))
     return found
 
@@ -720,10 +725,11 @@
         return np.logical_or.reduce([known, *(known[[b for _, b in pairs]] for pairs in swaps)])
 
     even = [xor_pairs(counts, 0, 1), xor_pairs(counts, 1, 0)]
-    known = meet(even[0], odd_pairs(counts, 1, 0))
-    known = meet(even[1], odd_pairs(counts, 0, 0), xor_pairs(counts, 4, 0))
+    own = meet(xor_pairs(counts, 2, 3), xor_pairs(counts, 6, 3))
     known = meet(even[0], odd_pairs(counts, 1, 1))
-    return meet(even[1], odd_pairs(counts, 0, 0)).all()
+    known = meet(even[1], odd_pairs(counts, 0, 1), xor_pairs(counts, 4, 0)) | own
+    known = meet(even[0], odd_pairs(counts, 1, 2))
+    return meet(even[1], odd_pairs(counts, 0, 1)).all()
 
 
 def body(counts, height, noise):
@@ -734,7 +740,7 @@
     both_axes = ("row", "col")
     depth = table_shape(counts)[0]
 
-    def swap(a, b, axis, bit=0):
+    def swap(a, b, axis, bit=1):
         gb = lax.ppermute(b, both_axes, odd_pairs(counts, both_axes.index(axis), bit))
         return lax.ppermute(a, axis, pairs_from(lax.axis_size(axis), 0)), gb
 
@@ -752,6 +758,8 @@
                 table = table + small_swap(table, *((0, bit) if axis else (bit, 0)))
                 bit *= 2
     ga, gb = swap(a, b, "col")
+    edge_stats, own = call(statistics_kernel, [(1, 128), (depth, 128)], both, table)
+    far = [small_swap(own, 2, 3), small_swap(own, 6, 3)]
     r3, h3, b, a, table = call(
         functools.partial(widen_kernel, counts),
         [(128, 128)] * 2 + [(24 + depth, FC)] * 2 + [(depth, 128)],
@@ -762,7 +770,7 @@
     )
     ga, gb = swap(a, b, "row")
     weight, table = call(weights_kernel, [(EXT, 2 * SPEC), (depth, 128)], both, table, basis)
-    far = small_swap(table, 4, 0)
+    far.append(small_swap(table, 4, 0))
     t = call(forward_kernel, [(EXT, 2 * SPEC)], both, r3, basis)[0]
     t, table, b, a = call(
         functools.partial(first_kernel, counts),
@@ -774,7 +782,7 @@
         basis,
         table,
     )
-    table = merged(table, far)
+    table = merged(table, *far)
     wide = jnp.pad(table, ((0, 0), (0, EXT - 128)))
     y, m = call(
         functools.partial(inverse_kernel, counts),
@@ -786,7 +794,7 @@
         gb,
         ga,
     )
-    ga, gb = swap(*(jnp.concatenate([x, wide], axis=0) for x in (a, b)), "col", 1)
+    ga, gb = swap(*(jnp.concatenate([x, wide], axis=0) for x in (a, b)), "col", 2)
     y, table, b, a = call(
         functools.partial(columns_kernel, counts),
         [(EXT, FC), (depth, 128)] + [(24 + depth, FC)] * 2,
@@ -819,12 +827,12 @@
         weight,
         basis,
     )
-    ga, gb = swap(a, b, "col", 1)
-    y, stats = call(inverse_stats_kernel, [(EXT, FC), (1, 128)], t, basis, both, m, z, w)
+    ga, gb = swap(a, b, "col")
+    y, stats = call(inverse_stats_kernel, [(EXT, FC), (1, 128)], t, basis, both, z, w, edge_stats)
     y, b, a = call(
         functools.partial(columns_kernel, counts), [(EXT, FC)] + [(16, FC)] * 2, y, gb, ga
     )
-    ga, gb = swap(a, b, "row", 1)
+    ga, gb = swap(a, b, "row")
     inner_v, stats = call(
         functools.partial(inner_dots_kernel, counts),
         [(96, TC), (1, 128)],

time: 47.7 us -> 48.6 us (1.019)
  starting transfers between devices: 17.6 us -> 20.8 us
  waiting for transfers between devices: 11.1 us -> 8.53 us
    ppermute x6, starting transfers between devices: 6.37 us -> 11.5 us  [swap(): return (lax.ppermute(a, axis, pairs_from(lax.axis_size(axis), 0)), gb)]
    ppermute x6, starting transfers between devices: 8.83 us -> 4.26 us  [swap(): lax.ppermute(b, both_axes, odd_pairs(counts, both_axes.index(axis), bit))]
    ppermute x6, waiting for transfers between devices: 4.48 us -> 1.13 us  [swap(): return (lax.ppermute(a, axis, pairs_from(lax.axis_size(axis), 0)), gb)]
    ppermute x1 -> x3, starting transfers between devices: 2.43 us -> 5.09 us  [small_swap(): return lax.ppermute(x, both_axes, xor_pairs(counts, rows, cols))]
    ppermute x1 -> x3, waiting for transfers between devices: 0.07 us -> 2.19 us  [small_swap(): return lax.ppermute(x, both_axes, xor_pairs(counts, rows, cols))]
    ppermute x6, waiting for transfers between devices: 6.5 us -> 5.2 us  [swap(): lax.ppermute(b, both_axes, odd_pairs(counts, both_axes.index(axis), bit))]
    pallas_call x14 -> x15, Pallas kernels: 7.86 us -> 7.99 us  [call(): pl.pallas_call(kernel, out_shape=shapes, compiler_params=pltpu.CompilerPa...]
  transfers between devices with their start and end apart: 13 -> 15, of which waited for: 8 -> 7; matrix products, arithmetic and copies ran while one was open for 0% -> 0% of each run, Pallas kernels for 9% -> 10%
where the time goes in v16:
time: 48.6 us; the launch traced here: 48.4 us
  starting transfers between devices  20.8 us (43%)
  blocking collectives  9.31 us (19%)
  waiting for transfers between devices  8.53 us (18%)
  Pallas kernels  7.99 us (16%)
  other arithmetic  1 us (2%)
  between operations  0.77 us (2%)
    ppermute x6, starting transfers between devices, swap(): return (lax.ppermute(a, axis, pairs_from(lax.axis_size(axis), 0)), gb)  11.5 us
    all_to_all x1, blocking collectives, body(): stats = lax.all_to_all(stats, both_axes, 0, 0, tiled=True)  9.31 us
    pallas_call x15, Pallas kernels, call(): pl.pallas_call(kernel, out_shape=shapes, compiler_params=pltpu.CompilerPa...  7.99 us
    ppermute x6, waiting for transfers between devices, swap(): lax.ppermute(b, both_axes, odd_pairs(counts, both_axes.index(axis), bit))  5.2 us
    ppermute x3, starting transfers between devices, small_swap(): return lax.ppermute(x, both_axes, xor_pairs(counts, rows, cols))  5.09 us
    ppermute x6, starting transfers between devices, swap(): lax.ppermute(b, both_axes, odd_pairs(counts, both_axes.index(axis), bit))  4.26 us
    ppermute x3, waiting for transfers between devices, small_swap(): return lax.ppermute(x, both_axes, xor_pairs(counts, rows, cols))  2.19 us
    ppermute x6, waiting for transfers between devices, swap(): return (lax.ppermute(a, axis, pairs_from(lax.axis_size(axis), 0)), gb)  1.13 us
  transfers between devices with their start and end apart: 15, of which 7 were waited for; matrix products, arithmetic and copies ran while one was open for 0% of the time, Pallas kernels for 10%

profile of v16, /device:TPU:0, one launch (start us, length us, event | category | flops | bytes accessed | tf_op | source)
XLA Modules:
  0.0 48.4 jit_solution(14593731558076429115)
XLA Ops:
  0.6 1.0 %pad_add_fusion.both_ref = f32[256,256]{1,0:T(8,128)S(1)} fusion(f32[128,256]{1,0:T(8,128)} %param.3, f32[128,256]{1,0:T(8,128)} %param.4), kind=kLoop, calls=%fused_computation | loop fusion | flops 65536 | bytes 524288 | tf_op jit(solution)/shard_map/add | solution.py:750
  1.6 0.2 shard_map.50
  1.8 0.5 %collective-permute-start = (f32[40,128]{1,0:T(8,128)S(1)}, f32[40,128]{1,0:T(8,128)S(1)}, u32[]{:S(2)}, u32[]{:S(2)}) collective-permute-start(f32[40,128]{1,0:T(8,128)S(1)} %get-tuple-element.45), channel_id=1, source_target_pairs={{0,4},{1,2},{2,1},{3,7},{4,0},{5,6},{6,5},{7,3},{8,12},{9,10},{10,... | collective-permute-start | bytes 61448 | tf_op jit(solution)/shard_map/ppermute | solution.py:744
  2.3 4.0 %collective-permute-start.1 = (f32[40,128]{1,0:T(8,128)S(1)}, f32[40,128]{1,0:T(8,128)S(1)}, u32[]{:S(2)}, u32[]{:S(2)}) collective-permute-start(f32[40,128]{1,0:T(8,128)S(1)} %get-tuple-element.46), channel_id=1, source_target_pairs={{0,1},{1,0},{2,3},{3,2},{4,5},{5,4},{6,7},{7,6},{8,9},{9,8},{10,11... | collective-permute-start | bytes 61448 | tf_op jit(solution)/shard_map/ppermute | solution.py:745
  6.3 0.1 shard_map.56
  6.4 0.0 copy-start
  6.4 4.5 %collective-permute-start.5 = (f32[8,128]{1,0:T(8,128)S(1)}, f32[8,128]{1,0:T(8,128)S(1)}, u32[]{:S(2)}, u32[]{:S(2)}) collective-permute-start(f32[8,128]{1,0:T(8,128)S(1)} %get-tuple-element.58), channel_id=1, source_target_pairs={{0,27},{1,26},{2,25},{3,24},{4,31},{5,30},{6,29},{7,28},{8,19},{9,... | collective-permute-start | bytes 12296 | tf_op jit(solution)/shard_map/ppermute | solution.py:748
  10.9 0.5 collective-permute-start.4
  11.4 0.0 collective-permute-done.gb_ref
  11.4 0.0 collective-permute-done.1.ga_ref
  11.4 0.2 shard_map.51
  11.6 0.1 collective-permute-start.2
  11.7 2.6 %collective-permute-start.3 = (f32[32,384]{1,0:T(8,128)S(1)}, f32[32,384]{1,0:T(8,128)S(1)}, u32[]{:S(2)}, u32[]{:S(2)}) collective-permute-start(f32[32,384]{1,0:T(8,128)S(1)} %get-tuple-element.48), channel_id=1, source_target_pairs={{0,4},{4,0},{8,12},{12,8},{16,20},{20,16},{24,28},{28,24},{1,5},{5... | collective-permute-start | bytes 147464 | tf_op jit(solution)/shard_map/ppermute | solution.py:745
  14.3 0.1 shard_map.53
  14.4 0.1 collective-permute-start.6
  14.5 0.6 %shard_map.52.tile_ref = f32[144,512]{1,0:T(8,128)S(1)} custom-call(f32[256,256]{1,0:T(8,128)S(1)} %pad_add_fusion.both_ref, f32[128,128]{1,0:T(8,128)S(1)} %get-tuple-element.49.r3_ref, f32[1104,512]{1,0:T(8,128)S(1)} %copy-done), custom_call_target="tpu_custom_call" | custom-call | flops 1000000000 | bytes 1000000 | tf_op jit(solution)/shard_map/pallas_call | solution.py:688
  15.1 0.7 %collective-permute-done.2.gb_ref = f32[32,384]{1,0:T(8,128)S(1)} collective-permute-done((f32[32,384]{1,0:T(8,128)S(1)}, f32[32,384]{1,0:T(8,128)S(1)}, u32[]{:S(2)}, u32[]{:S(2)}) %collective-permute-start.2) | collective-permute-done | bytes 49184 | tf_op jit(solution)/shard_map/ppermute | solution.py:744
  15.8 0.0 collective-permute-done.3.ga_ref
  15.8 1.0 %shard_map.54 = (f32[144,512]{1,0:T(8,128)S(1)}, f32[8,128]{1,0:T(8,128)S(1)}, f32[24,144]{1,0:T(8,128)S(1)}, f32[24,144]{1,0:T(8,128)S(1)}) custom-call(f32[32,384]{1,0:T(8,128)S(1)} %collective-permute-done.2.gb_ref, f32[32,384]{1,0:T(8,128)S(1)} %collective-permute-done.3.ga_ref, f32[144,512]{1,0:T(8,128)S(1)} %shard_map.52.tile_ref, ...), custom_call_target="tpu_custom_call" | custom-call | flops 1000000000 | bytes 1000000 | tf_op jit(solution)/shard_map/pallas_call | solution.py:688
  16.8 0.0 collective-permute-done.5
  16.8 0.0 collective-permute-done.4
  16.8 2.2 %collective-permute-done.6 = f32[8,128]{1,0:T(8,128)S(1)} collective-permute-done((f32[8,128]{1,0:T(8,128)S(1)}, f32[8,128]{1,0:T(8,128)S(1)}, u32[]{:S(2)}, u32[]{:S(2)}) %collective-permute-start.6) | collective-permute-done | bytes 4128 | tf_op jit(solution)/shard_map/ppermute | solution.py:748
  19.0 0.1 collective-permute-start.8
  19.1 1.6 %collective-permute-start.7 = (f32[32,144]{1,0:T(8,128)S(1)}, f32[32,144]{1,0:T(8,128)S(1)}, u32[]{:S(2)}, u32[]{:S(2)}) collective-permute-start(f32[32,144]{1,0:T(8,128)S(1)} %get-tuple-element.87), channel_id=1, source_target_pairs={{0,1},{1,0},{2,3},{3,2},{4,5},{5,4},{6,7},{7,6},{8,9},{9,8},{10,11... | collective-permute-start | bytes 55304 | tf_op jit(solution)/shard_map/ppermute | solution.py:745
  20.7 0.8 %shard_map.55 = (f32[144,384]{1,0:T(8,128)S(1)}, f32[160,384]{1,0:T(8,128)S(1)}) custom-call(f32[144,512]{1,0:T(8,128)S(1)} %get-tuple-element.53.t_ref, f32[1104,512]{1,0:T(8,128)S(1)} %copy-done, f32[256,256]{1,0:T(8,128)S(1)} %pad_add_fusion.both_ref, f32[128,128]{1,0:T(8,128)S(1)} %get-tuple-element.54.h3_ref, ...), custom_call_target="tpu_custom_call" | custom-call | flops 1000000000 | bytes 1000000 | tf_op jit(solution)/shard_map/pallas_call | solution.py:688
  21.5 1.5 %collective-permute-done.8.refs_1_ = f32[32,144]{1,0:T(8,128)S(1)} collective-permute-done((f32[32,144]{1,0:T(8,128)S(1)}, f32[32,144]{1,0:T(8,128)S(1)}, u32[]{:S(2)}, u32[]{:S(2)}) %collective-permute-start.8) | collective-permute-done | bytes 18464 | tf_op jit(solution)/shard_map/ppermute | solution.py:744
  23.0 0.1 collective-permute-done.7.refs_0_
  23.1 0.2 shard_map.57
  23.3 1.6 %collective-permute-start.9 = (f32[32,384]{1,0:T(8,128)S(1)}, f32[32,384]{1,0:T(8,128)S(1)}, u32[]{:S(2)}, u32[]{:S(2)}) collective-permute-start(f32[32,384]{1,0:T(8,128)S(1)} %get-tuple-element.62), channel_id=1, source_target_pairs={{0,1},{1,0},{2,3},{3,2},{4,8},{5,9},{6,10},{7,11},{8,4},{9,5},{10,... | collective-permute-start | bytes 147464 | tf_op jit(solution)/shard_map/ppermute | solution.py:744
  24.8 0.6 %collective-permute-start.10 = (f32[32,384]{1,0:T(8,128)S(1)}, f32[32,384]{1,0:T(8,128)S(1)}, u32[]{:S(2)}, u32[]{:S(2)}) collective-permute-start(f32[32,384]{1,0:T(8,128)S(1)} %get-tuple-element.63), channel_id=1, source_target_pairs={{0,4},{4,0},{8,12},{12,8},{16,20},{20,16},{24,28},{28,24},{1,5},{5... | collective-permute-start | bytes 147464 | tf_op jit(solution)/shard_map/ppermute | solution.py:745
  25.4 0.7 %shard_map.58 = (f32[96,256]{1,0:T(8,128)S(1)}, f32[96,256]{1,0:T(8,128)S(1)}, f32[144,384]{1,0:T(8,128)S(1)}, f32[144,384]{1,0:T(8,128)S(1)}, f32[16,128]{1,0:T(8,128)S(1)}) custom-call(f32[144,384]{1,0:T(8,128)S(1)} %get-tuple-element.60.y_ref, f32[160,384]{1,0:T(8,128)S(1)} %get-tuple-element.61.m_ref, f32[1104,512]{1,0:T(8,128)S(1)} %copy-done), custom_call_target="tpu_custom_call" | custom-call | flops 1000000000 | bytes 1000000 | tf_op jit(solution)/shard_map/pallas_call | solution.py:688
  26.1 1.4 %collective-permute-done.9.gb_ref = f32[32,384]{1,0:T(8,128)S(1)} collective-permute-done((f32[32,384]{1,0:T(8,128)S(1)}, f32[32,384]{1,0:T(8,128)S(1)}, u32[]{:S(2)}, u32[]{:S(2)}) %collective-permute-start.9) | collective-permute-done | bytes 49184 | tf_op jit(solution)/shard_map/ppermute | solution.py:744
  27.4 0.0 collective-permute-done.10.ga_ref
  27.4 1.3 %shard_map.59 = (f32[128,256]{1,0:T(8,128)S(1)}, f32[128,256]{1,0:T(8,128)S(1)}, f32[144,512]{1,0:T(8,128)S(1)}, f32[16,144]{1,0:T(8,128)S(1)}, f32[16,144]{1,0:T(8,128)S(1)}) custom-call(f32[144,384]{1,0:T(8,128)S(1)} %get-tuple-element.60.y_ref, f32[160,384]{1,0:T(8,128)S(1)} %get-tuple-element.61.m_ref, f32[32,384]{1,0:T(8,128)S(1)} %collective-permute-done.9.gb_ref, ...), custom_call_target="tpu_custom_call" | custom-call | flops 1000000000 | bytes 1000000 | tf_op jit(solution)/shard_map/pallas_call | solution.py:688
  28.7 0.1 collective-permute-start.11
  28.8 2.8 %collective-permute-start.12 = (f32[16,144]{1,0:T(8,128)S(1)}, f32[16,144]{1,0:T(8,128)S(1)}, u32[]{:S(2)}, u32[]{:S(2)}) collective-permute-start(f32[16,144]{1,0:T(8,128)S(1)} %get-tuple-element.76), channel_id=1, source_target_pairs={{0,1},{1,0},{2,3},{3,2},{4,5},{5,4},{6,7},{7,6},{8,9},{9,8},{10,11... | collective-permute-start | bytes 27656 | tf_op jit(solution)/shard_map/ppermute | solution.py:745
  31.6 0.8 %shard_map.60 = (f32[144,384]{1,0:T(8,128)S(1)}, f32[1,128]{1,0:T(1,128)S(1)}) custom-call(f32[144,512]{1,0:T(8,128)S(1)} %get-tuple-element.70.t_ref, f32[1104,512]{1,0:T(8,128)S(1)} %copy-done, f32[256,256]{1,0:T(8,128)S(1)} %pad_add_fusion.both_ref, f32[128,256]{1,0:T(8,128)S(1)} %get-tuple-element.71.z_ref, f32[128,256]{1,0:T(8,128)S(1)} %get-tuple-element.72.w_ref, ...), custom_call_target="tpu_custom_call" | custom-call | flops 1000000000 | bytes 1000000 | tf_op jit(solution)/shard_map/pallas_call | solution.py:688
  32.5 0.0 collective-permute-done.11.refs_0_
  32.5 1.0 %collective-permute-done.12.refs_1_ = f32[16,144]{1,0:T(8,128)S(1)} collective-permute-done((f32[16,144]{1,0:T(8,128)S(1)}, f32[16,144]{1,0:T(8,128)S(1)}, u32[]{:S(2)}, u32[]{:S(2)}) %collective-permute-start.12) | collective-permute-done | bytes 9248 | tf_op jit(solution)/shard_map/ppermute | solution.py:745
  33.5 0.2 shard_map.61
  33.7 1.9 %collective-permute-start.13 = (f32[16,384]{1,0:T(8,128)S(1)}, f32[16,384]{1,0:T(8,128)S(1)}, u32[]{:S(2)}, u32[]{:S(2)}) collective-permute-start(f32[16,384]{1,0:T(8,128)S(1)} %get-tuple-element.78), channel_id=1, source_target_pairs={{0,1},{1,0},{2,3},{3,2},{4,8},{5,9},{6,10},{7,11},{8,4},{9,5},{10,... | collective-permute-start | bytes 73736 | tf_op jit(solution)/shard_map/ppermute | solution.py:744
  35.6 0.0 collective-permute-start.14
  35.6 0.4 shard_map.62
  36.0 1.6 %collective-permute-done.13.gb_ref = f32[16,384]{1,0:T(8,128)S(1)} collective-permute-done((f32[16,384]{1,0:T(8,128)S(1)}, f32[16,384]{1,0:T(8,128)S(1)}, u32[]{:S(2)}, u32[]{:S(2)}) %collective-permute-start.13) | collective-permute-done | bytes 24608 | tf_op jit(solution)/shard_map/ppermute | solution.py:744
  37.6 0.0 collective-permute-done.14.ga_ref
  37.6 0.3 shard_map.63
  37.9 9.3 %all_to_all.11 = f32[32,1,128]{2,1,0:T(1,128)S(1)} all-to-all(f32[32,1,128]{2,1,0:T(1,128)S(1)} %bitcast.5), channel_id=1, replica_groups=mesh['row'=8,'col'=4] {'row','col'}, dimensions={0} | all-to-all | bytes 32768 | tf_op jit(solution)/shard_map/all_to_all | solution.py:857
  47.2 1.3 %shard_map.64 = (f32[128,256]{1,0:T(8,128)}, f32[128,256]{1,0:T(8,128)}) custom-call(f32[32,128]{1,0:T(8,128)S(1)} %bitcast.4, f32[1104,512]{1,0:T(8,128)S(1)} %copy-done, f32[160,384]{1,0:T(8,128)S(1)} %get-tuple-element.61.m_ref, f32[96,256]{1,0:T(8,128)S(1)} %get-tuple-element.66.f_ref, f32[256,256]{1,0:T(8,128)S(1)} %pad_add_fusion.both_ref, ...), custom_call_target="tpu_custom_call" | custom-call | flops 1000000000 | bytes 1000000 | tf_op jit(solution)/shard_map/pallas_call | solution.py:688
  (3 shorter events, 0.0 us)
Async XLA Ops:
  1.8 9.6 %collective-permute-start = (f32[40,128]{1,0:T(8,128)S(1)}, f32[40,128]{1,0:T(8,128)S(1)}, u32[]{:S(2)}, u32[]{:S(2)}) collective-permute-start(f32[40,128]{1,0:T(8,128)S(1)} %get-tuple-element.45), channel_id=1, source_target_pairs={{0,4},{1,2},{2,1},{3,7},{4,0},{5,6},{6,5},{7,3},{8,12},{9,10},{10,... | collective-permute-start | bytes 61448 | tf_op jit(solution)/shard_map/ppermute | solution.py:744
  2.3 9.1 %collective-permute-start.1 = (f32[40,128]{1,0:T(8,128)S(1)}, f32[40,128]{1,0:T(8,128)S(1)}, u32[]{:S(2)}, u32[]{:S(2)}) collective-permute-start(f32[40,128]{1,0:T(8,128)S(1)} %get-tuple-element.46), channel_id=1, source_target_pairs={{0,1},{1,0},{2,3},{3,2},{4,5},{5,4},{6,7},{7,6},{8,9},{9,8},{10,11... | collective-permute-start | bytes 61448 | tf_op jit(solution)/shard_map/ppermute | solution.py:745
  6.4 7.9 %copy-start = (f32[1104,512]{1,0:T(8,128)S(1)}, f32[1104,512]{1,0:T(8,128)}, u32[]{:S(2)}) copy-start(f32[1104,512]{1,0:T(8,128)} %constant.6.clone.basis_ref) | copy-start | bytes 6782980
  6.4 10.4 %collective-permute-start.5 = (f32[8,128]{1,0:T(8,128)S(1)}, f32[8,128]{1,0:T(8,128)S(1)}, u32[]{:S(2)}, u32[]{:S(2)}) collective-permute-start(f32[8,128]{1,0:T(8,128)S(1)} %get-tuple-element.58), channel_id=1, source_target_pairs={{0,27},{1,26},{2,25},{3,24},{4,31},{5,30},{6,29},{7,28},{8,19},{9,... | collective-permute-start | bytes 12296 | tf_op jit(solution)/shard_map/ppermute | solution.py:748
  10.9 5.9 %collective-permute-start.4 = (f32[8,128]{1,0:T(8,128)S(1)}, f32[8,128]{1,0:T(8,128)S(1)}, u32[]{:S(2)}, u32[]{:S(2)}) collective-permute-start(f32[8,128]{1,0:T(8,128)S(1)} %get-tuple-element.58), channel_id=1, source_target_pairs={{0,11},{1,10},{2,9},{3,8},{4,15},{5,14},{6,13},{7,12},{8,3},{9,2},... | collective-permute-start | bytes 12296 | tf_op jit(solution)/shard_map/ppermute | solution.py:748
  11.6 4.2 %collective-permute-start.2 = (f32[32,384]{1,0:T(8,128)S(1)}, f32[32,384]{1,0:T(8,128)S(1)}, u32[]{:S(2)}, u32[]{:S(2)}) collective-permute-start(f32[32,384]{1,0:T(8,128)S(1)} %get-tuple-element.47), channel_id=1, source_target_pairs={{0,1},{1,0},{2,3},{3,2},{4,8},{5,9},{6,10},{7,11},{8,4},{9,5},{10,... | collective-permute-start | bytes 147464 | tf_op jit(solution)/shard_map/ppermute | solution.py:744
  11.7 4.1 %collective-permute-start.3 = (f32[32,384]{1,0:T(8,128)S(1)}, f32[32,384]{1,0:T(8,128)S(1)}, u32[]{:S(2)}, u32[]{:S(2)}) collective-permute-start(f32[32,384]{1,0:T(8,128)S(1)} %get-tuple-element.48), channel_id=1, source_target_pairs={{0,4},{4,0},{8,12},{12,8},{16,20},{20,16},{24,28},{28,24},{1,5},{5... | collective-permute-start | bytes 147464 | tf_op jit(solution)/shard_map/ppermute | solution.py:745
  14.4 4.6 %collective-permute-start.6 = (f32[8,128]{1,0:T(8,128)S(1)}, f32[8,128]{1,0:T(8,128)S(1)}, u32[]{:S(2)}, u32[]{:S(2)}) collective-permute-start(f32[8,128]{1,0:T(8,128)S(1)} %get-tuple-element.52.table_ref), channel_id=1, source_target_pairs={{0,16},{1,17},{2,18},{3,19},{4,20},{5,21},{6,22},{7,23},{8,24},{9,... | collective-permute-start | bytes 12296 | tf_op jit(solution)/shard_map/ppermute | solution.py:748
  19.0 4.0 %collective-permute-start.8 = (f32[32,144]{1,0:T(8,128)S(1)}, f32[32,144]{1,0:T(8,128)S(1)}, u32[]{:S(2)}, u32[]{:S(2)}) collective-permute-start(f32[32,144]{1,0:T(8,128)S(1)} %get-tuple-element.86), channel_id=1, source_target_pairs={{0,8},{1,2},{2,1},{3,11},{4,12},{5,6},{6,5},{7,15},{8,0},{9,10},{1... | collective-permute-start | bytes 55304 | tf_op jit(solution)/shard_map/ppermute | solution.py:744
  19.1 4.0 %collective-permute-start.7 = (f32[32,144]{1,0:T(8,128)S(1)}, f32[32,144]{1,0:T(8,128)S(1)}, u32[]{:S(2)}, u32[]{:S(2)}) collective-permute-start(f32[32,144]{1,0:T(8,128)S(1)} %get-tuple-element.87), channel_id=1, source_target_pairs={{0,1},{1,0},{2,3},{3,2},{4,5},{5,4},{6,7},{7,6},{8,9},{9,8},{10,11... | collective-permute-start | bytes 55304 | tf_op jit(solution)/shard_map/ppermute | solution.py:745
  23.3 4.2 %collective-permute-start.9 = (f32[32,384]{1,0:T(8,128)S(1)}, f32[32,384]{1,0:T(8,128)S(1)}, u32[]{:S(2)}, u32[]{:S(2)}) collective-permute-start(f32[32,384]{1,0:T(8,128)S(1)} %get-tuple-element.62), channel_id=1, source_target_pairs={{0,1},{1,0},{2,3},{3,2},{4,8},{5,9},{6,10},{7,11},{8,4},{9,5},{10,... | collective-permute-start | bytes 147464 | tf_op jit(solution)/shard_map/ppermute | solution.py:744
  24.8 2.6 %collective-permute-start.10 = (f32[32,384]{1,0:T(8,128)S(1)}, f32[32,384]{1,0:T(8,128)S(1)}, u32[]{:S(2)}, u32[]{:S(2)}) collective-permute-start(f32[32,384]{1,0:T(8,128)S(1)} %get-tuple-element.63), channel_id=1, source_target_pairs={{0,4},{4,0},{8,12},{12,8},{16,20},{20,16},{24,28},{28,24},{1,5},{5... | collective-permute-start | bytes 147464 | tf_op jit(solution)/shard_map/ppermute | solution.py:745
  28.7 3.8 %collective-permute-start.11 = (f32[16,144]{1,0:T(8,128)S(1)}, f32[16,144]{1,0:T(8,128)S(1)}, u32[]{:S(2)}, u32[]{:S(2)}) collective-permute-start(f32[16,144]{1,0:T(8,128)S(1)} %get-tuple-element.75), channel_id=1, source_target_pairs={{0,4},{1,2},{2,1},{3,7},{4,0},{5,6},{6,5},{7,3},{8,12},{9,10},{10,... | collective-permute-start | bytes 27656 | tf_op jit(solution)/shard_map/ppermute | solution.py:744
  28.8 4.7 %collective-permute-start.12 = (f32[16,144]{1,0:T(8,128)S(1)}, f32[16,144]{1,0:T(8,128)S(1)}, u32[]{:S(2)}, u32[]{:S(2)}) collective-permute-start(f32[16,144]{1,0:T(8,128)S(1)} %get-tuple-element.76), channel_id=1, source_target_pairs={{0,1},{1,0},{2,3},{3,2},{4,5},{5,4},{6,7},{7,6},{8,9},{9,8},{10,11... | collective-permute-start | bytes 27656 | tf_op jit(solution)/shard_map/ppermute | solution.py:745
  33.7 3.9 %collective-permute-start.13 = (f32[16,384]{1,0:T(8,128)S(1)}, f32[16,384]{1,0:T(8,128)S(1)}, u32[]{:S(2)}, u32[]{:S(2)}) collective-permute-start(f32[16,384]{1,0:T(8,128)S(1)} %get-tuple-element.78), channel_id=1, source_target_pairs={{0,1},{1,0},{2,3},{3,2},{4,8},{5,9},{6,10},{7,11},{8,4},{9,5},{10,... | collective-permute-start | bytes 73736 | tf_op jit(solution)/shard_map/ppermute | solution.py:744
  35.6 2.0 %collective-permute-start.14 = (f32[16,384]{1,0:T(8,128)S(1)}, f32[16,384]{1,0:T(8,128)S(1)}, u32[]{:S(2)}, u32[]{:S(2)}) collective-permute-start(f32[16,384]{1,0:T(8,128)S(1)} %get-tuple-element.79), channel_id=1, source_target_pairs={{0,4},{4,0},{8,12},{12,8},{16,20},{20,16},{24,28},{28,24},{1,5},{5... | collective-permute-start | bytes 73736 | tf_op jit(solution)/shard_map/ppermute | solution.py:745

commit v17 on v16

--- a/solution.py
+++ b/solution.py
@@ -705,10 +705,10 @@
     for i in range(counts[0]):
         for j in range(counts[1]):
             at = [i, j]
-            if at[axis] in (0, counts[axis] - 1):
+            if bit and at[axis] in (0, counts[axis] - 1):
                 at[1 - axis] ^= bit
             else:
-                at[axis] += 1 if at[axis] % 2 else -1
+                at[axis] = (at[axis] + (1 if at[axis] % 2 else -1)) % counts[axis]
             found.append((i * counts[1] + j, at[0] * counts[1] + at[1]))
     return found
 
@@ -725,9 +725,9 @@
         return np.logical_or.reduce([known, *(known[[b for _, b in pairs]] for pairs in swaps)])
 
     even = [xor_pairs(counts, 0, 1), xor_pairs(counts, 1, 0)]
-    own = meet(xor_pairs(counts, 2, 3), xor_pairs(counts, 6, 3))
+    own = meet(xor_pairs(counts, 2, 3))
     known = meet(even[0], odd_pairs(counts, 1, 1))
-    known = meet(even[1], odd_pairs(counts, 0, 1), xor_pairs(counts, 4, 0)) | own
+    known = meet(even[1], odd_pairs(counts, 0, 0), xor_pairs(counts, 4, 2)) | own
     known = meet(even[0], odd_pairs(counts, 1, 2))
     return meet(even[1], odd_pairs(counts, 0, 1)).all()
 
@@ -759,7 +759,7 @@
                 bit *= 2
     ga, gb = swap(a, b, "col")
     edge_stats, own = call(statistics_kernel, [(1, 128), (depth, 128)], both, table)
-    far = [small_swap(own, 2, 3), small_swap(own, 6, 3)]
+    far = [small_swap(own, 2, 3)]
     r3, h3, b, a, table = call(
         functools.partial(widen_kernel, counts),
         [(128, 128)] * 2 + [(24 + depth, FC)] * 2 + [(depth, 128)],
@@ -768,9 +768,9 @@
         gb,
         ga,
     )
-    ga, gb = swap(a, b, "row")
+    ga, gb = swap(a, b, "row", 0)
     weight, table = call(weights_kernel, [(EXT, 2 * SPEC), (depth, 128)], both, table, basis)
-    far.append(small_swap(table, 4, 0))
+    far.append(small_swap(table, 4, 2))
     t = call(forward_kernel, [(EXT, 2 * SPEC)], both, r3, basis)[0]
     t, table, b, a = call(
         functools.partial(first_kernel, counts),

time: 48.6 us -> 48 us (0.988)
  waiting for transfers between devices: 8.53 us -> 7.38 us
  blocking collectives: 9.31 us -> 10.1 us
    ppermute x6, starting transfers between devices: 11.5 us -> 7.47 us  [swap(): return (lax.ppermute(a, axis, pairs_from(lax.axis_size(axis), 0)), gb)]
    ppermute x6, starting transfers between devices: 4.26 us -> 6.99 us  [swap(): lax.ppermute(b, both_axes, odd_pairs(counts, both_axes.index(axis), bit))]
    ppermute x3 -> x2, waiting for transfers between devices: 2.19 us -> 0.21 us  [small_swap(): return lax.ppermute(x, both_axes, xor_pairs(counts, rows, cols))]
    ppermute x6, waiting for transfers between devices: 1.13 us -> 3.07 us  [swap(): return (lax.ppermute(a, axis, pairs_from(lax.axis_size(axis), 0)), gb)]
    ppermute x6, waiting for transfers between devices: 5.2 us -> 4.1 us  [swap(): lax.ppermute(b, both_axes, odd_pairs(counts, both_axes.index(axis), bit))]
    ppermute x3 -> x2, starting transfers between devices: 5.09 us -> 6.18 us  [small_swap(): return lax.ppermute(x, both_axes, xor_pairs(counts, rows, cols))]
    all_to_all x1, blocking collectives: 9.31 us -> 10.1 us  [body(): stats = lax.all_to_all(stats, both_axes, 0, 0, tiled=True)]
  transfers between devices with their start and end apart: 15 -> 14, of which waited for: 7 -> 6; matrix products, arithmetic and copies ran while one was open for 0% -> 0% of each run, Pallas kernels for 10% -> 10%
where the time goes in v17:
time: 48 us; the launch traced here: 47.8 us
  starting transfers between devices  20.6 us (43%)
  blocking collectives  10.1 us (21%)
  Pallas kernels  7.98 us (17%)
  waiting for transfers between devices  7.38 us (15%)
  other arithmetic  1 us (2%)
  between operations  0.76 us (2%)
    all_to_all x1, blocking collectives, body(): stats = lax.all_to_all(stats, both_axes, 0, 0, tiled=True)  10.1 us
    pallas_call x15, Pallas kernels, call(): pl.pallas_call(kernel, out_shape=shapes, compiler_params=pltpu.CompilerPa...  7.98 us
    ppermute x6, starting transfers between devices, swap(): return (lax.ppermute(a, axis, pairs_from(lax.axis_size(axis), 0)), gb)  7.47 us
    ppermute x6, starting transfers between devices, swap(): lax.ppermute(b, both_axes, odd_pairs(counts, both_axes.index(axis), bit))  6.99 us
    ppermute x2, starting transfers between devices, small_swap(): return lax.ppermute(x, both_axes, xor_pairs(counts, rows, cols))  6.18 us
    ppermute x6, waiting for transfers between devices, swap(): lax.ppermute(b, both_axes, odd_pairs(counts, both_axes.index(axis), bit))  4.1 us
    ppermute x6, waiting for transfers between devices, swap(): return (lax.ppermute(a, axis, pairs_from(lax.axis_size(axis), 0)), gb)  3.07 us
    add x1, other arithmetic, body(): jnp.pad(noise, ((0, TR), (0, 0))) + jnp.pad(height, ((TR, 0), (0, 0)))  0.99 us
  transfers between devices with their start and end apart: 14, of which 6 were waited for; matrix products, arithmetic and copies ran while one was open for 0% of the time, Pallas kernels for 10%

profile of v17, /device:TPU:0, one launch (start us, length us, event | category | flops | bytes accessed | tf_op | source)
XLA Modules:
  0.0 47.8 jit_solution(8249409202762699652)
XLA Ops:
  0.6 1.0 %pad_add_fusion.both_ref = f32[256,256]{1,0:T(8,128)S(1)} fusion(f32[128,256]{1,0:T(8,128)} %param.3, f32[128,256]{1,0:T(8,128)} %param.4), kind=kLoop, calls=%fused_computation | loop fusion | flops 65536 | bytes 524288 | tf_op jit(solution)/shard_map/add | solution.py:750
  1.6 0.2 shard_map.50
  1.8 0.5 %collective-permute-start = (f32[40,128]{1,0:T(8,128)S(1)}, f32[40,128]{1,0:T(8,128)S(1)}, u32[]{:S(2)}, u32[]{:S(2)}) collective-permute-start(f32[40,128]{1,0:T(8,128)S(1)} %get-tuple-element.45), channel_id=1, source_target_pairs={{0,4},{1,2},{2,1},{3,7},{4,0},{5,6},{6,5},{7,3},{8,12},{9,10},{10,... | collective-permute-start | bytes 61448 | tf_op jit(solution)/shard_map/ppermute | solution.py:744
  2.3 4.0 %collective-permute-start.1 = (f32[40,128]{1,0:T(8,128)S(1)}, f32[40,128]{1,0:T(8,128)S(1)}, u32[]{:S(2)}, u32[]{:S(2)}) collective-permute-start(f32[40,128]{1,0:T(8,128)S(1)} %get-tuple-element.46), channel_id=1, source_target_pairs={{0,1},{1,0},{2,3},{3,2},{4,5},{5,4},{6,7},{7,6},{8,9},{9,8},{10,11... | collective-permute-start | bytes 61448 | tf_op jit(solution)/shard_map/ppermute | solution.py:745
  6.3 0.1 shard_map.56
  6.4 0.0 copy-start
  6.4 2.5 %collective-permute-start.4 = (f32[8,128]{1,0:T(8,128)S(1)}, f32[8,128]{1,0:T(8,128)S(1)}, u32[]{:S(2)}, u32[]{:S(2)}) collective-permute-start(f32[8,128]{1,0:T(8,128)S(1)} %get-tuple-element.58), channel_id=1, source_target_pairs={{0,11},{1,10},{2,9},{3,8},{4,15},{5,14},{6,13},{7,12},{8,3},{9,2},... | collective-permute-start | bytes 12296 | tf_op jit(solution)/shard_map/ppermute | solution.py:748
  8.9 0.0 collective-permute-done.gb_ref
  8.9 0.0 collective-permute-done.1.ga_ref
  8.9 0.2 shard_map.51
  9.1 1.3 %collective-permute-start.2 = (f32[32,384]{1,0:T(8,128)S(1)}, f32[32,384]{1,0:T(8,128)S(1)}, u32[]{:S(2)}, u32[]{:S(2)}) collective-permute-start(f32[32,384]{1,0:T(8,128)S(1)} %get-tuple-element.47), channel_id=1, source_target_pairs={{0,28},{1,29},{2,30},{3,31},{4,8},{5,9},{6,10},{7,11},{8,4},{9,5},... | collective-permute-start | bytes 147464 | tf_op jit(solution)/shard_map/ppermute | solution.py:744
  10.4 0.0 collective-permute-start.3
  10.4 0.0 copy-done
  10.4 0.1 shard_map.53
  10.6 3.7 %collective-permute-start.5 = (f32[8,128]{1,0:T(8,128)S(1)}, f32[8,128]{1,0:T(8,128)S(1)}, u32[]{:S(2)}, u32[]{:S(2)}) collective-permute-start(f32[8,128]{1,0:T(8,128)S(1)} %get-tuple-element.52.table_ref), channel_id=1, source_target_pairs={{0,18},{1,19},{2,16},{3,17},{4,22},{5,23},{6,20},{7,21},{8,26},{9,... | collective-permute-start | bytes 12296 | tf_op jit(solution)/shard_map/ppermute | solution.py:748
  14.2 0.6 %shard_map.52.tile_ref = f32[144,512]{1,0:T(8,128)S(1)} custom-call(f32[256,256]{1,0:T(8,128)S(1)} %pad_add_fusion.both_ref, f32[128,128]{1,0:T(8,128)S(1)} %get-tuple-element.49.r3_ref, f32[1104,512]{1,0:T(8,128)S(1)} %copy-done), custom_call_target="tpu_custom_call" | custom-call | flops 1000000000 | bytes 1000000 | tf_op jit(solution)/shard_map/pallas_call | solution.py:688
  14.8 0.0 collective-permute-done.2.gb_ref
  14.8 0.0 collective-permute-done.3.ga_ref
  14.8 1.0 %shard_map.54 = (f32[144,512]{1,0:T(8,128)S(1)}, f32[8,128]{1,0:T(8,128)S(1)}, f32[24,144]{1,0:T(8,128)S(1)}, f32[24,144]{1,0:T(8,128)S(1)}) custom-call(f32[32,384]{1,0:T(8,128)S(1)} %collective-permute-done.2.gb_ref, f32[32,384]{1,0:T(8,128)S(1)} %collective-permute-done.3.ga_ref, f32[144,512]{1,0:T(8,128)S(1)} %shard_map.52.tile_ref, ...), custom_call_target="tpu_custom_call" | custom-call | flops 1000000000 | bytes 1000000 | tf_op jit(solution)/shard_map/pallas_call | solution.py:688
  15.8 0.0 collective-permute-done.4
  15.8 0.2 collective-permute-done.5
  16.1 2.1 %collective-permute-start.7 = (f32[32,144]{1,0:T(8,128)S(1)}, f32[32,144]{1,0:T(8,128)S(1)}, u32[]{:S(2)}, u32[]{:S(2)}) collective-permute-start(f32[32,144]{1,0:T(8,128)S(1)} %get-tuple-element.86), channel_id=1, source_target_pairs={{0,8},{1,2},{2,1},{3,11},{4,12},{5,6},{6,5},{7,15},{8,0},{9,10},{1... | collective-permute-start | bytes 55304 | tf_op jit(solution)/shard_map/ppermute | solution.py:744
  18.2 1.0 %collective-permute-start.6 = (f32[32,144]{1,0:T(8,128)S(1)}, f32[32,144]{1,0:T(8,128)S(1)}, u32[]{:S(2)}, u32[]{:S(2)}) collective-permute-start(f32[32,144]{1,0:T(8,128)S(1)} %get-tuple-element.87), channel_id=1, source_target_pairs={{0,1},{1,0},{2,3},{3,2},{4,5},{5,4},{6,7},{7,6},{8,9},{9,8},{10,11... | collective-permute-start | bytes 55304 | tf_op jit(solution)/shard_map/ppermute | solution.py:745
  19.2 0.8 %shard_map.55 = (f32[144,384]{1,0:T(8,128)S(1)}, f32[160,384]{1,0:T(8,128)S(1)}) custom-call(f32[144,512]{1,0:T(8,128)S(1)} %get-tuple-element.53.t_ref, f32[1104,512]{1,0:T(8,128)S(1)} %copy-done, f32[256,256]{1,0:T(8,128)S(1)} %pad_add_fusion.both_ref, f32[128,128]{1,0:T(8,128)S(1)} %get-tuple-element.54.h3_ref, ...), custom_call_target="tpu_custom_call" | custom-call | flops 1000000000 | bytes 1000000 | tf_op jit(solution)/shard_map/pallas_call | solution.py:688
  20.0 0.1 collective-permute-done.7.refs_1_
  20.1 2.0 %collective-permute-done.6.refs_0_ = f32[32,144]{1,0:T(8,128)S(1)} collective-permute-done((f32[32,144]{1,0:T(8,128)S(1)}, f32[32,144]{1,0:T(8,128)S(1)}, u32[]{:S(2)}, u32[]{:S(2)}) %collective-permute-start.6) | collective-permute-done | bytes 18464 | tf_op jit(solution)/shard_map/ppermute | solution.py:745
  22.1 0.2 shard_map.57
  22.3 1.1 %collective-permute-start.8 = (f32[32,384]{1,0:T(8,128)S(1)}, f32[32,384]{1,0:T(8,128)S(1)}, u32[]{:S(2)}, u32[]{:S(2)}) collective-permute-start(f32[32,384]{1,0:T(8,128)S(1)} %get-tuple-element.62), channel_id=1, source_target_pairs={{0,1},{1,0},{2,3},{3,2},{4,8},{5,9},{6,10},{7,11},{8,4},{9,5},{10,... | collective-permute-start | bytes 147464 | tf_op jit(solution)/shard_map/ppermute | solution.py:744
  23.3 0.0 collective-permute-start.9
  23.3 0.7 %shard_map.58 = (f32[96,256]{1,0:T(8,128)S(1)}, f32[96,256]{1,0:T(8,128)S(1)}, f32[144,384]{1,0:T(8,128)S(1)}, f32[144,384]{1,0:T(8,128)S(1)}, f32[16,128]{1,0:T(8,128)S(1)}) custom-call(f32[144,384]{1,0:T(8,128)S(1)} %get-tuple-element.60.y_ref, f32[160,384]{1,0:T(8,128)S(1)} %get-tuple-element.61.m_ref, f32[1104,512]{1,0:T(8,128)S(1)} %copy-done), custom_call_target="tpu_custom_call" | custom-call | flops 1000000000 | bytes 1000000 | tf_op jit(solution)/shard_map/pallas_call | solution.py:688
  24.0 2.4 %collective-permute-done.8.gb_ref = f32[32,384]{1,0:T(8,128)S(1)} collective-permute-done((f32[32,384]{1,0:T(8,128)S(1)}, f32[32,384]{1,0:T(8,128)S(1)}, u32[]{:S(2)}, u32[]{:S(2)}) %collective-permute-start.8) | collective-permute-done | bytes 49184 | tf_op jit(solution)/shard_map/ppermute | solution.py:744
  26.4 0.0 collective-permute-done.9.ga_ref
  26.4 1.3 %shard_map.59 = (f32[128,256]{1,0:T(8,128)S(1)}, f32[128,256]{1,0:T(8,128)S(1)}, f32[144,512]{1,0:T(8,128)S(1)}, f32[16,144]{1,0:T(8,128)S(1)}, f32[16,144]{1,0:T(8,128)S(1)}) custom-call(f32[144,384]{1,0:T(8,128)S(1)} %get-tuple-element.60.y_ref, f32[160,384]{1,0:T(8,128)S(1)} %get-tuple-element.61.m_ref, f32[32,384]{1,0:T(8,128)S(1)} %collective-permute-done.8.gb_ref, ...), custom_call_target="tpu_custom_call" | custom-call | flops 1000000000 | bytes 1000000 | tf_op jit(solution)/shard_map/pallas_call | solution.py:688
  27.7 0.1 collective-permute-start.10
  27.8 2.5 %collective-permute-start.11 = (f32[16,144]{1,0:T(8,128)S(1)}, f32[16,144]{1,0:T(8,128)S(1)}, u32[]{:S(2)}, u32[]{:S(2)}) collective-permute-start(f32[16,144]{1,0:T(8,128)S(1)} %get-tuple-element.76), channel_id=1, source_target_pairs={{0,1},{1,0},{2,3},{3,2},{4,5},{5,4},{6,7},{7,6},{8,9},{9,8},{10,11... | collective-permute-start | bytes 27656 | tf_op jit(solution)/shard_map/ppermute | solution.py:745
  30.3 0.8 %shard_map.60 = (f32[144,384]{1,0:T(8,128)S(1)}, f32[1,128]{1,0:T(1,128)S(1)}) custom-call(f32[144,512]{1,0:T(8,128)S(1)} %get-tuple-element.70.t_ref, f32[1104,512]{1,0:T(8,128)S(1)} %copy-done, f32[256,256]{1,0:T(8,128)S(1)} %pad_add_fusion.both_ref, f32[128,256]{1,0:T(8,128)S(1)} %get-tuple-element.71.z_ref, f32[128,256]{1,0:T(8,128)S(1)} %get-tuple-element.72.w_ref, ...), custom_call_target="tpu_custom_call" | custom-call | flops 1000000000 | bytes 1000000 | tf_op jit(solution)/shard_map/pallas_call | solution.py:688
  31.1 0.0 collective-permute-done.10.refs_0_
  31.1 1.0 %collective-permute-done.11.refs_1_ = f32[16,144]{1,0:T(8,128)S(1)} collective-permute-done((f32[16,144]{1,0:T(8,128)S(1)}, f32[16,144]{1,0:T(8,128)S(1)}, u32[]{:S(2)}, u32[]{:S(2)}) %collective-permute-start.11) | collective-permute-done | bytes 9248 | tf_op jit(solution)/shard_map/ppermute | solution.py:745
  32.2 0.2 shard_map.61
  32.3 1.9 %collective-permute-start.12 = (f32[16,384]{1,0:T(8,128)S(1)}, f32[16,384]{1,0:T(8,128)S(1)}, u32[]{:S(2)}, u32[]{:S(2)}) collective-permute-start(f32[16,384]{1,0:T(8,128)S(1)} %get-tuple-element.78), channel_id=1, source_target_pairs={{0,1},{1,0},{2,3},{3,2},{4,8},{5,9},{6,10},{7,11},{8,4},{9,5},{10,... | collective-permute-start | bytes 73736 | tf_op jit(solution)/shard_map/ppermute | solution.py:744
  34.2 0.0 collective-permute-start.13
  34.2 0.4 shard_map.62
  34.6 1.6 %collective-permute-done.12.gb_ref = f32[16,384]{1,0:T(8,128)S(1)} collective-permute-done((f32[16,384]{1,0:T(8,128)S(1)}, f32[16,384]{1,0:T(8,128)S(1)}, u32[]{:S(2)}, u32[]{:S(2)}) %collective-permute-start.12) | collective-permute-done | bytes 24608 | tf_op jit(solution)/shard_map/ppermute | solution.py:744
  36.2 0.0 collective-permute-done.13.ga_ref
  36.2 0.3 shard_map.63
  36.5 10.1 %all_to_all.11 = f32[32,1,128]{2,1,0:T(1,128)S(1)} all-to-all(f32[32,1,128]{2,1,0:T(1,128)S(1)} %bitcast.5), channel_id=1, replica_groups=mesh['row'=8,'col'=4] {'row','col'}, dimensions={0} | all-to-all | bytes 32768 | tf_op jit(solution)/shard_map/all_to_all | solution.py:857
  46.6 1.3 %shard_map.64 = (f32[128,256]{1,0:T(8,128)}, f32[128,256]{1,0:T(8,128)}) custom-call(f32[32,128]{1,0:T(8,128)S(1)} %bitcast.4, f32[1104,512]{1,0:T(8,128)S(1)} %copy-done, f32[160,384]{1,0:T(8,128)S(1)} %get-tuple-element.61.m_ref, f32[96,256]{1,0:T(8,128)S(1)} %get-tuple-element.66.f_ref, f32[256,256]{1,0:T(8,128)S(1)} %pad_add_fusion.both_ref, ...), custom_call_target="tpu_custom_call" | custom-call | flops 1000000000 | bytes 1000000 | tf_op jit(solution)/shard_map/pallas_call | solution.py:688
  (2 shorter events, 0.0 us)
Async XLA Ops:
  1.8 7.1 %collective-permute-start = (f32[40,128]{1,0:T(8,128)S(1)}, f32[40,128]{1,0:T(8,128)S(1)}, u32[]{:S(2)}, u32[]{:S(2)}) collective-permute-start(f32[40,128]{1,0:T(8,128)S(1)} %get-tuple-element.45), channel_id=1, source_target_pairs={{0,4},{1,2},{2,1},{3,7},{4,0},{5,6},{6,5},{7,3},{8,12},{9,10},{10,... | collective-permute-start | bytes 61448 | tf_op jit(solution)/shard_map/ppermute | solution.py:744
  2.3 6.6 %collective-permute-start.1 = (f32[40,128]{1,0:T(8,128)S(1)}, f32[40,128]{1,0:T(8,128)S(1)}, u32[]{:S(2)}, u32[]{:S(2)}) collective-permute-start(f32[40,128]{1,0:T(8,128)S(1)} %get-tuple-element.46), channel_id=1, source_target_pairs={{0,1},{1,0},{2,3},{3,2},{4,5},{5,4},{6,7},{7,6},{8,9},{9,8},{10,11... | collective-permute-start | bytes 61448 | tf_op jit(solution)/shard_map/ppermute | solution.py:745
  6.4 4.0 %copy-start = (f32[1104,512]{1,0:T(8,128)S(1)}, f32[1104,512]{1,0:T(8,128)}, u32[]{:S(2)}) copy-start(f32[1104,512]{1,0:T(8,128)} %constant.6.clone.basis_ref) | copy-start | bytes 6782980
  6.4 9.4 %collective-permute-start.4 = (f32[8,128]{1,0:T(8,128)S(1)}, f32[8,128]{1,0:T(8,128)S(1)}, u32[]{:S(2)}, u32[]{:S(2)}) collective-permute-start(f32[8,128]{1,0:T(8,128)S(1)} %get-tuple-element.58), channel_id=1, source_target_pairs={{0,11},{1,10},{2,9},{3,8},{4,15},{5,14},{6,13},{7,12},{8,3},{9,2},... | collective-permute-start | bytes 12296 | tf_op jit(solution)/shard_map/ppermute | solution.py:748
  9.1 5.7 %collective-permute-start.2 = (f32[32,384]{1,0:T(8,128)S(1)}, f32[32,384]{1,0:T(8,128)S(1)}, u32[]{:S(2)}, u32[]{:S(2)}) collective-permute-start(f32[32,384]{1,0:T(8,128)S(1)} %get-tuple-element.47), channel_id=1, source_target_pairs={{0,28},{1,29},{2,30},{3,31},{4,8},{5,9},{6,10},{7,11},{8,4},{9,5},... | collective-permute-start | bytes 147464 | tf_op jit(solution)/shard_map/ppermute | solution.py:744
  10.4 4.4 %collective-permute-start.3 = (f32[32,384]{1,0:T(8,128)S(1)}, f32[32,384]{1,0:T(8,128)S(1)}, u32[]{:S(2)}, u32[]{:S(2)}) collective-permute-start(f32[32,384]{1,0:T(8,128)S(1)} %get-tuple-element.48), channel_id=1, source_target_pairs={{0,4},{4,0},{8,12},{12,8},{16,20},{20,16},{24,28},{28,24},{1,5},{5... | collective-permute-start | bytes 147464 | tf_op jit(solution)/shard_map/ppermute | solution.py:745
  10.6 5.5 %collective-permute-start.5 = (f32[8,128]{1,0:T(8,128)S(1)}, f32[8,128]{1,0:T(8,128)S(1)}, u32[]{:S(2)}, u32[]{:S(2)}) collective-permute-start(f32[8,128]{1,0:T(8,128)S(1)} %get-tuple-element.52.table_ref), channel_id=1, source_target_pairs={{0,18},{1,19},{2,16},{3,17},{4,22},{5,23},{6,20},{7,21},{8,26},{9,... | collective-permute-start | bytes 12296 | tf_op jit(solution)/shard_map/ppermute | solution.py:748
  16.1 4.0 %collective-permute-start.7 = (f32[32,144]{1,0:T(8,128)S(1)}, f32[32,144]{1,0:T(8,128)S(1)}, u32[]{:S(2)}, u32[]{:S(2)}) collective-permute-start(f32[32,144]{1,0:T(8,128)S(1)} %get-tuple-element.86), channel_id=1, source_target_pairs={{0,8},{1,2},{2,1},{3,11},{4,12},{5,6},{6,5},{7,15},{8,0},{9,10},{1... | collective-permute-start | bytes 55304 | tf_op jit(solution)/shard_map/ppermute | solution.py:744
  18.2 3.9 %collective-permute-start.6 = (f32[32,144]{1,0:T(8,128)S(1)}, f32[32,144]{1,0:T(8,128)S(1)}, u32[]{:S(2)}, u32[]{:S(2)}) collective-permute-start(f32[32,144]{1,0:T(8,128)S(1)} %get-tuple-element.87), channel_id=1, source_target_pairs={{0,1},{1,0},{2,3},{3,2},{4,5},{5,4},{6,7},{7,6},{8,9},{9,8},{10,11... | collective-permute-start | bytes 55304 | tf_op jit(solution)/shard_map/ppermute | solution.py:745
  22.3 4.2 %collective-permute-start.8 = (f32[32,384]{1,0:T(8,128)S(1)}, f32[32,384]{1,0:T(8,128)S(1)}, u32[]{:S(2)}, u32[]{:S(2)}) collective-permute-start(f32[32,384]{1,0:T(8,128)S(1)} %get-tuple-element.62), channel_id=1, source_target_pairs={{0,1},{1,0},{2,3},{3,2},{4,8},{5,9},{6,10},{7,11},{8,4},{9,5},{10,... | collective-permute-start | bytes 147464 | tf_op jit(solution)/shard_map/ppermute | solution.py:744
  23.3 3.1 %collective-permute-start.9 = (f32[32,384]{1,0:T(8,128)S(1)}, f32[32,384]{1,0:T(8,128)S(1)}, u32[]{:S(2)}, u32[]{:S(2)}) collective-permute-start(f32[32,384]{1,0:T(8,128)S(1)} %get-tuple-element.63), channel_id=1, source_target_pairs={{0,4},{4,0},{8,12},{12,8},{16,20},{20,16},{24,28},{28,24},{1,5},{5... | collective-permute-start | bytes 147464 | tf_op jit(solution)/shard_map/ppermute | solution.py:745
  27.7 3.4 %collective-permute-start.10 = (f32[16,144]{1,0:T(8,128)S(1)}, f32[16,144]{1,0:T(8,128)S(1)}, u32[]{:S(2)}, u32[]{:S(2)}) collective-permute-start(f32[16,144]{1,0:T(8,128)S(1)} %get-tuple-element.75), channel_id=1, source_target_pairs={{0,4},{1,2},{2,1},{3,7},{4,0},{5,6},{6,5},{7,3},{8,12},{9,10},{10,... | collective-permute-start | bytes 27656 | tf_op jit(solution)/shard_map/ppermute | solution.py:744
  27.8 4.4 %collective-permute-start.11 = (f32[16,144]{1,0:T(8,128)S(1)}, f32[16,144]{1,0:T(8,128)S(1)}, u32[]{:S(2)}, u32[]{:S(2)}) collective-permute-start(f32[16,144]{1,0:T(8,128)S(1)} %get-tuple-element.76), channel_id=1, source_target_pairs={{0,1},{1,0},{2,3},{3,2},{4,5},{5,4},{6,7},{7,6},{8,9},{9,8},{10,11... | collective-permute-start | bytes 27656 | tf_op jit(solution)/shard_map/ppermute | solution.py:745
  32.3 3.9 %collective-permute-start.12 = (f32[16,384]{1,0:T(8,128)S(1)}, f32[16,384]{1,0:T(8,128)S(1)}, u32[]{:S(2)}, u32[]{:S(2)}) collective-permute-start(f32[16,384]{1,0:T(8,128)S(1)} %get-tuple-element.78), channel_id=1, source_target_pairs={{0,1},{1,0},{2,3},{3,2},{4,8},{5,9},{6,10},{7,11},{8,4},{9,5},{10,... | collective-permute-start | bytes 73736 | tf_op jit(solution)/shard_map/ppermute | solution.py:744
  34.2 2.0 %collective-permute-start.13 = (f32[16,384]{1,0:T(8,128)S(1)}, f32[16,384]{1,0:T(8,128)S(1)}, u32[]{:S(2)}, u32[]{:S(2)}) collective-permute-start(f32[16,384]{1,0:T(8,128)S(1)} %get-tuple-element.79), channel_id=1, source_target_pairs={{0,4},{4,0},{8,12},{12,8},{16,20},{20,16},{24,28},{28,24},{1,5},{5... | collective-permute-start | bytes 73736 | tf_op jit(solution)/shard_map/ppermute | solution.py:745

commit v18 on v14

--- a/solution.py
+++ b/solution.py
@@ -341,6 +341,31 @@
     return before, after
 
 
+def fold(rows, table):
+    lane = lanes_of((8, 128))
+    free = (lane >= 32) & (lane < 96)
+    third = jnp.concatenate(
+        [
+            jnp.where(free, pltpu.roll(table, 32, 1), rows[:8, 256:]),
+            jnp.where(free, pltpu.roll(table, 96, 1), rows[8:16, 256:]),
+            rows[16:, 256:],
+        ],
+        axis=0,
+    )
+    return jnp.concatenate([rows[:, :256], third], axis=1)
+
+
+def unfold(ref):
+    low, high = ref[:8, 256:], ref[8:16, 256:]
+    return jnp.where(lanes_of((8, 128)) < 64, pltpu.roll(low, 96, 1), pltpu.roll(high, 32, 1))
+
+
+def row_sides(index, count, ga_ref, gb_ref, rows):
+    lane = lanes_of((1, FC))
+    used = (lane < 288) | (lane >= 352)
+    return [jnp.where(used, x, 0.0) for x in sides(index, count, ga_ref[rows], gb_ref[rows])]
+
+
 def send(index, a_ref, b_ref, before, after):
     even = is_even(index)
     a_ref[...] = jnp.where(even, after, before)
@@ -387,17 +412,16 @@
     r, h = both_ref[:TR], both_ref[TR:]
     table = merged(own_ref[...], ga_ref[32:], gb_ref[32:])
     table_ref[...] = table
-    wide = jnp.concatenate([table, jnp.zeros((table.shape[0], FC - 128), jnp.float32)], axis=1)
 
     def strip(r_rows, h_rows):
-        return jnp.concatenate(
+        rows = jnp.concatenate(
             [
                 jnp.concatenate([r[r_rows], r3[r_rows]], axis=1),
                 jnp.concatenate([h[h_rows], h3[h_rows]], axis=1),
-                wide,
             ],
             axis=0,
         )
+        return fold(rows, table)
 
     send(i, a_ref, b_ref, strip(slice(0, 8), slice(0, 16)), strip(slice(120, 128), slice(112, 128)))
 
@@ -429,17 +453,17 @@
     a_ref,
 ):
     i, j = place()
-    above, below = sides(i, counts[0], ga_ref[:8], gb_ref[:8])
+    above, below = row_sides(i, counts[0], ga_ref, gb_ref, slice(0, 8))
     u = column_transform(jnp.concatenate([below, above], axis=0), basis_ref)
     t = (tile_ref[...] + row_transform(u, basis_ref, halo_rows)) * weights_ref[...]
     t_ref[...] = t
     send(j, a_ref, b_ref, *strips_of(t, basis_ref, 24))
-    table_out[...] = merged(table_ref[...], ga_ref[24:, :128], gb_ref[24:, :128])
+    table_out[...] = merged(table_ref[...], unfold(ga_ref), unfold(gb_ref))
 
 
 def inverse_kernel(counts, t_ref, basis_ref, both_ref, h3_ref, gb_ref, ga_ref, y_ref, m_ref):
     y_ref[...] = solution_of(t_ref[...], basis_ref)
-    above, below = sides(lax.axis_index("row"), counts[0], ga_ref[8:24], gb_ref[8:24])
+    above, below = row_sides(lax.axis_index("row"), counts[0], ga_ref, gb_ref, slice(8, 24))
     h = jnp.concatenate([both_ref[TR:], h3_ref[...]], axis=1)
     tall = jnp.concatenate([h, below, above], axis=0)
     m_ref[...] = tall * tall * tall
@@ -455,8 +479,7 @@
         table_ref, out_ref, table_out, b_ref, a_ref = refs
         table = merged(table_ref[...], ga_ref[24:, :128], gb_ref[24:, :128])
         table_out[...] = table
-        wide = jnp.concatenate([table, jnp.zeros((table.shape[0], FC - 128), jnp.float32)], axis=1)
-        strips = [jnp.concatenate([x, wide], axis=0) for x in strips]
+        strips = [fold(x, table) for x in strips]
     else:
         out_ref, b_ref, a_ref = refs
     out_ref[...] = y
@@ -502,9 +525,9 @@
     i, j = place()
     y = y_ref[...]
     mask = edge_mask(counts)
-    s = edges(y, *sides(i, counts[0], ga_ref[:24], gb_ref[:24]))
+    s = edges(y, *row_sides(i, counts[0], ga_ref, gb_ref, slice(0, 24)))
     s = jnp.where(mask, s, 0.0)
-    table = merged(table_ref[...], ga_ref[24:, :128], gb_ref[24:, :128])
+    table = merged(table_ref[...], unfold(ga_ref), unfold(gb_ref))
     picked = jnp.sum(near_ref[...] * as_row(table, width), axis=1, keepdims=True)
     bands = as_bands([picked[k : k + 1] for k in range(12)])
     coarse = edge_bands(bands)
@@ -754,7 +777,7 @@
     ga, gb = swap(a, b, "col")
     r3, h3, b, a, table = call(
         functools.partial(widen_kernel, counts),
-        [(128, 128)] * 2 + [(24 + depth, FC)] * 2 + [(depth, 128)],
+        [(128, 128)] * 2 + [(24, FC)] * 2 + [(depth, 128)],
         both,
         table,
         gb,
@@ -763,7 +786,7 @@
     ga, gb = swap(a, b, "row")
     weight, table = call(weights_kernel, [(EXT, 2 * SPEC), (depth, 128)], both, table, basis)
     far = small_swap(table, 4, 0)
-    t = call(forward_kernel, [(EXT, 2 * SPEC)], both, r3, basis)[0]
+    t = call(forward_kernel, [(EXT, 2 * SPEC)], both, r3, basis, flops=5 * 10**8)[0]
     t, table, b, a = call(
         functools.partial(first_kernel, counts),
         [(EXT, 2 * SPEC), (depth, 128)] + [(24, EXT)] * 2,
@@ -789,7 +812,7 @@
     ga, gb = swap(*(jnp.concatenate([x, wide], axis=0) for x in (a, b)), "col", 1)
     y, table, b, a = call(
         functools.partial(columns_kernel, counts),
-        [(EXT, FC), (depth, 128)] + [(24 + depth, FC)] * 2,
+        [(EXT, FC), (depth, 128)] + [(24, FC)] * 2,
         y,
         ga,
         gb,

time: 47.7 us -> 47.5 us (level)
  no operation moved by 1% of the time
where the time goes in v18:
time: 47.5 us; the launch traced here: 47.3 us
  starting transfers between devices  17.3 us (36%)
  waiting for transfers between devices  11 us (23%)
  blocking collectives  9.26 us (19%)
  Pallas kernels  7.93 us (17%)
  other arithmetic  1 us (2%)
  between operations  0.75 us (2%)
    all_to_all x1, blocking collectives, body(): stats = lax.all_to_all(stats, both_axes, 0, 0, tiled=True)  9.26 us
    ppermute x6, starting transfers between devices, swap(): lax.ppermute(b, both_axes, odd_pairs(counts, both_axes.index(axis), bit))  8.83 us
    pallas_call x14, Pallas kernels, call(): pl.pallas_call(kernel, out_shape=shapes, compiler_params=pltpu.CompilerPa...  7.93 us
    ppermute x6, waiting for transfers between devices, swap(): lax.ppermute(b, both_axes, odd_pairs(counts, both_axes.index(axis), bit))  6.11 us
    ppermute x6, starting transfers between devices, swap(): return (lax.ppermute(a, axis, pairs_from(lax.axis_size(axis), 0)), gb)  6.09 us
    ppermute x6, waiting for transfers between devices, swap(): return (lax.ppermute(a, axis, pairs_from(lax.axis_size(axis), 0)), gb)  4.58 us
    ppermute x1, starting transfers between devices, small_swap(): return lax.ppermute(x, both_axes, xor_pairs(counts, rows, cols))  2.43 us
    add x1, other arithmetic, body(): jnp.pad(noise, ((0, TR), (0, 0))) + jnp.pad(height, ((TR, 0), (0, 0)))  0.99 us
  transfers between devices with their start and end apart: 13, of which 8 were waited for; matrix products, arithmetic and copies ran while one was open for 0% of the time, Pallas kernels for 9%

profile of v18, /device:TPU:0, one launch (start us, length us, event | category | flops | bytes accessed | tf_op | source)
XLA Modules:
  0.0 47.3 jit_solution(8782357206959569511)
XLA Ops:
  0.6 1.0 %pad_add_fusion.both_ref = f32[256,256]{1,0:T(8,128)S(1)} fusion(f32[128,256]{1,0:T(8,128)} %param.3, f32[128,256]{1,0:T(8,128)} %param.4), kind=kLoop, calls=%fused_computation | loop fusion | flops 65536 | bytes 524288 | tf_op jit(solution)/shard_map/add | solution.py:767
  1.6 0.2 shard_map.50
  1.8 0.0 copy-start
  1.8 4.0 %collective-permute-start = (f32[40,128]{1,0:T(8,128)S(1)}, f32[40,128]{1,0:T(8,128)S(1)}, u32[]{:S(2)}, u32[]{:S(2)}) collective-permute-start(f32[40,128]{1,0:T(8,128)S(1)} %get-tuple-element.43), channel_id=1, source_target_pairs={{0,3},{1,2},{2,1},{3,0},{4,7},{5,6},{6,5},{7,4},{8,11},{9,10},{10,... | collective-permute-start | bytes 61448 | tf_op jit(solution)/shard_map/ppermute | solution.py:761
  5.8 0.5 %collective-permute-start.1 = (f32[40,128]{1,0:T(8,128)S(1)}, f32[40,128]{1,0:T(8,128)S(1)}, u32[]{:S(2)}, u32[]{:S(2)}) collective-permute-start(f32[40,128]{1,0:T(8,128)S(1)} %get-tuple-element.44), channel_id=1, source_target_pairs={{0,1},{1,0},{2,3},{3,2},{4,5},{5,4},{6,7},{7,6},{8,9},{9,8},{10,11... | collective-permute-start | bytes 61448 | tf_op jit(solution)/shard_map/ppermute | solution.py:762
  6.3 1.2 %collective-permute-done.gb_ref = f32[40,128]{1,0:T(8,128)S(1)} collective-permute-done((f32[40,128]{1,0:T(8,128)S(1)}, f32[40,128]{1,0:T(8,128)S(1)}, u32[]{:S(2)}, u32[]{:S(2)}) %collective-permute-start) | collective-permute-done | bytes 20512 | tf_op jit(solution)/shard_map/ppermute | solution.py:761
  7.5 2.0 %collective-permute-done.1.ga_ref = f32[40,128]{1,0:T(8,128)S(1)} collective-permute-done((f32[40,128]{1,0:T(8,128)S(1)}, f32[40,128]{1,0:T(8,128)S(1)}, u32[]{:S(2)}, u32[]{:S(2)}) %collective-permute-start.1) | collective-permute-done | bytes 20512 | tf_op jit(solution)/shard_map/ppermute | solution.py:762
  9.5 0.2 shard_map.51
  9.7 2.0 %collective-permute-start.2 = (f32[24,384]{1,0:T(8,128)S(1)}, f32[24,384]{1,0:T(8,128)S(1)}, u32[]{:S(2)}, u32[]{:S(2)}) collective-permute-start(f32[24,384]{1,0:T(8,128)S(1)} %get-tuple-element.45), channel_id=1, source_target_pairs={{0,28},{1,29},{2,30},{3,31},{4,8},{5,9},{6,10},{7,11},{8,4},{9,5},... | collective-permute-start | bytes 110600 | tf_op jit(solution)/shard_map/ppermute | solution.py:761
  11.7 0.0 collective-permute-start.3
  11.7 0.0 copy-done
  11.7 0.1 shard_map.53
  11.9 2.4 %collective-permute-start.4 = (f32[8,128]{1,0:T(8,128)S(1)}, f32[8,128]{1,0:T(8,128)S(1)}, u32[]{:S(2)}, u32[]{:S(2)}) collective-permute-start(f32[8,128]{1,0:T(8,128)S(1)} %get-tuple-element.50.table_ref), channel_id=1, source_target_pairs={{0,16},{1,17},{2,18},{3,19},{4,20},{5,21},{6,22},{7,23},{8,24},{9,... | collective-permute-start | bytes 12296 | tf_op jit(solution)/shard_map/ppermute | solution.py:765
  14.3 0.6 %shard_map.52.tile_ref = f32[144,512]{1,0:T(8,128)S(1)} custom-call(f32[256,256]{1,0:T(8,128)S(1)} %pad_add_fusion.both_ref, f32[128,128]{1,0:T(8,128)S(1)} %get-tuple-element.47.r3_ref, f32[1104,512]{1,0:T(8,128)S(1)} %copy-done), custom_call_target="tpu_custom_call" | custom-call | flops 500000000 | bytes 1000000 | tf_op jit(solution)/shard_map/pallas_call | solution.py:706
  14.9 0.2 collective-permute-done.2.gb_ref
  15.1 0.0 collective-permute-done.3.ga_ref
  15.1 1.0 %shard_map.54 = (f32[144,512]{1,0:T(8,128)S(1)}, f32[8,128]{1,0:T(8,128)S(1)}, f32[24,144]{1,0:T(8,128)S(1)}, f32[24,144]{1,0:T(8,128)S(1)}) custom-call(f32[24,384]{1,0:T(8,128)S(1)} %collective-permute-done.2.gb_ref, f32[24,384]{1,0:T(8,128)S(1)} %collective-permute-done.3.ga_ref, f32[144,512]{1,0:T(8,128)S(1)} %shard_map.52.tile_ref, ...), custom_call_target="tpu_custom_call" | custom-call | flops 1000000000 | bytes 1000000 | tf_op jit(solution)/shard_map/pallas_call | solution.py:706
  16.1 0.3 collective-permute-done.4
  16.5 0.1 collective-permute-start.6
  16.5 1.8 %collective-permute-start.5 = (f32[32,144]{1,0:T(8,128)S(1)}, f32[32,144]{1,0:T(8,128)S(1)}, u32[]{:S(2)}, u32[]{:S(2)}) collective-permute-start(f32[32,144]{1,0:T(8,128)S(1)} %get-tuple-element.83), channel_id=1, source_target_pairs={{0,1},{1,0},{2,3},{3,2},{4,5},{5,4},{6,7},{7,6},{8,9},{9,8},{10,11... | collective-permute-start | bytes 55304 | tf_op jit(solution)/shard_map/ppermute | solution.py:762
  18.4 0.8 %shard_map.55 = (f32[144,384]{1,0:T(8,128)S(1)}, f32[160,384]{1,0:T(8,128)S(1)}) custom-call(f32[144,512]{1,0:T(8,128)S(1)} %get-tuple-element.51.t_ref, f32[1104,512]{1,0:T(8,128)S(1)} %copy-done, f32[256,256]{1,0:T(8,128)S(1)} %pad_add_fusion.both_ref, f32[128,128]{1,0:T(8,128)S(1)} %get-tuple-element.52.h3_ref, ...), custom_call_target="tpu_custom_call" | custom-call | flops 1000000000 | bytes 1000000 | tf_op jit(solution)/shard_map/pallas_call | solution.py:706
  19.2 0.0 collective-permute-done.6.refs_1_
  19.2 1.5 %collective-permute-done.5.refs_0_ = f32[32,144]{1,0:T(8,128)S(1)} collective-permute-done((f32[32,144]{1,0:T(8,128)S(1)}, f32[32,144]{1,0:T(8,128)S(1)}, u32[]{:S(2)}, u32[]{:S(2)}) %collective-permute-start.5) | collective-permute-done | bytes 18464 | tf_op jit(solution)/shard_map/ppermute | solution.py:762
  20.7 0.2 shard_map.56
  20.9 0.8 %collective-permute-start.7 = (f32[24,384]{1,0:T(8,128)S(1)}, f32[24,384]{1,0:T(8,128)S(1)}, u32[]{:S(2)}, u32[]{:S(2)}) collective-permute-start(f32[24,384]{1,0:T(8,128)S(1)} %get-tuple-element.59), channel_id=1, source_target_pairs={{0,28},{1,29},{2,30},{3,31},{4,8},{5,9},{6,10},{7,11},{8,4},{9,5},... | collective-permute-start | bytes 110600 | tf_op jit(solution)/shard_map/ppermute | solution.py:761
  21.7 0.8 %collective-permute-start.8 = (f32[24,384]{1,0:T(8,128)S(1)}, f32[24,384]{1,0:T(8,128)S(1)}, u32[]{:S(2)}, u32[]{:S(2)}) collective-permute-start(f32[24,384]{1,0:T(8,128)S(1)} %get-tuple-element.60), channel_id=1, source_target_pairs={{0,4},{4,0},{8,12},{12,8},{16,20},{20,16},{24,28},{28,24},{1,5},{5... | collective-permute-start | bytes 110600 | tf_op jit(solution)/shard_map/ppermute | solution.py:762
  22.5 0.7 %shard_map.57 = (f32[96,256]{1,0:T(8,128)S(1)}, f32[96,256]{1,0:T(8,128)S(1)}, f32[144,384]{1,0:T(8,128)S(1)}, f32[144,384]{1,0:T(8,128)S(1)}, f32[16,128]{1,0:T(8,128)S(1)}) custom-call(f32[144,384]{1,0:T(8,128)S(1)} %get-tuple-element.57.y_ref, f32[160,384]{1,0:T(8,128)S(1)} %get-tuple-element.58.m_ref, f32[1104,512]{1,0:T(8,128)S(1)} %copy-done), custom_call_target="tpu_custom_call" | custom-call | flops 1000000000 | bytes 1000000 | tf_op jit(solution)/shard_map/pallas_call | solution.py:706
  23.1 3.0 %collective-permute-done.7.gb_ref = f32[24,384]{1,0:T(8,128)S(1)} collective-permute-done((f32[24,384]{1,0:T(8,128)S(1)}, f32[24,384]{1,0:T(8,128)S(1)}, u32[]{:S(2)}, u32[]{:S(2)}) %collective-permute-start.7) | collective-permute-done | bytes 36896 | tf_op jit(solution)/shard_map/ppermute | solution.py:761
  26.1 0.0 collective-permute-done.8.ga_ref
  26.1 1.3 %shard_map.58 = (f32[128,256]{1,0:T(8,128)S(1)}, f32[128,256]{1,0:T(8,128)S(1)}, f32[144,512]{1,0:T(8,128)S(1)}, f32[16,144]{1,0:T(8,128)S(1)}, f32[16,144]{1,0:T(8,128)S(1)}) custom-call(f32[144,384]{1,0:T(8,128)S(1)} %get-tuple-element.57.y_ref, f32[160,384]{1,0:T(8,128)S(1)} %get-tuple-element.58.m_ref, f32[24,384]{1,0:T(8,128)S(1)} %collective-permute-done.7.gb_ref, ...), custom_call_target="tpu_custom_call" | custom-call | flops 1000000000 | bytes 1000000 | tf_op jit(solution)/shard_map/pallas_call | solution.py:706
  27.5 0.1 collective-permute-start.9
  27.6 3.0 %collective-permute-start.10 = (f32[16,144]{1,0:T(8,128)S(1)}, f32[16,144]{1,0:T(8,128)S(1)}, u32[]{:S(2)}, u32[]{:S(2)}) collective-permute-start(f32[16,144]{1,0:T(8,128)S(1)} %get-tuple-element.72), channel_id=1, source_target_pairs={{0,1},{1,0},{2,3},{3,2},{4,5},{5,4},{6,7},{7,6},{8,9},{9,8},{10,11... | collective-permute-start | bytes 27656 | tf_op jit(solution)/shard_map/ppermute | solution.py:762
  30.5 0.8 %shard_map.59 = (f32[144,384]{1,0:T(8,128)S(1)}, f32[1,128]{1,0:T(1,128)S(1)}) custom-call(f32[144,512]{1,0:T(8,128)S(1)} %get-tuple-element.67.t_ref, f32[1104,512]{1,0:T(8,128)S(1)} %copy-done, f32[256,256]{1,0:T(8,128)S(1)} %pad_add_fusion.both_ref, f32[160,384]{1,0:T(8,128)S(1)} %get-tuple-element.58.m_ref, f32[128,256]{1,0:T(8,128)S(1)} %get-tuple-element.68.z_ref, ...), custom_call_target="tpu_custom_call" | custom-call | flops 1000000000 | bytes 1000000 | tf_op jit(solution)/shard_map/pallas_call | solution.py:706
  31.4 0.0 collective-permute-done.9.refs_0_
  31.4 1.0 %collective-permute-done.10.refs_1_ = f32[16,144]{1,0:T(8,128)S(1)} collective-permute-done((f32[16,144]{1,0:T(8,128)S(1)}, f32[16,144]{1,0:T(8,128)S(1)}, u32[]{:S(2)}, u32[]{:S(2)}) %collective-permute-start.10) | collective-permute-done | bytes 9248 | tf_op jit(solution)/shard_map/ppermute | solution.py:762
  32.4 0.2 shard_map.60
  32.6 1.9 %collective-permute-start.11 = (f32[16,384]{1,0:T(8,128)S(1)}, f32[16,384]{1,0:T(8,128)S(1)}, u32[]{:S(2)}, u32[]{:S(2)}) collective-permute-start(f32[16,384]{1,0:T(8,128)S(1)} %get-tuple-element.74), channel_id=1, source_target_pairs={{0,1},{1,0},{2,3},{3,2},{4,8},{5,9},{6,10},{7,11},{8,4},{9,5},{10,... | collective-permute-start | bytes 73736 | tf_op jit(solution)/shard_map/ppermute | solution.py:761
  34.5 0.0 collective-permute-start.12
  34.5 0.4 shard_map.61
  34.9 1.6 %collective-permute-done.11.gb_ref = f32[16,384]{1,0:T(8,128)S(1)} collective-permute-done((f32[16,384]{1,0:T(8,128)S(1)}, f32[16,384]{1,0:T(8,128)S(1)}, u32[]{:S(2)}, u32[]{:S(2)}) %collective-permute-start.11) | collective-permute-done | bytes 24608 | tf_op jit(solution)/shard_map/ppermute | solution.py:761
  36.5 0.0 collective-permute-done.12.ga_ref
  36.5 0.3 shard_map.62
  36.8 9.3 %all_to_all.11 = f32[32,1,128]{2,1,0:T(1,128)S(1)} all-to-all(f32[32,1,128]{2,1,0:T(1,128)S(1)} %bitcast.5), channel_id=1, replica_groups=mesh['row'=8,'col'=4] {'row','col'}, dimensions={0} | all-to-all | bytes 32768 | tf_op jit(solution)/shard_map/all_to_all | solution.py:872
  46.0 1.3 %shard_map.63 = (f32[128,256]{1,0:T(8,128)}, f32[128,256]{1,0:T(8,128)}) custom-call(f32[32,128]{1,0:T(8,128)S(1)} %bitcast.4, f32[1104,512]{1,0:T(8,128)S(1)} %copy-done, f32[160,384]{1,0:T(8,128)S(1)} %get-tuple-element.58.m_ref, f32[96,256]{1,0:T(8,128)S(1)} %get-tuple-element.63.f_ref, f32[256,256]{1,0:T(8,128)S(1)} %pad_add_fusion.both_ref, ...), custom_call_target="tpu_custom_call" | custom-call | flops 1000000000 | bytes 1000000 | tf_op jit(solution)/shard_map/pallas_call | solution.py:706
  (2 shorter events, 0.0 us)
Async XLA Ops:
  1.8 9.9 %copy-start = (f32[1104,512]{1,0:T(8,128)S(1)}, f32[1104,512]{1,0:T(8,128)}, u32[]{:S(2)}) copy-start(f32[1104,512]{1,0:T(8,128)} %constant.6.clone.basis_ref) | copy-start | bytes 6782980
  1.8 5.7 %collective-permute-start = (f32[40,128]{1,0:T(8,128)S(1)}, f32[40,128]{1,0:T(8,128)S(1)}, u32[]{:S(2)}, u32[]{:S(2)}) collective-permute-start(f32[40,128]{1,0:T(8,128)S(1)} %get-tuple-element.43), channel_id=1, source_target_pairs={{0,3},{1,2},{2,1},{3,0},{4,7},{5,6},{6,5},{7,4},{8,11},{9,10},{10,... | collective-permute-start | bytes 61448 | tf_op jit(solution)/shard_map/ppermute | solution.py:761
  5.8 3.8 %collective-permute-start.1 = (f32[40,128]{1,0:T(8,128)S(1)}, f32[40,128]{1,0:T(8,128)S(1)}, u32[]{:S(2)}, u32[]{:S(2)}) collective-permute-start(f32[40,128]{1,0:T(8,128)S(1)} %get-tuple-element.44), channel_id=1, source_target_pairs={{0,1},{1,0},{2,3},{3,2},{4,5},{5,4},{6,7},{7,6},{8,9},{9,8},{10,11... | collective-permute-start | bytes 61448 | tf_op jit(solution)/shard_map/ppermute | solution.py:762
  9.7 5.4 %collective-permute-start.2 = (f32[24,384]{1,0:T(8,128)S(1)}, f32[24,384]{1,0:T(8,128)S(1)}, u32[]{:S(2)}, u32[]{:S(2)}) collective-permute-start(f32[24,384]{1,0:T(8,128)S(1)} %get-tuple-element.45), channel_id=1, source_target_pairs={{0,28},{1,29},{2,30},{3,31},{4,8},{5,9},{6,10},{7,11},{8,4},{9,5},... | collective-permute-start | bytes 110600 | tf_op jit(solution)/shard_map/ppermute | solution.py:761
  11.7 3.4 %collective-permute-start.3 = (f32[24,384]{1,0:T(8,128)S(1)}, f32[24,384]{1,0:T(8,128)S(1)}, u32[]{:S(2)}, u32[]{:S(2)}) collective-permute-start(f32[24,384]{1,0:T(8,128)S(1)} %get-tuple-element.46), channel_id=1, source_target_pairs={{0,4},{4,0},{8,12},{12,8},{16,20},{20,16},{24,28},{28,24},{1,5},{5... | collective-permute-start | bytes 110600 | tf_op jit(solution)/shard_map/ppermute | solution.py:762
  11.9 4.6 %collective-permute-start.4 = (f32[8,128]{1,0:T(8,128)S(1)}, f32[8,128]{1,0:T(8,128)S(1)}, u32[]{:S(2)}, u32[]{:S(2)}) collective-permute-start(f32[8,128]{1,0:T(8,128)S(1)} %get-tuple-element.50.table_ref), channel_id=1, source_target_pairs={{0,16},{1,17},{2,18},{3,19},{4,20},{5,21},{6,22},{7,23},{8,24},{9,... | collective-permute-start | bytes 12296 | tf_op jit(solution)/shard_map/ppermute | solution.py:765
  16.5 2.7 %collective-permute-start.6 = (f32[32,144]{1,0:T(8,128)S(1)}, f32[32,144]{1,0:T(8,128)S(1)}, u32[]{:S(2)}, u32[]{:S(2)}) collective-permute-start(f32[32,144]{1,0:T(8,128)S(1)} %get-tuple-element.82), channel_id=1, source_target_pairs={{0,4},{1,2},{2,1},{3,7},{4,0},{5,6},{6,5},{7,3},{8,12},{9,10},{10,... | collective-permute-start | bytes 55304 | tf_op jit(solution)/shard_map/ppermute | solution.py:761
  16.5 4.2 %collective-permute-start.5 = (f32[32,144]{1,0:T(8,128)S(1)}, f32[32,144]{1,0:T(8,128)S(1)}, u32[]{:S(2)}, u32[]{:S(2)}) collective-permute-start(f32[32,144]{1,0:T(8,128)S(1)} %get-tuple-element.83), channel_id=1, source_target_pairs={{0,1},{1,0},{2,3},{3,2},{4,5},{5,4},{6,7},{7,6},{8,9},{9,8},{10,11... | collective-permute-start | bytes 55304 | tf_op jit(solution)/shard_map/ppermute | solution.py:762
  20.9 5.2 %collective-permute-start.7 = (f32[24,384]{1,0:T(8,128)S(1)}, f32[24,384]{1,0:T(8,128)S(1)}, u32[]{:S(2)}, u32[]{:S(2)}) collective-permute-start(f32[24,384]{1,0:T(8,128)S(1)} %get-tuple-element.59), channel_id=1, source_target_pairs={{0,28},{1,29},{2,30},{3,31},{4,8},{5,9},{6,10},{7,11},{8,4},{9,5},... | collective-permute-start | bytes 110600 | tf_op jit(solution)/shard_map/ppermute | solution.py:761
  21.7 4.4 %collective-permute-start.8 = (f32[24,384]{1,0:T(8,128)S(1)}, f32[24,384]{1,0:T(8,128)S(1)}, u32[]{:S(2)}, u32[]{:S(2)}) collective-permute-start(f32[24,384]{1,0:T(8,128)S(1)} %get-tuple-element.60), channel_id=1, source_target_pairs={{0,4},{4,0},{8,12},{12,8},{16,20},{20,16},{24,28},{28,24},{1,5},{5... | collective-permute-start | bytes 110600 | tf_op jit(solution)/shard_map/ppermute | solution.py:762
  27.5 3.9 %collective-permute-start.9 = (f32[16,144]{1,0:T(8,128)S(1)}, f32[16,144]{1,0:T(8,128)S(1)}, u32[]{:S(2)}, u32[]{:S(2)}) collective-permute-start(f32[16,144]{1,0:T(8,128)S(1)} %get-tuple-element.71), channel_id=1, source_target_pairs={{0,4},{1,2},{2,1},{3,7},{4,0},{5,6},{6,5},{7,3},{8,12},{9,10},{10,... | collective-permute-start | bytes 27656 | tf_op jit(solution)/shard_map/ppermute | solution.py:761
  27.6 4.9 %collective-permute-start.10 = (f32[16,144]{1,0:T(8,128)S(1)}, f32[16,144]{1,0:T(8,128)S(1)}, u32[]{:S(2)}, u32[]{:S(2)}) collective-permute-start(f32[16,144]{1,0:T(8,128)S(1)} %get-tuple-element.72), channel_id=1, source_target_pairs={{0,1},{1,0},{2,3},{3,2},{4,5},{5,4},{6,7},{7,6},{8,9},{9,8},{10,11... | collective-permute-start | bytes 27656 | tf_op jit(solution)/shard_map/ppermute | solution.py:762
  32.6 3.9 %collective-permute-start.11 = (f32[16,384]{1,0:T(8,128)S(1)}, f32[16,384]{1,0:T(8,128)S(1)}, u32[]{:S(2)}, u32[]{:S(2)}) collective-permute-start(f32[16,384]{1,0:T(8,128)S(1)} %get-tuple-element.74), channel_id=1, source_target_pairs={{0,1},{1,0},{2,3},{3,2},{4,8},{5,9},{6,10},{7,11},{8,4},{9,5},{10,... | collective-permute-start | bytes 73736 | tf_op jit(solution)/shard_map/ppermute | solution.py:761
  34.5 2.0 %collective-permute-start.12 = (f32[16,384]{1,0:T(8,128)S(1)}, f32[16,384]{1,0:T(8,128)S(1)}, u32[]{:S(2)}, u32[]{:S(2)}) collective-permute-start(f32[16,384]{1,0:T(8,128)S(1)} %get-tuple-element.75), channel_id=1, source_target_pairs={{0,4},{4,0},{8,12},{12,8},{16,20},{20,16},{24,28},{28,24},{1,5},{5... | collective-permute-start | bytes 73736 | tf_op jit(solution)/shard_map/ppermute | solution.py:762

commit v19 on v14

--- a/solution.py
+++ b/solution.py
@@ -433,11 +433,17 @@
     u = column_transform(jnp.concatenate([below, above], axis=0), basis_ref)
     t = (tile_ref[...] + row_transform(u, basis_ref, halo_rows)) * weights_ref[...]
     t_ref[...] = t
-    send(j, a_ref, b_ref, *strips_of(t, basis_ref, 24))
-    table_out[...] = merged(table_ref[...], ga_ref[24:, :128], gb_ref[24:, :128])
-
-
-def inverse_kernel(counts, t_ref, basis_ref, both_ref, h3_ref, gb_ref, ga_ref, y_ref, m_ref):
+    table = merged(table_ref[...], ga_ref[24:, :128], gb_ref[24:, :128])
+    table_out[...] = table
+    wide = jnp.concatenate([table, jnp.zeros((table.shape[0], EXT - 128), jnp.float32)], axis=1)
+    strips = (jnp.concatenate([x, wide], axis=0) for x in strips_of(t, basis_ref, 24))
+    send(j, a_ref, b_ref, *strips)
+
+
+def inverse_kernel(
+    counts, t_ref, basis_ref, both_ref, h3_ref, gb_ref, ga_ref, table_ref, y_ref, m_ref, table_out
+):
+    table_out[...] = table_ref[...]
     y_ref[...] = solution_of(t_ref[...], basis_ref)
     above, below = sides(lax.axis_index("row"), counts[0], ga_ref[8:24], gb_ref[8:24])
     h = jnp.concatenate([both_ref[TR:], h3_ref[...]], axis=1)
@@ -445,15 +451,14 @@
     m_ref[...] = tall * tall * tall
 
 
-def columns_kernel(counts, y_ref, *refs):
+def columns_kernel(counts, y_ref, gb_ref, ga_ref, *refs):
     i, j = place()
-    (ga_ref, gb_ref), refs = (refs[:2] if len(refs) == 7 else refs[1::-1]), refs[2:]
-    deep = 24 if len(refs) == 5 else 16
+    deep = 24 if len(refs) == 6 else 16
     y = add_columns(y_ref[...], *sides(j, counts[1], ga_ref[:deep], gb_ref[:deep]))
     strips = pack_rows(y, deep)
-    if len(refs) == 5:
-        table_ref, out_ref, table_out, b_ref, a_ref = refs
-        table = merged(table_ref[...], ga_ref[24:, :128], gb_ref[24:, :128])
+    if len(refs) == 6:
+        table_ref, far_ref, out_ref, table_out, b_ref, a_ref = refs
+        table = merged(table_ref[...], far_ref[...], ga_ref[24:, :128], gb_ref[24:, :128])
         table_out[...] = table
         wide = jnp.concatenate([table, jnp.zeros((table.shape[0], FC - 128), jnp.float32)], axis=1)
         strips = [jnp.concatenate([x, wide], axis=0) for x in strips]
@@ -486,6 +491,7 @@
     gb_ref,
     ga_ref,
     table_ref,
+    farther_ref,
     inner_w_ref,
     f_ref,
     gw_ref,
@@ -504,7 +510,7 @@
     mask = edge_mask(counts)
     s = edges(y, *sides(i, counts[0], ga_ref[:24], gb_ref[:24]))
     s = jnp.where(mask, s, 0.0)
-    table = merged(table_ref[...], ga_ref[24:, :128], gb_ref[24:, :128])
+    table = merged(table_ref[...], farther_ref[...], ga_ref[24:, :128], gb_ref[24:, :128])
     picked = jnp.sum(near_ref[...] * as_row(table, width), axis=1, keepdims=True)
     bands = as_bands([picked[k : k + 1] for k in range(12)])
     coarse = edge_bands(bands)
@@ -721,9 +727,11 @@
 
     even = [xor_pairs(counts, 0, 1), xor_pairs(counts, 1, 0)]
     known = meet(even[0], odd_pairs(counts, 1, 0))
-    known = meet(even[1], odd_pairs(counts, 0, 0), xor_pairs(counts, 4, 0))
-    known = meet(even[0], odd_pairs(counts, 1, 1))
-    return meet(even[1], odd_pairs(counts, 0, 0)).all()
+    first = meet(xor_pairs(counts, 4, 0))
+    known = meet(even[1], odd_pairs(counts, 0, 0))
+    second = meet(xor_pairs(counts, 4, 2))
+    known = meet(even[0], odd_pairs(counts, 1, 1)) | first
+    return (meet(even[1], odd_pairs(counts, 0, 0)) | second).all()
 
 
 def body(counts, height, noise):
@@ -766,7 +774,7 @@
     t = call(forward_kernel, [(EXT, 2 * SPEC)], both, r3, basis)[0]
     t, table, b, a = call(
         functools.partial(first_kernel, counts),
-        [(EXT, 2 * SPEC), (depth, 128)] + [(24, EXT)] * 2,
+        [(EXT, 2 * SPEC), (depth, 128)] + [(24 + depth, EXT)] * 2,
         gb,
         ga,
         t,
@@ -774,26 +782,27 @@
         basis,
         table,
     )
-    table = merged(table, far)
-    wide = jnp.pad(table, ((0, 0), (0, EXT - 128)))
-    y, m = call(
+    y, m, table_too = call(
         functools.partial(inverse_kernel, counts),
-        [(EXT, FC), (FR, FC)],
+        [(EXT, FC), (FR, FC), (depth, 128)],
         t,
         basis,
         both,
         h3,
         gb,
         ga,
-    )
-    ga, gb = swap(*(jnp.concatenate([x, wide], axis=0) for x in (a, b)), "col", 1)
+        table,
+    )
+    ga, gb = swap(a, b, "col", 1)
+    farther = small_swap(table_too, 4, 2)
     y, table, b, a = call(
         functools.partial(columns_kernel, counts),
         [(EXT, FC), (depth, 128)] + [(24 + depth, FC)] * 2,
         y,
+        gb,
         ga,
-        gb,
         table,
+        far,
     )
     ga, gb = swap(a, b, "row")
     inner_w, f, gw, gf, near = call(
@@ -811,6 +820,7 @@
         gb,
         ga,
         table,
+        farther,
         inner_w,
         f,
         gw,

time: 47.7 us -> 47.6 us (level)
  starting transfers between devices: 17.6 us -> 17.1 us
    ppermute x1 -> x2, waiting for transfers between devices: 0.07 us -> 2.27 us  [small_swap(): return lax.ppermute(x, both_axes, xor_pairs(counts, rows, cols))]
    ppermute x6, waiting for transfers between devices: 6.5 us -> 4.85 us  [swap(): lax.ppermute(b, both_axes, odd_pairs(counts, both_axes.index(axis), bit))]
    ppermute x1 -> x2, starting transfers between devices: 2.43 us -> 2.5 us  [small_swap(): return lax.ppermute(x, both_axes, xor_pairs(counts, rows, cols))]
  transfers between devices with their start and end apart: 13 -> 14, of which waited for: 8 -> 8; matrix products, arithmetic and copies ran while one was open for 0% -> 0% of each run, Pallas kernels for 9% -> 10%
where the time goes in v19:
time: 47.6 us; the launch traced here: 47.5 us
  starting transfers between devices  17.1 us (36%)
  waiting for transfers between devices  11.5 us (24%)
  blocking collectives  9.2 us (19%)
  Pallas kernels  7.87 us (17%)
  other arithmetic  0.99 us (2%)
  between operations  0.76 us (2%)
    all_to_all x1, blocking collectives, body(): stats = lax.all_to_all(stats, both_axes, 0, 0, tiled=True)  9.2 us
    ppermute x6, starting transfers between devices, swap(): lax.ppermute(b, both_axes, odd_pairs(counts, both_axes.index(axis), bit))  8.59 us
    pallas_call x14, Pallas kernels, call(): pl.pallas_call(kernel, out_shape=shapes, compiler_params=pltpu.CompilerPa...  7.87 us
    ppermute x6, starting transfers between devices, swap(): return (lax.ppermute(a, axis, pairs_from(lax.axis_size(axis), 0)), gb)  6.05 us
    ppermute x6, waiting for transfers between devices, swap(): lax.ppermute(b, both_axes, odd_pairs(counts, both_axes.index(axis), bit))  4.85 us
    ppermute x6, waiting for transfers between devices, swap(): return (lax.ppermute(a, axis, pairs_from(lax.axis_size(axis), 0)), gb)  4.39 us
    ppermute x2, starting transfers between devices, small_swap(): return lax.ppermute(x, both_axes, xor_pairs(counts, rows, cols))  2.5 us
    ppermute x2, waiting for transfers between devices, small_swap(): return lax.ppermute(x, both_axes, xor_pairs(counts, rows, cols))  2.27 us
  transfers between devices with their start and end apart: 14, of which 8 were waited for; matrix products, arithmetic and copies ran while one was open for 0% of the time, Pallas kernels for 10%

profile of v19, /device:TPU:0, one launch (start us, length us, event | category | flops | bytes accessed | tf_op | source)
XLA Modules:
  0.0 47.5 jit_solution(8914244307706609746)
XLA Ops:
  0.6 1.0 %pad_add_fusion.both_ref = f32[256,256]{1,0:T(8,128)S(1)} fusion(f32[128,256]{1,0:T(8,128)} %param.3, f32[128,256]{1,0:T(8,128)} %param.4), kind=kLoop, calls=%fused_computation | loop fusion | flops 65536 | bytes 524288 | tf_op jit(solution)/shard_map/add | solution.py:752
  1.6 0.2 shard_map.50
  1.8 0.0 copy-start
  1.8 4.0 %collective-permute-start = (f32[40,128]{1,0:T(8,128)S(1)}, f32[40,128]{1,0:T(8,128)S(1)}, u32[]{:S(2)}, u32[]{:S(2)}) collective-permute-start(f32[40,128]{1,0:T(8,128)S(1)} %get-tuple-element.44), channel_id=1, source_target_pairs={{0,3},{1,2},{2,1},{3,0},{4,7},{5,6},{6,5},{7,4},{8,11},{9,10},{10,... | collective-permute-start | bytes 61448 | tf_op jit(solution)/shard_map/ppermute | solution.py:746
  5.8 0.5 %collective-permute-start.1 = (f32[40,128]{1,0:T(8,128)S(1)}, f32[40,128]{1,0:T(8,128)S(1)}, u32[]{:S(2)}, u32[]{:S(2)}) collective-permute-start(f32[40,128]{1,0:T(8,128)S(1)} %get-tuple-element.45), channel_id=1, source_target_pairs={{0,1},{1,0},{2,3},{3,2},{4,5},{5,4},{6,7},{7,6},{8,9},{9,8},{10,11... | collective-permute-start | bytes 61448 | tf_op jit(solution)/shard_map/ppermute | solution.py:747
  6.3 1.2 %collective-permute-done.gb_ref = f32[40,128]{1,0:T(8,128)S(1)} collective-permute-done((f32[40,128]{1,0:T(8,128)S(1)}, f32[40,128]{1,0:T(8,128)S(1)}, u32[]{:S(2)}, u32[]{:S(2)}) %collective-permute-start) | collective-permute-done | bytes 20512 | tf_op jit(solution)/shard_map/ppermute | solution.py:746
  7.5 2.0 %collective-permute-done.1.ga_ref = f32[40,128]{1,0:T(8,128)S(1)} collective-permute-done((f32[40,128]{1,0:T(8,128)S(1)}, f32[40,128]{1,0:T(8,128)S(1)}, u32[]{:S(2)}, u32[]{:S(2)}) %collective-permute-start.1) | collective-permute-done | bytes 20512 | tf_op jit(solution)/shard_map/ppermute | solution.py:747
  9.5 0.2 shard_map.51
  9.7 2.0 %collective-permute-start.2 = (f32[32,384]{1,0:T(8,128)S(1)}, f32[32,384]{1,0:T(8,128)S(1)}, u32[]{:S(2)}, u32[]{:S(2)}) collective-permute-start(f32[32,384]{1,0:T(8,128)S(1)} %get-tuple-element.46), channel_id=1, source_target_pairs={{0,28},{1,29},{2,30},{3,31},{4,8},{5,9},{6,10},{7,11},{8,4},{9,5},... | collective-permute-start | bytes 147464 | tf_op jit(solution)/shard_map/ppermute | solution.py:746
  11.7 0.0 collective-permute-start.3
  11.7 0.0 copy-done
  11.7 0.1 shard_map.53
  11.9 2.4 %collective-permute-start.6 = (f32[8,128]{1,0:T(8,128)S(1)}, f32[8,128]{1,0:T(8,128)S(1)}, u32[]{:S(2)}, u32[]{:S(2)}) collective-permute-start(f32[8,128]{1,0:T(8,128)S(1)} %get-tuple-element.51.table_ref), channel_id=1, source_target_pairs={{0,16},{1,17},{2,18},{3,19},{4,20},{5,21},{6,22},{7,23},{8,24},{9,... | collective-permute-start | bytes 12296 | tf_op jit(solution)/shard_map/ppermute | solution.py:750
  14.3 0.6 %shard_map.52.tile_ref = f32[144,512]{1,0:T(8,128)S(1)} custom-call(f32[256,256]{1,0:T(8,128)S(1)} %pad_add_fusion.both_ref, f32[128,128]{1,0:T(8,128)S(1)} %get-tuple-element.48.r3_ref, f32[1104,512]{1,0:T(8,128)S(1)} %copy-done), custom_call_target="tpu_custom_call" | custom-call | flops 1000000000 | bytes 1000000 | tf_op jit(solution)/shard_map/pallas_call | solution.py:689
  14.9 0.5 %collective-permute-done.2.gb_ref = f32[32,384]{1,0:T(8,128)S(1)} collective-permute-done((f32[32,384]{1,0:T(8,128)S(1)}, f32[32,384]{1,0:T(8,128)S(1)}, u32[]{:S(2)}, u32[]{:S(2)}) %collective-permute-start.2) | collective-permute-done | bytes 49184 | tf_op jit(solution)/shard_map/ppermute | solution.py:746
  15.4 0.0 collective-permute-done.3.ga_ref
  15.4 1.0 %shard_map.54 = (f32[144,512]{1,0:T(8,128)S(1)}, f32[8,128]{1,0:T(8,128)S(1)}, f32[32,144]{1,0:T(8,128)S(1)}, f32[32,144]{1,0:T(8,128)S(1)}) custom-call(f32[32,384]{1,0:T(8,128)S(1)} %collective-permute-done.2.gb_ref, f32[32,384]{1,0:T(8,128)S(1)} %collective-permute-done.3.ga_ref, f32[144,512]{1,0:T(8,128)S(1)} %shard_map.52.tile_ref, ...), custom_call_target="tpu_custom_call" | custom-call | flops 1000000000 | bytes 1000000 | tf_op jit(solution)/shard_map/pallas_call | solution.py:689
  16.4 0.1 collective-permute-start.4
  16.5 1.9 %collective-permute-start.5 = (f32[32,144]{1,0:T(8,128)S(1)}, f32[32,144]{1,0:T(8,128)S(1)}, u32[]{:S(2)}, u32[]{:S(2)}) collective-permute-start(f32[32,144]{1,0:T(8,128)S(1)} %get-tuple-element.57), channel_id=1, source_target_pairs={{0,1},{1,0},{2,3},{3,2},{4,5},{5,4},{6,7},{7,6},{8,9},{9,8},{10,11... | collective-permute-start | bytes 55304 | tf_op jit(solution)/shard_map/ppermute | solution.py:747
  18.4 0.8 %shard_map.55 = (f32[144,384]{1,0:T(8,128)S(1)}, f32[160,384]{1,0:T(8,128)S(1)}, f32[8,128]{1,0:T(8,128)S(1)}) custom-call(f32[144,512]{1,0:T(8,128)S(1)} %get-tuple-element.52.t_ref, f32[1104,512]{1,0:T(8,128)S(1)} %copy-done, f32[256,256]{1,0:T(8,128)S(1)} %pad_add_fusion.both_ref, f32[128,128]{1,0:T(8,128)S(1)} %get-tuple-element.53.h3_ref, ...), custom_call_target="tpu_custom_call" | custom-call | flops 1000000000 | bytes 1000000 | tf_op jit(solution)/shard_map/pallas_call | solution.py:689
  19.3 0.1 collective-permute-start.9
  19.3 0.0 collective-permute-done.6.refs_1_
  19.3 0.0 collective-permute-done.4.gb_ref
  19.4 1.3 %collective-permute-done.5.ga_ref = f32[32,144]{1,0:T(8,128)S(1)} collective-permute-done((f32[32,144]{1,0:T(8,128)S(1)}, f32[32,144]{1,0:T(8,128)S(1)}, u32[]{:S(2)}, u32[]{:S(2)}) %collective-permute-start.5) | collective-permute-done | bytes 18464 | tf_op jit(solution)/shard_map/ppermute | solution.py:747
  20.7 0.2 shard_map.56
  20.8 0.6 %collective-permute-start.7 = (f32[32,384]{1,0:T(8,128)S(1)}, f32[32,384]{1,0:T(8,128)S(1)}, u32[]{:S(2)}, u32[]{:S(2)}) collective-permute-start(f32[32,384]{1,0:T(8,128)S(1)} %get-tuple-element.60), channel_id=1, source_target_pairs={{0,28},{1,29},{2,30},{3,31},{4,8},{5,9},{6,10},{7,11},{8,4},{9,5},... | collective-permute-start | bytes 147464 | tf_op jit(solution)/shard_map/ppermute | solution.py:746
  21.4 0.4 collective-permute-start.8
  21.8 0.7 %shard_map.57 = (f32[96,256]{1,0:T(8,128)S(1)}, f32[96,256]{1,0:T(8,128)S(1)}, f32[144,384]{1,0:T(8,128)S(1)}, f32[144,384]{1,0:T(8,128)S(1)}, f32[16,128]{1,0:T(8,128)S(1)}) custom-call(f32[144,384]{1,0:T(8,128)S(1)} %get-tuple-element.58.y_ref, f32[160,384]{1,0:T(8,128)S(1)} %get-tuple-element.59.m_ref, f32[1104,512]{1,0:T(8,128)S(1)} %copy-done), custom_call_target="tpu_custom_call" | custom-call | flops 1000000000 | bytes 1000000 | tf_op jit(solution)/shard_map/pallas_call | solution.py:689
  22.5 2.3 %collective-permute-done.9.farther_ref = f32[8,128]{1,0:T(8,128)S(1)} collective-permute-done((f32[8,128]{1,0:T(8,128)S(1)}, f32[8,128]{1,0:T(8,128)S(1)}, u32[]{:S(2)}, u32[]{:S(2)}) %collective-permute-start.9) | collective-permute-done | bytes 4128 | tf_op jit(solution)/shard_map/ppermute | solution.py:750
  24.7 1.5 %collective-permute-done.7.gb_ref = f32[32,384]{1,0:T(8,128)S(1)} collective-permute-done((f32[32,384]{1,0:T(8,128)S(1)}, f32[32,384]{1,0:T(8,128)S(1)}, u32[]{:S(2)}, u32[]{:S(2)}) %collective-permute-start.7) | collective-permute-done | bytes 49184 | tf_op jit(solution)/shard_map/ppermute | solution.py:746
  26.2 0.0 collective-permute-done.8.ga_ref
  26.2 1.3 %shard_map.58 = (f32[128,256]{1,0:T(8,128)S(1)}, f32[128,256]{1,0:T(8,128)S(1)}, f32[144,512]{1,0:T(8,128)S(1)}, f32[16,144]{1,0:T(8,128)S(1)}, f32[16,144]{1,0:T(8,128)S(1)}) custom-call(f32[144,384]{1,0:T(8,128)S(1)} %get-tuple-element.58.y_ref, f32[160,384]{1,0:T(8,128)S(1)} %get-tuple-element.59.m_ref, f32[32,384]{1,0:T(8,128)S(1)} %collective-permute-done.7.gb_ref, ...), custom_call_target="tpu_custom_call" | custom-call | flops 1000000000 | bytes 1000000 | tf_op jit(solution)/shard_map/pallas_call | solution.py:689
  27.5 0.1 collective-permute-start.10
  27.6 3.2 %collective-permute-start.11 = (f32[16,144]{1,0:T(8,128)S(1)}, f32[16,144]{1,0:T(8,128)S(1)}, u32[]{:S(2)}, u32[]{:S(2)}) collective-permute-start(f32[16,144]{1,0:T(8,128)S(1)} %get-tuple-element.74), channel_id=1, source_target_pairs={{0,1},{1,0},{2,3},{3,2},{4,5},{5,4},{6,7},{7,6},{8,9},{9,8},{10,11... | collective-permute-start | bytes 27656 | tf_op jit(solution)/shard_map/ppermute | solution.py:747
  30.8 0.8 %shard_map.59 = (f32[144,384]{1,0:T(8,128)S(1)}, f32[1,128]{1,0:T(1,128)S(1)}) custom-call(f32[144,512]{1,0:T(8,128)S(1)} %get-tuple-element.69.t_ref, f32[1104,512]{1,0:T(8,128)S(1)} %copy-done, f32[256,256]{1,0:T(8,128)S(1)} %pad_add_fusion.both_ref, f32[160,384]{1,0:T(8,128)S(1)} %get-tuple-element.59.m_ref, f32[128,256]{1,0:T(8,128)S(1)} %get-tuple-element.70.z_ref, ...), custom_call_target="tpu_custom_call" | custom-call | flops 1000000000 | bytes 1000000 | tf_op jit(solution)/shard_map/pallas_call | solution.py:689
  31.6 0.0 collective-permute-done.10.gb_ref
  31.6 1.1 %collective-permute-done.11.ga_ref = f32[16,144]{1,0:T(8,128)S(1)} collective-permute-done((f32[16,144]{1,0:T(8,128)S(1)}, f32[16,144]{1,0:T(8,128)S(1)}, u32[]{:S(2)}, u32[]{:S(2)}) %collective-permute-start.11) | collective-permute-done | bytes 9248 | tf_op jit(solution)/shard_map/ppermute | solution.py:747
  32.6 0.2 shard_map.60
  32.8 1.9 %collective-permute-start.12 = (f32[16,384]{1,0:T(8,128)S(1)}, f32[16,384]{1,0:T(8,128)S(1)}, u32[]{:S(2)}, u32[]{:S(2)}) collective-permute-start(f32[16,384]{1,0:T(8,128)S(1)} %get-tuple-element.76), channel_id=1, source_target_pairs={{0,1},{1,0},{2,3},{3,2},{4,8},{5,9},{6,10},{7,11},{8,4},{9,5},{10,... | collective-permute-start | bytes 73736 | tf_op jit(solution)/shard_map/ppermute | solution.py:746
  34.7 0.0 collective-permute-start.13
  34.7 0.4 shard_map.61
  35.1 1.6 %collective-permute-done.12.gb_ref = f32[16,384]{1,0:T(8,128)S(1)} collective-permute-done((f32[16,384]{1,0:T(8,128)S(1)}, f32[16,384]{1,0:T(8,128)S(1)}, u32[]{:S(2)}, u32[]{:S(2)}) %collective-permute-start.12) | collective-permute-done | bytes 24608 | tf_op jit(solution)/shard_map/ppermute | solution.py:746
  36.7 0.0 collective-permute-done.13.ga_ref
  36.7 0.3 shard_map.62
  37.0 9.2 %all_to_all.11 = f32[32,1,128]{2,1,0:T(1,128)S(1)} all-to-all(f32[32,1,128]{2,1,0:T(1,128)S(1)} %bitcast.5), channel_id=1, replica_groups=mesh['row'=8,'col'=4] {'row','col'}, dimensions={0} | all-to-all | bytes 32768 | tf_op jit(solution)/shard_map/all_to_all | solution.py:859
  46.2 1.3 %shard_map.63 = (f32[128,256]{1,0:T(8,128)}, f32[128,256]{1,0:T(8,128)}) custom-call(f32[32,128]{1,0:T(8,128)S(1)} %bitcast.4, f32[1104,512]{1,0:T(8,128)S(1)} %copy-done, f32[160,384]{1,0:T(8,128)S(1)} %get-tuple-element.59.m_ref, f32[96,256]{1,0:T(8,128)S(1)} %get-tuple-element.65.f_ref, f32[256,256]{1,0:T(8,128)S(1)} %pad_add_fusion.both_ref, ...), custom_call_target="tpu_custom_call" | custom-call | flops 1000000000 | bytes 1000000 | tf_op jit(solution)/shard_map/pallas_call | solution.py:689
Async XLA Ops:
  1.8 9.9 %copy-start = (f32[1104,512]{1,0:T(8,128)S(1)}, f32[1104,512]{1,0:T(8,128)}, u32[]{:S(2)}) copy-start(f32[1104,512]{1,0:T(8,128)} %constant.5.clone.basis_ref) | copy-start | bytes 6782980
  1.8 5.7 %collective-permute-start = (f32[40,128]{1,0:T(8,128)S(1)}, f32[40,128]{1,0:T(8,128)S(1)}, u32[]{:S(2)}, u32[]{:S(2)}) collective-permute-start(f32[40,128]{1,0:T(8,128)S(1)} %get-tuple-element.44), channel_id=1, source_target_pairs={{0,3},{1,2},{2,1},{3,0},{4,7},{5,6},{6,5},{7,4},{8,11},{9,10},{10,... | collective-permute-start | bytes 61448 | tf_op jit(solution)/shard_map/ppermute | solution.py:746
  5.8 3.8 %collective-permute-start.1 = (f32[40,128]{1,0:T(8,128)S(1)}, f32[40,128]{1,0:T(8,128)S(1)}, u32[]{:S(2)}, u32[]{:S(2)}) collective-permute-start(f32[40,128]{1,0:T(8,128)S(1)} %get-tuple-element.45), channel_id=1, source_target_pairs={{0,1},{1,0},{2,3},{3,2},{4,5},{5,4},{6,7},{7,6},{8,9},{9,8},{10,11... | collective-permute-start | bytes 61448 | tf_op jit(solution)/shard_map/ppermute | solution.py:747
  9.7 5.6 %collective-permute-start.2 = (f32[32,384]{1,0:T(8,128)S(1)}, f32[32,384]{1,0:T(8,128)S(1)}, u32[]{:S(2)}, u32[]{:S(2)}) collective-permute-start(f32[32,384]{1,0:T(8,128)S(1)} %get-tuple-element.46), channel_id=1, source_target_pairs={{0,28},{1,29},{2,30},{3,31},{4,8},{5,9},{6,10},{7,11},{8,4},{9,5},... | collective-permute-start | bytes 147464 | tf_op jit(solution)/shard_map/ppermute | solution.py:746
  11.7 3.7 %collective-permute-start.3 = (f32[32,384]{1,0:T(8,128)S(1)}, f32[32,384]{1,0:T(8,128)S(1)}, u32[]{:S(2)}, u32[]{:S(2)}) collective-permute-start(f32[32,384]{1,0:T(8,128)S(1)} %get-tuple-element.47), channel_id=1, source_target_pairs={{0,4},{4,0},{8,12},{12,8},{16,20},{20,16},{24,28},{28,24},{1,5},{5... | collective-permute-start | bytes 147464 | tf_op jit(solution)/shard_map/ppermute | solution.py:747
  11.9 7.5 %collective-permute-start.6 = (f32[8,128]{1,0:T(8,128)S(1)}, f32[8,128]{1,0:T(8,128)S(1)}, u32[]{:S(2)}, u32[]{:S(2)}) collective-permute-start(f32[8,128]{1,0:T(8,128)S(1)} %get-tuple-element.51.table_ref), channel_id=1, source_target_pairs={{0,16},{1,17},{2,18},{3,19},{4,20},{5,21},{6,22},{7,23},{8,24},{9,... | collective-permute-start | bytes 12296 | tf_op jit(solution)/shard_map/ppermute | solution.py:750
  16.4 2.9 %collective-permute-start.4 = (f32[32,144]{1,0:T(8,128)S(1)}, f32[32,144]{1,0:T(8,128)S(1)}, u32[]{:S(2)}, u32[]{:S(2)}) collective-permute-start(f32[32,144]{1,0:T(8,128)S(1)} %get-tuple-element.56), channel_id=1, source_target_pairs={{0,4},{1,2},{2,1},{3,7},{4,0},{5,6},{6,5},{7,3},{8,12},{9,10},{10,... | collective-permute-start | bytes 55304 | tf_op jit(solution)/shard_map/ppermute | solution.py:746
  16.5 4.2 %collective-permute-start.5 = (f32[32,144]{1,0:T(8,128)S(1)}, f32[32,144]{1,0:T(8,128)S(1)}, u32[]{:S(2)}, u32[]{:S(2)}) collective-permute-start(f32[32,144]{1,0:T(8,128)S(1)} %get-tuple-element.57), channel_id=1, source_target_pairs={{0,1},{1,0},{2,3},{3,2},{4,5},{5,4},{6,7},{7,6},{8,9},{9,8},{10,11... | collective-permute-start | bytes 55304 | tf_op jit(solution)/shard_map/ppermute | solution.py:747
  19.3 5.5 %collective-permute-start.9 = (f32[8,128]{1,0:T(8,128)S(1)}, f32[8,128]{1,0:T(8,128)S(1)}, u32[]{:S(2)}, u32[]{:S(2)}) collective-permute-start(f32[8,128]{1,0:T(8,128)S(1)} %get-tuple-element.63), channel_id=1, source_target_pairs={{0,18},{1,19},{2,16},{3,17},{4,22},{5,23},{6,20},{7,21},{8,26},{9,... | collective-permute-start | bytes 12296 | tf_op jit(solution)/shard_map/ppermute | solution.py:750
  20.8 5.4 %collective-permute-start.7 = (f32[32,384]{1,0:T(8,128)S(1)}, f32[32,384]{1,0:T(8,128)S(1)}, u32[]{:S(2)}, u32[]{:S(2)}) collective-permute-start(f32[32,384]{1,0:T(8,128)S(1)} %get-tuple-element.60), channel_id=1, source_target_pairs={{0,28},{1,29},{2,30},{3,31},{4,8},{5,9},{6,10},{7,11},{8,4},{9,5},... | collective-permute-start | bytes 147464 | tf_op jit(solution)/shard_map/ppermute | solution.py:746
  21.4 4.8 %collective-permute-start.8 = (f32[32,384]{1,0:T(8,128)S(1)}, f32[32,384]{1,0:T(8,128)S(1)}, u32[]{:S(2)}, u32[]{:S(2)}) collective-permute-start(f32[32,384]{1,0:T(8,128)S(1)} %get-tuple-element.61), channel_id=1, source_target_pairs={{0,4},{4,0},{8,12},{12,8},{16,20},{20,16},{24,28},{28,24},{1,5},{5... | collective-permute-start | bytes 147464 | tf_op jit(solution)/shard_map/ppermute | solution.py:747
  27.5 4.1 %collective-permute-start.10 = (f32[16,144]{1,0:T(8,128)S(1)}, f32[16,144]{1,0:T(8,128)S(1)}, u32[]{:S(2)}, u32[]{:S(2)}) collective-permute-start(f32[16,144]{1,0:T(8,128)S(1)} %get-tuple-element.73), channel_id=1, source_target_pairs={{0,4},{1,2},{2,1},{3,7},{4,0},{5,6},{6,5},{7,3},{8,12},{9,10},{10,... | collective-permute-start | bytes 27656 | tf_op jit(solution)/shard_map/ppermute | solution.py:746
  27.6 5.0 %collective-permute-start.11 = (f32[16,144]{1,0:T(8,128)S(1)}, f32[16,144]{1,0:T(8,128)S(1)}, u32[]{:S(2)}, u32[]{:S(2)}) collective-permute-start(f32[16,144]{1,0:T(8,128)S(1)} %get-tuple-element.74), channel_id=1, source_target_pairs={{0,1},{1,0},{2,3},{3,2},{4,5},{5,4},{6,7},{7,6},{8,9},{9,8},{10,11... | collective-permute-start | bytes 27656 | tf_op jit(solution)/shard_map/ppermute | solution.py:747
  32.8 3.9 %collective-permute-start.12 = (f32[16,384]{1,0:T(8,128)S(1)}, f32[16,384]{1,0:T(8,128)S(1)}, u32[]{:S(2)}, u32[]{:S(2)}) collective-permute-start(f32[16,384]{1,0:T(8,128)S(1)} %get-tuple-element.76), channel_id=1, source_target_pairs={{0,1},{1,0},{2,3},{3,2},{4,8},{5,9},{6,10},{7,11},{8,4},{9,5},{10,... | collective-permute-start | bytes 73736 | tf_op jit(solution)/shard_map/ppermute | solution.py:746
  34.7 2.0 %collective-permute-start.13 = (f32[16,384]{1,0:T(8,128)S(1)}, f32[16,384]{1,0:T(8,128)S(1)}, u32[]{:S(2)}, u32[]{:S(2)}) collective-permute-start(f32[16,384]{1,0:T(8,128)S(1)} %get-tuple-element.77), channel_id=1, source_target_pairs={{0,4},{4,0},{8,12},{12,8},{16,20},{20,16},{24,28},{28,24},{1,5},{5... | collective-permute-start | bytes 73736 | tf_op jit(solution)/shard_map/ppermute | solution.py:747

commit v20 on v19

--- a/solution.py
+++ b/solution.py
@@ -492,6 +492,7 @@
     ga_ref,
     table_ref,
     farther_ref,
+    farthest_ref,
     inner_w_ref,
     f_ref,
     gw_ref,
@@ -510,7 +511,8 @@
     mask = edge_mask(counts)
     s = edges(y, *sides(i, counts[0], ga_ref[:24], gb_ref[:24]))
     s = jnp.where(mask, s, 0.0)
-    table = merged(table_ref[...], farther_ref[...], ga_ref[24:, :128], gb_ref[24:, :128])
+    table = merged(table_ref[...], farther_ref[...], farthest_ref[...])
+    table = merged(table, ga_ref[24:, :128], gb_ref[24:, :128])
     picked = jnp.sum(near_ref[...] * as_row(table, width), axis=1, keepdims=True)
     bands = as_bands([picked[k : k + 1] for k in range(12)])
     coarse = edge_bands(bands)
@@ -727,11 +729,11 @@
 
     even = [xor_pairs(counts, 0, 1), xor_pairs(counts, 1, 0)]
     known = meet(even[0], odd_pairs(counts, 1, 0))
-    first = meet(xor_pairs(counts, 4, 0))
+    first = meet(xor_pairs(counts, 6, 0))
     known = meet(even[1], odd_pairs(counts, 0, 0))
-    second = meet(xor_pairs(counts, 4, 2))
+    second = meet(xor_pairs(counts, 4, 0), xor_pairs(counts, 4, 2))
     known = meet(even[0], odd_pairs(counts, 1, 1)) | first
-    return (meet(even[1], odd_pairs(counts, 0, 0)) | second).all()
+    return (meet(even[1], odd_pairs(counts, 0, 1)) | second).all()
 
 
 def body(counts, height, noise):
@@ -770,7 +772,7 @@
     )
     ga, gb = swap(a, b, "row")
     weight, table = call(weights_kernel, [(EXT, 2 * SPEC), (depth, 128)], both, table, basis)
-    far = small_swap(table, 4, 0)
+    far = small_swap(table, 6, 0)
     t = call(forward_kernel, [(EXT, 2 * SPEC)], both, r3, basis)[0]
     t, table, b, a = call(
         functools.partial(first_kernel, counts),
@@ -794,7 +796,7 @@
         table,
     )
     ga, gb = swap(a, b, "col", 1)
-    farther = small_swap(table_too, 4, 2)
+    farther = small_swap(table_too, 4, 0), small_swap(table_too, 4, 2)
     y, table, b, a = call(
         functools.partial(columns_kernel, counts),
         [(EXT, FC), (depth, 128)] + [(24 + depth, FC)] * 2,
@@ -804,7 +806,7 @@
         table,
         far,
     )
-    ga, gb = swap(a, b, "row")
+    ga, gb = swap(a, b, "row", 1)
     inner_w, f, gw, gf, near = call(
         functools.partial(inner_kernel, counts, width),
         [(96, TC)] * 2 + [(EXT, FC)] * 2 + [(16, width)],
@@ -820,7 +822,7 @@
         gb,
         ga,
         table,
-        farther,
+        *farther,
         inner_w,
         f,
         gw,

time: 47.6 us -> 48.3 us (1.015)
  starting transfers between devices: 17.1 us -> 20.6 us
  waiting for transfers between devices: 11.5 us -> 8.18 us
  blocking collectives: 9.2 us -> 9.72 us
    ppermute x2 -> x3, waiting for transfers between devices: 2.27 us -> 0.07 us  [small_swap(): return lax.ppermute(x, both_axes, xor_pairs(counts, rows, cols))]
    ppermute x2 -> x3, starting transfers between devices: 2.5 us -> 4.54 us  [small_swap(): return lax.ppermute(x, both_axes, xor_pairs(counts, rows, cols))]
    ppermute x6, starting transfers between devices: 8.59 us -> 10.1 us  [swap(): lax.ppermute(b, both_axes, odd_pairs(counts, both_axes.index(axis), bit))]
    ppermute x6, waiting for transfers between devices: 4.39 us -> 3.08 us  [swap(): return (lax.ppermute(a, axis, pairs_from(lax.axis_size(axis), 0)), gb)]
    all_to_all x1, blocking collectives: 9.2 us -> 9.72 us  [body(): stats = lax.all_to_all(stats, both_axes, 0, 0, tiled=True)]
  transfers between devices with their start and end apart: 14 -> 15, of which waited for: 8 -> 7; matrix products, arithmetic and copies ran while one was open for 0% -> 0% of each run, Pallas kernels for 10% -> 9%
where the time goes in v20:
time: 48.3 us; the launch traced here: 48.1 us
  starting transfers between devices  20.6 us (43%)
  blocking collectives  9.72 us (20%)
  waiting for transfers between devices  8.18 us (17%)
  Pallas kernels  7.88 us (16%)
  other arithmetic  0.99 us (2%)
  between operations  0.74 us (2%)
    ppermute x6, starting transfers between devices, swap(): lax.ppermute(b, both_axes, odd_pairs(counts, both_axes.index(axis), bit))  10.1 us
    all_to_all x1, blocking collectives, body(): stats = lax.all_to_all(stats, both_axes, 0, 0, tiled=True)  9.72 us
    pallas_call x14, Pallas kernels, call(): pl.pallas_call(kernel, out_shape=shapes, compiler_params=pltpu.CompilerPa...  7.88 us
    ppermute x6, starting transfers between devices, swap(): return (lax.ppermute(a, axis, pairs_from(lax.axis_size(axis), 0)), gb)  5.94 us
    ppermute x6, waiting for transfers between devices, swap(): lax.ppermute(b, both_axes, odd_pairs(counts, both_axes.index(axis), bit))  5.03 us
    ppermute x3, starting transfers between devices, small_swap(): return lax.ppermute(x, both_axes, xor_pairs(counts, rows, cols))  4.54 us
    ppermute x6, waiting for transfers between devices, swap(): return (lax.ppermute(a, axis, pairs_from(lax.axis_size(axis), 0)), gb)  3.08 us
    add x1, other arithmetic, body(): jnp.pad(noise, ((0, TR), (0, 0))) + jnp.pad(height, ((TR, 0), (0, 0)))  0.99 us
  transfers between devices with their start and end apart: 15, of which 7 were waited for; matrix products, arithmetic and copies ran while one was open for 0% of the time, Pallas kernels for 9%

profile of v20, /device:TPU:0, one launch (start us, length us, event | category | flops | bytes accessed | tf_op | source)
XLA Modules:
  0.0 48.1 jit_solution(13931385061820826563)
XLA Ops:
  0.6 1.0 %pad_add_fusion.both_ref = f32[256,256]{1,0:T(8,128)S(1)} fusion(f32[128,256]{1,0:T(8,128)} %param.3, f32[128,256]{1,0:T(8,128)} %param.4), kind=kLoop, calls=%fused_computation | loop fusion | flops 65536 | bytes 524288 | tf_op jit(solution)/shard_map/add | solution.py:754
  1.6 0.2 shard_map.50
  1.8 0.0 copy-start
  1.8 4.0 %collective-permute-start = (f32[40,128]{1,0:T(8,128)S(1)}, f32[40,128]{1,0:T(8,128)S(1)}, u32[]{:S(2)}, u32[]{:S(2)}) collective-permute-start(f32[40,128]{1,0:T(8,128)S(1)} %get-tuple-element.44), channel_id=1, source_target_pairs={{0,3},{1,2},{2,1},{3,0},{4,7},{5,6},{6,5},{7,4},{8,11},{9,10},{10,... | collective-permute-start | bytes 61448 | tf_op jit(solution)/shard_map/ppermute | solution.py:748
  5.8 0.5 %collective-permute-start.1 = (f32[40,128]{1,0:T(8,128)S(1)}, f32[40,128]{1,0:T(8,128)S(1)}, u32[]{:S(2)}, u32[]{:S(2)}) collective-permute-start(f32[40,128]{1,0:T(8,128)S(1)} %get-tuple-element.45), channel_id=1, source_target_pairs={{0,1},{1,0},{2,3},{3,2},{4,5},{5,4},{6,7},{7,6},{8,9},{9,8},{10,11... | collective-permute-start | bytes 61448 | tf_op jit(solution)/shard_map/ppermute | solution.py:749
  6.3 1.2 %collective-permute-done.gb_ref = f32[40,128]{1,0:T(8,128)S(1)} collective-permute-done((f32[40,128]{1,0:T(8,128)S(1)}, f32[40,128]{1,0:T(8,128)S(1)}, u32[]{:S(2)}, u32[]{:S(2)}) %collective-permute-start) | collective-permute-done | bytes 20512 | tf_op jit(solution)/shard_map/ppermute | solution.py:748
  7.5 2.0 %collective-permute-done.1.ga_ref = f32[40,128]{1,0:T(8,128)S(1)} collective-permute-done((f32[40,128]{1,0:T(8,128)S(1)}, f32[40,128]{1,0:T(8,128)S(1)}, u32[]{:S(2)}, u32[]{:S(2)}) %collective-permute-start.1) | collective-permute-done | bytes 20512 | tf_op jit(solution)/shard_map/ppermute | solution.py:749
  9.5 0.2 shard_map.51
  9.7 2.0 %collective-permute-start.2 = (f32[32,384]{1,0:T(8,128)S(1)}, f32[32,384]{1,0:T(8,128)S(1)}, u32[]{:S(2)}, u32[]{:S(2)}) collective-permute-start(f32[32,384]{1,0:T(8,128)S(1)} %get-tuple-element.46), channel_id=1, source_target_pairs={{0,28},{1,29},{2,30},{3,31},{4,8},{5,9},{6,10},{7,11},{8,4},{9,5},... | collective-permute-start | bytes 147464 | tf_op jit(solution)/shard_map/ppermute | solution.py:748
  11.7 0.0 collective-permute-start.3
  11.7 0.0 copy-done
  11.7 0.1 shard_map.53
  11.9 2.1 %collective-permute-start.6 = (f32[8,128]{1,0:T(8,128)S(1)}, f32[8,128]{1,0:T(8,128)S(1)}, u32[]{:S(2)}, u32[]{:S(2)}) collective-permute-start(f32[8,128]{1,0:T(8,128)S(1)} %get-tuple-element.51.table_ref), channel_id=1, source_target_pairs={{0,24},{1,25},{2,26},{3,27},{4,28},{5,29},{6,30},{7,31},{8,16},{9,... | collective-permute-start | bytes 12296 | tf_op jit(solution)/shard_map/ppermute | solution.py:752
  14.0 0.6 %shard_map.52.tile_ref = f32[144,512]{1,0:T(8,128)S(1)} custom-call(f32[256,256]{1,0:T(8,128)S(1)} %pad_add_fusion.both_ref, f32[128,128]{1,0:T(8,128)S(1)} %get-tuple-element.48.r3_ref, f32[1104,512]{1,0:T(8,128)S(1)} %copy-done), custom_call_target="tpu_custom_call" | custom-call | flops 1000000000 | bytes 1000000 | tf_op jit(solution)/shard_map/pallas_call | solution.py:691
  14.5 0.8 %collective-permute-done.2.gb_ref = f32[32,384]{1,0:T(8,128)S(1)} collective-permute-done((f32[32,384]{1,0:T(8,128)S(1)}, f32[32,384]{1,0:T(8,128)S(1)}, u32[]{:S(2)}, u32[]{:S(2)}) %collective-permute-start.2) | collective-permute-done | bytes 49184 | tf_op jit(solution)/shard_map/ppermute | solution.py:748
  15.4 0.0 collective-permute-done.3.ga_ref
  15.4 1.0 %shard_map.54 = (f32[144,512]{1,0:T(8,128)S(1)}, f32[8,128]{1,0:T(8,128)S(1)}, f32[32,144]{1,0:T(8,128)S(1)}, f32[32,144]{1,0:T(8,128)S(1)}) custom-call(f32[32,384]{1,0:T(8,128)S(1)} %collective-permute-done.2.gb_ref, f32[32,384]{1,0:T(8,128)S(1)} %collective-permute-done.3.ga_ref, f32[144,512]{1,0:T(8,128)S(1)} %shard_map.52.tile_ref, ...), custom_call_target="tpu_custom_call" | custom-call | flops 1000000000 | bytes 1000000 | tf_op jit(solution)/shard_map/pallas_call | solution.py:691
  16.4 0.1 collective-permute-start.4
  16.5 2.0 %collective-permute-start.5 = (f32[32,144]{1,0:T(8,128)S(1)}, f32[32,144]{1,0:T(8,128)S(1)}, u32[]{:S(2)}, u32[]{:S(2)}) collective-permute-start(f32[32,144]{1,0:T(8,128)S(1)} %get-tuple-element.57), channel_id=1, source_target_pairs={{0,1},{1,0},{2,3},{3,2},{4,5},{5,4},{6,7},{7,6},{8,9},{9,8},{10,11... | collective-permute-start | bytes 55304 | tf_op jit(solution)/shard_map/ppermute | solution.py:749
  18.4 0.8 %shard_map.55 = (f32[144,384]{1,0:T(8,128)S(1)}, f32[160,384]{1,0:T(8,128)S(1)}, f32[8,128]{1,0:T(8,128)S(1)}) custom-call(f32[144,512]{1,0:T(8,128)S(1)} %get-tuple-element.52.t_ref, f32[1104,512]{1,0:T(8,128)S(1)} %copy-done, f32[256,256]{1,0:T(8,128)S(1)} %pad_add_fusion.both_ref, f32[128,128]{1,0:T(8,128)S(1)} %get-tuple-element.53.h3_ref, ...), custom_call_target="tpu_custom_call" | custom-call | flops 1000000000 | bytes 1000000 | tf_op jit(solution)/shard_map/pallas_call | solution.py:691
  19.3 0.1 collective-permute-start.10
  19.3 2.4 %collective-permute-start.9 = (f32[8,128]{1,0:T(8,128)S(1)}, f32[8,128]{1,0:T(8,128)S(1)}, u32[]{:S(2)}, u32[]{:S(2)}) collective-permute-start(f32[8,128]{1,0:T(8,128)S(1)} %get-tuple-element.63), channel_id=1, source_target_pairs={{0,16},{1,17},{2,18},{3,19},{4,20},{5,21},{6,22},{7,23},{8,24},{9,... | collective-permute-start | bytes 12296 | tf_op jit(solution)/shard_map/ppermute | solution.py:752
  21.7 0.0 collective-permute-done.6.refs_1_
  21.7 0.0 collective-permute-done.4.gb_ref
  21.7 0.0 collective-permute-done.5.ga_ref
  21.7 0.2 shard_map.56
  21.9 2.1 %collective-permute-start.7 = (f32[32,384]{1,0:T(8,128)S(1)}, f32[32,384]{1,0:T(8,128)S(1)}, u32[]{:S(2)}, u32[]{:S(2)}) collective-permute-start(f32[32,384]{1,0:T(8,128)S(1)} %get-tuple-element.60), channel_id=1, source_target_pairs={{0,1},{1,0},{2,3},{3,2},{4,8},{5,9},{6,10},{7,11},{8,4},{9,5},{10,... | collective-permute-start | bytes 147464 | tf_op jit(solution)/shard_map/ppermute | solution.py:748
  24.0 0.0 collective-permute-start.8
  24.0 0.7 %shard_map.57 = (f32[96,256]{1,0:T(8,128)S(1)}, f32[96,256]{1,0:T(8,128)S(1)}, f32[144,384]{1,0:T(8,128)S(1)}, f32[144,384]{1,0:T(8,128)S(1)}, f32[16,128]{1,0:T(8,128)S(1)}) custom-call(f32[144,384]{1,0:T(8,128)S(1)} %get-tuple-element.58.y_ref, f32[160,384]{1,0:T(8,128)S(1)} %get-tuple-element.59.m_ref, f32[1104,512]{1,0:T(8,128)S(1)} %copy-done), custom_call_target="tpu_custom_call" | custom-call | flops 1000000000 | bytes 1000000 | tf_op jit(solution)/shard_map/pallas_call | solution.py:691
  24.7 0.1 collective-permute-done.10.farthest_ref
  24.7 0.0 collective-permute-done.9.farther_ref
  24.7 1.3 %collective-permute-done.7.gb_ref = f32[32,384]{1,0:T(8,128)S(1)} collective-permute-done((f32[32,384]{1,0:T(8,128)S(1)}, f32[32,384]{1,0:T(8,128)S(1)}, u32[]{:S(2)}, u32[]{:S(2)}) %collective-permute-start.7) | collective-permute-done | bytes 49184 | tf_op jit(solution)/shard_map/ppermute | solution.py:748
  26.1 0.0 collective-permute-done.8.ga_ref
  26.1 1.3 %shard_map.58 = (f32[128,256]{1,0:T(8,128)S(1)}, f32[128,256]{1,0:T(8,128)S(1)}, f32[144,512]{1,0:T(8,128)S(1)}, f32[16,144]{1,0:T(8,128)S(1)}, f32[16,144]{1,0:T(8,128)S(1)}) custom-call(f32[144,384]{1,0:T(8,128)S(1)} %get-tuple-element.58.y_ref, f32[160,384]{1,0:T(8,128)S(1)} %get-tuple-element.59.m_ref, f32[32,384]{1,0:T(8,128)S(1)} %collective-permute-done.7.gb_ref, ...), custom_call_target="tpu_custom_call" | custom-call | flops 1000000000 | bytes 1000000 | tf_op jit(solution)/shard_map/pallas_call | solution.py:691
  27.3 0.1 collective-permute-start.11
  27.5 3.4 %collective-permute-start.12 = (f32[16,144]{1,0:T(8,128)S(1)}, f32[16,144]{1,0:T(8,128)S(1)}, u32[]{:S(2)}, u32[]{:S(2)}) collective-permute-start(f32[16,144]{1,0:T(8,128)S(1)} %get-tuple-element.74), channel_id=1, source_target_pairs={{0,1},{1,0},{2,3},{3,2},{4,5},{5,4},{6,7},{7,6},{8,9},{9,8},{10,11... | collective-permute-start | bytes 27656 | tf_op jit(solution)/shard_map/ppermute | solution.py:749
  30.9 0.8 %shard_map.59 = (f32[144,384]{1,0:T(8,128)S(1)}, f32[1,128]{1,0:T(1,128)S(1)}) custom-call(f32[144,512]{1,0:T(8,128)S(1)} %get-tuple-element.69.t_ref, f32[1104,512]{1,0:T(8,128)S(1)} %copy-done, f32[256,256]{1,0:T(8,128)S(1)} %pad_add_fusion.both_ref, f32[160,384]{1,0:T(8,128)S(1)} %get-tuple-element.59.m_ref, f32[128,256]{1,0:T(8,128)S(1)} %get-tuple-element.70.z_ref, ...), custom_call_target="tpu_custom_call" | custom-call | flops 1000000000 | bytes 1000000 | tf_op jit(solution)/shard_map/pallas_call | solution.py:691
  31.7 0.0 collective-permute-done.11.gb_ref
  31.7 1.1 %collective-permute-done.12.ga_ref = f32[16,144]{1,0:T(8,128)S(1)} collective-permute-done((f32[16,144]{1,0:T(8,128)S(1)}, f32[16,144]{1,0:T(8,128)S(1)}, u32[]{:S(2)}, u32[]{:S(2)}) %collective-permute-start.12) | collective-permute-done | bytes 9248 | tf_op jit(solution)/shard_map/ppermute | solution.py:749
  32.8 0.2 shard_map.60
  33.0 1.9 %collective-permute-start.13 = (f32[16,384]{1,0:T(8,128)S(1)}, f32[16,384]{1,0:T(8,128)S(1)}, u32[]{:S(2)}, u32[]{:S(2)}) collective-permute-start(f32[16,384]{1,0:T(8,128)S(1)} %get-tuple-element.76), channel_id=1, source_target_pairs={{0,1},{1,0},{2,3},{3,2},{4,8},{5,9},{6,10},{7,11},{8,4},{9,5},{10,... | collective-permute-start | bytes 73736 | tf_op jit(solution)/shard_map/ppermute | solution.py:748
  34.9 0.0 collective-permute-start.14
  34.9 0.4 shard_map.61
  35.2 1.6 %collective-permute-done.13.gb_ref = f32[16,384]{1,0:T(8,128)S(1)} collective-permute-done((f32[16,384]{1,0:T(8,128)S(1)}, f32[16,384]{1,0:T(8,128)S(1)}, u32[]{:S(2)}, u32[]{:S(2)}) %collective-permute-start.13) | collective-permute-done | bytes 24608 | tf_op jit(solution)/shard_map/ppermute | solution.py:748
  36.9 0.0 collective-permute-done.14.ga_ref
  36.9 0.3 shard_map.62
  37.1 9.7 %all_to_all.11 = f32[32,1,128]{2,1,0:T(1,128)S(1)} all-to-all(f32[32,1,128]{2,1,0:T(1,128)S(1)} %bitcast.5), channel_id=1, replica_groups=mesh['row'=8,'col'=4] {'row','col'}, dimensions={0} | all-to-all | bytes 32768 | tf_op jit(solution)/shard_map/all_to_all | solution.py:861
  46.8 1.3 %shard_map.63 = (f32[128,256]{1,0:T(8,128)}, f32[128,256]{1,0:T(8,128)}) custom-call(f32[32,128]{1,0:T(8,128)S(1)} %bitcast.4, f32[1104,512]{1,0:T(8,128)S(1)} %copy-done, f32[160,384]{1,0:T(8,128)S(1)} %get-tuple-element.59.m_ref, f32[96,256]{1,0:T(8,128)S(1)} %get-tuple-element.65.f_ref, f32[256,256]{1,0:T(8,128)S(1)} %pad_add_fusion.both_ref, ...), custom_call_target="tpu_custom_call" | custom-call | flops 1000000000 | bytes 1000000 | tf_op jit(solution)/shard_map/pallas_call | solution.py:691
Async XLA Ops:
  1.8 9.9 %copy-start = (f32[1104,512]{1,0:T(8,128)S(1)}, f32[1104,512]{1,0:T(8,128)}, u32[]{:S(2)}) copy-start(f32[1104,512]{1,0:T(8,128)} %constant.5.clone.basis_ref) | copy-start | bytes 6782980
  1.8 5.7 %collective-permute-start = (f32[40,128]{1,0:T(8,128)S(1)}, f32[40,128]{1,0:T(8,128)S(1)}, u32[]{:S(2)}, u32[]{:S(2)}) collective-permute-start(f32[40,128]{1,0:T(8,128)S(1)} %get-tuple-element.44), channel_id=1, source_target_pairs={{0,3},{1,2},{2,1},{3,0},{4,7},{5,6},{6,5},{7,4},{8,11},{9,10},{10,... | collective-permute-start | bytes 61448 | tf_op jit(solution)/shard_map/ppermute | solution.py:748
  5.8 3.8 %collective-permute-start.1 = (f32[40,128]{1,0:T(8,128)S(1)}, f32[40,128]{1,0:T(8,128)S(1)}, u32[]{:S(2)}, u32[]{:S(2)}) collective-permute-start(f32[40,128]{1,0:T(8,128)S(1)} %get-tuple-element.45), channel_id=1, source_target_pairs={{0,1},{1,0},{2,3},{3,2},{4,5},{5,4},{6,7},{7,6},{8,9},{9,8},{10,11... | collective-permute-start | bytes 61448 | tf_op jit(solution)/shard_map/ppermute | solution.py:749
  9.7 5.6 %collective-permute-start.2 = (f32[32,384]{1,0:T(8,128)S(1)}, f32[32,384]{1,0:T(8,128)S(1)}, u32[]{:S(2)}, u32[]{:S(2)}) collective-permute-start(f32[32,384]{1,0:T(8,128)S(1)} %get-tuple-element.46), channel_id=1, source_target_pairs={{0,28},{1,29},{2,30},{3,31},{4,8},{5,9},{6,10},{7,11},{8,4},{9,5},... | collective-permute-start | bytes 147464 | tf_op jit(solution)/shard_map/ppermute | solution.py:748
  11.7 3.7 %collective-permute-start.3 = (f32[32,384]{1,0:T(8,128)S(1)}, f32[32,384]{1,0:T(8,128)S(1)}, u32[]{:S(2)}, u32[]{:S(2)}) collective-permute-start(f32[32,384]{1,0:T(8,128)S(1)} %get-tuple-element.47), channel_id=1, source_target_pairs={{0,4},{4,0},{8,12},{12,8},{16,20},{20,16},{24,28},{28,24},{1,5},{5... | collective-permute-start | bytes 147464 | tf_op jit(solution)/shard_map/ppermute | solution.py:749
  11.9 9.8 %collective-permute-start.6 = (f32[8,128]{1,0:T(8,128)S(1)}, f32[8,128]{1,0:T(8,128)S(1)}, u32[]{:S(2)}, u32[]{:S(2)}) collective-permute-start(f32[8,128]{1,0:T(8,128)S(1)} %get-tuple-element.51.table_ref), channel_id=1, source_target_pairs={{0,24},{1,25},{2,26},{3,27},{4,28},{5,29},{6,30},{7,31},{8,16},{9,... | collective-permute-start | bytes 12296 | tf_op jit(solution)/shard_map/ppermute | solution.py:752
  16.4 5.3 %collective-permute-start.4 = (f32[32,144]{1,0:T(8,128)S(1)}, f32[32,144]{1,0:T(8,128)S(1)}, u32[]{:S(2)}, u32[]{:S(2)}) collective-permute-start(f32[32,144]{1,0:T(8,128)S(1)} %get-tuple-element.56), channel_id=1, source_target_pairs={{0,4},{1,2},{2,1},{3,7},{4,0},{5,6},{6,5},{7,3},{8,12},{9,10},{10,... | collective-permute-start | bytes 55304 | tf_op jit(solution)/shard_map/ppermute | solution.py:748
  16.5 5.3 %collective-permute-start.5 = (f32[32,144]{1,0:T(8,128)S(1)}, f32[32,144]{1,0:T(8,128)S(1)}, u32[]{:S(2)}, u32[]{:S(2)}) collective-permute-start(f32[32,144]{1,0:T(8,128)S(1)} %get-tuple-element.57), channel_id=1, source_target_pairs={{0,1},{1,0},{2,3},{3,2},{4,5},{5,4},{6,7},{7,6},{8,9},{9,8},{10,11... | collective-permute-start | bytes 55304 | tf_op jit(solution)/shard_map/ppermute | solution.py:749
  19.3 5.5 %collective-permute-start.10 = (f32[8,128]{1,0:T(8,128)S(1)}, f32[8,128]{1,0:T(8,128)S(1)}, u32[]{:S(2)}, u32[]{:S(2)}) collective-permute-start(f32[8,128]{1,0:T(8,128)S(1)} %get-tuple-element.63), channel_id=1, source_target_pairs={{0,18},{1,19},{2,16},{3,17},{4,22},{5,23},{6,20},{7,21},{8,26},{9,... | collective-permute-start | bytes 12296 | tf_op jit(solution)/shard_map/ppermute | solution.py:752
  19.3 5.4 %collective-permute-start.9 = (f32[8,128]{1,0:T(8,128)S(1)}, f32[8,128]{1,0:T(8,128)S(1)}, u32[]{:S(2)}, u32[]{:S(2)}) collective-permute-start(f32[8,128]{1,0:T(8,128)S(1)} %get-tuple-element.63), channel_id=1, source_target_pairs={{0,16},{1,17},{2,18},{3,19},{4,20},{5,21},{6,22},{7,23},{8,24},{9,... | collective-permute-start | bytes 12296 | tf_op jit(solution)/shard_map/ppermute | solution.py:752
  21.9 4.2 %collective-permute-start.7 = (f32[32,384]{1,0:T(8,128)S(1)}, f32[32,384]{1,0:T(8,128)S(1)}, u32[]{:S(2)}, u32[]{:S(2)}) collective-permute-start(f32[32,384]{1,0:T(8,128)S(1)} %get-tuple-element.60), channel_id=1, source_target_pairs={{0,1},{1,0},{2,3},{3,2},{4,8},{5,9},{6,10},{7,11},{8,4},{9,5},{10,... | collective-permute-start | bytes 147464 | tf_op jit(solution)/shard_map/ppermute | solution.py:748
  24.0 2.1 %collective-permute-start.8 = (f32[32,384]{1,0:T(8,128)S(1)}, f32[32,384]{1,0:T(8,128)S(1)}, u32[]{:S(2)}, u32[]{:S(2)}) collective-permute-start(f32[32,384]{1,0:T(8,128)S(1)} %get-tuple-element.61), channel_id=1, source_target_pairs={{0,4},{4,0},{8,12},{12,8},{16,20},{20,16},{24,28},{28,24},{1,5},{5... | collective-permute-start | bytes 147464 | tf_op jit(solution)/shard_map/ppermute | solution.py:749
  27.3 4.4 %collective-permute-start.11 = (f32[16,144]{1,0:T(8,128)S(1)}, f32[16,144]{1,0:T(8,128)S(1)}, u32[]{:S(2)}, u32[]{:S(2)}) collective-permute-start(f32[16,144]{1,0:T(8,128)S(1)} %get-tuple-element.73), channel_id=1, source_target_pairs={{0,4},{1,2},{2,1},{3,7},{4,0},{5,6},{6,5},{7,3},{8,12},{9,10},{10,... | collective-permute-start | bytes 27656 | tf_op jit(solution)/shard_map/ppermute | solution.py:748
  27.5 5.3 %collective-permute-start.12 = (f32[16,144]{1,0:T(8,128)S(1)}, f32[16,144]{1,0:T(8,128)S(1)}, u32[]{:S(2)}, u32[]{:S(2)}) collective-permute-start(f32[16,144]{1,0:T(8,128)S(1)} %get-tuple-element.74), channel_id=1, source_target_pairs={{0,1},{1,0},{2,3},{3,2},{4,5},{5,4},{6,7},{7,6},{8,9},{9,8},{10,11... | collective-permute-start | bytes 27656 | tf_op jit(solution)/shard_map/ppermute | solution.py:749
  33.0 3.9 %collective-permute-start.13 = (f32[16,384]{1,0:T(8,128)S(1)}, f32[16,384]{1,0:T(8,128)S(1)}, u32[]{:S(2)}, u32[]{:S(2)}) collective-permute-start(f32[16,384]{1,0:T(8,128)S(1)} %get-tuple-element.76), channel_id=1, source_target_pairs={{0,1},{1,0},{2,3},{3,2},{4,8},{5,9},{6,10},{7,11},{8,4},{9,5},{10,... | collective-permute-start | bytes 73736 | tf_op jit(solution)/shard_map/ppermute | solution.py:748
  34.9 2.0 %collective-permute-start.14 = (f32[16,384]{1,0:T(8,128)S(1)}, f32[16,384]{1,0:T(8,128)S(1)}, u32[]{:S(2)}, u32[]{:S(2)}) collective-permute-start(f32[16,384]{1,0:T(8,128)S(1)} %get-tuple-element.77), channel_id=1, source_target_pairs={{0,4},{4,0},{8,12},{12,8},{16,20},{20,16},{24,28},{28,24},{1,5},{5... | collective-permute-start | bytes 73736 | tf_op jit(solution)/shard_map/ppermute | solution.py:749

commit v21 on v14

--- a/solution.py
+++ b/solution.py
@@ -341,6 +341,18 @@
     return before, after
 
 
+def crossed(a, b):
+    odd = lax.rem(lax.axis_index("row"), 2) == 1
+    return jnp.where(odd, b, a), jnp.where(odd, a, b)
+
+
+def send_columns(index, a_ref, b_ref, before, after):
+    even = is_even(index)
+    a_ref[...], b_ref[...] = crossed(
+        jnp.where(even, after, before), jnp.where(even, before, after)
+    )
+
+
 def send(index, a_ref, b_ref, before, after):
     even = is_even(index)
     a_ref[...] = jnp.where(even, after, before)
@@ -362,7 +374,7 @@
     turned = packed.T
     table = table_of(core_sums(r), counts)
     table_ref[...] = table
-    send(
+    send_columns(
         lax.axis_index("col"),
         a_ref,
         b_ref,
@@ -373,7 +385,7 @@
 
 def widen_kernel(counts, both_ref, own_ref, gb_ref, ga_ref, r3_ref, h3_ref, b_ref, a_ref, table_ref):
     i, j = place()
-    from_left, from_right = sides(j, counts[1], ga_ref[:32], gb_ref[:32])
+    from_left, from_right = sides(j, counts[1], *crossed(ga_ref[:32], gb_ref[:32]))
     turned = jnp.concatenate([from_right, jnp.zeros((64, 128), jnp.float32), from_left], axis=0)
     back = turned.T
     lane = lanes_of((128, 128))
@@ -433,7 +445,7 @@
     u = column_transform(jnp.concatenate([below, above], axis=0), basis_ref)
     t = (tile_ref[...] + row_transform(u, basis_ref, halo_rows)) * weights_ref[...]
     t_ref[...] = t
-    send(j, a_ref, b_ref, *strips_of(t, basis_ref, 24))
+    send_columns(j, a_ref, b_ref, *strips_of(t, basis_ref, 24))
     table_out[...] = merged(table_ref[...], ga_ref[24:, :128], gb_ref[24:, :128])
 
 
@@ -449,7 +461,7 @@
     i, j = place()
     (ga_ref, gb_ref), refs = (refs[:2] if len(refs) == 7 else refs[1::-1]), refs[2:]
     deep = 24 if len(refs) == 5 else 16
-    y = add_columns(y_ref[...], *sides(j, counts[1], ga_ref[:deep], gb_ref[:deep]))
+    y = add_columns(y_ref[...], *sides(j, counts[1], *crossed(ga_ref[:deep], gb_ref[:deep])))
     strips = pack_rows(y, deep)
     if len(refs) == 5:
         table_ref, out_ref, table_out, b_ref, a_ref = refs
@@ -523,7 +535,7 @@
     u = u + row_transform(jnp.concatenate([w[8:32], w[48:72]], axis=0), basis_ref, edge_rows)
     t = column_transform(u, basis_ref) * weights_ref[...]
     t_ref[...] = t
-    send(j, a_ref, b_ref, *strips_of(t, basis_ref, 16))
+    send_columns(j, a_ref, b_ref, *strips_of(t, basis_ref, 16))
 
 
 def inverse_stats_kernel(t_ref, basis_ref, both_ref, m_ref, z_ref, w_ref, y_ref, stats_ref):
@@ -722,7 +734,7 @@
     even = [xor_pairs(counts, 0, 1), xor_pairs(counts, 1, 0)]
     known = meet(even[0], odd_pairs(counts, 1, 0))
     known = meet(even[1], odd_pairs(counts, 0, 0), xor_pairs(counts, 4, 0))
-    known = meet(even[0], odd_pairs(counts, 1, 1))
+    known = meet(even[0], odd_pairs(counts, 1, 2))
     return meet(even[1], odd_pairs(counts, 0, 0)).all()
 
 
@@ -734,6 +746,14 @@
     both_axes = ("row", "col")
     depth = table_shape(counts)[0]
 
+    def swap_columns(a, b, bit=0):
+        even, odd = xor_pairs(counts, 0, 1), odd_pairs(counts, 1, bit)
+        rows = [k // nc % 2 for k in range(devices)]
+        first = [(even if row else odd)[k] for k, row in enumerate(rows)]
+        second = [(odd if row else even)[k] for k, row in enumerate(rows)]
+        gb = lax.ppermute(b, both_axes, first)
+        return lax.ppermute(a, both_axes, second), gb
+
     def swap(a, b, axis, bit=0):
         gb = lax.ppermute(b, both_axes, odd_pairs(counts, both_axes.index(axis), bit))
         return lax.ppermute(a, axis, pairs_from(lax.axis_size(axis), 0)), gb
@@ -751,7 +771,7 @@
             while bit < count:
                 table = table + small_swap(table, *((0, bit) if axis else (bit, 0)))
                 bit *= 2
-    ga, gb = swap(a, b, "col")
+    ga, gb = swap_columns(a, b)
     r3, h3, b, a, table = call(
         functools.partial(widen_kernel, counts),
         [(128, 128)] * 2 + [(24 + depth, FC)] * 2 + [(depth, 128)],
@@ -786,7 +806,7 @@
         gb,
         ga,
     )
-    ga, gb = swap(*(jnp.concatenate([x, wide], axis=0) for x in (a, b)), "col", 1)
+    ga, gb = swap_columns(*(jnp.concatenate([x, wide], axis=0) for x in (a, b)), 2)
     y, table, b, a = call(
         functools.partial(columns_kernel, counts),
         [(EXT, FC), (depth, 128)] + [(24 + depth, FC)] * 2,
@@ -819,7 +839,7 @@
         weight,
         basis,
     )
-    ga, gb = swap(a, b, "col", 1)
+    ga, gb = swap_columns(a, b, 2)
     y, stats = call(inverse_stats_kernel, [(EXT, FC), (1, 128)], t, basis, both, m, z, w)
     y, b, a = call(
         functools.partial(columns_kernel, counts), [(EXT, FC)] + [(16, FC)] * 2, y, gb, ga

time: 47.7 us -> 48.7 us (1.021)
  waiting for transfers between devices: 11.1 us -> 11.8 us
  blocking collectives: 9.2 us -> 9.76 us
    ppermute x0 -> x6, starting transfers between devices: none -> 10.2 us  [the longest x3 5.48 us: swap_columns(): gb = lax.ppermute(b, both_axes, first)]
    ppermute x0 -> x6, waiting for transfers between devices: none -> 5.76 us  [the longest x3 4.06 us: swap_columns(): return (lax.ppermute(a, both_axes, second), gb)]
    ppermute x6 -> x3, starting transfers between devices: 6.37 us -> 0.78 us  [swap(): return (lax.ppermute(a, axis, pairs_from(lax.axis_size(axis), 0)), gb)]
    ppermute x6 -> x3, starting transfers between devices: 8.83 us -> 3.97 us  [swap(): lax.ppermute(b, both_axes, odd_pairs(counts, both_axes.index(axis), bit))]
    ppermute x6 -> x3, waiting for transfers between devices: 4.48 us -> 0.01 us  [swap(): return (lax.ppermute(a, axis, pairs_from(lax.axis_size(axis), 0)), gb)]
    all_to_all x1, blocking collectives: 9.2 us -> 9.76 us  [body(): stats = lax.all_to_all(stats, both_axes, 0, 0, tiled=True)]
    ppermute x6 -> x3, waiting for transfers between devices: 6.5 us -> 5.98 us  [swap(): lax.ppermute(b, both_axes, odd_pairs(counts, both_axes.index(axis), bit))]
  transfers between devices with their start and end apart: 13 -> 13, of which waited for: 8 -> 10; matrix products, arithmetic and copies ran while one was open for 0% -> 0% of each run, Pallas kernels for 9% -> 9%
where the time goes in v21:
time: 48.7 us; the launch traced here: 48.5 us
  starting transfers between devices  17.4 us (36%)
  waiting for transfers between devices  11.8 us (24%)
  blocking collectives  9.76 us (20%)
  Pallas kernels  7.87 us (16%)
  other arithmetic  1 us (2%)
  between operations  0.73 us (1%)
    all_to_all x1, blocking collectives, body(): stats = lax.all_to_all(stats, both_axes, 0, 0, tiled=True)  9.76 us
    pallas_call x14, Pallas kernels, call(): pl.pallas_call(kernel, out_shape=shapes, compiler_params=pltpu.CompilerPa...  7.87 us
    ppermute x3, waiting for transfers between devices, swap(): lax.ppermute(b, both_axes, odd_pairs(counts, both_axes.index(axis), bit))  5.98 us
    ppermute x3, starting transfers between devices, swap_columns(): gb = lax.ppermute(b, both_axes, first)  5.48 us
    ppermute x3, starting transfers between devices, swap_columns(): return (lax.ppermute(a, both_axes, second), gb)  4.7 us
    ppermute x3, waiting for transfers between devices, swap_columns(): return (lax.ppermute(a, both_axes, second), gb)  4.06 us
    ppermute x3, starting transfers between devices, swap(): lax.ppermute(b, both_axes, odd_pairs(counts, both_axes.index(axis), bit))  3.97 us
    ppermute x1, starting transfers between devices, small_swap(): return lax.ppermute(x, both_axes, xor_pairs(counts, rows, cols))  2.43 us
  transfers between devices with their start and end apart: 13, of which 10 were waited for; matrix products, arithmetic and copies ran while one was open for 0% of the time, Pallas kernels for 9%

profile of v21, /device:TPU:0, one launch (start us, length us, event | category | flops | bytes accessed | tf_op | source)
XLA Modules:
  0.0 48.5 jit_solution(6175987365100805126)
XLA Ops:
  0.6 1.0 %pad_add_fusion.both_ref = f32[256,256]{1,0:T(8,128)S(1)} fusion(f32[128,256]{1,0:T(8,128)} %param.3, f32[128,256]{1,0:T(8,128)} %param.4), kind=kLoop, calls=%fused_computation | loop fusion | flops 65536 | bytes 524288 | tf_op jit(solution)/shard_map/add | solution.py:764
  1.6 0.2 shard_map.50
  1.8 0.0 copy-start
  1.8 4.0 %collective-permute-start = (f32[40,128]{1,0:T(8,128)S(1)}, f32[40,128]{1,0:T(8,128)S(1)}, u32[]{:S(2)}, u32[]{:S(2)}) collective-permute-start(f32[40,128]{1,0:T(8,128)S(1)} %get-tuple-element.43), channel_id=1, source_target_pairs={{0,3},{1,2},{2,1},{3,0},{4,5},{5,4},{6,7},{7,6},{8,11},{9,10},{10,... | collective-permute-start | bytes 61448 | tf_op jit(solution)/shard_map/ppermute | solution.py:754
  5.8 0.5 %collective-permute-start.1 = (f32[40,128]{1,0:T(8,128)S(1)}, f32[40,128]{1,0:T(8,128)S(1)}, u32[]{:S(2)}, u32[]{:S(2)}) collective-permute-start(f32[40,128]{1,0:T(8,128)S(1)} %get-tuple-element.44), channel_id=1, source_target_pairs={{0,1},{1,0},{2,3},{3,2},{4,7},{5,6},{6,5},{7,4},{8,9},{9,8},{10,11... | collective-permute-start | bytes 61448 | tf_op jit(solution)/shard_map/ppermute | solution.py:755
  6.3 1.2 %collective-permute-done.gb_ref = f32[40,128]{1,0:T(8,128)S(1)} collective-permute-done((f32[40,128]{1,0:T(8,128)S(1)}, f32[40,128]{1,0:T(8,128)S(1)}, u32[]{:S(2)}, u32[]{:S(2)}) %collective-permute-start) | collective-permute-done | bytes 20512 | tf_op jit(solution)/shard_map/ppermute | solution.py:754
  7.5 2.0 %collective-permute-done.1.ga_ref = f32[40,128]{1,0:T(8,128)S(1)} collective-permute-done((f32[40,128]{1,0:T(8,128)S(1)}, f32[40,128]{1,0:T(8,128)S(1)}, u32[]{:S(2)}, u32[]{:S(2)}) %collective-permute-start.1) | collective-permute-done | bytes 20512 | tf_op jit(solution)/shard_map/ppermute | solution.py:755
  9.5 0.2 shard_map.51
  9.8 2.0 %collective-permute-start.2 = (f32[32,384]{1,0:T(8,128)S(1)}, f32[32,384]{1,0:T(8,128)S(1)}, u32[]{:S(2)}, u32[]{:S(2)}) collective-permute-start(f32[32,384]{1,0:T(8,128)S(1)} %get-tuple-element.45), channel_id=1, source_target_pairs={{0,28},{1,29},{2,30},{3,31},{4,8},{5,9},{6,10},{7,11},{8,4},{9,5},... | collective-permute-start | bytes 147464 | tf_op jit(solution)/shard_map/ppermute | solution.py:758
  11.7 0.0 collective-permute-start.3
  11.7 0.0 copy-done
  11.7 0.1 shard_map.53
  11.9 2.4 %collective-permute-start.4 = (f32[8,128]{1,0:T(8,128)S(1)}, f32[8,128]{1,0:T(8,128)S(1)}, u32[]{:S(2)}, u32[]{:S(2)}) collective-permute-start(f32[8,128]{1,0:T(8,128)S(1)} %get-tuple-element.50.table_ref), channel_id=1, source_target_pairs={{0,16},{1,17},{2,18},{3,19},{4,20},{5,21},{6,22},{7,23},{8,24},{9,... | collective-permute-start | bytes 12296 | tf_op jit(solution)/shard_map/ppermute | solution.py:762
  14.3 0.6 %shard_map.52.tile_ref = f32[144,512]{1,0:T(8,128)S(1)} custom-call(f32[256,256]{1,0:T(8,128)S(1)} %pad_add_fusion.both_ref, f32[128,128]{1,0:T(8,128)S(1)} %get-tuple-element.47.r3_ref, f32[1104,512]{1,0:T(8,128)S(1)} %copy-done), custom_call_target="tpu_custom_call" | custom-call | flops 1000000000 | bytes 1000000 | tf_op jit(solution)/shard_map/pallas_call | solution.py:695
  14.9 0.5 %collective-permute-done.2.gb_ref = f32[32,384]{1,0:T(8,128)S(1)} collective-permute-done((f32[32,384]{1,0:T(8,128)S(1)}, f32[32,384]{1,0:T(8,128)S(1)}, u32[]{:S(2)}, u32[]{:S(2)}) %collective-permute-start.2) | collective-permute-done | bytes 49184 | tf_op jit(solution)/shard_map/ppermute | solution.py:758
  15.4 0.0 collective-permute-done.3.ga_ref
  15.4 1.0 %shard_map.54 = (f32[144,512]{1,0:T(8,128)S(1)}, f32[8,128]{1,0:T(8,128)S(1)}, f32[24,144]{1,0:T(8,128)S(1)}, f32[24,144]{1,0:T(8,128)S(1)}) custom-call(f32[32,384]{1,0:T(8,128)S(1)} %collective-permute-done.2.gb_ref, f32[32,384]{1,0:T(8,128)S(1)} %collective-permute-done.3.ga_ref, f32[144,512]{1,0:T(8,128)S(1)} %shard_map.52.tile_ref, ...), custom_call_target="tpu_custom_call" | custom-call | flops 1000000000 | bytes 1000000 | tf_op jit(solution)/shard_map/pallas_call | solution.py:695
  16.4 0.1 collective-permute-done.4
  16.5 1.4 %collective-permute-start.6 = (f32[32,144]{1,0:T(8,128)S(1)}, f32[32,144]{1,0:T(8,128)S(1)}, u32[]{:S(2)}, u32[]{:S(2)}) collective-permute-start(f32[32,144]{1,0:T(8,128)S(1)} %get-tuple-element.82), channel_id=1, source_target_pairs={{0,8},{1,2},{2,1},{3,11},{4,5},{5,4},{6,7},{7,6},{8,0},{9,10},{10,... | collective-permute-start | bytes 55304 | tf_op jit(solution)/shard_map/ppermute | solution.py:754
  17.9 1.6 %collective-permute-start.5 = (f32[32,144]{1,0:T(8,128)S(1)}, f32[32,144]{1,0:T(8,128)S(1)}, u32[]{:S(2)}, u32[]{:S(2)}) collective-permute-start(f32[32,144]{1,0:T(8,128)S(1)} %get-tuple-element.83), channel_id=1, source_target_pairs={{0,1},{1,0},{2,3},{3,2},{4,12},{5,6},{6,5},{7,15},{8,9},{9,8},{10,... | collective-permute-start | bytes 55304 | tf_op jit(solution)/shard_map/ppermute | solution.py:755
  19.5 0.8 %shard_map.55 = (f32[144,384]{1,0:T(8,128)S(1)}, f32[160,384]{1,0:T(8,128)S(1)}) custom-call(f32[144,512]{1,0:T(8,128)S(1)} %get-tuple-element.51.t_ref, f32[1104,512]{1,0:T(8,128)S(1)} %copy-done, f32[256,256]{1,0:T(8,128)S(1)} %pad_add_fusion.both_ref, f32[128,128]{1,0:T(8,128)S(1)} %get-tuple-element.52.h3_ref, ...), custom_call_target="tpu_custom_call" | custom-call | flops 1000000000 | bytes 1000000 | tf_op jit(solution)/shard_map/pallas_call | solution.py:695
  20.4 0.1 collective-permute-done.6.refs_1_
  20.5 1.3 %collective-permute-done.5.refs_0_ = f32[32,144]{1,0:T(8,128)S(1)} collective-permute-done((f32[32,144]{1,0:T(8,128)S(1)}, f32[32,144]{1,0:T(8,128)S(1)}, u32[]{:S(2)}, u32[]{:S(2)}) %collective-permute-start.5) | collective-permute-done | bytes 18464 | tf_op jit(solution)/shard_map/ppermute | solution.py:755
  21.8 0.2 shard_map.56
  22.0 0.1 collective-permute-start.7
  22.1 0.8 %collective-permute-start.8 = (f32[32,384]{1,0:T(8,128)S(1)}, f32[32,384]{1,0:T(8,128)S(1)}, u32[]{:S(2)}, u32[]{:S(2)}) collective-permute-start(f32[32,384]{1,0:T(8,128)S(1)} %get-tuple-element.60), channel_id=1, source_target_pairs={{0,4},{4,0},{8,12},{12,8},{16,20},{20,16},{24,28},{28,24},{1,5},{5... | collective-permute-start | bytes 147464 | tf_op jit(solution)/shard_map/ppermute | solution.py:759
  22.8 0.7 %shard_map.57 = (f32[96,256]{1,0:T(8,128)S(1)}, f32[96,256]{1,0:T(8,128)S(1)}, f32[144,384]{1,0:T(8,128)S(1)}, f32[144,384]{1,0:T(8,128)S(1)}, f32[16,128]{1,0:T(8,128)S(1)}) custom-call(f32[144,384]{1,0:T(8,128)S(1)} %get-tuple-element.57.y_ref, f32[160,384]{1,0:T(8,128)S(1)} %get-tuple-element.58.m_ref, f32[1104,512]{1,0:T(8,128)S(1)} %copy-done), custom_call_target="tpu_custom_call" | custom-call | flops 1000000000 | bytes 1000000 | tf_op jit(solution)/shard_map/pallas_call | solution.py:695
  23.5 3.9 %collective-permute-done.7.gb_ref = f32[32,384]{1,0:T(8,128)S(1)} collective-permute-done((f32[32,384]{1,0:T(8,128)S(1)}, f32[32,384]{1,0:T(8,128)S(1)}, u32[]{:S(2)}, u32[]{:S(2)}) %collective-permute-start.7) | collective-permute-done | bytes 49184 | tf_op jit(solution)/shard_map/ppermute | solution.py:758
  27.4 0.0 collective-permute-done.8.ga_ref
  27.4 1.3 %shard_map.58 = (f32[128,256]{1,0:T(8,128)S(1)}, f32[128,256]{1,0:T(8,128)S(1)}, f32[144,512]{1,0:T(8,128)S(1)}, f32[16,144]{1,0:T(8,128)S(1)}, f32[16,144]{1,0:T(8,128)S(1)}) custom-call(f32[144,384]{1,0:T(8,128)S(1)} %get-tuple-element.57.y_ref, f32[160,384]{1,0:T(8,128)S(1)} %get-tuple-element.58.m_ref, f32[32,384]{1,0:T(8,128)S(1)} %collective-permute-done.7.gb_ref, ...), custom_call_target="tpu_custom_call" | custom-call | flops 1000000000 | bytes 1000000 | tf_op jit(solution)/shard_map/pallas_call | solution.py:695
  28.6 0.1 collective-permute-start.9
  28.7 2.5 %collective-permute-start.10 = (f32[16,144]{1,0:T(8,128)S(1)}, f32[16,144]{1,0:T(8,128)S(1)}, u32[]{:S(2)}, u32[]{:S(2)}) collective-permute-start(f32[16,144]{1,0:T(8,128)S(1)} %get-tuple-element.72), channel_id=1, source_target_pairs={{0,1},{1,0},{2,3},{3,2},{4,12},{5,6},{6,5},{7,15},{8,9},{9,8},{10,... | collective-permute-start | bytes 27656 | tf_op jit(solution)/shard_map/ppermute | solution.py:755
  31.3 0.8 %shard_map.59 = (f32[144,384]{1,0:T(8,128)S(1)}, f32[1,128]{1,0:T(1,128)S(1)}) custom-call(f32[144,512]{1,0:T(8,128)S(1)} %get-tuple-element.67.t_ref, f32[1104,512]{1,0:T(8,128)S(1)} %copy-done, f32[256,256]{1,0:T(8,128)S(1)} %pad_add_fusion.both_ref, f32[160,384]{1,0:T(8,128)S(1)} %get-tuple-element.58.m_ref, f32[128,256]{1,0:T(8,128)S(1)} %get-tuple-element.68.z_ref, ...), custom_call_target="tpu_custom_call" | custom-call | flops 1000000000 | bytes 1000000 | tf_op jit(solution)/shard_map/pallas_call | solution.py:695
  32.1 0.4 collective-permute-done.9.refs_0_
  32.5 0.7 %collective-permute-done.10.refs_1_ = f32[16,144]{1,0:T(8,128)S(1)} collective-permute-done((f32[16,144]{1,0:T(8,128)S(1)}, f32[16,144]{1,0:T(8,128)S(1)}, u32[]{:S(2)}, u32[]{:S(2)}) %collective-permute-start.10) | collective-permute-done | bytes 9248 | tf_op jit(solution)/shard_map/ppermute | solution.py:755
  33.2 0.2 shard_map.60
  33.3 1.9 %collective-permute-start.11 = (f32[16,384]{1,0:T(8,128)S(1)}, f32[16,384]{1,0:T(8,128)S(1)}, u32[]{:S(2)}, u32[]{:S(2)}) collective-permute-start(f32[16,384]{1,0:T(8,128)S(1)} %get-tuple-element.74), channel_id=1, source_target_pairs={{0,1},{1,0},{2,3},{3,2},{4,8},{5,9},{6,10},{7,11},{8,4},{9,5},{10,... | collective-permute-start | bytes 73736 | tf_op jit(solution)/shard_map/ppermute | solution.py:758
  35.3 0.0 collective-permute-start.12
  35.3 0.4 shard_map.61
  35.6 1.6 %collective-permute-done.11.gb_ref = f32[16,384]{1,0:T(8,128)S(1)} collective-permute-done((f32[16,384]{1,0:T(8,128)S(1)}, f32[16,384]{1,0:T(8,128)S(1)}, u32[]{:S(2)}, u32[]{:S(2)}) %collective-permute-start.11) | collective-permute-done | bytes 24608 | tf_op jit(solution)/shard_map/ppermute | solution.py:758
  37.2 0.0 collective-permute-done.12.ga_ref
  37.2 0.3 shard_map.62
  37.5 9.8 %all_to_all.11 = f32[32,1,128]{2,1,0:T(1,128)S(1)} all-to-all(f32[32,1,128]{2,1,0:T(1,128)S(1)} %bitcast.5), channel_id=1, replica_groups=mesh['row'=8,'col'=4] {'row','col'}, dimensions={0} | all-to-all | bytes 32768 | tf_op jit(solution)/shard_map/all_to_all | solution.py:869
  47.3 1.3 %shard_map.63 = (f32[128,256]{1,0:T(8,128)}, f32[128,256]{1,0:T(8,128)}) custom-call(f32[32,128]{1,0:T(8,128)S(1)} %bitcast.4, f32[1104,512]{1,0:T(8,128)S(1)} %copy-done, f32[160,384]{1,0:T(8,128)S(1)} %get-tuple-element.58.m_ref, f32[96,256]{1,0:T(8,128)S(1)} %get-tuple-element.63.f_ref, f32[256,256]{1,0:T(8,128)S(1)} %pad_add_fusion.both_ref, ...), custom_call_target="tpu_custom_call" | custom-call | flops 1000000000 | bytes 1000000 | tf_op jit(solution)/shard_map/pallas_call | solution.py:695
  (2 shorter events, 0.0 us)
Async XLA Ops:
  1.8 9.9 %copy-start = (f32[1104,512]{1,0:T(8,128)S(1)}, f32[1104,512]{1,0:T(8,128)}, u32[]{:S(2)}) copy-start(f32[1104,512]{1,0:T(8,128)} %constant.6.clone.basis_ref) | copy-start | bytes 6782980
  1.8 5.7 %collective-permute-start = (f32[40,128]{1,0:T(8,128)S(1)}, f32[40,128]{1,0:T(8,128)S(1)}, u32[]{:S(2)}, u32[]{:S(2)}) collective-permute-start(f32[40,128]{1,0:T(8,128)S(1)} %get-tuple-element.43), channel_id=1, source_target_pairs={{0,3},{1,2},{2,1},{3,0},{4,5},{5,4},{6,7},{7,6},{8,11},{9,10},{10,... | collective-permute-start | bytes 61448 | tf_op jit(solution)/shard_map/ppermute | solution.py:754
  5.8 3.8 %collective-permute-start.1 = (f32[40,128]{1,0:T(8,128)S(1)}, f32[40,128]{1,0:T(8,128)S(1)}, u32[]{:S(2)}, u32[]{:S(2)}) collective-permute-start(f32[40,128]{1,0:T(8,128)S(1)} %get-tuple-element.44), channel_id=1, source_target_pairs={{0,1},{1,0},{2,3},{3,2},{4,7},{5,6},{6,5},{7,4},{8,9},{9,8},{10,11... | collective-permute-start | bytes 61448 | tf_op jit(solution)/shard_map/ppermute | solution.py:755
  9.8 5.6 %collective-permute-start.2 = (f32[32,384]{1,0:T(8,128)S(1)}, f32[32,384]{1,0:T(8,128)S(1)}, u32[]{:S(2)}, u32[]{:S(2)}) collective-permute-start(f32[32,384]{1,0:T(8,128)S(1)} %get-tuple-element.45), channel_id=1, source_target_pairs={{0,28},{1,29},{2,30},{3,31},{4,8},{5,9},{6,10},{7,11},{8,4},{9,5},... | collective-permute-start | bytes 147464 | tf_op jit(solution)/shard_map/ppermute | solution.py:758
  11.7 3.7 %collective-permute-start.3 = (f32[32,384]{1,0:T(8,128)S(1)}, f32[32,384]{1,0:T(8,128)S(1)}, u32[]{:S(2)}, u32[]{:S(2)}) collective-permute-start(f32[32,384]{1,0:T(8,128)S(1)} %get-tuple-element.46), channel_id=1, source_target_pairs={{0,4},{4,0},{8,12},{12,8},{16,20},{20,16},{24,28},{28,24},{1,5},{5... | collective-permute-start | bytes 147464 | tf_op jit(solution)/shard_map/ppermute | solution.py:759
  11.9 4.6 %collective-permute-start.4 = (f32[8,128]{1,0:T(8,128)S(1)}, f32[8,128]{1,0:T(8,128)S(1)}, u32[]{:S(2)}, u32[]{:S(2)}) collective-permute-start(f32[8,128]{1,0:T(8,128)S(1)} %get-tuple-element.50.table_ref), channel_id=1, source_target_pairs={{0,16},{1,17},{2,18},{3,19},{4,20},{5,21},{6,22},{7,23},{8,24},{9,... | collective-permute-start | bytes 12296 | tf_op jit(solution)/shard_map/ppermute | solution.py:762
  16.5 4.0 %collective-permute-start.6 = (f32[32,144]{1,0:T(8,128)S(1)}, f32[32,144]{1,0:T(8,128)S(1)}, u32[]{:S(2)}, u32[]{:S(2)}) collective-permute-start(f32[32,144]{1,0:T(8,128)S(1)} %get-tuple-element.82), channel_id=1, source_target_pairs={{0,8},{1,2},{2,1},{3,11},{4,5},{5,4},{6,7},{7,6},{8,0},{9,10},{10,... | collective-permute-start | bytes 55304 | tf_op jit(solution)/shard_map/ppermute | solution.py:754
  17.9 3.9 %collective-permute-start.5 = (f32[32,144]{1,0:T(8,128)S(1)}, f32[32,144]{1,0:T(8,128)S(1)}, u32[]{:S(2)}, u32[]{:S(2)}) collective-permute-start(f32[32,144]{1,0:T(8,128)S(1)} %get-tuple-element.83), channel_id=1, source_target_pairs={{0,1},{1,0},{2,3},{3,2},{4,12},{5,6},{6,5},{7,15},{8,9},{9,8},{10,... | collective-permute-start | bytes 55304 | tf_op jit(solution)/shard_map/ppermute | solution.py:755
  22.0 5.4 %collective-permute-start.7 = (f32[32,384]{1,0:T(8,128)S(1)}, f32[32,384]{1,0:T(8,128)S(1)}, u32[]{:S(2)}, u32[]{:S(2)}) collective-permute-start(f32[32,384]{1,0:T(8,128)S(1)} %get-tuple-element.59), channel_id=1, source_target_pairs={{0,28},{1,29},{2,30},{3,31},{4,8},{5,9},{6,10},{7,11},{8,4},{9,5},... | collective-permute-start | bytes 147464 | tf_op jit(solution)/shard_map/ppermute | solution.py:758
  22.1 5.3 %collective-permute-start.8 = (f32[32,384]{1,0:T(8,128)S(1)}, f32[32,384]{1,0:T(8,128)S(1)}, u32[]{:S(2)}, u32[]{:S(2)}) collective-permute-start(f32[32,384]{1,0:T(8,128)S(1)} %get-tuple-element.60), channel_id=1, source_target_pairs={{0,4},{4,0},{8,12},{12,8},{16,20},{20,16},{24,28},{28,24},{1,5},{5... | collective-permute-start | bytes 147464 | tf_op jit(solution)/shard_map/ppermute | solution.py:759
  28.6 3.8 %collective-permute-start.9 = (f32[16,144]{1,0:T(8,128)S(1)}, f32[16,144]{1,0:T(8,128)S(1)}, u32[]{:S(2)}, u32[]{:S(2)}) collective-permute-start(f32[16,144]{1,0:T(8,128)S(1)} %get-tuple-element.71), channel_id=1, source_target_pairs={{0,8},{1,2},{2,1},{3,11},{4,5},{5,4},{6,7},{7,6},{8,0},{9,10},{10,... | collective-permute-start | bytes 27656 | tf_op jit(solution)/shard_map/ppermute | solution.py:754
  28.7 4.4 %collective-permute-start.10 = (f32[16,144]{1,0:T(8,128)S(1)}, f32[16,144]{1,0:T(8,128)S(1)}, u32[]{:S(2)}, u32[]{:S(2)}) collective-permute-start(f32[16,144]{1,0:T(8,128)S(1)} %get-tuple-element.72), channel_id=1, source_target_pairs={{0,1},{1,0},{2,3},{3,2},{4,12},{5,6},{6,5},{7,15},{8,9},{9,8},{10,... | collective-permute-start | bytes 27656 | tf_op jit(solution)/shard_map/ppermute | solution.py:755
  33.3 3.9 %collective-permute-start.11 = (f32[16,384]{1,0:T(8,128)S(1)}, f32[16,384]{1,0:T(8,128)S(1)}, u32[]{:S(2)}, u32[]{:S(2)}) collective-permute-start(f32[16,384]{1,0:T(8,128)S(1)} %get-tuple-element.74), channel_id=1, source_target_pairs={{0,1},{1,0},{2,3},{3,2},{4,8},{5,9},{6,10},{7,11},{8,4},{9,5},{10,... | collective-permute-start | bytes 73736 | tf_op jit(solution)/shard_map/ppermute | solution.py:758
  35.3 2.0 %collective-permute-start.12 = (f32[16,384]{1,0:T(8,128)S(1)}, f32[16,384]{1,0:T(8,128)S(1)}, u32[]{:S(2)}, u32[]{:S(2)}) collective-permute-start(f32[16,384]{1,0:T(8,128)S(1)} %get-tuple-element.75), channel_id=1, source_target_pairs={{0,4},{4,0},{8,12},{12,8},{16,20},{20,16},{24,28},{28,24},{1,5},{5... | collective-permute-start | bytes 73736 | tf_op jit(solution)/shard_map/ppermute | solution.py:759

commit v22 on v14

--- a/solution.py
+++ b/solution.py
@@ -486,8 +486,6 @@
     gb_ref,
     ga_ref,
     table_ref,
-    inner_w_ref,
-    f_ref,
     gw_ref,
     gf_ref,
     near_ref,
@@ -495,6 +493,7 @@
     basis_ref,
     z_ref,
     w_ref,
+    band_ref,
     t_ref,
     b_ref,
     a_ref,
@@ -514,8 +513,9 @@
     w = jnp.where(mask, DAMP * z + lap(flow), 0.0) * SHRINK
     step = jumps(bands[1])
     damped = (DAMP * SHRINK) * bands[1]
-    z_ref[...] = with_edges(z, y[16:112, :TC] + bands[1][:, :TC])
-    w_ref[...] = with_edges(w, inner_w_ref[...] + step[:, :TC] * f_ref[...] + damped[:, :TC])
+    z_ref[...] = jnp.concatenate([z[16:32, :TC], z[48:64, :TC]], axis=0)
+    w_ref[...] = jnp.concatenate([w[16:32, :TC], w[48:64, :TC]], axis=0)
+    band_ref[...] = jnp.concatenate([bands[1], step, damped, jnp.zeros((5, FC), jnp.float32)], axis=0)
     lane = lanes_of((EXT, 256))
     ones = jnp.where((lane >= 16) & (lane < 112), rows_t_part(basis_ref), 0.0)
     ones = jnp.sum(ones, axis=1, keepdims=True)
@@ -526,7 +526,29 @@
     send(j, a_ref, b_ref, *strips_of(t, basis_ref, 16))
 
 
-def inverse_stats_kernel(t_ref, basis_ref, both_ref, m_ref, z_ref, w_ref, y_ref, stats_ref):
+def tile_of(edge, inner):
+    return jnp.concatenate([edge[:16], inner, edge[16:]], axis=0)
+
+
+def inverse_stats_kernel(
+    t_ref,
+    basis_ref,
+    both_ref,
+    m_ref,
+    first_ref,
+    inner_w_ref,
+    f_ref,
+    edge_z_ref,
+    edge_w_ref,
+    band_ref,
+    y_ref,
+    stats_ref,
+    z_ref,
+    w_ref,
+):
+    on, step, damped = (band_ref[k : k + 1, :TC] for k in range(3))
+    z_ref[...] = tile_of(edge_z_ref, first_ref[16:112, :TC] + on)
+    w_ref[...] = tile_of(edge_w_ref, inner_w_ref[...] + step * f_ref[...] + damped)
     y_ref[...] = solution_of(t_ref[...], basis_ref)
     rt, mt, zt, wt = both_ref[:TR], m_ref[:TR, :TC], z_ref[...], w_ref[...]
     lane, row = lanes_of((1, 256)), rows_of((128, 1))
@@ -577,16 +599,16 @@
 
 
 def dots_kernel(
-    counts, y_ref, m_ref, gb_ref, ga_ref, both_ref, w_ref, stats_ref, inner_v_ref, q_ref, v_ref, stats_out
+    counts, y_ref, m_ref, gb_ref, ga_ref, both_ref, w_ref, stats_ref, q_ref, v_ref, stats_out
 ):
     i, j = place()
     y = y_ref[...]
     q = edges(y, *sides(i, counts[0], ga_ref[...], gb_ref[...]))
     q = jnp.where(edge_mask(counts), q, 0.0)
     v = DAMP * q + lap(edge_part(m_ref) * lap(q))
-    q_ref[...] = with_edges(q, y[16:112, :TC])
-    v_ref[...] = with_edges(v, inner_v_ref[...])
     qe, ve = (jnp.concatenate([x[16:32, :TC], x[48:64, :TC]], axis=0) for x in (q, v))
+    q_ref[...] = qe
+    v_ref[...] = ve
     re = jnp.concatenate([both_ref[:16], both_ref[112:128]], axis=0)
     we = jnp.concatenate([w_ref[:16], w_ref[112:]], axis=0)
     rest = [core_sums(ve), core_sums(re * qe), core_sums(we * qe), core_sums(ve * qe)]
@@ -605,6 +627,8 @@
     both_ref,
     z_ref,
     w_ref,
+    y_ref,
+    inner_v_ref,
     q_ref,
     v_ref,
     solution_ref,
@@ -671,8 +695,8 @@
     coarse = edge_bands(bands)
     image = DAMP * coarse + lap(edge_part(m_ref) * lap(coarse))
     image = with_edges(image, (jumps(bands[1]) * (1.0 / SHRINK))[:, :TC] * f_ref[...] + DAMP * on)
-    y = q_ref[...] + on
-    v = v_ref[...] + image
+    y = tile_of(q_ref, y_ref[16:112, :TC]) + on
+    v = tile_of(v_ref, inner_v_ref[...]) + image
     z, w = z_ref[...], w_ref[...]
     solution_ref[...] = (a * SHRINK) * z + a1 * (beta1 * z - a * y)
     residual_ref[...] = both_ref[:TR] - a * w - a1 * ((beta1 * (1.0 / SHRINK)) * w - a * v)
@@ -803,16 +827,14 @@
         m,
         basis,
     )
-    z, w, t, b, a = call(
+    edge_z, edge_w, band, t, b, a = call(
         functools.partial(second_kernel, counts, width),
-        [(TR, TC)] * 2 + [(EXT, 2 * SPEC)] + [(16, EXT)] * 2,
+        [(32, TC)] * 2 + [(8, FC), (EXT, 2 * SPEC)] + [(16, EXT)] * 2,
         y,
         m,
         gb,
         ga,
         table,
-        inner_w,
-        f,
         gw,
         gf,
         near,
@@ -820,7 +842,20 @@
         basis,
     )
     ga, gb = swap(a, b, "col", 1)
-    y, stats = call(inverse_stats_kernel, [(EXT, FC), (1, 128)], t, basis, both, m, z, w)
+    y, stats, z, w = call(
+        inverse_stats_kernel,
+        [(EXT, FC), (1, 128)] + [(TR, TC)] * 2,
+        t,
+        basis,
+        both,
+        m,
+        y,
+        inner_w,
+        f,
+        edge_z,
+        edge_w,
+        band,
+    )
     y, b, a = call(
         functools.partial(columns_kernel, counts), [(EXT, FC)] + [(16, FC)] * 2, y, gb, ga
     )
@@ -836,7 +871,7 @@
     )
     q, v, stats = call(
         functools.partial(dots_kernel, counts),
-        [(TR, TC)] * 2 + [(devices, 128)],
+        [(32, TC)] * 2 + [(devices, 128)],
         y,
         m,
         gb,
@@ -844,7 +879,6 @@
         both,
         w,
         stats,
-        inner_v,
     )
     stats = lax.all_to_all(stats, both_axes, 0, 0, tiled=True)
     return tuple(
@@ -858,6 +892,8 @@
             both,
             z,
             w,
+            y,
+            inner_v,
             q,
             v,
         )

time: 47.7 us -> 47.6 us (level)
  no operation moved by 1% of the time
where the time goes in v22:
time: 47.6 us; the launch traced here: 47.5 us
  starting transfers between devices  17.6 us (37%)
  waiting for transfers between devices  11 us (23%)
  blocking collectives  9.2 us (19%)
  Pallas kernels  7.86 us (17%)
  other arithmetic  1 us (2%)
  between operations  0.75 us (2%)
    all_to_all x1, blocking collectives, body(): stats = lax.all_to_all(stats, both_axes, 0, 0, tiled=True)  9.2 us
    ppermute x6, starting transfers between devices, swap(): lax.ppermute(b, both_axes, odd_pairs(counts, both_axes.index(axis), bit))  8.84 us
    pallas_call x14, Pallas kernels, call(): pl.pallas_call(kernel, out_shape=shapes, compiler_params=pltpu.CompilerPa...  7.86 us
    ppermute x6, waiting for transfers between devices, swap(): lax.ppermute(b, both_axes, odd_pairs(counts, both_axes.index(axis), bit))  6.5 us
    ppermute x6, starting transfers between devices, swap(): return (lax.ppermute(a, axis, pairs_from(lax.axis_size(axis), 0)), gb)  6.36 us
    ppermute x6, waiting for transfers between devices, swap(): return (lax.ppermute(a, axis, pairs_from(lax.axis_size(axis), 0)), gb)  4.47 us
    ppermute x1, starting transfers between devices, small_swap(): return lax.ppermute(x, both_axes, xor_pairs(counts, rows, cols))  2.43 us
    add x1, other arithmetic, body(): jnp.pad(noise, ((0, TR), (0, 0))) + jnp.pad(height, ((TR, 0), (0, 0)))  0.99 us
  transfers between devices with their start and end apart: 13, of which 8 were waited for; matrix products, arithmetic and copies ran while one was open for 0% of the time, Pallas kernels for 9%

profile of v22, /device:TPU:0, one launch (start us, length us, event | category | flops | bytes accessed | tf_op | source)
XLA Modules:
  0.0 47.5 jit_solution(1947500913178614113)
XLA Ops:
  0.6 1.0 %pad_add_fusion.both_ref = f32[256,256]{1,0:T(8,128)S(1)} fusion(f32[128,256]{1,0:T(8,128)} %param.3, f32[128,256]{1,0:T(8,128)} %param.4), kind=kLoop, calls=%fused_computation | loop fusion | flops 65536 | bytes 524288 | tf_op jit(solution)/shard_map/add | solution.py:768
  1.6 0.2 shard_map.50
  1.8 0.0 copy-start
  1.8 4.0 %collective-permute-start = (f32[40,128]{1,0:T(8,128)S(1)}, f32[40,128]{1,0:T(8,128)S(1)}, u32[]{:S(2)}, u32[]{:S(2)}) collective-permute-start(f32[40,128]{1,0:T(8,128)S(1)} %get-tuple-element.46), channel_id=1, source_target_pairs={{0,3},{1,2},{2,1},{3,0},{4,7},{5,6},{6,5},{7,4},{8,11},{9,10},{10,... | collective-permute-start | bytes 61448 | tf_op jit(solution)/shard_map/ppermute | solution.py:762
  5.8 0.5 %collective-permute-start.1 = (f32[40,128]{1,0:T(8,128)S(1)}, f32[40,128]{1,0:T(8,128)S(1)}, u32[]{:S(2)}, u32[]{:S(2)}) collective-permute-start(f32[40,128]{1,0:T(8,128)S(1)} %get-tuple-element.47), channel_id=1, source_target_pairs={{0,1},{1,0},{2,3},{3,2},{4,5},{5,4},{6,7},{7,6},{8,9},{9,8},{10,11... | collective-permute-start | bytes 61448 | tf_op jit(solution)/shard_map/ppermute | solution.py:763
  6.3 1.2 %collective-permute-done.gb_ref = f32[40,128]{1,0:T(8,128)S(1)} collective-permute-done((f32[40,128]{1,0:T(8,128)S(1)}, f32[40,128]{1,0:T(8,128)S(1)}, u32[]{:S(2)}, u32[]{:S(2)}) %collective-permute-start) | collective-permute-done | bytes 20512 | tf_op jit(solution)/shard_map/ppermute | solution.py:762
  7.5 2.0 %collective-permute-done.1.ga_ref = f32[40,128]{1,0:T(8,128)S(1)} collective-permute-done((f32[40,128]{1,0:T(8,128)S(1)}, f32[40,128]{1,0:T(8,128)S(1)}, u32[]{:S(2)}, u32[]{:S(2)}) %collective-permute-start.1) | collective-permute-done | bytes 20512 | tf_op jit(solution)/shard_map/ppermute | solution.py:763
  9.5 0.2 shard_map.51
  9.7 2.0 %collective-permute-start.2 = (f32[32,384]{1,0:T(8,128)S(1)}, f32[32,384]{1,0:T(8,128)S(1)}, u32[]{:S(2)}, u32[]{:S(2)}) collective-permute-start(f32[32,384]{1,0:T(8,128)S(1)} %get-tuple-element.48), channel_id=1, source_target_pairs={{0,28},{1,29},{2,30},{3,31},{4,8},{5,9},{6,10},{7,11},{8,4},{9,5},... | collective-permute-start | bytes 147464 | tf_op jit(solution)/shard_map/ppermute | solution.py:762
  11.7 0.0 collective-permute-start.3
  11.7 0.0 copy-done
  11.7 0.1 shard_map.53
  11.9 2.4 %collective-permute-start.4 = (f32[8,128]{1,0:T(8,128)S(1)}, f32[8,128]{1,0:T(8,128)S(1)}, u32[]{:S(2)}, u32[]{:S(2)}) collective-permute-start(f32[8,128]{1,0:T(8,128)S(1)} %get-tuple-element.53.table_ref), channel_id=1, source_target_pairs={{0,16},{1,17},{2,18},{3,19},{4,20},{5,21},{6,22},{7,23},{8,24},{9,... | collective-permute-start | bytes 12296 | tf_op jit(solution)/shard_map/ppermute | solution.py:766
  14.3 0.6 %shard_map.52.tile_ref = f32[144,512]{1,0:T(8,128)S(1)} custom-call(f32[256,256]{1,0:T(8,128)S(1)} %pad_add_fusion.both_ref, f32[128,128]{1,0:T(8,128)S(1)} %get-tuple-element.50.r3_ref, f32[1104,512]{1,0:T(8,128)S(1)} %copy-done), custom_call_target="tpu_custom_call" | custom-call | flops 1000000000 | bytes 1000000 | tf_op jit(solution)/shard_map/pallas_call | solution.py:707
  14.9 0.5 %collective-permute-done.2.gb_ref = f32[32,384]{1,0:T(8,128)S(1)} collective-permute-done((f32[32,384]{1,0:T(8,128)S(1)}, f32[32,384]{1,0:T(8,128)S(1)}, u32[]{:S(2)}, u32[]{:S(2)}) %collective-permute-start.2) | collective-permute-done | bytes 49184 | tf_op jit(solution)/shard_map/ppermute | solution.py:762
  15.4 0.0 collective-permute-done.3.ga_ref
  15.4 1.0 %shard_map.54 = (f32[144,512]{1,0:T(8,128)S(1)}, f32[8,128]{1,0:T(8,128)S(1)}, f32[24,144]{1,0:T(8,128)S(1)}, f32[24,144]{1,0:T(8,128)S(1)}) custom-call(f32[32,384]{1,0:T(8,128)S(1)} %collective-permute-done.2.gb_ref, f32[32,384]{1,0:T(8,128)S(1)} %collective-permute-done.3.ga_ref, f32[144,512]{1,0:T(8,128)S(1)} %shard_map.52.tile_ref, ...), custom_call_target="tpu_custom_call" | custom-call | flops 1000000000 | bytes 1000000 | tf_op jit(solution)/shard_map/pallas_call | solution.py:707
  16.4 0.1 collective-permute-done.4
  16.5 0.1 collective-permute-start.6
  16.6 1.9 %collective-permute-start.5 = (f32[32,144]{1,0:T(8,128)S(1)}, f32[32,144]{1,0:T(8,128)S(1)}, u32[]{:S(2)}, u32[]{:S(2)}) collective-permute-start(f32[32,144]{1,0:T(8,128)S(1)} %get-tuple-element.89), channel_id=1, source_target_pairs={{0,1},{1,0},{2,3},{3,2},{4,5},{5,4},{6,7},{7,6},{8,9},{9,8},{10,11... | collective-permute-start | bytes 55304 | tf_op jit(solution)/shard_map/ppermute | solution.py:763
  18.5 0.8 %shard_map.55 = (f32[144,384]{1,0:T(8,128)S(1)}, f32[160,384]{1,0:T(8,128)S(1)}) custom-call(f32[144,512]{1,0:T(8,128)S(1)} %get-tuple-element.54.t_ref, f32[1104,512]{1,0:T(8,128)S(1)} %copy-done, f32[256,256]{1,0:T(8,128)S(1)} %pad_add_fusion.both_ref, f32[128,128]{1,0:T(8,128)S(1)} %get-tuple-element.55.h3_ref, ...), custom_call_target="tpu_custom_call" | custom-call | flops 1000000000 | bytes 1000000 | tf_op jit(solution)/shard_map/pallas_call | solution.py:707
  19.3 0.0 collective-permute-done.6.refs_1_
  19.3 1.4 %collective-permute-done.5.refs_0_ = f32[32,144]{1,0:T(8,128)S(1)} collective-permute-done((f32[32,144]{1,0:T(8,128)S(1)}, f32[32,144]{1,0:T(8,128)S(1)}, u32[]{:S(2)}, u32[]{:S(2)}) %collective-permute-start.5) | collective-permute-done | bytes 18464 | tf_op jit(solution)/shard_map/ppermute | solution.py:763
  20.7 0.2 shard_map.56
  20.9 0.8 %collective-permute-start.7 = (f32[32,384]{1,0:T(8,128)S(1)}, f32[32,384]{1,0:T(8,128)S(1)}, u32[]{:S(2)}, u32[]{:S(2)}) collective-permute-start(f32[32,384]{1,0:T(8,128)S(1)} %get-tuple-element.62), channel_id=1, source_target_pairs={{0,28},{1,29},{2,30},{3,31},{4,8},{5,9},{6,10},{7,11},{8,4},{9,5},... | collective-permute-start | bytes 147464 | tf_op jit(solution)/shard_map/ppermute | solution.py:762
  21.7 0.8 %collective-permute-start.8 = (f32[32,384]{1,0:T(8,128)S(1)}, f32[32,384]{1,0:T(8,128)S(1)}, u32[]{:S(2)}, u32[]{:S(2)}) collective-permute-start(f32[32,384]{1,0:T(8,128)S(1)} %get-tuple-element.63), channel_id=1, source_target_pairs={{0,4},{4,0},{8,12},{12,8},{16,20},{20,16},{24,28},{28,24},{1,5},{5... | collective-permute-start | bytes 147464 | tf_op jit(solution)/shard_map/ppermute | solution.py:763
  22.5 0.7 %shard_map.57 = (f32[96,256]{1,0:T(8,128)S(1)}, f32[96,256]{1,0:T(8,128)S(1)}, f32[144,384]{1,0:T(8,128)S(1)}, f32[144,384]{1,0:T(8,128)S(1)}, f32[16,128]{1,0:T(8,128)S(1)}) custom-call(f32[144,384]{1,0:T(8,128)S(1)} %get-tuple-element.60.y_ref.first_ref, f32[160,384]{1,0:T(8,128)S(1)} %get-tuple-element.61.m_ref, f32[1104,512]{1,0:T(8,128)S(1)} %copy-done), custom_call_target="tpu_custom_call" | custom-call | flops 1000000000 | bytes 1000000 | tf_op jit(solution)/shard_map/pallas_call | solution.py:707
  23.1 3.2 %collective-permute-done.7.gb_ref = f32[32,384]{1,0:T(8,128)S(1)} collective-permute-done((f32[32,384]{1,0:T(8,128)S(1)}, f32[32,384]{1,0:T(8,128)S(1)}, u32[]{:S(2)}, u32[]{:S(2)}) %collective-permute-start.7) | collective-permute-done | bytes 49184 | tf_op jit(solution)/shard_map/ppermute | solution.py:762
  26.3 0.0 collective-permute-done.8.ga_ref
  26.3 1.2 %shard_map.58 = (f32[32,256]{1,0:T(8,128)S(1)}, f32[32,256]{1,0:T(8,128)S(1)}, f32[8,384]{1,0:T(8,128)S(1)}, f32[144,512]{1,0:T(8,128)S(1)}, f32[16,144]{1,0:T(8,128)S(1)}, /*index=5*/f32[16,144]{1,0:T(8,128)S(1)}) custom-call(f32[144,384]{1,0:T(8,128)S(1)} %get-tuple-element.60.y_ref.first_ref, f32[160,384]{1,0:T(8,128)S(1)} %get-tuple-element.61.m_ref, ...), custom_call_target="tpu_custom_call" | custom-call | flops 1000000000 | bytes 1000000 | tf_op jit(solution)/shard_map/pallas_call | solution.py:707
  27.5 0.1 collective-permute-start.9
  27.6 3.1 %collective-permute-start.10 = (f32[16,144]{1,0:T(8,128)S(1)}, f32[16,144]{1,0:T(8,128)S(1)}, u32[]{:S(2)}, u32[]{:S(2)}) collective-permute-start(f32[16,144]{1,0:T(8,128)S(1)} %get-tuple-element.76), channel_id=1, source_target_pairs={{0,1},{1,0},{2,3},{3,2},{4,5},{5,4},{6,7},{7,6},{8,9},{9,8},{10,11... | collective-permute-start | bytes 27656 | tf_op jit(solution)/shard_map/ppermute | solution.py:763
  30.8 0.8 %shard_map.59 = (f32[144,384]{1,0:T(8,128)S(1)}, f32[1,128]{1,0:T(1,128)S(1)}, f32[128,256]{1,0:T(8,128)S(1)}, f32[128,256]{1,0:T(8,128)S(1)}) custom-call(f32[144,512]{1,0:T(8,128)S(1)} %get-tuple-element.68.t_ref, f32[1104,512]{1,0:T(8,128)S(1)} %copy-done, f32[256,256]{1,0:T(8,128)S(1)} %pad_add_fusion.both_ref, f32[160,384]{1,0:T(8,128)S(1)} %get-tuple-element.61.m_ref, ...), custom_call_target="tpu_custom_call" | custom-call | flops 1000000000 | bytes 1000000 | tf_op jit(solution)/shard_map/pallas_call | solution.py:707
  31.6 0.0 collective-permute-done.9.refs_0_
  31.6 1.0 %collective-permute-done.10.refs_1_ = f32[16,144]{1,0:T(8,128)S(1)} collective-permute-done((f32[16,144]{1,0:T(8,128)S(1)}, f32[16,144]{1,0:T(8,128)S(1)}, u32[]{:S(2)}, u32[]{:S(2)}) %collective-permute-start.10) | collective-permute-done | bytes 9248 | tf_op jit(solution)/shard_map/ppermute | solution.py:763
  32.7 0.2 shard_map.60
  32.8 1.9 %collective-permute-start.11 = (f32[16,384]{1,0:T(8,128)S(1)}, f32[16,384]{1,0:T(8,128)S(1)}, u32[]{:S(2)}, u32[]{:S(2)}) collective-permute-start(f32[16,384]{1,0:T(8,128)S(1)} %get-tuple-element.78), channel_id=1, source_target_pairs={{0,1},{1,0},{2,3},{3,2},{4,8},{5,9},{6,10},{7,11},{8,4},{9,5},{10,... | collective-permute-start | bytes 73736 | tf_op jit(solution)/shard_map/ppermute | solution.py:762
  34.8 0.0 collective-permute-start.12
  34.8 0.4 shard_map.61
  35.1 1.6 %collective-permute-done.11.gb_ref = f32[16,384]{1,0:T(8,128)S(1)} collective-permute-done((f32[16,384]{1,0:T(8,128)S(1)}, f32[16,384]{1,0:T(8,128)S(1)}, u32[]{:S(2)}, u32[]{:S(2)}) %collective-permute-start.11) | collective-permute-done | bytes 24608 | tf_op jit(solution)/shard_map/ppermute | solution.py:762
  36.7 0.0 collective-permute-done.12.ga_ref
  36.7 0.3 shard_map.62
  37.0 9.2 %all_to_all.11 = f32[32,1,128]{2,1,0:T(1,128)S(1)} all-to-all(f32[32,1,128]{2,1,0:T(1,128)S(1)} %bitcast.5), channel_id=1, replica_groups=mesh['row'=8,'col'=4] {'row','col'}, dimensions={0} | all-to-all | bytes 32768 | tf_op jit(solution)/shard_map/all_to_all | solution.py:883
  46.2 1.3 %shard_map.63 = (f32[128,256]{1,0:T(8,128)}, f32[128,256]{1,0:T(8,128)}) custom-call(f32[32,128]{1,0:T(8,128)S(1)} %bitcast.4, f32[1104,512]{1,0:T(8,128)S(1)} %copy-done, f32[160,384]{1,0:T(8,128)S(1)} %get-tuple-element.61.m_ref, f32[96,256]{1,0:T(8,128)S(1)} %get-tuple-element.70.f_ref, f32[256,256]{1,0:T(8,128)S(1)} %pad_add_fusion.both_ref, ...), custom_call_target="tpu_custom_call" | custom-call | flops 1000000000 | bytes 1000000 | tf_op jit(solution)/shard_map/pallas_call | solution.py:707
  (2 shorter events, 0.0 us)
Async XLA Ops:
  1.8 9.9 %copy-start = (f32[1104,512]{1,0:T(8,128)S(1)}, f32[1104,512]{1,0:T(8,128)}, u32[]{:S(2)}) copy-start(f32[1104,512]{1,0:T(8,128)} %constant.6.clone.basis_ref) | copy-start | bytes 6782980
  1.8 5.7 %collective-permute-start = (f32[40,128]{1,0:T(8,128)S(1)}, f32[40,128]{1,0:T(8,128)S(1)}, u32[]{:S(2)}, u32[]{:S(2)}) collective-permute-start(f32[40,128]{1,0:T(8,128)S(1)} %get-tuple-element.46), channel_id=1, source_target_pairs={{0,3},{1,2},{2,1},{3,0},{4,7},{5,6},{6,5},{7,4},{8,11},{9,10},{10,... | collective-permute-start | bytes 61448 | tf_op jit(solution)/shard_map/ppermute | solution.py:762
  5.8 3.8 %collective-permute-start.1 = (f32[40,128]{1,0:T(8,128)S(1)}, f32[40,128]{1,0:T(8,128)S(1)}, u32[]{:S(2)}, u32[]{:S(2)}) collective-permute-start(f32[40,128]{1,0:T(8,128)S(1)} %get-tuple-element.47), channel_id=1, source_target_pairs={{0,1},{1,0},{2,3},{3,2},{4,5},{5,4},{6,7},{7,6},{8,9},{9,8},{10,11... | collective-permute-start | bytes 61448 | tf_op jit(solution)/shard_map/ppermute | solution.py:763
  9.7 5.6 %collective-permute-start.2 = (f32[32,384]{1,0:T(8,128)S(1)}, f32[32,384]{1,0:T(8,128)S(1)}, u32[]{:S(2)}, u32[]{:S(2)}) collective-permute-start(f32[32,384]{1,0:T(8,128)S(1)} %get-tuple-element.48), channel_id=1, source_target_pairs={{0,28},{1,29},{2,30},{3,31},{4,8},{5,9},{6,10},{7,11},{8,4},{9,5},... | collective-permute-start | bytes 147464 | tf_op jit(solution)/shard_map/ppermute | solution.py:762
  11.7 3.7 %collective-permute-start.3 = (f32[32,384]{1,0:T(8,128)S(1)}, f32[32,384]{1,0:T(8,128)S(1)}, u32[]{:S(2)}, u32[]{:S(2)}) collective-permute-start(f32[32,384]{1,0:T(8,128)S(1)} %get-tuple-element.49), channel_id=1, source_target_pairs={{0,4},{4,0},{8,12},{12,8},{16,20},{20,16},{24,28},{28,24},{1,5},{5... | collective-permute-start | bytes 147464 | tf_op jit(solution)/shard_map/ppermute | solution.py:763
  11.9 4.6 %collective-permute-start.4 = (f32[8,128]{1,0:T(8,128)S(1)}, f32[8,128]{1,0:T(8,128)S(1)}, u32[]{:S(2)}, u32[]{:S(2)}) collective-permute-start(f32[8,128]{1,0:T(8,128)S(1)} %get-tuple-element.53.table_ref), channel_id=1, source_target_pairs={{0,16},{1,17},{2,18},{3,19},{4,20},{5,21},{6,22},{7,23},{8,24},{9,... | collective-permute-start | bytes 12296 | tf_op jit(solution)/shard_map/ppermute | solution.py:766
  16.5 2.8 %collective-permute-start.6 = (f32[32,144]{1,0:T(8,128)S(1)}, f32[32,144]{1,0:T(8,128)S(1)}, u32[]{:S(2)}, u32[]{:S(2)}) collective-permute-start(f32[32,144]{1,0:T(8,128)S(1)} %get-tuple-element.88), channel_id=1, source_target_pairs={{0,4},{1,2},{2,1},{3,7},{4,0},{5,6},{6,5},{7,3},{8,12},{9,10},{10,... | collective-permute-start | bytes 55304 | tf_op jit(solution)/shard_map/ppermute | solution.py:762
  16.6 4.2 %collective-permute-start.5 = (f32[32,144]{1,0:T(8,128)S(1)}, f32[32,144]{1,0:T(8,128)S(1)}, u32[]{:S(2)}, u32[]{:S(2)}) collective-permute-start(f32[32,144]{1,0:T(8,128)S(1)} %get-tuple-element.89), channel_id=1, source_target_pairs={{0,1},{1,0},{2,3},{3,2},{4,5},{5,4},{6,7},{7,6},{8,9},{9,8},{10,11... | collective-permute-start | bytes 55304 | tf_op jit(solution)/shard_map/ppermute | solution.py:763
  20.9 5.4 %collective-permute-start.7 = (f32[32,384]{1,0:T(8,128)S(1)}, f32[32,384]{1,0:T(8,128)S(1)}, u32[]{:S(2)}, u32[]{:S(2)}) collective-permute-start(f32[32,384]{1,0:T(8,128)S(1)} %get-tuple-element.62), channel_id=1, source_target_pairs={{0,28},{1,29},{2,30},{3,31},{4,8},{5,9},{6,10},{7,11},{8,4},{9,5},... | collective-permute-start | bytes 147464 | tf_op jit(solution)/shard_map/ppermute | solution.py:762
  21.7 4.6 %collective-permute-start.8 = (f32[32,384]{1,0:T(8,128)S(1)}, f32[32,384]{1,0:T(8,128)S(1)}, u32[]{:S(2)}, u32[]{:S(2)}) collective-permute-start(f32[32,384]{1,0:T(8,128)S(1)} %get-tuple-element.63), channel_id=1, source_target_pairs={{0,4},{4,0},{8,12},{12,8},{16,20},{20,16},{24,28},{28,24},{1,5},{5... | collective-permute-start | bytes 147464 | tf_op jit(solution)/shard_map/ppermute | solution.py:763
  27.5 4.1 %collective-permute-start.9 = (f32[16,144]{1,0:T(8,128)S(1)}, f32[16,144]{1,0:T(8,128)S(1)}, u32[]{:S(2)}, u32[]{:S(2)}) collective-permute-start(f32[16,144]{1,0:T(8,128)S(1)} %get-tuple-element.75), channel_id=1, source_target_pairs={{0,4},{1,2},{2,1},{3,7},{4,0},{5,6},{6,5},{7,3},{8,12},{9,10},{10,... | collective-permute-start | bytes 27656 | tf_op jit(solution)/shard_map/ppermute | solution.py:762
  27.6 5.0 %collective-permute-start.10 = (f32[16,144]{1,0:T(8,128)S(1)}, f32[16,144]{1,0:T(8,128)S(1)}, u32[]{:S(2)}, u32[]{:S(2)}) collective-permute-start(f32[16,144]{1,0:T(8,128)S(1)} %get-tuple-element.76), channel_id=1, source_target_pairs={{0,1},{1,0},{2,3},{3,2},{4,5},{5,4},{6,7},{7,6},{8,9},{9,8},{10,11... | collective-permute-start | bytes 27656 | tf_op jit(solution)/shard_map/ppermute | solution.py:763
  32.8 3.9 %collective-permute-start.11 = (f32[16,384]{1,0:T(8,128)S(1)}, f32[16,384]{1,0:T(8,128)S(1)}, u32[]{:S(2)}, u32[]{:S(2)}) collective-permute-start(f32[16,384]{1,0:T(8,128)S(1)} %get-tuple-element.78), channel_id=1, source_target_pairs={{0,1},{1,0},{2,3},{3,2},{4,8},{5,9},{6,10},{7,11},{8,4},{9,5},{10,... | collective-permute-start | bytes 73736 | tf_op jit(solution)/shard_map/ppermute | solution.py:762
  34.8 2.0 %collective-permute-start.12 = (f32[16,384]{1,0:T(8,128)S(1)}, f32[16,384]{1,0:T(8,128)S(1)}, u32[]{:S(2)}, u32[]{:S(2)}) collective-permute-start(f32[16,384]{1,0:T(8,128)S(1)} %get-tuple-element.79), channel_id=1, source_target_pairs={{0,4},{4,0},{8,12},{12,8},{16,20},{20,16},{24,28},{28,24},{1,5},{5... | collective-permute-start | bytes 73736 | tf_op jit(solution)/shard_map/ppermute | solution.py:763

commit v23 on v19

--- a/solution.py
+++ b/solution.py
@@ -341,6 +341,31 @@
     return before, after
 
 
+def fold(rows, table):
+    lane = lanes_of((8, 128))
+    free = (lane >= 32) & (lane < 96)
+    third = jnp.concatenate(
+        [
+            jnp.where(free, pltpu.roll(table, 32, 1), rows[:8, 256:]),
+            jnp.where(free, pltpu.roll(table, 96, 1), rows[8:16, 256:]),
+            rows[16:, 256:],
+        ],
+        axis=0,
+    )
+    return jnp.concatenate([rows[:, :256], third], axis=1)
+
+
+def unfold(ref):
+    low, high = ref[:8, 256:], ref[8:16, 256:]
+    return jnp.where(lanes_of((8, 128)) < 64, pltpu.roll(low, 96, 1), pltpu.roll(high, 32, 1))
+
+
+def row_sides(index, count, ga_ref, gb_ref, rows):
+    lane = lanes_of((1, FC))
+    used = (lane < 288) | (lane >= 352)
+    return [jnp.where(used, x, 0.0) for x in sides(index, count, ga_ref[rows], gb_ref[rows])]
+
+
 def send(index, a_ref, b_ref, before, after):
     even = is_even(index)
     a_ref[...] = jnp.where(even, after, before)
@@ -387,17 +412,16 @@
     r, h = both_ref[:TR], both_ref[TR:]
     table = merged(own_ref[...], ga_ref[32:], gb_ref[32:])
     table_ref[...] = table
-    wide = jnp.concatenate([table, jnp.zeros((table.shape[0], FC - 128), jnp.float32)], axis=1)
 
     def strip(r_rows, h_rows):
-        return jnp.concatenate(
+        rows = jnp.concatenate(
             [
                 jnp.concatenate([r[r_rows], r3[r_rows]], axis=1),
                 jnp.concatenate([h[h_rows], h3[h_rows]], axis=1),
-                wide,
             ],
             axis=0,
         )
+        return fold(rows, table)
 
     send(i, a_ref, b_ref, strip(slice(0, 8), slice(0, 16)), strip(slice(120, 128), slice(112, 128)))
 
@@ -429,11 +453,11 @@
     a_ref,
 ):
     i, j = place()
-    above, below = sides(i, counts[0], ga_ref[:8], gb_ref[:8])
+    above, below = row_sides(i, counts[0], ga_ref, gb_ref, slice(0, 8))
     u = column_transform(jnp.concatenate([below, above], axis=0), basis_ref)
     t = (tile_ref[...] + row_transform(u, basis_ref, halo_rows)) * weights_ref[...]
     t_ref[...] = t
-    table = merged(table_ref[...], ga_ref[24:, :128], gb_ref[24:, :128])
+    table = merged(table_ref[...], unfold(ga_ref), unfold(gb_ref))
     table_out[...] = table
     wide = jnp.concatenate([table, jnp.zeros((table.shape[0], EXT - 128), jnp.float32)], axis=1)
     strips = (jnp.concatenate([x, wide], axis=0) for x in strips_of(t, basis_ref, 24))
@@ -445,7 +469,7 @@
 ):
     table_out[...] = table_ref[...]
     y_ref[...] = solution_of(t_ref[...], basis_ref)
-    above, below = sides(lax.axis_index("row"), counts[0], ga_ref[8:24], gb_ref[8:24])
+    above, below = row_sides(lax.axis_index("row"), counts[0], ga_ref, gb_ref, slice(8, 24))
     h = jnp.concatenate([both_ref[TR:], h3_ref[...]], axis=1)
     tall = jnp.concatenate([h, below, above], axis=0)
     m_ref[...] = tall * tall * tall
@@ -460,8 +484,7 @@
         table_ref, far_ref, out_ref, table_out, b_ref, a_ref = refs
         table = merged(table_ref[...], far_ref[...], ga_ref[24:, :128], gb_ref[24:, :128])
         table_out[...] = table
-        wide = jnp.concatenate([table, jnp.zeros((table.shape[0], FC - 128), jnp.float32)], axis=1)
-        strips = [jnp.concatenate([x, wide], axis=0) for x in strips]
+        strips = [fold(x, table) for x in strips]
     else:
         out_ref, b_ref, a_ref = refs
     out_ref[...] = y
@@ -508,9 +531,9 @@
     i, j = place()
     y = y_ref[...]
     mask = edge_mask(counts)
-    s = edges(y, *sides(i, counts[0], ga_ref[:24], gb_ref[:24]))
+    s = edges(y, *row_sides(i, counts[0], ga_ref, gb_ref, slice(0, 24)))
     s = jnp.where(mask, s, 0.0)
-    table = merged(table_ref[...], farther_ref[...], ga_ref[24:, :128], gb_ref[24:, :128])
+    table = merged(table_ref[...], farther_ref[...], unfold(ga_ref), unfold(gb_ref))
     picked = jnp.sum(near_ref[...] * as_row(table, width), axis=1, keepdims=True)
     bands = as_bands([picked[k : k + 1] for k in range(12)])
     coarse = edge_bands(bands)
@@ -762,7 +785,7 @@
     ga, gb = swap(a, b, "col")
     r3, h3, b, a, table = call(
         functools.partial(widen_kernel, counts),
-        [(128, 128)] * 2 + [(24 + depth, FC)] * 2 + [(depth, 128)],
+        [(128, 128)] * 2 + [(24, FC)] * 2 + [(depth, 128)],
         both,
         table,
         gb,
@@ -771,7 +794,7 @@
     ga, gb = swap(a, b, "row")
     weight, table = call(weights_kernel, [(EXT, 2 * SPEC), (depth, 128)], both, table, basis)
     far = small_swap(table, 4, 0)
-    t = call(forward_kernel, [(EXT, 2 * SPEC)], both, r3, basis)[0]
+    t = call(forward_kernel, [(EXT, 2 * SPEC)], both, r3, basis, flops=5 * 10**8)[0]
     t, table, b, a = call(
         functools.partial(first_kernel, counts),
         [(EXT, 2 * SPEC), (depth, 128)] + [(24 + depth, EXT)] * 2,
@@ -797,7 +820,7 @@
     farther = small_swap(table_too, 4, 2)
     y, table, b, a = call(
         functools.partial(columns_kernel, counts),
-        [(EXT, FC), (depth, 128)] + [(24 + depth, FC)] * 2,
+        [(EXT, FC), (depth, 128)] + [(24, FC)] * 2,
         y,
         gb,
         ga,

time: 47.6 us -> 47.3 us (level)
  no operation moved by 1% of the time
where the time goes in v23:
time: 47.3 us; the launch traced here: 47.1 us
  starting transfers between devices  17 us (36%)
  waiting for transfers between devices  11.3 us (24%)
  blocking collectives  9.2 us (19%)
  Pallas kernels  7.94 us (17%)
  other arithmetic  0.99 us (2%)
  between operations  0.74 us (2%)
    all_to_all x1, blocking collectives, body(): stats = lax.all_to_all(stats, both_axes, 0, 0, tiled=True)  9.2 us
    ppermute x6, starting transfers between devices, swap(): lax.ppermute(b, both_axes, odd_pairs(counts, both_axes.index(axis), bit))  8.7 us
    pallas_call x14, Pallas kernels, call(): pl.pallas_call(kernel, out_shape=shapes, compiler_params=pltpu.CompilerPa...  7.94 us
    ppermute x6, starting transfers between devices, swap(): return (lax.ppermute(a, axis, pairs_from(lax.axis_size(axis), 0)), gb)  5.65 us
    ppermute x6, waiting for transfers between devices, swap(): lax.ppermute(b, both_axes, odd_pairs(counts, both_axes.index(axis), bit))  4.45 us
    ppermute x6, waiting for transfers between devices, swap(): return (lax.ppermute(a, axis, pairs_from(lax.axis_size(axis), 0)), gb)  4.28 us
    ppermute x2, starting transfers between devices, small_swap(): return lax.ppermute(x, both_axes, xor_pairs(counts, rows, cols))  2.63 us
    ppermute x2, waiting for transfers between devices, small_swap(): return lax.ppermute(x, both_axes, xor_pairs(counts, rows, cols))  2.54 us
  transfers between devices with their start and end apart: 14, of which 8 were waited for; matrix products, arithmetic and copies ran while one was open for 0% of the time, Pallas kernels for 10%

profile of v23, /device:TPU:0, one launch (start us, length us, event | category | flops | bytes accessed | tf_op | source)
XLA Modules:
  0.0 47.1 jit_solution(17160423031071057797)
XLA Ops:
  0.6 1.0 %pad_add_fusion.both_ref = f32[256,256]{1,0:T(8,128)S(1)} fusion(f32[128,256]{1,0:T(8,128)} %param.3, f32[128,256]{1,0:T(8,128)} %param.4), kind=kLoop, calls=%fused_computation | loop fusion | flops 65536 | bytes 524288 | tf_op jit(solution)/shard_map/add | solution.py:775
  1.6 0.2 shard_map.50
  1.8 0.0 copy-start
  1.8 4.0 %collective-permute-start = (f32[40,128]{1,0:T(8,128)S(1)}, f32[40,128]{1,0:T(8,128)S(1)}, u32[]{:S(2)}, u32[]{:S(2)}) collective-permute-start(f32[40,128]{1,0:T(8,128)S(1)} %get-tuple-element.44), channel_id=1, source_target_pairs={{0,3},{1,2},{2,1},{3,0},{4,7},{5,6},{6,5},{7,4},{8,11},{9,10},{10,... | collective-permute-start | bytes 61448 | tf_op jit(solution)/shard_map/ppermute | solution.py:769
  5.8 0.5 %collective-permute-start.1 = (f32[40,128]{1,0:T(8,128)S(1)}, f32[40,128]{1,0:T(8,128)S(1)}, u32[]{:S(2)}, u32[]{:S(2)}) collective-permute-start(f32[40,128]{1,0:T(8,128)S(1)} %get-tuple-element.45), channel_id=1, source_target_pairs={{0,1},{1,0},{2,3},{3,2},{4,5},{5,4},{6,7},{7,6},{8,9},{9,8},{10,11... | collective-permute-start | bytes 61448 | tf_op jit(solution)/shard_map/ppermute | solution.py:770
  6.3 1.2 %collective-permute-done.gb_ref = f32[40,128]{1,0:T(8,128)S(1)} collective-permute-done((f32[40,128]{1,0:T(8,128)S(1)}, f32[40,128]{1,0:T(8,128)S(1)}, u32[]{:S(2)}, u32[]{:S(2)}) %collective-permute-start) | collective-permute-done | bytes 20512 | tf_op jit(solution)/shard_map/ppermute | solution.py:769
  7.5 2.0 %collective-permute-done.1.ga_ref = f32[40,128]{1,0:T(8,128)S(1)} collective-permute-done((f32[40,128]{1,0:T(8,128)S(1)}, f32[40,128]{1,0:T(8,128)S(1)}, u32[]{:S(2)}, u32[]{:S(2)}) %collective-permute-start.1) | collective-permute-done | bytes 20512 | tf_op jit(solution)/shard_map/ppermute | solution.py:770
  9.5 0.2 shard_map.51
  9.7 2.0 %collective-permute-start.2 = (f32[24,384]{1,0:T(8,128)S(1)}, f32[24,384]{1,0:T(8,128)S(1)}, u32[]{:S(2)}, u32[]{:S(2)}) collective-permute-start(f32[24,384]{1,0:T(8,128)S(1)} %get-tuple-element.46), channel_id=1, source_target_pairs={{0,28},{1,29},{2,30},{3,31},{4,8},{5,9},{6,10},{7,11},{8,4},{9,5},... | collective-permute-start | bytes 110600 | tf_op jit(solution)/shard_map/ppermute | solution.py:769
  11.7 0.0 collective-permute-start.3
  11.7 0.0 copy-done
  11.7 0.1 shard_map.53
  11.9 2.4 %collective-permute-start.6 = (f32[8,128]{1,0:T(8,128)S(1)}, f32[8,128]{1,0:T(8,128)S(1)}, u32[]{:S(2)}, u32[]{:S(2)}) collective-permute-start(f32[8,128]{1,0:T(8,128)S(1)} %get-tuple-element.51.table_ref), channel_id=1, source_target_pairs={{0,16},{1,17},{2,18},{3,19},{4,20},{5,21},{6,22},{7,23},{8,24},{9,... | collective-permute-start | bytes 12296 | tf_op jit(solution)/shard_map/ppermute | solution.py:773
  14.3 0.6 %shard_map.52.tile_ref = f32[144,512]{1,0:T(8,128)S(1)} custom-call(f32[256,256]{1,0:T(8,128)S(1)} %pad_add_fusion.both_ref, f32[128,128]{1,0:T(8,128)S(1)} %get-tuple-element.48.r3_ref, f32[1104,512]{1,0:T(8,128)S(1)} %copy-done), custom_call_target="tpu_custom_call" | custom-call | flops 500000000 | bytes 1000000 | tf_op jit(solution)/shard_map/pallas_call | solution.py:712
  14.9 0.2 collective-permute-done.2.gb_ref
  15.1 0.0 collective-permute-done.3.ga_ref
  15.1 1.0 %shard_map.54 = (f32[144,512]{1,0:T(8,128)S(1)}, f32[8,128]{1,0:T(8,128)S(1)}, f32[32,144]{1,0:T(8,128)S(1)}, f32[32,144]{1,0:T(8,128)S(1)}) custom-call(f32[24,384]{1,0:T(8,128)S(1)} %collective-permute-done.2.gb_ref, f32[24,384]{1,0:T(8,128)S(1)} %collective-permute-done.3.ga_ref, f32[144,512]{1,0:T(8,128)S(1)} %shard_map.52.tile_ref, ...), custom_call_target="tpu_custom_call" | custom-call | flops 1000000000 | bytes 1000000 | tf_op jit(solution)/shard_map/pallas_call | solution.py:712
  16.1 0.1 collective-permute-start.4
  16.2 2.0 %collective-permute-start.5 = (f32[32,144]{1,0:T(8,128)S(1)}, f32[32,144]{1,0:T(8,128)S(1)}, u32[]{:S(2)}, u32[]{:S(2)}) collective-permute-start(f32[32,144]{1,0:T(8,128)S(1)} %get-tuple-element.57), channel_id=1, source_target_pairs={{0,1},{1,0},{2,3},{3,2},{4,5},{5,4},{6,7},{7,6},{8,9},{9,8},{10,11... | collective-permute-start | bytes 55304 | tf_op jit(solution)/shard_map/ppermute | solution.py:770
  18.2 0.8 %shard_map.55 = (f32[144,384]{1,0:T(8,128)S(1)}, f32[160,384]{1,0:T(8,128)S(1)}, f32[8,128]{1,0:T(8,128)S(1)}) custom-call(f32[144,512]{1,0:T(8,128)S(1)} %get-tuple-element.52.t_ref, f32[1104,512]{1,0:T(8,128)S(1)} %copy-done, f32[256,256]{1,0:T(8,128)S(1)} %pad_add_fusion.both_ref, f32[128,128]{1,0:T(8,128)S(1)} %get-tuple-element.53.h3_ref, ...), custom_call_target="tpu_custom_call" | custom-call | flops 1000000000 | bytes 1000000 | tf_op jit(solution)/shard_map/pallas_call | solution.py:712
  19.0 0.2 collective-permute-start.9
  19.2 0.0 collective-permute-done.6.refs_1_
  19.2 0.0 collective-permute-done.4.gb_ref
  19.2 1.2 %collective-permute-done.5.ga_ref = f32[32,144]{1,0:T(8,128)S(1)} collective-permute-done((f32[32,144]{1,0:T(8,128)S(1)}, f32[32,144]{1,0:T(8,128)S(1)}, u32[]{:S(2)}, u32[]{:S(2)}) %collective-permute-start.5) | collective-permute-done | bytes 18464 | tf_op jit(solution)/shard_map/ppermute | solution.py:770
  20.4 0.2 shard_map.56
  20.6 0.7 %collective-permute-start.7 = (f32[24,384]{1,0:T(8,128)S(1)}, f32[24,384]{1,0:T(8,128)S(1)}, u32[]{:S(2)}, u32[]{:S(2)}) collective-permute-start(f32[24,384]{1,0:T(8,128)S(1)} %get-tuple-element.60), channel_id=1, source_target_pairs={{0,28},{1,29},{2,30},{3,31},{4,8},{5,9},{6,10},{7,11},{8,4},{9,5},... | collective-permute-start | bytes 110600 | tf_op jit(solution)/shard_map/ppermute | solution.py:769
  21.3 0.0 collective-permute-start.8
  21.3 0.7 %shard_map.57 = (f32[96,256]{1,0:T(8,128)S(1)}, f32[96,256]{1,0:T(8,128)S(1)}, f32[144,384]{1,0:T(8,128)S(1)}, f32[144,384]{1,0:T(8,128)S(1)}, f32[16,128]{1,0:T(8,128)S(1)}) custom-call(f32[144,384]{1,0:T(8,128)S(1)} %get-tuple-element.58.y_ref, f32[160,384]{1,0:T(8,128)S(1)} %get-tuple-element.59.m_ref, f32[1104,512]{1,0:T(8,128)S(1)} %copy-done), custom_call_target="tpu_custom_call" | custom-call | flops 1000000000 | bytes 1000000 | tf_op jit(solution)/shard_map/pallas_call | solution.py:712
  21.9 2.5 %collective-permute-done.9.farther_ref = f32[8,128]{1,0:T(8,128)S(1)} collective-permute-done((f32[8,128]{1,0:T(8,128)S(1)}, f32[8,128]{1,0:T(8,128)S(1)}, u32[]{:S(2)}, u32[]{:S(2)}) %collective-permute-start.9) | collective-permute-done | bytes 4128 | tf_op jit(solution)/shard_map/ppermute | solution.py:773
  24.5 1.4 %collective-permute-done.7.gb_ref = f32[24,384]{1,0:T(8,128)S(1)} collective-permute-done((f32[24,384]{1,0:T(8,128)S(1)}, f32[24,384]{1,0:T(8,128)S(1)}, u32[]{:S(2)}, u32[]{:S(2)}) %collective-permute-start.7) | collective-permute-done | bytes 36896 | tf_op jit(solution)/shard_map/ppermute | solution.py:769
  25.8 0.0 collective-permute-done.8.ga_ref
  25.8 1.3 %shard_map.58 = (f32[128,256]{1,0:T(8,128)S(1)}, f32[128,256]{1,0:T(8,128)S(1)}, f32[144,512]{1,0:T(8,128)S(1)}, f32[16,144]{1,0:T(8,128)S(1)}, f32[16,144]{1,0:T(8,128)S(1)}) custom-call(f32[144,384]{1,0:T(8,128)S(1)} %get-tuple-element.58.y_ref, f32[160,384]{1,0:T(8,128)S(1)} %get-tuple-element.59.m_ref, f32[24,384]{1,0:T(8,128)S(1)} %collective-permute-done.7.gb_ref, ...), custom_call_target="tpu_custom_call" | custom-call | flops 1000000000 | bytes 1000000 | tf_op jit(solution)/shard_map/pallas_call | solution.py:712
  27.2 0.1 collective-permute-start.10
  27.3 3.2 %collective-permute-start.11 = (f32[16,144]{1,0:T(8,128)S(1)}, f32[16,144]{1,0:T(8,128)S(1)}, u32[]{:S(2)}, u32[]{:S(2)}) collective-permute-start(f32[16,144]{1,0:T(8,128)S(1)} %get-tuple-element.74), channel_id=1, source_target_pairs={{0,1},{1,0},{2,3},{3,2},{4,5},{5,4},{6,7},{7,6},{8,9},{9,8},{10,11... | collective-permute-start | bytes 27656 | tf_op jit(solution)/shard_map/ppermute | solution.py:770
  30.4 0.8 %shard_map.59 = (f32[144,384]{1,0:T(8,128)S(1)}, f32[1,128]{1,0:T(1,128)S(1)}) custom-call(f32[144,512]{1,0:T(8,128)S(1)} %get-tuple-element.69.t_ref, f32[1104,512]{1,0:T(8,128)S(1)} %copy-done, f32[256,256]{1,0:T(8,128)S(1)} %pad_add_fusion.both_ref, f32[160,384]{1,0:T(8,128)S(1)} %get-tuple-element.59.m_ref, f32[128,256]{1,0:T(8,128)S(1)} %get-tuple-element.70.z_ref, ...), custom_call_target="tpu_custom_call" | custom-call | flops 1000000000 | bytes 1000000 | tf_op jit(solution)/shard_map/pallas_call | solution.py:712
  31.3 0.0 collective-permute-done.10.gb_ref
  31.3 1.1 %collective-permute-done.11.ga_ref = f32[16,144]{1,0:T(8,128)S(1)} collective-permute-done((f32[16,144]{1,0:T(8,128)S(1)}, f32[16,144]{1,0:T(8,128)S(1)}, u32[]{:S(2)}, u32[]{:S(2)}) %collective-permute-start.11) | collective-permute-done | bytes 9248 | tf_op jit(solution)/shard_map/ppermute | solution.py:770
  32.3 0.2 shard_map.60
  32.5 1.9 %collective-permute-start.12 = (f32[16,384]{1,0:T(8,128)S(1)}, f32[16,384]{1,0:T(8,128)S(1)}, u32[]{:S(2)}, u32[]{:S(2)}) collective-permute-start(f32[16,384]{1,0:T(8,128)S(1)} %get-tuple-element.76), channel_id=1, source_target_pairs={{0,1},{1,0},{2,3},{3,2},{4,8},{5,9},{6,10},{7,11},{8,4},{9,5},{10,... | collective-permute-start | bytes 73736 | tf_op jit(solution)/shard_map/ppermute | solution.py:769
  34.4 0.0 collective-permute-start.13
  34.4 0.4 shard_map.61
  34.8 1.6 %collective-permute-done.12.gb_ref = f32[16,384]{1,0:T(8,128)S(1)} collective-permute-done((f32[16,384]{1,0:T(8,128)S(1)}, f32[16,384]{1,0:T(8,128)S(1)}, u32[]{:S(2)}, u32[]{:S(2)}) %collective-permute-start.12) | collective-permute-done | bytes 24608 | tf_op jit(solution)/shard_map/ppermute | solution.py:769
  36.4 0.0 collective-permute-done.13.ga_ref
  36.4 0.3 shard_map.62
  36.7 9.2 %all_to_all.11 = f32[32,1,128]{2,1,0:T(1,128)S(1)} all-to-all(f32[32,1,128]{2,1,0:T(1,128)S(1)} %bitcast.5), channel_id=1, replica_groups=mesh['row'=8,'col'=4] {'row','col'}, dimensions={0} | all-to-all | bytes 32768 | tf_op jit(solution)/shard_map/all_to_all | solution.py:882
  45.9 1.3 %shard_map.63 = (f32[128,256]{1,0:T(8,128)}, f32[128,256]{1,0:T(8,128)}) custom-call(f32[32,128]{1,0:T(8,128)S(1)} %bitcast.4, f32[1104,512]{1,0:T(8,128)S(1)} %copy-done, f32[160,384]{1,0:T(8,128)S(1)} %get-tuple-element.59.m_ref, f32[96,256]{1,0:T(8,128)S(1)} %get-tuple-element.65.f_ref, f32[256,256]{1,0:T(8,128)S(1)} %pad_add_fusion.both_ref, ...), custom_call_target="tpu_custom_call" | custom-call | flops 1000000000 | bytes 1000000 | tf_op jit(solution)/shard_map/pallas_call | solution.py:712
Async XLA Ops:
  1.8 9.9 %copy-start = (f32[1104,512]{1,0:T(8,128)S(1)}, f32[1104,512]{1,0:T(8,128)}, u32[]{:S(2)}) copy-start(f32[1104,512]{1,0:T(8,128)} %constant.5.clone.basis_ref) | copy-start | bytes 6782980
  1.8 5.7 %collective-permute-start = (f32[40,128]{1,0:T(8,128)S(1)}, f32[40,128]{1,0:T(8,128)S(1)}, u32[]{:S(2)}, u32[]{:S(2)}) collective-permute-start(f32[40,128]{1,0:T(8,128)S(1)} %get-tuple-element.44), channel_id=1, source_target_pairs={{0,3},{1,2},{2,1},{3,0},{4,7},{5,6},{6,5},{7,4},{8,11},{9,10},{10,... | collective-permute-start | bytes 61448 | tf_op jit(solution)/shard_map/ppermute | solution.py:769
  5.8 3.8 %collective-permute-start.1 = (f32[40,128]{1,0:T(8,128)S(1)}, f32[40,128]{1,0:T(8,128)S(1)}, u32[]{:S(2)}, u32[]{:S(2)}) collective-permute-start(f32[40,128]{1,0:T(8,128)S(1)} %get-tuple-element.45), channel_id=1, source_target_pairs={{0,1},{1,0},{2,3},{3,2},{4,5},{5,4},{6,7},{7,6},{8,9},{9,8},{10,11... | collective-permute-start | bytes 61448 | tf_op jit(solution)/shard_map/ppermute | solution.py:770
  9.7 5.4 %collective-permute-start.2 = (f32[24,384]{1,0:T(8,128)S(1)}, f32[24,384]{1,0:T(8,128)S(1)}, u32[]{:S(2)}, u32[]{:S(2)}) collective-permute-start(f32[24,384]{1,0:T(8,128)S(1)} %get-tuple-element.46), channel_id=1, source_target_pairs={{0,28},{1,29},{2,30},{3,31},{4,8},{5,9},{6,10},{7,11},{8,4},{9,5},... | collective-permute-start | bytes 110600 | tf_op jit(solution)/shard_map/ppermute | solution.py:769
  11.7 3.4 %collective-permute-start.3 = (f32[24,384]{1,0:T(8,128)S(1)}, f32[24,384]{1,0:T(8,128)S(1)}, u32[]{:S(2)}, u32[]{:S(2)}) collective-permute-start(f32[24,384]{1,0:T(8,128)S(1)} %get-tuple-element.47), channel_id=1, source_target_pairs={{0,4},{4,0},{8,12},{12,8},{16,20},{20,16},{24,28},{28,24},{1,5},{5... | collective-permute-start | bytes 110600 | tf_op jit(solution)/shard_map/ppermute | solution.py:770
  11.9 7.3 %collective-permute-start.6 = (f32[8,128]{1,0:T(8,128)S(1)}, f32[8,128]{1,0:T(8,128)S(1)}, u32[]{:S(2)}, u32[]{:S(2)}) collective-permute-start(f32[8,128]{1,0:T(8,128)S(1)} %get-tuple-element.51.table_ref), channel_id=1, source_target_pairs={{0,16},{1,17},{2,18},{3,19},{4,20},{5,21},{6,22},{7,23},{8,24},{9,... | collective-permute-start | bytes 12296 | tf_op jit(solution)/shard_map/ppermute | solution.py:773
  16.1 3.1 %collective-permute-start.4 = (f32[32,144]{1,0:T(8,128)S(1)}, f32[32,144]{1,0:T(8,128)S(1)}, u32[]{:S(2)}, u32[]{:S(2)}) collective-permute-start(f32[32,144]{1,0:T(8,128)S(1)} %get-tuple-element.56), channel_id=1, source_target_pairs={{0,4},{1,2},{2,1},{3,7},{4,0},{5,6},{6,5},{7,3},{8,12},{9,10},{10,... | collective-permute-start | bytes 55304 | tf_op jit(solution)/shard_map/ppermute | solution.py:769
  16.2 4.2 %collective-permute-start.5 = (f32[32,144]{1,0:T(8,128)S(1)}, f32[32,144]{1,0:T(8,128)S(1)}, u32[]{:S(2)}, u32[]{:S(2)}) collective-permute-start(f32[32,144]{1,0:T(8,128)S(1)} %get-tuple-element.57), channel_id=1, source_target_pairs={{0,1},{1,0},{2,3},{3,2},{4,5},{5,4},{6,7},{7,6},{8,9},{9,8},{10,11... | collective-permute-start | bytes 55304 | tf_op jit(solution)/shard_map/ppermute | solution.py:770
  19.0 5.5 %collective-permute-start.9 = (f32[8,128]{1,0:T(8,128)S(1)}, f32[8,128]{1,0:T(8,128)S(1)}, u32[]{:S(2)}, u32[]{:S(2)}) collective-permute-start(f32[8,128]{1,0:T(8,128)S(1)} %get-tuple-element.63), channel_id=1, source_target_pairs={{0,18},{1,19},{2,16},{3,17},{4,22},{5,23},{6,20},{7,21},{8,26},{9,... | collective-permute-start | bytes 12296 | tf_op jit(solution)/shard_map/ppermute | solution.py:773
  20.6 5.2 %collective-permute-start.7 = (f32[24,384]{1,0:T(8,128)S(1)}, f32[24,384]{1,0:T(8,128)S(1)}, u32[]{:S(2)}, u32[]{:S(2)}) collective-permute-start(f32[24,384]{1,0:T(8,128)S(1)} %get-tuple-element.60), channel_id=1, source_target_pairs={{0,28},{1,29},{2,30},{3,31},{4,8},{5,9},{6,10},{7,11},{8,4},{9,5},... | collective-permute-start | bytes 110600 | tf_op jit(solution)/shard_map/ppermute | solution.py:769
  21.3 4.6 %collective-permute-start.8 = (f32[24,384]{1,0:T(8,128)S(1)}, f32[24,384]{1,0:T(8,128)S(1)}, u32[]{:S(2)}, u32[]{:S(2)}) collective-permute-start(f32[24,384]{1,0:T(8,128)S(1)} %get-tuple-element.61), channel_id=1, source_target_pairs={{0,4},{4,0},{8,12},{12,8},{16,20},{20,16},{24,28},{28,24},{1,5},{5... | collective-permute-start | bytes 110600 | tf_op jit(solution)/shard_map/ppermute | solution.py:770
  27.2 4.1 %collective-permute-start.10 = (f32[16,144]{1,0:T(8,128)S(1)}, f32[16,144]{1,0:T(8,128)S(1)}, u32[]{:S(2)}, u32[]{:S(2)}) collective-permute-start(f32[16,144]{1,0:T(8,128)S(1)} %get-tuple-element.73), channel_id=1, source_target_pairs={{0,4},{1,2},{2,1},{3,7},{4,0},{5,6},{6,5},{7,3},{8,12},{9,10},{10,... | collective-permute-start | bytes 27656 | tf_op jit(solution)/shard_map/ppermute | solution.py:769
  27.3 5.0 %collective-permute-start.11 = (f32[16,144]{1,0:T(8,128)S(1)}, f32[16,144]{1,0:T(8,128)S(1)}, u32[]{:S(2)}, u32[]{:S(2)}) collective-permute-start(f32[16,144]{1,0:T(8,128)S(1)} %get-tuple-element.74), channel_id=1, source_target_pairs={{0,1},{1,0},{2,3},{3,2},{4,5},{5,4},{6,7},{7,6},{8,9},{9,8},{10,11... | collective-permute-start | bytes 27656 | tf_op jit(solution)/shard_map/ppermute | solution.py:770
  32.5 3.9 %collective-permute-start.12 = (f32[16,384]{1,0:T(8,128)S(1)}, f32[16,384]{1,0:T(8,128)S(1)}, u32[]{:S(2)}, u32[]{:S(2)}) collective-permute-start(f32[16,384]{1,0:T(8,128)S(1)} %get-tuple-element.76), channel_id=1, source_target_pairs={{0,1},{1,0},{2,3},{3,2},{4,8},{5,9},{6,10},{7,11},{8,4},{9,5},{10,... | collective-permute-start | bytes 73736 | tf_op jit(solution)/shard_map/ppermute | solution.py:769
  34.4 2.0 %collective-permute-start.13 = (f32[16,384]{1,0:T(8,128)S(1)}, f32[16,384]{1,0:T(8,128)S(1)}, u32[]{:S(2)}, u32[]{:S(2)}) collective-permute-start(f32[16,384]{1,0:T(8,128)S(1)} %get-tuple-element.77), channel_id=1, source_target_pairs={{0,4},{4,0},{8,12},{12,8},{16,20},{20,16},{24,28},{28,24},{1,5},{5... | collective-permute-start | bytes 73736 | tf_op jit(solution)/shard_map/ppermute | solution.py:770

commit v24 on v23

--- a/solution.py
+++ b/solution.py
@@ -515,8 +515,6 @@
     ga_ref,
     table_ref,
     farther_ref,
-    inner_w_ref,
-    f_ref,
     gw_ref,
     gf_ref,
     near_ref,
@@ -524,6 +522,7 @@
     basis_ref,
     z_ref,
     w_ref,
+    band_ref,
     t_ref,
     b_ref,
     a_ref,
@@ -543,8 +542,9 @@
     w = jnp.where(mask, DAMP * z + lap(flow), 0.0) * SHRINK
     step = jumps(bands[1])
     damped = (DAMP * SHRINK) * bands[1]
-    z_ref[...] = with_edges(z, y[16:112, :TC] + bands[1][:, :TC])
-    w_ref[...] = with_edges(w, inner_w_ref[...] + step[:, :TC] * f_ref[...] + damped[:, :TC])
+    z_ref[...] = jnp.concatenate([z[16:32, :TC], z[48:64, :TC]], axis=0)
+    w_ref[...] = jnp.concatenate([w[16:32, :TC], w[48:64, :TC]], axis=0)
+    band_ref[...] = jnp.concatenate([bands[1], step, damped, jnp.zeros((5, FC), jnp.float32)], axis=0)
     lane = lanes_of((EXT, 256))
     ones = jnp.where((lane >= 16) & (lane < 112), rows_t_part(basis_ref), 0.0)
     ones = jnp.sum(ones, axis=1, keepdims=True)
@@ -555,7 +555,29 @@
     send(j, a_ref, b_ref, *strips_of(t, basis_ref, 16))
 
 
-def inverse_stats_kernel(t_ref, basis_ref, both_ref, m_ref, z_ref, w_ref, y_ref, stats_ref):
+def tile_of(edge, inner):
+    return jnp.concatenate([edge[:16], inner, edge[16:]], axis=0)
+
+
+def inverse_stats_kernel(
+    t_ref,
+    basis_ref,
+    both_ref,
+    m_ref,
+    first_ref,
+    inner_w_ref,
+    f_ref,
+    edge_z_ref,
+    edge_w_ref,
+    band_ref,
+    y_ref,
+    stats_ref,
+    z_ref,
+    w_ref,
+):
+    on, step, damped = (band_ref[k : k + 1, :TC] for k in range(3))
+    z_ref[...] = tile_of(edge_z_ref, first_ref[16:112, :TC] + on)
+    w_ref[...] = tile_of(edge_w_ref, inner_w_ref[...] + step * f_ref[...] + damped)
     y_ref[...] = solution_of(t_ref[...], basis_ref)
     rt, mt, zt, wt = both_ref[:TR], m_ref[:TR, :TC], z_ref[...], w_ref[...]
     lane, row = lanes_of((1, 256)), rows_of((128, 1))
@@ -606,16 +628,16 @@
 
 
 def dots_kernel(
-    counts, y_ref, m_ref, gb_ref, ga_ref, both_ref, w_ref, stats_ref, inner_v_ref, q_ref, v_ref, stats_out
+    counts, y_ref, m_ref, gb_ref, ga_ref, both_ref, w_ref, stats_ref, q_ref, v_ref, stats_out
 ):
     i, j = place()
     y = y_ref[...]
     q = edges(y, *sides(i, counts[0], ga_ref[...], gb_ref[...]))
     q = jnp.where(edge_mask(counts), q, 0.0)
     v = DAMP * q + lap(edge_part(m_ref) * lap(q))
-    q_ref[...] = with_edges(q, y[16:112, :TC])
-    v_ref[...] = with_edges(v, inner_v_ref[...])
     qe, ve = (jnp.concatenate([x[16:32, :TC], x[48:64, :TC]], axis=0) for x in (q, v))
+    q_ref[...] = qe
+    v_ref[...] = ve
     re = jnp.concatenate([both_ref[:16], both_ref[112:128]], axis=0)
     we = jnp.concatenate([w_ref[:16], w_ref[112:]], axis=0)
     rest = [core_sums(ve), core_sums(re * qe), core_sums(we * qe), core_sums(ve * qe)]
@@ -634,6 +656,8 @@
     both_ref,
     z_ref,
     w_ref,
+    y_ref,
+    inner_v_ref,
     q_ref,
     v_ref,
     solution_ref,
@@ -700,8 +724,8 @@
     coarse = edge_bands(bands)
     image = DAMP * coarse + lap(edge_part(m_ref) * lap(coarse))
     image = with_edges(image, (jumps(bands[1]) * (1.0 / SHRINK))[:, :TC] * f_ref[...] + DAMP * on)
-    y = q_ref[...] + on
-    v = v_ref[...] + image
+    y = tile_of(q_ref, y_ref[16:112, :TC]) + on
+    v = tile_of(v_ref, inner_v_ref[...]) + image
     z, w = z_ref[...], w_ref[...]
     solution_ref[...] = (a * SHRINK) * z + a1 * (beta1 * z - a * y)
     residual_ref[...] = both_ref[:TR] - a * w - a1 * ((beta1 * (1.0 / SHRINK)) * w - a * v)
@@ -835,17 +859,15 @@
         m,
         basis,
     )
-    z, w, t, b, a = call(
+    edge_z, edge_w, band, t, b, a = call(
         functools.partial(second_kernel, counts, width),
-        [(TR, TC)] * 2 + [(EXT, 2 * SPEC)] + [(16, EXT)] * 2,
+        [(32, TC)] * 2 + [(8, FC), (EXT, 2 * SPEC)] + [(16, EXT)] * 2,
         y,
         m,
         gb,
         ga,
         table,
         farther,
-        inner_w,
-        f,
         gw,
         gf,
         near,
@@ -853,7 +875,20 @@
         basis,
     )
     ga, gb = swap(a, b, "col", 1)
-    y, stats = call(inverse_stats_kernel, [(EXT, FC), (1, 128)], t, basis, both, m, z, w)
+    y, stats, z, w = call(
+        inverse_stats_kernel,
+        [(EXT, FC), (1, 128)] + [(TR, TC)] * 2,
+        t,
+        basis,
+        both,
+        m,
+        y,
+        inner_w,
+        f,
+        edge_z,
+        edge_w,
+        band,
+    )
     y, b, a = call(
         functools.partial(columns_kernel, counts), [(EXT, FC)] + [(16, FC)] * 2, y, gb, ga
     )
@@ -869,7 +904,7 @@
     )
     q, v, stats = call(
         functools.partial(dots_kernel, counts),
-        [(TR, TC)] * 2 + [(devices, 128)],
+        [(32, TC)] * 2 + [(devices, 128)],
         y,
         m,
         gb,
@@ -877,7 +912,6 @@
         both,
         w,
         stats,
-        inner_v,
     )
     stats = lax.all_to_all(stats, both_axes, 0, 0, tiled=True)
     return tuple(
@@ -891,6 +925,8 @@
             both,
             z,
             w,
+            y,
+            inner_v,
             q,
             v,
         )

time: 47.3 us -> 47.3 us (level)
  no operation moved by 1% of the time
where the time goes in v24:
time: 47.3 us; the launch traced here: 47.1 us
  starting transfers between devices  17 us (36%)
  waiting for transfers between devices  11.3 us (24%)
  blocking collectives  9.2 us (19%)
  Pallas kernels  7.94 us (17%)
  other arithmetic  0.99 us (2%)
  between operations  0.74 us (2%)
    all_to_all x1, blocking collectives, body(): stats = lax.all_to_all(stats, both_axes, 0, 0, tiled=True)  9.2 us
    ppermute x6, starting transfers between devices, swap(): lax.ppermute(b, both_axes, odd_pairs(counts, both_axes.index(axis), bit))  8.7 us
    pallas_call x14, Pallas kernels, call(): pl.pallas_call(kernel, out_shape=shapes, compiler_params=pltpu.CompilerPa...  7.94 us
    ppermute x6, starting transfers between devices, swap(): return (lax.ppermute(a, axis, pairs_from(lax.axis_size(axis), 0)), gb)  5.65 us
    ppermute x6, waiting for transfers between devices, swap(): lax.ppermute(b, both_axes, odd_pairs(counts, both_axes.index(axis), bit))  4.45 us
    ppermute x6, waiting for transfers between devices, swap(): return (lax.ppermute(a, axis, pairs_from(lax.axis_size(axis), 0)), gb)  4.27 us
    ppermute x2, starting transfers between devices, small_swap(): return lax.ppermute(x, both_axes, xor_pairs(counts, rows, cols))  2.62 us
    ppermute x2, waiting for transfers between devices, small_swap(): return lax.ppermute(x, both_axes, xor_pairs(counts, rows, cols))  2.54 us
  transfers between devices with their start and end apart: 14, of which 8 were waited for; matrix products, arithmetic and copies ran while one was open for 0% of the time, Pallas kernels for 10%

profile of v24, /device:TPU:0, one launch (start us, length us, event | category | flops | bytes accessed | tf_op | source)
XLA Modules:
  0.0 47.1 jit_solution(378027485573992430)
XLA Ops:
  0.6 1.0 %pad_add_fusion.both_ref = f32[256,256]{1,0:T(8,128)S(1)} fusion(f32[128,256]{1,0:T(8,128)} %param.3, f32[128,256]{1,0:T(8,128)} %param.4), kind=kLoop, calls=%fused_computation | loop fusion | flops 65536 | bytes 524288 | tf_op jit(solution)/shard_map/add | solution.py:799
  1.6 0.2 shard_map.50
  1.8 0.0 copy-start
  1.8 4.0 %collective-permute-start = (f32[40,128]{1,0:T(8,128)S(1)}, f32[40,128]{1,0:T(8,128)S(1)}, u32[]{:S(2)}, u32[]{:S(2)}) collective-permute-start(f32[40,128]{1,0:T(8,128)S(1)} %get-tuple-element.47), channel_id=1, source_target_pairs={{0,3},{1,2},{2,1},{3,0},{4,7},{5,6},{6,5},{7,4},{8,11},{9,10},{10,... | collective-permute-start | bytes 61448 | tf_op jit(solution)/shard_map/ppermute | solution.py:793
  5.8 0.5 %collective-permute-start.1 = (f32[40,128]{1,0:T(8,128)S(1)}, f32[40,128]{1,0:T(8,128)S(1)}, u32[]{:S(2)}, u32[]{:S(2)}) collective-permute-start(f32[40,128]{1,0:T(8,128)S(1)} %get-tuple-element.48), channel_id=1, source_target_pairs={{0,1},{1,0},{2,3},{3,2},{4,5},{5,4},{6,7},{7,6},{8,9},{9,8},{10,11... | collective-permute-start | bytes 61448 | tf_op jit(solution)/shard_map/ppermute | solution.py:794
  6.3 1.2 %collective-permute-done.gb_ref = f32[40,128]{1,0:T(8,128)S(1)} collective-permute-done((f32[40,128]{1,0:T(8,128)S(1)}, f32[40,128]{1,0:T(8,128)S(1)}, u32[]{:S(2)}, u32[]{:S(2)}) %collective-permute-start) | collective-permute-done | bytes 20512 | tf_op jit(solution)/shard_map/ppermute | solution.py:793
  7.5 2.0 %collective-permute-done.1.ga_ref = f32[40,128]{1,0:T(8,128)S(1)} collective-permute-done((f32[40,128]{1,0:T(8,128)S(1)}, f32[40,128]{1,0:T(8,128)S(1)}, u32[]{:S(2)}, u32[]{:S(2)}) %collective-permute-start.1) | collective-permute-done | bytes 20512 | tf_op jit(solution)/shard_map/ppermute | solution.py:794
  9.5 0.2 shard_map.51
  9.7 2.0 %collective-permute-start.2 = (f32[24,384]{1,0:T(8,128)S(1)}, f32[24,384]{1,0:T(8,128)S(1)}, u32[]{:S(2)}, u32[]{:S(2)}) collective-permute-start(f32[24,384]{1,0:T(8,128)S(1)} %get-tuple-element.49), channel_id=1, source_target_pairs={{0,28},{1,29},{2,30},{3,31},{4,8},{5,9},{6,10},{7,11},{8,4},{9,5},... | collective-permute-start | bytes 110600 | tf_op jit(solution)/shard_map/ppermute | solution.py:793
  11.7 0.0 collective-permute-start.3
  11.7 0.0 copy-done
  11.7 0.1 shard_map.53
  11.9 2.4 %collective-permute-start.6 = (f32[8,128]{1,0:T(8,128)S(1)}, f32[8,128]{1,0:T(8,128)S(1)}, u32[]{:S(2)}, u32[]{:S(2)}) collective-permute-start(f32[8,128]{1,0:T(8,128)S(1)} %get-tuple-element.54.table_ref), channel_id=1, source_target_pairs={{0,16},{1,17},{2,18},{3,19},{4,20},{5,21},{6,22},{7,23},{8,24},{9,... | collective-permute-start | bytes 12296 | tf_op jit(solution)/shard_map/ppermute | solution.py:797
  14.3 0.6 %shard_map.52.tile_ref = f32[144,512]{1,0:T(8,128)S(1)} custom-call(f32[256,256]{1,0:T(8,128)S(1)} %pad_add_fusion.both_ref, f32[128,128]{1,0:T(8,128)S(1)} %get-tuple-element.51.r3_ref, f32[1104,512]{1,0:T(8,128)S(1)} %copy-done), custom_call_target="tpu_custom_call" | custom-call | flops 500000000 | bytes 1000000 | tf_op jit(solution)/shard_map/pallas_call | solution.py:736
  14.9 0.2 collective-permute-done.2.gb_ref
  15.1 0.0 collective-permute-done.3.ga_ref
  15.1 1.0 %shard_map.54 = (f32[144,512]{1,0:T(8,128)S(1)}, f32[8,128]{1,0:T(8,128)S(1)}, f32[32,144]{1,0:T(8,128)S(1)}, f32[32,144]{1,0:T(8,128)S(1)}) custom-call(f32[24,384]{1,0:T(8,128)S(1)} %collective-permute-done.2.gb_ref, f32[24,384]{1,0:T(8,128)S(1)} %collective-permute-done.3.ga_ref, f32[144,512]{1,0:T(8,128)S(1)} %shard_map.52.tile_ref, ...), custom_call_target="tpu_custom_call" | custom-call | flops 1000000000 | bytes 1000000 | tf_op jit(solution)/shard_map/pallas_call | solution.py:736
  16.1 0.1 collective-permute-start.4
  16.2 2.0 %collective-permute-start.5 = (f32[32,144]{1,0:T(8,128)S(1)}, f32[32,144]{1,0:T(8,128)S(1)}, u32[]{:S(2)}, u32[]{:S(2)}) collective-permute-start(f32[32,144]{1,0:T(8,128)S(1)} %get-tuple-element.60), channel_id=1, source_target_pairs={{0,1},{1,0},{2,3},{3,2},{4,5},{5,4},{6,7},{7,6},{8,9},{9,8},{10,11... | collective-permute-start | bytes 55304 | tf_op jit(solution)/shard_map/ppermute | solution.py:794
  18.2 0.8 %shard_map.55 = (f32[144,384]{1,0:T(8,128)S(1)}, f32[160,384]{1,0:T(8,128)S(1)}, f32[8,128]{1,0:T(8,128)S(1)}) custom-call(f32[144,512]{1,0:T(8,128)S(1)} %get-tuple-element.55.t_ref, f32[1104,512]{1,0:T(8,128)S(1)} %copy-done, f32[256,256]{1,0:T(8,128)S(1)} %pad_add_fusion.both_ref, f32[128,128]{1,0:T(8,128)S(1)} %get-tuple-element.56.h3_ref, ...), custom_call_target="tpu_custom_call" | custom-call | flops 1000000000 | bytes 1000000 | tf_op jit(solution)/shard_map/pallas_call | solution.py:736
  19.0 0.2 collective-permute-start.9
  19.2 0.0 collective-permute-done.6.refs_1_
  19.2 0.0 collective-permute-done.4.gb_ref
  19.2 1.2 %collective-permute-done.5.ga_ref = f32[32,144]{1,0:T(8,128)S(1)} collective-permute-done((f32[32,144]{1,0:T(8,128)S(1)}, f32[32,144]{1,0:T(8,128)S(1)}, u32[]{:S(2)}, u32[]{:S(2)}) %collective-permute-start.5) | collective-permute-done | bytes 18464 | tf_op jit(solution)/shard_map/ppermute | solution.py:794
  20.4 0.2 shard_map.56
  20.6 0.7 %collective-permute-start.7 = (f32[24,384]{1,0:T(8,128)S(1)}, f32[24,384]{1,0:T(8,128)S(1)}, u32[]{:S(2)}, u32[]{:S(2)}) collective-permute-start(f32[24,384]{1,0:T(8,128)S(1)} %get-tuple-element.63), channel_id=1, source_target_pairs={{0,28},{1,29},{2,30},{3,31},{4,8},{5,9},{6,10},{7,11},{8,4},{9,5},... | collective-permute-start | bytes 110600 | tf_op jit(solution)/shard_map/ppermute | solution.py:793
  21.3 0.0 collective-permute-start.8
  21.3 0.7 %shard_map.57 = (f32[96,256]{1,0:T(8,128)S(1)}, f32[96,256]{1,0:T(8,128)S(1)}, f32[144,384]{1,0:T(8,128)S(1)}, f32[144,384]{1,0:T(8,128)S(1)}, f32[16,128]{1,0:T(8,128)S(1)}) custom-call(f32[144,384]{1,0:T(8,128)S(1)} %get-tuple-element.61.y_ref.first_ref, f32[160,384]{1,0:T(8,128)S(1)} %get-tuple-element.62.m_ref, f32[1104,512]{1,0:T(8,128)S(1)} %copy-done), custom_call_target="tpu_custom_call" | custom-call | flops 1000000000 | bytes 1000000 | tf_op jit(solution)/shard_map/pallas_call | solution.py:736
  21.9 2.5 %collective-permute-done.9.farther_ref = f32[8,128]{1,0:T(8,128)S(1)} collective-permute-done((f32[8,128]{1,0:T(8,128)S(1)}, f32[8,128]{1,0:T(8,128)S(1)}, u32[]{:S(2)}, u32[]{:S(2)}) %collective-permute-start.9) | collective-permute-done | bytes 4128 | tf_op jit(solution)/shard_map/ppermute | solution.py:797
  24.5 1.4 %collective-permute-done.7.gb_ref = f32[24,384]{1,0:T(8,128)S(1)} collective-permute-done((f32[24,384]{1,0:T(8,128)S(1)}, f32[24,384]{1,0:T(8,128)S(1)}, u32[]{:S(2)}, u32[]{:S(2)}) %collective-permute-start.7) | collective-permute-done | bytes 36896 | tf_op jit(solution)/shard_map/ppermute | solution.py:793
  25.8 0.0 collective-permute-done.8.ga_ref
  25.8 1.3 %shard_map.58 = (f32[32,256]{1,0:T(8,128)S(1)}, f32[32,256]{1,0:T(8,128)S(1)}, f32[8,384]{1,0:T(8,128)S(1)}, f32[144,512]{1,0:T(8,128)S(1)}, f32[16,144]{1,0:T(8,128)S(1)}, /*index=5*/f32[16,144]{1,0:T(8,128)S(1)}) custom-call(f32[144,384]{1,0:T(8,128)S(1)} %get-tuple-element.61.y_ref.first_ref, f32[160,384]{1,0:T(8,128)S(1)} %get-tuple-element.62.m_ref, ...), custom_call_target="tpu_custom_call" | custom-call | flops 1000000000 | bytes 1000000 | tf_op jit(solution)/shard_map/pallas_call | solution.py:736
  27.2 0.1 collective-permute-start.10
  27.3 3.2 %collective-permute-start.11 = (f32[16,144]{1,0:T(8,128)S(1)}, f32[16,144]{1,0:T(8,128)S(1)}, u32[]{:S(2)}, u32[]{:S(2)}) collective-permute-start(f32[16,144]{1,0:T(8,128)S(1)} %get-tuple-element.78), channel_id=1, source_target_pairs={{0,1},{1,0},{2,3},{3,2},{4,5},{5,4},{6,7},{7,6},{8,9},{9,8},{10,11... | collective-permute-start | bytes 27656 | tf_op jit(solution)/shard_map/ppermute | solution.py:794
  30.4 0.8 %shard_map.59 = (f32[144,384]{1,0:T(8,128)S(1)}, f32[1,128]{1,0:T(1,128)S(1)}, f32[128,256]{1,0:T(8,128)S(1)}, f32[128,256]{1,0:T(8,128)S(1)}) custom-call(f32[144,512]{1,0:T(8,128)S(1)} %get-tuple-element.70.t_ref, f32[1104,512]{1,0:T(8,128)S(1)} %copy-done, f32[256,256]{1,0:T(8,128)S(1)} %pad_add_fusion.both_ref, f32[160,384]{1,0:T(8,128)S(1)} %get-tuple-element.62.m_ref, ...), custom_call_target="tpu_custom_call" | custom-call | flops 1000000000 | bytes 1000000 | tf_op jit(solution)/shard_map/pallas_call | solution.py:736
  31.3 0.0 collective-permute-done.10.gb_ref
  31.3 1.0 %collective-permute-done.11.ga_ref = f32[16,144]{1,0:T(8,128)S(1)} collective-permute-done((f32[16,144]{1,0:T(8,128)S(1)}, f32[16,144]{1,0:T(8,128)S(1)}, u32[]{:S(2)}, u32[]{:S(2)}) %collective-permute-start.11) | collective-permute-done | bytes 9248 | tf_op jit(solution)/shard_map/ppermute | solution.py:794
  32.3 0.2 shard_map.60
  32.5 1.9 %collective-permute-start.12 = (f32[16,384]{1,0:T(8,128)S(1)}, f32[16,384]{1,0:T(8,128)S(1)}, u32[]{:S(2)}, u32[]{:S(2)}) collective-permute-start(f32[16,384]{1,0:T(8,128)S(1)} %get-tuple-element.80), channel_id=1, source_target_pairs={{0,1},{1,0},{2,3},{3,2},{4,8},{5,9},{6,10},{7,11},{8,4},{9,5},{10,... | collective-permute-start | bytes 73736 | tf_op jit(solution)/shard_map/ppermute | solution.py:793
  34.4 0.0 collective-permute-start.13
  34.4 0.4 shard_map.61
  34.8 1.6 %collective-permute-done.12.gb_ref = f32[16,384]{1,0:T(8,128)S(1)} collective-permute-done((f32[16,384]{1,0:T(8,128)S(1)}, f32[16,384]{1,0:T(8,128)S(1)}, u32[]{:S(2)}, u32[]{:S(2)}) %collective-permute-start.12) | collective-permute-done | bytes 24608 | tf_op jit(solution)/shard_map/ppermute | solution.py:793
  36.4 0.0 collective-permute-done.13.ga_ref
  36.4 0.3 shard_map.62
  36.6 9.2 %all_to_all.11 = f32[32,1,128]{2,1,0:T(1,128)S(1)} all-to-all(f32[32,1,128]{2,1,0:T(1,128)S(1)} %bitcast.5), channel_id=1, replica_groups=mesh['row'=8,'col'=4] {'row','col'}, dimensions={0} | all-to-all | bytes 32768 | tf_op jit(solution)/shard_map/all_to_all | solution.py:916
  45.8 1.3 %shard_map.63 = (f32[128,256]{1,0:T(8,128)}, f32[128,256]{1,0:T(8,128)}) custom-call(f32[32,128]{1,0:T(8,128)S(1)} %bitcast.4, f32[1104,512]{1,0:T(8,128)S(1)} %copy-done, f32[160,384]{1,0:T(8,128)S(1)} %get-tuple-element.62.m_ref, f32[96,256]{1,0:T(8,128)S(1)} %get-tuple-element.72.f_ref, f32[256,256]{1,0:T(8,128)S(1)} %pad_add_fusion.both_ref, ...), custom_call_target="tpu_custom_call" | custom-call | flops 1000000000 | bytes 1000000 | tf_op jit(solution)/shard_map/pallas_call | solution.py:736
Async XLA Ops:
  1.8 9.9 %copy-start = (f32[1104,512]{1,0:T(8,128)S(1)}, f32[1104,512]{1,0:T(8,128)}, u32[]{:S(2)}) copy-start(f32[1104,512]{1,0:T(8,128)} %constant.5.clone.basis_ref) | copy-start | bytes 6782980
  1.8 5.7 %collective-permute-start = (f32[40,128]{1,0:T(8,128)S(1)}, f32[40,128]{1,0:T(8,128)S(1)}, u32[]{:S(2)}, u32[]{:S(2)}) collective-permute-start(f32[40,128]{1,0:T(8,128)S(1)} %get-tuple-element.47), channel_id=1, source_target_pairs={{0,3},{1,2},{2,1},{3,0},{4,7},{5,6},{6,5},{7,4},{8,11},{9,10},{10,... | collective-permute-start | bytes 61448 | tf_op jit(solution)/shard_map/ppermute | solution.py:793
  5.8 3.8 %collective-permute-start.1 = (f32[40,128]{1,0:T(8,128)S(1)}, f32[40,128]{1,0:T(8,128)S(1)}, u32[]{:S(2)}, u32[]{:S(2)}) collective-permute-start(f32[40,128]{1,0:T(8,128)S(1)} %get-tuple-element.48), channel_id=1, source_target_pairs={{0,1},{1,0},{2,3},{3,2},{4,5},{5,4},{6,7},{7,6},{8,9},{9,8},{10,11... | collective-permute-start | bytes 61448 | tf_op jit(solution)/shard_map/ppermute | solution.py:794
  9.7 5.4 %collective-permute-start.2 = (f32[24,384]{1,0:T(8,128)S(1)}, f32[24,384]{1,0:T(8,128)S(1)}, u32[]{:S(2)}, u32[]{:S(2)}) collective-permute-start(f32[24,384]{1,0:T(8,128)S(1)} %get-tuple-element.49), channel_id=1, source_target_pairs={{0,28},{1,29},{2,30},{3,31},{4,8},{5,9},{6,10},{7,11},{8,4},{9,5},... | collective-permute-start | bytes 110600 | tf_op jit(solution)/shard_map/ppermute | solution.py:793
  11.7 3.4 %collective-permute-start.3 = (f32[24,384]{1,0:T(8,128)S(1)}, f32[24,384]{1,0:T(8,128)S(1)}, u32[]{:S(2)}, u32[]{:S(2)}) collective-permute-start(f32[24,384]{1,0:T(8,128)S(1)} %get-tuple-element.50), channel_id=1, source_target_pairs={{0,4},{4,0},{8,12},{12,8},{16,20},{20,16},{24,28},{28,24},{1,5},{5... | collective-permute-start | bytes 110600 | tf_op jit(solution)/shard_map/ppermute | solution.py:794
  11.9 7.3 %collective-permute-start.6 = (f32[8,128]{1,0:T(8,128)S(1)}, f32[8,128]{1,0:T(8,128)S(1)}, u32[]{:S(2)}, u32[]{:S(2)}) collective-permute-start(f32[8,128]{1,0:T(8,128)S(1)} %get-tuple-element.54.table_ref), channel_id=1, source_target_pairs={{0,16},{1,17},{2,18},{3,19},{4,20},{5,21},{6,22},{7,23},{8,24},{9,... | collective-permute-start | bytes 12296 | tf_op jit(solution)/shard_map/ppermute | solution.py:797
  16.1 3.1 %collective-permute-start.4 = (f32[32,144]{1,0:T(8,128)S(1)}, f32[32,144]{1,0:T(8,128)S(1)}, u32[]{:S(2)}, u32[]{:S(2)}) collective-permute-start(f32[32,144]{1,0:T(8,128)S(1)} %get-tuple-element.59), channel_id=1, source_target_pairs={{0,4},{1,2},{2,1},{3,7},{4,0},{5,6},{6,5},{7,3},{8,12},{9,10},{10,... | collective-permute-start | bytes 55304 | tf_op jit(solution)/shard_map/ppermute | solution.py:793
  16.2 4.2 %collective-permute-start.5 = (f32[32,144]{1,0:T(8,128)S(1)}, f32[32,144]{1,0:T(8,128)S(1)}, u32[]{:S(2)}, u32[]{:S(2)}) collective-permute-start(f32[32,144]{1,0:T(8,128)S(1)} %get-tuple-element.60), channel_id=1, source_target_pairs={{0,1},{1,0},{2,3},{3,2},{4,5},{5,4},{6,7},{7,6},{8,9},{9,8},{10,11... | collective-permute-start | bytes 55304 | tf_op jit(solution)/shard_map/ppermute | solution.py:794
  19.0 5.5 %collective-permute-start.9 = (f32[8,128]{1,0:T(8,128)S(1)}, f32[8,128]{1,0:T(8,128)S(1)}, u32[]{:S(2)}, u32[]{:S(2)}) collective-permute-start(f32[8,128]{1,0:T(8,128)S(1)} %get-tuple-element.66), channel_id=1, source_target_pairs={{0,18},{1,19},{2,16},{3,17},{4,22},{5,23},{6,20},{7,21},{8,26},{9,... | collective-permute-start | bytes 12296 | tf_op jit(solution)/shard_map/ppermute | solution.py:797
  20.6 5.2 %collective-permute-start.7 = (f32[24,384]{1,0:T(8,128)S(1)}, f32[24,384]{1,0:T(8,128)S(1)}, u32[]{:S(2)}, u32[]{:S(2)}) collective-permute-start(f32[24,384]{1,0:T(8,128)S(1)} %get-tuple-element.63), channel_id=1, source_target_pairs={{0,28},{1,29},{2,30},{3,31},{4,8},{5,9},{6,10},{7,11},{8,4},{9,5},... | collective-permute-start | bytes 110600 | tf_op jit(solution)/shard_map/ppermute | solution.py:793
  21.3 4.6 %collective-permute-start.8 = (f32[24,384]{1,0:T(8,128)S(1)}, f32[24,384]{1,0:T(8,128)S(1)}, u32[]{:S(2)}, u32[]{:S(2)}) collective-permute-start(f32[24,384]{1,0:T(8,128)S(1)} %get-tuple-element.64), channel_id=1, source_target_pairs={{0,4},{4,0},{8,12},{12,8},{16,20},{20,16},{24,28},{28,24},{1,5},{5... | collective-permute-start | bytes 110600 | tf_op jit(solution)/shard_map/ppermute | solution.py:794
  27.2 4.1 %collective-permute-start.10 = (f32[16,144]{1,0:T(8,128)S(1)}, f32[16,144]{1,0:T(8,128)S(1)}, u32[]{:S(2)}, u32[]{:S(2)}) collective-permute-start(f32[16,144]{1,0:T(8,128)S(1)} %get-tuple-element.77), channel_id=1, source_target_pairs={{0,4},{1,2},{2,1},{3,7},{4,0},{5,6},{6,5},{7,3},{8,12},{9,10},{10,... | collective-permute-start | bytes 27656 | tf_op jit(solution)/shard_map/ppermute | solution.py:793
  27.3 5.0 %collective-permute-start.11 = (f32[16,144]{1,0:T(8,128)S(1)}, f32[16,144]{1,0:T(8,128)S(1)}, u32[]{:S(2)}, u32[]{:S(2)}) collective-permute-start(f32[16,144]{1,0:T(8,128)S(1)} %get-tuple-element.78), channel_id=1, source_target_pairs={{0,1},{1,0},{2,3},{3,2},{4,5},{5,4},{6,7},{7,6},{8,9},{9,8},{10,11... | collective-permute-start | bytes 27656 | tf_op jit(solution)/shard_map/ppermute | solution.py:794
  32.5 3.9 %collective-permute-start.12 = (f32[16,384]{1,0:T(8,128)S(1)}, f32[16,384]{1,0:T(8,128)S(1)}, u32[]{:S(2)}, u32[]{:S(2)}) collective-permute-start(f32[16,384]{1,0:T(8,128)S(1)} %get-tuple-element.80), channel_id=1, source_target_pairs={{0,1},{1,0},{2,3},{3,2},{4,8},{5,9},{6,10},{7,11},{8,4},{9,5},{10,... | collective-permute-start | bytes 73736 | tf_op jit(solution)/shard_map/ppermute | solution.py:793
  34.4 2.0 %collective-permute-start.13 = (f32[16,384]{1,0:T(8,128)S(1)}, f32[16,384]{1,0:T(8,128)S(1)}, u32[]{:S(2)}, u32[]{:S(2)}) collective-permute-start(f32[16,384]{1,0:T(8,128)S(1)} %get-tuple-element.81), channel_id=1, source_target_pairs={{0,4},{4,0},{8,12},{12,8},{16,20},{20,16},{24,28},{28,24},{1,5},{5... | collective-permute-start | bytes 73736 | tf_op jit(solution)/shard_map/ppermute | solution.py:794

commit v25 on v23

--- a/solution.py
+++ b/solution.py
@@ -752,7 +752,7 @@
     known = meet(even[0], odd_pairs(counts, 1, 0))
     first = meet(xor_pairs(counts, 4, 0))
     known = meet(even[1], odd_pairs(counts, 0, 0))
-    second = meet(xor_pairs(counts, 4, 2))
+    second = meet(xor_pairs(counts, 4, 1))
     known = meet(even[0], odd_pairs(counts, 1, 1)) | first
     return (meet(even[1], odd_pairs(counts, 0, 0)) | second).all()
 
@@ -817,7 +817,7 @@
         table,
     )
     ga, gb = swap(a, b, "col", 1)
-    farther = small_swap(table_too, 4, 2)
+    farther = small_swap(table_too, 4, 1)
     y, table, b, a = call(
         functools.partial(columns_kernel, counts),
         [(EXT, FC), (depth, 128)] + [(24, FC)] * 2,

time: 47.3 us -> 47.3 us (level)
  waiting for transfers between devices: 11.3 us -> 10.7 us
  starting transfers between devices: 17 us -> 17.5 us
where the time goes in v25:
time: 47.3 us; the launch traced here: 47.1 us
  starting transfers between devices  17.5 us (37%)
  waiting for transfers between devices  10.7 us (23%)
  blocking collectives  9.2 us (19%)
  Pallas kernels  7.94 us (17%)
  other arithmetic  0.99 us (2%)
  between operations  0.74 us (2%)
    all_to_all x1, blocking collectives, body(): stats = lax.all_to_all(stats, both_axes, 0, 0, tiled=True)  9.2 us
    ppermute x6, starting transfers between devices, swap(): lax.ppermute(b, both_axes, odd_pairs(counts, both_axes.index(axis), bit))  8.7 us
    pallas_call x14, Pallas kernels, call(): pl.pallas_call(kernel, out_shape=shapes, compiler_params=pltpu.CompilerPa...  7.94 us
    ppermute x6, starting transfers between devices, swap(): return (lax.ppermute(a, axis, pairs_from(lax.axis_size(axis), 0)), gb)  6.07 us
    ppermute x6, waiting for transfers between devices, swap(): lax.ppermute(b, both_axes, odd_pairs(counts, both_axes.index(axis), bit))  4.45 us
    ppermute x6, waiting for transfers between devices, swap(): return (lax.ppermute(a, axis, pairs_from(lax.axis_size(axis), 0)), gb)  4.14 us
    ppermute x2, starting transfers between devices, small_swap(): return lax.ppermute(x, both_axes, xor_pairs(counts, rows, cols))  2.76 us
    ppermute x2, waiting for transfers between devices, small_swap(): return lax.ppermute(x, both_axes, xor_pairs(counts, rows, cols))  2.12 us
  transfers between devices with their start and end apart: 14, of which 8 were waited for; matrix products, arithmetic and copies ran while one was open for 0% of the time, Pallas kernels for 10%

profile of v25, /device:TPU:0, one launch (start us, length us, event | category | flops | bytes accessed | tf_op | source)
XLA Modules:
  0.0 47.1 jit_solution(1398889013622523926)
XLA Ops:
  0.6 1.0 %pad_add_fusion.both_ref = f32[256,256]{1,0:T(8,128)S(1)} fusion(f32[128,256]{1,0:T(8,128)} %param.3, f32[128,256]{1,0:T(8,128)} %param.4), kind=kLoop, calls=%fused_computation | loop fusion | flops 65536 | bytes 524288 | tf_op jit(solution)/shard_map/add | solution.py:775
  1.6 0.2 shard_map.50
  1.8 0.0 copy-start
  1.8 4.0 %collective-permute-start = (f32[40,128]{1,0:T(8,128)S(1)}, f32[40,128]{1,0:T(8,128)S(1)}, u32[]{:S(2)}, u32[]{:S(2)}) collective-permute-start(f32[40,128]{1,0:T(8,128)S(1)} %get-tuple-element.44), channel_id=1, source_target_pairs={{0,3},{1,2},{2,1},{3,0},{4,7},{5,6},{6,5},{7,4},{8,11},{9,10},{10,... | collective-permute-start | bytes 61448 | tf_op jit(solution)/shard_map/ppermute | solution.py:769
  5.8 0.5 %collective-permute-start.1 = (f32[40,128]{1,0:T(8,128)S(1)}, f32[40,128]{1,0:T(8,128)S(1)}, u32[]{:S(2)}, u32[]{:S(2)}) collective-permute-start(f32[40,128]{1,0:T(8,128)S(1)} %get-tuple-element.45), channel_id=1, source_target_pairs={{0,1},{1,0},{2,3},{3,2},{4,5},{5,4},{6,7},{7,6},{8,9},{9,8},{10,11... | collective-permute-start | bytes 61448 | tf_op jit(solution)/shard_map/ppermute | solution.py:770
  6.3 1.2 %collective-permute-done.gb_ref = f32[40,128]{1,0:T(8,128)S(1)} collective-permute-done((f32[40,128]{1,0:T(8,128)S(1)}, f32[40,128]{1,0:T(8,128)S(1)}, u32[]{:S(2)}, u32[]{:S(2)}) %collective-permute-start) | collective-permute-done | bytes 20512 | tf_op jit(solution)/shard_map/ppermute | solution.py:769
  7.5 2.0 %collective-permute-done.1.ga_ref = f32[40,128]{1,0:T(8,128)S(1)} collective-permute-done((f32[40,128]{1,0:T(8,128)S(1)}, f32[40,128]{1,0:T(8,128)S(1)}, u32[]{:S(2)}, u32[]{:S(2)}) %collective-permute-start.1) | collective-permute-done | bytes 20512 | tf_op jit(solution)/shard_map/ppermute | solution.py:770
  9.5 0.2 shard_map.51
  9.7 2.0 %collective-permute-start.2 = (f32[24,384]{1,0:T(8,128)S(1)}, f32[24,384]{1,0:T(8,128)S(1)}, u32[]{:S(2)}, u32[]{:S(2)}) collective-permute-start(f32[24,384]{1,0:T(8,128)S(1)} %get-tuple-element.46), channel_id=1, source_target_pairs={{0,28},{1,29},{2,30},{3,31},{4,8},{5,9},{6,10},{7,11},{8,4},{9,5},... | collective-permute-start | bytes 110600 | tf_op jit(solution)/shard_map/ppermute | solution.py:769
  11.7 0.0 collective-permute-start.3
  11.7 0.0 copy-done
  11.7 0.1 shard_map.53
  11.9 2.4 %collective-permute-start.6 = (f32[8,128]{1,0:T(8,128)S(1)}, f32[8,128]{1,0:T(8,128)S(1)}, u32[]{:S(2)}, u32[]{:S(2)}) collective-permute-start(f32[8,128]{1,0:T(8,128)S(1)} %get-tuple-element.51.table_ref), channel_id=1, source_target_pairs={{0,16},{1,17},{2,18},{3,19},{4,20},{5,21},{6,22},{7,23},{8,24},{9,... | collective-permute-start | bytes 12296 | tf_op jit(solution)/shard_map/ppermute | solution.py:773
  14.3 0.6 %shard_map.52.tile_ref = f32[144,512]{1,0:T(8,128)S(1)} custom-call(f32[256,256]{1,0:T(8,128)S(1)} %pad_add_fusion.both_ref, f32[128,128]{1,0:T(8,128)S(1)} %get-tuple-element.48.r3_ref, f32[1104,512]{1,0:T(8,128)S(1)} %copy-done), custom_call_target="tpu_custom_call" | custom-call | flops 500000000 | bytes 1000000 | tf_op jit(solution)/shard_map/pallas_call | solution.py:712
  14.9 0.2 collective-permute-done.2.gb_ref
  15.1 0.0 collective-permute-done.3.ga_ref
  15.1 1.0 %shard_map.54 = (f32[144,512]{1,0:T(8,128)S(1)}, f32[8,128]{1,0:T(8,128)S(1)}, f32[32,144]{1,0:T(8,128)S(1)}, f32[32,144]{1,0:T(8,128)S(1)}) custom-call(f32[24,384]{1,0:T(8,128)S(1)} %collective-permute-done.2.gb_ref, f32[24,384]{1,0:T(8,128)S(1)} %collective-permute-done.3.ga_ref, f32[144,512]{1,0:T(8,128)S(1)} %shard_map.52.tile_ref, ...), custom_call_target="tpu_custom_call" | custom-call | flops 1000000000 | bytes 1000000 | tf_op jit(solution)/shard_map/pallas_call | solution.py:712
  16.1 0.1 collective-permute-start.4
  16.2 2.0 %collective-permute-start.5 = (f32[32,144]{1,0:T(8,128)S(1)}, f32[32,144]{1,0:T(8,128)S(1)}, u32[]{:S(2)}, u32[]{:S(2)}) collective-permute-start(f32[32,144]{1,0:T(8,128)S(1)} %get-tuple-element.57), channel_id=1, source_target_pairs={{0,1},{1,0},{2,3},{3,2},{4,5},{5,4},{6,7},{7,6},{8,9},{9,8},{10,11... | collective-permute-start | bytes 55304 | tf_op jit(solution)/shard_map/ppermute | solution.py:770
  18.2 0.8 %shard_map.55 = (f32[144,384]{1,0:T(8,128)S(1)}, f32[160,384]{1,0:T(8,128)S(1)}, f32[8,128]{1,0:T(8,128)S(1)}) custom-call(f32[144,512]{1,0:T(8,128)S(1)} %get-tuple-element.52.t_ref, f32[1104,512]{1,0:T(8,128)S(1)} %copy-done, f32[256,256]{1,0:T(8,128)S(1)} %pad_add_fusion.both_ref, f32[128,128]{1,0:T(8,128)S(1)} %get-tuple-element.53.h3_ref, ...), custom_call_target="tpu_custom_call" | custom-call | flops 1000000000 | bytes 1000000 | tf_op jit(solution)/shard_map/pallas_call | solution.py:712
  19.0 0.3 collective-permute-start.9
  19.3 0.0 collective-permute-done.6.refs_1_
  19.3 0.0 collective-permute-done.4.gb_ref
  19.3 1.1 %collective-permute-done.5.ga_ref = f32[32,144]{1,0:T(8,128)S(1)} collective-permute-done((f32[32,144]{1,0:T(8,128)S(1)}, f32[32,144]{1,0:T(8,128)S(1)}, u32[]{:S(2)}, u32[]{:S(2)}) %collective-permute-start.5) | collective-permute-done | bytes 18464 | tf_op jit(solution)/shard_map/ppermute | solution.py:770
  20.4 0.2 shard_map.56
  20.6 0.7 %collective-permute-start.7 = (f32[24,384]{1,0:T(8,128)S(1)}, f32[24,384]{1,0:T(8,128)S(1)}, u32[]{:S(2)}, u32[]{:S(2)}) collective-permute-start(f32[24,384]{1,0:T(8,128)S(1)} %get-tuple-element.60), channel_id=1, source_target_pairs={{0,28},{1,29},{2,30},{3,31},{4,8},{5,9},{6,10},{7,11},{8,4},{9,5},... | collective-permute-start | bytes 110600 | tf_op jit(solution)/shard_map/ppermute | solution.py:769
  21.3 0.4 collective-permute-start.8
  21.7 0.7 %shard_map.57 = (f32[96,256]{1,0:T(8,128)S(1)}, f32[96,256]{1,0:T(8,128)S(1)}, f32[144,384]{1,0:T(8,128)S(1)}, f32[144,384]{1,0:T(8,128)S(1)}, f32[16,128]{1,0:T(8,128)S(1)}) custom-call(f32[144,384]{1,0:T(8,128)S(1)} %get-tuple-element.58.y_ref, f32[160,384]{1,0:T(8,128)S(1)} %get-tuple-element.59.m_ref, f32[1104,512]{1,0:T(8,128)S(1)} %copy-done), custom_call_target="tpu_custom_call" | custom-call | flops 1000000000 | bytes 1000000 | tf_op jit(solution)/shard_map/pallas_call | solution.py:712
  22.3 2.1 %collective-permute-done.9.farther_ref = f32[8,128]{1,0:T(8,128)S(1)} collective-permute-done((f32[8,128]{1,0:T(8,128)S(1)}, f32[8,128]{1,0:T(8,128)S(1)}, u32[]{:S(2)}, u32[]{:S(2)}) %collective-permute-start.9) | collective-permute-done | bytes 4128 | tf_op jit(solution)/shard_map/ppermute | solution.py:773
  24.5 1.4 %collective-permute-done.7.gb_ref = f32[24,384]{1,0:T(8,128)S(1)} collective-permute-done((f32[24,384]{1,0:T(8,128)S(1)}, f32[24,384]{1,0:T(8,128)S(1)}, u32[]{:S(2)}, u32[]{:S(2)}) %collective-permute-start.7) | collective-permute-done | bytes 36896 | tf_op jit(solution)/shard_map/ppermute | solution.py:769
  25.8 0.0 collective-permute-done.8.ga_ref
  25.8 1.3 %shard_map.58 = (f32[128,256]{1,0:T(8,128)S(1)}, f32[128,256]{1,0:T(8,128)S(1)}, f32[144,512]{1,0:T(8,128)S(1)}, f32[16,144]{1,0:T(8,128)S(1)}, f32[16,144]{1,0:T(8,128)S(1)}) custom-call(f32[144,384]{1,0:T(8,128)S(1)} %get-tuple-element.58.y_ref, f32[160,384]{1,0:T(8,128)S(1)} %get-tuple-element.59.m_ref, f32[24,384]{1,0:T(8,128)S(1)} %collective-permute-done.7.gb_ref, ...), custom_call_target="tpu_custom_call" | custom-call | flops 1000000000 | bytes 1000000 | tf_op jit(solution)/shard_map/pallas_call | solution.py:712
  27.2 0.1 collective-permute-start.10
  27.3 3.2 %collective-permute-start.11 = (f32[16,144]{1,0:T(8,128)S(1)}, f32[16,144]{1,0:T(8,128)S(1)}, u32[]{:S(2)}, u32[]{:S(2)}) collective-permute-start(f32[16,144]{1,0:T(8,128)S(1)} %get-tuple-element.74), channel_id=1, source_target_pairs={{0,1},{1,0},{2,3},{3,2},{4,5},{5,4},{6,7},{7,6},{8,9},{9,8},{10,11... | collective-permute-start | bytes 27656 | tf_op jit(solution)/shard_map/ppermute | solution.py:770
  30.4 0.8 %shard_map.59 = (f32[144,384]{1,0:T(8,128)S(1)}, f32[1,128]{1,0:T(1,128)S(1)}) custom-call(f32[144,512]{1,0:T(8,128)S(1)} %get-tuple-element.69.t_ref, f32[1104,512]{1,0:T(8,128)S(1)} %copy-done, f32[256,256]{1,0:T(8,128)S(1)} %pad_add_fusion.both_ref, f32[160,384]{1,0:T(8,128)S(1)} %get-tuple-element.59.m_ref, f32[128,256]{1,0:T(8,128)S(1)} %get-tuple-element.70.z_ref, ...), custom_call_target="tpu_custom_call" | custom-call | flops 1000000000 | bytes 1000000 | tf_op jit(solution)/shard_map/pallas_call | solution.py:712
  31.3 0.0 collective-permute-done.10.gb_ref
  31.3 1.1 %collective-permute-done.11.ga_ref = f32[16,144]{1,0:T(8,128)S(1)} collective-permute-done((f32[16,144]{1,0:T(8,128)S(1)}, f32[16,144]{1,0:T(8,128)S(1)}, u32[]{:S(2)}, u32[]{:S(2)}) %collective-permute-start.11) | collective-permute-done | bytes 9248 | tf_op jit(solution)/shard_map/ppermute | solution.py:770
  32.3 0.2 shard_map.60
  32.5 1.9 %collective-permute-start.12 = (f32[16,384]{1,0:T(8,128)S(1)}, f32[16,384]{1,0:T(8,128)S(1)}, u32[]{:S(2)}, u32[]{:S(2)}) collective-permute-start(f32[16,384]{1,0:T(8,128)S(1)} %get-tuple-element.76), channel_id=1, source_target_pairs={{0,1},{1,0},{2,3},{3,2},{4,8},{5,9},{6,10},{7,11},{8,4},{9,5},{10,... | collective-permute-start | bytes 73736 | tf_op jit(solution)/shard_map/ppermute | solution.py:769
  34.4 0.0 collective-permute-start.13
  34.4 0.4 shard_map.61
  34.8 1.6 %collective-permute-done.12.gb_ref = f32[16,384]{1,0:T(8,128)S(1)} collective-permute-done((f32[16,384]{1,0:T(8,128)S(1)}, f32[16,384]{1,0:T(8,128)S(1)}, u32[]{:S(2)}, u32[]{:S(2)}) %collective-permute-start.12) | collective-permute-done | bytes 24608 | tf_op jit(solution)/shard_map/ppermute | solution.py:769
  36.4 0.0 collective-permute-done.13.ga_ref
  36.4 0.3 shard_map.62
  36.7 9.2 %all_to_all.11 = f32[32,1,128]{2,1,0:T(1,128)S(1)} all-to-all(f32[32,1,128]{2,1,0:T(1,128)S(1)} %bitcast.5), channel_id=1, replica_groups=mesh['row'=8,'col'=4] {'row','col'}, dimensions={0} | all-to-all | bytes 32768 | tf_op jit(solution)/shard_map/all_to_all | solution.py:882
  45.9 1.3 %shard_map.63 = (f32[128,256]{1,0:T(8,128)}, f32[128,256]{1,0:T(8,128)}) custom-call(f32[32,128]{1,0:T(8,128)S(1)} %bitcast.4, f32[1104,512]{1,0:T(8,128)S(1)} %copy-done, f32[160,384]{1,0:T(8,128)S(1)} %get-tuple-element.59.m_ref, f32[96,256]{1,0:T(8,128)S(1)} %get-tuple-element.65.f_ref, f32[256,256]{1,0:T(8,128)S(1)} %pad_add_fusion.both_ref, ...), custom_call_target="tpu_custom_call" | custom-call | flops 1000000000 | bytes 1000000 | tf_op jit(solution)/shard_map/pallas_call | solution.py:712
Async XLA Ops:
  1.8 9.9 %copy-start = (f32[1104,512]{1,0:T(8,128)S(1)}, f32[1104,512]{1,0:T(8,128)}, u32[]{:S(2)}) copy-start(f32[1104,512]{1,0:T(8,128)} %constant.5.clone.basis_ref) | copy-start | bytes 6782980
  1.8 5.7 %collective-permute-start = (f32[40,128]{1,0:T(8,128)S(1)}, f32[40,128]{1,0:T(8,128)S(1)}, u32[]{:S(2)}, u32[]{:S(2)}) collective-permute-start(f32[40,128]{1,0:T(8,128)S(1)} %get-tuple-element.44), channel_id=1, source_target_pairs={{0,3},{1,2},{2,1},{3,0},{4,7},{5,6},{6,5},{7,4},{8,11},{9,10},{10,... | collective-permute-start | bytes 61448 | tf_op jit(solution)/shard_map/ppermute | solution.py:769
  5.8 3.8 %collective-permute-start.1 = (f32[40,128]{1,0:T(8,128)S(1)}, f32[40,128]{1,0:T(8,128)S(1)}, u32[]{:S(2)}, u32[]{:S(2)}) collective-permute-start(f32[40,128]{1,0:T(8,128)S(1)} %get-tuple-element.45), channel_id=1, source_target_pairs={{0,1},{1,0},{2,3},{3,2},{4,5},{5,4},{6,7},{7,6},{8,9},{9,8},{10,11... | collective-permute-start | bytes 61448 | tf_op jit(solution)/shard_map/ppermute | solution.py:770
  9.7 5.4 %collective-permute-start.2 = (f32[24,384]{1,0:T(8,128)S(1)}, f32[24,384]{1,0:T(8,128)S(1)}, u32[]{:S(2)}, u32[]{:S(2)}) collective-permute-start(f32[24,384]{1,0:T(8,128)S(1)} %get-tuple-element.46), channel_id=1, source_target_pairs={{0,28},{1,29},{2,30},{3,31},{4,8},{5,9},{6,10},{7,11},{8,4},{9,5},... | collective-permute-start | bytes 110600 | tf_op jit(solution)/shard_map/ppermute | solution.py:769
  11.7 3.4 %collective-permute-start.3 = (f32[24,384]{1,0:T(8,128)S(1)}, f32[24,384]{1,0:T(8,128)S(1)}, u32[]{:S(2)}, u32[]{:S(2)}) collective-permute-start(f32[24,384]{1,0:T(8,128)S(1)} %get-tuple-element.47), channel_id=1, source_target_pairs={{0,4},{4,0},{8,12},{12,8},{16,20},{20,16},{24,28},{28,24},{1,5},{5... | collective-permute-start | bytes 110600 | tf_op jit(solution)/shard_map/ppermute | solution.py:770
  11.9 7.5 %collective-permute-start.6 = (f32[8,128]{1,0:T(8,128)S(1)}, f32[8,128]{1,0:T(8,128)S(1)}, u32[]{:S(2)}, u32[]{:S(2)}) collective-permute-start(f32[8,128]{1,0:T(8,128)S(1)} %get-tuple-element.51.table_ref), channel_id=1, source_target_pairs={{0,16},{1,17},{2,18},{3,19},{4,20},{5,21},{6,22},{7,23},{8,24},{9,... | collective-permute-start | bytes 12296 | tf_op jit(solution)/shard_map/ppermute | solution.py:773
  16.1 3.2 %collective-permute-start.4 = (f32[32,144]{1,0:T(8,128)S(1)}, f32[32,144]{1,0:T(8,128)S(1)}, u32[]{:S(2)}, u32[]{:S(2)}) collective-permute-start(f32[32,144]{1,0:T(8,128)S(1)} %get-tuple-element.56), channel_id=1, source_target_pairs={{0,4},{1,2},{2,1},{3,7},{4,0},{5,6},{6,5},{7,3},{8,12},{9,10},{10,... | collective-permute-start | bytes 55304 | tf_op jit(solution)/shard_map/ppermute | solution.py:769
  16.2 4.2 %collective-permute-start.5 = (f32[32,144]{1,0:T(8,128)S(1)}, f32[32,144]{1,0:T(8,128)S(1)}, u32[]{:S(2)}, u32[]{:S(2)}) collective-permute-start(f32[32,144]{1,0:T(8,128)S(1)} %get-tuple-element.57), channel_id=1, source_target_pairs={{0,1},{1,0},{2,3},{3,2},{4,5},{5,4},{6,7},{7,6},{8,9},{9,8},{10,11... | collective-permute-start | bytes 55304 | tf_op jit(solution)/shard_map/ppermute | solution.py:770
  19.0 5.5 %collective-permute-start.9 = (f32[8,128]{1,0:T(8,128)S(1)}, f32[8,128]{1,0:T(8,128)S(1)}, u32[]{:S(2)}, u32[]{:S(2)}) collective-permute-start(f32[8,128]{1,0:T(8,128)S(1)} %get-tuple-element.63), channel_id=1, source_target_pairs={{0,17},{1,16},{2,19},{3,18},{4,21},{5,20},{6,23},{7,22},{8,25},{9,... | collective-permute-start | bytes 12296 | tf_op jit(solution)/shard_map/ppermute | solution.py:773
  20.6 5.2 %collective-permute-start.7 = (f32[24,384]{1,0:T(8,128)S(1)}, f32[24,384]{1,0:T(8,128)S(1)}, u32[]{:S(2)}, u32[]{:S(2)}) collective-permute-start(f32[24,384]{1,0:T(8,128)S(1)} %get-tuple-element.60), channel_id=1, source_target_pairs={{0,28},{1,29},{2,30},{3,31},{4,8},{5,9},{6,10},{7,11},{8,4},{9,5},... | collective-permute-start | bytes 110600 | tf_op jit(solution)/shard_map/ppermute | solution.py:769
  21.3 4.6 %collective-permute-start.8 = (f32[24,384]{1,0:T(8,128)S(1)}, f32[24,384]{1,0:T(8,128)S(1)}, u32[]{:S(2)}, u32[]{:S(2)}) collective-permute-start(f32[24,384]{1,0:T(8,128)S(1)} %get-tuple-element.61), channel_id=1, source_target_pairs={{0,4},{4,0},{8,12},{12,8},{16,20},{20,16},{24,28},{28,24},{1,5},{5... | collective-permute-start | bytes 110600 | tf_op jit(solution)/shard_map/ppermute | solution.py:770
  27.2 4.1 %collective-permute-start.10 = (f32[16,144]{1,0:T(8,128)S(1)}, f32[16,144]{1,0:T(8,128)S(1)}, u32[]{:S(2)}, u32[]{:S(2)}) collective-permute-start(f32[16,144]{1,0:T(8,128)S(1)} %get-tuple-element.73), channel_id=1, source_target_pairs={{0,4},{1,2},{2,1},{3,7},{4,0},{5,6},{6,5},{7,3},{8,12},{9,10},{10,... | collective-permute-start | bytes 27656 | tf_op jit(solution)/shard_map/ppermute | solution.py:769
  27.3 5.0 %collective-permute-start.11 = (f32[16,144]{1,0:T(8,128)S(1)}, f32[16,144]{1,0:T(8,128)S(1)}, u32[]{:S(2)}, u32[]{:S(2)}) collective-permute-start(f32[16,144]{1,0:T(8,128)S(1)} %get-tuple-element.74), channel_id=1, source_target_pairs={{0,1},{1,0},{2,3},{3,2},{4,5},{5,4},{6,7},{7,6},{8,9},{9,8},{10,11... | collective-permute-start | bytes 27656 | tf_op jit(solution)/shard_map/ppermute | solution.py:770
  32.5 3.9 %collective-permute-start.12 = (f32[16,384]{1,0:T(8,128)S(1)}, f32[16,384]{1,0:T(8,128)S(1)}, u32[]{:S(2)}, u32[]{:S(2)}) collective-permute-start(f32[16,384]{1,0:T(8,128)S(1)} %get-tuple-element.76), channel_id=1, source_target_pairs={{0,1},{1,0},{2,3},{3,2},{4,8},{5,9},{6,10},{7,11},{8,4},{9,5},{10,... | collective-permute-start | bytes 73736 | tf_op jit(solution)/shard_map/ppermute | solution.py:769
  34.4 2.0 %collective-permute-start.13 = (f32[16,384]{1,0:T(8,128)S(1)}, f32[16,384]{1,0:T(8,128)S(1)}, u32[]{:S(2)}, u32[]{:S(2)}) collective-permute-start(f32[16,384]{1,0:T(8,128)S(1)} %get-tuple-element.77), channel_id=1, source_target_pairs={{0,4},{4,0},{8,12},{12,8},{16,20},{20,16},{24,28},{28,24},{1,5},{5... | collective-permute-start | bytes 73736 | tf_op jit(solution)/shard_map/ppermute | solution.py:770
